TPU v7x, 32 devices: a whole 2x2x4 slice. The times are simulated.
32 devices in a mesh: pipe: 4 (over y, x), dp: 8 (over z, core).
Axes of the slice: x: 2, y: 2, z: 4, core: 2. Of those that a mesh axis runs over, the one named last changes fastest.
Arguments:
- tokens: bfloat16 [2, 16, 32, 4096], P(None, 'dp'), may hold values from -6 to 6
- cotangents: bfloat16 [2, 16, 32, 4096], P(None, 'dp'), may hold values from -1 to 1
- starts: int32 [2, 16, 4], P(None, 'dp'), may hold values from 0 to 31, as said below
- counts: int32 [2, 16], P(None, 'dp'), may hold values from 1 to 4
- layer_gains: bfloat16 [4, 4096], P('pipe', 'dp'), may hold values from 0.5 to 1.5
- first_map: bfloat16 [4, 4096, 128], P('pipe', 'dp'), may hold values from -0.09375 to 0.09375
- second_map: bfloat16 [4, 128, 4096], P('pipe', None, 'dp'), may hold values from -0.5 to 0.5
Outputs:
- gain_grad: float32 [4, 4096], P('pipe', 'dp')
- first_grad: float32 [4, 4096, 128], P('pipe', 'dp')
- second_grad: float32 [4, 128, 4096], P('pipe', None, 'dp')
Inputs may be any that keep to these rules, and one draw needn't show every extreme that they name: `starts`: each row begins with 0 and rises strictly; a micro-batch's documents begin at the first counts entries of its row, the later entries are not used.
All inputs are finite; a program needn't handle non-finite values.
Results may differ from a plain program's by a relative error of at most 0.03.
Values may be sent and summed in bfloat16 or wider, within the bound.
No kernel may reach another device: no remote copies, remote signals or barrier semaphores. Data moves between devices by JAX's collectives and lax.ppermute only.
A program may use at most 64 MiB of HBM per device.

v0:
```python
import jax
import jax.numpy as jnp
from jax import lax
from jax.sharding import PartitionSpec as P

HD = 128


def partner(shard, axis, distance):
    return lax.ppermute(shard, axis, [(i, i ^ 1 << distance) for i in range(lax.axis_size(axis))])


def passed_along(value, axis, steps):
    count = lax.axis_size(axis)
    initial, last = (max(0, -steps), min(count, count - steps))
    return lax.ppermute(value, axis, [(source, source + steps) for source in range(initial, last)])


def shortened(shard):

    def short(part):
        return part.astype(jnp.bfloat16) if part.dtype == jnp.float32 else part

    return jax.tree.map(short, shard)


def doc_allowed(row_starts, row_count, length):
    positions = jnp.arange(length, dtype=jnp.int32)
    entries = jnp.arange(row_starts.shape[0], dtype=jnp.int32)
    started = (row_starts[None, :] <= positions[:, None]) & (entries < row_count)[None, :]
    document = jnp.sum(started.astype(jnp.int32), axis=1)
    matched = document[:, None] == document[None, :]
    return matched & (positions[None, :] <= positions[:, None])


def apply_layer(activation, gain_row, first_weight, second_weight, allowed):
    length = activation.shape[0]
    model_width = activation.shape[1]
    widened = activation.astype(jnp.float32)
    factor = lax.rsqrt(jnp.mean(widened * widened, axis=1, keepdims=True) + 1e-05)
    normed = (widened * factor * gain_row).astype(jnp.bfloat16)
    split_heads = normed.reshape(length, model_width // HD, HD)
    scores = (
        jnp.einsum("qhd,khd->hqk", split_heads, split_heads, preferred_element_type=jnp.float32)
        / HD
    )
    weights = jnp.where(allowed[None, :, :], jnp.exp(scores), 0.0)
    probabilities = (weights / jnp.sum(weights, axis=2, keepdims=True)).astype(jnp.bfloat16)
    mixed_heads = jnp.einsum(
        "hqk,khd->qhd", probabilities, split_heads, preferred_element_type=jnp.float32
    )
    mixed_heads = mixed_heads.reshape(length, model_width).astype(jnp.bfloat16)
    reduced = jnp.dot(mixed_heads, first_weight, preferred_element_type=jnp.float32).astype(
        jnp.bfloat16
    )
    return (widened + jnp.dot(reduced, second_weight, preferred_element_type=jnp.float32)).astype(
        jnp.bfloat16
    )


def layer_back(activation, gain_row, first_weight, second_weight, allowed, cotangent):
    _, pullback = jax.vjp(
        lambda act_in, gain_in, first_in, second_in: apply_layer(
            act_in, gain_in, first_in, second_in, allowed
        ),
        activation,
        gain_row,
        first_weight,
        second_weight,
    )
    return pullback(cotangent)


def add_masked(running_sums, gradients, live_flag):
    return tuple(
        (
            current + jnp.where(live_flag, gradient.astype(jnp.float32), 0.0)
            for current, gradient in zip(running_sums, gradients)
        )
    )


def round_parts(running_sums):
    return tuple(
        (lax.optimization_barrier(current.astype(jnp.bfloat16)) for current in running_sums)
    )


def per_device(tokens, cotangents, starts, counts, layer_gains, first_map, second_map):
    sections = lax.axis_size("pipe")
    my_section = lax.axis_index("pipe")
    bit_count = sections.bit_length() - 1
    micro_count = tokens.shape[1]
    length = tokens.shape[2]
    model_width = tokens.shape[3]
    tick_count = sections + micro_count - 1
    allowed_all = jax.vmap(
        jax.vmap(lambda row_starts, row_count: doc_allowed(row_starts, row_count, length))
    )(starts, counts)
    mirrored = (layer_gains, first_map, second_map)
    for bit_number in range(bit_count):
        mirrored = partner((mirrored[0], mirrored[1], mirrored[2]), "pipe", bit_number)
    stacked = (
        jnp.concatenate((layer_gains, mirrored[0]), axis=0),
        jnp.concatenate((first_map, mirrored[1]), axis=0),
        jnp.concatenate((second_map, mirrored[2]), axis=0),
    )
    full_gain, full_first, full_second = (
        lax.all_gather(stacked[0], "dp", axis=1, tiled=True),
        lax.all_gather(stacked[1], "dp", axis=1, tiled=True),
        lax.all_gather(stacked[2], "dp", axis=2, tiled=True),
    )

    def slot_of(index_value):
        live_flag = (index_value >= 0) & (index_value < micro_count)
        return (jnp.clip(index_value, 0, micro_count - 1), live_flag)

    def forward_tick(tick_index, loop_state):
        from_below, from_above, stashed = loop_state
        down_slot, down_live = slot_of(tick_index - my_section)
        up_slot, up_live = slot_of(tick_index - (sections - 1 - my_section))
        down_input = jnp.where(my_section == 0, tokens[0, down_slot], from_below)
        up_input = jnp.where(my_section == sections - 1, tokens[1, up_slot], from_above)
        down_output = apply_layer(
            down_input, full_gain[0], full_first[0], full_second[0], allowed_all[0, down_slot]
        )
        up_output = apply_layer(
            up_input, full_gain[1], full_first[1], full_second[1], allowed_all[1, up_slot]
        )
        stashed = stashed.at[0, down_slot].set(
            jnp.where(down_live, down_input, stashed[0, down_slot])
        )
        stashed = stashed.at[1, up_slot].set(jnp.where(up_live, up_input, stashed[1, up_slot]))
        from_below = passed_along(down_output, "pipe", 1)
        from_above = passed_along(up_output, "pipe", -1)
        return (from_below, from_above, stashed)

    empty_rows = jnp.zeros((length, model_width), jnp.bfloat16)
    empty_stash = jnp.zeros((2, micro_count, length, model_width), jnp.bfloat16)
    _, _, stashed = lax.fori_loop(
        0, tick_count, forward_tick, (empty_rows, empty_rows, empty_stash)
    )
    zero_sums = (
        jnp.zeros((model_width,), jnp.float32),
        jnp.zeros((model_width, first_map.shape[2]), jnp.float32),
        jnp.zeros((second_map.shape[1], model_width), jnp.float32),
    )

    def backward_tick(tick_index, loop_state):
        from_above, from_below, down_sums, up_sums = loop_state
        down_slot, down_live = slot_of(tick_index - (sections - 1 - my_section))
        up_slot, up_live = slot_of(tick_index - my_section)
        down_cot = jnp.where(my_section == sections - 1, cotangents[0, down_slot], from_above)
        up_cot = jnp.where(my_section == 0, cotangents[1, up_slot], from_below)
        down_back = layer_back(
            stashed[0, down_slot],
            full_gain[0],
            full_first[0],
            full_second[0],
            allowed_all[0, down_slot],
            down_cot,
        )
        up_back = layer_back(
            stashed[1, up_slot],
            full_gain[1],
            full_first[1],
            full_second[1],
            allowed_all[1, up_slot],
            up_cot,
        )
        down_sums = add_masked(down_sums, down_back[1:], down_live)
        up_sums = add_masked(up_sums, up_back[1:], up_live)
        from_above = passed_along(down_back[0], "pipe", -1)
        from_below = passed_along(up_back[0], "pipe", 1)
        return (from_above, from_below, down_sums, up_sums)

    _, _, down_sums, up_sums = lax.fori_loop(
        0, tick_count, backward_tick, (empty_rows, empty_rows, zero_sums, zero_sums)
    )
    down_parts = round_parts(down_sums)
    up_parts = round_parts(up_sums)
    received = up_parts
    for bit_number in range(bit_count):
        received = jax.tree.map(
            lambda part, own: part.astype(own.dtype),
            partner(shortened(received), "pipe", bit_number),
            received,
        )
    pair_sums = tuple(
        (
            own_part.astype(jnp.float32) + other_part.astype(jnp.float32)
            for own_part, other_part in zip(down_parts, received)
        )
    )
    gain_total, first_total, second_total = (
        lax.psum_scatter(
            pair_sums[0].astype(jnp.bfloat16), "dp", scatter_dimension=0, tiled=True
        ).astype(jnp.float32),
        lax.psum_scatter(
            pair_sums[1].astype(jnp.bfloat16), "dp", scatter_dimension=0, tiled=True
        ).astype(jnp.float32),
        lax.psum_scatter(
            pair_sums[2].astype(jnp.bfloat16), "dp", scatter_dimension=1, tiled=True
        ).astype(jnp.float32),
    )
    return (gain_total[None], first_total[None], second_total[None])


def solution(mesh):
    in_specs = (
        P(None, "dp", None, None),
        P(None, "dp", None, None),
        P(None, "dp", None),
        P(None, "dp"),
        P("pipe", "dp"),
        P("pipe", "dp", None),
        P("pipe", None, "dp"),
    )
    out_specs = (P("pipe", "dp"), P("pipe", "dp", None), P("pipe", None, "dp"))
    return jax.shard_map(
        per_device, mesh=mesh, in_specs=in_specs, out_specs=out_specs, check_vma=False
    )
```

profile of v0, /device:TPU:0, one launch (start us, length us, event | category | flops | bytes accessed | tf_op | source)
XLA Modules:
  0.0 517.4 jit_solution(10443518779571611971)
XLA Ops:
  40.7 13.2 %all_gather.11 = bf16[2,4096]{1,0:T(2,128)(2,1)S(1)} all-gather(bf16[2,512]{1,0:T(2,128)(2,1)S(1)} %pad_maximum_fusion.2), channel_id=1, replica_groups=mesh['pipe'=4,'dp'=8] {'dp'}, dimensions={1}, use_global_device_ids=true | all-gather | bytes 18432 | tf_op jit(solution)/shard_map/all_gather | solution.py:109
  53.9 28.4 %all-gather.5.cloned.1.call-done = bf16[2,4096,128]{2,1,0:T(8,128)(2,1)} async-done(((bf16[2,512,128]{2,1,0:T(8,128)(2,1)}), bf16[2,4096,128]{2,1,0:T(8,128)(2,1)}) %all-gather.5.cloned.1.call-update) | async-done | bytes 2097168 | tf_op jit(solution)/shard_map/all_gather | solution.py:110
  83.1 143.7 %while.49 = (s32[]{:T(128)}, bf16[32,4096]{1,0:T(8,128)(2,1)S(1)}, bf16[32,4096]{1,0:T(8,128)(2,1)}, bf16[2,2,32,4096]{3,2,1,0:T(8,128)(2,1)S(1)}, pred[]{:T(512...) while((s32[]{:T(128)}, bf16[32,4096]{1,0:T(8,128)(2,1)S(1)}, ...), condition=%wide.region_8.9_spmd, body=%wide.region_1.8_spmd.sunk | while | flops 172771520 | bytes 23715560 | solution.py:140
  101.7 4.5 collective-permute-start
  106.3 6.0 %collective-permute-done = bf16[32,4096]{1,0:T(8,128)(2,1)S(1)} collective-permute-done((bf16[32,4096]{1,0:T(8,128)(2,1)}, bf16[32,4096]{1,0:T(8,128)(2,1)S(1)}, u32[]{:S(2)}, u32[]{:S(2)}) %collective-permute-start) | collective-permute-done | bytes 262176 | tf_op jit(solution)/shard_map/while/body/eval_jaxpr/ppermute | solution.py:16
  130.9 4.9 collective-permute-start
  135.8 5.1 collective-permute-done
  159.6 5.8 %collective-permute-start = (bf16[32,4096]{1,0:T(8,128)(2,1)}, bf16[32,4096]{1,0:T(8,128)(2,1)S(1)}, u32[]{:S(2)}, u32[]{:S(2)}) collective-permute-start(bf16[32,4096]{1,0:T(8,128)(2,1)} %fusion.281), channel_id=1, source_target_pairs={{0,8},{8,16},{16,24},{1,9},{9,17},{17,25},{2,10},{10,18},{18,26},{... | collective-permute-start | bytes 786440 | tf_op jit(solution)/shard_map/while/body/eval_jaxpr/ppermute | solution.py:16
  165.4 4.2 collective-permute-done
  188.2 5.8 %collective-permute-start = (bf16[32,4096]{1,0:T(8,128)(2,1)}, bf16[32,4096]{1,0:T(8,128)(2,1)S(1)}, u32[]{:S(2)}, u32[]{:S(2)}) collective-permute-start(bf16[32,4096]{1,0:T(8,128)(2,1)} %fusion.281), channel_id=1, source_target_pairs={{0,8},{8,16},{16,24},{1,9},{9,17},{17,25},{2,10},{10,18},{18,26},{... | collective-permute-start | bytes 786440 | tf_op jit(solution)/shard_map/while/body/eval_jaxpr/ppermute | solution.py:16
  194.0 4.2 collective-permute-done
  216.8 5.8 %collective-permute-start = (bf16[32,4096]{1,0:T(8,128)(2,1)}, bf16[32,4096]{1,0:T(8,128)(2,1)S(1)}, u32[]{:S(2)}, u32[]{:S(2)}) collective-permute-start(bf16[32,4096]{1,0:T(8,128)(2,1)} %fusion.281), channel_id=1, source_target_pairs={{0,8},{8,16},{16,24},{1,9},{9,17},{17,25},{2,10},{10,18},{18,26},{... | collective-permute-start | bytes 786440 | tf_op jit(solution)/shard_map/while/body/eval_jaxpr/ppermute | solution.py:16
  222.6 4.2 collective-permute-done
  228.2 173.2 %while.50 = (s32[]{:T(128)}, bf16[32,4096]{1,0:T(8,128)(2,1)}, bf16[32,4096]{1,0:T(8,128)(2,1)}, f32[4096]{0:T(1024)S(1)}, f32[4096,128]{1,0:T(8,128)}, /*index=...) while((s32[]{:T(128)}, bf16[32,4096]{1,0:T(8,128)(2,1)}, ...), condition=%wide.region_20.21_spmd.clone, body=%wide.region_9.20_spmd.clone.sunk | while | flops 456771968 | bytes 73035120 | solution.py:177
  239.8 6.6 %collective-permute-start.3 = (bf16[32,4096]{1,0:T(8,128)(2,1)}, bf16[32,4096]{1,0:T(8,128)(2,1)}, u32[]{:S(2)}, u32[]{:S(2)}) collective-permute-start(bf16[32,4096]{1,0:T(8,128)(2,1)} %get-tuple-element.1028), channel_id=1, source_target_pairs={{0,8},{8,16},{16,24},{1,9},{9,17},{17,25},{2,10},{10,18},{18,26},{... | collective-permute-start | bytes 786440 | tf_op jit(solution)/shard_map/while/body/eval_jaxpr/ppermute | solution.py:16
  272.9 5.9 %collective-permute-start.3 = (bf16[32,4096]{1,0:T(8,128)(2,1)}, bf16[32,4096]{1,0:T(8,128)(2,1)}, u32[]{:S(2)}, u32[]{:S(2)}) collective-permute-start(bf16[32,4096]{1,0:T(8,128)(2,1)} %get-tuple-element.1028), channel_id=1, source_target_pairs={{0,8},{8,16},{16,24},{1,9},{9,17},{17,25},{2,10},{10,18},{18,26},{... | collective-permute-start | bytes 786440 | tf_op jit(solution)/shard_map/while/body/eval_jaxpr/ppermute | solution.py:16
  281.9 3.9 fusion.335
  289.2 3.7 fusion.338
  308.2 5.6 %collective-permute-start.3 = (bf16[32,4096]{1,0:T(8,128)(2,1)}, bf16[32,4096]{1,0:T(8,128)(2,1)}, u32[]{:S(2)}, u32[]{:S(2)}) collective-permute-start(bf16[32,4096]{1,0:T(8,128)(2,1)} %get-tuple-element.1028), channel_id=1, source_target_pairs={{0,8},{8,16},{16,24},{1,9},{9,17},{17,25},{2,10},{10,18},{18,26},{... | collective-permute-start | bytes 786440 | tf_op jit(solution)/shard_map/while/body/eval_jaxpr/ppermute | solution.py:16
  316.8 3.9 fusion.335
  324.2 3.7 fusion.338
  343.1 5.6 %collective-permute-start.3 = (bf16[32,4096]{1,0:T(8,128)(2,1)}, bf16[32,4096]{1,0:T(8,128)(2,1)}, u32[]{:S(2)}, u32[]{:S(2)}) collective-permute-start(bf16[32,4096]{1,0:T(8,128)(2,1)} %get-tuple-element.1028), channel_id=1, source_target_pairs={{0,8},{8,16},{16,24},{1,9},{9,17},{17,25},{2,10},{10,18},{18,26},{... | collective-permute-start | bytes 786440 | tf_op jit(solution)/shard_map/while/body/eval_jaxpr/ppermute | solution.py:16
  351.8 3.9 fusion.335
  359.1 3.7 fusion.338
  378.1 5.6 %collective-permute-start.3 = (bf16[32,4096]{1,0:T(8,128)(2,1)}, bf16[32,4096]{1,0:T(8,128)(2,1)}, u32[]{:S(2)}, u32[]{:S(2)}) collective-permute-start(bf16[32,4096]{1,0:T(8,128)(2,1)} %get-tuple-element.1028), channel_id=1, source_target_pairs={{0,8},{8,16},{16,24},{1,9},{9,17},{17,25},{2,10},{10,18},{18,26},{... | collective-permute-start | bytes 786440 | tf_op jit(solution)/shard_map/while/body/eval_jaxpr/ppermute | solution.py:16
  386.7 3.9 fusion.335
  394.1 3.7 fusion.338
  405.6 19.2 %collective-permute-done.14 = bf16[128,4096]{1,0:T(8,128)(2,1)S(1)} collective-permute-done((bf16[128,4096]{1,0:T(8,128)(2,1)S(1)}, bf16[128,4096]{1,0:T(8,128)(2,1)S(1)}, u32[]{:S(2)}, u32[]{:S(2)}) %collective-permute-start.14) | collective-permute-done | bytes 1048608 | tf_op jit(solution)/shard_map/ppermute | solution.py:10
  428.8 14.6 %collective-permute-done.15 = bf16[128,4096]{1,0:T(8,128)(2,1)S(1)} collective-permute-done((bf16[128,4096]{1,0:T(8,128)(2,1)S(1)}, bf16[128,4096]{1,0:T(8,128)(2,1)S(1)}, u32[]{:S(2)}, u32[]{:S(2)}) %collective-permute-start.15) | collective-permute-done | bytes 1048608 | tf_op jit(solution)/shard_map/ppermute | solution.py:10
  447.2 15.7 %collective-permute-done.13 = bf16[4096,128]{1,0:T(8,128)(2,1)S(1)} collective-permute-done((bf16[4096,128]{1,0:T(8,128)(2,1)}, bf16[4096,128]{1,0:T(8,128)(2,1)S(1)}, u32[]{:S(2)}, u32[]{:S(2)}) %collective-permute-start.13) | collective-permute-done | bytes 1048608 | tf_op jit(solution)/shard_map/ppermute | solution.py:10
  471.6 14.0 %all-reduce = bf16[4096]{0:T(1024)(128)(2,1)S(1)} all-reduce(bf16[4096]{0:T(1024)(128)(2,1)S(1)} %add_convert_fusion.2), channel_id=2, replica_groups=mesh['pipe'=4,'dp'=8] {'dp'}, use_global_device_ids=true, to_apply=%region_21.22.clone | all-reduce | flops 4096 | bytes 16384
  487.9 21.4 %reduce-scatter.3.cloned.1.call-done = bf16[512,128]{1,0:T(8,128)(2,1)} async-done(((bf16[4096,128]{1,0:T(8,128)(2,1)}), bf16[512,128]{1,0:T(8,128)(2,1)}) %reduce-scatter.3.cloned.1.call-update) | async-done | bytes 131088 | tf_op jit(solution)/shard_map/reduce_scatter | solution.py:199
  (459 shorter events, 264.5 us)
Async XLA Ops:
  7.2 46.7 %all-gather.3.cloned.1.call-start = ((), (), s32[]{:S(2)}) async-start(), calls=%async_computation.2 | async-start | bytes 2359296 | tf_op jit(solution)/shard_map/all_gather | solution.py:111
  7.2 6.7 %collective-permute-start.4 = (bf16[1,128,512]{2,1,0:T(8,128)(2,1)}, bf16[1,128,512]{2,1,0:T(8,128)(2,1)S(1)}, u32[]{:S(2)}, u32[]{:S(2)}) collective-permute-start(bf16[1,128,512]{2,1,0:T(8,128)(2,1)} %param.21), channel_id=1, source_target_pairs={{0,8},{8,0},{16,24},{24,16},{1,9},{9,1},{17,25},{25,17},{2,10},{10... | collective-permute-start | bytes 393224 | tf_op jit(solution)/shard_map/ppermute | solution.py:10
  13.9 5.0 collective-permute-start.5
  20.6 61.7 %all-gather.5.cloned.1.call-start = ((), (), s32[]{:S(2)}) async-start(), calls=%async_computation.3 | async-start | bytes 2359296 | tf_op jit(solution)/shard_map/all_gather | solution.py:110
  20.6 5.2 %collective-permute-start.6 = (bf16[1,512,128]{2,1,0:T(8,128)(2,1)}, bf16[1,512,128]{2,1,0:T(8,128)(2,1)S(1)}, u32[]{:S(2)}, u32[]{:S(2)}) collective-permute-start(bf16[1,512,128]{2,1,0:T(8,128)(2,1)} %param.20), channel_id=1, source_target_pairs={{0,8},{8,0},{16,24},{24,16},{1,9},{9,1},{17,25},{25,17},{2,10},{10... | collective-permute-start | bytes 393224 | tf_op jit(solution)/shard_map/ppermute | solution.py:10
  25.9 5.0 collective-permute-start.7
  32.5 453.8 %reduce-scatter.5.cloned.1.call-start = ((), (), s32[]{:S(2)}) async-start(), calls=%async_computation.5 | async-start | bytes 1179648 | tf_op jit(solution)/shard_map/reduce_scatter | solution.py:202
  94.3 12.0 %collective-permute-start.1 = (bf16[32,4096]{1,0:T(8,128)(2,1)}, bf16[32,4096]{1,0:T(8,128)(2,1)}, u32[]{:S(2)}, u32[]{:S(2)}) collective-permute-start(bf16[32,4096]{1,0:T(8,128)(2,1)} %fusion.286), channel_id=1, source_target_pairs={{8,0},{16,8},{24,16},{9,1},{17,9},{25,17},{10,2},{18,10},{26,18},{... | collective-permute-start | bytes 786440 | tf_op jit(solution)/shard_map/while/body/eval_jaxpr/ppermute | solution.py:16
  101.7 10.5 %collective-permute-start = (bf16[32,4096]{1,0:T(8,128)(2,1)}, bf16[32,4096]{1,0:T(8,128)(2,1)S(1)}, u32[]{:S(2)}, u32[]{:S(2)}) collective-permute-start(bf16[32,4096]{1,0:T(8,128)(2,1)} %fusion.281), channel_id=1, source_target_pairs={{0,8},{8,16},{16,24},{1,9},{9,17},{17,25},{2,10},{10,18},{18,26},{... | collective-permute-start | bytes 786440 | tf_op jit(solution)/shard_map/while/body/eval_jaxpr/ppermute | solution.py:16
  123.5 12.3 %collective-permute-start.1 = (bf16[32,4096]{1,0:T(8,128)(2,1)}, bf16[32,4096]{1,0:T(8,128)(2,1)}, u32[]{:S(2)}, u32[]{:S(2)}) collective-permute-start(bf16[32,4096]{1,0:T(8,128)(2,1)} %fusion.286), channel_id=1, source_target_pairs={{8,0},{16,8},{24,16},{9,1},{17,9},{25,17},{10,2},{18,10},{26,18},{... | collective-permute-start | bytes 786440 | tf_op jit(solution)/shard_map/while/body/eval_jaxpr/ppermute | solution.py:16
  130.9 10.0 %collective-permute-start = (bf16[32,4096]{1,0:T(8,128)(2,1)}, bf16[32,4096]{1,0:T(8,128)(2,1)S(1)}, u32[]{:S(2)}, u32[]{:S(2)}) collective-permute-start(bf16[32,4096]{1,0:T(8,128)(2,1)} %fusion.281), channel_id=1, source_target_pairs={{0,8},{8,16},{16,24},{1,9},{9,17},{17,25},{2,10},{10,18},{18,26},{... | collective-permute-start | bytes 786440 | tf_op jit(solution)/shard_map/while/body/eval_jaxpr/ppermute | solution.py:16
  152.1 13.2 %collective-permute-start.1 = (bf16[32,4096]{1,0:T(8,128)(2,1)}, bf16[32,4096]{1,0:T(8,128)(2,1)}, u32[]{:S(2)}, u32[]{:S(2)}) collective-permute-start(bf16[32,4096]{1,0:T(8,128)(2,1)} %fusion.286), channel_id=1, source_target_pairs={{8,0},{16,8},{24,16},{9,1},{17,9},{25,17},{10,2},{18,10},{26,18},{... | collective-permute-start | bytes 786440 | tf_op jit(solution)/shard_map/while/body/eval_jaxpr/ppermute | solution.py:16
  159.6 10.0 %collective-permute-start = (bf16[32,4096]{1,0:T(8,128)(2,1)}, bf16[32,4096]{1,0:T(8,128)(2,1)S(1)}, u32[]{:S(2)}, u32[]{:S(2)}) collective-permute-start(bf16[32,4096]{1,0:T(8,128)(2,1)} %fusion.281), channel_id=1, source_target_pairs={{0,8},{8,16},{16,24},{1,9},{9,17},{17,25},{2,10},{10,18},{18,26},{... | collective-permute-start | bytes 786440 | tf_op jit(solution)/shard_map/while/body/eval_jaxpr/ppermute | solution.py:16
  180.8 13.2 %collective-permute-start.1 = (bf16[32,4096]{1,0:T(8,128)(2,1)}, bf16[32,4096]{1,0:T(8,128)(2,1)}, u32[]{:S(2)}, u32[]{:S(2)}) collective-permute-start(bf16[32,4096]{1,0:T(8,128)(2,1)} %fusion.286), channel_id=1, source_target_pairs={{8,0},{16,8},{24,16},{9,1},{17,9},{25,17},{10,2},{18,10},{26,18},{... | collective-permute-start | bytes 786440 | tf_op jit(solution)/shard_map/while/body/eval_jaxpr/ppermute | solution.py:16
  188.2 10.0 %collective-permute-start = (bf16[32,4096]{1,0:T(8,128)(2,1)}, bf16[32,4096]{1,0:T(8,128)(2,1)S(1)}, u32[]{:S(2)}, u32[]{:S(2)}) collective-permute-start(bf16[32,4096]{1,0:T(8,128)(2,1)} %fusion.281), channel_id=1, source_target_pairs={{0,8},{8,16},{16,24},{1,9},{9,17},{17,25},{2,10},{10,18},{18,26},{... | collective-permute-start | bytes 786440 | tf_op jit(solution)/shard_map/while/body/eval_jaxpr/ppermute | solution.py:16
  209.4 13.2 %collective-permute-start.1 = (bf16[32,4096]{1,0:T(8,128)(2,1)}, bf16[32,4096]{1,0:T(8,128)(2,1)}, u32[]{:S(2)}, u32[]{:S(2)}) collective-permute-start(bf16[32,4096]{1,0:T(8,128)(2,1)} %fusion.286), channel_id=1, source_target_pairs={{8,0},{16,8},{24,16},{9,1},{17,9},{25,17},{10,2},{18,10},{26,18},{... | collective-permute-start | bytes 786440 | tf_op jit(solution)/shard_map/while/body/eval_jaxpr/ppermute | solution.py:16
  216.8 10.0 %collective-permute-start = (bf16[32,4096]{1,0:T(8,128)(2,1)}, bf16[32,4096]{1,0:T(8,128)(2,1)S(1)}, u32[]{:S(2)}, u32[]{:S(2)}) collective-permute-start(bf16[32,4096]{1,0:T(8,128)(2,1)} %fusion.281), channel_id=1, source_target_pairs={{0,8},{8,16},{16,24},{1,9},{9,17},{17,25},{2,10},{10,18},{18,26},{... | collective-permute-start | bytes 786440 | tf_op jit(solution)/shard_map/while/body/eval_jaxpr/ppermute | solution.py:16
  238.5 22.7 %collective-permute-start.2 = (bf16[32,4096]{1,0:T(8,128)(2,1)}, bf16[32,4096]{1,0:T(8,128)(2,1)}, u32[]{:S(2)}, u32[]{:S(2)}) collective-permute-start(bf16[32,4096]{1,0:T(8,128)(2,1)} %fusion.332), channel_id=1, source_target_pairs={{8,0},{16,8},{24,16},{9,1},{17,9},{25,17},{10,2},{18,10},{26,18},{... | collective-permute-start | bytes 786440 | tf_op jit(solution)/shard_map/while/body/eval_jaxpr/ppermute | solution.py:16
  239.8 21.4 %collective-permute-start.3 = (bf16[32,4096]{1,0:T(8,128)(2,1)}, bf16[32,4096]{1,0:T(8,128)(2,1)}, u32[]{:S(2)}, u32[]{:S(2)}) collective-permute-start(bf16[32,4096]{1,0:T(8,128)(2,1)} %get-tuple-element.1028), channel_id=1, source_target_pairs={{0,8},{8,16},{16,24},{1,9},{9,17},{17,25},{2,10},{10,18},{18,26},{... | collective-permute-start | bytes 786440 | tf_op jit(solution)/shard_map/while/body/eval_jaxpr/ppermute | solution.py:16
  271.6 25.0 %collective-permute-start.2 = (bf16[32,4096]{1,0:T(8,128)(2,1)}, bf16[32,4096]{1,0:T(8,128)(2,1)}, u32[]{:S(2)}, u32[]{:S(2)}) collective-permute-start(bf16[32,4096]{1,0:T(8,128)(2,1)} %fusion.332), channel_id=1, source_target_pairs={{8,0},{16,8},{24,16},{9,1},{17,9},{25,17},{10,2},{18,10},{26,18},{... | collective-permute-start | bytes 786440 | tf_op jit(solution)/shard_map/while/body/eval_jaxpr/ppermute | solution.py:16
  272.9 23.7 %collective-permute-start.3 = (bf16[32,4096]{1,0:T(8,128)(2,1)}, bf16[32,4096]{1,0:T(8,128)(2,1)}, u32[]{:S(2)}, u32[]{:S(2)}) collective-permute-start(bf16[32,4096]{1,0:T(8,128)(2,1)} %get-tuple-element.1028), channel_id=1, source_target_pairs={{0,8},{8,16},{16,24},{1,9},{9,17},{17,25},{2,10},{10,18},{18,26},{... | collective-permute-start | bytes 786440 | tf_op jit(solution)/shard_map/while/body/eval_jaxpr/ppermute | solution.py:16
  306.9 24.6 %collective-permute-start.2 = (bf16[32,4096]{1,0:T(8,128)(2,1)}, bf16[32,4096]{1,0:T(8,128)(2,1)}, u32[]{:S(2)}, u32[]{:S(2)}) collective-permute-start(bf16[32,4096]{1,0:T(8,128)(2,1)} %fusion.332), channel_id=1, source_target_pairs={{8,0},{16,8},{24,16},{9,1},{17,9},{25,17},{10,2},{18,10},{26,18},{... | collective-permute-start | bytes 786440 | tf_op jit(solution)/shard_map/while/body/eval_jaxpr/ppermute | solution.py:16
  308.2 23.3 %collective-permute-start.3 = (bf16[32,4096]{1,0:T(8,128)(2,1)}, bf16[32,4096]{1,0:T(8,128)(2,1)}, u32[]{:S(2)}, u32[]{:S(2)}) collective-permute-start(bf16[32,4096]{1,0:T(8,128)(2,1)} %get-tuple-element.1028), channel_id=1, source_target_pairs={{0,8},{8,16},{16,24},{1,9},{9,17},{17,25},{2,10},{10,18},{18,26},{... | collective-permute-start | bytes 786440 | tf_op jit(solution)/shard_map/while/body/eval_jaxpr/ppermute | solution.py:16
  341.8 24.6 %collective-permute-start.2 = (bf16[32,4096]{1,0:T(8,128)(2,1)}, bf16[32,4096]{1,0:T(8,128)(2,1)}, u32[]{:S(2)}, u32[]{:S(2)}) collective-permute-start(bf16[32,4096]{1,0:T(8,128)(2,1)} %fusion.332), channel_id=1, source_target_pairs={{8,0},{16,8},{24,16},{9,1},{17,9},{25,17},{10,2},{18,10},{26,18},{... | collective-permute-start | bytes 786440 | tf_op jit(solution)/shard_map/while/body/eval_jaxpr/ppermute | solution.py:16
  343.1 23.3 %collective-permute-start.3 = (bf16[32,4096]{1,0:T(8,128)(2,1)}, bf16[32,4096]{1,0:T(8,128)(2,1)}, u32[]{:S(2)}, u32[]{:S(2)}) collective-permute-start(bf16[32,4096]{1,0:T(8,128)(2,1)} %get-tuple-element.1028), channel_id=1, source_target_pairs={{0,8},{8,16},{16,24},{1,9},{9,17},{17,25},{2,10},{10,18},{18,26},{... | collective-permute-start | bytes 786440 | tf_op jit(solution)/shard_map/while/body/eval_jaxpr/ppermute | solution.py:16
  376.8 24.6 %collective-permute-start.2 = (bf16[32,4096]{1,0:T(8,128)(2,1)}, bf16[32,4096]{1,0:T(8,128)(2,1)}, u32[]{:S(2)}, u32[]{:S(2)}) collective-permute-start(bf16[32,4096]{1,0:T(8,128)(2,1)} %fusion.332), channel_id=1, source_target_pairs={{8,0},{16,8},{24,16},{9,1},{17,9},{25,17},{10,2},{18,10},{26,18},{... | collective-permute-start | bytes 786440 | tf_op jit(solution)/shard_map/while/body/eval_jaxpr/ppermute | solution.py:16
  378.1 23.3 %collective-permute-start.3 = (bf16[32,4096]{1,0:T(8,128)(2,1)}, bf16[32,4096]{1,0:T(8,128)(2,1)}, u32[]{:S(2)}, u32[]{:S(2)}) collective-permute-start(bf16[32,4096]{1,0:T(8,128)(2,1)} %get-tuple-element.1028), channel_id=1, source_target_pairs={{0,8},{8,16},{16,24},{1,9},{9,17},{17,25},{2,10},{10,18},{18,26},{... | collective-permute-start | bytes 786440 | tf_op jit(solution)/shard_map/while/body/eval_jaxpr/ppermute | solution.py:16
  403.3 21.5 %collective-permute-start.14 = (bf16[128,4096]{1,0:T(8,128)(2,1)S(1)}, bf16[128,4096]{1,0:T(8,128)(2,1)S(1)}, u32[]{:S(2)}, u32[]{:S(2)}) collective-permute-start(bf16[128,4096]{1,0:T(8,128)(2,1)S(1)} %convert_element_type.624), channel_id=1, source_target_pairs={{0,8},{8,0},{16,24},{24,16},{1,9},{9,1},{17,25},{25,17},{2,10},{10... | collective-permute-start | bytes 3145736 | tf_op jit(solution)/shard_map/ppermute | solution.py:10
  424.8 18.6 %collective-permute-start.15 = (bf16[128,4096]{1,0:T(8,128)(2,1)S(1)}, bf16[128,4096]{1,0:T(8,128)(2,1)S(1)}, u32[]{:S(2)}, u32[]{:S(2)}) collective-permute-start(bf16[128,4096]{1,0:T(8,128)(2,1)S(1)} %collective-permute-done.14), channel_id=1, source_target_pairs={{0,16},{8,24},{16,0},{24,8},{1,17},{9,25},{17,1},{25,9},{2,18},{10... | collective-permute-start | bytes 3145736 | tf_op jit(solution)/shard_map/ppermute | solution.py:10
  428.8 15.9 %collective-permute-start.12 = (bf16[4096,128]{1,0:T(8,128)(2,1)}, bf16[4096,128]{1,0:T(8,128)(2,1)}, u32[]{:S(2)}, u32[]{:S(2)}) collective-permute-start(bf16[4096,128]{1,0:T(8,128)(2,1)} %convert_element_type.619), channel_id=1, source_target_pairs={{0,8},{8,0},{16,24},{24,16},{1,9},{9,1},{17,25},{25,17},{2,10},{10... | collective-permute-start | bytes 3145736 | tf_op jit(solution)/shard_map/ppermute | solution.py:10
  444.6 64.6 %reduce-scatter.3.cloned.1.call-start = ((), (), s32[]{:S(2)}) async-start(), calls=%async_computation.4 | async-start | bytes 1179648 | tf_op jit(solution)/shard_map/reduce_scatter | solution.py:199
  444.7 18.2 %collective-permute-start.13 = (bf16[4096,128]{1,0:T(8,128)(2,1)}, bf16[4096,128]{1,0:T(8,128)(2,1)S(1)}, u32[]{:S(2)}, u32[]{:S(2)}) collective-permute-start(bf16[4096,128]{1,0:T(8,128)(2,1)} %collective-permute-done.12), channel_id=1, source_target_pairs={{0,16},{8,24},{16,0},{24,8},{1,17},{9,25},{17,1},{25,9},{2,18},{10... | collective-permute-start | bytes 3145736 | tf_op jit(solution)/shard_map/ppermute | solution.py:10
  (49 other events, 310.2 us)
Sparse Core Ops, SparseCore 0:
  20.7 30.6 all-gather.2
  53.6 28.6 all-gather.4
  444.8 31.6 reduce-scatter.4
  478.6 30.6 reduce-scatter.2
where the time goes:
time: 520 us; the launch traced here: 517 us
  matrix products  168 us (32%)
  waiting for transfers between devices  141 us (27%)
  starting transfers between devices  92.2 us (18%)
  other arithmetic  64.2 us (12%)
  blocking collectives  27.2 us (5%)
  between operations  14.6 us (3%)
  local copies, waits for them, and re-layouts  8.05 us (2%)
    ppermute x20, starting transfers between devices, passed_along(): lax.ppermute(value, axis, [(source, source + steps) for source in range(i...  68.8 us
    ppermute x12, waiting for transfers between devices, partner(): lax.ppermute(shard, axis, [(i, i ^ 1 << distance) for i in range(lax.axis...  67.4 us
    dot_general x30, matrix products, apply_layer(): jnp.dot(reduced, second_weight, preferred_element_type=jnp.float32)  66.9 us
    dot_general x40, matrix products, apply_layer(): jnp.einsum('hqk,khd->qhd', probabilities, split_heads, preferred_element_...  43.1 us
    dot_general x20, matrix products, apply_layer(): jnp.dot(mixed_heads, first_weight, preferred_element_type=jnp.float32)  38.3 us
    all_gather x1, waiting for transfers between devices, per_device(): lax.all_gather(stacked[1], 'dp', axis=1, tiled=True)  28.4 us
    ppermute x20, waiting for transfers between devices, passed_along(): lax.ppermute(value, axis, [(source, source + steps) for source in range(i...  23.6 us
    ppermute x12, starting transfers between devices, partner(): lax.ppermute(shard, axis, [(i, i ^ 1 << distance) for i in range(lax.axis...  23.2 us
  transfers between devices with their start and end apart: 36, of which 18 were waited for; matrix products, arithmetic and copies ran while one was open for 25% of the time, Pallas kernels for 0%

commit v1 on v0

v1 whole, which is shorter than its diff:
```python
import functools

import jax
import jax.numpy as jnp
from jax import lax
from jax.experimental import pallas as pl
from jax.experimental.pallas import tpu as pltpu
from jax.sharding import Mesh, PartitionSpec as P

HD = 128
EPS = 1e-05
BF = jnp.bfloat16
F32 = jnp.float32
PARAMS = pltpu.CompilerParams(vmem_limit_bytes=48 * 1024 * 1024)


def dot(a, b):
    return jnp.dot(a, b, preferred_element_type=F32)


def dot_nt(a, b):
    return lax.dot_general(a, b, (((1,), (1,)), ((), ())), preferred_element_type=F32)


def dot_tn(a, b):
    return lax.dot_general(a, b, (((0,), (0,)), ((), ())), preferred_element_type=F32)


def two_parts(value):
    high = value.astype(BF)
    return high, (value - high.astype(F32)).astype(BF)


def vmem_specs(count):
    return [pl.BlockSpec(memory_space=pltpu.VMEM)] * count


def layer_spec(shape, layer):
    return pl.BlockSpec((1,) + shape[1:], lambda *_: (layer, 0, 0, 0))


def slice_rows(own):
    return 2 * own + 16


def pack_kernel(slots, live, starts, counts, tok, cot, gain, first, second, pay, weights):
    micro = pl.program_id(0)
    groups, length, width = pay.shape[0], tok.shape[1], tok.shape[2]
    local = width // groups
    own = first.shape[1]
    slot = slots[micro]
    widened = tok[0].astype(F32)
    mean = jnp.mean(widened * widened, axis=1, keepdims=True)
    mean_high, mean_low = two_parts(mean)
    position = lax.broadcasted_iota(jnp.int32, (length, HD), 0)
    document = jnp.zeros((length, HD), jnp.int32)
    for entry in range(starts.shape[1]):
        started = (starts[slot, entry] <= position) & (entry < counts[slot])
        document = document + started.astype(jnp.int32)
    lane = lax.broadcasted_iota(jnp.int32, (length, HD), 1)
    tail = jnp.where(
        lane == 0,
        document.astype(F32),
        jnp.where(lane == 1, mean_high.astype(F32), mean_low.astype(F32)),
    ).astype(BF)
    keep = live[micro] > 0
    for group in range(groups):
        part = slice(group * local, (group + 1) * local)
        pay[group, :, 0:local] = tok[0, :, part]
        cotangent = cot[0, :, part]
        pay[group, :, local : 2 * local] = jnp.where(keep, cotangent, jnp.zeros_like(cotangent))
        pay[group, :, 2 * local :] = tail

    @pl.when(micro == 0)
    def _():
        weights[0:own, :] = first[0]
        weights[own : 2 * own, :] = second[0].astype(F32).T.astype(BF)
        gains = [
            gain[0:1, head * HD : (head + 1) * HD].astype(F32) for head in range(own // HD)
        ]
        gains.append(jnp.zeros((16 - own // HD, HD), F32))
        weights[2 * own :, :] = jnp.concatenate(gains, axis=0).astype(BF)


def pack(slots, live, starts, counts, tokens, cotangents, gain, first, second, groups):
    micro_total, length, width = tokens.shape
    micro_local = slots.shape[0]
    own = first.shape[1]
    local = width // groups

    def picked(micro, slots, *_):
        return (slots[micro], 0, 0)

    whole = lambda shape: pl.BlockSpec(shape, lambda *_: (0,) * len(shape))
    return pl.pallas_call(
        pack_kernel,
        grid_spec=pltpu.PrefetchScalarGridSpec(
            num_scalar_prefetch=4,
            grid=(micro_local,),
            in_specs=[
                pl.BlockSpec((1, length, width), picked),
                pl.BlockSpec((1, length, width), picked),
                whole(gain.shape),
                whole(first.shape),
                whole(second.shape),
            ],
            out_specs=[
                pl.BlockSpec((groups, length, 2 * local + HD), lambda micro, *_: (0, micro, 0)),
                whole((slice_rows(own), HD)),
            ],
        ),
        out_shape=[
            jax.ShapeDtypeStruct((groups, micro_local * length, 2 * local + HD), BF),
            jax.ShapeDtypeStruct((slice_rows(own), HD), BF),
        ],
        compiler_params=PARAMS,
        name="pack",
    )(slots, live, starts, counts, tokens, cotangents, gain, first, second)


def head_gain(weights, head):
    own = (weights.shape[2] - 16) // 2
    per_slice = own // HD
    row = 2 * own + head % per_slice
    return weights[0, head // per_slice, row : row + 1, :].astype(F32)


def block_size(rows):
    return HD if rows % HD == 0 else rows


def to_rank(value, weights, at):
    own = (weights.shape[2] - 16) // 2
    total = None
    for side in range(weights.shape[1]):
        term = dot(value[:, side * own : (side + 1) * own], weights[0, side, at : at + own, :])
        total = term if total is None else total + term
    return total


def from_rank(value, weights, at, side):
    own = (weights.shape[2] - 16) // 2
    return dot_nt(value, weights[0, side, at : at + own, :])


def gram(weights):
    own = (weights.shape[2] - 16) // 2
    total = None
    for side in range(weights.shape[1]):
        part = weights[0, side, own : 2 * own, :]
        term = dot_tn(part, part)
        total = term if total is None else total + term
    return total


def attend(x, mean, weights, mask, probs, mixed):
    rows, local = x.shape
    size = block_size(rows)
    factor = lax.rsqrt(mean + EPS)
    for block in range(rows // size):
        span = slice(block * size, (block + 1) * size)
        allowed = mask[block] > 0
        for head in range(local // HD):
            part = slice(head * HD, (head + 1) * HD)
            normed = (x[span, part].astype(F32) * factor[span] * head_gain(weights, head)).astype(BF)
            scores = dot_nt(normed, normed) * (1.0 / HD)
            raw = jnp.where(allowed, jnp.exp(scores), 0.0)
            prob = (raw / jnp.sum(raw, axis=1, keepdims=True)).astype(BF)
            probs[block, head] = prob
            mixed[span, part] = dot(prob, normed).astype(BF)


def send_forward(x, weights, mixed, pay):
    rows = x.shape[0]
    own = (weights.shape[2] - 16) // 2
    pay[0:rows, :] = to_rank(mixed[...], weights, 0).astype(BF)
    pay[rows : 2 * rows, :] = to_rank(x[...], weights, own).astype(BF)
    pay[2 * rows : 2 * rows + HD, :] = gram(weights).astype(BF)


def total_of(pays, start, stop):
    total = pays[0][start:stop, :].astype(F32)
    for pay in pays[1:]:
        total = total + pay[start:stop, :].astype(F32)
    return total


def receive_forward(pays, x_before, mean_before, weights_before, width, x, mean, reduced, cross):
    rows, local = x_before.shape
    own = (weights_before.shape[2] - 16) // 2
    low_rank = total_of(pays, 0, rows).astype(BF)
    before = total_of(pays, rows, 2 * rows)
    high, low = two_parts(total_of(pays, 2 * rows, 2 * rows + HD))
    through = dot(low_rank, high) + dot(low_rank, low)
    wide = low_rank.astype(F32)
    change = jnp.sum(wide * (2.0 * before + through), axis=1, keepdims=True) / width
    new_mean = jnp.maximum(mean_before[:, 0:1] + change, 0.0)
    mean[...] = jnp.broadcast_to(new_mean, mean.shape)
    reduced[...] = low_rank
    cross[...] = before + through
    for side in range(weights_before.shape[1]):
        part = slice(side * own, (side + 1) * own)
        x[:, part] = (
            x_before[:, part].astype(F32) + from_rank(low_rank, weights_before, own, side)
        ).astype(BF)


def first_kernel(length, received, weights, x, cot, mask, mean, probs, mixed, pay):
    rows, local = x.shape
    size = block_size(rows)
    x[...] = received[:, 0:local]
    cot[...] = received[:, local : 2 * local]
    tail = received[:, 2 * local :].astype(F32)
    mean[...] = jnp.broadcast_to(tail[:, 1:2] + tail[:, 2:3], mean.shape)
    build_mask(tail[:, 0:1], mask, size, length)
    attend(x, mean[:, 0:1], weights, mask, probs, mixed)
    send_forward(x, weights, mixed, pay)


def build_mask(document, mask, size, length):
    query = lax.broadcasted_iota(jnp.int32, (size, size), 0)
    key = lax.broadcasted_iota(jnp.int32, (size, size), 1)
    for block in range(mask.shape[0]):
        by_query = jnp.broadcast_to(document[block * size : (block + 1) * size], (size, size))
        by_key = by_query.T
        allowed = (by_query == by_key) & (key <= query) & (query // length == key // length)
        mask[block] = allowed.astype(F32).astype(BF)


def middle_kernel(count, last, width, *refs):
    pays, refs = refs[:count], refs[count:]
    x_before, mean_before, mask, weights_before, weights = refs[:5]
    refs = refs[5:]
    if last:
        cot, weights_after = refs[:2]
        refs = refs[2:]
    x, mean, reduced, cross, probs, mixed, pay = refs
    receive_forward(
        pays, x_before, mean_before, weights_before, width, x, mean, reduced, cross
    )
    attend(x, mean[:, 0:1], weights, mask, probs, mixed)
    send_forward(x, weights, mixed, pay)
    if last:
        rows = x.shape[0]
        own = (weights.shape[2] - 16) // 2
        pay[2 * rows + HD :, :] = to_rank(cot[...], weights_after, own).astype(BF)


def layer_backward(
    dout, dred, x, mean, mask, weights, weights_before, probs, mixed, reduced, grads, carried, pay
):
    rows, local = x.shape
    size = block_size(rows)
    own = (weights.shape[2] - 16) // 2
    per_slice = own // HD
    rank = dred.shape[1]
    factor = lax.rsqrt(mean + EPS)
    first = dot_tn(dred, mixed[...]).astype(BF)
    for side in range(weights.shape[1]):
        grads[side, 0:rank, :] = first[:, side * own : (side + 1) * own]
    if reduced is not None:
        second = dot_tn(reduced, dout[...]).astype(BF)
        for side in range(weights.shape[1]):
            grads[side, rank : 2 * rank, :] = second[:, side * own : (side + 1) * own]
    back_mixed = [
        from_rank(dred, weights, 0, side).astype(BF) for side in range(weights.shape[1])
    ]
    gain_sums = [None] * (local // HD)
    for block in range(rows // size):
        span = slice(block * size, (block + 1) * size)
        scale = factor[span]
        norm_dot = jnp.zeros((size, HD), F32)
        for head in range(local // HD):
            part = slice(head * HD, (head + 1) * HD)
            side, inner = head // per_slice, (head % per_slice) * HD
            wide = x[span, part].astype(F32)
            gain = head_gain(weights, head)
            unit = wide * scale
            normed = (unit * gain).astype(BF)
            prob = probs[block, head]
            upstream = back_mixed[side][span, inner : inner + HD]
            back_prob = dot_nt(upstream, normed)
            prob_wide = prob.astype(F32)
            inner_sum = jnp.sum(back_prob * prob_wide, axis=1, keepdims=True)
            back_score = prob_wide * (back_prob - inner_sum) * (1.0 / HD)
            both = (back_score + back_score.T).astype(BF)
            back_normed = (dot_tn(prob, upstream) + dot(both, normed)).astype(BF).astype(F32)
            term = jnp.sum(back_normed * unit, axis=0, keepdims=True)
            gain_sums[head] = term if gain_sums[head] is None else gain_sums[head] + term
            if carried is not None:
                scaled = back_normed * gain
                norm_dot = norm_dot + scaled * wide
                carried[span, part] = (dout[span, part].astype(F32) + scaled * scale).astype(BF)
        if carried is not None:
            column = jnp.broadcast_to(jnp.sum(norm_dot, axis=1, keepdims=True), (size, size))
            line = column.T[0:1, :]
            high, low = two_parts(line)
            base = rows + 16 * block
            pay[base : base + 16, :] = jnp.concatenate(
                (high.astype(F32), low.astype(F32), jnp.zeros((14, size), F32)), axis=0
            ).astype(BF)
    zeros = jnp.zeros((15, HD), F32)
    for head in range(local // HD):
        side, inner = head // per_slice, (head % per_slice) * HD
        grads[side, 2 * rank : 2 * rank + 16, inner : inner + HD] = jnp.concatenate(
            (gain_sums[head], zeros), axis=0
        ).astype(BF)
    if carried is not None:
        pay[0:rows, :] = to_rank(carried[...], weights_before, own).astype(BF)


def turn_kernel(count, width, *refs):
    pays, refs = refs[:count], refs[count:]
    (x_before, mean_before, mask, weights_before, weights, cot) = refs[:6]
    (x, mean, reduced, cross, grads, carried, pay) = refs[6:13]
    probs, mixed = refs[13:]
    rows = x.shape[0]
    receive_forward(
        pays, x_before, mean_before, weights_before, width, x, mean, reduced, cross
    )
    attend(x, mean[:, 0:1], weights, mask, probs, mixed)
    dred = total_of(pays, 2 * rows + HD, 3 * rows + HD).astype(BF)
    layer_backward(
        cot, dred, x, mean[:, 0:1], mask, weights, weights_before, probs, mixed, None, grads,
        carried, pay,
    )
    pay[pay.shape[0] - rows :, :] = to_rank(mixed[...], weights, 0).astype(BF)


def back_kernel(count, after_turn, to_first, width, *refs):
    pays, refs = refs[:count], refs[count:]
    carried_after, x_after, mean_after, cross_after = refs[:4]
    x, mean, mask, weights = refs[4:8]
    refs = refs[8:]
    if not to_first:
        weights_before = refs[0]
        refs = refs[1:]
    else:
        weights_before = None
    probs, mixed, reduced = refs[:3]
    refs = refs[3:]
    if after_turn:
        cot, turn_grads = refs[:2]
        refs = refs[2:]
    else:
        refs = refs[1:]
    grads = refs[0]
    refs = refs[1:]
    if to_first:
        carried = pay = None
    else:
        carried, pay = refs[:2]
        refs = refs[2:]
    dout = refs[0]
    rows, local = x.shape
    size = block_size(rows)
    own = (weights.shape[2] - 16) // 2
    rank = reduced.shape[1]
    dred_parts = []
    for block in range(rows // size):
        span = slice(block * size, (block + 1) * size)
        base = rows + 16 * block
        lines = total_of(pays, base, base + 16)
        line = lines[0:1] + lines[1:2]
        column = jnp.broadcast_to(line, (size, size)).T
        factor = lax.rsqrt(mean_after[span, 0:1] + EPS)
        pull = column[:, 0:1] * (factor * factor * factor / width)
        dred_parts.append(
            (
                total_of(pays, block * size, (block + 1) * size) - cross_after[span, :] * pull
            ).astype(BF)
        )
        dout[span, :] = (
            carried_after[span, :].astype(F32) - x_after[span, :].astype(F32) * pull
        ).astype(BF)
    dred = dred_parts[0] if len(dred_parts) == 1 else jnp.concatenate(dred_parts, axis=0)
    if after_turn:
        last_reduced = total_of(pays, pays[0].shape[0] - rows, pays[0].shape[0]).astype(BF)
        second = dot_tn(last_reduced, cot[...]).astype(BF)
        for side in range(weights.shape[1]):
            grads[1, side, 0:rank, :] = turn_grads[side, 0:rank, :]
            grads[1, side, rank : 2 * rank, :] = second[:, side * own : (side + 1) * own]
            grads[1, side, 2 * rank :, :] = turn_grads[side, 2 * rank :, :]
    layer_backward(
        dout, dred, x, mean[:, 0:1], mask, weights, weights_before, probs, mixed, reduced[...],
        grads.at[0], carried, pay,
    )


def finish_kernel(parts, gain, first, second):
    rank = second.shape[1]
    total = parts[0].astype(F32)
    for index in range(1, parts.shape[0]):
        total = total + parts[index].astype(F32)
    first[0] = total[0:rank].T
    second[0] = total[rank : 2 * rank]
    gain[...] = total[2 * rank : 2 * rank + 1]


def per_device(tokens, cotangents, starts, counts, layer_gains, first_map, second_map):
    sections = lax.axis_size("pipe")
    groups = lax.axis_size("z")
    my_section = lax.axis_index("pipe")
    directions, micro_count, length, width = tokens.shape
    micro_total = directions * micro_count
    micro_local = -(-micro_total // sections)
    rows = groups * micro_local * length
    local = width // groups
    own = first_map.shape[1]
    rank = first_map.shape[2]
    heads = local // HD
    size = block_size(rows)
    blocks = rows // size
    sides = lax.axis_size("core")

    wanted = my_section * micro_local + jnp.arange(micro_local, dtype=jnp.int32)
    live = (wanted < micro_total).astype(jnp.int32)
    slots = jnp.minimum(wanted, micro_total - 1)
    payload, packed = pack(
        slots,
        live,
        starts.reshape(micro_total, -1),
        counts.reshape(micro_total),
        tokens.reshape(micro_total, length, width),
        cotangents.reshape(micro_total, length, width),
        layer_gains,
        first_map,
        second_map,
        groups,
    )
    received = lax.all_to_all(payload, "z", split_axis=0, concat_axis=0, tiled=True)
    received = received.reshape(rows, 2 * local + HD)
    weights = lax.all_gather(packed, ("pipe", "core"), axis=0, tiled=False)
    weights = weights.reshape(sections, sides, slice_rows(own), HD)

    def exchange(pay):
        pays = [pay]
        for shift in range(1, groups):
            pays.append(
                lax.ppermute(pay, "z", [(i, (i + shift) % groups) for i in range(groups)])
            )
        return pays

    def shaped(shape, kind=BF):
        return jax.ShapeDtypeStruct(shape, kind)

    wide_shape = shaped((rows, local))
    mean_shape = shaped((rows, HD), F32)
    rank_shape = shaped((rows, rank))
    cross_shape = shaped((rows, rank), F32)
    probs_shape = shaped((blocks, heads, size, size))
    grads_shape = (sides, 2 * rank + 16, own)
    forward_rows = 2 * rows + HD

    def call(kernel, operands, specs, outs, name, **more):
        return pl.pallas_call(
            kernel,
            grid=(1,),
            in_specs=specs,
            out_specs=more.pop("out_specs", None) or vmem_specs(len(outs)),
            out_shape=outs,
            compiler_params=PARAMS,
            name=name,
            **more,
        )(*operands)

    def layer_of(index):
        return layer_spec(weights.shape, index)

    x, cot, mask, mean, probs, mixed, pay = call(
        functools.partial(first_kernel, length),
        (received, weights),
        vmem_specs(1) + [layer_of(0)],
        [
            wide_shape,
            wide_shape,
            shaped((blocks, size, size)),
            mean_shape,
            probs_shape,
            wide_shape,
            shaped((forward_rows, HD)),
        ],
        "forward_first",
    )
    xs, means, reduceds, crosses = [x], [mean], [], [None]
    all_probs, all_mixed = [probs], [mixed]
    for layer in range(1, sections - 1):
        pays = exchange(pay)
        last = layer == sections - 2
        operands = (*pays, xs[-1], means[-1], mask, weights, weights)
        specs = vmem_specs(len(pays) + 3) + [layer_of(layer - 1), layer_of(layer)]
        if last:
            operands += (cot, weights)
            specs += vmem_specs(1) + [layer_of(layer + 1)]
        x, mean, reduced, cross, probs, mixed, pay = call(
            functools.partial(middle_kernel, len(pays), last, float(width)),
            operands,
            specs,
            [
                wide_shape,
                mean_shape,
                rank_shape,
                cross_shape,
                probs_shape,
                wide_shape,
                shaped((forward_rows + (rows if last else 0), HD)),
            ],
            "forward_middle",
        )
        xs.append(x)
        means.append(mean)
        reduceds.append(reduced)
        crosses.append(cross)
        all_probs.append(probs)
        all_mixed.append(mixed)

    pays = exchange(pay)
    top = sections - 1
    back_rows = rows + 16 * blocks
    x, mean, reduced, cross, turn_grads, carried, pay = call(
        functools.partial(turn_kernel, len(pays), float(width)),
        (*pays, xs[-1], means[-1], mask, weights, weights, cot),
        vmem_specs(len(pays) + 3) + [layer_of(top - 1), layer_of(top)] + vmem_specs(1),
        [
            wide_shape,
            mean_shape,
            rank_shape,
            cross_shape,
            shaped(grads_shape),
            wide_shape,
            shaped((back_rows + rows, HD)),
        ],
        "turn",
        scratch_shapes=[
            pltpu.VMEM(probs_shape.shape, BF),
            pltpu.VMEM(wide_shape.shape, BF),
        ],
    )
    xs.append(x)
    means.append(mean)
    reduceds.append(reduced)
    crosses.append(cross)

    grads = None
    for layer in range(top - 1, -1, -1):
        pays = exchange(pay)
        after_turn = layer == top - 1
        to_first = layer == 0
        operands = (
            *pays, carried, xs[layer + 1], means[layer + 1], crosses[layer + 1],
            xs[layer], means[layer], mask, weights,
        )
        specs = vmem_specs(len(pays) + 7) + [layer_of(layer)]
        if not to_first:
            operands += (weights,)
            specs += [layer_of(layer - 1)]
        operands += (all_probs[layer], all_mixed[layer], reduceds[layer])
        specs += vmem_specs(3)
        more = {}
        if after_turn:
            operands += (cot, turn_grads)
            specs += vmem_specs(2)
            block = (2,) + grads_shape
            place = layer // 2
        else:
            operands += (grads,)
            specs += [pl.BlockSpec(memory_space=pl.ANY)]
            more["input_output_aliases"] = {len(operands) - 1: 0}
            block = (1,) + grads_shape
            place = layer
        outs = [shaped((sections,) + grads_shape)]
        out_specs = [pl.BlockSpec(block, lambda *_, place=place: (place, 0, 0, 0))]
        if not to_first:
            outs += [wide_shape, shaped((back_rows, HD))]
            out_specs += vmem_specs(2)
        result = call(
            functools.partial(back_kernel, len(pays), after_turn, to_first, float(width)),
            operands,
            specs,
            outs,
            "backward",
            out_specs=out_specs,
            scratch_shapes=[pltpu.VMEM(wide_shape.shape, BF)],
            **more,
        )
        grads = result[0]
        if not to_first:
            carried, pay = result[1:]

    parts = lax.all_to_all(
        grads.reshape((sections * sides,) + grads_shape[1:]),
        ("pipe", "core"),
        split_axis=0,
        concat_axis=0,
        tiled=True,
    )
    gain_grad, first_grad, second_grad = call(
        finish_kernel,
        (parts,),
        vmem_specs(1),
        [
            shaped((1, own), F32),
            shaped((1, own, rank), F32),
            shaped((1, rank, own), F32),
        ],
        "finish",
    )
    return (gain_grad, first_grad, second_grad)


def solution(mesh):
    fine = Mesh(
        mesh.devices.reshape(mesh.shape["pipe"], mesh.shape["dp"] // 2, 2), ("pipe", "z", "core")
    )
    data = ("z", "core")
    in_specs = (
        P(None, data, None, None),
        P(None, data, None, None),
        P(None, data, None),
        P(None, data),
        P("pipe", data),
        P("pipe", data, None),
        P("pipe", None, data),
    )
    out_specs = (P("pipe", data), P("pipe", data, None), P("pipe", None, data))
    mapped = jax.shard_map(
        per_device, mesh=fine, in_specs=in_specs, out_specs=out_specs, check_vma=False
    )

    return mapped
```

time: 520 us -> 165 us (0.32)
  matrix products: 168 us -> 0 us
  waiting for transfers between devices: 141 us -> 47.4 us
  starting transfers between devices: 92.2 us -> 22.4 us
  other arithmetic: 64.2 us -> 0 us
  blocking collectives: 27.2 us -> 51.9 us
  Pallas kernels: 0 us -> 19.6 us
    dot_general x130 -> x0, matrix products: 168 us -> none  [the longest x30 66.9 us: apply_layer(): jnp.dot(reduced, second_weight, preferred_element_type=jnp.float32)]
    ppermute x32 -> x18, starting transfers between devices: 92 us -> 22.4 us  [exchange(): lax.ppermute(pay, 'z', [(i, (i + shift) % groups) for i in range(groups)])]
    ppermute x32 -> x18, waiting for transfers between devices: 91 us -> 37.8 us  [exchange(): lax.ppermute(pay, 'z', [(i, (i + shift) % groups) for i in range(groups)])]
    all_to_all x0 -> x2, blocking collectives: none -> 51.9 us  [the longest x1 30.6 us: per_device(): lax.all_to_all(grads.reshape((sections * sides,) + grads_shape[1:]), ('pi...]
    reduce_scatter x2 -> x0, waiting for transfers between devices: 21.4 us -> none  [the longest x1 21.4 us: per_device(): lax.psum_scatter(pair_sums[1].astype(jnp.bfloat16), 'dp', scatter_dimensi...]
    pallas_call x0 -> x9, Pallas kernels: none -> 19.6 us  [the longest x8 18.1 us: call(): pl.pallas_call(kernel, grid=(1,), in_specs=specs, out_specs=more.pop('out...]
    all_gather x2 -> x1, waiting for transfers between devices: 28.4 us -> 9.59 us  [per_device(): weights = lax.all_gather(packed, ('pipe', 'core'), axis=0, tiled=False)]
    scatter x10 -> x0, other arithmetic: 17.8 us -> none  [the longest x5 9.04 us: forward_tick(): stashed.at[1, up_slot]]
  transfers between devices with their start and end apart: 36 -> 19, of which waited for: 18 -> 15; matrix products, arithmetic and copies ran while one was open for 25% -> 0% of each run, Pallas kernels for 0% -> 0%
where the time goes in v1:
time: 165 us
  blocking collectives  51.9 us (31%)
  waiting for transfers between devices  47.4 us (29%)
  starting transfers between devices  22.4 us (14%)
  Pallas kernels  19.6 us (12%)
  between operations  14.1 us (9%)
  local copies, waits for them, and re-layouts  9.61 us (6%)
    ppermute x18, waiting for transfers between devices, exchange(): lax.ppermute(pay, 'z', [(i, (i + shift) % groups) for i in range(groups)])  37.8 us
    all_to_all x1, blocking collectives, per_device(): lax.all_to_all(grads.reshape((sections * sides,) + grads_shape[1:]), ('pi...  30.6 us
    ppermute x18, starting transfers between devices, exchange(): lax.ppermute(pay, 'z', [(i, (i + shift) % groups) for i in range(groups)])  22.4 us
    all_to_all x1, blocking collectives, per_device(): lax.all_to_all(payload, 'z', split_axis=0, concat_axis=0, tiled=True)  21.3 us
    pallas_call x8, Pallas kernels, call(): pl.pallas_call(kernel, grid=(1,), in_specs=specs, out_specs=more.pop('out...  18.1 us
    all_gather x1, waiting for transfers between devices, per_device(): weights = lax.all_gather(packed, ('pipe', 'core'), axis=0, tiled=False)  9.59 us
    unnamed x18, local copies, waits for them, and re-layouts  8.85 us
  transfers between devices with their start and end apart: 19, of which 15 were waited for; matrix products, arithmetic and copies ran while one was open for 0% of the time, Pallas kernels for 0%

profile of v1, /device:TPU:0, one launch (start us, length us, event | category | flops | bytes accessed | tf_op | source)
XLA Modules:
  0.0 165.0 jit_solution(18174259894300030699)
XLA Ops:
  13.6 1.5 pack.1
  15.1 21.3 %all_to_all.10 = bf16[4,32,2176]{2,1,0:T(8,128)(2,1)S(1)} all-to-all(bf16[4,32,2176]{2,1,0:T(8,128)(2,1)S(1)} %get-tuple-element.39), channel_id=1, replica_groups=mesh['pipe'=4,'z'=4,'core'=2] {'z'}, dimensions={0} | all-to-all | bytes 1114112 | tf_op jit(solution)/shard_map/all_to_all | solution.py:431
  36.4 9.6 %all-gather.3.cloned.1.call-done = bf16[8320,128]{1,0:T(8,128)(2,1)} async-done(((bf16[1040,128]{1,0:T(8,128)(2,1)}), bf16[8320,128]{1,0:T(8,128)(2,1)}) %all-gather.3.cloned.1.call-update) | async-done | bytes 2129936 | tf_op jit(solution)/shard_map/all_gather | solution.py:433
  46.0 1.6 copy-done
  47.6 2.6 %forward_first.1 = (bf16[128,1024]{1,0:T(8,128)(2,1)S(1)}, bf16[128,1024]{1,0:T(8,128)(2,1)S(1)}, bf16[1,128,128]{2,1,0:T(8,128)(2,1)S(1)}, f32[128,128]{1,0:T(8...) custom-call(bf16[128,2176]{1,0:T(8,128)(2,1)S(1)} %bitcast.22, ...), custom_call_target="tpu_custom_call" | custom-call | tf_op jit(solution)/shard_map/forward_first/pallas_call | solution.py:456
  50.2 3.4 %collective-permute-start.2 = (bf16[384,128]{1,0:T(8,128)(2,1)S(1)}, bf16[384,128]{1,0:T(8,128)(2,1)S(1)}, u32[]{:S(2)}, u32[]{:S(2)}) collective-permute-start(bf16[384,128]{1,0:T(8,128)(2,1)S(1)} %get-tuple-element.41.refs_0_), channel_id=1, source_target_pairs={{0,6},{2,0},{4,2},{6,4},{1,7},{3,1},{5,3},{7,5},{8,14},{10,8},{12,... | collective-permute-start | bytes 294920 | tf_op jit(solution)/shard_map/ppermute | solution.py:440
  54.7 2.1 %collective-permute-done.2.refs_3_ = bf16[384,128]{1,0:T(8,128)(2,1)S(1)} collective-permute-done((bf16[384,128]{1,0:T(8,128)(2,1)S(1)}, bf16[384,128]{1,0:T(8,128)(2,1)S(1)}, u32[]{:S(2)}, u32[]{:S(2)}) %collective-permute-start.2) | collective-permute-done | bytes 98336 | tf_op jit(solution)/shard_map/ppermute | solution.py:440
  56.8 6.3 %collective-permute-done.1.refs_2_ = bf16[384,128]{1,0:T(8,128)(2,1)S(1)} collective-permute-done((bf16[384,128]{1,0:T(8,128)(2,1)S(1)}, bf16[384,128]{1,0:T(8,128)(2,1)S(1)}, u32[]{:S(2)}, u32[]{:S(2)}) %collective-permute-start.1) | collective-permute-done | bytes 98336 | tf_op jit(solution)/shard_map/ppermute | solution.py:440
  63.1 2.4 %forward_middle.2 = (bf16[128,1024]{1,0:T(8,128)(2,1)S(1)}, f32[128,128]{1,0:T(8,128)S(1)}, bf16[128,128]{1,0:T(8,128)(2,1)S(1)}, f32[128,128]{1,0:T(8,128)S(1)}...) custom-call(bf16[384,128]{1,0:T(8,128)(2,1)S(1)} %get-tuple-element.41.refs_0_, ...), custom_call_target="tpu_custom_call" | custom-call | tf_op jit(solution)/shard_map/forward_middle/pallas_call | solution.py:456
  65.5 1.7 %collective-permute-start.5 = (bf16[384,128]{1,0:T(8,128)(2,1)S(1)}, bf16[384,128]{1,0:T(8,128)(2,1)S(1)}, u32[]{:S(2)}, u32[]{:S(2)}) collective-permute-start(bf16[384,128]{1,0:T(8,128)(2,1)S(1)} %get-tuple-element.45.refs_0_), channel_id=1, source_target_pairs={{0,6},{2,0},{4,2},{6,4},{1,7},{3,1},{5,3},{7,5},{8,14},{10,8},{12,... | collective-permute-start | bytes 294920 | tf_op jit(solution)/shard_map/ppermute | solution.py:440
  67.7 1.9 %collective-permute-start.3 = (bf16[384,128]{1,0:T(8,128)(2,1)S(1)}, bf16[384,128]{1,0:T(8,128)(2,1)S(1)}, u32[]{:S(2)}, u32[]{:S(2)}) collective-permute-start(bf16[384,128]{1,0:T(8,128)(2,1)S(1)} %get-tuple-element.45.refs_0_), channel_id=1, source_target_pairs={{0,2},{2,4},{4,6},{6,0},{1,3},{3,5},{5,7},{7,1},{8,10},{10,12},{12... | collective-permute-start | bytes 294920 | tf_op jit(solution)/shard_map/ppermute | solution.py:440
  70.7 5.7 %collective-permute-done.4.refs_2_ = bf16[384,128]{1,0:T(8,128)(2,1)S(1)} collective-permute-done((bf16[384,128]{1,0:T(8,128)(2,1)S(1)}, bf16[384,128]{1,0:T(8,128)(2,1)S(1)}, u32[]{:S(2)}, u32[]{:S(2)}) %collective-permute-start.4) | collective-permute-done | bytes 98336 | tf_op jit(solution)/shard_map/ppermute | solution.py:440
  76.4 2.5 %forward_middle.3 = (bf16[128,1024]{1,0:T(8,128)(2,1)S(1)}, f32[128,128]{1,0:T(8,128)S(1)}, bf16[128,128]{1,0:T(8,128)(2,1)S(1)}, f32[128,128]{1,0:T(8,128)S(1)}...) custom-call(bf16[384,128]{1,0:T(8,128)(2,1)S(1)} %get-tuple-element.45.refs_0_, ...), custom_call_target="tpu_custom_call" | custom-call | tf_op jit(solution)/shard_map/forward_middle/pallas_call | solution.py:456
  80.6 1.9 %collective-permute-start.6 = (bf16[512,128]{1,0:T(8,128)(2,1)S(1)}, bf16[512,128]{1,0:T(8,128)(2,1)S(1)}, u32[]{:S(2)}, u32[]{:S(2)}) collective-permute-start(bf16[512,128]{1,0:T(8,128)(2,1)S(1)} %get-tuple-element.49.refs_0_), channel_id=1, source_target_pairs={{0,2},{2,4},{4,6},{6,0},{1,3},{3,5},{5,7},{7,1},{8,10},{10,12},{12... | collective-permute-start | bytes 393224 | tf_op jit(solution)/shard_map/ppermute | solution.py:440
  82.5 1.9 %collective-permute-done.8.refs_3_ = bf16[512,128]{1,0:T(8,128)(2,1)S(1)} collective-permute-done((bf16[512,128]{1,0:T(8,128)(2,1)S(1)}, bf16[512,128]{1,0:T(8,128)(2,1)S(1)}, u32[]{:S(2)}, u32[]{:S(2)}) %collective-permute-start.8) | collective-permute-done | bytes 131104 | tf_op jit(solution)/shard_map/ppermute | solution.py:440
  84.4 7.9 %collective-permute-done.7.refs_2_ = bf16[512,128]{1,0:T(8,128)(2,1)S(1)} collective-permute-done((bf16[512,128]{1,0:T(8,128)(2,1)S(1)}, bf16[512,128]{1,0:T(8,128)(2,1)S(1)}, u32[]{:S(2)}, u32[]{:S(2)}) %collective-permute-start.7) | collective-permute-done | bytes 131104 | tf_op jit(solution)/shard_map/ppermute | solution.py:440
  92.3 3.3 %turn.1 = (bf16[128,1024]{1,0:T(8,128)(2,1)S(1)}, f32[128,128]{1,0:T(8,128)S(1)}, bf16[128,128]{1,0:T(8,128)(2,1)S(1)}, f32[128,128]{1,0:T(8,128)S(1)}, bf16[2,2...) custom-call(bf16[512,128]{1,0:T(8,128)(2,1)S(1)} %get-tuple-element.49.refs_0_, ...), custom_call_target="tpu_custom_call" | custom-call | tf_op jit(solution)/shard_map/turn/pallas_call | solution.py:456
  95.8 1.5 collective-permute-start.10
  97.2 1.9 %collective-permute-start.9 = (bf16[272,128]{1,0:T(8,128)(2,1)S(1)}, bf16[272,128]{1,0:T(8,128)(2,1)S(1)}, u32[]{:S(2)}, u32[]{:S(2)}) collective-permute-start(bf16[272,128]{1,0:T(8,128)(2,1)S(1)} %get-tuple-element.52.refs_0_), channel_id=1, source_target_pairs={{0,2},{2,4},{4,6},{6,0},{1,3},{3,5},{5,7},{7,1},{8,10},{10,12},{12... | collective-permute-start | bytes 208904 | tf_op jit(solution)/shard_map/ppermute | solution.py:440
  99.2 1.3 collective-permute-done.11.refs_3_
  100.4 3.6 %collective-permute-done.10.refs_2_ = bf16[272,128]{1,0:T(8,128)(2,1)S(1)} collective-permute-done((bf16[272,128]{1,0:T(8,128)(2,1)S(1)}, bf16[272,128]{1,0:T(8,128)(2,1)S(1)}, u32[]{:S(2)}, u32[]{:S(2)}) %collective-permute-start.10) | collective-permute-done | bytes 69664 | tf_op jit(solution)/shard_map/ppermute | solution.py:440
  104.0 2.6 %backward.3 = (bf16[4,2,272,512]{3,2,1,0:T(8,128)(2,1)}, bf16[128,1024]{1,0:T(8,128)(2,1)S(1)}, bf16[144,128]{1,0:T(8,128)(2,1)S(1)}) custom-call(bf16[272,128]{1,0:T(8,128)(2,1)S(1)} %get-tuple-element.52.refs_0_, bf16[272,128]{1,0:T(8,128)(2,1)S(1)} %collective-permute-done.9.refs_1_, bf16[272,128]{1,0:T(8,128)(2,1)S(1)} %collective-permute-done.10.refs_2_, ...), custom_call_target="tpu_custom_call" | custom-call | tf_op jit(solution)/shard_map/backward/pallas_call | solution.py:456
  106.6 1.5 collective-permute-start.14
  108.1 1.9 %collective-permute-start.12 = (bf16[144,128]{1,0:T(8,128)(2,1)S(1)}, bf16[144,128]{1,0:T(8,128)(2,1)S(1)}, u32[]{:S(2)}, u32[]{:S(2)}) collective-permute-start(bf16[144,128]{1,0:T(8,128)(2,1)S(1)} %get-tuple-element.61.refs_0_), channel_id=1, source_target_pairs={{0,2},{2,4},{4,6},{6,0},{1,3},{3,5},{5,7},{7,1},{8,10},{10,12},{12... | collective-permute-start | bytes 110600 | tf_op jit(solution)/shard_map/ppermute | solution.py:440
  110.6 2.8 %collective-permute-done.13.refs_2_ = bf16[144,128]{1,0:T(8,128)(2,1)S(1)} collective-permute-done((bf16[144,128]{1,0:T(8,128)(2,1)S(1)}, bf16[144,128]{1,0:T(8,128)(2,1)S(1)}, u32[]{:S(2)}, u32[]{:S(2)}) %collective-permute-start.13) | collective-permute-done | bytes 36896 | tf_op jit(solution)/shard_map/ppermute | solution.py:440
  113.9 2.3 %backward.4 = (bf16[4,2,272,512]{3,2,1,0:T(8,128)(2,1)}, bf16[128,1024]{1,0:T(8,128)(2,1)S(1)}, bf16[144,128]{1,0:T(8,128)(2,1)S(1)}) custom-call(bf16[144,128]{1,0:T(8,128)(2,1)S(1)} %get-tuple-element.61.refs_0_, bf16[144,128]{1,0:T(8,128)(2,1)S(1)} %collective-permute-done.12.refs_1_, ...), custom_call_target="tpu_custom_call", output_to_operand_aliasing={{0}: (16, {})} | custom-call | tf_op jit(solution)/shard_map/backward/pallas_call | solution.py:456
  116.2 1.2 collective-permute-start.17
  117.8 1.6 collective-permute-start.15
  120.2 2.5 %collective-permute-done.16.refs_2_ = bf16[144,128]{1,0:T(8,128)(2,1)S(1)} collective-permute-done((bf16[144,128]{1,0:T(8,128)(2,1)S(1)}, bf16[144,128]{1,0:T(8,128)(2,1)S(1)}, u32[]{:S(2)}, u32[]{:S(2)}) %collective-permute-start.16) | collective-permute-done | bytes 36896 | tf_op jit(solution)/shard_map/ppermute | solution.py:440
  123.6 1.6 copy-done.2
  125.2 1.4 backward.5
  126.6 30.6 %all_to_all.11.parts = bf16[8,272,512]{2,1,0:T(8,128)(2,1)S(1)} all-to-all(bf16[8,272,512]{2,1,0:T(8,128)(2,1)S(1)} %bitcast.21), channel_id=1, replica_groups=mesh['pipe'=4,'z'=4,'core'=2] {'pipe','core'}, dimensions={0} | all-to-all | bytes 4456448 | tf_op jit(solution)/shard_map/all_to_all | solution.py:590
  (37 shorter events, 15.0 us)
Async XLA Ops:
  7.2 38.8 %all-gather.3.cloned.1.call-start = ((), (), s32[]{:S(2)}) async-start(), calls=%async_computation.2 | async-start | bytes 2396160 | tf_op jit(solution)/shard_map/all_gather | solution.py:433
  8.0 1.2 copy-start.3
  9.2 1.2 copy-start.4
  10.4 0.9 copy-start.5
  11.3 0.9 copy-start.6
  12.2 0.7 copy-start.7
  12.9 0.7 copy-start.8
  46.0 1.6 copy-start
  47.6 15.5 %copy-start.1 = (bf16[8320,128]{1,0:T(8,128)(2,1)S(1)}, bf16[8320,128]{1,0:T(8,128)(2,1)}, u32[]{:S(2)}) copy-start(bf16[8320,128]{1,0:T(8,128)(2,1)} %all-gather.3.cloned.1.call-done) | copy-start | bytes 6389764
  50.2 6.6 %collective-permute-start.2 = (bf16[384,128]{1,0:T(8,128)(2,1)S(1)}, bf16[384,128]{1,0:T(8,128)(2,1)S(1)}, u32[]{:S(2)}, u32[]{:S(2)}) collective-permute-start(bf16[384,128]{1,0:T(8,128)(2,1)S(1)} %get-tuple-element.41.refs_0_), channel_id=1, source_target_pairs={{0,6},{2,0},{4,2},{6,4},{1,7},{3,1},{5,3},{7,5},{8,14},{10,8},{12,... | collective-permute-start | bytes 294920 | tf_op jit(solution)/shard_map/ppermute | solution.py:440
  53.6 9.5 %collective-permute-start.1 = (bf16[384,128]{1,0:T(8,128)(2,1)S(1)}, bf16[384,128]{1,0:T(8,128)(2,1)S(1)}, u32[]{:S(2)}, u32[]{:S(2)}) collective-permute-start(bf16[384,128]{1,0:T(8,128)(2,1)S(1)} %get-tuple-element.41.refs_0_), channel_id=1, source_target_pairs={{0,4},{2,6},{4,0},{6,2},{1,5},{3,7},{5,1},{7,3},{8,12},{10,14},{12... | collective-permute-start | bytes 294920 | tf_op jit(solution)/shard_map/ppermute | solution.py:440
  53.6 9.5 %collective-permute-start = (bf16[384,128]{1,0:T(8,128)(2,1)S(1)}, bf16[384,128]{1,0:T(8,128)(2,1)S(1)}, u32[]{:S(2)}, u32[]{:S(2)}) collective-permute-start(bf16[384,128]{1,0:T(8,128)(2,1)S(1)} %get-tuple-element.41.refs_0_), channel_id=1, source_target_pairs={{0,2},{2,4},{4,6},{6,0},{1,3},{3,5},{5,7},{7,1},{8,10},{10,12},{12... | collective-permute-start | bytes 294920 | tf_op jit(solution)/shard_map/ppermute | solution.py:440
  65.5 5.2 %collective-permute-start.5 = (bf16[384,128]{1,0:T(8,128)(2,1)S(1)}, bf16[384,128]{1,0:T(8,128)(2,1)S(1)}, u32[]{:S(2)}, u32[]{:S(2)}) collective-permute-start(bf16[384,128]{1,0:T(8,128)(2,1)S(1)} %get-tuple-element.45.refs_0_), channel_id=1, source_target_pairs={{0,6},{2,0},{4,2},{6,4},{1,7},{3,1},{5,3},{7,5},{8,14},{10,8},{12,... | collective-permute-start | bytes 294920 | tf_op jit(solution)/shard_map/ppermute | solution.py:440
  67.1 9.2 %collective-permute-start.4 = (bf16[384,128]{1,0:T(8,128)(2,1)S(1)}, bf16[384,128]{1,0:T(8,128)(2,1)S(1)}, u32[]{:S(2)}, u32[]{:S(2)}) collective-permute-start(bf16[384,128]{1,0:T(8,128)(2,1)S(1)} %get-tuple-element.45.refs_0_), channel_id=1, source_target_pairs={{0,4},{2,6},{4,0},{6,2},{1,5},{3,7},{5,1},{7,3},{8,12},{10,14},{12... | collective-permute-start | bytes 294920 | tf_op jit(solution)/shard_map/ppermute | solution.py:440
  67.7 8.7 %collective-permute-start.3 = (bf16[384,128]{1,0:T(8,128)(2,1)S(1)}, bf16[384,128]{1,0:T(8,128)(2,1)S(1)}, u32[]{:S(2)}, u32[]{:S(2)}) collective-permute-start(bf16[384,128]{1,0:T(8,128)(2,1)S(1)} %get-tuple-element.45.refs_0_), channel_id=1, source_target_pairs={{0,2},{2,4},{4,6},{6,0},{1,3},{3,5},{5,7},{7,1},{8,10},{10,12},{12... | collective-permute-start | bytes 294920 | tf_op jit(solution)/shard_map/ppermute | solution.py:440
  78.8 5.6 %collective-permute-start.8 = (bf16[512,128]{1,0:T(8,128)(2,1)S(1)}, bf16[512,128]{1,0:T(8,128)(2,1)S(1)}, u32[]{:S(2)}, u32[]{:S(2)}) collective-permute-start(bf16[512,128]{1,0:T(8,128)(2,1)S(1)} %get-tuple-element.49.refs_0_), channel_id=1, source_target_pairs={{0,6},{2,0},{4,2},{6,4},{1,7},{3,1},{5,3},{7,5},{8,14},{10,8},{12,... | collective-permute-start | bytes 393224 | tf_op jit(solution)/shard_map/ppermute | solution.py:440
  79.6 12.7 %collective-permute-start.7 = (bf16[512,128]{1,0:T(8,128)(2,1)S(1)}, bf16[512,128]{1,0:T(8,128)(2,1)S(1)}, u32[]{:S(2)}, u32[]{:S(2)}) collective-permute-start(bf16[512,128]{1,0:T(8,128)(2,1)S(1)} %get-tuple-element.49.refs_0_), channel_id=1, source_target_pairs={{0,4},{2,6},{4,0},{6,2},{1,5},{3,7},{5,1},{7,3},{8,12},{10,14},{12... | collective-permute-start | bytes 393224 | tf_op jit(solution)/shard_map/ppermute | solution.py:440
  80.6 11.8 %collective-permute-start.6 = (bf16[512,128]{1,0:T(8,128)(2,1)S(1)}, bf16[512,128]{1,0:T(8,128)(2,1)S(1)}, u32[]{:S(2)}, u32[]{:S(2)}) collective-permute-start(bf16[512,128]{1,0:T(8,128)(2,1)S(1)} %get-tuple-element.49.refs_0_), channel_id=1, source_target_pairs={{0,2},{2,4},{4,6},{6,0},{1,3},{3,5},{5,7},{7,1},{8,10},{10,12},{12... | collective-permute-start | bytes 393224 | tf_op jit(solution)/shard_map/ppermute | solution.py:440
  95.7 4.8 %collective-permute-start.11 = (bf16[272,128]{1,0:T(8,128)(2,1)S(1)}, bf16[272,128]{1,0:T(8,128)(2,1)S(1)}, u32[]{:S(2)}, u32[]{:S(2)}) collective-permute-start(bf16[272,128]{1,0:T(8,128)(2,1)S(1)} %get-tuple-element.52.refs_0_), channel_id=1, source_target_pairs={{0,6},{2,0},{4,2},{6,4},{1,7},{3,1},{5,3},{7,5},{8,14},{10,8},{12,... | collective-permute-start | bytes 208904 | tf_op jit(solution)/shard_map/ppermute | solution.py:440
  95.8 8.3 %collective-permute-start.10 = (bf16[272,128]{1,0:T(8,128)(2,1)S(1)}, bf16[272,128]{1,0:T(8,128)(2,1)S(1)}, u32[]{:S(2)}, u32[]{:S(2)}) collective-permute-start(bf16[272,128]{1,0:T(8,128)(2,1)S(1)} %get-tuple-element.52.refs_0_), channel_id=1, source_target_pairs={{0,4},{2,6},{4,0},{6,2},{1,5},{3,7},{5,1},{7,3},{8,12},{10,14},{12... | collective-permute-start | bytes 208904 | tf_op jit(solution)/shard_map/ppermute | solution.py:440
  97.2 6.8 %collective-permute-start.9 = (bf16[272,128]{1,0:T(8,128)(2,1)S(1)}, bf16[272,128]{1,0:T(8,128)(2,1)S(1)}, u32[]{:S(2)}, u32[]{:S(2)}) collective-permute-start(bf16[272,128]{1,0:T(8,128)(2,1)S(1)} %get-tuple-element.52.refs_0_), channel_id=1, source_target_pairs={{0,2},{2,4},{4,6},{6,0},{1,3},{3,5},{5,7},{7,1},{8,10},{10,12},{12... | collective-permute-start | bytes 208904 | tf_op jit(solution)/shard_map/ppermute | solution.py:440
  106.6 4.0 %collective-permute-start.14 = (bf16[144,128]{1,0:T(8,128)(2,1)S(1)}, bf16[144,128]{1,0:T(8,128)(2,1)S(1)}, u32[]{:S(2)}, u32[]{:S(2)}) collective-permute-start(bf16[144,128]{1,0:T(8,128)(2,1)S(1)} %get-tuple-element.61.refs_0_), channel_id=1, source_target_pairs={{0,6},{2,0},{4,2},{6,4},{1,7},{3,1},{5,3},{7,5},{8,14},{10,8},{12,... | collective-permute-start | bytes 110600 | tf_op jit(solution)/shard_map/ppermute | solution.py:440
  108.1 5.2 %collective-permute-start.13 = (bf16[144,128]{1,0:T(8,128)(2,1)S(1)}, bf16[144,128]{1,0:T(8,128)(2,1)S(1)}, u32[]{:S(2)}, u32[]{:S(2)}) collective-permute-start(bf16[144,128]{1,0:T(8,128)(2,1)S(1)} %get-tuple-element.61.refs_0_), channel_id=1, source_target_pairs={{0,4},{2,6},{4,0},{6,2},{1,5},{3,7},{5,1},{7,3},{8,12},{10,14},{12... | collective-permute-start | bytes 110600 | tf_op jit(solution)/shard_map/ppermute | solution.py:440
  108.1 5.8 %collective-permute-start.12 = (bf16[144,128]{1,0:T(8,128)(2,1)S(1)}, bf16[144,128]{1,0:T(8,128)(2,1)S(1)}, u32[]{:S(2)}, u32[]{:S(2)}) collective-permute-start(bf16[144,128]{1,0:T(8,128)(2,1)S(1)} %get-tuple-element.61.refs_0_), channel_id=1, source_target_pairs={{0,2},{2,4},{4,6},{6,0},{1,3},{3,5},{5,7},{7,1},{8,10},{10,12},{12... | collective-permute-start | bytes 110600 | tf_op jit(solution)/shard_map/ppermute | solution.py:440
  116.2 4.0 %collective-permute-start.17 = (bf16[144,128]{1,0:T(8,128)(2,1)S(1)}, bf16[144,128]{1,0:T(8,128)(2,1)S(1)}, u32[]{:S(2)}, u32[]{:S(2)}) collective-permute-start(bf16[144,128]{1,0:T(8,128)(2,1)S(1)} %get-tuple-element.68.refs_0_), channel_id=1, source_target_pairs={{0,6},{2,0},{4,2},{6,4},{1,7},{3,1},{5,3},{7,5},{8,14},{10,8},{12,... | collective-permute-start | bytes 110600 | tf_op jit(solution)/shard_map/ppermute | solution.py:440
  117.5 5.3 %collective-permute-start.16 = (bf16[144,128]{1,0:T(8,128)(2,1)S(1)}, bf16[144,128]{1,0:T(8,128)(2,1)S(1)}, u32[]{:S(2)}, u32[]{:S(2)}) collective-permute-start(bf16[144,128]{1,0:T(8,128)(2,1)S(1)} %get-tuple-element.68.refs_0_), channel_id=1, source_target_pairs={{0,4},{2,6},{4,0},{6,2},{1,5},{3,7},{5,1},{7,3},{8,12},{10,14},{12... | collective-permute-start | bytes 110600 | tf_op jit(solution)/shard_map/ppermute | solution.py:440
  117.8 5.8 %collective-permute-start.15 = (bf16[144,128]{1,0:T(8,128)(2,1)S(1)}, bf16[144,128]{1,0:T(8,128)(2,1)S(1)}, u32[]{:S(2)}, u32[]{:S(2)}) collective-permute-start(bf16[144,128]{1,0:T(8,128)(2,1)S(1)} %get-tuple-element.68.refs_0_), channel_id=1, source_target_pairs={{0,2},{2,4},{4,6},{6,0},{1,3},{3,5},{5,7},{7,1},{8,10},{10,12},{12... | collective-permute-start | bytes 110600 | tf_op jit(solution)/shard_map/ppermute | solution.py:440
  123.6 1.6 copy-start.2
Sparse Core Ops, SparseCore 0:
  15.2 30.7 all-gather.2

commit v2 on v1

--- a/solution.py
+++ b/solution.py
@@ -43,79 +43,99 @@
     return 2 * own + 16
 
 
-def pack_kernel(slots, live, starts, counts, tok, cot, gain, first, second, pay, weights):
-    micro = pl.program_id(0)
-    groups, length, width = pay.shape[0], tok.shape[1], tok.shape[2]
+def pack_kernel(groups, micro_local, *refs):
+    tokens, cotangents, starts, counts, gain, first, second = refs[:7]
+    token_parts, cot_parts = refs[7 : 7 + groups], refs[7 + groups : 7 + 2 * groups]
+    weights = refs[7 + 2 * groups]
+    tok, cot, starts_in, counts_in, gain_in, second_in, sems = refs[8 + 2 * groups :]
+    directions, micro_count, length, width = tokens.shape
     local = width // groups
     own = first.shape[1]
-    slot = slots[micro]
-    widened = tok[0].astype(F32)
-    mean = jnp.mean(widened * widened, axis=1, keepdims=True)
-    mean_high, mean_low = two_parts(mean)
-    position = lax.broadcasted_iota(jnp.int32, (length, HD), 0)
-    document = jnp.zeros((length, HD), jnp.int32)
-    for entry in range(starts.shape[1]):
-        started = (starts[slot, entry] <= position) & (entry < counts[slot])
-        document = document + started.astype(jnp.int32)
-    lane = lax.broadcasted_iota(jnp.int32, (length, HD), 1)
-    tail = jnp.where(
-        lane == 0,
-        document.astype(F32),
-        jnp.where(lane == 1, mean_high.astype(F32), mean_low.astype(F32)),
-    ).astype(BF)
-    keep = live[micro] > 0
-    for group in range(groups):
-        part = slice(group * local, (group + 1) * local)
-        pay[group, :, 0:local] = tok[0, :, part]
-        cotangent = cot[0, :, part]
-        pay[group, :, local : 2 * local] = jnp.where(keep, cotangent, jnp.zeros_like(cotangent))
-        pay[group, :, 2 * local :] = tail
-
-    @pl.when(micro == 0)
-    def _():
-        weights[0:own, :] = first[0]
-        weights[own : 2 * own, :] = second[0].astype(F32).T.astype(BF)
-        gains = [
-            gain[0:1, head * HD : (head + 1) * HD].astype(F32) for head in range(own // HD)
-        ]
-        gains.append(jnp.zeros((16 - own // HD, HD), F32))
-        weights[2 * own :, :] = jnp.concatenate(gains, axis=0).astype(BF)
-
-
-def pack(slots, live, starts, counts, tokens, cotangents, gain, first, second, groups):
-    micro_total, length, width = tokens.shape
-    micro_local = slots.shape[0]
+    section = lax.axis_index("pipe")
+    group = lax.axis_index("z")
+    picks = []
+    copies = [
+        pltpu.make_async_copy(second.at[0], second_in, sems.at[0]),
+        pltpu.make_async_copy(gain, gain_in, sems.at[1]),
+        pltpu.make_async_copy(first.at[0], weights.at[pl.ds(0, own)], sems.at[2]),
+        pltpu.make_async_copy(starts, starts_in, sems.at[3]),
+        pltpu.make_async_copy(counts, counts_in, sems.at[4]),
+    ]
+    for micro in range(micro_local):
+        wanted = section * micro_local + micro
+        slot = jnp.minimum(wanted, directions * micro_count - 1)
+        direction, place = slot // micro_count, slot % micro_count
+        picks.append((wanted < directions * micro_count, direction, place))
+        rows = pl.ds(micro * length, length)
+        copies.append(
+            pltpu.make_async_copy(
+                tokens.at[direction, place], tok.at[rows], sems.at[5 + 2 * micro]
+            )
+        )
+        copies.append(
+            pltpu.make_async_copy(
+                cotangents.at[direction, place], cot.at[rows], sems.at[6 + 2 * micro]
+            )
+        )
+    for copy in copies:
+        copy.start()
+    for copy in copies:
+        copy.wait()
+    weights[own : 2 * own, :] = second_in[...].astype(F32).T.astype(BF)
+    gains = [gain_in[0:1, head * HD : (head + 1) * HD].astype(F32) for head in range(own // HD)]
+    gains.append(jnp.zeros((16 - own // HD, HD), F32))
+    weights[2 * own :, :] = jnp.concatenate(gains, axis=0).astype(BF)
+    for micro, (keep, direction, place) in enumerate(picks):
+        rows = slice(micro * length, (micro + 1) * length)
+        widened = tok[rows, :].astype(F32)
+        mean = jnp.mean(widened * widened, axis=1, keepdims=True)
+        mean_high, mean_low = two_parts(mean)
+        position = lax.broadcasted_iota(jnp.int32, (length, HD), 0)
+        document = jnp.zeros((length, HD), jnp.int32)
+        for entry in range(starts.shape[2]):
+            begun = starts_in[direction, place, entry] <= position
+            begun = begun & (entry < counts_in[direction, place])
+            document = document + begun.astype(jnp.int32)
+        lane = lax.broadcasted_iota(jnp.int32, (length, HD), 1)
+        tail = jnp.where(
+            lane == 0,
+            document.astype(F32),
+            jnp.where(lane == 1, mean_high.astype(F32), mean_low.astype(F32)),
+        ).astype(BF)
+        for shift in range(groups):
+            start = pl.multiple_of(((group + shift) % groups) * local, local)
+            token_parts[shift][rows, 0:local] = tok[rows, pl.ds(start, local)]
+            token_parts[shift][rows, local:] = tail
+            cotangent = cot[rows, pl.ds(start, local)]
+            cot_parts[shift][rows, :] = jnp.where(keep, cotangent, jnp.zeros_like(cotangent))
+
+
+def pack(tokens, cotangents, starts, counts, gain, first, second, groups, micro_local):
+    length, width = tokens.shape[2:]
     own = first.shape[1]
     local = width // groups
-
-    def picked(micro, slots, *_):
-        return (slots[micro], 0, 0)
-
-    whole = lambda shape: pl.BlockSpec(shape, lambda *_: (0,) * len(shape))
-    return pl.pallas_call(
-        pack_kernel,
-        grid_spec=pltpu.PrefetchScalarGridSpec(
-            num_scalar_prefetch=4,
-            grid=(micro_local,),
-            in_specs=[
-                pl.BlockSpec((1, length, width), picked),
-                pl.BlockSpec((1, length, width), picked),
-                whole(gain.shape),
-                whole(first.shape),
-                whole(second.shape),
-            ],
-            out_specs=[
-                pl.BlockSpec((groups, length, 2 * local + HD), lambda micro, *_: (0, micro, 0)),
-                whole((slice_rows(own), HD)),
-            ],
-        ),
-        out_shape=[
-            jax.ShapeDtypeStruct((groups, micro_local * length, 2 * local + HD), BF),
-            jax.ShapeDtypeStruct((slice_rows(own), HD), BF),
+    rows = micro_local * length
+    shape = jax.ShapeDtypeStruct
+    results = pl.pallas_call(
+        functools.partial(pack_kernel, groups, micro_local),
+        in_specs=[pl.BlockSpec(memory_space=pltpu.HBM)] * 7,
+        out_specs=vmem_specs(2 * groups + 1),
+        out_shape=[shape((rows, local + HD), BF)] * groups
+        + [shape((rows, local), BF)] * groups
+        + [shape((slice_rows(own), HD), BF)],
+        scratch_shapes=[
+            pltpu.VMEM((rows, width), BF),
+            pltpu.VMEM((rows, width), BF),
+            pltpu.SMEM(starts.shape, jnp.int32),
+            pltpu.SMEM(counts.shape, jnp.int32),
+            pltpu.VMEM(gain.shape, BF),
+            pltpu.VMEM(second.shape[1:], BF),
+            pltpu.SemaphoreType.DMA((5 + 2 * micro_local,)),
         ],
         compiler_params=PARAMS,
         name="pack",
-    )(slots, live, starts, counts, tokens, cotangents, gain, first, second)
+    )(tokens, cotangents, starts, counts, gain, first, second)
+    return results[:groups], results[groups : 2 * groups], results[2 * groups]
 
 
 def head_gain(weights, head):
@@ -205,16 +225,41 @@
         ).astype(BF)
 
 
-def first_kernel(length, received, weights, x, cot, mask, mean, probs, mixed, pay):
+def first_kernel(length, groups, sections, *refs):
+    received, refs = refs[:groups], refs[groups:]
+    mine, theirs = refs[:sections], refs[sections : 2 * sections]
+    x, mask, mean, probs, mixed, pay, weights, tails, sems = refs[2 * sections :]
+    section, core = lax.axis_index("pipe"), lax.axis_index("core")
     rows, local = x.shape
     size = block_size(rows)
-    x[...] = received[:, 0:local]
-    cot[...] = received[:, local : 2 * local]
-    tail = received[:, 2 * local :].astype(F32)
+    copies = []
+    for distance in range(sections):
+        layer = section ^ distance
+        for parts, side in ((mine, core), (theirs, 1 - core)):
+            copies.append(
+                pltpu.make_async_copy(
+                    parts[distance], weights.at[layer, side], sems.at[distance, side]
+                )
+            )
+    for copy in copies:
+        copy.start()
+    place_rows(received, tails, slice(local, None))
+    place_rows(received, x, slice(0, local))
+    tail = tails[...].astype(F32)
     mean[...] = jnp.broadcast_to(tail[:, 1:2] + tail[:, 2:3], mean.shape)
     build_mask(tail[:, 0:1], mask, size, length)
+    for copy in copies:
+        copy.wait()
     attend(x, mean[:, 0:1], weights, mask, probs, mixed)
     send_forward(x, weights, mixed, pay)
+
+
+def place_rows(received, target, columns):
+    groups = len(received)
+    rows = received[0].shape[0]
+    for shift, part in enumerate(received):
+        source = (lax.axis_index("z") + groups - shift) % groups
+        target[pl.ds(pl.multiple_of(source * rows, rows), rows), :] = part[:, columns]
 
 
 def build_mask(document, mask, size, length):
@@ -227,20 +272,22 @@
         mask[block] = allowed.astype(F32).astype(BF)
 
 
-def middle_kernel(count, last, width, *refs):
+def middle_kernel(count, last, width, groups, *refs):
     pays, refs = refs[:count], refs[count:]
     x_before, mean_before, mask, weights_before, weights = refs[:5]
     refs = refs[5:]
     if last:
-        cot, weights_after = refs[:2]
-        refs = refs[2:]
-    x, mean, reduced, cross, probs, mixed, pay = refs
+        received, weights_after = refs[:groups], refs[groups]
+        refs = refs[groups + 1 :]
+    x, mean, reduced, cross, probs, mixed, pay = refs[:7]
     receive_forward(
         pays, x_before, mean_before, weights_before, width, x, mean, reduced, cross
     )
     attend(x, mean[:, 0:1], weights, mask, probs, mixed)
     send_forward(x, weights, mixed, pay)
     if last:
+        cot = refs[7]
+        place_rows(received, cot, slice(None))
         rows = x.shape[0]
         own = (weights.shape[2] - 16) // 2
         pay[2 * rows + HD :, :] = to_rank(cot[...], weights_after, own).astype(BF)
@@ -327,31 +374,34 @@
     pay[pay.shape[0] - rows :, :] = to_rank(mixed[...], weights, 0).astype(BF)
 
 
+def split_sides(grads, keep, send):
+    core = lax.axis_index("core")
+    keep[...] = grads[core]
+    send[...] = grads[1 - core]
+
+
 def back_kernel(count, after_turn, to_first, width, *refs):
     pays, refs = refs[:count], refs[count:]
     carried_after, x_after, mean_after, cross_after = refs[:4]
     x, mean, mask, weights = refs[4:8]
     refs = refs[8:]
+    weights_before = carried = pay = None
     if not to_first:
-        weights_before = refs[0]
-        refs = refs[1:]
-    else:
-        weights_before = None
+        weights_before, refs = refs[0], refs[1:]
     probs, mixed, reduced = refs[:3]
     refs = refs[3:]
     if after_turn:
         cot, turn_grads = refs[:2]
         refs = refs[2:]
-    else:
-        refs = refs[1:]
-    grads = refs[0]
-    refs = refs[1:]
-    if to_first:
-        carried = pay = None
-    else:
+    keep, send = refs[:2]
+    refs = refs[2:]
+    if after_turn:
+        last_keep, last_send = refs[:2]
+        refs = refs[2:]
+    if not to_first:
         carried, pay = refs[:2]
         refs = refs[2:]
-    dout = refs[0]
+    dout, grads = refs
     rows, local = x.shape
     size = block_size(rows)
     own = (weights.shape[2] - 16) // 2
@@ -378,20 +428,34 @@
         last_reduced = total_of(pays, pays[0].shape[0] - rows, pays[0].shape[0]).astype(BF)
         second = dot_tn(last_reduced, cot[...]).astype(BF)
         for side in range(weights.shape[1]):
-            grads[1, side, 0:rank, :] = turn_grads[side, 0:rank, :]
-            grads[1, side, rank : 2 * rank, :] = second[:, side * own : (side + 1) * own]
-            grads[1, side, 2 * rank :, :] = turn_grads[side, 2 * rank :, :]
+            grads[side, 0:rank, :] = turn_grads[side, 0:rank, :]
+            grads[side, rank : 2 * rank, :] = second[:, side * own : (side + 1) * own]
+            grads[side, 2 * rank :, :] = turn_grads[side, 2 * rank :, :]
+        split_sides(grads, last_keep, last_send)
     layer_backward(
         dout, dred, x, mean[:, 0:1], mask, weights, weights_before, probs, mixed, reduced[...],
-        grads.at[0], carried, pay,
-    )
-
-
-def finish_kernel(parts, gain, first, second):
+        grads, carried, pay,
+    )
+    split_sides(grads, keep, send)
+
+
+def combine_kernel(sections, *refs):
+    kept, swapped = refs[:sections], refs[sections : 2 * sections]
+    outs, sums = refs[2 * sections : 3 * sections], refs[3 * sections]
+    section = lax.axis_index("pipe")
+    for layer in range(sections):
+        sums[layer] = (kept[layer][...].astype(F32) + swapped[layer][...].astype(F32)).astype(BF)
+    for distance in range(sections):
+        outs[distance][...] = sums[section ^ distance]
+
+
+def finish_kernel(sections, *refs):
+    parts = refs[:sections]
+    gain, first, second = refs[sections:]
     rank = second.shape[1]
-    total = parts[0].astype(F32)
-    for index in range(1, parts.shape[0]):
-        total = total + parts[index].astype(F32)
+    total = parts[0][...].astype(F32)
+    for part in parts[1:]:
+        total = total + part[...].astype(F32)
     first[0] = total[0:rank].T
     second[0] = total[rank : 2 * rank]
     gain[...] = total[2 * rank : 2 * rank + 1]
@@ -400,10 +464,8 @@
 def per_device(tokens, cotangents, starts, counts, layer_gains, first_map, second_map):
     sections = lax.axis_size("pipe")
     groups = lax.axis_size("z")
-    my_section = lax.axis_index("pipe")
     directions, micro_count, length, width = tokens.shape
-    micro_total = directions * micro_count
-    micro_local = -(-micro_total // sections)
+    micro_local = -(-directions * micro_count // sections)
     rows = groups * micro_local * length
     local = width // groups
     own = first_map.shape[1]
@@ -412,34 +474,29 @@
     size = block_size(rows)
     blocks = rows // size
     sides = lax.axis_size("core")
-
-    wanted = my_section * micro_local + jnp.arange(micro_local, dtype=jnp.int32)
-    live = (wanted < micro_total).astype(jnp.int32)
-    slots = jnp.minimum(wanted, micro_total - 1)
-    payload, packed = pack(
-        slots,
-        live,
-        starts.reshape(micro_total, -1),
-        counts.reshape(micro_total),
-        tokens.reshape(micro_total, length, width),
-        cotangents.reshape(micro_total, length, width),
-        layer_gains,
-        first_map,
-        second_map,
-        groups,
-    )
-    received = lax.all_to_all(payload, "z", split_axis=0, concat_axis=0, tiled=True)
-    received = received.reshape(rows, 2 * local + HD)
-    weights = lax.all_gather(packed, ("pipe", "core"), axis=0, tiled=False)
-    weights = weights.reshape(sections, sides, slice_rows(own), HD)
+    top = sections - 1
+
+    def shifted(value, shift):
+        return lax.ppermute(value, "z", [(i, (i + shift) % groups) for i in range(groups)])
+
+    def across(value, distance):
+        return lax.ppermute(value, "pipe", [(i, i ^ distance) for i in range(sections)])
+
+    def swapped(value):
+        return lax.ppermute(value, "core", [(i, 1 - i) for i in range(sides)])
 
     def exchange(pay):
-        pays = [pay]
-        for shift in range(1, groups):
-            pays.append(
-                lax.ppermute(pay, "z", [(i, (i + shift) % groups) for i in range(groups)])
-            )
-        return pays
+        return [pay] + [shifted(pay, shift) for shift in range(1, groups)]
+
+    token_parts, cot_parts, packed = pack(
+        tokens, cotangents, starts, counts, layer_gains, first_map, second_map, groups, micro_local
+    )
+    received = [token_parts[0]]
+    received += [shifted(token_parts[shift], shift) for shift in range(1, groups)]
+    mine = [packed] + [across(packed, distance) for distance in range(1, sections)]
+    theirs = [swapped(part) for part in mine]
+    cot_received = [cot_parts[0]]
+    cot_received += [shifted(cot_parts[shift], shift) for shift in range(1, groups)]
 
     def shaped(shape, kind=BF):
         return jax.ShapeDtypeStruct(shape, kind)
@@ -450,6 +507,8 @@
     cross_shape = shaped((rows, rank), F32)
     probs_shape = shaped((blocks, heads, size, size))
     grads_shape = (sides, 2 * rank + 16, own)
+    half_shape = shaped(grads_shape[1:])
+    weights_shape = shaped((sections, sides, slice_rows(own), HD))
     forward_rows = 2 * rows + HD
 
     def call(kernel, operands, specs, outs, name, **more):
@@ -457,7 +516,7 @@
             kernel,
             grid=(1,),
             in_specs=specs,
-            out_specs=more.pop("out_specs", None) or vmem_specs(len(outs)),
+            out_specs=vmem_specs(len(outs)),
             out_shape=outs,
             compiler_params=PARAMS,
             name=name,
@@ -465,46 +524,52 @@
         )(*operands)
 
     def layer_of(index):
-        return layer_spec(weights.shape, index)
-
-    x, cot, mask, mean, probs, mixed, pay = call(
-        functools.partial(first_kernel, length),
-        (received, weights),
-        vmem_specs(1) + [layer_of(0)],
+        return layer_spec(weights_shape.shape, index)
+
+    x, mask, mean, probs, mixed, pay, weights = call(
+        functools.partial(first_kernel, length, groups, sections),
+        (*received, *mine, *theirs),
+        vmem_specs(groups + 2 * sections),
         [
-            wide_shape,
             wide_shape,
             shaped((blocks, size, size)),
             mean_shape,
             probs_shape,
             wide_shape,
             shaped((forward_rows, HD)),
+            weights_shape,
         ],
         "forward_first",
+        scratch_shapes=[
+            pltpu.VMEM((rows, HD), BF),
+            pltpu.SemaphoreType.DMA((sections, sides)),
+        ],
     )
     xs, means, reduceds, crosses = [x], [mean], [], [None]
     all_probs, all_mixed = [probs], [mixed]
-    for layer in range(1, sections - 1):
+    for layer in range(1, top):
         pays = exchange(pay)
-        last = layer == sections - 2
+        last = layer == top - 1
         operands = (*pays, xs[-1], means[-1], mask, weights, weights)
         specs = vmem_specs(len(pays) + 3) + [layer_of(layer - 1), layer_of(layer)]
+        outs = [
+            wide_shape,
+            mean_shape,
+            rank_shape,
+            cross_shape,
+            probs_shape,
+            wide_shape,
+            shaped((forward_rows + (rows if last else 0), HD)),
+        ]
         if last:
-            operands += (cot, weights)
-            specs += vmem_specs(1) + [layer_of(layer + 1)]
-        x, mean, reduced, cross, probs, mixed, pay = call(
-            functools.partial(middle_kernel, len(pays), last, float(width)),
+            operands += (*cot_received, weights)
+            specs += vmem_specs(groups) + [layer_of(layer + 1)]
+            outs += [wide_shape]
+        x, mean, reduced, cross, probs, mixed, pay, *cots = call(
+            functools.partial(middle_kernel, len(pays), last, float(width), groups),
             operands,
             specs,
-            [
-                wide_shape,
-                mean_shape,
-                rank_shape,
-                cross_shape,
-                probs_shape,
-                wide_shape,
-                shaped((forward_rows + (rows if last else 0), HD)),
-            ],
+            outs,
             "forward_middle",
         )
         xs.append(x)
@@ -513,9 +578,9 @@
         crosses.append(cross)
         all_probs.append(probs)
         all_mixed.append(mixed)
+    cot = cots[0]
 
     pays = exchange(pay)
-    top = sections - 1
     back_rows = rows + 16 * blocks
     x, mean, reduced, cross, turn_grads, carried, pay = call(
         functools.partial(turn_kernel, len(pays), float(width)),
@@ -541,7 +606,7 @@
     reduceds.append(reduced)
     crosses.append(cross)
 
-    grads = None
+    kept, taken = [None] * sections, [None] * sections
     for layer in range(top - 1, -1, -1):
         pays = exchange(pay)
         after_turn = layer == top - 1
@@ -556,48 +621,40 @@
             specs += [layer_of(layer - 1)]
         operands += (all_probs[layer], all_mixed[layer], reduceds[layer])
         specs += vmem_specs(3)
-        more = {}
+        outs = [half_shape] * 2
         if after_turn:
             operands += (cot, turn_grads)
             specs += vmem_specs(2)
-            block = (2,) + grads_shape
-            place = layer // 2
-        else:
-            operands += (grads,)
-            specs += [pl.BlockSpec(memory_space=pl.ANY)]
-            more["input_output_aliases"] = {len(operands) - 1: 0}
-            block = (1,) + grads_shape
-            place = layer
-        outs = [shaped((sections,) + grads_shape)]
-        out_specs = [pl.BlockSpec(block, lambda *_, place=place: (place, 0, 0, 0))]
+            outs += [half_shape] * 2
         if not to_first:
             outs += [wide_shape, shaped((back_rows, HD))]
-            out_specs += vmem_specs(2)
         result = call(
             functools.partial(back_kernel, len(pays), after_turn, to_first, float(width)),
             operands,
             specs,
             outs,
             "backward",
-            out_specs=out_specs,
-            scratch_shapes=[pltpu.VMEM(wide_shape.shape, BF)],
-            **more,
+            scratch_shapes=[pltpu.VMEM(wide_shape.shape, BF), pltpu.VMEM(grads_shape, BF)],
         )
-        grads = result[0]
+        kept[layer], taken[layer] = result[0], swapped(result[1])
+        if after_turn:
+            kept[top], taken[top] = result[2], swapped(result[3])
         if not to_first:
-            carried, pay = result[1:]
-
-    parts = lax.all_to_all(
-        grads.reshape((sections * sides,) + grads_shape[1:]),
-        ("pipe", "core"),
-        split_axis=0,
-        concat_axis=0,
-        tiled=True,
-    )
+            carried, pay = result[-2:]
+
+    parts = call(
+        functools.partial(combine_kernel, sections),
+        (*kept, *taken),
+        vmem_specs(2 * sections),
+        [half_shape] * sections,
+        "combine",
+        scratch_shapes=[pltpu.VMEM((sections,) + grads_shape[1:], BF)],
+    )
+    arrived = [parts[0]] + [across(parts[distance], distance) for distance in range(1, sections)]
     gain_grad, first_grad, second_grad = call(
-        finish_kernel,
-        (parts,),
-        vmem_specs(1),
+        functools.partial(finish_kernel, sections),
+        arrived,
+        vmem_specs(sections),
         [
             shaped((1, own), F32),
             shaped((1, own, rank), F32),

time: 165 us -> 132 us (0.80)
  blocking collectives: 51.9 us -> 0 us
  waiting for transfers between devices: 47.4 us -> 65.5 us
  starting transfers between devices: 22.4 us -> 40.4 us
  between operations: 14.1 us -> 0.78 us
  local copies, waits for them, and re-layouts: 9.61 us -> 6.29 us
    all_to_all x2 -> x0, blocking collectives: 51.9 us -> none  [the longest x1 30.6 us: per_device(): lax.all_to_all(grads.reshape((sections * sides,) + grads_shape[1:]), ('pi...]
    ppermute x18 -> x38, waiting for transfers between devices: 37.8 us -> 65.5 us  [the longest x24 39.9 us: shifted(): lax.ppermute(value, 'z', [(i, (i + shift) % groups) for i in range(groups)])]
    ppermute x18 -> x38, starting transfers between devices: 22.4 us -> 40.4 us  [the longest x24 31.4 us: shifted(): lax.ppermute(value, 'z', [(i, (i + shift) % groups) for i in range(groups)])]
    all_gather x1 -> x0, waiting for transfers between devices: 9.59 us -> none  [per_device(): weights = lax.all_gather(packed, ('pipe', 'core'), axis=0, tiled=False)]
    unnamed x18 -> x14, local copies, waits for them, and re-layouts: 8.85 us -> 6.29 us
    pallas_call x9 -> x10, Pallas kernels: 19.6 us -> 18.7 us  [the longest x9 17.6 us: call(): pl.pallas_call(kernel, grid=(1,), in_specs=specs, out_specs=vmem_specs(le...]
  transfers between devices with their start and end apart: 19 -> 38, of which waited for: 15 -> 24; matrix products, arithmetic and copies ran while one was open for 0% -> 0% of each run, Pallas kernels for 0% -> 3%
where the time goes in v2:
time: 132 us
  waiting for transfers between devices  65.5 us (50%)
  starting transfers between devices  40.4 us (31%)
  Pallas kernels  18.7 us (14%)
  local copies, waits for them, and re-layouts  6.29 us (5%)
    ppermute x24, waiting for transfers between devices, shifted(): lax.ppermute(value, 'z', [(i, (i + shift) % groups) for i in range(groups)])  39.9 us
    ppermute x24, starting transfers between devices, shifted(): lax.ppermute(value, 'z', [(i, (i + shift) % groups) for i in range(groups)])  31.4 us
    ppermute x6, waiting for transfers between devices, across(): lax.ppermute(value, 'pipe', [(i, i ^ distance) for i in range(sections)])  24.1 us
    pallas_call x9, Pallas kernels, call(): pl.pallas_call(kernel, grid=(1,), in_specs=specs, out_specs=vmem_specs(le...  17.6 us
    ppermute x6, starting transfers between devices, across(): lax.ppermute(value, 'pipe', [(i, i ^ distance) for i in range(sections)])  8.15 us
    unnamed x14, local copies, waits for them, and re-layouts  6.29 us
  transfers between devices with their start and end apart: 38, of which 24 were waited for; matrix products, arithmetic and copies ran while one was open for 0% of the time, Pallas kernels for 3%

profile of v2, /device:TPU:0, one launch (start us, length us, event | category | flops | bytes accessed | tf_op | source)
XLA Modules:
  0.0 131.7 jit_solution(442352472554422475)
XLA Ops:
  8.1 4.0 %collective-permute-start.5 = (bf16[1040,128]{1,0:T(8,128)(2,1)S(1)}, bf16[1040,128]{1,0:T(8,128)(2,1)S(1)}, u32[]{:S(2)}, u32[]{:S(2)}) collective-permute-start(bf16[1040,128]{1,0:T(8,128)(2,1)S(1)} %get-tuple-element.61.refs_4_), channel_id=1, source_target_pairs={{0,24},{8,16},{16,8},{24,0},{1,25},{9,17},{17,9},{25,1},{2,26},{10... | collective-permute-start | bytes 798728 | tf_op jit(solution)/shard_map/ppermute | solution.py:483
  12.7 6.6 %collective-permute-done.5.refs_7_ = bf16[1040,128]{1,0:T(8,128)(2,1)S(1)} collective-permute-done((bf16[1040,128]{1,0:T(8,128)(2,1)S(1)}, bf16[1040,128]{1,0:T(8,128)(2,1)S(1)}, u32[]{:S(2)}, u32[]{:S(2)}) %collective-permute-start.5) | collective-permute-done | bytes 266272 | tf_op jit(solution)/shard_map/ppermute | solution.py:483
  19.3 4.8 %collective-permute-done.4.refs_6_ = bf16[1040,128]{1,0:T(8,128)(2,1)S(1)} collective-permute-done((bf16[1040,128]{1,0:T(8,128)(2,1)S(1)}, bf16[1040,128]{1,0:T(8,128)(2,1)S(1)}, u32[]{:S(2)}, u32[]{:S(2)}) %collective-permute-start.4) | collective-permute-done | bytes 266272 | tf_op jit(solution)/shard_map/ppermute | solution.py:483
  24.6 1.8 %collective-permute-start = (bf16[32,1152]{1,0:T(8,128)(2,1)S(1)}, bf16[32,1152]{1,0:T(8,128)(2,1)S(1)}, u32[]{:S(2)}, u32[]{:S(2)}) collective-permute-start(bf16[32,1152]{1,0:T(8,128)(2,1)S(1)} %get-tuple-element.58), channel_id=1, source_target_pairs={{0,2},{2,4},{4,6},{6,0},{1,3},{3,5},{5,7},{7,1},{8,10},{10,12},{12... | collective-permute-start | bytes 221192 | tf_op jit(solution)/shard_map/ppermute | solution.py:480
  26.4 4.6 %collective-permute-done.refs_1_ = bf16[32,1152]{1,0:T(8,128)(2,1)S(1)} collective-permute-done((bf16[32,1152]{1,0:T(8,128)(2,1)S(1)}, bf16[32,1152]{1,0:T(8,128)(2,1)S(1)}, u32[]{:S(2)}, u32[]{:S(2)}) %collective-permute-start) | collective-permute-done | bytes 73760 | tf_op jit(solution)/shard_map/ppermute | solution.py:480
  31.8 4.9 %collective-permute-done.1.refs_2_ = bf16[32,1152]{1,0:T(8,128)(2,1)S(1)} collective-permute-done((bf16[32,1152]{1,0:T(8,128)(2,1)S(1)}, bf16[32,1152]{1,0:T(8,128)(2,1)S(1)}, u32[]{:S(2)}, u32[]{:S(2)}) %collective-permute-start.1) | collective-permute-done | bytes 73760 | tf_op jit(solution)/shard_map/ppermute | solution.py:480
  36.7 2.0 %collective-permute-start.2 = (bf16[32,1152]{1,0:T(8,128)(2,1)S(1)}, bf16[32,1152]{1,0:T(8,128)(2,1)S(1)}, u32[]{:S(2)}, u32[]{:S(2)}) collective-permute-start(bf16[32,1152]{1,0:T(8,128)(2,1)S(1)} %get-tuple-element.60), channel_id=1, source_target_pairs={{0,6},{2,0},{4,2},{6,4},{1,7},{3,1},{5,3},{7,5},{8,14},{10,8},{12,... | collective-permute-start | bytes 221192 | tf_op jit(solution)/shard_map/ppermute | solution.py:480
  38.7 2.3 %collective-permute-done.2.refs_3_ = bf16[32,1152]{1,0:T(8,128)(2,1)S(1)} collective-permute-done((bf16[32,1152]{1,0:T(8,128)(2,1)S(1)}, bf16[32,1152]{1,0:T(8,128)(2,1)S(1)}, u32[]{:S(2)}, u32[]{:S(2)}) %collective-permute-start.2) | collective-permute-done | bytes 73760 | tf_op jit(solution)/shard_map/ppermute | solution.py:480
  41.1 3.0 %forward_first.1 = (bf16[128,1024]{1,0:T(8,128)(2,1)S(1)}, bf16[1,128,128]{2,1,0:T(8,128)(2,1)S(1)}, f32[128,128]{1,0:T(8,128)S(1)}, bf16[1,8,128,128]{3,2,1,0:T...) custom-call(bf16[32,1152]{1,0:T(8,128)(2,1)S(1)} %get-tuple-element., ...), custom_call_target="tpu_custom_call" | custom-call | tf_op jit(solution)/shard_map/forward_first/pallas_call | solution.py:515
  44.1 3.9 %collective-permute-start.12 = (bf16[384,128]{1,0:T(8,128)(2,1)S(1)}, bf16[384,128]{1,0:T(8,128)(2,1)S(1)}, u32[]{:S(2)}, u32[]{:S(2)}) collective-permute-start(bf16[384,128]{1,0:T(8,128)(2,1)S(1)} %get-tuple-element.62.refs_0_), channel_id=1, source_target_pairs={{0,6},{2,0},{4,2},{6,4},{1,7},{3,1},{5,3},{7,5},{8,14},{10,8},{12,... | collective-permute-start | bytes 294920 | tf_op jit(solution)/shard_map/ppermute | solution.py:480
  48.6 2.8 %collective-permute-start.16 = (bf16[32,1024]{1,0:T(8,128)(2,1)S(1)}, bf16[32,1024]{1,0:T(8,128)(2,1)S(1)}, u32[]{:S(2)}, u32[]{:S(2)}) collective-permute-start(bf16[32,1024]{1,0:T(8,128)(2,1)S(1)} %get-tuple-element.71), channel_id=1, source_target_pairs={{0,2},{2,4},{4,6},{6,0},{1,3},{3,5},{5,7},{7,1},{8,10},{10,12},{12... | collective-permute-start | bytes 196616 | tf_op jit(solution)/shard_map/ppermute | solution.py:480
  51.5 4.2 %collective-permute-done.11.refs_2_ = bf16[384,128]{1,0:T(8,128)(2,1)S(1)} collective-permute-done((bf16[384,128]{1,0:T(8,128)(2,1)S(1)}, bf16[384,128]{1,0:T(8,128)(2,1)S(1)}, u32[]{:S(2)}, u32[]{:S(2)}) %collective-permute-start.11) | collective-permute-done | bytes 98336 | tf_op jit(solution)/shard_map/ppermute | solution.py:480
  55.7 2.4 %forward_middle.2 = (bf16[128,1024]{1,0:T(8,128)(2,1)S(1)}, f32[128,128]{1,0:T(8,128)S(1)}, bf16[128,128]{1,0:T(8,128)(2,1)S(1)}, f32[128,128]{1,0:T(8,128)S(1)}...) custom-call(bf16[384,128]{1,0:T(8,128)(2,1)S(1)} %get-tuple-element.62.refs_0_, ...), custom_call_target="tpu_custom_call" | custom-call | tf_op jit(solution)/shard_map/forward_middle/pallas_call | solution.py:515
  59.0 1.9 %collective-permute-start.13 = (bf16[384,128]{1,0:T(8,128)(2,1)S(1)}, bf16[384,128]{1,0:T(8,128)(2,1)S(1)}, u32[]{:S(2)}, u32[]{:S(2)}) collective-permute-start(bf16[384,128]{1,0:T(8,128)(2,1)S(1)} %get-tuple-element.67.refs_0_), channel_id=1, source_target_pairs={{0,2},{2,4},{4,6},{6,0},{1,3},{3,5},{5,7},{7,1},{8,10},{10,12},{12... | collective-permute-start | bytes 294920 | tf_op jit(solution)/shard_map/ppermute | solution.py:480
  61.0 2.1 %collective-permute-start.17 = (bf16[32,1024]{1,0:T(8,128)(2,1)S(1)}, bf16[32,1024]{1,0:T(8,128)(2,1)S(1)}, u32[]{:S(2)}, u32[]{:S(2)}) collective-permute-start(bf16[32,1024]{1,0:T(8,128)(2,1)S(1)} %get-tuple-element.72), channel_id=1, source_target_pairs={{0,4},{2,6},{4,0},{6,2},{1,5},{3,7},{5,1},{7,3},{8,12},{10,14},{12... | collective-permute-start | bytes 196616 | tf_op jit(solution)/shard_map/ppermute | solution.py:480
  63.1 1.6 %collective-permute-start.18 = (bf16[32,1024]{1,0:T(8,128)(2,1)S(1)}, bf16[32,1024]{1,0:T(8,128)(2,1)S(1)}, u32[]{:S(2)}, u32[]{:S(2)}) collective-permute-start(bf16[32,1024]{1,0:T(8,128)(2,1)S(1)} %get-tuple-element.73), channel_id=1, source_target_pairs={{0,6},{2,0},{4,2},{6,4},{1,7},{3,1},{5,3},{7,5},{8,14},{10,8},{12,... | collective-permute-start | bytes 196616 | tf_op jit(solution)/shard_map/ppermute | solution.py:480
  64.7 3.6 %collective-permute-done.17.refs_11_ = bf16[32,1024]{1,0:T(8,128)(2,1)S(1)} collective-permute-done((bf16[32,1024]{1,0:T(8,128)(2,1)S(1)}, bf16[32,1024]{1,0:T(8,128)(2,1)S(1)}, u32[]{:S(2)}, u32[]{:S(2)}) %collective-permute-start.17) | collective-permute-done | bytes 65568 | tf_op jit(solution)/shard_map/ppermute | solution.py:480
  68.8 2.5 %forward_middle.3 = (bf16[128,1024]{1,0:T(8,128)(2,1)S(1)}, f32[128,128]{1,0:T(8,128)S(1)}, bf16[128,128]{1,0:T(8,128)(2,1)S(1)}, f32[128,128]{1,0:T(8,128)S(1)}...) custom-call(bf16[384,128]{1,0:T(8,128)(2,1)S(1)} %get-tuple-element., ...), custom_call_target="tpu_custom_call" | custom-call | tf_op jit(solution)/shard_map/forward_middle/pallas_call | solution.py:515
  71.3 2.3 %collective-permute-start.21 = (bf16[512,128]{1,0:T(8,128)(2,1)S(1)}, bf16[512,128]{1,0:T(8,128)(2,1)S(1)}, u32[]{:S(2)}, u32[]{:S(2)}) collective-permute-start(bf16[512,128]{1,0:T(8,128)(2,1)S(1)} %get-tuple-element.74.refs_0_), channel_id=1, source_target_pairs={{0,6},{2,0},{4,2},{6,4},{1,7},{3,1},{5,3},{7,5},{8,14},{10,8},{12,... | collective-permute-start | bytes 393224 | tf_op jit(solution)/shard_map/ppermute | solution.py:480
  74.3 3.5 %collective-permute-done.21.refs_3_ = bf16[512,128]{1,0:T(8,128)(2,1)S(1)} collective-permute-done((bf16[512,128]{1,0:T(8,128)(2,1)S(1)}, bf16[512,128]{1,0:T(8,128)(2,1)S(1)}, u32[]{:S(2)}, u32[]{:S(2)}) %collective-permute-start.21) | collective-permute-done | bytes 131104 | tf_op jit(solution)/shard_map/ppermute | solution.py:480
  77.7 4.2 %collective-permute-done.20.refs_2_ = bf16[512,128]{1,0:T(8,128)(2,1)S(1)} collective-permute-done((bf16[512,128]{1,0:T(8,128)(2,1)S(1)}, bf16[512,128]{1,0:T(8,128)(2,1)S(1)}, u32[]{:S(2)}, u32[]{:S(2)}) %collective-permute-start.20) | collective-permute-done | bytes 131104 | tf_op jit(solution)/shard_map/ppermute | solution.py:480
  81.9 3.3 %turn.1 = (bf16[128,1024]{1,0:T(8,128)(2,1)S(1)}, f32[128,128]{1,0:T(8,128)S(1)}, bf16[128,128]{1,0:T(8,128)(2,1)S(1)}, f32[128,128]{1,0:T(8,128)S(1)}, bf16[2,2...) custom-call(bf16[512,128]{1,0:T(8,128)(2,1)S(1)} %get-tuple-element.74.refs_0_, ...), custom_call_target="tpu_custom_call" | custom-call | tf_op jit(solution)/shard_map/turn/pallas_call | solution.py:515
  87.2 1.9 %collective-permute-start.22 = (bf16[272,128]{1,0:T(8,128)(2,1)S(1)}, bf16[272,128]{1,0:T(8,128)(2,1)S(1)}, u32[]{:S(2)}, u32[]{:S(2)}) collective-permute-start(bf16[272,128]{1,0:T(8,128)(2,1)S(1)} %get-tuple-element.78.refs_0_), channel_id=1, source_target_pairs={{0,2},{2,4},{4,6},{6,0},{1,3},{3,5},{5,7},{7,1},{8,10},{10,12},{12... | collective-permute-start | bytes 208904 | tf_op jit(solution)/shard_map/ppermute | solution.py:480
  90.4 2.2 %collective-permute-done.23.refs_2_ = bf16[272,128]{1,0:T(8,128)(2,1)S(1)} collective-permute-done((bf16[272,128]{1,0:T(8,128)(2,1)S(1)}, bf16[272,128]{1,0:T(8,128)(2,1)S(1)}, u32[]{:S(2)}, u32[]{:S(2)}) %collective-permute-start.23) | collective-permute-done | bytes 69664 | tf_op jit(solution)/shard_map/ppermute | solution.py:480
  93.3 1.7 %backward.3 = (bf16[272,512]{1,0:T(8,128)(2,1)S(1)}, bf16[272,512]{1,0:T(8,128)(2,1)S(1)}, bf16[272,512]{1,0:T(8,128)(2,1)S(1)}, bf16[272,512]{1,0:T(8,128)(2,1)...) custom-call(bf16[272,128]{1,0:T(8,128)(2,1)S(1)} %get-tuple-element.78.refs_0_, ...), custom_call_target="tpu_custom_call" | custom-call | tf_op jit(solution)/shard_map/backward/pallas_call | solution.py:515
  99.1 3.1 %collective-permute-done.26.refs_2_ = bf16[144,128]{1,0:T(8,128)(2,1)S(1)} collective-permute-done((bf16[144,128]{1,0:T(8,128)(2,1)S(1)}, bf16[144,128]{1,0:T(8,128)(2,1)S(1)}, u32[]{:S(2)}, u32[]{:S(2)}) %collective-permute-start.26) | collective-permute-done | bytes 36896 | tf_op jit(solution)/shard_map/ppermute | solution.py:480
  102.5 1.7 %backward.4 = (bf16[272,512]{1,0:T(8,128)(2,1)S(1)}, bf16[272,512]{1,0:T(8,128)(2,1)S(1)}, bf16[128,1024]{1,0:T(8,128)(2,1)S(1)}, bf16[144,128]{1,0:T(8,128)(2,1)S(1)}) custom-call(bf16[144,128]{1,0:T(8,128)(2,1)S(1)} %get-tuple-element.87.refs_0_, bf16[144,128]{1,0:T(8,128)(2,1)S(1)} %collective-permute-done.25.refs_1_, ...), custom_call_target="tpu_custom_call" | custom-call | tf_op jit(solution)/shard_map/backward/pallas_call | solution.py:515
  105.4 1.9 %collective-permute-start.28 = (bf16[144,128]{1,0:T(8,128)(2,1)S(1)}, bf16[144,128]{1,0:T(8,128)(2,1)S(1)}, u32[]{:S(2)}, u32[]{:S(2)}) collective-permute-start(bf16[144,128]{1,0:T(8,128)(2,1)S(1)} %get-tuple-element.93.refs_0_), channel_id=1, source_target_pairs={{0,2},{2,4},{4,6},{6,0},{1,3},{3,5},{5,7},{7,1},{8,10},{10,12},{12... | collective-permute-start | bytes 110600 | tf_op jit(solution)/shard_map/ppermute | solution.py:480
  108.2 1.8 %collective-permute-done.29.refs_2_ = bf16[144,128]{1,0:T(8,128)(2,1)S(1)} collective-permute-done((bf16[144,128]{1,0:T(8,128)(2,1)S(1)}, bf16[144,128]{1,0:T(8,128)(2,1)S(1)}, u32[]{:S(2)}, u32[]{:S(2)}) %collective-permute-start.29) | collective-permute-done | bytes 36896 | tf_op jit(solution)/shard_map/ppermute | solution.py:480
  114.8 1.5 %collective-permute-start.35 = (bf16[272,512]{1,0:T(8,128)(2,1)S(1)}, bf16[272,512]{1,0:T(8,128)(2,1)S(1)}, u32[]{:S(2)}, u32[]{:S(2)}) collective-permute-start(bf16[272,512]{1,0:T(8,128)(2,1)S(1)} %get-tuple-element.108), channel_id=1, source_target_pairs={{0,8},{8,0},{16,24},{24,16},{1,9},{9,1},{17,25},{25,17},{2,10},{10... | collective-permute-start | bytes 835592 | tf_op jit(solution)/shard_map/ppermute | solution.py:483
  118.4 6.0 %collective-permute-done.35.refs_1_ = bf16[272,512]{1,0:T(8,128)(2,1)S(1)} collective-permute-done((bf16[272,512]{1,0:T(8,128)(2,1)S(1)}, bf16[272,512]{1,0:T(8,128)(2,1)S(1)}, u32[]{:S(2)}, u32[]{:S(2)}) %collective-permute-start.35) | collective-permute-done | bytes 278560 | tf_op jit(solution)/shard_map/ppermute | solution.py:483
  124.4 4.9 %collective-permute-done.36.refs_2_ = bf16[272,512]{1,0:T(8,128)(2,1)S(1)} collective-permute-done((bf16[272,512]{1,0:T(8,128)(2,1)S(1)}, bf16[272,512]{1,0:T(8,128)(2,1)S(1)}, u32[]{:S(2)}, u32[]{:S(2)}) %collective-permute-start.36) | collective-permute-done | bytes 278560 | tf_op jit(solution)/shard_map/ppermute | solution.py:483
  (68 shorter events, 31.7 us)
Async XLA Ops:
  8.1 11.2 %collective-permute-start.5 = (bf16[1040,128]{1,0:T(8,128)(2,1)S(1)}, bf16[1040,128]{1,0:T(8,128)(2,1)S(1)}, u32[]{:S(2)}, u32[]{:S(2)}) collective-permute-start(bf16[1040,128]{1,0:T(8,128)(2,1)S(1)} %get-tuple-element.61.refs_4_), channel_id=1, source_target_pairs={{0,24},{8,16},{16,8},{24,0},{1,25},{9,17},{17,9},{25,1},{2,26},{10... | collective-permute-start | bytes 798728 | tf_op jit(solution)/shard_map/ppermute | solution.py:483
  12.0 12.1 %collective-permute-start.4 = (bf16[1040,128]{1,0:T(8,128)(2,1)S(1)}, bf16[1040,128]{1,0:T(8,128)(2,1)S(1)}, u32[]{:S(2)}, u32[]{:S(2)}) collective-permute-start(bf16[1040,128]{1,0:T(8,128)(2,1)S(1)} %get-tuple-element.61.refs_4_), channel_id=1, source_target_pairs={{0,16},{8,24},{16,0},{24,8},{1,17},{9,25},{17,1},{25,9},{2,18},{10... | collective-permute-start | bytes 798728 | tf_op jit(solution)/shard_map/ppermute | solution.py:483
  12.5 11.9 %collective-permute-start.3 = (bf16[1040,128]{1,0:T(8,128)(2,1)S(1)}, bf16[1040,128]{1,0:T(8,128)(2,1)S(1)}, u32[]{:S(2)}, u32[]{:S(2)}) collective-permute-start(bf16[1040,128]{1,0:T(8,128)(2,1)S(1)} %get-tuple-element.61.refs_4_), channel_id=1, source_target_pairs={{0,8},{8,0},{16,24},{24,16},{1,9},{9,1},{17,25},{25,17},{2,10},{10... | collective-permute-start | bytes 798728 | tf_op jit(solution)/shard_map/ppermute | solution.py:483
  12.7 28.4 %collective-permute-start.6 = (bf16[1040,128]{1,0:T(8,128)(2,1)S(1)}, bf16[1040,128]{1,0:T(8,128)(2,1)S(1)}, u32[]{:S(2)}, u32[]{:S(2)}) collective-permute-start(bf16[1040,128]{1,0:T(8,128)(2,1)S(1)} %get-tuple-element.61.refs_4_), channel_id=1, source_target_pairs={{0,1},{1,0},{2,3},{3,2},{4,5},{5,4},{6,7},{7,6},{8,9},{9,8},{10,11... | collective-permute-start | bytes 798728 | tf_op jit(solution)/shard_map/ppermute | solution.py:486
  19.3 21.8 %collective-permute-start.9 = (bf16[1040,128]{1,0:T(8,128)(2,1)S(1)}, bf16[1040,128]{1,0:T(8,128)(2,1)S(1)}, u32[]{:S(2)}, u32[]{:S(2)}) collective-permute-start(bf16[1040,128]{1,0:T(8,128)(2,1)S(1)} %collective-permute-done.5.refs_7_), channel_id=1, source_target_pairs={{0,1},{1,0},{2,3},{3,2},{4,5},{5,4},{6,7},{7,6},{8,9},{9,8},{10,11... | collective-permute-start | bytes 798728 | tf_op jit(solution)/shard_map/ppermute | solution.py:486
  24.1 16.9 %collective-permute-start.8 = (bf16[1040,128]{1,0:T(8,128)(2,1)S(1)}, bf16[1040,128]{1,0:T(8,128)(2,1)S(1)}, u32[]{:S(2)}, u32[]{:S(2)}) collective-permute-start(bf16[1040,128]{1,0:T(8,128)(2,1)S(1)} %collective-permute-done.4.refs_6_), channel_id=1, source_target_pairs={{0,1},{1,0},{2,3},{3,2},{4,5},{5,4},{6,7},{7,6},{8,9},{9,8},{10,11... | collective-permute-start | bytes 798728 | tf_op jit(solution)/shard_map/ppermute | solution.py:486
  24.4 16.6 %collective-permute-start.7 = (bf16[1040,128]{1,0:T(8,128)(2,1)S(1)}, bf16[1040,128]{1,0:T(8,128)(2,1)S(1)}, u32[]{:S(2)}, u32[]{:S(2)}) collective-permute-start(bf16[1040,128]{1,0:T(8,128)(2,1)S(1)} %collective-permute-done.3.refs_5_), channel_id=1, source_target_pairs={{0,1},{1,0},{2,3},{3,2},{4,5},{5,4},{6,7},{7,6},{8,9},{9,8},{10,11... | collective-permute-start | bytes 798728 | tf_op jit(solution)/shard_map/ppermute | solution.py:486
  24.6 6.3 %collective-permute-start = (bf16[32,1152]{1,0:T(8,128)(2,1)S(1)}, bf16[32,1152]{1,0:T(8,128)(2,1)S(1)}, u32[]{:S(2)}, u32[]{:S(2)}) collective-permute-start(bf16[32,1152]{1,0:T(8,128)(2,1)S(1)} %get-tuple-element.58), channel_id=1, source_target_pairs={{0,2},{2,4},{4,6},{6,0},{1,3},{3,5},{5,7},{7,1},{8,10},{10,12},{12... | collective-permute-start | bytes 221192 | tf_op jit(solution)/shard_map/ppermute | solution.py:480
  30.9 5.7 %collective-permute-start.1 = (bf16[32,1152]{1,0:T(8,128)(2,1)S(1)}, bf16[32,1152]{1,0:T(8,128)(2,1)S(1)}, u32[]{:S(2)}, u32[]{:S(2)}) collective-permute-start(bf16[32,1152]{1,0:T(8,128)(2,1)S(1)} %get-tuple-element.59), channel_id=1, source_target_pairs={{0,4},{2,6},{4,0},{6,2},{1,5},{3,7},{5,1},{7,3},{8,12},{10,14},{12... | collective-permute-start | bytes 221192 | tf_op jit(solution)/shard_map/ppermute | solution.py:480
  44.1 7.4 %collective-permute-start.12 = (bf16[384,128]{1,0:T(8,128)(2,1)S(1)}, bf16[384,128]{1,0:T(8,128)(2,1)S(1)}, u32[]{:S(2)}, u32[]{:S(2)}) collective-permute-start(bf16[384,128]{1,0:T(8,128)(2,1)S(1)} %get-tuple-element.62.refs_0_), channel_id=1, source_target_pairs={{0,6},{2,0},{4,2},{6,4},{1,7},{3,1},{5,3},{7,5},{8,14},{10,8},{12,... | collective-permute-start | bytes 294920 | tf_op jit(solution)/shard_map/ppermute | solution.py:480
  48.0 7.7 %collective-permute-start.11 = (bf16[384,128]{1,0:T(8,128)(2,1)S(1)}, bf16[384,128]{1,0:T(8,128)(2,1)S(1)}, u32[]{:S(2)}, u32[]{:S(2)}) collective-permute-start(bf16[384,128]{1,0:T(8,128)(2,1)S(1)} %get-tuple-element.62.refs_0_), channel_id=1, source_target_pairs={{0,4},{2,6},{4,0},{6,2},{1,5},{3,7},{5,1},{7,3},{8,12},{10,14},{12... | collective-permute-start | bytes 294920 | tf_op jit(solution)/shard_map/ppermute | solution.py:480
  48.0 7.7 %collective-permute-start.10 = (bf16[384,128]{1,0:T(8,128)(2,1)S(1)}, bf16[384,128]{1,0:T(8,128)(2,1)S(1)}, u32[]{:S(2)}, u32[]{:S(2)}) collective-permute-start(bf16[384,128]{1,0:T(8,128)(2,1)S(1)} %get-tuple-element.62.refs_0_), channel_id=1, source_target_pairs={{0,2},{2,4},{4,6},{6,0},{1,3},{3,5},{5,7},{7,1},{8,10},{10,12},{12... | collective-permute-start | bytes 294920 | tf_op jit(solution)/shard_map/ppermute | solution.py:480
  48.6 14.5 %collective-permute-start.16 = (bf16[32,1024]{1,0:T(8,128)(2,1)S(1)}, bf16[32,1024]{1,0:T(8,128)(2,1)S(1)}, u32[]{:S(2)}, u32[]{:S(2)}) collective-permute-start(bf16[32,1024]{1,0:T(8,128)(2,1)S(1)} %get-tuple-element.71), channel_id=1, source_target_pairs={{0,2},{2,4},{4,6},{6,0},{1,3},{3,5},{5,7},{7,1},{8,10},{10,12},{12... | collective-permute-start | bytes 196616 | tf_op jit(solution)/shard_map/ppermute | solution.py:480
  58.1 10.7 %collective-permute-start.15 = (bf16[384,128]{1,0:T(8,128)(2,1)S(1)}, bf16[384,128]{1,0:T(8,128)(2,1)S(1)}, u32[]{:S(2)}, u32[]{:S(2)}) collective-permute-start(bf16[384,128]{1,0:T(8,128)(2,1)S(1)} %get-tuple-element.67.refs_0_), channel_id=1, source_target_pairs={{0,6},{2,0},{4,2},{6,4},{1,7},{3,1},{5,3},{7,5},{8,14},{10,8},{12,... | collective-permute-start | bytes 294920 | tf_op jit(solution)/shard_map/ppermute | solution.py:480
  58.9 9.9 %collective-permute-start.14 = (bf16[384,128]{1,0:T(8,128)(2,1)S(1)}, bf16[384,128]{1,0:T(8,128)(2,1)S(1)}, u32[]{:S(2)}, u32[]{:S(2)}) collective-permute-start(bf16[384,128]{1,0:T(8,128)(2,1)S(1)} %get-tuple-element.67.refs_0_), channel_id=1, source_target_pairs={{0,4},{2,6},{4,0},{6,2},{1,5},{3,7},{5,1},{7,3},{8,12},{10,14},{12... | collective-permute-start | bytes 294920 | tf_op jit(solution)/shard_map/ppermute | solution.py:480
  59.0 9.8 %collective-permute-start.13 = (bf16[384,128]{1,0:T(8,128)(2,1)S(1)}, bf16[384,128]{1,0:T(8,128)(2,1)S(1)}, u32[]{:S(2)}, u32[]{:S(2)}) collective-permute-start(bf16[384,128]{1,0:T(8,128)(2,1)S(1)} %get-tuple-element.67.refs_0_), channel_id=1, source_target_pairs={{0,2},{2,4},{4,6},{6,0},{1,3},{3,5},{5,7},{7,1},{8,10},{10,12},{12... | collective-permute-start | bytes 294920 | tf_op jit(solution)/shard_map/ppermute | solution.py:480
  61.0 7.3 %collective-permute-start.17 = (bf16[32,1024]{1,0:T(8,128)(2,1)S(1)}, bf16[32,1024]{1,0:T(8,128)(2,1)S(1)}, u32[]{:S(2)}, u32[]{:S(2)}) collective-permute-start(bf16[32,1024]{1,0:T(8,128)(2,1)S(1)} %get-tuple-element.72), channel_id=1, source_target_pairs={{0,4},{2,6},{4,0},{6,2},{1,5},{3,7},{5,1},{7,3},{8,12},{10,14},{12... | collective-permute-start | bytes 196616 | tf_op jit(solution)/shard_map/ppermute | solution.py:480
  63.1 5.7 %collective-permute-start.18 = (bf16[32,1024]{1,0:T(8,128)(2,1)S(1)}, bf16[32,1024]{1,0:T(8,128)(2,1)S(1)}, u32[]{:S(2)}, u32[]{:S(2)}) collective-permute-start(bf16[32,1024]{1,0:T(8,128)(2,1)S(1)} %get-tuple-element.73), channel_id=1, source_target_pairs={{0,6},{2,0},{4,2},{6,4},{1,7},{3,1},{5,3},{7,5},{8,14},{10,8},{12,... | collective-permute-start | bytes 196616 | tf_op jit(solution)/shard_map/ppermute | solution.py:480
  71.3 6.4 %collective-permute-start.21 = (bf16[512,128]{1,0:T(8,128)(2,1)S(1)}, bf16[512,128]{1,0:T(8,128)(2,1)S(1)}, u32[]{:S(2)}, u32[]{:S(2)}) collective-permute-start(bf16[512,128]{1,0:T(8,128)(2,1)S(1)} %get-tuple-element.74.refs_0_), channel_id=1, source_target_pairs={{0,6},{2,0},{4,2},{6,4},{1,7},{3,1},{5,3},{7,5},{8,14},{10,8},{12,... | collective-permute-start | bytes 393224 | tf_op jit(solution)/shard_map/ppermute | solution.py:480
  73.6 8.3 %collective-permute-start.20 = (bf16[512,128]{1,0:T(8,128)(2,1)S(1)}, bf16[512,128]{1,0:T(8,128)(2,1)S(1)}, u32[]{:S(2)}, u32[]{:S(2)}) collective-permute-start(bf16[512,128]{1,0:T(8,128)(2,1)S(1)} %get-tuple-element.74.refs_0_), channel_id=1, source_target_pairs={{0,4},{2,6},{4,0},{6,2},{1,5},{3,7},{5,1},{7,3},{8,12},{10,14},{12... | collective-permute-start | bytes 393224 | tf_op jit(solution)/shard_map/ppermute | solution.py:480
  73.6 8.3 %collective-permute-start.19 = (bf16[512,128]{1,0:T(8,128)(2,1)S(1)}, bf16[512,128]{1,0:T(8,128)(2,1)S(1)}, u32[]{:S(2)}, u32[]{:S(2)}) collective-permute-start(bf16[512,128]{1,0:T(8,128)(2,1)S(1)} %get-tuple-element.74.refs_0_), channel_id=1, source_target_pairs={{0,2},{2,4},{4,6},{6,0},{1,3},{3,5},{5,7},{7,1},{8,10},{10,12},{12... | collective-permute-start | bytes 393224 | tf_op jit(solution)/shard_map/ppermute | solution.py:480
  85.3 5.1 %collective-permute-start.24 = (bf16[272,128]{1,0:T(8,128)(2,1)S(1)}, bf16[272,128]{1,0:T(8,128)(2,1)S(1)}, u32[]{:S(2)}, u32[]{:S(2)}) collective-permute-start(bf16[272,128]{1,0:T(8,128)(2,1)S(1)} %get-tuple-element.78.refs_0_), channel_id=1, source_target_pairs={{0,6},{2,0},{4,2},{6,4},{1,7},{3,1},{5,3},{7,5},{8,14},{10,8},{12,... | collective-permute-start | bytes 208904 | tf_op jit(solution)/shard_map/ppermute | solution.py:480
  86.6 6.0 %collective-permute-start.23 = (bf16[272,128]{1,0:T(8,128)(2,1)S(1)}, bf16[272,128]{1,0:T(8,128)(2,1)S(1)}, u32[]{:S(2)}, u32[]{:S(2)}) collective-permute-start(bf16[272,128]{1,0:T(8,128)(2,1)S(1)} %get-tuple-element.78.refs_0_), channel_id=1, source_target_pairs={{0,4},{2,6},{4,0},{6,2},{1,5},{3,7},{5,1},{7,3},{8,12},{10,14},{12... | collective-permute-start | bytes 208904 | tf_op jit(solution)/shard_map/ppermute | solution.py:480
  87.2 6.1 %collective-permute-start.22 = (bf16[272,128]{1,0:T(8,128)(2,1)S(1)}, bf16[272,128]{1,0:T(8,128)(2,1)S(1)}, u32[]{:S(2)}, u32[]{:S(2)}) collective-permute-start(bf16[272,128]{1,0:T(8,128)(2,1)S(1)} %get-tuple-element.78.refs_0_), channel_id=1, source_target_pairs={{0,2},{2,4},{4,6},{6,0},{1,3},{3,5},{5,7},{7,1},{8,10},{10,12},{12... | collective-permute-start | bytes 208904 | tf_op jit(solution)/shard_map/ppermute | solution.py:480
  96.5 5.6 %collective-permute-start.26 = (bf16[144,128]{1,0:T(8,128)(2,1)S(1)}, bf16[144,128]{1,0:T(8,128)(2,1)S(1)}, u32[]{:S(2)}, u32[]{:S(2)}) collective-permute-start(bf16[144,128]{1,0:T(8,128)(2,1)S(1)} %get-tuple-element.87.refs_0_), channel_id=1, source_target_pairs={{0,4},{2,6},{4,0},{6,2},{1,5},{3,7},{5,1},{7,3},{8,12},{10,14},{12... | collective-permute-start | bytes 110600 | tf_op jit(solution)/shard_map/ppermute | solution.py:480
  96.7 5.8 %collective-permute-start.25 = (bf16[144,128]{1,0:T(8,128)(2,1)S(1)}, bf16[144,128]{1,0:T(8,128)(2,1)S(1)}, u32[]{:S(2)}, u32[]{:S(2)}) collective-permute-start(bf16[144,128]{1,0:T(8,128)(2,1)S(1)} %get-tuple-element.87.refs_0_), channel_id=1, source_target_pairs={{0,2},{2,4},{4,6},{6,0},{1,3},{3,5},{5,7},{7,1},{8,10},{10,12},{12... | collective-permute-start | bytes 110600 | tf_op jit(solution)/shard_map/ppermute | solution.py:480
  105.4 5.8 %collective-permute-start.28 = (bf16[144,128]{1,0:T(8,128)(2,1)S(1)}, bf16[144,128]{1,0:T(8,128)(2,1)S(1)}, u32[]{:S(2)}, u32[]{:S(2)}) collective-permute-start(bf16[144,128]{1,0:T(8,128)(2,1)S(1)} %get-tuple-element.93.refs_0_), channel_id=1, source_target_pairs={{0,2},{2,4},{4,6},{6,0},{1,3},{3,5},{5,7},{7,1},{8,10},{10,12},{12... | collective-permute-start | bytes 110600 | tf_op jit(solution)/shard_map/ppermute | solution.py:480
  107.4 5.3 %collective-permute-start.33 = (bf16[272,512]{1,0:T(8,128)(2,1)S(1)}, bf16[272,512]{1,0:T(8,128)(2,1)S(1)}, u32[]{:S(2)}, u32[]{:S(2)}) collective-permute-start(bf16[272,512]{1,0:T(8,128)(2,1)S(1)} %get-tuple-element.105), channel_id=1, source_target_pairs={{0,1},{1,0},{2,3},{3,2},{4,5},{5,4},{6,7},{7,6},{8,9},{9,8},{10,11... | collective-permute-start | bytes 835592 | tf_op jit(solution)/shard_map/ppermute | solution.py:486
  107.4 5.3 %collective-permute-start.34 = (bf16[272,512]{1,0:T(8,128)(2,1)S(1)}, bf16[272,512]{1,0:T(8,128)(2,1)S(1)}, u32[]{:S(2)}, u32[]{:S(2)}) collective-permute-start(bf16[272,512]{1,0:T(8,128)(2,1)S(1)} %get-tuple-element.106), channel_id=1, source_target_pairs={{0,1},{1,0},{2,3},{3,2},{4,5},{5,4},{6,7},{7,6},{8,9},{9,8},{10,11... | collective-permute-start | bytes 835592 | tf_op jit(solution)/shard_map/ppermute | solution.py:486
  114.8 9.6 %collective-permute-start.35 = (bf16[272,512]{1,0:T(8,128)(2,1)S(1)}, bf16[272,512]{1,0:T(8,128)(2,1)S(1)}, u32[]{:S(2)}, u32[]{:S(2)}) collective-permute-start(bf16[272,512]{1,0:T(8,128)(2,1)S(1)} %get-tuple-element.108), channel_id=1, source_target_pairs={{0,8},{8,0},{16,24},{24,16},{1,9},{9,1},{17,25},{25,17},{2,10},{10... | collective-permute-start | bytes 835592 | tf_op jit(solution)/shard_map/ppermute | solution.py:483
  116.3 12.9 %collective-permute-start.36 = (bf16[272,512]{1,0:T(8,128)(2,1)S(1)}, bf16[272,512]{1,0:T(8,128)(2,1)S(1)}, u32[]{:S(2)}, u32[]{:S(2)}) collective-permute-start(bf16[272,512]{1,0:T(8,128)(2,1)S(1)} %get-tuple-element.109), channel_id=1, source_target_pairs={{0,16},{8,24},{16,0},{24,8},{1,17},{9,25},{17,1},{25,9},{2,18},{10... | collective-permute-start | bytes 835592 | tf_op jit(solution)/shard_map/ppermute | solution.py:483
  117.3 13.4 %collective-permute-start.37 = (bf16[272,512]{1,0:T(8,128)(2,1)S(1)}, bf16[272,512]{1,0:T(8,128)(2,1)S(1)}, u32[]{:S(2)}, u32[]{:S(2)}) collective-permute-start(bf16[272,512]{1,0:T(8,128)(2,1)S(1)} %get-tuple-element.110), channel_id=1, source_target_pairs={{0,24},{8,16},{16,8},{24,0},{1,25},{9,17},{17,9},{25,1},{2,26},{10... | collective-permute-start | bytes 835592 | tf_op jit(solution)/shard_map/ppermute | solution.py:483
  (13 other events, 29.6 us)

commit v3 on v2

--- a/solution.py
+++ b/solution.py
@@ -12,6 +12,7 @@
 BF = jnp.bfloat16
 F32 = jnp.float32
 PARAMS = pltpu.CompilerParams(vmem_limit_bytes=48 * 1024 * 1024)
+PACK_PARAMS = pltpu.CompilerParams(vmem_limit_bytes=60 * 1024 * 1024)
 
 
 def dot(a, b):
@@ -45,9 +46,8 @@
 
 def pack_kernel(groups, micro_local, *refs):
     tokens, cotangents, starts, counts, gain, first, second = refs[:7]
-    token_parts, cot_parts = refs[7 : 7 + groups], refs[7 + groups : 7 + 2 * groups]
-    weights = refs[7 + 2 * groups]
-    tok, cot, starts_in, counts_in, gain_in, second_in, sems = refs[8 + 2 * groups :]
+    parts, weights = refs[7 : 7 + groups], refs[7 + groups]
+    tok, cot, starts_in, counts_in, gain_in, second_in, sems = refs[8 + groups :]
     directions, micro_count, length, width = tokens.shape
     local = width // groups
     own = first.shape[1]
@@ -104,10 +104,12 @@
         ).astype(BF)
         for shift in range(groups):
             start = pl.multiple_of(((group + shift) % groups) * local, local)
-            token_parts[shift][rows, 0:local] = tok[rows, pl.ds(start, local)]
-            token_parts[shift][rows, local:] = tail
+            parts[shift][rows, 0:local] = tok[rows, pl.ds(start, local)]
             cotangent = cot[rows, pl.ds(start, local)]
-            cot_parts[shift][rows, :] = jnp.where(keep, cotangent, jnp.zeros_like(cotangent))
+            parts[shift][rows, local : 2 * local] = jnp.where(
+                keep, cotangent, jnp.zeros_like(cotangent)
+            )
+            parts[shift][rows, 2 * local :] = tail
 
 
 def pack(tokens, cotangents, starts, counts, gain, first, second, groups, micro_local):
@@ -119,9 +121,8 @@
     results = pl.pallas_call(
         functools.partial(pack_kernel, groups, micro_local),
         in_specs=[pl.BlockSpec(memory_space=pltpu.HBM)] * 7,
-        out_specs=vmem_specs(2 * groups + 1),
-        out_shape=[shape((rows, local + HD), BF)] * groups
-        + [shape((rows, local), BF)] * groups
+        out_specs=vmem_specs(groups + 1),
+        out_shape=[shape((rows, 2 * local + HD), BF)] * groups
         + [shape((slice_rows(own), HD), BF)],
         scratch_shapes=[
             pltpu.VMEM((rows, width), BF),
@@ -132,10 +133,10 @@
             pltpu.VMEM(second.shape[1:], BF),
             pltpu.SemaphoreType.DMA((5 + 2 * micro_local,)),
         ],
-        compiler_params=PARAMS,
+        compiler_params=PACK_PARAMS,
         name="pack",
     )(tokens, cotangents, starts, counts, gain, first, second)
-    return results[:groups], results[groups : 2 * groups], results[2 * groups]
+    return results[:groups], results[groups]
 
 
 def head_gain(weights, head):
@@ -228,7 +229,7 @@
 def first_kernel(length, groups, sections, *refs):
     received, refs = refs[:groups], refs[groups:]
     mine, theirs = refs[:sections], refs[sections : 2 * sections]
-    x, mask, mean, probs, mixed, pay, weights, tails, sems = refs[2 * sections :]
+    x, cot, mask, mean, probs, mixed, pay, weights, tails, sems = refs[2 * sections :]
     section, core = lax.axis_index("pipe"), lax.axis_index("core")
     rows, local = x.shape
     size = block_size(rows)
@@ -243,8 +244,9 @@
             )
     for copy in copies:
         copy.start()
-    place_rows(received, tails, slice(local, None))
+    place_rows(received, tails, slice(2 * local, None))
     place_rows(received, x, slice(0, local))
+    place_rows(received, cot, slice(local, 2 * local))
     tail = tails[...].astype(F32)
     mean[...] = jnp.broadcast_to(tail[:, 1:2] + tail[:, 2:3], mean.shape)
     build_mask(tail[:, 0:1], mask, size, length)
@@ -272,22 +274,20 @@
         mask[block] = allowed.astype(F32).astype(BF)
 
 
-def middle_kernel(count, last, width, groups, *refs):
+def middle_kernel(count, last, width, *refs):
     pays, refs = refs[:count], refs[count:]
     x_before, mean_before, mask, weights_before, weights = refs[:5]
     refs = refs[5:]
     if last:
-        received, weights_after = refs[:groups], refs[groups]
-        refs = refs[groups + 1 :]
-    x, mean, reduced, cross, probs, mixed, pay = refs[:7]
+        cot, weights_after = refs[:2]
+        refs = refs[2:]
+    x, mean, reduced, cross, probs, mixed, pay = refs
     receive_forward(
         pays, x_before, mean_before, weights_before, width, x, mean, reduced, cross
     )
     attend(x, mean[:, 0:1], weights, mask, probs, mixed)
     send_forward(x, weights, mixed, pay)
     if last:
-        cot = refs[7]
-        place_rows(received, cot, slice(None))
         rows = x.shape[0]
         own = (weights.shape[2] - 16) // 2
         pay[2 * rows + HD :, :] = to_rank(cot[...], weights_after, own).astype(BF)
@@ -488,15 +488,14 @@
     def exchange(pay):
         return [pay] + [shifted(pay, shift) for shift in range(1, groups)]
 
-    token_parts, cot_parts, packed = pack(
+    token_parts, packed = pack(
         tokens, cotangents, starts, counts, layer_gains, first_map, second_map, groups, micro_local
     )
     received = [token_parts[0]]
     received += [shifted(token_parts[shift], shift) for shift in range(1, groups)]
     mine = [packed] + [across(packed, distance) for distance in range(1, sections)]
+    received, mine = lax.optimization_barrier((received, mine))
     theirs = [swapped(part) for part in mine]
-    cot_received = [cot_parts[0]]
-    cot_received += [shifted(cot_parts[shift], shift) for shift in range(1, groups)]
 
     def shaped(shape, kind=BF):
         return jax.ShapeDtypeStruct(shape, kind)
@@ -526,11 +525,12 @@
     def layer_of(index):
         return layer_spec(weights_shape.shape, index)
 
-    x, mask, mean, probs, mixed, pay, weights = call(
+    x, cot, mask, mean, probs, mixed, pay, weights = call(
         functools.partial(first_kernel, length, groups, sections),
         (*received, *mine, *theirs),
         vmem_specs(groups + 2 * sections),
         [
+            wide_shape,
             wide_shape,
             shaped((blocks, size, size)),
             mean_shape,
@@ -562,11 +562,10 @@
             shaped((forward_rows + (rows if last else 0), HD)),
         ]
         if last:
-            operands += (*cot_received, weights)
-            specs += vmem_specs(groups) + [layer_of(layer + 1)]
-            outs += [wide_shape]
-        x, mean, reduced, cross, probs, mixed, pay, *cots = call(
-            functools.partial(middle_kernel, len(pays), last, float(width), groups),
+            operands += (cot, weights)
+            specs += vmem_specs(1) + [layer_of(layer + 1)]
+        x, mean, reduced, cross, probs, mixed, pay = call(
+            functools.partial(middle_kernel, len(pays), last, float(width)),
             operands,
             specs,
             outs,
@@ -578,7 +577,6 @@
         crosses.append(cross)
         all_probs.append(probs)
         all_mixed.append(mixed)
-    cot = cots[0]
 
     pays = exchange(pay)
     back_rows = rows + 16 * blocks

time: 132 us -> 121 us (0.917)
  waiting for transfers between devices: 65.5 us -> 60 us
  local copies, waits for them, and re-layouts: 6.29 us -> 1.86 us
  starting transfers between devices: 40.4 us -> 38.7 us
    ppermute x6, waiting for transfers between devices: 24.1 us -> 14.1 us  [across(): lax.ppermute(value, 'pipe', [(i, i ^ distance) for i in range(sections)])]
    unnamed x14 -> x4, local copies, waits for them, and re-layouts: 6.29 us -> 1.86 us
    ppermute x24 -> x21, waiting for transfers between devices: 39.9 us -> 42.7 us  [shifted(): lax.ppermute(value, 'z', [(i, (i + shift) % groups) for i in range(groups)])]
    ppermute x8, waiting for transfers between devices: 1.53 us -> 3.18 us  [swapped(): return lax.ppermute(value, 'core', [(i, 1 - i) for i in range(sides)])]
    ppermute x24 -> x21, starting transfers between devices: 31.4 us -> 30 us  [shifted(): lax.ppermute(value, 'z', [(i, (i + shift) % groups) for i in range(groups)])]
  transfers between devices with their start and end apart: 38 -> 35, of which waited for: 24 -> 23; matrix products, arithmetic and copies ran while one was open for 0% -> 0% of each run, Pallas kernels for 3% -> 1%
where the time goes in v3:
time: 121 us
  waiting for transfers between devices  60 us (50%)
  starting transfers between devices  38.7 us (32%)
  Pallas kernels  19.9 us (16%)
  local copies, waits for them, and re-layouts  1.86 us (2%)
    ppermute x21, waiting for transfers between devices, shifted(): lax.ppermute(value, 'z', [(i, (i + shift) % groups) for i in range(groups)])  42.7 us
    ppermute x21, starting transfers between devices, shifted(): lax.ppermute(value, 'z', [(i, (i + shift) % groups) for i in range(groups)])  30 us
    pallas_call x9, Pallas kernels, call(): pl.pallas_call(kernel, grid=(1,), in_specs=specs, out_specs=vmem_specs(le...  17.6 us
    ppermute x6, waiting for transfers between devices, across(): lax.ppermute(value, 'pipe', [(i, i ^ distance) for i in range(sections)])  14.1 us
    ppermute x6, starting transfers between devices, across(): lax.ppermute(value, 'pipe', [(i, i ^ distance) for i in range(sections)])  7.04 us
    ppermute x8, waiting for transfers between devices, swapped(): return lax.ppermute(value, 'core', [(i, 1 - i) for i in range(sides)])  3.18 us
  transfers between devices with their start and end apart: 35, of which 23 were waited for; matrix products, arithmetic and copies ran while one was open for 0% of the time, Pallas kernels for 1%

profile of v3, /device:TPU:0, one launch (start us, length us, event | category | flops | bytes accessed | tf_op | source)
XLA Modules:
  0.0 121.2 jit_solution(9644080941862899665)
XLA Ops:
  0.6 2.3 %pack.1 = (bf16[32,2176]{1,0:T(8,128)(2,1)}, bf16[32,2176]{1,0:T(8,128)(2,1)}, bf16[32,2176]{1,0:T(8,128)(2,1)}, bf16[32,2176]{1,0:T(8,128)(2,1)}, bf16[1040,128]{1,0:T(8,128)(2,1)}) custom-call(bf16[2,2,32,4096]{3,2,1,0:T(8,128)(2,1)} %refs_0_.1, bf16[2,2,32,4096]{3,2,1,0:T(8,128)(2,1)} %refs_1_.1, s32[2,2,4]{2,1,0:T(2,128)} %refs_2_.1, s32[2,2]{1,0:T(2,128)} %refs_3_.1, ...), custom_call_target="tpu_custom_call" | custom-call | tf_op jit(solution)/shard_map/pack/pallas_call | solution.py:121
  2.9 3.1 %collective-permute-start = (bf16[32,2176]{1,0:T(8,128)(2,1)}, bf16[32,2176]{1,0:T(8,128)(2,1)S(1)}, u32[]{:S(2)}, u32[]{:S(2)}) collective-permute-start(bf16[32,2176]{1,0:T(8,128)(2,1)} %get-tuple-element.62), channel_id=1, source_target_pairs={{0,2},{2,4},{4,6},{6,0},{1,3},{3,5},{5,7},{7,1},{8,10},{10,12},{12... | collective-permute-start | bytes 417800 | tf_op jit(solution)/shard_map/ppermute | solution.py:480
  6.0 2.4 %collective-permute-start.5 = (bf16[1040,128]{1,0:T(8,128)(2,1)}, bf16[1040,128]{1,0:T(8,128)(2,1)S(1)}, u32[]{:S(2)}, u32[]{:S(2)}) collective-permute-start(bf16[1040,128]{1,0:T(8,128)(2,1)} %get-tuple-element.70.refs_4_), channel_id=1, source_target_pairs={{0,24},{8,16},{16,8},{24,0},{1,25},{9,17},{17,9},{25,1},{2,26},{10... | collective-permute-start | bytes 798728 | tf_op jit(solution)/shard_map/ppermute | solution.py:483
  9.5 2.6 %collective-permute-start.1 = (bf16[32,2176]{1,0:T(8,128)(2,1)}, bf16[32,2176]{1,0:T(8,128)(2,1)S(1)}, u32[]{:S(2)}, u32[]{:S(2)}) collective-permute-start(bf16[32,2176]{1,0:T(8,128)(2,1)} %get-tuple-element.63), channel_id=1, source_target_pairs={{0,4},{2,6},{4,0},{6,2},{1,5},{3,7},{5,1},{7,3},{8,12},{10,14},{12... | collective-permute-start | bytes 417800 | tf_op jit(solution)/shard_map/ppermute | solution.py:480
  12.1 1.6 %collective-permute-start.2 = (bf16[32,2176]{1,0:T(8,128)(2,1)}, bf16[32,2176]{1,0:T(8,128)(2,1)S(1)}, u32[]{:S(2)}, u32[]{:S(2)}) collective-permute-start(bf16[32,2176]{1,0:T(8,128)(2,1)} %get-tuple-element.64), channel_id=1, source_target_pairs={{0,6},{2,0},{4,2},{6,4},{1,7},{3,1},{5,3},{7,5},{8,14},{10,8},{12,... | collective-permute-start | bytes 417800 | tf_op jit(solution)/shard_map/ppermute | solution.py:480
  13.7 5.4 %collective-permute-done.1.refs_2_ = bf16[32,2176]{1,0:T(8,128)(2,1)S(1)} collective-permute-done((bf16[32,2176]{1,0:T(8,128)(2,1)}, bf16[32,2176]{1,0:T(8,128)(2,1)S(1)}, u32[]{:S(2)}, u32[]{:S(2)}) %collective-permute-start.1) | collective-permute-done | bytes 139296 | tf_op jit(solution)/shard_map/ppermute | solution.py:480
  19.1 1.6 %collective-permute-done.4.refs_6_ = bf16[1040,128]{1,0:T(8,128)(2,1)S(1)} collective-permute-done((bf16[1040,128]{1,0:T(8,128)(2,1)}, bf16[1040,128]{1,0:T(8,128)(2,1)S(1)}, u32[]{:S(2)}, u32[]{:S(2)}) %collective-permute-start.4) | collective-permute-done | bytes 266272 | tf_op jit(solution)/shard_map/ppermute | solution.py:483
  25.3 3.0 %forward_first.1 = (bf16[128,1024]{1,0:T(8,128)(2,1)S(1)}, bf16[128,1024]{1,0:T(8,128)(2,1)S(1)}, bf16[1,128,128]{2,1,0:T(8,128)(2,1)S(1)}, f32[128,128]{1,0:T(8...) custom-call(bf16[32,2176]{1,0:T(8,128)(2,1)S(1)} %copy-done.1, ...), custom_call_target="tpu_custom_call" | custom-call | tf_op jit(solution)/shard_map/forward_first/pallas_call | solution.py:514
  28.4 2.6 %collective-permute-start.12 = (bf16[384,128]{1,0:T(8,128)(2,1)S(1)}, bf16[384,128]{1,0:T(8,128)(2,1)S(1)}, u32[]{:S(2)}, u32[]{:S(2)}) collective-permute-start(bf16[384,128]{1,0:T(8,128)(2,1)S(1)} %get-tuple-element.74.refs_0_), channel_id=1, source_target_pairs={{0,6},{2,0},{4,2},{6,4},{1,7},{3,1},{5,3},{7,5},{8,14},{10,8},{12,... | collective-permute-start | bytes 294920 | tf_op jit(solution)/shard_map/ppermute | solution.py:480
  31.4 1.6 %collective-permute-start.10 = (bf16[384,128]{1,0:T(8,128)(2,1)S(1)}, bf16[384,128]{1,0:T(8,128)(2,1)S(1)}, u32[]{:S(2)}, u32[]{:S(2)}) collective-permute-start(bf16[384,128]{1,0:T(8,128)(2,1)S(1)} %get-tuple-element.74.refs_0_), channel_id=1, source_target_pairs={{0,2},{2,4},{4,6},{6,0},{1,3},{3,5},{5,7},{7,1},{8,10},{10,12},{12... | collective-permute-start | bytes 294920 | tf_op jit(solution)/shard_map/ppermute | solution.py:480
  34.2 6.5 %collective-permute-done.11.refs_2_ = bf16[384,128]{1,0:T(8,128)(2,1)S(1)} collective-permute-done((bf16[384,128]{1,0:T(8,128)(2,1)S(1)}, bf16[384,128]{1,0:T(8,128)(2,1)S(1)}, u32[]{:S(2)}, u32[]{:S(2)}) %collective-permute-start.11) | collective-permute-done | bytes 98336 | tf_op jit(solution)/shard_map/ppermute | solution.py:480
  40.6 2.4 %forward_middle.2 = (bf16[128,1024]{1,0:T(8,128)(2,1)S(1)}, f32[128,128]{1,0:T(8,128)S(1)}, bf16[128,128]{1,0:T(8,128)(2,1)S(1)}, f32[128,128]{1,0:T(8,128)S(1)}...) custom-call(bf16[384,128]{1,0:T(8,128)(2,1)S(1)} %get-tuple-element.74.refs_0_, ...), custom_call_target="tpu_custom_call" | custom-call | tf_op jit(solution)/shard_map/forward_middle/pallas_call | solution.py:514
  45.6 1.9 %collective-permute-start.13 = (bf16[384,128]{1,0:T(8,128)(2,1)S(1)}, bf16[384,128]{1,0:T(8,128)(2,1)S(1)}, u32[]{:S(2)}, u32[]{:S(2)}) collective-permute-start(bf16[384,128]{1,0:T(8,128)(2,1)S(1)} %get-tuple-element.79.refs_0_), channel_id=1, source_target_pairs={{0,2},{2,4},{4,6},{6,0},{1,3},{3,5},{5,7},{7,1},{8,10},{10,12},{12... | collective-permute-start | bytes 294920 | tf_op jit(solution)/shard_map/ppermute | solution.py:480
  47.7 7.1 %collective-permute-done.14.refs_2_ = bf16[384,128]{1,0:T(8,128)(2,1)S(1)} collective-permute-done((bf16[384,128]{1,0:T(8,128)(2,1)S(1)}, bf16[384,128]{1,0:T(8,128)(2,1)S(1)}, u32[]{:S(2)}, u32[]{:S(2)}) %collective-permute-start.14) | collective-permute-done | bytes 98336 | tf_op jit(solution)/shard_map/ppermute | solution.py:480
  54.8 2.5 %forward_middle.3 = (bf16[128,1024]{1,0:T(8,128)(2,1)S(1)}, f32[128,128]{1,0:T(8,128)S(1)}, bf16[128,128]{1,0:T(8,128)(2,1)S(1)}, f32[128,128]{1,0:T(8,128)S(1)}...) custom-call(bf16[384,128]{1,0:T(8,128)(2,1)S(1)} %get-tuple-element.79.refs_0_, ...), custom_call_target="tpu_custom_call" | custom-call | tf_op jit(solution)/shard_map/forward_middle/pallas_call | solution.py:514
  58.8 1.9 %collective-permute-start.16 = (bf16[512,128]{1,0:T(8,128)(2,1)S(1)}, bf16[512,128]{1,0:T(8,128)(2,1)S(1)}, u32[]{:S(2)}, u32[]{:S(2)}) collective-permute-start(bf16[512,128]{1,0:T(8,128)(2,1)S(1)} %get-tuple-element.83.refs_0_), channel_id=1, source_target_pairs={{0,2},{2,4},{4,6},{6,0},{1,3},{3,5},{5,7},{7,1},{8,10},{10,12},{12... | collective-permute-start | bytes 393224 | tf_op jit(solution)/shard_map/ppermute | solution.py:480
  60.8 2.0 %collective-permute-done.18.refs_3_ = bf16[512,128]{1,0:T(8,128)(2,1)S(1)} collective-permute-done((bf16[512,128]{1,0:T(8,128)(2,1)S(1)}, bf16[512,128]{1,0:T(8,128)(2,1)S(1)}, u32[]{:S(2)}, u32[]{:S(2)}) %collective-permute-start.18) | collective-permute-done | bytes 131104 | tf_op jit(solution)/shard_map/ppermute | solution.py:480
  62.7 8.1 %collective-permute-done.17.refs_2_ = bf16[512,128]{1,0:T(8,128)(2,1)S(1)} collective-permute-done((bf16[512,128]{1,0:T(8,128)(2,1)S(1)}, bf16[512,128]{1,0:T(8,128)(2,1)S(1)}, u32[]{:S(2)}, u32[]{:S(2)}) %collective-permute-start.17) | collective-permute-done | bytes 131104 | tf_op jit(solution)/shard_map/ppermute | solution.py:480
  70.9 3.3 %turn.1 = (bf16[128,1024]{1,0:T(8,128)(2,1)S(1)}, f32[128,128]{1,0:T(8,128)S(1)}, bf16[128,128]{1,0:T(8,128)(2,1)S(1)}, f32[128,128]{1,0:T(8,128)S(1)}, bf16[2,2...) custom-call(bf16[512,128]{1,0:T(8,128)(2,1)S(1)} %get-tuple-element.83.refs_0_, ...), custom_call_target="tpu_custom_call" | custom-call | tf_op jit(solution)/shard_map/turn/pallas_call | solution.py:514
  75.8 1.9 %collective-permute-start.19 = (bf16[272,128]{1,0:T(8,128)(2,1)S(1)}, bf16[272,128]{1,0:T(8,128)(2,1)S(1)}, u32[]{:S(2)}, u32[]{:S(2)}) collective-permute-start(bf16[272,128]{1,0:T(8,128)(2,1)S(1)} %get-tuple-element.86.refs_0_), channel_id=1, source_target_pairs={{0,2},{2,4},{4,6},{6,0},{1,3},{3,5},{5,7},{7,1},{8,10},{10,12},{12... | collective-permute-start | bytes 208904 | tf_op jit(solution)/shard_map/ppermute | solution.py:480
  79.0 3.6 %collective-permute-done.20.refs_2_ = bf16[272,128]{1,0:T(8,128)(2,1)S(1)} collective-permute-done((bf16[272,128]{1,0:T(8,128)(2,1)S(1)}, bf16[272,128]{1,0:T(8,128)(2,1)S(1)}, u32[]{:S(2)}, u32[]{:S(2)}) %collective-permute-start.20) | collective-permute-done | bytes 69664 | tf_op jit(solution)/shard_map/ppermute | solution.py:480
  82.5 1.7 %backward.3 = (bf16[272,512]{1,0:T(8,128)(2,1)S(1)}, bf16[272,512]{1,0:T(8,128)(2,1)S(1)}, bf16[272,512]{1,0:T(8,128)(2,1)S(1)}, bf16[272,512]{1,0:T(8,128)(2,1)...) custom-call(bf16[272,128]{1,0:T(8,128)(2,1)S(1)} %get-tuple-element.86.refs_0_, ...), custom_call_target="tpu_custom_call" | custom-call | tf_op jit(solution)/shard_map/backward/pallas_call | solution.py:514
  84.3 1.6 %collective-permute-start.24 = (bf16[144,128]{1,0:T(8,128)(2,1)S(1)}, bf16[144,128]{1,0:T(8,128)(2,1)S(1)}, u32[]{:S(2)}, u32[]{:S(2)}) collective-permute-start(bf16[144,128]{1,0:T(8,128)(2,1)S(1)} %get-tuple-element.95.refs_0_), channel_id=1, source_target_pairs={{0,6},{2,0},{4,2},{6,4},{1,7},{3,1},{5,3},{7,5},{8,14},{10,8},{12,... | collective-permute-start | bytes 110600 | tf_op jit(solution)/shard_map/ppermute | solution.py:480
  85.8 1.9 %collective-permute-start.22 = (bf16[144,128]{1,0:T(8,128)(2,1)S(1)}, bf16[144,128]{1,0:T(8,128)(2,1)S(1)}, u32[]{:S(2)}, u32[]{:S(2)}) collective-permute-start(bf16[144,128]{1,0:T(8,128)(2,1)S(1)} %get-tuple-element.95.refs_0_), channel_id=1, source_target_pairs={{0,2},{2,4},{4,6},{6,0},{1,3},{3,5},{5,7},{7,1},{8,10},{10,12},{12... | collective-permute-start | bytes 110600 | tf_op jit(solution)/shard_map/ppermute | solution.py:480
  88.3 2.9 %collective-permute-done.23.refs_2_ = bf16[144,128]{1,0:T(8,128)(2,1)S(1)} collective-permute-done((bf16[144,128]{1,0:T(8,128)(2,1)S(1)}, bf16[144,128]{1,0:T(8,128)(2,1)S(1)}, u32[]{:S(2)}, u32[]{:S(2)}) %collective-permute-start.23) | collective-permute-done | bytes 36896 | tf_op jit(solution)/shard_map/ppermute | solution.py:480
  91.6 1.7 %backward.4 = (bf16[272,512]{1,0:T(8,128)(2,1)S(1)}, bf16[272,512]{1,0:T(8,128)(2,1)S(1)}, bf16[128,1024]{1,0:T(8,128)(2,1)S(1)}, bf16[144,128]{1,0:T(8,128)(2,1)S(1)}) custom-call(bf16[144,128]{1,0:T(8,128)(2,1)S(1)} %get-tuple-element.95.refs_0_, bf16[144,128]{1,0:T(8,128)(2,1)S(1)} %collective-permute-done.22.refs_1_, ...), custom_call_target="tpu_custom_call" | custom-call | tf_op jit(solution)/shard_map/backward/pallas_call | solution.py:514
  94.9 1.6 %collective-permute-start.25 = (bf16[144,128]{1,0:T(8,128)(2,1)S(1)}, bf16[144,128]{1,0:T(8,128)(2,1)S(1)}, u32[]{:S(2)}, u32[]{:S(2)}) collective-permute-start(bf16[144,128]{1,0:T(8,128)(2,1)S(1)} %get-tuple-element.101.refs_0_), channel_id=1, source_target_pairs={{0,2},{2,4},{4,6},{6,0},{1,3},{3,5},{5,7},{7,1},{8,10},{10,12},{12... | collective-permute-start | bytes 110600 | tf_op jit(solution)/shard_map/ppermute | solution.py:480
  97.3 2.5 %collective-permute-done.26.refs_2_ = bf16[144,128]{1,0:T(8,128)(2,1)S(1)} collective-permute-done((bf16[144,128]{1,0:T(8,128)(2,1)S(1)}, bf16[144,128]{1,0:T(8,128)(2,1)S(1)}, u32[]{:S(2)}, u32[]{:S(2)}) %collective-permute-start.26) | collective-permute-done | bytes 36896 | tf_op jit(solution)/shard_map/ppermute | solution.py:480
  102.2 1.5 %collective-permute-done.28.refs_4_ = bf16[272,512]{1,0:T(8,128)(2,1)S(1)} collective-permute-done((bf16[272,512]{1,0:T(8,128)(2,1)S(1)}, bf16[272,512]{1,0:T(8,128)(2,1)S(1)}, u32[]{:S(2)}, u32[]{:S(2)}) %collective-permute-start.28) | collective-permute-done | bytes 278560 | tf_op jit(solution)/shard_map/ppermute | solution.py:486
  104.3 1.6 %collective-permute-start.32 = (bf16[272,512]{1,0:T(8,128)(2,1)S(1)}, bf16[272,512]{1,0:T(8,128)(2,1)S(1)}, u32[]{:S(2)}, u32[]{:S(2)}) collective-permute-start(bf16[272,512]{1,0:T(8,128)(2,1)S(1)} %get-tuple-element.116), channel_id=1, source_target_pairs={{0,8},{8,0},{16,24},{24,16},{1,9},{9,1},{17,25},{25,17},{2,10},{10... | collective-permute-start | bytes 835592 | tf_op jit(solution)/shard_map/ppermute | solution.py:483
  107.8 6.0 %collective-permute-done.32.refs_1_ = bf16[272,512]{1,0:T(8,128)(2,1)S(1)} collective-permute-done((bf16[272,512]{1,0:T(8,128)(2,1)S(1)}, bf16[272,512]{1,0:T(8,128)(2,1)S(1)}, u32[]{:S(2)}, u32[]{:S(2)}) %collective-permute-start.32) | collective-permute-done | bytes 278560 | tf_op jit(solution)/shard_map/ppermute | solution.py:483
  113.8 6.4 %collective-permute-done.33.refs_2_ = bf16[272,512]{1,0:T(8,128)(2,1)S(1)} collective-permute-done((bf16[272,512]{1,0:T(8,128)(2,1)S(1)}, bf16[272,512]{1,0:T(8,128)(2,1)S(1)}, u32[]{:S(2)}, u32[]{:S(2)}) %collective-permute-start.33) | collective-permute-done | bytes 278560 | tf_op jit(solution)/shard_map/ppermute | solution.py:483
  (52 shorter events, 23.7 us)
Async XLA Ops:
  2.9 9.2 %collective-permute-start = (bf16[32,2176]{1,0:T(8,128)(2,1)}, bf16[32,2176]{1,0:T(8,128)(2,1)S(1)}, u32[]{:S(2)}, u32[]{:S(2)}) collective-permute-start(bf16[32,2176]{1,0:T(8,128)(2,1)} %get-tuple-element.62), channel_id=1, source_target_pairs={{0,2},{2,4},{4,6},{6,0},{1,3},{3,5},{5,7},{7,1},{8,10},{10,12},{12... | collective-permute-start | bytes 417800 | tf_op jit(solution)/shard_map/ppermute | solution.py:480
  6.0 13.1 %collective-permute-start.5 = (bf16[1040,128]{1,0:T(8,128)(2,1)}, bf16[1040,128]{1,0:T(8,128)(2,1)S(1)}, u32[]{:S(2)}, u32[]{:S(2)}) collective-permute-start(bf16[1040,128]{1,0:T(8,128)(2,1)} %get-tuple-element.70.refs_4_), channel_id=1, source_target_pairs={{0,24},{8,16},{16,8},{24,0},{1,25},{9,17},{17,9},{25,1},{2,26},{10... | collective-permute-start | bytes 798728 | tf_op jit(solution)/shard_map/ppermute | solution.py:483
  8.5 12.2 %collective-permute-start.4 = (bf16[1040,128]{1,0:T(8,128)(2,1)}, bf16[1040,128]{1,0:T(8,128)(2,1)S(1)}, u32[]{:S(2)}, u32[]{:S(2)}) collective-permute-start(bf16[1040,128]{1,0:T(8,128)(2,1)} %get-tuple-element.70.refs_4_), channel_id=1, source_target_pairs={{0,16},{8,24},{16,0},{24,8},{1,17},{9,25},{17,1},{25,9},{2,18},{10... | collective-permute-start | bytes 798728 | tf_op jit(solution)/shard_map/ppermute | solution.py:483
  9.0 11.8 %collective-permute-start.3 = (bf16[1040,128]{1,0:T(8,128)(2,1)}, bf16[1040,128]{1,0:T(8,128)(2,1)S(1)}, u32[]{:S(2)}, u32[]{:S(2)}) collective-permute-start(bf16[1040,128]{1,0:T(8,128)(2,1)} %get-tuple-element.70.refs_4_), channel_id=1, source_target_pairs={{0,8},{8,0},{16,24},{24,16},{1,9},{9,1},{17,25},{25,17},{2,10},{10... | collective-permute-start | bytes 798728 | tf_op jit(solution)/shard_map/ppermute | solution.py:483
  9.5 9.6 %collective-permute-start.1 = (bf16[32,2176]{1,0:T(8,128)(2,1)}, bf16[32,2176]{1,0:T(8,128)(2,1)S(1)}, u32[]{:S(2)}, u32[]{:S(2)}) collective-permute-start(bf16[32,2176]{1,0:T(8,128)(2,1)} %get-tuple-element.63), channel_id=1, source_target_pairs={{0,4},{2,6},{4,0},{6,2},{1,5},{3,7},{5,1},{7,3},{8,12},{10,14},{12... | collective-permute-start | bytes 417800 | tf_op jit(solution)/shard_map/ppermute | solution.py:480
  12.1 7.0 %collective-permute-start.2 = (bf16[32,2176]{1,0:T(8,128)(2,1)}, bf16[32,2176]{1,0:T(8,128)(2,1)S(1)}, u32[]{:S(2)}, u32[]{:S(2)}) collective-permute-start(bf16[32,2176]{1,0:T(8,128)(2,1)} %get-tuple-element.64), channel_id=1, source_target_pairs={{0,6},{2,0},{4,2},{6,4},{1,7},{3,1},{5,3},{7,5},{8,14},{10,8},{12,... | collective-permute-start | bytes 417800 | tf_op jit(solution)/shard_map/ppermute | solution.py:480
  20.8 2.1 %collective-permute-start.6 = (bf16[1040,128]{1,0:T(8,128)(2,1)}, bf16[1040,128]{1,0:T(8,128)(2,1)S(1)}, u32[]{:S(2)}, u32[]{:S(2)}) collective-permute-start(bf16[1040,128]{1,0:T(8,128)(2,1)} %get-tuple-element.70.refs_4_), channel_id=1, source_target_pairs={{0,1},{1,0},{2,3},{3,2},{4,5},{5,4},{6,7},{7,6},{8,9},{9,8},{10,11... | collective-permute-start | bytes 798728 | tf_op jit(solution)/shard_map/ppermute | solution.py:486
  21.3 2.2 %collective-permute-start.9 = (bf16[1040,128]{1,0:T(8,128)(2,1)S(1)}, bf16[1040,128]{1,0:T(8,128)(2,1)S(1)}, u32[]{:S(2)}, u32[]{:S(2)}) collective-permute-start(bf16[1040,128]{1,0:T(8,128)(2,1)S(1)} %collective-permute-done.5.refs_7_), channel_id=1, source_target_pairs={{0,1},{1,0},{2,3},{3,2},{4,5},{5,4},{6,7},{7,6},{8,9},{9,8},{10,11... | collective-permute-start | bytes 798728 | tf_op jit(solution)/shard_map/ppermute | solution.py:486
  28.4 5.8 %collective-permute-start.12 = (bf16[384,128]{1,0:T(8,128)(2,1)S(1)}, bf16[384,128]{1,0:T(8,128)(2,1)S(1)}, u32[]{:S(2)}, u32[]{:S(2)}) collective-permute-start(bf16[384,128]{1,0:T(8,128)(2,1)S(1)} %get-tuple-element.74.refs_0_), channel_id=1, source_target_pairs={{0,6},{2,0},{4,2},{6,4},{1,7},{3,1},{5,3},{7,5},{8,14},{10,8},{12,... | collective-permute-start | bytes 294920 | tf_op jit(solution)/shard_map/ppermute | solution.py:480
  31.0 9.7 %collective-permute-start.11 = (bf16[384,128]{1,0:T(8,128)(2,1)S(1)}, bf16[384,128]{1,0:T(8,128)(2,1)S(1)}, u32[]{:S(2)}, u32[]{:S(2)}) collective-permute-start(bf16[384,128]{1,0:T(8,128)(2,1)S(1)} %get-tuple-element.74.refs_0_), channel_id=1, source_target_pairs={{0,4},{2,6},{4,0},{6,2},{1,5},{3,7},{5,1},{7,3},{8,12},{10,14},{12... | collective-permute-start | bytes 294920 | tf_op jit(solution)/shard_map/ppermute | solution.py:480
  31.4 9.2 %collective-permute-start.10 = (bf16[384,128]{1,0:T(8,128)(2,1)S(1)}, bf16[384,128]{1,0:T(8,128)(2,1)S(1)}, u32[]{:S(2)}, u32[]{:S(2)}) collective-permute-start(bf16[384,128]{1,0:T(8,128)(2,1)S(1)} %get-tuple-element.74.refs_0_), channel_id=1, source_target_pairs={{0,2},{2,4},{4,6},{6,0},{1,3},{3,5},{5,7},{7,1},{8,10},{10,12},{12... | collective-permute-start | bytes 294920 | tf_op jit(solution)/shard_map/ppermute | solution.py:480
  43.0 4.7 %collective-permute-start.15 = (bf16[384,128]{1,0:T(8,128)(2,1)S(1)}, bf16[384,128]{1,0:T(8,128)(2,1)S(1)}, u32[]{:S(2)}, u32[]{:S(2)}) collective-permute-start(bf16[384,128]{1,0:T(8,128)(2,1)S(1)} %get-tuple-element.79.refs_0_), channel_id=1, source_target_pairs={{0,6},{2,0},{4,2},{6,4},{1,7},{3,1},{5,3},{7,5},{8,14},{10,8},{12,... | collective-permute-start | bytes 294920 | tf_op jit(solution)/shard_map/ppermute | solution.py:480
  44.4 10.4 %collective-permute-start.14 = (bf16[384,128]{1,0:T(8,128)(2,1)S(1)}, bf16[384,128]{1,0:T(8,128)(2,1)S(1)}, u32[]{:S(2)}, u32[]{:S(2)}) collective-permute-start(bf16[384,128]{1,0:T(8,128)(2,1)S(1)} %get-tuple-element.79.refs_0_), channel_id=1, source_target_pairs={{0,4},{2,6},{4,0},{6,2},{1,5},{3,7},{5,1},{7,3},{8,12},{10,14},{12... | collective-permute-start | bytes 294920 | tf_op jit(solution)/shard_map/ppermute | solution.py:480
  45.6 9.2 %collective-permute-start.13 = (bf16[384,128]{1,0:T(8,128)(2,1)S(1)}, bf16[384,128]{1,0:T(8,128)(2,1)S(1)}, u32[]{:S(2)}, u32[]{:S(2)}) collective-permute-start(bf16[384,128]{1,0:T(8,128)(2,1)S(1)} %get-tuple-element.79.refs_0_), channel_id=1, source_target_pairs={{0,2},{2,4},{4,6},{6,0},{1,3},{3,5},{5,7},{7,1},{8,10},{10,12},{12... | collective-permute-start | bytes 294920 | tf_op jit(solution)/shard_map/ppermute | solution.py:480
  57.3 5.5 %collective-permute-start.18 = (bf16[512,128]{1,0:T(8,128)(2,1)S(1)}, bf16[512,128]{1,0:T(8,128)(2,1)S(1)}, u32[]{:S(2)}, u32[]{:S(2)}) collective-permute-start(bf16[512,128]{1,0:T(8,128)(2,1)S(1)} %get-tuple-element.83.refs_0_), channel_id=1, source_target_pairs={{0,6},{2,0},{4,2},{6,4},{1,7},{3,1},{5,3},{7,5},{8,14},{10,8},{12,... | collective-permute-start | bytes 393224 | tf_op jit(solution)/shard_map/ppermute | solution.py:480
  57.6 13.2 %collective-permute-start.17 = (bf16[512,128]{1,0:T(8,128)(2,1)S(1)}, bf16[512,128]{1,0:T(8,128)(2,1)S(1)}, u32[]{:S(2)}, u32[]{:S(2)}) collective-permute-start(bf16[512,128]{1,0:T(8,128)(2,1)S(1)} %get-tuple-element.83.refs_0_), channel_id=1, source_target_pairs={{0,4},{2,6},{4,0},{6,2},{1,5},{3,7},{5,1},{7,3},{8,12},{10,14},{12... | collective-permute-start | bytes 393224 | tf_op jit(solution)/shard_map/ppermute | solution.py:480
  58.8 12.0 %collective-permute-start.16 = (bf16[512,128]{1,0:T(8,128)(2,1)S(1)}, bf16[512,128]{1,0:T(8,128)(2,1)S(1)}, u32[]{:S(2)}, u32[]{:S(2)}) collective-permute-start(bf16[512,128]{1,0:T(8,128)(2,1)S(1)} %get-tuple-element.83.refs_0_), channel_id=1, source_target_pairs={{0,2},{2,4},{4,6},{6,0},{1,3},{3,5},{5,7},{7,1},{8,10},{10,12},{12... | collective-permute-start | bytes 393224 | tf_op jit(solution)/shard_map/ppermute | solution.py:480
  74.2 4.8 %collective-permute-start.21 = (bf16[272,128]{1,0:T(8,128)(2,1)S(1)}, bf16[272,128]{1,0:T(8,128)(2,1)S(1)}, u32[]{:S(2)}, u32[]{:S(2)}) collective-permute-start(bf16[272,128]{1,0:T(8,128)(2,1)S(1)} %get-tuple-element.86.refs_0_), channel_id=1, source_target_pairs={{0,6},{2,0},{4,2},{6,4},{1,7},{3,1},{5,3},{7,5},{8,14},{10,8},{12,... | collective-permute-start | bytes 208904 | tf_op jit(solution)/shard_map/ppermute | solution.py:480
  74.3 8.3 %collective-permute-start.20 = (bf16[272,128]{1,0:T(8,128)(2,1)S(1)}, bf16[272,128]{1,0:T(8,128)(2,1)S(1)}, u32[]{:S(2)}, u32[]{:S(2)}) collective-permute-start(bf16[272,128]{1,0:T(8,128)(2,1)S(1)} %get-tuple-element.86.refs_0_), channel_id=1, source_target_pairs={{0,4},{2,6},{4,0},{6,2},{1,5},{3,7},{5,1},{7,3},{8,12},{10,14},{12... | collective-permute-start | bytes 208904 | tf_op jit(solution)/shard_map/ppermute | solution.py:480
  75.8 6.8 %collective-permute-start.19 = (bf16[272,128]{1,0:T(8,128)(2,1)S(1)}, bf16[272,128]{1,0:T(8,128)(2,1)S(1)}, u32[]{:S(2)}, u32[]{:S(2)}) collective-permute-start(bf16[272,128]{1,0:T(8,128)(2,1)S(1)} %get-tuple-element.86.refs_0_), channel_id=1, source_target_pairs={{0,2},{2,4},{4,6},{6,0},{1,3},{3,5},{5,7},{7,1},{8,10},{10,12},{12... | collective-permute-start | bytes 208904 | tf_op jit(solution)/shard_map/ppermute | solution.py:480
  84.3 4.0 %collective-permute-start.24 = (bf16[144,128]{1,0:T(8,128)(2,1)S(1)}, bf16[144,128]{1,0:T(8,128)(2,1)S(1)}, u32[]{:S(2)}, u32[]{:S(2)}) collective-permute-start(bf16[144,128]{1,0:T(8,128)(2,1)S(1)} %get-tuple-element.95.refs_0_), channel_id=1, source_target_pairs={{0,6},{2,0},{4,2},{6,4},{1,7},{3,1},{5,3},{7,5},{8,14},{10,8},{12,... | collective-permute-start | bytes 110600 | tf_op jit(solution)/shard_map/ppermute | solution.py:480
  85.8 5.3 %collective-permute-start.23 = (bf16[144,128]{1,0:T(8,128)(2,1)S(1)}, bf16[144,128]{1,0:T(8,128)(2,1)S(1)}, u32[]{:S(2)}, u32[]{:S(2)}) collective-permute-start(bf16[144,128]{1,0:T(8,128)(2,1)S(1)} %get-tuple-element.95.refs_0_), channel_id=1, source_target_pairs={{0,4},{2,6},{4,0},{6,2},{1,5},{3,7},{5,1},{7,3},{8,12},{10,14},{12... | collective-permute-start | bytes 110600 | tf_op jit(solution)/shard_map/ppermute | solution.py:480
  85.8 5.8 %collective-permute-start.22 = (bf16[144,128]{1,0:T(8,128)(2,1)S(1)}, bf16[144,128]{1,0:T(8,128)(2,1)S(1)}, u32[]{:S(2)}, u32[]{:S(2)}) collective-permute-start(bf16[144,128]{1,0:T(8,128)(2,1)S(1)} %get-tuple-element.95.refs_0_), channel_id=1, source_target_pairs={{0,2},{2,4},{4,6},{6,0},{1,3},{3,5},{5,7},{7,1},{8,10},{10,12},{12... | collective-permute-start | bytes 110600 | tf_op jit(solution)/shard_map/ppermute | solution.py:480
  93.3 4.0 %collective-permute-start.27 = (bf16[144,128]{1,0:T(8,128)(2,1)S(1)}, bf16[144,128]{1,0:T(8,128)(2,1)S(1)}, u32[]{:S(2)}, u32[]{:S(2)}) collective-permute-start(bf16[144,128]{1,0:T(8,128)(2,1)S(1)} %get-tuple-element.101.refs_0_), channel_id=1, source_target_pairs={{0,6},{2,0},{4,2},{6,4},{1,7},{3,1},{5,3},{7,5},{8,14},{10,8},{12,... | collective-permute-start | bytes 110600 | tf_op jit(solution)/shard_map/ppermute | solution.py:480
  94.6 5.3 %collective-permute-start.26 = (bf16[144,128]{1,0:T(8,128)(2,1)S(1)}, bf16[144,128]{1,0:T(8,128)(2,1)S(1)}, u32[]{:S(2)}, u32[]{:S(2)}) collective-permute-start(bf16[144,128]{1,0:T(8,128)(2,1)S(1)} %get-tuple-element.101.refs_0_), channel_id=1, source_target_pairs={{0,4},{2,6},{4,0},{6,2},{1,5},{3,7},{5,1},{7,3},{8,12},{10,14},{12... | collective-permute-start | bytes 110600 | tf_op jit(solution)/shard_map/ppermute | solution.py:480
  94.9 5.8 %collective-permute-start.25 = (bf16[144,128]{1,0:T(8,128)(2,1)S(1)}, bf16[144,128]{1,0:T(8,128)(2,1)S(1)}, u32[]{:S(2)}, u32[]{:S(2)}) collective-permute-start(bf16[144,128]{1,0:T(8,128)(2,1)S(1)} %get-tuple-element.101.refs_0_), channel_id=1, source_target_pairs={{0,2},{2,4},{4,6},{6,0},{1,3},{3,5},{5,7},{7,1},{8,10},{10,12},{12... | collective-permute-start | bytes 110600 | tf_op jit(solution)/shard_map/ppermute | solution.py:480
  96.5 5.7 %collective-permute-start.30 = (bf16[272,512]{1,0:T(8,128)(2,1)S(1)}, bf16[272,512]{1,0:T(8,128)(2,1)S(1)}, u32[]{:S(2)}, u32[]{:S(2)}) collective-permute-start(bf16[272,512]{1,0:T(8,128)(2,1)S(1)} %get-tuple-element.113), channel_id=1, source_target_pairs={{0,1},{1,0},{2,3},{3,2},{4,5},{5,4},{6,7},{7,6},{8,9},{9,8},{10,11... | collective-permute-start | bytes 835592 | tf_op jit(solution)/shard_map/ppermute | solution.py:486
  96.5 5.7 %collective-permute-start.31 = (bf16[272,512]{1,0:T(8,128)(2,1)S(1)}, bf16[272,512]{1,0:T(8,128)(2,1)S(1)}, u32[]{:S(2)}, u32[]{:S(2)}) collective-permute-start(bf16[272,512]{1,0:T(8,128)(2,1)S(1)} %get-tuple-element.114), channel_id=1, source_target_pairs={{0,1},{1,0},{2,3},{3,2},{4,5},{5,4},{6,7},{7,6},{8,9},{9,8},{10,11... | collective-permute-start | bytes 835592 | tf_op jit(solution)/shard_map/ppermute | solution.py:486
  97.3 4.9 %collective-permute-start.29 = (bf16[272,512]{1,0:T(8,128)(2,1)S(1)}, bf16[272,512]{1,0:T(8,128)(2,1)S(1)}, u32[]{:S(2)}, u32[]{:S(2)}) collective-permute-start(bf16[272,512]{1,0:T(8,128)(2,1)S(1)} %get-tuple-element.112), channel_id=1, source_target_pairs={{0,1},{1,0},{2,3},{3,2},{4,5},{5,4},{6,7},{7,6},{8,9},{9,8},{10,11... | collective-permute-start | bytes 835592 | tf_op jit(solution)/shard_map/ppermute | solution.py:486
  104.3 9.6 %collective-permute-start.32 = (bf16[272,512]{1,0:T(8,128)(2,1)S(1)}, bf16[272,512]{1,0:T(8,128)(2,1)S(1)}, u32[]{:S(2)}, u32[]{:S(2)}) collective-permute-start(bf16[272,512]{1,0:T(8,128)(2,1)S(1)} %get-tuple-element.116), channel_id=1, source_target_pairs={{0,8},{8,0},{16,24},{24,16},{1,9},{9,1},{17,25},{25,17},{2,10},{10... | collective-permute-start | bytes 835592 | tf_op jit(solution)/shard_map/ppermute | solution.py:483
  105.8 14.4 %collective-permute-start.33 = (bf16[272,512]{1,0:T(8,128)(2,1)S(1)}, bf16[272,512]{1,0:T(8,128)(2,1)S(1)}, u32[]{:S(2)}, u32[]{:S(2)}) collective-permute-start(bf16[272,512]{1,0:T(8,128)(2,1)S(1)} %get-tuple-element.117), channel_id=1, source_target_pairs={{0,16},{8,24},{16,0},{24,8},{1,17},{9,25},{17,1},{25,9},{2,18},{10... | collective-permute-start | bytes 835592 | tf_op jit(solution)/shard_map/ppermute | solution.py:483
  106.4 13.8 %collective-permute-start.34 = (bf16[272,512]{1,0:T(8,128)(2,1)S(1)}, bf16[272,512]{1,0:T(8,128)(2,1)S(1)}, u32[]{:S(2)}, u32[]{:S(2)}) collective-permute-start(bf16[272,512]{1,0:T(8,128)(2,1)S(1)} %get-tuple-element.118), channel_id=1, source_target_pairs={{0,24},{8,16},{16,8},{24,0},{1,25},{9,17},{17,9},{25,1},{2,26},{10... | collective-permute-start | bytes 835592 | tf_op jit(solution)/shard_map/ppermute | solution.py:483
  (5 other events, 7.4 us)

commit v4 on v3

--- a/solution.py
+++ b/solution.py
@@ -439,6 +439,10 @@
     split_sides(grads, keep, send)
 
 
+def add_kernel(near, far, total):
+    total[...] = (near[...].astype(F32) + far[...].astype(F32)).astype(BF)
+
+
 def combine_kernel(sections, *refs):
     kept, swapped = refs[:sections], refs[sections : 2 * sections]
     outs, sums = refs[2 * sections : 3 * sections], refs[3 * sections]
@@ -486,7 +490,13 @@
         return lax.ppermute(value, "core", [(i, 1 - i) for i in range(sides)])
 
     def exchange(pay):
-        return [pay] + [shifted(pay, shift) for shift in range(1, groups)]
+        distance = 1
+        while True:
+            far = lax.ppermute(pay, "z", [(i, i ^ distance) for i in range(groups)])
+            distance *= 2
+            if distance >= groups:
+                return [pay, far]
+            pay = call(add_kernel, (pay, far), vmem_specs(2), [shaped(pay.shape)], "add_pair")[0]
 
     token_parts, packed = pack(
         tokens, cotangents, starts, counts, layer_gains, first_map, second_map, groups, micro_local

time: 121 us -> 126 us (1.041)
  waiting for transfers between devices: 60 us -> 78.7 us
  starting transfers between devices: 38.7 us -> 24.2 us
    ppermute x0 -> x12, waiting for transfers between devices: none -> 56.1 us  [exchange(): far = lax.ppermute(pay, 'z', [(i, i ^ distance) for i in range(groups)])]
    ppermute x21 -> x3, waiting for transfers between devices: 42.7 us -> 5.41 us  [shifted(): lax.ppermute(value, 'z', [(i, (i + shift) % groups) for i in range(groups)])]
    ppermute x21 -> x3, starting transfers between devices: 30 us -> 7.23 us  [shifted(): lax.ppermute(value, 'z', [(i, (i + shift) % groups) for i in range(groups)])]
    ppermute x0 -> x12, starting transfers between devices: none -> 8.28 us  [exchange(): far = lax.ppermute(pay, 'z', [(i, i ^ distance) for i in range(groups)])]
    pallas_call x9 -> x15, Pallas kernels: 17.6 us -> 17.7 us  [call(): pl.pallas_call(kernel, grid=(1,), in_specs=specs, out_specs=vmem_specs(le...]
  transfers between devices with their start and end apart: 35 -> 29, of which waited for: 23 -> 21; matrix products, arithmetic and copies ran while one was open for 0% -> 0% of each run, Pallas kernels for 1% -> 1%
where the time goes in v4:
time: 126 us
  waiting for transfers between devices  78.7 us (62%)
  starting transfers between devices  24.2 us (19%)
  Pallas kernels  20 us (16%)
  local copies, waits for them, and re-layouts  1.86 us (1%)
    ppermute x12, waiting for transfers between devices, exchange(): far = lax.ppermute(pay, 'z', [(i, i ^ distance) for i in range(groups)])  56.1 us
    pallas_call x15, Pallas kernels, call(): pl.pallas_call(kernel, grid=(1,), in_specs=specs, out_specs=vmem_specs(le...  17.7 us
    ppermute x6, waiting for transfers between devices, across(): lax.ppermute(value, 'pipe', [(i, i ^ distance) for i in range(sections)])  14.1 us
    ppermute x12, starting transfers between devices, exchange(): far = lax.ppermute(pay, 'z', [(i, i ^ distance) for i in range(groups)])  8.28 us
    ppermute x3, starting transfers between devices, shifted(): lax.ppermute(value, 'z', [(i, (i + shift) % groups) for i in range(groups)])  7.23 us
    ppermute x6, starting transfers between devices, across(): lax.ppermute(value, 'pipe', [(i, i ^ distance) for i in range(sections)])  7.04 us
    ppermute x3, waiting for transfers between devices, shifted(): lax.ppermute(value, 'z', [(i, (i + shift) % groups) for i in range(groups)])  5.41 us
    ppermute x8, waiting for transfers between devices, swapped(): return lax.ppermute(value, 'core', [(i, 1 - i) for i in range(sides)])  3.18 us
  transfers between devices with their start and end apart: 29, of which 21 were waited for; matrix products, arithmetic and copies ran while one was open for 0% of the time, Pallas kernels for 1%

profile of v4, /device:TPU:0, one launch (start us, length us, event | category | flops | bytes accessed | tf_op | source)
XLA Modules:
  0.0 125.5 jit_solution(2227736780154486045)
XLA Ops:
  0.6 2.3 %pack.1 = (bf16[32,2176]{1,0:T(8,128)(2,1)}, bf16[32,2176]{1,0:T(8,128)(2,1)}, bf16[32,2176]{1,0:T(8,128)(2,1)}, bf16[32,2176]{1,0:T(8,128)(2,1)}, bf16[1040,128]{1,0:T(8,128)(2,1)}) custom-call(bf16[2,2,32,4096]{3,2,1,0:T(8,128)(2,1)} %refs_0_.1, bf16[2,2,32,4096]{3,2,1,0:T(8,128)(2,1)} %refs_1_.1, s32[2,2,4]{2,1,0:T(2,128)} %refs_2_.1, s32[2,2]{1,0:T(2,128)} %refs_3_.1, ...), custom_call_target="tpu_custom_call" | custom-call | tf_op jit(solution)/shard_map/pack/pallas_call | solution.py:121
  2.9 3.1 %collective-permute-start = (bf16[32,2176]{1,0:T(8,128)(2,1)}, bf16[32,2176]{1,0:T(8,128)(2,1)S(1)}, u32[]{:S(2)}, u32[]{:S(2)}) collective-permute-start(bf16[32,2176]{1,0:T(8,128)(2,1)} %get-tuple-element.62), channel_id=1, source_target_pairs={{0,2},{2,4},{4,6},{6,0},{1,3},{3,5},{5,7},{7,1},{8,10},{10,12},{12... | collective-permute-start | bytes 417800 | tf_op jit(solution)/shard_map/ppermute | solution.py:484
  6.0 2.4 %collective-permute-start.5 = (bf16[1040,128]{1,0:T(8,128)(2,1)}, bf16[1040,128]{1,0:T(8,128)(2,1)S(1)}, u32[]{:S(2)}, u32[]{:S(2)}) collective-permute-start(bf16[1040,128]{1,0:T(8,128)(2,1)} %get-tuple-element.70.refs_4_), channel_id=1, source_target_pairs={{0,24},{8,16},{16,8},{24,0},{1,25},{9,17},{17,9},{25,1},{2,26},{10... | collective-permute-start | bytes 798728 | tf_op jit(solution)/shard_map/ppermute | solution.py:487
  9.5 2.6 %collective-permute-start.1 = (bf16[32,2176]{1,0:T(8,128)(2,1)}, bf16[32,2176]{1,0:T(8,128)(2,1)S(1)}, u32[]{:S(2)}, u32[]{:S(2)}) collective-permute-start(bf16[32,2176]{1,0:T(8,128)(2,1)} %get-tuple-element.63), channel_id=1, source_target_pairs={{0,4},{2,6},{4,0},{6,2},{1,5},{3,7},{5,1},{7,3},{8,12},{10,14},{12... | collective-permute-start | bytes 417800 | tf_op jit(solution)/shard_map/ppermute | solution.py:484
  12.1 1.6 %collective-permute-start.2 = (bf16[32,2176]{1,0:T(8,128)(2,1)}, bf16[32,2176]{1,0:T(8,128)(2,1)S(1)}, u32[]{:S(2)}, u32[]{:S(2)}) collective-permute-start(bf16[32,2176]{1,0:T(8,128)(2,1)} %get-tuple-element.64), channel_id=1, source_target_pairs={{0,6},{2,0},{4,2},{6,4},{1,7},{3,1},{5,3},{7,5},{8,14},{10,8},{12,... | collective-permute-start | bytes 417800 | tf_op jit(solution)/shard_map/ppermute | solution.py:484
  13.7 5.4 %collective-permute-done.1.refs_2_ = bf16[32,2176]{1,0:T(8,128)(2,1)S(1)} collective-permute-done((bf16[32,2176]{1,0:T(8,128)(2,1)}, bf16[32,2176]{1,0:T(8,128)(2,1)S(1)}, u32[]{:S(2)}, u32[]{:S(2)}) %collective-permute-start.1) | collective-permute-done | bytes 139296 | tf_op jit(solution)/shard_map/ppermute | solution.py:484
  19.1 1.6 %collective-permute-done.4.refs_6_ = bf16[1040,128]{1,0:T(8,128)(2,1)S(1)} collective-permute-done((bf16[1040,128]{1,0:T(8,128)(2,1)}, bf16[1040,128]{1,0:T(8,128)(2,1)S(1)}, u32[]{:S(2)}, u32[]{:S(2)}) %collective-permute-start.4) | collective-permute-done | bytes 266272 | tf_op jit(solution)/shard_map/ppermute | solution.py:487
  25.3 3.0 %forward_first.1 = (bf16[128,1024]{1,0:T(8,128)(2,1)S(1)}, bf16[128,1024]{1,0:T(8,128)(2,1)S(1)}, bf16[1,128,128]{2,1,0:T(8,128)(2,1)S(1)}, f32[128,128]{1,0:T(8...) custom-call(bf16[32,2176]{1,0:T(8,128)(2,1)S(1)} %copy-done.1, ...), custom_call_target="tpu_custom_call" | custom-call | tf_op jit(solution)/shard_map/forward_first/pallas_call | solution.py:524
  28.4 1.6 %collective-permute-start.10 = (bf16[384,128]{1,0:T(8,128)(2,1)S(1)}, bf16[384,128]{1,0:T(8,128)(2,1)S(1)}, u32[]{:S(2)}, u32[]{:S(2)}) collective-permute-start(bf16[384,128]{1,0:T(8,128)(2,1)S(1)} %get-tuple-element.74.near), channel_id=1, source_target_pairs={{0,2},{2,0},{4,6},{6,4},{1,3},{3,1},{5,7},{7,5},{8,10},{10,8},{12,... | collective-permute-start | bytes 294920 | tf_op jit(solution)/shard_map/ppermute | solution.py:495
  30.0 3.3 %collective-permute-done.10.far = bf16[384,128]{1,0:T(8,128)(2,1)S(1)} collective-permute-done((bf16[384,128]{1,0:T(8,128)(2,1)S(1)}, bf16[384,128]{1,0:T(8,128)(2,1)S(1)}, u32[]{:S(2)}, u32[]{:S(2)}) %collective-permute-start.10) | collective-permute-done | bytes 98336 | tf_op jit(solution)/shard_map/ppermute | solution.py:495
  33.3 2.7 %collective-permute-start.11 = (bf16[384,128]{1,0:T(8,128)(2,1)S(1)}, bf16[384,128]{1,0:T(8,128)(2,1)S(1)}, u32[]{:S(2)}, u32[]{:S(2)}) collective-permute-start(bf16[384,128]{1,0:T(8,128)(2,1)S(1)} %add_pair.6.refs_0_), channel_id=1, source_target_pairs={{0,4},{2,6},{4,0},{6,2},{1,5},{3,7},{5,1},{7,3},{8,12},{10,14},{12... | collective-permute-start | bytes 294920 | tf_op jit(solution)/shard_map/ppermute | solution.py:495
  35.9 4.4 %collective-permute-done.11.refs_1_ = bf16[384,128]{1,0:T(8,128)(2,1)S(1)} collective-permute-done((bf16[384,128]{1,0:T(8,128)(2,1)S(1)}, bf16[384,128]{1,0:T(8,128)(2,1)S(1)}, u32[]{:S(2)}, u32[]{:S(2)}) %collective-permute-start.11) | collective-permute-done | bytes 98336 | tf_op jit(solution)/shard_map/ppermute | solution.py:495
  40.4 2.4 %forward_middle.2 = (bf16[128,1024]{1,0:T(8,128)(2,1)S(1)}, f32[128,128]{1,0:T(8,128)S(1)}, bf16[128,128]{1,0:T(8,128)(2,1)S(1)}, f32[128,128]{1,0:T(8,128)S(1)}...) custom-call(bf16[384,128]{1,0:T(8,128)(2,1)S(1)} %add_pair.6.refs_0_, ...), custom_call_target="tpu_custom_call" | custom-call | tf_op jit(solution)/shard_map/forward_middle/pallas_call | solution.py:524
  43.0 5.5 %collective-permute-done.12.far = bf16[384,128]{1,0:T(8,128)(2,1)S(1)} collective-permute-done((bf16[384,128]{1,0:T(8,128)(2,1)S(1)}, bf16[384,128]{1,0:T(8,128)(2,1)S(1)}, u32[]{:S(2)}, u32[]{:S(2)}) %collective-permute-start.12) | collective-permute-done | bytes 98336 | tf_op jit(solution)/shard_map/ppermute | solution.py:495
  49.2 5.0 %collective-permute-done.13.refs_1_ = bf16[384,128]{1,0:T(8,128)(2,1)S(1)} collective-permute-done((bf16[384,128]{1,0:T(8,128)(2,1)S(1)}, bf16[384,128]{1,0:T(8,128)(2,1)S(1)}, u32[]{:S(2)}, u32[]{:S(2)}) %collective-permute-start.13) | collective-permute-done | bytes 98336 | tf_op jit(solution)/shard_map/ppermute | solution.py:495
  54.2 2.5 %forward_middle.3 = (bf16[128,1024]{1,0:T(8,128)(2,1)S(1)}, f32[128,128]{1,0:T(8,128)S(1)}, bf16[128,128]{1,0:T(8,128)(2,1)S(1)}, f32[128,128]{1,0:T(8,128)S(1)}...) custom-call(bf16[384,128]{1,0:T(8,128)(2,1)S(1)} %add_pair.7.refs_0_, ...), custom_call_target="tpu_custom_call" | custom-call | tf_op jit(solution)/shard_map/forward_middle/pallas_call | solution.py:524
  56.8 5.7 %collective-permute-done.14.far = bf16[512,128]{1,0:T(8,128)(2,1)S(1)} collective-permute-done((bf16[512,128]{1,0:T(8,128)(2,1)S(1)}, bf16[512,128]{1,0:T(8,128)(2,1)S(1)}, u32[]{:S(2)}, u32[]{:S(2)}) %collective-permute-start.14) | collective-permute-done | bytes 131104 | tf_op jit(solution)/shard_map/ppermute | solution.py:495
  63.4 6.2 %collective-permute-done.15.refs_1_ = bf16[512,128]{1,0:T(8,128)(2,1)S(1)} collective-permute-done((bf16[512,128]{1,0:T(8,128)(2,1)S(1)}, bf16[512,128]{1,0:T(8,128)(2,1)S(1)}, u32[]{:S(2)}, u32[]{:S(2)}) %collective-permute-start.15) | collective-permute-done | bytes 131104 | tf_op jit(solution)/shard_map/ppermute | solution.py:495
  69.7 3.4 %turn.1 = (bf16[128,1024]{1,0:T(8,128)(2,1)S(1)}, f32[128,128]{1,0:T(8,128)S(1)}, bf16[128,128]{1,0:T(8,128)(2,1)S(1)}, f32[128,128]{1,0:T(8,128)S(1)}, bf16[2,2...) custom-call(bf16[512,128]{1,0:T(8,128)(2,1)S(1)} %add_pair.8.refs_0_, ...), custom_call_target="tpu_custom_call" | custom-call | tf_op jit(solution)/shard_map/turn/pallas_call | solution.py:524
  73.1 4.7 %collective-permute-done.16.far = bf16[272,128]{1,0:T(8,128)(2,1)S(1)} collective-permute-done((bf16[272,128]{1,0:T(8,128)(2,1)S(1)}, bf16[272,128]{1,0:T(8,128)(2,1)S(1)}, u32[]{:S(2)}, u32[]{:S(2)}) %collective-permute-start.16) | collective-permute-done | bytes 69664 | tf_op jit(solution)/shard_map/ppermute | solution.py:495
  78.1 5.5 %collective-permute-done.17.refs_1_ = bf16[272,128]{1,0:T(8,128)(2,1)S(1)} collective-permute-done((bf16[272,128]{1,0:T(8,128)(2,1)S(1)}, bf16[272,128]{1,0:T(8,128)(2,1)S(1)}, u32[]{:S(2)}, u32[]{:S(2)}) %collective-permute-start.17) | collective-permute-done | bytes 69664 | tf_op jit(solution)/shard_map/ppermute | solution.py:495
  83.7 1.7 %backward.3 = (bf16[272,512]{1,0:T(8,128)(2,1)S(1)}, bf16[272,512]{1,0:T(8,128)(2,1)S(1)}, bf16[272,512]{1,0:T(8,128)(2,1)S(1)}, bf16[272,512]{1,0:T(8,128)(2,1)...) custom-call(bf16[272,128]{1,0:T(8,128)(2,1)S(1)} %add_pair.9.refs_0_, ...), custom_call_target="tpu_custom_call" | custom-call | tf_op jit(solution)/shard_map/backward/pallas_call | solution.py:524
  85.5 3.9 %collective-permute-done.18.far = bf16[144,128]{1,0:T(8,128)(2,1)S(1)} collective-permute-done((bf16[144,128]{1,0:T(8,128)(2,1)S(1)}, bf16[144,128]{1,0:T(8,128)(2,1)S(1)}, u32[]{:S(2)}, u32[]{:S(2)}) %collective-permute-start.18) | collective-permute-done | bytes 36896 | tf_op jit(solution)/shard_map/ppermute | solution.py:495
  90.2 4.2 %collective-permute-done.19.refs_1_ = bf16[144,128]{1,0:T(8,128)(2,1)S(1)} collective-permute-done((bf16[144,128]{1,0:T(8,128)(2,1)S(1)}, bf16[144,128]{1,0:T(8,128)(2,1)S(1)}, u32[]{:S(2)}, u32[]{:S(2)}) %collective-permute-start.19) | collective-permute-done | bytes 36896 | tf_op jit(solution)/shard_map/ppermute | solution.py:495
  94.4 1.7 %backward.4 = (bf16[272,512]{1,0:T(8,128)(2,1)S(1)}, bf16[272,512]{1,0:T(8,128)(2,1)S(1)}, bf16[128,1024]{1,0:T(8,128)(2,1)S(1)}, bf16[144,128]{1,0:T(8,128)(2,1)S(1)}) custom-call(bf16[144,128]{1,0:T(8,128)(2,1)S(1)} %add_pair.10.refs_0_, bf16[144,128]{1,0:T(8,128)(2,1)S(1)} %collective-permute-done.19.refs_1_, ...), custom_call_target="tpu_custom_call" | custom-call | tf_op jit(solution)/shard_map/backward/pallas_call | solution.py:524
  96.1 3.9 %collective-permute-done.20.far = bf16[144,128]{1,0:T(8,128)(2,1)S(1)} collective-permute-done((bf16[144,128]{1,0:T(8,128)(2,1)S(1)}, bf16[144,128]{1,0:T(8,128)(2,1)S(1)}, u32[]{:S(2)}, u32[]{:S(2)}) %collective-permute-start.20) | collective-permute-done | bytes 36896 | tf_op jit(solution)/shard_map/ppermute | solution.py:495
  101.4 3.7 %collective-permute-done.21.refs_1_ = bf16[144,128]{1,0:T(8,128)(2,1)S(1)} collective-permute-done((bf16[144,128]{1,0:T(8,128)(2,1)S(1)}, bf16[144,128]{1,0:T(8,128)(2,1)S(1)}, u32[]{:S(2)}, u32[]{:S(2)}) %collective-permute-start.21) | collective-permute-done | bytes 36896 | tf_op jit(solution)/shard_map/ppermute | solution.py:495
  106.6 1.5 %collective-permute-done.22.refs_4_ = bf16[272,512]{1,0:T(8,128)(2,1)S(1)} collective-permute-done((bf16[272,512]{1,0:T(8,128)(2,1)S(1)}, bf16[272,512]{1,0:T(8,128)(2,1)S(1)}, u32[]{:S(2)}, u32[]{:S(2)}) %collective-permute-start.22) | collective-permute-done | bytes 278560 | tf_op jit(solution)/shard_map/ppermute | solution.py:490
  108.6 1.6 %collective-permute-start.26 = (bf16[272,512]{1,0:T(8,128)(2,1)S(1)}, bf16[272,512]{1,0:T(8,128)(2,1)S(1)}, u32[]{:S(2)}, u32[]{:S(2)}) collective-permute-start(bf16[272,512]{1,0:T(8,128)(2,1)S(1)} %get-tuple-element.116), channel_id=1, source_target_pairs={{0,8},{8,0},{16,24},{24,16},{1,9},{9,1},{17,25},{25,17},{2,10},{10... | collective-permute-start | bytes 835592 | tf_op jit(solution)/shard_map/ppermute | solution.py:487
  110.5 1.7 %collective-permute-start.28 = (bf16[272,512]{1,0:T(8,128)(2,1)S(1)}, bf16[272,512]{1,0:T(8,128)(2,1)S(1)}, u32[]{:S(2)}, u32[]{:S(2)}) collective-permute-start(bf16[272,512]{1,0:T(8,128)(2,1)S(1)} %get-tuple-element.118), channel_id=1, source_target_pairs={{0,24},{8,16},{16,8},{24,0},{1,25},{9,17},{17,9},{25,1},{2,26},{10... | collective-permute-start | bytes 835592 | tf_op jit(solution)/shard_map/ppermute | solution.py:487
  112.2 6.0 %collective-permute-done.26.refs_1_ = bf16[272,512]{1,0:T(8,128)(2,1)S(1)} collective-permute-done((bf16[272,512]{1,0:T(8,128)(2,1)S(1)}, bf16[272,512]{1,0:T(8,128)(2,1)S(1)}, u32[]{:S(2)}, u32[]{:S(2)}) %collective-permute-start.26) | collective-permute-done | bytes 278560 | tf_op jit(solution)/shard_map/ppermute | solution.py:487
  118.2 6.4 %collective-permute-done.27.refs_2_ = bf16[272,512]{1,0:T(8,128)(2,1)S(1)} collective-permute-done((bf16[272,512]{1,0:T(8,128)(2,1)S(1)}, bf16[272,512]{1,0:T(8,128)(2,1)S(1)}, u32[]{:S(2)}, u32[]{:S(2)}) %collective-permute-start.27) | collective-permute-done | bytes 278560 | tf_op jit(solution)/shard_map/ppermute | solution.py:487
  (46 shorter events, 13.7 us)
Async XLA Ops:
  2.9 9.2 %collective-permute-start = (bf16[32,2176]{1,0:T(8,128)(2,1)}, bf16[32,2176]{1,0:T(8,128)(2,1)S(1)}, u32[]{:S(2)}, u32[]{:S(2)}) collective-permute-start(bf16[32,2176]{1,0:T(8,128)(2,1)} %get-tuple-element.62), channel_id=1, source_target_pairs={{0,2},{2,4},{4,6},{6,0},{1,3},{3,5},{5,7},{7,1},{8,10},{10,12},{12... | collective-permute-start | bytes 417800 | tf_op jit(solution)/shard_map/ppermute | solution.py:484
  6.0 13.1 %collective-permute-start.5 = (bf16[1040,128]{1,0:T(8,128)(2,1)}, bf16[1040,128]{1,0:T(8,128)(2,1)S(1)}, u32[]{:S(2)}, u32[]{:S(2)}) collective-permute-start(bf16[1040,128]{1,0:T(8,128)(2,1)} %get-tuple-element.70.refs_4_), channel_id=1, source_target_pairs={{0,24},{8,16},{16,8},{24,0},{1,25},{9,17},{17,9},{25,1},{2,26},{10... | collective-permute-start | bytes 798728 | tf_op jit(solution)/shard_map/ppermute | solution.py:487
  8.5 12.2 %collective-permute-start.4 = (bf16[1040,128]{1,0:T(8,128)(2,1)}, bf16[1040,128]{1,0:T(8,128)(2,1)S(1)}, u32[]{:S(2)}, u32[]{:S(2)}) collective-permute-start(bf16[1040,128]{1,0:T(8,128)(2,1)} %get-tuple-element.70.refs_4_), channel_id=1, source_target_pairs={{0,16},{8,24},{16,0},{24,8},{1,17},{9,25},{17,1},{25,9},{2,18},{10... | collective-permute-start | bytes 798728 | tf_op jit(solution)/shard_map/ppermute | solution.py:487
  9.0 11.8 %collective-permute-start.3 = (bf16[1040,128]{1,0:T(8,128)(2,1)}, bf16[1040,128]{1,0:T(8,128)(2,1)S(1)}, u32[]{:S(2)}, u32[]{:S(2)}) collective-permute-start(bf16[1040,128]{1,0:T(8,128)(2,1)} %get-tuple-element.70.refs_4_), channel_id=1, source_target_pairs={{0,8},{8,0},{16,24},{24,16},{1,9},{9,1},{17,25},{25,17},{2,10},{10... | collective-permute-start | bytes 798728 | tf_op jit(solution)/shard_map/ppermute | solution.py:487
  9.5 9.6 %collective-permute-start.1 = (bf16[32,2176]{1,0:T(8,128)(2,1)}, bf16[32,2176]{1,0:T(8,128)(2,1)S(1)}, u32[]{:S(2)}, u32[]{:S(2)}) collective-permute-start(bf16[32,2176]{1,0:T(8,128)(2,1)} %get-tuple-element.63), channel_id=1, source_target_pairs={{0,4},{2,6},{4,0},{6,2},{1,5},{3,7},{5,1},{7,3},{8,12},{10,14},{12... | collective-permute-start | bytes 417800 | tf_op jit(solution)/shard_map/ppermute | solution.py:484
  12.1 7.0 %collective-permute-start.2 = (bf16[32,2176]{1,0:T(8,128)(2,1)}, bf16[32,2176]{1,0:T(8,128)(2,1)S(1)}, u32[]{:S(2)}, u32[]{:S(2)}) collective-permute-start(bf16[32,2176]{1,0:T(8,128)(2,1)} %get-tuple-element.64), channel_id=1, source_target_pairs={{0,6},{2,0},{4,2},{6,4},{1,7},{3,1},{5,3},{7,5},{8,14},{10,8},{12,... | collective-permute-start | bytes 417800 | tf_op jit(solution)/shard_map/ppermute | solution.py:484
  20.8 2.1 %collective-permute-start.6 = (bf16[1040,128]{1,0:T(8,128)(2,1)}, bf16[1040,128]{1,0:T(8,128)(2,1)S(1)}, u32[]{:S(2)}, u32[]{:S(2)}) collective-permute-start(bf16[1040,128]{1,0:T(8,128)(2,1)} %get-tuple-element.70.refs_4_), channel_id=1, source_target_pairs={{0,1},{1,0},{2,3},{3,2},{4,5},{5,4},{6,7},{7,6},{8,9},{9,8},{10,11... | collective-permute-start | bytes 798728 | tf_op jit(solution)/shard_map/ppermute | solution.py:490
  20.8 2.1 %collective-permute-start.7 = (bf16[1040,128]{1,0:T(8,128)(2,1)S(1)}, bf16[1040,128]{1,0:T(8,128)(2,1)S(1)}, u32[]{:S(2)}, u32[]{:S(2)}) collective-permute-start(bf16[1040,128]{1,0:T(8,128)(2,1)S(1)} %collective-permute-done.3.refs_5_), channel_id=1, source_target_pairs={{0,1},{1,0},{2,3},{3,2},{4,5},{5,4},{6,7},{7,6},{8,9},{9,8},{10,11... | collective-permute-start | bytes 798728 | tf_op jit(solution)/shard_map/ppermute | solution.py:490
  21.3 1.8 %collective-permute-start.8 = (bf16[1040,128]{1,0:T(8,128)(2,1)S(1)}, bf16[1040,128]{1,0:T(8,128)(2,1)S(1)}, u32[]{:S(2)}, u32[]{:S(2)}) collective-permute-start(bf16[1040,128]{1,0:T(8,128)(2,1)S(1)} %collective-permute-done.4.refs_6_), channel_id=1, source_target_pairs={{0,1},{1,0},{2,3},{3,2},{4,5},{5,4},{6,7},{7,6},{8,9},{9,8},{10,11... | collective-permute-start | bytes 798728 | tf_op jit(solution)/shard_map/ppermute | solution.py:490
  21.3 2.2 %collective-permute-start.9 = (bf16[1040,128]{1,0:T(8,128)(2,1)S(1)}, bf16[1040,128]{1,0:T(8,128)(2,1)S(1)}, u32[]{:S(2)}, u32[]{:S(2)}) collective-permute-start(bf16[1040,128]{1,0:T(8,128)(2,1)S(1)} %collective-permute-done.5.refs_7_), channel_id=1, source_target_pairs={{0,1},{1,0},{2,3},{3,2},{4,5},{5,4},{6,7},{7,6},{8,9},{9,8},{10,11... | collective-permute-start | bytes 798728 | tf_op jit(solution)/shard_map/ppermute | solution.py:490
  23.5 1.0 copy-start
  24.4 0.9 copy-start.1
  28.4 4.9 %collective-permute-start.10 = (bf16[384,128]{1,0:T(8,128)(2,1)S(1)}, bf16[384,128]{1,0:T(8,128)(2,1)S(1)}, u32[]{:S(2)}, u32[]{:S(2)}) collective-permute-start(bf16[384,128]{1,0:T(8,128)(2,1)S(1)} %get-tuple-element.74.near), channel_id=1, source_target_pairs={{0,2},{2,0},{4,6},{6,4},{1,3},{3,1},{5,7},{7,5},{8,10},{10,8},{12,... | collective-permute-start | bytes 294920 | tf_op jit(solution)/shard_map/ppermute | solution.py:495
  33.3 7.1 %collective-permute-start.11 = (bf16[384,128]{1,0:T(8,128)(2,1)S(1)}, bf16[384,128]{1,0:T(8,128)(2,1)S(1)}, u32[]{:S(2)}, u32[]{:S(2)}) collective-permute-start(bf16[384,128]{1,0:T(8,128)(2,1)S(1)} %add_pair.6.refs_0_), channel_id=1, source_target_pairs={{0,4},{2,6},{4,0},{6,2},{1,5},{3,7},{5,1},{7,3},{8,12},{10,14},{12... | collective-permute-start | bytes 294920 | tf_op jit(solution)/shard_map/ppermute | solution.py:495
  42.8 5.7 %collective-permute-start.12 = (bf16[384,128]{1,0:T(8,128)(2,1)S(1)}, bf16[384,128]{1,0:T(8,128)(2,1)S(1)}, u32[]{:S(2)}, u32[]{:S(2)}) collective-permute-start(bf16[384,128]{1,0:T(8,128)(2,1)S(1)} %get-tuple-element.79.near), channel_id=1, source_target_pairs={{0,2},{2,0},{4,6},{6,4},{1,3},{3,1},{5,7},{7,5},{8,10},{10,8},{12,... | collective-permute-start | bytes 294920 | tf_op jit(solution)/shard_map/ppermute | solution.py:495
  48.5 5.7 %collective-permute-start.13 = (bf16[384,128]{1,0:T(8,128)(2,1)S(1)}, bf16[384,128]{1,0:T(8,128)(2,1)S(1)}, u32[]{:S(2)}, u32[]{:S(2)}) collective-permute-start(bf16[384,128]{1,0:T(8,128)(2,1)S(1)} %add_pair.7.refs_0_), channel_id=1, source_target_pairs={{0,4},{2,6},{4,0},{6,2},{1,5},{3,7},{5,1},{7,3},{8,12},{10,14},{12... | collective-permute-start | bytes 294920 | tf_op jit(solution)/shard_map/ppermute | solution.py:495
  56.7 5.8 %collective-permute-start.14 = (bf16[512,128]{1,0:T(8,128)(2,1)S(1)}, bf16[512,128]{1,0:T(8,128)(2,1)S(1)}, u32[]{:S(2)}, u32[]{:S(2)}) collective-permute-start(bf16[512,128]{1,0:T(8,128)(2,1)S(1)} %get-tuple-element.83.near), channel_id=1, source_target_pairs={{0,2},{2,0},{4,6},{6,4},{1,3},{3,1},{5,7},{7,5},{8,10},{10,8},{12,... | collective-permute-start | bytes 393224 | tf_op jit(solution)/shard_map/ppermute | solution.py:495
  62.5 7.2 %collective-permute-start.15 = (bf16[512,128]{1,0:T(8,128)(2,1)S(1)}, bf16[512,128]{1,0:T(8,128)(2,1)S(1)}, u32[]{:S(2)}, u32[]{:S(2)}) collective-permute-start(bf16[512,128]{1,0:T(8,128)(2,1)S(1)} %add_pair.8.refs_0_), channel_id=1, source_target_pairs={{0,4},{2,6},{4,0},{6,2},{1,5},{3,7},{5,1},{7,3},{8,12},{10,14},{12... | collective-permute-start | bytes 393224 | tf_op jit(solution)/shard_map/ppermute | solution.py:495
  73.0 4.8 %collective-permute-start.16 = (bf16[272,128]{1,0:T(8,128)(2,1)S(1)}, bf16[272,128]{1,0:T(8,128)(2,1)S(1)}, u32[]{:S(2)}, u32[]{:S(2)}) collective-permute-start(bf16[272,128]{1,0:T(8,128)(2,1)S(1)} %get-tuple-element.86.near), channel_id=1, source_target_pairs={{0,2},{2,0},{4,6},{6,4},{1,3},{3,1},{5,7},{7,5},{8,10},{10,8},{12,... | collective-permute-start | bytes 208904 | tf_op jit(solution)/shard_map/ppermute | solution.py:495
  77.8 5.9 %collective-permute-start.17 = (bf16[272,128]{1,0:T(8,128)(2,1)S(1)}, bf16[272,128]{1,0:T(8,128)(2,1)S(1)}, u32[]{:S(2)}, u32[]{:S(2)}) collective-permute-start(bf16[272,128]{1,0:T(8,128)(2,1)S(1)} %add_pair.9.refs_0_), channel_id=1, source_target_pairs={{0,4},{2,6},{4,0},{6,2},{1,5},{3,7},{5,1},{7,3},{8,12},{10,14},{12... | collective-permute-start | bytes 208904 | tf_op jit(solution)/shard_map/ppermute | solution.py:495
  85.4 4.0 %collective-permute-start.18 = (bf16[144,128]{1,0:T(8,128)(2,1)S(1)}, bf16[144,128]{1,0:T(8,128)(2,1)S(1)}, u32[]{:S(2)}, u32[]{:S(2)}) collective-permute-start(bf16[144,128]{1,0:T(8,128)(2,1)S(1)} %get-tuple-element.95.near), channel_id=1, source_target_pairs={{0,2},{2,0},{4,6},{6,4},{1,3},{3,1},{5,7},{7,5},{8,10},{10,8},{12,... | collective-permute-start | bytes 110600 | tf_op jit(solution)/shard_map/ppermute | solution.py:495
  89.5 4.9 %collective-permute-start.19 = (bf16[144,128]{1,0:T(8,128)(2,1)S(1)}, bf16[144,128]{1,0:T(8,128)(2,1)S(1)}, u32[]{:S(2)}, u32[]{:S(2)}) collective-permute-start(bf16[144,128]{1,0:T(8,128)(2,1)S(1)} %add_pair.10.refs_0_), channel_id=1, source_target_pairs={{0,4},{2,6},{4,0},{6,2},{1,5},{3,7},{5,1},{7,3},{8,12},{10,14},{12... | collective-permute-start | bytes 110600 | tf_op jit(solution)/shard_map/ppermute | solution.py:495
  96.1 4.0 %collective-permute-start.20 = (bf16[144,128]{1,0:T(8,128)(2,1)S(1)}, bf16[144,128]{1,0:T(8,128)(2,1)S(1)}, u32[]{:S(2)}, u32[]{:S(2)}) collective-permute-start(bf16[144,128]{1,0:T(8,128)(2,1)S(1)} %get-tuple-element.101.near), channel_id=1, source_target_pairs={{0,2},{2,0},{4,6},{6,4},{1,3},{3,1},{5,7},{7,5},{8,10},{10,8},{12,... | collective-permute-start | bytes 110600 | tf_op jit(solution)/shard_map/ppermute | solution.py:495
  100.1 4.9 %collective-permute-start.21 = (bf16[144,128]{1,0:T(8,128)(2,1)S(1)}, bf16[144,128]{1,0:T(8,128)(2,1)S(1)}, u32[]{:S(2)}, u32[]{:S(2)}) collective-permute-start(bf16[144,128]{1,0:T(8,128)(2,1)S(1)} %add_pair.11.refs_0_), channel_id=1, source_target_pairs={{0,4},{2,6},{4,0},{6,2},{1,5},{3,7},{5,1},{7,3},{8,12},{10,14},{12... | collective-permute-start | bytes 110600 | tf_op jit(solution)/shard_map/ppermute | solution.py:495
  100.8 5.7 %collective-permute-start.24 = (bf16[272,512]{1,0:T(8,128)(2,1)S(1)}, bf16[272,512]{1,0:T(8,128)(2,1)S(1)}, u32[]{:S(2)}, u32[]{:S(2)}) collective-permute-start(bf16[272,512]{1,0:T(8,128)(2,1)S(1)} %get-tuple-element.113), channel_id=1, source_target_pairs={{0,1},{1,0},{2,3},{3,2},{4,5},{5,4},{6,7},{7,6},{8,9},{9,8},{10,11... | collective-permute-start | bytes 835592 | tf_op jit(solution)/shard_map/ppermute | solution.py:490
  100.8 5.7 %collective-permute-start.25 = (bf16[272,512]{1,0:T(8,128)(2,1)S(1)}, bf16[272,512]{1,0:T(8,128)(2,1)S(1)}, u32[]{:S(2)}, u32[]{:S(2)}) collective-permute-start(bf16[272,512]{1,0:T(8,128)(2,1)S(1)} %get-tuple-element.114), channel_id=1, source_target_pairs={{0,1},{1,0},{2,3},{3,2},{4,5},{5,4},{6,7},{7,6},{8,9},{9,8},{10,11... | collective-permute-start | bytes 835592 | tf_op jit(solution)/shard_map/ppermute | solution.py:490
  101.4 5.2 %collective-permute-start.23 = (bf16[272,512]{1,0:T(8,128)(2,1)S(1)}, bf16[272,512]{1,0:T(8,128)(2,1)S(1)}, u32[]{:S(2)}, u32[]{:S(2)}) collective-permute-start(bf16[272,512]{1,0:T(8,128)(2,1)S(1)} %get-tuple-element.112), channel_id=1, source_target_pairs={{0,1},{1,0},{2,3},{3,2},{4,5},{5,4},{6,7},{7,6},{8,9},{9,8},{10,11... | collective-permute-start | bytes 835592 | tf_op jit(solution)/shard_map/ppermute | solution.py:490
  106.4 1.6 %collective-permute-start.22 = (bf16[272,512]{1,0:T(8,128)(2,1)S(1)}, bf16[272,512]{1,0:T(8,128)(2,1)S(1)}, u32[]{:S(2)}, u32[]{:S(2)}) collective-permute-start(bf16[272,512]{1,0:T(8,128)(2,1)S(1)} %get-tuple-element.111), channel_id=1, source_target_pairs={{0,1},{1,0},{2,3},{3,2},{4,5},{5,4},{6,7},{7,6},{8,9},{9,8},{10,11... | collective-permute-start | bytes 835592 | tf_op jit(solution)/shard_map/ppermute | solution.py:490
  108.6 9.6 %collective-permute-start.26 = (bf16[272,512]{1,0:T(8,128)(2,1)S(1)}, bf16[272,512]{1,0:T(8,128)(2,1)S(1)}, u32[]{:S(2)}, u32[]{:S(2)}) collective-permute-start(bf16[272,512]{1,0:T(8,128)(2,1)S(1)} %get-tuple-element.116), channel_id=1, source_target_pairs={{0,8},{8,0},{16,24},{24,16},{1,9},{9,1},{17,25},{25,17},{2,10},{10... | collective-permute-start | bytes 835592 | tf_op jit(solution)/shard_map/ppermute | solution.py:487
  110.2 14.4 %collective-permute-start.27 = (bf16[272,512]{1,0:T(8,128)(2,1)S(1)}, bf16[272,512]{1,0:T(8,128)(2,1)S(1)}, u32[]{:S(2)}, u32[]{:S(2)}) collective-permute-start(bf16[272,512]{1,0:T(8,128)(2,1)S(1)} %get-tuple-element.117), channel_id=1, source_target_pairs={{0,16},{8,24},{16,0},{24,8},{1,17},{9,25},{17,1},{25,9},{2,18},{10... | collective-permute-start | bytes 835592 | tf_op jit(solution)/shard_map/ppermute | solution.py:487
  110.5 14.1 %collective-permute-start.28 = (bf16[272,512]{1,0:T(8,128)(2,1)S(1)}, bf16[272,512]{1,0:T(8,128)(2,1)S(1)}, u32[]{:S(2)}, u32[]{:S(2)}) collective-permute-start(bf16[272,512]{1,0:T(8,128)(2,1)S(1)} %get-tuple-element.118), channel_id=1, source_target_pairs={{0,24},{8,16},{16,8},{24,0},{1,25},{9,17},{17,9},{25,1},{2,26},{10... | collective-permute-start | bytes 835592 | tf_op jit(solution)/shard_map/ppermute | solution.py:487

commit v5 on v3

--- a/solution.py
+++ b/solution.py
@@ -196,7 +196,6 @@
     own = (weights.shape[2] - 16) // 2
     pay[0:rows, :] = to_rank(mixed[...], weights, 0).astype(BF)
     pay[rows : 2 * rows, :] = to_rank(x[...], weights, own).astype(BF)
-    pay[2 * rows : 2 * rows + HD, :] = gram(weights).astype(BF)
 
 
 def total_of(pays, start, stop):
@@ -206,12 +205,14 @@
     return total
 
 
-def receive_forward(pays, x_before, mean_before, weights_before, width, x, mean, reduced, cross):
+def receive_forward(
+    pays, gram_total, x_before, mean_before, weights_before, width, x, mean, reduced, cross
+):
     rows, local = x_before.shape
     own = (weights_before.shape[2] - 16) // 2
     low_rank = total_of(pays, 0, rows).astype(BF)
     before = total_of(pays, rows, 2 * rows)
-    high, low = two_parts(total_of(pays, 2 * rows, 2 * rows + HD))
+    high, low = two_parts(gram_total)
     through = dot(low_rank, high) + dot(low_rank, low)
     wide = low_rank.astype(F32)
     change = jnp.sum(wide * (2.0 * before + through), axis=1, keepdims=True) / width
@@ -226,34 +227,46 @@
         ).astype(BF)
 
 
-def first_kernel(length, groups, sections, *refs):
-    received, refs = refs[:groups], refs[groups:]
-    mine, theirs = refs[:sections], refs[sections : 2 * sections]
-    x, cot, mask, mean, probs, mixed, pay, weights, tails, sems = refs[2 * sections :]
-    section, core = lax.axis_index("pipe"), lax.axis_index("core")
+def arrange_kernel(length, groups, *refs):
+    received, packed = refs[:groups], refs[groups]
+    x, cot, mask, mean, packed_out, tails = refs[groups + 1 :]
     rows, local = x.shape
-    size = block_size(rows)
-    copies = []
-    for distance in range(sections):
-        layer = section ^ distance
-        for parts, side in ((mine, core), (theirs, 1 - core)):
-            copies.append(
-                pltpu.make_async_copy(
-                    parts[distance], weights.at[layer, side], sems.at[distance, side]
-                )
-            )
-    for copy in copies:
-        copy.start()
     place_rows(received, tails, slice(2 * local, None))
     place_rows(received, x, slice(0, local))
     place_rows(received, cot, slice(local, 2 * local))
     tail = tails[...].astype(F32)
     mean[...] = jnp.broadcast_to(tail[:, 1:2] + tail[:, 2:3], mean.shape)
-    build_mask(tail[:, 0:1], mask, size, length)
+    build_mask(tail[:, 0:1], mask, block_size(rows), length)
+    packed_out[...] = packed[...]
+
+
+def first_kernel(sections, *refs):
+    mine, theirs = refs[:sections], refs[sections : 2 * sections]
+    x, cot, mask, mean, probs, mixed, pay, side, weights, sems = refs[2 * sections :]
+    section, core = lax.axis_index("pipe"), lax.axis_index("core")
+    rows = x.shape[0]
+    copies = []
+    for distance in range(sections):
+        layer = section ^ distance
+        for parts, place in ((mine, core), (theirs, 1 - core)):
+            copies.append(
+                pltpu.make_async_copy(
+                    parts[distance], weights.at[layer, place], sems.at[distance, place]
+                )
+            )
+    for copy in copies:
+        copy.start()
     for copy in copies:
         copy.wait()
-    attend(x, mean[:, 0:1], weights, mask, probs, mixed)
-    send_forward(x, weights, mixed, pay)
+    own = (weights.shape[2] - 16) // 2
+    layers = [weights.at[pl.ds(layer, 1)] for layer in range(sections)]
+    attend(x, mean[:, 0:1], layers[0], mask, probs, mixed)
+    send_forward(x, layers[0], mixed, pay)
+    pay[2 * rows :, :] = gram(layers[0]).astype(BF)
+    side[0:rows, :] = to_rank(cot[...], layers[-1], own).astype(BF)
+    for layer in range(1, sections - 1):
+        base = rows + HD * (layer - 1)
+        side[base : base + HD, :] = gram(layers[layer]).astype(BF)
 
 
 def place_rows(received, target, columns):
@@ -274,23 +287,25 @@
         mask[block] = allowed.astype(F32).astype(BF)
 
 
-def middle_kernel(count, last, width, *refs):
-    pays, refs = refs[:count], refs[count:]
+def gram_of(pays, sides, layer, rows):
+    if layer == 0:
+        return total_of(pays, 2 * rows, 2 * rows + HD)
+    base = rows + HD * (layer - 1)
+    return total_of(sides, base, base + HD)
+
+
+def middle_kernel(count, layer, width, *refs):
+    pays, sides, refs = refs[:count], refs[count : 2 * count], refs[2 * count :]
+    if layer == 1:
+        sides, refs = (), sides + refs
     x_before, mean_before, mask, weights_before, weights = refs[:5]
-    refs = refs[5:]
-    if last:
-        cot, weights_after = refs[:2]
-        refs = refs[2:]
-    x, mean, reduced, cross, probs, mixed, pay = refs
+    x, mean, reduced, cross, probs, mixed, pay = refs[5:]
     receive_forward(
-        pays, x_before, mean_before, weights_before, width, x, mean, reduced, cross
+        pays, gram_of(pays, sides, layer - 1, x.shape[0]), x_before, mean_before, weights_before,
+        width, x, mean, reduced, cross,
     )
     attend(x, mean[:, 0:1], weights, mask, probs, mixed)
     send_forward(x, weights, mixed, pay)
-    if last:
-        rows = x.shape[0]
-        own = (weights.shape[2] - 16) // 2
-        pay[2 * rows + HD :, :] = to_rank(cot[...], weights_after, own).astype(BF)
 
 
 def layer_backward(
@@ -356,22 +371,23 @@
         pay[0:rows, :] = to_rank(carried[...], weights_before, own).astype(BF)
 
 
-def turn_kernel(count, width, *refs):
-    pays, refs = refs[:count], refs[count:]
+def turn_kernel(count, layer, width, *refs):
+    pays, sides, refs = refs[:count], refs[count : 2 * count], refs[2 * count :]
     (x_before, mean_before, mask, weights_before, weights, cot) = refs[:6]
-    (x, mean, reduced, cross, grads, carried, pay) = refs[6:13]
-    probs, mixed = refs[13:]
+    (x, mean, reduced, cross, grads, carried, pay, last_part) = refs[6:14]
+    probs, mixed = refs[14:]
     rows = x.shape[0]
     receive_forward(
-        pays, x_before, mean_before, weights_before, width, x, mean, reduced, cross
+        pays, gram_of(pays, sides, layer - 1, rows), x_before, mean_before, weights_before,
+        width, x, mean, reduced, cross,
     )
     attend(x, mean[:, 0:1], weights, mask, probs, mixed)
-    dred = total_of(pays, 2 * rows + HD, 3 * rows + HD).astype(BF)
+    last_part[...] = to_rank(mixed[...], weights, 0).astype(BF)
+    dred = total_of(sides, 0, rows).astype(BF)
     layer_backward(
         cot, dred, x, mean[:, 0:1], mask, weights, weights_before, probs, mixed, None, grads,
         carried, pay,
     )
-    pay[pay.shape[0] - rows :, :] = to_rank(mixed[...], weights, 0).astype(BF)
 
 
 def split_sides(grads, keep, send):
@@ -380,7 +396,7 @@
     send[...] = grads[1 - core]
 
 
-def back_kernel(count, after_turn, to_first, width, *refs):
+def back_kernel(count, with_last, to_first, width, *refs):
     pays, refs = refs[:count], refs[count:]
     carried_after, x_after, mean_after, cross_after = refs[:4]
     x, mean, mask, weights = refs[4:8]
@@ -390,12 +406,12 @@
         weights_before, refs = refs[0], refs[1:]
     probs, mixed, reduced = refs[:3]
     refs = refs[3:]
-    if after_turn:
-        cot, turn_grads = refs[:2]
-        refs = refs[2:]
+    if with_last:
+        last_parts, cot, turn_grads = refs[:count], refs[count], refs[count + 1]
+        refs = refs[count + 2 :]
     keep, send = refs[:2]
     refs = refs[2:]
-    if after_turn:
+    if with_last:
         last_keep, last_send = refs[:2]
         refs = refs[2:]
     if not to_first:
@@ -424,8 +440,8 @@
             carried_after[span, :].astype(F32) - x_after[span, :].astype(F32) * pull
         ).astype(BF)
     dred = dred_parts[0] if len(dred_parts) == 1 else jnp.concatenate(dred_parts, axis=0)
-    if after_turn:
-        last_reduced = total_of(pays, pays[0].shape[0] - rows, pays[0].shape[0]).astype(BF)
+    if with_last:
+        last_reduced = total_of(last_parts, 0, rows).astype(BF)
         second = dot_tn(last_reduced, cot[...]).astype(BF)
         for side in range(weights.shape[1]):
             grads[side, 0:rank, :] = turn_grads[side, 0:rank, :]
@@ -508,7 +524,6 @@
     grads_shape = (sides, 2 * rank + 16, own)
     half_shape = shaped(grads_shape[1:])
     weights_shape = shaped((sections, sides, slice_rows(own), HD))
-    forward_rows = 2 * rows + HD
 
     def call(kernel, operands, specs, outs, name, **more):
         return pl.pallas_call(
@@ -525,50 +540,54 @@
     def layer_of(index):
         return layer_spec(weights_shape.shape, index)
 
-    x, cot, mask, mean, probs, mixed, pay, weights = call(
-        functools.partial(first_kernel, length, groups, sections),
-        (*received, *mine, *theirs),
-        vmem_specs(groups + 2 * sections),
+    x, cot, mask, mean, mine[0] = call(
+        functools.partial(arrange_kernel, length, groups),
+        (*received, mine[0]),
+        vmem_specs(groups + 1),
         [
             wide_shape,
             wide_shape,
             shaped((blocks, size, size)),
             mean_shape,
+            shaped(packed.shape),
+        ],
+        "arrange",
+        scratch_shapes=[pltpu.VMEM((rows, HD), BF)],
+    )
+    probs, mixed, pay, side, weights = call(
+        functools.partial(first_kernel, sections),
+        (*mine, *theirs, x, cot, mask, mean),
+        vmem_specs(2 * sections + 4),
+        [
             probs_shape,
             wide_shape,
-            shaped((forward_rows, HD)),
+            shaped((2 * rows + HD, HD)),
+            shaped((rows + HD * (top - 1), HD)),
             weights_shape,
         ],
         "forward_first",
-        scratch_shapes=[
-            pltpu.VMEM((rows, HD), BF),
-            pltpu.SemaphoreType.DMA((sections, sides)),
-        ],
+        scratch_shapes=[pltpu.SemaphoreType.DMA((sections, sides))],
     )
     xs, means, reduceds, crosses = [x], [mean], [], [None]
     all_probs, all_mixed = [probs], [mixed]
+    pays = exchange(pay)
+    arrived = exchange(side)
     for layer in range(1, top):
-        pays = exchange(pay)
-        last = layer == top - 1
-        operands = (*pays, xs[-1], means[-1], mask, weights, weights)
-        specs = vmem_specs(len(pays) + 3) + [layer_of(layer - 1), layer_of(layer)]
-        outs = [
-            wide_shape,
-            mean_shape,
-            rank_shape,
-            cross_shape,
-            probs_shape,
-            wide_shape,
-            shaped((forward_rows + (rows if last else 0), HD)),
-        ]
-        if last:
-            operands += (cot, weights)
-            specs += vmem_specs(1) + [layer_of(layer + 1)]
+        operands = (*pays, *(arrived if layer > 1 else ()))
+        specs = vmem_specs(len(operands) + 3) + [layer_of(layer - 1), layer_of(layer)]
         x, mean, reduced, cross, probs, mixed, pay = call(
-            functools.partial(middle_kernel, len(pays), last, float(width)),
-            operands,
+            functools.partial(middle_kernel, groups, layer, float(width)),
+            (*operands, xs[-1], means[-1], mask, weights, weights),
             specs,
-            outs,
+            [
+                wide_shape,
+                mean_shape,
+                rank_shape,
+                cross_shape,
+                probs_shape,
+                wide_shape,
+                shaped((2 * rows, HD)),
+            ],
             "forward_middle",
         )
         xs.append(x)
@@ -577,13 +596,13 @@
         crosses.append(cross)
         all_probs.append(probs)
         all_mixed.append(mixed)
-
-    pays = exchange(pay)
+        pays = exchange(pay)
+
     back_rows = rows + 16 * blocks
-    x, mean, reduced, cross, turn_grads, carried, pay = call(
-        functools.partial(turn_kernel, len(pays), float(width)),
-        (*pays, xs[-1], means[-1], mask, weights, weights, cot),
-        vmem_specs(len(pays) + 3) + [layer_of(top - 1), layer_of(top)] + vmem_specs(1),
+    x, mean, reduced, cross, turn_grads, carried, pay, last_part = call(
+        functools.partial(turn_kernel, groups, top, float(width)),
+        (*pays, *arrived, xs[-1], means[-1], mask, weights, weights, cot),
+        vmem_specs(2 * groups + 3) + [layer_of(top - 1), layer_of(top)] + vmem_specs(1),
         [
             wide_shape,
             mean_shape,
@@ -591,7 +610,8 @@
             cross_shape,
             shaped(grads_shape),
             wide_shape,
-            shaped((back_rows + rows, HD)),
+            shaped((back_rows, HD)),
+            rank_shape,
         ],
         "turn",
         scratch_shapes=[
@@ -607,7 +627,9 @@
     kept, taken = [None] * sections, [None] * sections
     for layer in range(top - 1, -1, -1):
         pays = exchange(pay)
-        after_turn = layer == top - 1
+        if layer == top - 1:
+            last_parts = exchange(last_part)
+        with_last = layer == top - 2
         to_first = layer == 0
         operands = (
             *pays, carried, xs[layer + 1], means[layer + 1], crosses[layer + 1],
@@ -620,14 +642,14 @@
         operands += (all_probs[layer], all_mixed[layer], reduceds[layer])
         specs += vmem_specs(3)
         outs = [half_shape] * 2
-        if after_turn:
-            operands += (cot, turn_grads)
-            specs += vmem_specs(2)
+        if with_last:
+            operands += (*last_parts, cot, turn_grads)
+            specs += vmem_specs(groups + 2)
             outs += [half_shape] * 2
         if not to_first:
             outs += [wide_shape, shaped((back_rows, HD))]
         result = call(
-            functools.partial(back_kernel, len(pays), after_turn, to_first, float(width)),
+            functools.partial(back_kernel, groups, with_last, to_first, float(width)),
             operands,
             specs,
             outs,
@@ -635,7 +657,7 @@
             scratch_shapes=[pltpu.VMEM(wide_shape.shape, BF), pltpu.VMEM(grads_shape, BF)],
         )
         kept[layer], taken[layer] = result[0], swapped(result[1])
-        if after_turn:
+        if with_last:
             kept[top], taken[top] = result[2], swapped(result[3])
         if not to_first:
             carried, pay = result[-2:]

time: 121 us -> 118 us (0.975)
  waiting for transfers between devices: 60 us -> 46.6 us
  starting transfers between devices: 38.7 us -> 48.3 us
    ppermute x21 -> x27, waiting for transfers between devices: 42.7 us -> 30.9 us  [shifted(): lax.ppermute(value, 'z', [(i, (i + shift) % groups) for i in range(groups)])]
    ppermute x21 -> x27, starting transfers between devices: 30 us -> 39.6 us  [shifted(): lax.ppermute(value, 'z', [(i, (i + shift) % groups) for i in range(groups)])]
    ppermute x8, waiting for transfers between devices: 3.18 us -> 1.53 us  [swapped(): return lax.ppermute(value, 'core', [(i, 1 - i) for i in range(sides)])]
    pallas_call x9 -> x10, Pallas kernels: 17.6 us -> 17.5 us  [call(): pl.pallas_call(kernel, grid=(1,), in_specs=specs, out_specs=vmem_specs(le...]
  transfers between devices with their start and end apart: 35 -> 41, of which waited for: 23 -> 17; matrix products, arithmetic and copies ran while one was open for 0% -> 0% of each run, Pallas kernels for 1% -> 5%
where the time goes in v5:
time: 118 us; the launch traced here: 117 us
  starting transfers between devices  48.3 us (41%)
  waiting for transfers between devices  46.6 us (39%)
  Pallas kernels  19.8 us (17%)
  local copies, waits for them, and re-layouts  1.86 us (2%)
    ppermute x27, starting transfers between devices, shifted(): lax.ppermute(value, 'z', [(i, (i + shift) % groups) for i in range(groups)])  39.6 us
    ppermute x27, waiting for transfers between devices, shifted(): lax.ppermute(value, 'z', [(i, (i + shift) % groups) for i in range(groups)])  30.9 us
    pallas_call x10, Pallas kernels, call(): pl.pallas_call(kernel, grid=(1,), in_specs=specs, out_specs=vmem_specs(le...  17.5 us
    ppermute x6, waiting for transfers between devices, across(): lax.ppermute(value, 'pipe', [(i, i ^ distance) for i in range(sections)])  14.1 us
    ppermute x6, starting transfers between devices, across(): lax.ppermute(value, 'pipe', [(i, i ^ distance) for i in range(sections)])  7.04 us
  transfers between devices with their start and end apart: 41, of which 17 were waited for; matrix products, arithmetic and copies ran while one was open for 0% of the time, Pallas kernels for 5%

profile of v5, /device:TPU:0, one launch (start us, length us, event | category | flops | bytes accessed | tf_op | source)
XLA Modules:
  0.0 117.3 jit_solution(5831685944252602057)
XLA Ops:
  0.6 2.3 %pack.1 = (bf16[32,2176]{1,0:T(8,128)(2,1)}, bf16[32,2176]{1,0:T(8,128)(2,1)}, bf16[32,2176]{1,0:T(8,128)(2,1)}, bf16[32,2176]{1,0:T(8,128)(2,1)}, bf16[1040,128]{1,0:T(8,128)(2,1)}) custom-call(bf16[2,2,32,4096]{3,2,1,0:T(8,128)(2,1)} %refs_0_.1, bf16[2,2,32,4096]{3,2,1,0:T(8,128)(2,1)} %refs_1_.1, s32[2,2,4]{2,1,0:T(2,128)} %refs_2_.1, s32[2,2]{1,0:T(2,128)} %refs_3_.1, ...), custom_call_target="tpu_custom_call" | custom-call | tf_op jit(solution)/shard_map/pack/pallas_call | solution.py:121
  2.9 3.1 %collective-permute-start = (bf16[32,2176]{1,0:T(8,128)(2,1)}, bf16[32,2176]{1,0:T(8,128)(2,1)S(1)}, u32[]{:S(2)}, u32[]{:S(2)}) collective-permute-start(bf16[32,2176]{1,0:T(8,128)(2,1)} %get-tuple-element.65), channel_id=1, source_target_pairs={{0,2},{2,4},{4,6},{6,0},{1,3},{3,5},{5,7},{7,1},{8,10},{10,12},{12... | collective-permute-start | bytes 417800 | tf_op jit(solution)/shard_map/ppermute | solution.py:496
  6.0 2.4 %collective-permute-start.5 = (bf16[1040,128]{1,0:T(8,128)(2,1)}, bf16[1040,128]{1,0:T(8,128)(2,1)S(1)}, u32[]{:S(2)}, u32[]{:S(2)}) collective-permute-start(bf16[1040,128]{1,0:T(8,128)(2,1)} %get-tuple-element.73.refs_4_), channel_id=1, source_target_pairs={{0,24},{8,16},{16,8},{24,0},{1,25},{9,17},{17,9},{25,1},{2,26},{10... | collective-permute-start | bytes 798728 | tf_op jit(solution)/shard_map/ppermute | solution.py:499
  9.5 2.6 %collective-permute-start.1 = (bf16[32,2176]{1,0:T(8,128)(2,1)}, bf16[32,2176]{1,0:T(8,128)(2,1)S(1)}, u32[]{:S(2)}, u32[]{:S(2)}) collective-permute-start(bf16[32,2176]{1,0:T(8,128)(2,1)} %get-tuple-element.66), channel_id=1, source_target_pairs={{0,4},{2,6},{4,0},{6,2},{1,5},{3,7},{5,1},{7,3},{8,12},{10,14},{12... | collective-permute-start | bytes 417800 | tf_op jit(solution)/shard_map/ppermute | solution.py:496
  12.1 1.6 %collective-permute-start.2 = (bf16[32,2176]{1,0:T(8,128)(2,1)}, bf16[32,2176]{1,0:T(8,128)(2,1)S(1)}, u32[]{:S(2)}, u32[]{:S(2)}) collective-permute-start(bf16[32,2176]{1,0:T(8,128)(2,1)} %get-tuple-element.67), channel_id=1, source_target_pairs={{0,6},{2,0},{4,2},{6,4},{1,7},{3,1},{5,3},{7,5},{8,14},{10,8},{12,... | collective-permute-start | bytes 417800 | tf_op jit(solution)/shard_map/ppermute | solution.py:496
  13.7 5.4 %collective-permute-done.1.refs_2_ = bf16[32,2176]{1,0:T(8,128)(2,1)S(1)} collective-permute-done((bf16[32,2176]{1,0:T(8,128)(2,1)}, bf16[32,2176]{1,0:T(8,128)(2,1)S(1)}, u32[]{:S(2)}, u32[]{:S(2)}) %collective-permute-start.1) | collective-permute-done | bytes 139296 | tf_op jit(solution)/shard_map/ppermute | solution.py:496
  19.1 1.6 %collective-permute-done.4.refs_2_ = bf16[1040,128]{1,0:T(8,128)(2,1)S(1)} collective-permute-done((bf16[1040,128]{1,0:T(8,128)(2,1)}, bf16[1040,128]{1,0:T(8,128)(2,1)S(1)}, u32[]{:S(2)}, u32[]{:S(2)}) %collective-permute-start.4) | collective-permute-done | bytes 266272 | tf_op jit(solution)/shard_map/ppermute | solution.py:499
  24.0 3.0 %forward_first.1 = (bf16[1,8,128,128]{3,2,1,0:T(8,128)(2,1)S(1)}, bf16[128,1024]{1,0:T(8,128)(2,1)S(1)}, bf16[384,128]{1,0:T(8,128)(2,1)S(1)}, bf16[384,128]{1,0:T(8,128)(2,1)S(1)}, bf16[4,2,1040,128]{3,2,1,0:T(8,128)(2,1)S(1)}) custom-call(bf16[1040,128]{1,0:T(8,128)(2,1)S(1)} %get-tuple-element.74.refs_0_, ...), custom_call_target="tpu_custom_call" | custom-call | tf_op jit(solution)/shard_map/forward_first/pallas_call | solution.py:529
  27.0 2.6 %collective-permute-start.12 = (bf16[384,128]{1,0:T(8,128)(2,1)S(1)}, bf16[384,128]{1,0:T(8,128)(2,1)S(1)}, u32[]{:S(2)}, u32[]{:S(2)}) collective-permute-start(bf16[384,128]{1,0:T(8,128)(2,1)S(1)} %get-tuple-element.82.refs_0_), channel_id=1, source_target_pairs={{0,6},{2,0},{4,2},{6,4},{1,7},{3,1},{5,3},{7,5},{8,14},{10,8},{12,... | collective-permute-start | bytes 294920 | tf_op jit(solution)/shard_map/ppermute | solution.py:496
  30.0 1.6 %collective-permute-start.10 = (bf16[384,128]{1,0:T(8,128)(2,1)S(1)}, bf16[384,128]{1,0:T(8,128)(2,1)S(1)}, u32[]{:S(2)}, u32[]{:S(2)}) collective-permute-start(bf16[384,128]{1,0:T(8,128)(2,1)S(1)} %get-tuple-element.82.refs_0_), channel_id=1, source_target_pairs={{0,2},{2,4},{4,6},{6,0},{1,3},{3,5},{5,7},{7,1},{8,10},{10,12},{12... | collective-permute-start | bytes 294920 | tf_op jit(solution)/shard_map/ppermute | solution.py:496
  31.6 2.2 %collective-permute-start.18 = (bf16[384,128]{1,0:T(8,128)(2,1)S(1)}, bf16[384,128]{1,0:T(8,128)(2,1)S(1)}, u32[]{:S(2)}, u32[]{:S(2)}) collective-permute-start(bf16[384,128]{1,0:T(8,128)(2,1)S(1)} %get-tuple-element.85.refs_4_), channel_id=1, source_target_pairs={{0,6},{2,0},{4,2},{6,4},{1,7},{3,1},{5,3},{7,5},{8,14},{10,8},{12,... | collective-permute-start | bytes 294920 | tf_op jit(solution)/shard_map/ppermute | solution.py:496
  34.5 5.8 %collective-permute-done.11.refs_2_ = bf16[384,128]{1,0:T(8,128)(2,1)S(1)} collective-permute-done((bf16[384,128]{1,0:T(8,128)(2,1)S(1)}, bf16[384,128]{1,0:T(8,128)(2,1)S(1)}, u32[]{:S(2)}, u32[]{:S(2)}) %collective-permute-start.11) | collective-permute-done | bytes 98336 | tf_op jit(solution)/shard_map/ppermute | solution.py:496
  40.4 2.3 %forward_middle.2 = (bf16[128,1024]{1,0:T(8,128)(2,1)S(1)}, f32[128,128]{1,0:T(8,128)S(1)}, bf16[128,128]{1,0:T(8,128)(2,1)S(1)}, f32[128,128]{1,0:T(8,128)S(1)}...) custom-call(bf16[384,128]{1,0:T(8,128)(2,1)S(1)} %get-tuple-element.82.refs_0_, ...), custom_call_target="tpu_custom_call" | custom-call | tf_op jit(solution)/shard_map/forward_middle/pallas_call | solution.py:529
  42.7 3.5 %collective-permute-start.15 = (bf16[256,128]{1,0:T(8,128)(2,1)S(1)}, bf16[256,128]{1,0:T(8,128)(2,1)S(1)}, u32[]{:S(2)}, u32[]{:S(2)}) collective-permute-start(bf16[256,128]{1,0:T(8,128)(2,1)S(1)} %get-tuple-element.84.refs_0_), channel_id=1, source_target_pairs={{0,6},{2,0},{4,2},{6,4},{1,7},{3,1},{5,3},{7,5},{8,14},{10,8},{12,... | collective-permute-start | bytes 196616 | tf_op jit(solution)/shard_map/ppermute | solution.py:496
  46.2 2.1 %collective-permute-start.14 = (bf16[256,128]{1,0:T(8,128)(2,1)S(1)}, bf16[256,128]{1,0:T(8,128)(2,1)S(1)}, u32[]{:S(2)}, u32[]{:S(2)}) collective-permute-start(bf16[256,128]{1,0:T(8,128)(2,1)S(1)} %get-tuple-element.84.refs_0_), channel_id=1, source_target_pairs={{0,4},{2,6},{4,0},{6,2},{1,5},{3,7},{5,1},{7,3},{8,12},{10,14},{12... | collective-permute-start | bytes 196616 | tf_op jit(solution)/shard_map/ppermute | solution.py:496
  48.3 1.9 %collective-permute-start.13 = (bf16[256,128]{1,0:T(8,128)(2,1)S(1)}, bf16[256,128]{1,0:T(8,128)(2,1)S(1)}, u32[]{:S(2)}, u32[]{:S(2)}) collective-permute-start(bf16[256,128]{1,0:T(8,128)(2,1)S(1)} %get-tuple-element.84.refs_0_), channel_id=1, source_target_pairs={{0,2},{2,4},{4,6},{6,0},{1,3},{3,5},{5,7},{7,1},{8,10},{10,12},{12... | collective-permute-start | bytes 196616 | tf_op jit(solution)/shard_map/ppermute | solution.py:496
  50.3 4.4 %collective-permute-done.14.refs_2_ = bf16[256,128]{1,0:T(8,128)(2,1)S(1)} collective-permute-done((bf16[256,128]{1,0:T(8,128)(2,1)S(1)}, bf16[256,128]{1,0:T(8,128)(2,1)S(1)}, u32[]{:S(2)}, u32[]{:S(2)}) %collective-permute-start.14) | collective-permute-done | bytes 65568 | tf_op jit(solution)/shard_map/ppermute | solution.py:496
  54.7 2.3 %forward_middle.3 = (bf16[128,1024]{1,0:T(8,128)(2,1)S(1)}, f32[128,128]{1,0:T(8,128)S(1)}, bf16[128,128]{1,0:T(8,128)(2,1)S(1)}, f32[128,128]{1,0:T(8,128)S(1)}...) custom-call(bf16[256,128]{1,0:T(8,128)(2,1)S(1)} %get-tuple-element.84.refs_0_, ...), custom_call_target="tpu_custom_call" | custom-call | tf_op jit(solution)/shard_map/forward_middle/pallas_call | solution.py:529
  58.4 1.9 %collective-permute-start.19 = (bf16[256,128]{1,0:T(8,128)(2,1)S(1)}, bf16[256,128]{1,0:T(8,128)(2,1)S(1)}, u32[]{:S(2)}, u32[]{:S(2)}) collective-permute-start(bf16[256,128]{1,0:T(8,128)(2,1)S(1)} %get-tuple-element.88.refs_0_), channel_id=1, source_target_pairs={{0,2},{2,4},{4,6},{6,0},{1,3},{3,5},{5,7},{7,1},{8,10},{10,12},{12... | collective-permute-start | bytes 196616 | tf_op jit(solution)/shard_map/ppermute | solution.py:496
  61.4 3.6 %collective-permute-done.20.refs_2_ = bf16[256,128]{1,0:T(8,128)(2,1)S(1)} collective-permute-done((bf16[256,128]{1,0:T(8,128)(2,1)S(1)}, bf16[256,128]{1,0:T(8,128)(2,1)S(1)}, u32[]{:S(2)}, u32[]{:S(2)}) %collective-permute-start.20) | collective-permute-done | bytes 65568 | tf_op jit(solution)/shard_map/ppermute | solution.py:496
  65.0 3.3 %turn.1 = (bf16[128,1024]{1,0:T(8,128)(2,1)S(1)}, f32[128,128]{1,0:T(8,128)S(1)}, bf16[128,128]{1,0:T(8,128)(2,1)S(1)}, f32[128,128]{1,0:T(8,128)S(1)}, bf16[2,2...) custom-call(bf16[256,128]{1,0:T(8,128)(2,1)S(1)} %get-tuple-element., ...), custom_call_target="tpu_custom_call" | custom-call | tf_op jit(solution)/shard_map/turn/pallas_call | solution.py:529
  68.3 1.8 %collective-permute-start.24 = (bf16[144,128]{1,0:T(8,128)(2,1)S(1)}, bf16[144,128]{1,0:T(8,128)(2,1)S(1)}, u32[]{:S(2)}, u32[]{:S(2)}) collective-permute-start(bf16[144,128]{1,0:T(8,128)(2,1)S(1)} %get-tuple-element.91.refs_0_), channel_id=1, source_target_pairs={{0,6},{2,0},{4,2},{6,4},{1,7},{3,1},{5,3},{7,5},{8,14},{10,8},{12,... | collective-permute-start | bytes 110600 | tf_op jit(solution)/shard_map/ppermute | solution.py:496
  70.1 1.9 %collective-permute-start.22 = (bf16[144,128]{1,0:T(8,128)(2,1)S(1)}, bf16[144,128]{1,0:T(8,128)(2,1)S(1)}, u32[]{:S(2)}, u32[]{:S(2)}) collective-permute-start(bf16[144,128]{1,0:T(8,128)(2,1)S(1)} %get-tuple-element.91.refs_0_), channel_id=1, source_target_pairs={{0,2},{2,4},{4,6},{6,0},{1,3},{3,5},{5,7},{7,1},{8,10},{10,12},{12... | collective-permute-start | bytes 110600 | tf_op jit(solution)/shard_map/ppermute | solution.py:496
  72.0 1.9 %collective-permute-start.30 = (bf16[128,128]{1,0:T(8,128)(2,1)S(1)}, bf16[128,128]{1,0:T(8,128)(2,1)S(1)}, u32[]{:S(2)}, u32[]{:S(2)}) collective-permute-start(bf16[128,128]{1,0:T(8,128)(2,1)S(1)} %get-tuple-element.105.refs_16_), channel_id=1, source_target_pairs={{0,6},{2,0},{4,2},{6,4},{1,7},{3,1},{5,3},{7,5},{8,14},{10,8},{12,... | collective-permute-start | bytes 98312 | tf_op jit(solution)/shard_map/ppermute | solution.py:496
  75.9 1.7 %backward.3 = (bf16[272,512]{1,0:T(8,128)(2,1)S(1)}, bf16[272,512]{1,0:T(8,128)(2,1)S(1)}, bf16[128,1024]{1,0:T(8,128)(2,1)S(1)}, bf16[144,128]{1,0:T(8,128)(2,1)S(1)}) custom-call(bf16[144,128]{1,0:T(8,128)(2,1)S(1)} %get-tuple-element.91.refs_0_, bf16[144,128]{1,0:T(8,128)(2,1)S(1)} %collective-permute-done.22.refs_1_, ...), custom_call_target="tpu_custom_call" | custom-call | tf_op jit(solution)/shard_map/backward/pallas_call | solution.py:529
  80.9 1.7 %collective-permute-start.29 = (bf16[128,128]{1,0:T(8,128)(2,1)S(1)}, bf16[128,128]{1,0:T(8,128)(2,1)S(1)}, u32[]{:S(2)}, u32[]{:S(2)}) collective-permute-start(bf16[128,128]{1,0:T(8,128)(2,1)S(1)} %get-tuple-element.105.refs_16_), channel_id=1, source_target_pairs={{0,4},{2,6},{4,0},{6,2},{1,5},{3,7},{5,1},{7,3},{8,12},{10,14},{12... | collective-permute-start | bytes 98312 | tf_op jit(solution)/shard_map/ppermute | solution.py:496
  83.7 1.9 %collective-permute-done.29.refs_18_ = bf16[128,128]{1,0:T(8,128)(2,1)S(1)} collective-permute-done((bf16[128,128]{1,0:T(8,128)(2,1)S(1)}, bf16[128,128]{1,0:T(8,128)(2,1)S(1)}, u32[]{:S(2)}, u32[]{:S(2)}) %collective-permute-start.29) | collective-permute-done | bytes 32800 | tf_op jit(solution)/shard_map/ppermute | solution.py:496
  85.7 2.6 %collective-permute-done.28.refs_17_ = bf16[128,128]{1,0:T(8,128)(2,1)S(1)} collective-permute-done((bf16[128,128]{1,0:T(8,128)(2,1)S(1)}, bf16[128,128]{1,0:T(8,128)(2,1)S(1)}, u32[]{:S(2)}, u32[]{:S(2)}) %collective-permute-start.28) | collective-permute-done | bytes 32800 | tf_op jit(solution)/shard_map/ppermute | solution.py:496
  88.3 1.7 %backward.4 = (bf16[272,512]{1,0:T(8,128)(2,1)S(1)}, bf16[272,512]{1,0:T(8,128)(2,1)S(1)}, bf16[272,512]{1,0:T(8,128)(2,1)S(1)}, bf16[272,512]{1,0:T(8,128)(2,1)...) custom-call(bf16[144,128]{1,0:T(8,128)(2,1)S(1)} %get-tuple-element.99.refs_0_, ...), custom_call_target="tpu_custom_call" | custom-call | tf_op jit(solution)/shard_map/backward/pallas_call | solution.py:529
  95.1 1.7 %collective-permute-done.31.refs_1_ = bf16[144,128]{1,0:T(8,128)(2,1)S(1)} collective-permute-done((bf16[144,128]{1,0:T(8,128)(2,1)S(1)}, bf16[144,128]{1,0:T(8,128)(2,1)S(1)}, u32[]{:S(2)}, u32[]{:S(2)}) %collective-permute-start.31) | collective-permute-done | bytes 36896 | tf_op jit(solution)/shard_map/ppermute | solution.py:496
  104.0 6.0 %collective-permute-done.38.refs_1_ = bf16[272,512]{1,0:T(8,128)(2,1)S(1)} collective-permute-done((bf16[272,512]{1,0:T(8,128)(2,1)S(1)}, bf16[272,512]{1,0:T(8,128)(2,1)S(1)}, u32[]{:S(2)}, u32[]{:S(2)}) %collective-permute-start.38) | collective-permute-done | bytes 278560 | tf_op jit(solution)/shard_map/ppermute | solution.py:499
  110.0 6.4 %collective-permute-done.39.refs_2_ = bf16[272,512]{1,0:T(8,128)(2,1)S(1)} collective-permute-done((bf16[272,512]{1,0:T(8,128)(2,1)S(1)}, bf16[272,512]{1,0:T(8,128)(2,1)S(1)}, u32[]{:S(2)}, u32[]{:S(2)}) %collective-permute-start.39) | collective-permute-done | bytes 278560 | tf_op jit(solution)/shard_map/ppermute | solution.py:499
  (65 shorter events, 27.5 us)
Async XLA Ops:
  2.9 9.2 %collective-permute-start = (bf16[32,2176]{1,0:T(8,128)(2,1)}, bf16[32,2176]{1,0:T(8,128)(2,1)S(1)}, u32[]{:S(2)}, u32[]{:S(2)}) collective-permute-start(bf16[32,2176]{1,0:T(8,128)(2,1)} %get-tuple-element.65), channel_id=1, source_target_pairs={{0,2},{2,4},{4,6},{6,0},{1,3},{3,5},{5,7},{7,1},{8,10},{10,12},{12... | collective-permute-start | bytes 417800 | tf_op jit(solution)/shard_map/ppermute | solution.py:496
  6.0 13.1 %collective-permute-start.5 = (bf16[1040,128]{1,0:T(8,128)(2,1)}, bf16[1040,128]{1,0:T(8,128)(2,1)S(1)}, u32[]{:S(2)}, u32[]{:S(2)}) collective-permute-start(bf16[1040,128]{1,0:T(8,128)(2,1)} %get-tuple-element.73.refs_4_), channel_id=1, source_target_pairs={{0,24},{8,16},{16,8},{24,0},{1,25},{9,17},{17,9},{25,1},{2,26},{10... | collective-permute-start | bytes 798728 | tf_op jit(solution)/shard_map/ppermute | solution.py:499
  8.5 12.2 %collective-permute-start.4 = (bf16[1040,128]{1,0:T(8,128)(2,1)}, bf16[1040,128]{1,0:T(8,128)(2,1)S(1)}, u32[]{:S(2)}, u32[]{:S(2)}) collective-permute-start(bf16[1040,128]{1,0:T(8,128)(2,1)} %get-tuple-element.73.refs_4_), channel_id=1, source_target_pairs={{0,16},{8,24},{16,0},{24,8},{1,17},{9,25},{17,1},{25,9},{2,18},{10... | collective-permute-start | bytes 798728 | tf_op jit(solution)/shard_map/ppermute | solution.py:499
  9.0 11.8 %collective-permute-start.3 = (bf16[1040,128]{1,0:T(8,128)(2,1)}, bf16[1040,128]{1,0:T(8,128)(2,1)S(1)}, u32[]{:S(2)}, u32[]{:S(2)}) collective-permute-start(bf16[1040,128]{1,0:T(8,128)(2,1)} %get-tuple-element.73.refs_4_), channel_id=1, source_target_pairs={{0,8},{8,0},{16,24},{24,16},{1,9},{9,1},{17,25},{25,17},{2,10},{10... | collective-permute-start | bytes 798728 | tf_op jit(solution)/shard_map/ppermute | solution.py:499
  9.5 9.6 %collective-permute-start.1 = (bf16[32,2176]{1,0:T(8,128)(2,1)}, bf16[32,2176]{1,0:T(8,128)(2,1)S(1)}, u32[]{:S(2)}, u32[]{:S(2)}) collective-permute-start(bf16[32,2176]{1,0:T(8,128)(2,1)} %get-tuple-element.66), channel_id=1, source_target_pairs={{0,4},{2,6},{4,0},{6,2},{1,5},{3,7},{5,1},{7,3},{8,12},{10,14},{12... | collective-permute-start | bytes 417800 | tf_op jit(solution)/shard_map/ppermute | solution.py:496
  12.1 7.0 %collective-permute-start.2 = (bf16[32,2176]{1,0:T(8,128)(2,1)}, bf16[32,2176]{1,0:T(8,128)(2,1)S(1)}, u32[]{:S(2)}, u32[]{:S(2)}) collective-permute-start(bf16[32,2176]{1,0:T(8,128)(2,1)} %get-tuple-element.67), channel_id=1, source_target_pairs={{0,6},{2,0},{4,2},{6,4},{1,7},{3,1},{5,3},{7,5},{8,14},{10,8},{12,... | collective-permute-start | bytes 417800 | tf_op jit(solution)/shard_map/ppermute | solution.py:496
  27.0 7.6 %collective-permute-start.12 = (bf16[384,128]{1,0:T(8,128)(2,1)S(1)}, bf16[384,128]{1,0:T(8,128)(2,1)S(1)}, u32[]{:S(2)}, u32[]{:S(2)}) collective-permute-start(bf16[384,128]{1,0:T(8,128)(2,1)S(1)} %get-tuple-element.82.refs_0_), channel_id=1, source_target_pairs={{0,6},{2,0},{4,2},{6,4},{1,7},{3,1},{5,3},{7,5},{8,14},{10,8},{12,... | collective-permute-start | bytes 294920 | tf_op jit(solution)/shard_map/ppermute | solution.py:496
  29.6 10.8 %collective-permute-start.11 = (bf16[384,128]{1,0:T(8,128)(2,1)S(1)}, bf16[384,128]{1,0:T(8,128)(2,1)S(1)}, u32[]{:S(2)}, u32[]{:S(2)}) collective-permute-start(bf16[384,128]{1,0:T(8,128)(2,1)S(1)} %get-tuple-element.82.refs_0_), channel_id=1, source_target_pairs={{0,4},{2,6},{4,0},{6,2},{1,5},{3,7},{5,1},{7,3},{8,12},{10,14},{12... | collective-permute-start | bytes 294920 | tf_op jit(solution)/shard_map/ppermute | solution.py:496
  30.0 10.3 %collective-permute-start.10 = (bf16[384,128]{1,0:T(8,128)(2,1)S(1)}, bf16[384,128]{1,0:T(8,128)(2,1)S(1)}, u32[]{:S(2)}, u32[]{:S(2)}) collective-permute-start(bf16[384,128]{1,0:T(8,128)(2,1)S(1)} %get-tuple-element.82.refs_0_), channel_id=1, source_target_pairs={{0,2},{2,4},{4,6},{6,0},{1,3},{3,5},{5,7},{7,1},{8,10},{10,12},{12... | collective-permute-start | bytes 294920 | tf_op jit(solution)/shard_map/ppermute | solution.py:496
  31.6 16.7 %collective-permute-start.18 = (bf16[384,128]{1,0:T(8,128)(2,1)S(1)}, bf16[384,128]{1,0:T(8,128)(2,1)S(1)}, u32[]{:S(2)}, u32[]{:S(2)}) collective-permute-start(bf16[384,128]{1,0:T(8,128)(2,1)S(1)} %get-tuple-element.85.refs_4_), channel_id=1, source_target_pairs={{0,6},{2,0},{4,2},{6,4},{1,7},{3,1},{5,3},{7,5},{8,14},{10,8},{12,... | collective-permute-start | bytes 294920 | tf_op jit(solution)/shard_map/ppermute | solution.py:496
  33.9 16.4 %collective-permute-start.17 = (bf16[384,128]{1,0:T(8,128)(2,1)S(1)}, bf16[384,128]{1,0:T(8,128)(2,1)S(1)}, u32[]{:S(2)}, u32[]{:S(2)}) collective-permute-start(bf16[384,128]{1,0:T(8,128)(2,1)S(1)} %get-tuple-element.85.refs_4_), channel_id=1, source_target_pairs={{0,4},{2,6},{4,0},{6,2},{1,5},{3,7},{5,1},{7,3},{8,12},{10,14},{12... | collective-permute-start | bytes 294920 | tf_op jit(solution)/shard_map/ppermute | solution.py:496
  34.5 15.8 %collective-permute-start.16 = (bf16[384,128]{1,0:T(8,128)(2,1)S(1)}, bf16[384,128]{1,0:T(8,128)(2,1)S(1)}, u32[]{:S(2)}, u32[]{:S(2)}) collective-permute-start(bf16[384,128]{1,0:T(8,128)(2,1)S(1)} %get-tuple-element.85.refs_4_), channel_id=1, source_target_pairs={{0,2},{2,4},{4,6},{6,0},{1,3},{3,5},{5,7},{7,1},{8,10},{10,12},{12... | collective-permute-start | bytes 294920 | tf_op jit(solution)/shard_map/ppermute | solution.py:496
  42.7 7.6 %collective-permute-start.15 = (bf16[256,128]{1,0:T(8,128)(2,1)S(1)}, bf16[256,128]{1,0:T(8,128)(2,1)S(1)}, u32[]{:S(2)}, u32[]{:S(2)}) collective-permute-start(bf16[256,128]{1,0:T(8,128)(2,1)S(1)} %get-tuple-element.84.refs_0_), channel_id=1, source_target_pairs={{0,6},{2,0},{4,2},{6,4},{1,7},{3,1},{5,3},{7,5},{8,14},{10,8},{12,... | collective-permute-start | bytes 196616 | tf_op jit(solution)/shard_map/ppermute | solution.py:496
  46.2 8.4 %collective-permute-start.14 = (bf16[256,128]{1,0:T(8,128)(2,1)S(1)}, bf16[256,128]{1,0:T(8,128)(2,1)S(1)}, u32[]{:S(2)}, u32[]{:S(2)}) collective-permute-start(bf16[256,128]{1,0:T(8,128)(2,1)S(1)} %get-tuple-element.84.refs_0_), channel_id=1, source_target_pairs={{0,4},{2,6},{4,0},{6,2},{1,5},{3,7},{5,1},{7,3},{8,12},{10,14},{12... | collective-permute-start | bytes 196616 | tf_op jit(solution)/shard_map/ppermute | solution.py:496
  48.3 6.3 %collective-permute-start.13 = (bf16[256,128]{1,0:T(8,128)(2,1)S(1)}, bf16[256,128]{1,0:T(8,128)(2,1)S(1)}, u32[]{:S(2)}, u32[]{:S(2)}) collective-permute-start(bf16[256,128]{1,0:T(8,128)(2,1)S(1)} %get-tuple-element.84.refs_0_), channel_id=1, source_target_pairs={{0,2},{2,4},{4,6},{6,0},{1,3},{3,5},{5,7},{7,1},{8,10},{10,12},{12... | collective-permute-start | bytes 196616 | tf_op jit(solution)/shard_map/ppermute | solution.py:496
  58.3 6.7 %collective-permute-start.20 = (bf16[256,128]{1,0:T(8,128)(2,1)S(1)}, bf16[256,128]{1,0:T(8,128)(2,1)S(1)}, u32[]{:S(2)}, u32[]{:S(2)}) collective-permute-start(bf16[256,128]{1,0:T(8,128)(2,1)S(1)} %get-tuple-element.88.refs_0_), channel_id=1, source_target_pairs={{0,4},{2,6},{4,0},{6,2},{1,5},{3,7},{5,1},{7,3},{8,12},{10,14},{12... | collective-permute-start | bytes 196616 | tf_op jit(solution)/shard_map/ppermute | solution.py:496
  58.4 6.6 %collective-permute-start.19 = (bf16[256,128]{1,0:T(8,128)(2,1)S(1)}, bf16[256,128]{1,0:T(8,128)(2,1)S(1)}, u32[]{:S(2)}, u32[]{:S(2)}) collective-permute-start(bf16[256,128]{1,0:T(8,128)(2,1)S(1)} %get-tuple-element.88.refs_0_), channel_id=1, source_target_pairs={{0,2},{2,4},{4,6},{6,0},{1,3},{3,5},{5,7},{7,1},{8,10},{10,12},{12... | collective-permute-start | bytes 196616 | tf_op jit(solution)/shard_map/ppermute | solution.py:496
  68.3 5.6 %collective-permute-start.24 = (bf16[144,128]{1,0:T(8,128)(2,1)S(1)}, bf16[144,128]{1,0:T(8,128)(2,1)S(1)}, u32[]{:S(2)}, u32[]{:S(2)}) collective-permute-start(bf16[144,128]{1,0:T(8,128)(2,1)S(1)} %get-tuple-element.91.refs_0_), channel_id=1, source_target_pairs={{0,6},{2,0},{4,2},{6,4},{1,7},{3,1},{5,3},{7,5},{8,14},{10,8},{12,... | collective-permute-start | bytes 110600 | tf_op jit(solution)/shard_map/ppermute | solution.py:496
  70.1 5.1 %collective-permute-start.23 = (bf16[144,128]{1,0:T(8,128)(2,1)S(1)}, bf16[144,128]{1,0:T(8,128)(2,1)S(1)}, u32[]{:S(2)}, u32[]{:S(2)}) collective-permute-start(bf16[144,128]{1,0:T(8,128)(2,1)S(1)} %get-tuple-element.91.refs_0_), channel_id=1, source_target_pairs={{0,4},{2,6},{4,0},{6,2},{1,5},{3,7},{5,1},{7,3},{8,12},{10,14},{12... | collective-permute-start | bytes 110600 | tf_op jit(solution)/shard_map/ppermute | solution.py:496
  70.1 5.8 %collective-permute-start.22 = (bf16[144,128]{1,0:T(8,128)(2,1)S(1)}, bf16[144,128]{1,0:T(8,128)(2,1)S(1)}, u32[]{:S(2)}, u32[]{:S(2)}) collective-permute-start(bf16[144,128]{1,0:T(8,128)(2,1)S(1)} %get-tuple-element.91.refs_0_), channel_id=1, source_target_pairs={{0,2},{2,4},{4,6},{6,0},{1,3},{3,5},{5,7},{7,1},{8,10},{10,12},{12... | collective-permute-start | bytes 110600 | tf_op jit(solution)/shard_map/ppermute | solution.py:496
  72.0 10.6 %collective-permute-start.30 = (bf16[128,128]{1,0:T(8,128)(2,1)S(1)}, bf16[128,128]{1,0:T(8,128)(2,1)S(1)}, u32[]{:S(2)}, u32[]{:S(2)}) collective-permute-start(bf16[128,128]{1,0:T(8,128)(2,1)S(1)} %get-tuple-element.105.refs_16_), channel_id=1, source_target_pairs={{0,6},{2,0},{4,2},{6,4},{1,7},{3,1},{5,3},{7,5},{8,14},{10,8},{12,... | collective-permute-start | bytes 98312 | tf_op jit(solution)/shard_map/ppermute | solution.py:496
  77.6 10.7 %collective-permute-start.27 = (bf16[144,128]{1,0:T(8,128)(2,1)S(1)}, bf16[144,128]{1,0:T(8,128)(2,1)S(1)}, u32[]{:S(2)}, u32[]{:S(2)}) collective-permute-start(bf16[144,128]{1,0:T(8,128)(2,1)S(1)} %get-tuple-element.99.refs_0_), channel_id=1, source_target_pairs={{0,6},{2,0},{4,2},{6,4},{1,7},{3,1},{5,3},{7,5},{8,14},{10,8},{12,... | collective-permute-start | bytes 110600 | tf_op jit(solution)/shard_map/ppermute | solution.py:496
  78.7 9.6 %collective-permute-start.26 = (bf16[144,128]{1,0:T(8,128)(2,1)S(1)}, bf16[144,128]{1,0:T(8,128)(2,1)S(1)}, u32[]{:S(2)}, u32[]{:S(2)}) collective-permute-start(bf16[144,128]{1,0:T(8,128)(2,1)S(1)} %get-tuple-element.99.refs_0_), channel_id=1, source_target_pairs={{0,4},{2,6},{4,0},{6,2},{1,5},{3,7},{5,1},{7,3},{8,12},{10,14},{12... | collective-permute-start | bytes 110600 | tf_op jit(solution)/shard_map/ppermute | solution.py:496
  79.3 9.0 %collective-permute-start.25 = (bf16[144,128]{1,0:T(8,128)(2,1)S(1)}, bf16[144,128]{1,0:T(8,128)(2,1)S(1)}, u32[]{:S(2)}, u32[]{:S(2)}) collective-permute-start(bf16[144,128]{1,0:T(8,128)(2,1)S(1)} %get-tuple-element.99.refs_0_), channel_id=1, source_target_pairs={{0,2},{2,4},{4,6},{6,0},{1,3},{3,5},{5,7},{7,1},{8,10},{10,12},{12... | collective-permute-start | bytes 110600 | tf_op jit(solution)/shard_map/ppermute | solution.py:496
  82.6 5.7 %collective-permute-start.28 = (bf16[128,128]{1,0:T(8,128)(2,1)S(1)}, bf16[128,128]{1,0:T(8,128)(2,1)S(1)}, u32[]{:S(2)}, u32[]{:S(2)}) collective-permute-start(bf16[128,128]{1,0:T(8,128)(2,1)S(1)} %get-tuple-element.105.refs_16_), channel_id=1, source_target_pairs={{0,2},{2,4},{4,6},{6,0},{1,3},{3,5},{5,7},{7,1},{8,10},{10,12},{12... | collective-permute-start | bytes 98312 | tf_op jit(solution)/shard_map/ppermute | solution.py:496
  90.3 4.9 %collective-permute-start.32 = (bf16[144,128]{1,0:T(8,128)(2,1)S(1)}, bf16[144,128]{1,0:T(8,128)(2,1)S(1)}, u32[]{:S(2)}, u32[]{:S(2)}) collective-permute-start(bf16[144,128]{1,0:T(8,128)(2,1)S(1)} %get-tuple-element.107.refs_0_), channel_id=1, source_target_pairs={{0,4},{2,6},{4,0},{6,2},{1,5},{3,7},{5,1},{7,3},{8,12},{10,14},{12... | collective-permute-start | bytes 110600 | tf_op jit(solution)/shard_map/ppermute | solution.py:496
  90.9 5.9 %collective-permute-start.31 = (bf16[144,128]{1,0:T(8,128)(2,1)S(1)}, bf16[144,128]{1,0:T(8,128)(2,1)S(1)}, u32[]{:S(2)}, u32[]{:S(2)}) collective-permute-start(bf16[144,128]{1,0:T(8,128)(2,1)S(1)} %get-tuple-element.107.refs_0_), channel_id=1, source_target_pairs={{0,2},{2,4},{4,6},{6,0},{1,3},{3,5},{5,7},{7,1},{8,10},{10,12},{12... | collective-permute-start | bytes 110600 | tf_op jit(solution)/shard_map/ppermute | solution.py:496
  92.1 6.2 %collective-permute-start.36 = (bf16[272,512]{1,0:T(8,128)(2,1)S(1)}, bf16[272,512]{1,0:T(8,128)(2,1)S(1)}, u32[]{:S(2)}, u32[]{:S(2)}) collective-permute-start(bf16[272,512]{1,0:T(8,128)(2,1)S(1)} %get-tuple-element.119), channel_id=1, source_target_pairs={{0,1},{1,0},{2,3},{3,2},{4,5},{5,4},{6,7},{7,6},{8,9},{9,8},{10,11... | collective-permute-start | bytes 835592 | tf_op jit(solution)/shard_map/ppermute | solution.py:502
  92.1 6.2 %collective-permute-start.35 = (bf16[272,512]{1,0:T(8,128)(2,1)S(1)}, bf16[272,512]{1,0:T(8,128)(2,1)S(1)}, u32[]{:S(2)}, u32[]{:S(2)}) collective-permute-start(bf16[272,512]{1,0:T(8,128)(2,1)S(1)} %get-tuple-element.118), channel_id=1, source_target_pairs={{0,1},{1,0},{2,3},{3,2},{4,5},{5,4},{6,7},{7,6},{8,9},{9,8},{10,11... | collective-permute-start | bytes 835592 | tf_op jit(solution)/shard_map/ppermute | solution.py:502
  100.4 9.6 %collective-permute-start.38 = (bf16[272,512]{1,0:T(8,128)(2,1)S(1)}, bf16[272,512]{1,0:T(8,128)(2,1)S(1)}, u32[]{:S(2)}, u32[]{:S(2)}) collective-permute-start(bf16[272,512]{1,0:T(8,128)(2,1)S(1)} %get-tuple-element.122), channel_id=1, source_target_pairs={{0,8},{8,0},{16,24},{24,16},{1,9},{9,1},{17,25},{25,17},{2,10},{10... | collective-permute-start | bytes 835592 | tf_op jit(solution)/shard_map/ppermute | solution.py:499
  102.0 14.4 %collective-permute-start.39 = (bf16[272,512]{1,0:T(8,128)(2,1)S(1)}, bf16[272,512]{1,0:T(8,128)(2,1)S(1)}, u32[]{:S(2)}, u32[]{:S(2)}) collective-permute-start(bf16[272,512]{1,0:T(8,128)(2,1)S(1)} %get-tuple-element.123), channel_id=1, source_target_pairs={{0,16},{8,24},{16,0},{24,8},{1,17},{9,25},{17,1},{25,9},{2,18},{10... | collective-permute-start | bytes 835592 | tf_op jit(solution)/shard_map/ppermute | solution.py:499
  103.5 12.9 %collective-permute-start.40 = (bf16[272,512]{1,0:T(8,128)(2,1)S(1)}, bf16[272,512]{1,0:T(8,128)(2,1)S(1)}, u32[]{:S(2)}, u32[]{:S(2)}) collective-permute-start(bf16[272,512]{1,0:T(8,128)(2,1)S(1)} %get-tuple-element.124), channel_id=1, source_target_pairs={{0,24},{8,16},{16,8},{24,0},{1,25},{9,17},{17,9},{25,1},{2,26},{10... | collective-permute-start | bytes 835592 | tf_op jit(solution)/shard_map/ppermute | solution.py:499
  (11 other events, 32.6 us)

commit v6 on v5

--- a/solution.py
+++ b/solution.py
@@ -32,6 +32,10 @@
     return high, (value - high.astype(F32)).astype(BF)
 
 
+def member():
+    return lax.axis_index("zl") * lax.axis_size("core") + lax.axis_index("core")
+
+
 def vmem_specs(count):
     return [pl.BlockSpec(memory_space=pltpu.VMEM)] * count
 
@@ -49,10 +53,9 @@
     parts, weights = refs[7 : 7 + groups], refs[7 + groups]
     tok, cot, starts_in, counts_in, gain_in, second_in, sems = refs[8 + groups :]
     directions, micro_count, length, width = tokens.shape
+    own = first.shape[1]
     local = width // groups
-    own = first.shape[1]
     section = lax.axis_index("pipe")
-    group = lax.axis_index("z")
     picks = []
     copies = [
         pltpu.make_async_copy(second.at[0], second_in, sems.at[0]),
@@ -102,14 +105,16 @@
             document.astype(F32),
             jnp.where(lane == 1, mean_high.astype(F32), mean_low.astype(F32)),
         ).astype(BF)
-        for shift in range(groups):
-            start = pl.multiple_of(((group + shift) % groups) * local, local)
-            parts[shift][rows, 0:local] = tok[rows, pl.ds(start, local)]
-            cotangent = cot[rows, pl.ds(start, local)]
-            parts[shift][rows, local : 2 * local] = jnp.where(
-                keep, cotangent, jnp.zeros_like(cotangent)
-            )
-            parts[shift][rows, 2 * local :] = tail
+        for distance in range(groups):
+            for side in range(local // own):
+                start = pl.multiple_of((side * groups + (member() ^ distance)) * own, own)
+                at = side * own
+                parts[distance][rows, at : at + own] = tok[rows, pl.ds(start, own)]
+                cotangent = cot[rows, pl.ds(start, own)]
+                parts[distance][rows, local + at : local + at + own] = jnp.where(
+                    keep, cotangent, jnp.zeros_like(cotangent)
+                )
+            parts[distance][rows, 2 * local :] = tail
 
 
 def pack(tokens, cotangents, starts, counts, gain, first, second, groups, micro_local):
@@ -240,18 +245,19 @@
     packed_out[...] = packed[...]
 
 
-def first_kernel(sections, *refs):
-    mine, theirs = refs[:sections], refs[sections : 2 * sections]
-    x, cot, mask, mean, probs, mixed, pay, side, weights, sems = refs[2 * sections :]
-    section, core = lax.axis_index("pipe"), lax.axis_index("core")
+def first_kernel(sections, sides, *refs):
+    parts, refs = refs[: sections * sides], refs[sections * sides :]
+    x, cot, mask, mean, probs, mixed, pay, side, weights, sems = refs
+    section, half = lax.axis_index("pipe"), lax.axis_index("zh")
     rows = x.shape[0]
     copies = []
-    for distance in range(sections):
-        layer = section ^ distance
-        for parts, place in ((mine, core), (theirs, 1 - core)):
+    for far in range(sides):
+        for distance in range(sections):
             copies.append(
                 pltpu.make_async_copy(
-                    parts[distance], weights.at[layer, place], sems.at[distance, place]
+                    parts[far * sections + distance],
+                    weights.at[section ^ distance, half ^ far],
+                    sems.at[distance, far],
                 )
             )
     for copy in copies:
@@ -270,10 +276,9 @@
 
 
 def place_rows(received, target, columns):
-    groups = len(received)
     rows = received[0].shape[0]
-    for shift, part in enumerate(received):
-        source = (lax.axis_index("z") + groups - shift) % groups
+    for distance, part in enumerate(received):
+        source = member() ^ distance
         target[pl.ds(pl.multiple_of(source * rows, rows), rows), :] = part[:, columns]
 
 
@@ -390,10 +395,9 @@
     )
 
 
-def split_sides(grads, keep, send):
-    core = lax.axis_index("core")
-    keep[...] = grads[core]
-    send[...] = grads[1 - core]
+def split_sides(grads, outs):
+    for far, out in enumerate(outs):
+        out[...] = grads[lax.axis_index("zh") ^ far]
 
 
 def back_kernel(count, with_last, to_first, width, *refs):
@@ -409,11 +413,10 @@
     if with_last:
         last_parts, cot, turn_grads = refs[:count], refs[count], refs[count + 1]
         refs = refs[count + 2 :]
-    keep, send = refs[:2]
-    refs = refs[2:]
+    sides = weights.shape[1]
+    outs, refs = refs[:sides], refs[sides:]
     if with_last:
-        last_keep, last_send = refs[:2]
-        refs = refs[2:]
+        last_outs, refs = refs[:sides], refs[sides:]
     if not to_first:
         carried, pay = refs[:2]
         refs = refs[2:]
@@ -447,20 +450,23 @@
             grads[side, 0:rank, :] = turn_grads[side, 0:rank, :]
             grads[side, rank : 2 * rank, :] = second[:, side * own : (side + 1) * own]
             grads[side, 2 * rank :, :] = turn_grads[side, 2 * rank :, :]
-        split_sides(grads, last_keep, last_send)
+        split_sides(grads, last_outs)
     layer_backward(
         dout, dred, x, mean[:, 0:1], mask, weights, weights_before, probs, mixed, reduced[...],
         grads, carried, pay,
     )
-    split_sides(grads, keep, send)
-
-
-def combine_kernel(sections, *refs):
-    kept, swapped = refs[:sections], refs[sections : 2 * sections]
-    outs, sums = refs[2 * sections : 3 * sections], refs[3 * sections]
+    split_sides(grads, outs)
+
+
+def combine_kernel(sections, sides, *refs):
+    parts, refs = refs[: sections * sides], refs[sections * sides :]
+    outs, sums = refs[:sections], refs[sections]
     section = lax.axis_index("pipe")
     for layer in range(sections):
-        sums[layer] = (kept[layer][...].astype(F32) + swapped[layer][...].astype(F32)).astype(BF)
+        total = parts[layer * sides][...].astype(F32)
+        for part in parts[layer * sides + 1 : (layer + 1) * sides]:
+            total = total + part[...].astype(F32)
+        sums[layer] = total.astype(BF)
     for distance in range(sections):
         outs[distance][...] = sums[section ^ distance]
 
@@ -479,7 +485,7 @@
 
 def per_device(tokens, cotangents, starts, counts, layer_gains, first_map, second_map):
     sections = lax.axis_size("pipe")
-    groups = lax.axis_size("z")
+    groups = lax.axis_size("zl") * lax.axis_size("core")
     directions, micro_count, length, width = tokens.shape
     micro_local = -(-directions * micro_count // sections)
     rows = groups * micro_local * length
@@ -489,29 +495,30 @@
     heads = local // HD
     size = block_size(rows)
     blocks = rows // size
-    sides = lax.axis_size("core")
+    sides = lax.axis_size("zh")
     top = sections - 1
 
-    def shifted(value, shift):
-        return lax.ppermute(value, "z", [(i, (i + shift) % groups) for i in range(groups)])
-
-    def across(value, distance):
-        return lax.ppermute(value, "pipe", [(i, i ^ distance) for i in range(sections)])
-
-    def swapped(value):
-        return lax.ppermute(value, "core", [(i, 1 - i) for i in range(sides)])
+    def moved(value, axes, distance):
+        size = lax.axis_size(axes)
+        return lax.ppermute(value, axes, [(i, i ^ distance) for i in range(size)])
+
+    def each(values, axes):
+        return [values[0]] + [
+            moved(value, axes, distance) for distance, value in enumerate(values) if distance
+        ]
 
     def exchange(pay):
-        return [pay] + [shifted(pay, shift) for shift in range(1, groups)]
+        return each([pay] * groups, ("zl", "core"))
 
     token_parts, packed = pack(
         tokens, cotangents, starts, counts, layer_gains, first_map, second_map, groups, micro_local
     )
-    received = [token_parts[0]]
-    received += [shifted(token_parts[shift], shift) for shift in range(1, groups)]
-    mine = [packed] + [across(packed, distance) for distance in range(1, sections)]
-    received, mine = lax.optimization_barrier((received, mine))
-    theirs = [swapped(part) for part in mine]
+    packed_far = each([packed] * sides, "zh")
+    mine = each([packed] * sections, "pipe")
+    received = each(token_parts, ("zl", "core"))
+    received, mine, packed_far = lax.optimization_barrier((received, mine, packed_far))
+    for part in packed_far[1:]:
+        mine = mine + each([part] * sections, "pipe")
 
     def shaped(shape, kind=BF):
         return jax.ShapeDtypeStruct(shape, kind)
@@ -555,9 +562,9 @@
         scratch_shapes=[pltpu.VMEM((rows, HD), BF)],
     )
     probs, mixed, pay, side, weights = call(
-        functools.partial(first_kernel, sections),
-        (*mine, *theirs, x, cot, mask, mean),
-        vmem_specs(2 * sections + 4),
+        functools.partial(first_kernel, sections, sides),
+        (*mine, x, cot, mask, mean),
+        vmem_specs(sides * sections + 4),
         [
             probs_shape,
             wide_shape,
@@ -624,7 +631,7 @@
     reduceds.append(reduced)
     crosses.append(cross)
 
-    kept, taken = [None] * sections, [None] * sections
+    halves = [None] * sections
     for layer in range(top - 1, -1, -1):
         pays = exchange(pay)
         if layer == top - 1:
@@ -641,11 +648,11 @@
             specs += [layer_of(layer - 1)]
         operands += (all_probs[layer], all_mixed[layer], reduceds[layer])
         specs += vmem_specs(3)
-        outs = [half_shape] * 2
+        outs = [half_shape] * sides
         if with_last:
             operands += (*last_parts, cot, turn_grads)
             specs += vmem_specs(groups + 2)
-            outs += [half_shape] * 2
+            outs += [half_shape] * sides
         if not to_first:
             outs += [wide_shape, shaped((back_rows, HD))]
         result = call(
@@ -656,21 +663,21 @@
             "backward",
             scratch_shapes=[pltpu.VMEM(wide_shape.shape, BF), pltpu.VMEM(grads_shape, BF)],
         )
-        kept[layer], taken[layer] = result[0], swapped(result[1])
+        halves[layer] = each(result[:sides], "zh")
         if with_last:
-            kept[top], taken[top] = result[2], swapped(result[3])
+            halves[top] = each(result[sides : 2 * sides], "zh")
         if not to_first:
             carried, pay = result[-2:]
 
     parts = call(
-        functools.partial(combine_kernel, sections),
-        (*kept, *taken),
-        vmem_specs(2 * sections),
+        functools.partial(combine_kernel, sections, sides),
+        sum(halves, []),
+        vmem_specs(sections * sides),
         [half_shape] * sections,
         "combine",
         scratch_shapes=[pltpu.VMEM((sections,) + grads_shape[1:], BF)],
     )
-    arrived = [parts[0]] + [across(parts[distance], distance) for distance in range(1, sections)]
+    arrived = each(parts, "pipe")
     gain_grad, first_grad, second_grad = call(
         functools.partial(finish_kernel, sections),
         arrived,
@@ -687,9 +694,10 @@
 
 def solution(mesh):
     fine = Mesh(
-        mesh.devices.reshape(mesh.shape["pipe"], mesh.shape["dp"] // 2, 2), ("pipe", "z", "core")
-    )
-    data = ("z", "core")
+        mesh.devices.reshape(mesh.shape["pipe"], mesh.shape["dp"] // 4, 2, 2),
+        ("pipe", "zh", "zl", "core"),
+    )
+    data = ("zh", "zl", "core")
     in_specs = (
         P(None, data, None, None),
         P(None, data, None, None),

time: 118 us -> 152 us (1.29)
  waiting for transfers between devices: 46.6 us -> 92.7 us
  starting transfers between devices: 48.3 us -> 37.2 us
    ppermute x41, waiting for transfers between devices: 46.6 us -> 92.7 us  [moved(): return lax.ppermute(value, axes, [(i, i ^ distance) for i in range(size)])]
    ppermute x41, starting transfers between devices: 48.3 us -> 37.2 us  [moved(): return lax.ppermute(value, axes, [(i, i ^ distance) for i in range(size)])]
  transfers between devices with their start and end apart: 41 -> 41, of which waited for: 17 -> 23; matrix products, arithmetic and copies ran while one was open for 0% -> 0% of each run, Pallas kernels for 5% -> 4%
where the time goes in v6:
time: 152 us
  waiting for transfers between devices  92.7 us (61%)
  starting transfers between devices  37.2 us (24%)
  Pallas kernels  19.8 us (13%)
  local copies, waits for them, and re-layouts  1.86 us (1%)
    ppermute x41, waiting for transfers between devices, moved(): return lax.ppermute(value, axes, [(i, i ^ distance) for i in range(size)])  92.7 us
    ppermute x41, starting transfers between devices, moved(): return lax.ppermute(value, axes, [(i, i ^ distance) for i in range(size)])  37.2 us
    pallas_call x10, Pallas kernels, call(): pl.pallas_call(kernel, grid=(1,), in_specs=specs, out_specs=vmem_specs(le...  17.5 us
  transfers between devices with their start and end apart: 41, of which 23 were waited for; matrix products, arithmetic and copies ran while one was open for 0% of the time, Pallas kernels for 4%

profile of v6, /device:TPU:0, one launch (start us, length us, event | category | flops | bytes accessed | tf_op | source)
XLA Modules:
  0.0 152.3 jit_solution(10537287483436726948)
XLA Ops:
  0.6 2.3 %pack.1 = (bf16[32,2176]{1,0:T(8,128)(2,1)}, bf16[32,2176]{1,0:T(8,128)(2,1)}, bf16[32,2176]{1,0:T(8,128)(2,1)}, bf16[32,2176]{1,0:T(8,128)(2,1)}, bf16[1040,128]{1,0:T(8,128)(2,1)}) custom-call(bf16[2,2,32,4096]{3,2,1,0:T(8,128)(2,1)} %refs_0_.1, bf16[2,2,32,4096]{3,2,1,0:T(8,128)(2,1)} %refs_1_.1, s32[2,2,4]{2,1,0:T(2,128)} %refs_2_.1, s32[2,2]{1,0:T(2,128)} %refs_3_.1, ...), custom_call_target="tpu_custom_call" | custom-call | tf_op jit(solution)/shard_map/pack/pallas_call | solution.py:126
  3.5 2.6 %collective-permute-start.1 = (bf16[32,2176]{1,0:T(8,128)(2,1)}, bf16[32,2176]{1,0:T(8,128)(2,1)S(1)}, u32[]{:S(2)}, u32[]{:S(2)}) collective-permute-start(bf16[32,2176]{1,0:T(8,128)(2,1)} %get-tuple-element.67), channel_id=1, source_target_pairs={{0,2},{1,3},{2,0},{3,1},{4,6},{5,7},{6,4},{7,5},{8,10},{9,11},{10,... | collective-permute-start | bytes 417800 | tf_op jit(solution)/shard_map/ppermute | solution.py:503
  6.1 2.6 %collective-permute-start.6 = (bf16[1040,128]{1,0:T(8,128)(2,1)}, bf16[1040,128]{1,0:T(8,128)(2,1)S(1)}, u32[]{:S(2)}, u32[]{:S(2)}) collective-permute-start(bf16[1040,128]{1,0:T(8,128)(2,1)} %get-tuple-element.74.refs_4_), channel_id=1, source_target_pairs={{0,4},{4,0},{1,5},{5,1},{2,6},{6,2},{3,7},{7,3},{8,12},{12,8},{9,1... | collective-permute-start | bytes 798728 | tf_op jit(solution)/shard_map/ppermute | solution.py:503
  8.7 2.4 %collective-permute-start.5 = (bf16[1040,128]{1,0:T(8,128)(2,1)}, bf16[1040,128]{1,0:T(8,128)(2,1)S(1)}, u32[]{:S(2)}, u32[]{:S(2)}) collective-permute-start(bf16[1040,128]{1,0:T(8,128)(2,1)} %get-tuple-element.74.refs_4_), channel_id=1, source_target_pairs={{0,24},{8,16},{16,8},{24,0},{1,25},{9,17},{17,9},{25,1},{2,26},{10... | collective-permute-start | bytes 798728 | tf_op jit(solution)/shard_map/ppermute | solution.py:503
  13.5 8.8 %collective-permute-done.2.refs_3_ = bf16[32,2176]{1,0:T(8,128)(2,1)S(1)} collective-permute-done((bf16[32,2176]{1,0:T(8,128)(2,1)}, bf16[32,2176]{1,0:T(8,128)(2,1)S(1)}, u32[]{:S(2)}, u32[]{:S(2)}) %collective-permute-start.2) | collective-permute-done | bytes 139296 | tf_op jit(solution)/shard_map/ppermute | solution.py:503
  23.8 1.6 %collective-permute-start.9 = (bf16[1040,128]{1,0:T(8,128)(2,1)S(1)}, bf16[1040,128]{1,0:T(8,128)(2,1)S(1)}, u32[]{:S(2)}, u32[]{:S(2)}) collective-permute-start(bf16[1040,128]{1,0:T(8,128)(2,1)S(1)} %collective-permute-done.6.refs_4_), channel_id=1, source_target_pairs={{0,24},{8,16},{16,8},{24,0},{1,25},{9,17},{17,9},{25,1},{2,26},{10... | collective-permute-start | bytes 798728 | tf_op jit(solution)/shard_map/ppermute | solution.py:503
  29.4 4.6 %collective-permute-done.9.refs_7_ = bf16[1040,128]{1,0:T(8,128)(2,1)S(1)} collective-permute-done((bf16[1040,128]{1,0:T(8,128)(2,1)S(1)}, bf16[1040,128]{1,0:T(8,128)(2,1)S(1)}, u32[]{:S(2)}, u32[]{:S(2)}) %collective-permute-start.9) | collective-permute-done | bytes 266272 | tf_op jit(solution)/shard_map/ppermute | solution.py:503
  34.0 4.6 %collective-permute-done.8.refs_6_ = bf16[1040,128]{1,0:T(8,128)(2,1)S(1)} collective-permute-done((bf16[1040,128]{1,0:T(8,128)(2,1)S(1)}, bf16[1040,128]{1,0:T(8,128)(2,1)S(1)}, u32[]{:S(2)}, u32[]{:S(2)}) %collective-permute-start.8) | collective-permute-done | bytes 266272 | tf_op jit(solution)/shard_map/ppermute | solution.py:503
  38.7 3.0 %forward_first.1 = (bf16[1,8,128,128]{3,2,1,0:T(8,128)(2,1)S(1)}, bf16[128,1024]{1,0:T(8,128)(2,1)S(1)}, bf16[384,128]{1,0:T(8,128)(2,1)S(1)}, bf16[384,128]{1,0:T(8,128)(2,1)S(1)}, bf16[4,2,1040,128]{3,2,1,0:T(8,128)(2,1)S(1)}) custom-call(bf16[1040,128]{1,0:T(8,128)(2,1)S(1)} %get-tuple-element.75.refs_0_, ...), custom_call_target="tpu_custom_call" | custom-call | tf_op jit(solution)/shard_map/forward_first/pallas_call | solution.py:536
  41.8 1.5 %collective-permute-start.11 = (bf16[384,128]{1,0:T(8,128)(2,1)S(1)}, bf16[384,128]{1,0:T(8,128)(2,1)S(1)}, u32[]{:S(2)}, u32[]{:S(2)}) collective-permute-start(bf16[384,128]{1,0:T(8,128)(2,1)S(1)} %get-tuple-element.84.refs_0_), channel_id=1, source_target_pairs={{0,2},{1,3},{2,0},{3,1},{4,6},{5,7},{6,4},{7,5},{8,10},{9,11},{10,... | collective-permute-start | bytes 294920 | tf_op jit(solution)/shard_map/ppermute | solution.py:503
  46.9 2.2 %collective-permute-done.11.refs_2_ = bf16[384,128]{1,0:T(8,128)(2,1)S(1)} collective-permute-done((bf16[384,128]{1,0:T(8,128)(2,1)S(1)}, bf16[384,128]{1,0:T(8,128)(2,1)S(1)}, u32[]{:S(2)}, u32[]{:S(2)}) %collective-permute-start.11) | collective-permute-done | bytes 98336 | tf_op jit(solution)/shard_map/ppermute | solution.py:503
  49.1 2.3 %forward_middle.2 = (bf16[128,1024]{1,0:T(8,128)(2,1)S(1)}, f32[128,128]{1,0:T(8,128)S(1)}, bf16[128,128]{1,0:T(8,128)(2,1)S(1)}, f32[128,128]{1,0:T(8,128)S(1)}...) custom-call(bf16[384,128]{1,0:T(8,128)(2,1)S(1)} %get-tuple-element.84.refs_0_, ...), custom_call_target="tpu_custom_call" | custom-call | tf_op jit(solution)/shard_map/forward_middle/pallas_call | solution.py:536
  51.5 1.5 %collective-permute-start.14 = (bf16[256,128]{1,0:T(8,128)(2,1)S(1)}, bf16[256,128]{1,0:T(8,128)(2,1)S(1)}, u32[]{:S(2)}, u32[]{:S(2)}) collective-permute-start(bf16[256,128]{1,0:T(8,128)(2,1)S(1)} %get-tuple-element.86.refs_0_), channel_id=1, source_target_pairs={{0,2},{1,3},{2,0},{3,1},{4,6},{5,7},{6,4},{7,5},{8,10},{9,11},{10,... | collective-permute-start | bytes 196616 | tf_op jit(solution)/shard_map/ppermute | solution.py:503
  53.3 2.4 %collective-permute-done.15.refs_3_ = bf16[256,128]{1,0:T(8,128)(2,1)S(1)} collective-permute-done((bf16[256,128]{1,0:T(8,128)(2,1)S(1)}, bf16[256,128]{1,0:T(8,128)(2,1)S(1)}, u32[]{:S(2)}, u32[]{:S(2)}) %collective-permute-start.15) | collective-permute-done | bytes 65568 | tf_op jit(solution)/shard_map/ppermute | solution.py:503
  57.3 2.3 %forward_middle.3 = (bf16[128,1024]{1,0:T(8,128)(2,1)S(1)}, f32[128,128]{1,0:T(8,128)S(1)}, bf16[128,128]{1,0:T(8,128)(2,1)S(1)}, f32[128,128]{1,0:T(8,128)S(1)}...) custom-call(bf16[256,128]{1,0:T(8,128)(2,1)S(1)} %get-tuple-element.86.refs_0_, ...), custom_call_target="tpu_custom_call" | custom-call | tf_op jit(solution)/shard_map/forward_middle/pallas_call | solution.py:536
  59.7 1.6 %collective-permute-start.20 = (bf16[256,128]{1,0:T(8,128)(2,1)S(1)}, bf16[256,128]{1,0:T(8,128)(2,1)S(1)}, u32[]{:S(2)}, u32[]{:S(2)}) collective-permute-start(bf16[256,128]{1,0:T(8,128)(2,1)S(1)} %get-tuple-element.90.refs_0_), channel_id=1, source_target_pairs={{0,2},{1,3},{2,0},{3,1},{4,6},{5,7},{6,4},{7,5},{8,10},{9,11},{10,... | collective-permute-start | bytes 196616 | tf_op jit(solution)/shard_map/ppermute | solution.py:503
  61.5 2.3 %collective-permute-done.21.refs_3_ = bf16[256,128]{1,0:T(8,128)(2,1)S(1)} collective-permute-done((bf16[256,128]{1,0:T(8,128)(2,1)S(1)}, bf16[256,128]{1,0:T(8,128)(2,1)S(1)}, u32[]{:S(2)}, u32[]{:S(2)}) %collective-permute-start.21) | collective-permute-done | bytes 65568 | tf_op jit(solution)/shard_map/ppermute | solution.py:503
  63.9 1.6 %collective-permute-done.20.refs_2_ = bf16[256,128]{1,0:T(8,128)(2,1)S(1)} collective-permute-done((bf16[256,128]{1,0:T(8,128)(2,1)S(1)}, bf16[256,128]{1,0:T(8,128)(2,1)S(1)}, u32[]{:S(2)}, u32[]{:S(2)}) %collective-permute-start.20) | collective-permute-done | bytes 65568 | tf_op jit(solution)/shard_map/ppermute | solution.py:503
  65.5 3.3 %turn.1 = (bf16[128,1024]{1,0:T(8,128)(2,1)S(1)}, f32[128,128]{1,0:T(8,128)S(1)}, bf16[128,128]{1,0:T(8,128)(2,1)S(1)}, f32[128,128]{1,0:T(8,128)S(1)}, bf16[2,2...) custom-call(bf16[256,128]{1,0:T(8,128)(2,1)S(1)} %get-tuple-element., ...), custom_call_target="tpu_custom_call" | custom-call | tf_op jit(solution)/shard_map/turn/pallas_call | solution.py:536
  68.8 1.5 %collective-permute-start.23 = (bf16[144,128]{1,0:T(8,128)(2,1)S(1)}, bf16[144,128]{1,0:T(8,128)(2,1)S(1)}, u32[]{:S(2)}, u32[]{:S(2)}) collective-permute-start(bf16[144,128]{1,0:T(8,128)(2,1)S(1)} %get-tuple-element.93.refs_0_), channel_id=1, source_target_pairs={{0,2},{1,3},{2,0},{3,1},{4,6},{5,7},{6,4},{7,5},{8,10},{9,11},{10,... | collective-permute-start | bytes 110600 | tf_op jit(solution)/shard_map/ppermute | solution.py:503
  73.4 1.7 %backward.3 = (bf16[272,512]{1,0:T(8,128)(2,1)S(1)}, bf16[272,512]{1,0:T(8,128)(2,1)S(1)}, bf16[128,1024]{1,0:T(8,128)(2,1)S(1)}, bf16[144,128]{1,0:T(8,128)(2,1)S(1)}) custom-call(bf16[144,128]{1,0:T(8,128)(2,1)S(1)} %get-tuple-element.93.refs_0_, bf16[144,128]{1,0:T(8,128)(2,1)S(1)} %collective-permute-done.22.refs_1_, ...), custom_call_target="tpu_custom_call" | custom-call | tf_op jit(solution)/shard_map/backward/pallas_call | solution.py:536
  78.1 2.8 %collective-permute-done.29.refs_18_ = bf16[128,128]{1,0:T(8,128)(2,1)S(1)} collective-permute-done((bf16[128,128]{1,0:T(8,128)(2,1)S(1)}, bf16[128,128]{1,0:T(8,128)(2,1)S(1)}, u32[]{:S(2)}, u32[]{:S(2)}) %collective-permute-start.29) | collective-permute-done | bytes 32800 | tf_op jit(solution)/shard_map/ppermute | solution.py:503
  80.9 1.7 %backward.4 = (bf16[272,512]{1,0:T(8,128)(2,1)S(1)}, bf16[272,512]{1,0:T(8,128)(2,1)S(1)}, bf16[272,512]{1,0:T(8,128)(2,1)S(1)}, bf16[272,512]{1,0:T(8,128)(2,1)...) custom-call(bf16[144,128]{1,0:T(8,128)(2,1)S(1)} %get-tuple-element.101.refs_0_, ...), custom_call_target="tpu_custom_call" | custom-call | tf_op jit(solution)/shard_map/backward/pallas_call | solution.py:536
  84.6 2.2 %collective-permute-start.36 = (bf16[272,512]{1,0:T(8,128)(2,1)S(1)}, bf16[272,512]{1,0:T(8,128)(2,1)S(1)}, u32[]{:S(2)}, u32[]{:S(2)}) collective-permute-start(bf16[272,512]{1,0:T(8,128)(2,1)S(1)} %get-tuple-element.120), channel_id=1, source_target_pairs={{0,4},{4,0},{1,5},{5,1},{2,6},{6,2},{3,7},{7,3},{8,12},{12,8},{9,1... | collective-permute-start | bytes 835592 | tf_op jit(solution)/shard_map/ppermute | solution.py:503
  87.5 2.2 %collective-permute-start.37 = (bf16[272,512]{1,0:T(8,128)(2,1)S(1)}, bf16[272,512]{1,0:T(8,128)(2,1)S(1)}, u32[]{:S(2)}, u32[]{:S(2)}) collective-permute-start(bf16[272,512]{1,0:T(8,128)(2,1)S(1)} %get-tuple-element.122), channel_id=1, source_target_pairs={{0,4},{4,0},{1,5},{5,1},{2,6},{6,2},{3,7},{7,3},{8,12},{12,8},{9,1... | collective-permute-start | bytes 835592 | tf_op jit(solution)/shard_map/ppermute | solution.py:503
  92.0 26.6 %collective-permute-done.36.refs_5_ = bf16[272,512]{1,0:T(8,128)(2,1)S(1)} collective-permute-done((bf16[272,512]{1,0:T(8,128)(2,1)S(1)}, bf16[272,512]{1,0:T(8,128)(2,1)S(1)}, u32[]{:S(2)}, u32[]{:S(2)}) %collective-permute-start.36) | collective-permute-done | bytes 278560 | tf_op jit(solution)/shard_map/ppermute | solution.py:503
  118.6 6.0 %collective-permute-done.35.refs_3_ = bf16[272,512]{1,0:T(8,128)(2,1)S(1)} collective-permute-done((bf16[272,512]{1,0:T(8,128)(2,1)S(1)}, bf16[272,512]{1,0:T(8,128)(2,1)S(1)}, u32[]{:S(2)}, u32[]{:S(2)}) %collective-permute-start.35) | collective-permute-done | bytes 278560 | tf_op jit(solution)/shard_map/ppermute | solution.py:503
  124.6 6.0 %collective-permute-done.37.refs_7_ = bf16[272,512]{1,0:T(8,128)(2,1)S(1)} collective-permute-done((bf16[272,512]{1,0:T(8,128)(2,1)S(1)}, bf16[272,512]{1,0:T(8,128)(2,1)S(1)}, u32[]{:S(2)}, u32[]{:S(2)}) %collective-permute-start.37) | collective-permute-done | bytes 278560 | tf_op jit(solution)/shard_map/ppermute | solution.py:503
  130.5 5.3 %collective-permute-done.34.refs_1_ = bf16[272,512]{1,0:T(8,128)(2,1)S(1)} collective-permute-done((bf16[272,512]{1,0:T(8,128)(2,1)S(1)}, bf16[272,512]{1,0:T(8,128)(2,1)S(1)}, u32[]{:S(2)}, u32[]{:S(2)}) %collective-permute-start.34) | collective-permute-done | bytes 278560 | tf_op jit(solution)/shard_map/ppermute | solution.py:503
  138.0 2.0 %collective-permute-start.40 = (bf16[272,512]{1,0:T(8,128)(2,1)S(1)}, bf16[272,512]{1,0:T(8,128)(2,1)S(1)}, u32[]{:S(2)}, u32[]{:S(2)}) collective-permute-start(bf16[272,512]{1,0:T(8,128)(2,1)S(1)} %get-tuple-element.126), channel_id=1, source_target_pairs={{0,24},{8,16},{16,8},{24,0},{1,25},{9,17},{17,9},{25,1},{2,26},{10... | collective-permute-start | bytes 835592 | tf_op jit(solution)/shard_map/ppermute | solution.py:503
  140.0 6.1 %collective-permute-done.38.refs_1_ = bf16[272,512]{1,0:T(8,128)(2,1)S(1)} collective-permute-done((bf16[272,512]{1,0:T(8,128)(2,1)S(1)}, bf16[272,512]{1,0:T(8,128)(2,1)S(1)}, u32[]{:S(2)}, u32[]{:S(2)}) %collective-permute-start.38) | collective-permute-done | bytes 278560 | tf_op jit(solution)/shard_map/ppermute | solution.py:503
  146.9 4.4 %collective-permute-done.40.refs_3_ = bf16[272,512]{1,0:T(8,128)(2,1)S(1)} collective-permute-done((bf16[272,512]{1,0:T(8,128)(2,1)S(1)}, bf16[272,512]{1,0:T(8,128)(2,1)S(1)}, u32[]{:S(2)}, u32[]{:S(2)}) %collective-permute-start.40) | collective-permute-done | bytes 278560 | tf_op jit(solution)/shard_map/ppermute | solution.py:503
  (65 shorter events, 29.2 us)
Async XLA Ops:
  2.9 8.7 %collective-permute-start = (bf16[32,2176]{1,0:T(8,128)(2,1)}, bf16[32,2176]{1,0:T(8,128)(2,1)S(1)}, u32[]{:S(2)}, u32[]{:S(2)}) collective-permute-start(bf16[32,2176]{1,0:T(8,128)(2,1)} %get-tuple-element.66), channel_id=1, source_target_pairs={{0,1},{1,0},{2,3},{3,2},{4,5},{5,4},{6,7},{7,6},{8,9},{9,8},{10,11... | collective-permute-start | bytes 417800 | tf_op jit(solution)/shard_map/ppermute | solution.py:503
  3.5 10.0 %collective-permute-start.1 = (bf16[32,2176]{1,0:T(8,128)(2,1)}, bf16[32,2176]{1,0:T(8,128)(2,1)S(1)}, u32[]{:S(2)}, u32[]{:S(2)}) collective-permute-start(bf16[32,2176]{1,0:T(8,128)(2,1)} %get-tuple-element.67), channel_id=1, source_target_pairs={{0,2},{1,3},{2,0},{3,1},{4,6},{5,7},{6,4},{7,5},{8,10},{9,11},{10,... | collective-permute-start | bytes 417800 | tf_op jit(solution)/shard_map/ppermute | solution.py:503
  6.1 16.1 %collective-permute-start.6 = (bf16[1040,128]{1,0:T(8,128)(2,1)}, bf16[1040,128]{1,0:T(8,128)(2,1)S(1)}, u32[]{:S(2)}, u32[]{:S(2)}) collective-permute-start(bf16[1040,128]{1,0:T(8,128)(2,1)} %get-tuple-element.74.refs_4_), channel_id=1, source_target_pairs={{0,4},{4,0},{1,5},{5,1},{2,6},{6,2},{3,7},{7,3},{8,12},{12,8},{9,1... | collective-permute-start | bytes 798728 | tf_op jit(solution)/shard_map/ppermute | solution.py:503
  8.7 13.6 %collective-permute-start.5 = (bf16[1040,128]{1,0:T(8,128)(2,1)}, bf16[1040,128]{1,0:T(8,128)(2,1)S(1)}, u32[]{:S(2)}, u32[]{:S(2)}) collective-permute-start(bf16[1040,128]{1,0:T(8,128)(2,1)} %get-tuple-element.74.refs_4_), channel_id=1, source_target_pairs={{0,24},{8,16},{16,8},{24,0},{1,25},{9,17},{17,9},{25,1},{2,26},{10... | collective-permute-start | bytes 798728 | tf_op jit(solution)/shard_map/ppermute | solution.py:503
  11.1 12.6 %collective-permute-start.4 = (bf16[1040,128]{1,0:T(8,128)(2,1)}, bf16[1040,128]{1,0:T(8,128)(2,1)S(1)}, u32[]{:S(2)}, u32[]{:S(2)}) collective-permute-start(bf16[1040,128]{1,0:T(8,128)(2,1)} %get-tuple-element.74.refs_4_), channel_id=1, source_target_pairs={{0,16},{8,24},{16,0},{24,8},{1,17},{9,25},{17,1},{25,9},{2,18},{10... | collective-permute-start | bytes 798728 | tf_op jit(solution)/shard_map/ppermute | solution.py:503
  11.7 12.1 %collective-permute-start.3 = (bf16[1040,128]{1,0:T(8,128)(2,1)}, bf16[1040,128]{1,0:T(8,128)(2,1)S(1)}, u32[]{:S(2)}, u32[]{:S(2)}) collective-permute-start(bf16[1040,128]{1,0:T(8,128)(2,1)} %get-tuple-element.74.refs_4_), channel_id=1, source_target_pairs={{0,8},{8,0},{16,24},{24,16},{1,9},{9,1},{17,25},{25,17},{2,10},{10... | collective-permute-start | bytes 798728 | tf_op jit(solution)/shard_map/ppermute | solution.py:503
  13.5 8.8 %collective-permute-start.2 = (bf16[32,2176]{1,0:T(8,128)(2,1)}, bf16[32,2176]{1,0:T(8,128)(2,1)S(1)}, u32[]{:S(2)}, u32[]{:S(2)}) collective-permute-start(bf16[32,2176]{1,0:T(8,128)(2,1)} %get-tuple-element.68), channel_id=1, source_target_pairs={{0,3},{1,2},{2,1},{3,0},{4,7},{5,6},{6,5},{7,4},{8,11},{9,10},{10,... | collective-permute-start | bytes 417800 | tf_op jit(solution)/shard_map/ppermute | solution.py:503
  23.8 10.2 %collective-permute-start.9 = (bf16[1040,128]{1,0:T(8,128)(2,1)S(1)}, bf16[1040,128]{1,0:T(8,128)(2,1)S(1)}, u32[]{:S(2)}, u32[]{:S(2)}) collective-permute-start(bf16[1040,128]{1,0:T(8,128)(2,1)S(1)} %collective-permute-done.6.refs_4_), channel_id=1, source_target_pairs={{0,24},{8,16},{16,8},{24,0},{1,25},{9,17},{17,9},{25,1},{2,26},{10... | collective-permute-start | bytes 798728 | tf_op jit(solution)/shard_map/ppermute | solution.py:503
  25.4 13.2 %collective-permute-start.8 = (bf16[1040,128]{1,0:T(8,128)(2,1)S(1)}, bf16[1040,128]{1,0:T(8,128)(2,1)S(1)}, u32[]{:S(2)}, u32[]{:S(2)}) collective-permute-start(bf16[1040,128]{1,0:T(8,128)(2,1)S(1)} %collective-permute-done.6.refs_4_), channel_id=1, source_target_pairs={{0,16},{8,24},{16,0},{24,8},{1,17},{9,25},{17,1},{25,9},{2,18},{10... | collective-permute-start | bytes 798728 | tf_op jit(solution)/shard_map/ppermute | solution.py:503
  26.8 12.0 %collective-permute-start.7 = (bf16[1040,128]{1,0:T(8,128)(2,1)S(1)}, bf16[1040,128]{1,0:T(8,128)(2,1)S(1)}, u32[]{:S(2)}, u32[]{:S(2)}) collective-permute-start(bf16[1040,128]{1,0:T(8,128)(2,1)S(1)} %collective-permute-done.6.refs_4_), channel_id=1, source_target_pairs={{0,8},{8,0},{16,24},{24,16},{1,9},{9,1},{17,25},{25,17},{2,10},{10... | collective-permute-start | bytes 798728 | tf_op jit(solution)/shard_map/ppermute | solution.py:503
  41.7 5.1 %collective-permute-start.12 = (bf16[384,128]{1,0:T(8,128)(2,1)S(1)}, bf16[384,128]{1,0:T(8,128)(2,1)S(1)}, u32[]{:S(2)}, u32[]{:S(2)}) collective-permute-start(bf16[384,128]{1,0:T(8,128)(2,1)S(1)} %get-tuple-element.84.refs_0_), channel_id=1, source_target_pairs={{0,3},{1,2},{2,1},{3,0},{4,7},{5,6},{6,5},{7,4},{8,11},{9,10},{10,... | collective-permute-start | bytes 294920 | tf_op jit(solution)/shard_map/ppermute | solution.py:503
  41.8 7.3 %collective-permute-start.11 = (bf16[384,128]{1,0:T(8,128)(2,1)S(1)}, bf16[384,128]{1,0:T(8,128)(2,1)S(1)}, u32[]{:S(2)}, u32[]{:S(2)}) collective-permute-start(bf16[384,128]{1,0:T(8,128)(2,1)S(1)} %get-tuple-element.84.refs_0_), channel_id=1, source_target_pairs={{0,2},{1,3},{2,0},{3,1},{4,6},{5,7},{6,4},{7,5},{8,10},{9,11},{10,... | collective-permute-start | bytes 294920 | tf_op jit(solution)/shard_map/ppermute | solution.py:503
  43.3 5.8 %collective-permute-start.10 = (bf16[384,128]{1,0:T(8,128)(2,1)S(1)}, bf16[384,128]{1,0:T(8,128)(2,1)S(1)}, u32[]{:S(2)}, u32[]{:S(2)}) collective-permute-start(bf16[384,128]{1,0:T(8,128)(2,1)S(1)} %get-tuple-element.84.refs_0_), channel_id=1, source_target_pairs={{0,1},{1,0},{2,3},{3,2},{4,5},{5,4},{6,7},{7,6},{8,9},{9,8},{10,11... | collective-permute-start | bytes 294920 | tf_op jit(solution)/shard_map/ppermute | solution.py:503
  43.6 9.4 %collective-permute-start.18 = (bf16[384,128]{1,0:T(8,128)(2,1)S(1)}, bf16[384,128]{1,0:T(8,128)(2,1)S(1)}, u32[]{:S(2)}, u32[]{:S(2)}) collective-permute-start(bf16[384,128]{1,0:T(8,128)(2,1)S(1)} %get-tuple-element.87.refs_4_), channel_id=1, source_target_pairs={{0,3},{1,2},{2,1},{3,0},{4,7},{5,6},{6,5},{7,4},{8,11},{9,10},{10,... | collective-permute-start | bytes 294920 | tf_op jit(solution)/shard_map/ppermute | solution.py:503
  44.0 9.4 %collective-permute-start.17 = (bf16[384,128]{1,0:T(8,128)(2,1)S(1)}, bf16[384,128]{1,0:T(8,128)(2,1)S(1)}, u32[]{:S(2)}, u32[]{:S(2)}) collective-permute-start(bf16[384,128]{1,0:T(8,128)(2,1)S(1)} %get-tuple-element.87.refs_4_), channel_id=1, source_target_pairs={{0,2},{1,3},{2,0},{3,1},{4,6},{5,7},{6,4},{7,5},{8,10},{9,11},{10,... | collective-permute-start | bytes 294920 | tf_op jit(solution)/shard_map/ppermute | solution.py:503
  46.8 6.6 %collective-permute-start.16 = (bf16[384,128]{1,0:T(8,128)(2,1)S(1)}, bf16[384,128]{1,0:T(8,128)(2,1)S(1)}, u32[]{:S(2)}, u32[]{:S(2)}) collective-permute-start(bf16[384,128]{1,0:T(8,128)(2,1)S(1)} %get-tuple-element.87.refs_4_), channel_id=1, source_target_pairs={{0,1},{1,0},{2,3},{3,2},{4,5},{5,4},{6,7},{7,6},{8,9},{9,8},{10,11... | collective-permute-start | bytes 294920 | tf_op jit(solution)/shard_map/ppermute | solution.py:503
  51.5 5.8 %collective-permute-start.14 = (bf16[256,128]{1,0:T(8,128)(2,1)S(1)}, bf16[256,128]{1,0:T(8,128)(2,1)S(1)}, u32[]{:S(2)}, u32[]{:S(2)}) collective-permute-start(bf16[256,128]{1,0:T(8,128)(2,1)S(1)} %get-tuple-element.86.refs_0_), channel_id=1, source_target_pairs={{0,2},{1,3},{2,0},{3,1},{4,6},{5,7},{6,4},{7,5},{8,10},{9,11},{10,... | collective-permute-start | bytes 196616 | tf_op jit(solution)/shard_map/ppermute | solution.py:503
  59.7 5.8 %collective-permute-start.20 = (bf16[256,128]{1,0:T(8,128)(2,1)S(1)}, bf16[256,128]{1,0:T(8,128)(2,1)S(1)}, u32[]{:S(2)}, u32[]{:S(2)}) collective-permute-start(bf16[256,128]{1,0:T(8,128)(2,1)S(1)} %get-tuple-element.90.refs_0_), channel_id=1, source_target_pairs={{0,2},{1,3},{2,0},{3,1},{4,6},{5,7},{6,4},{7,5},{8,10},{9,11},{10,... | collective-permute-start | bytes 196616 | tf_op jit(solution)/shard_map/ppermute | solution.py:503
  68.8 4.6 %collective-permute-start.23 = (bf16[144,128]{1,0:T(8,128)(2,1)S(1)}, bf16[144,128]{1,0:T(8,128)(2,1)S(1)}, u32[]{:S(2)}, u32[]{:S(2)}) collective-permute-start(bf16[144,128]{1,0:T(8,128)(2,1)S(1)} %get-tuple-element.93.refs_0_), channel_id=1, source_target_pairs={{0,2},{1,3},{2,0},{3,1},{4,6},{5,7},{6,4},{7,5},{8,10},{9,11},{10,... | collective-permute-start | bytes 110600 | tf_op jit(solution)/shard_map/ppermute | solution.py:503
  70.7 7.4 %collective-permute-start.30 = (bf16[128,128]{1,0:T(8,128)(2,1)S(1)}, bf16[128,128]{1,0:T(8,128)(2,1)S(1)}, u32[]{:S(2)}, u32[]{:S(2)}) collective-permute-start(bf16[128,128]{1,0:T(8,128)(2,1)S(1)} %get-tuple-element.107.refs_16_), channel_id=1, source_target_pairs={{0,3},{1,2},{2,1},{3,0},{4,7},{5,6},{6,5},{7,4},{8,11},{9,10},{10,... | collective-permute-start | bytes 98312 | tf_op jit(solution)/shard_map/ppermute | solution.py:503
  75.1 5.8 %collective-permute-start.27 = (bf16[144,128]{1,0:T(8,128)(2,1)S(1)}, bf16[144,128]{1,0:T(8,128)(2,1)S(1)}, u32[]{:S(2)}, u32[]{:S(2)}) collective-permute-start(bf16[144,128]{1,0:T(8,128)(2,1)S(1)} %get-tuple-element.101.refs_0_), channel_id=1, source_target_pairs={{0,3},{1,2},{2,1},{3,0},{4,7},{5,6},{6,5},{7,4},{8,11},{9,10},{10,... | collective-permute-start | bytes 110600 | tf_op jit(solution)/shard_map/ppermute | solution.py:503
  75.5 5.4 %collective-permute-start.26 = (bf16[144,128]{1,0:T(8,128)(2,1)S(1)}, bf16[144,128]{1,0:T(8,128)(2,1)S(1)}, u32[]{:S(2)}, u32[]{:S(2)}) collective-permute-start(bf16[144,128]{1,0:T(8,128)(2,1)S(1)} %get-tuple-element.101.refs_0_), channel_id=1, source_target_pairs={{0,2},{1,3},{2,0},{3,1},{4,6},{5,7},{6,4},{7,5},{8,10},{9,11},{10,... | collective-permute-start | bytes 110600 | tf_op jit(solution)/shard_map/ppermute | solution.py:503
  82.7 4.9 %collective-permute-start.33 = (bf16[144,128]{1,0:T(8,128)(2,1)S(1)}, bf16[144,128]{1,0:T(8,128)(2,1)S(1)}, u32[]{:S(2)}, u32[]{:S(2)}) collective-permute-start(bf16[144,128]{1,0:T(8,128)(2,1)S(1)} %get-tuple-element.109.refs_0_), channel_id=1, source_target_pairs={{0,3},{1,2},{2,1},{3,0},{4,7},{5,6},{6,5},{7,4},{8,11},{9,10},{10,... | collective-permute-start | bytes 110600 | tf_op jit(solution)/shard_map/ppermute | solution.py:503
  82.7 7.0 %collective-permute-start.32 = (bf16[144,128]{1,0:T(8,128)(2,1)S(1)}, bf16[144,128]{1,0:T(8,128)(2,1)S(1)}, u32[]{:S(2)}, u32[]{:S(2)}) collective-permute-start(bf16[144,128]{1,0:T(8,128)(2,1)S(1)} %get-tuple-element.109.refs_0_), channel_id=1, source_target_pairs={{0,2},{1,3},{2,0},{3,1},{4,6},{5,7},{6,4},{7,5},{8,10},{9,11},{10,... | collective-permute-start | bytes 110600 | tf_op jit(solution)/shard_map/ppermute | solution.py:503
  84.0 5.8 %collective-permute-start.31 = (bf16[144,128]{1,0:T(8,128)(2,1)S(1)}, bf16[144,128]{1,0:T(8,128)(2,1)S(1)}, u32[]{:S(2)}, u32[]{:S(2)}) collective-permute-start(bf16[144,128]{1,0:T(8,128)(2,1)S(1)} %get-tuple-element.109.refs_0_), channel_id=1, source_target_pairs={{0,1},{1,0},{2,3},{3,2},{4,5},{5,4},{6,7},{7,6},{8,9},{9,8},{10,11... | collective-permute-start | bytes 110600 | tf_op jit(solution)/shard_map/ppermute | solution.py:503
  84.6 34.0 %collective-permute-start.36 = (bf16[272,512]{1,0:T(8,128)(2,1)S(1)}, bf16[272,512]{1,0:T(8,128)(2,1)S(1)}, u32[]{:S(2)}, u32[]{:S(2)}) collective-permute-start(bf16[272,512]{1,0:T(8,128)(2,1)S(1)} %get-tuple-element.120), channel_id=1, source_target_pairs={{0,4},{4,0},{1,5},{5,1},{2,6},{6,2},{3,7},{7,3},{8,12},{12,8},{9,1... | collective-permute-start | bytes 835592 | tf_op jit(solution)/shard_map/ppermute | solution.py:503
  86.8 37.8 %collective-permute-start.35 = (bf16[272,512]{1,0:T(8,128)(2,1)S(1)}, bf16[272,512]{1,0:T(8,128)(2,1)S(1)}, u32[]{:S(2)}, u32[]{:S(2)}) collective-permute-start(bf16[272,512]{1,0:T(8,128)(2,1)S(1)} %get-tuple-element.118), channel_id=1, source_target_pairs={{0,4},{4,0},{1,5},{5,1},{2,6},{6,2},{3,7},{7,3},{8,12},{12,8},{9,1... | collective-permute-start | bytes 835592 | tf_op jit(solution)/shard_map/ppermute | solution.py:503
  87.5 43.0 %collective-permute-start.37 = (bf16[272,512]{1,0:T(8,128)(2,1)S(1)}, bf16[272,512]{1,0:T(8,128)(2,1)S(1)}, u32[]{:S(2)}, u32[]{:S(2)}) collective-permute-start(bf16[272,512]{1,0:T(8,128)(2,1)S(1)} %get-tuple-element.122), channel_id=1, source_target_pairs={{0,4},{4,0},{1,5},{5,1},{2,6},{6,2},{3,7},{7,3},{8,12},{12,8},{9,1... | collective-permute-start | bytes 835592 | tf_op jit(solution)/shard_map/ppermute | solution.py:503
  91.2 44.7 %collective-permute-start.34 = (bf16[272,512]{1,0:T(8,128)(2,1)S(1)}, bf16[272,512]{1,0:T(8,128)(2,1)S(1)}, u32[]{:S(2)}, u32[]{:S(2)}) collective-permute-start(bf16[272,512]{1,0:T(8,128)(2,1)S(1)} %get-tuple-element.116), channel_id=1, source_target_pairs={{0,4},{4,0},{1,5},{5,1},{2,6},{6,2},{3,7},{7,3},{8,12},{12,8},{9,1... | collective-permute-start | bytes 835592 | tf_op jit(solution)/shard_map/ppermute | solution.py:503
  136.4 9.7 %collective-permute-start.38 = (bf16[272,512]{1,0:T(8,128)(2,1)S(1)}, bf16[272,512]{1,0:T(8,128)(2,1)S(1)}, u32[]{:S(2)}, u32[]{:S(2)}) collective-permute-start(bf16[272,512]{1,0:T(8,128)(2,1)S(1)} %get-tuple-element.124), channel_id=1, source_target_pairs={{0,8},{8,0},{16,24},{24,16},{1,9},{9,1},{17,25},{25,17},{2,10},{10... | collective-permute-start | bytes 835592 | tf_op jit(solution)/shard_map/ppermute | solution.py:503
  137.8 9.2 %collective-permute-start.39 = (bf16[272,512]{1,0:T(8,128)(2,1)S(1)}, bf16[272,512]{1,0:T(8,128)(2,1)S(1)}, u32[]{:S(2)}, u32[]{:S(2)}) collective-permute-start(bf16[272,512]{1,0:T(8,128)(2,1)S(1)} %get-tuple-element.125), channel_id=1, source_target_pairs={{0,16},{8,24},{16,0},{24,8},{1,17},{9,25},{17,1},{25,9},{2,18},{10... | collective-permute-start | bytes 835592 | tf_op jit(solution)/shard_map/ppermute | solution.py:503
  138.0 13.3 %collective-permute-start.40 = (bf16[272,512]{1,0:T(8,128)(2,1)S(1)}, bf16[272,512]{1,0:T(8,128)(2,1)S(1)}, u32[]{:S(2)}, u32[]{:S(2)}) collective-permute-start(bf16[272,512]{1,0:T(8,128)(2,1)S(1)} %get-tuple-element.126), channel_id=1, source_target_pairs={{0,24},{8,16},{16,8},{24,0},{1,25},{9,17},{17,9},{25,1},{2,26},{10... | collective-permute-start | bytes 835592 | tf_op jit(solution)/shard_map/ppermute | solution.py:503
  (11 other events, 36.5 us)

commit v7 on v5

--- a/solution.py
+++ b/solution.py
@@ -9,6 +9,7 @@
 
 HD = 128
 EPS = 1e-05
+FOLDED = HD + 16
 BF = jnp.bfloat16
 F32 = jnp.float32
 PARAMS = pltpu.CompilerParams(vmem_limit_bytes=48 * 1024 * 1024)
@@ -44,22 +45,52 @@
     return 2 * own + 16
 
 
-def pack_kernel(groups, micro_local, *refs):
-    tokens, cotangents, starts, counts, gain, first, second = refs[:7]
-    parts, weights = refs[7 : 7 + groups], refs[7 + groups]
-    tok, cot, starts_in, counts_in, gain_in, second_in, sems = refs[8 + groups :]
+def pack_weights_kernel(gain, first, second, weights, gain_in, second_in, sems):
+    own = first.shape[1]
+    copies = [
+        pltpu.make_async_copy(second.at[0], second_in, sems.at[0]),
+        pltpu.make_async_copy(gain, gain_in, sems.at[1]),
+        pltpu.make_async_copy(first.at[0], weights.at[pl.ds(0, own)], sems.at[2]),
+    ]
+    for copy in copies:
+        copy.start()
+    for copy in copies:
+        copy.wait()
+    weights[own : 2 * own, :] = second_in[...].astype(F32).T.astype(BF)
+    gains = [gain_in[0:1, head * HD : (head + 1) * HD].astype(F32) for head in range(own // HD)]
+    gains.append(jnp.zeros((16 - own // HD, HD), F32))
+    weights[2 * own :, :] = jnp.concatenate(gains, axis=0).astype(BF)
+
+
+def pack_weights(gain, first, second):
+    own = first.shape[1]
+    return pl.pallas_call(
+        pack_weights_kernel,
+        in_specs=[pl.BlockSpec(memory_space=pltpu.HBM)] * 3,
+        out_specs=pl.BlockSpec(memory_space=pltpu.VMEM),
+        out_shape=jax.ShapeDtypeStruct((slice_rows(own), HD), BF),
+        scratch_shapes=[
+            pltpu.VMEM(gain.shape, BF),
+            pltpu.VMEM(second.shape[1:], BF),
+            pltpu.SemaphoreType.DMA((3,)),
+        ],
+        compiler_params=PACK_PARAMS,
+        name="pack_weights",
+    )(gain, first, second)
+
+
+def pack_tokens_kernel(groups, micro_local, *refs):
+    tokens, cotangents, starts, counts = refs[:4]
+    parts = refs[4 : 4 + groups]
+    tok, cot, starts_in, counts_in, sems = refs[4 + groups :]
     directions, micro_count, length, width = tokens.shape
     local = width // groups
-    own = first.shape[1]
     section = lax.axis_index("pipe")
     group = lax.axis_index("z")
     picks = []
     copies = [
-        pltpu.make_async_copy(second.at[0], second_in, sems.at[0]),
-        pltpu.make_async_copy(gain, gain_in, sems.at[1]),
-        pltpu.make_async_copy(first.at[0], weights.at[pl.ds(0, own)], sems.at[2]),
-        pltpu.make_async_copy(starts, starts_in, sems.at[3]),
-        pltpu.make_async_copy(counts, counts_in, sems.at[4]),
+        pltpu.make_async_copy(starts, starts_in, sems.at[0]),
+        pltpu.make_async_copy(counts, counts_in, sems.at[1]),
     ]
     for micro in range(micro_local):
         wanted = section * micro_local + micro
@@ -69,22 +100,18 @@
         rows = pl.ds(micro * length, length)
         copies.append(
             pltpu.make_async_copy(
-                tokens.at[direction, place], tok.at[rows], sems.at[5 + 2 * micro]
+                tokens.at[direction, place], tok.at[rows], sems.at[2 + 2 * micro]
             )
         )
         copies.append(
             pltpu.make_async_copy(
-                cotangents.at[direction, place], cot.at[rows], sems.at[6 + 2 * micro]
+                cotangents.at[direction, place], cot.at[rows], sems.at[3 + 2 * micro]
             )
         )
     for copy in copies:
         copy.start()
     for copy in copies:
         copy.wait()
-    weights[own : 2 * own, :] = second_in[...].astype(F32).T.astype(BF)
-    gains = [gain_in[0:1, head * HD : (head + 1) * HD].astype(F32) for head in range(own // HD)]
-    gains.append(jnp.zeros((16 - own // HD, HD), F32))
-    weights[2 * own :, :] = jnp.concatenate(gains, axis=0).astype(BF)
     for micro, (keep, direction, place) in enumerate(picks):
         rows = slice(micro * length, (micro + 1) * length)
         widened = tok[rows, :].astype(F32)
@@ -112,31 +139,25 @@
             parts[shift][rows, 2 * local :] = tail
 
 
-def pack(tokens, cotangents, starts, counts, gain, first, second, groups, micro_local):
+def pack_tokens(tokens, cotangents, starts, counts, groups, micro_local):
     length, width = tokens.shape[2:]
-    own = first.shape[1]
     local = width // groups
     rows = micro_local * length
-    shape = jax.ShapeDtypeStruct
-    results = pl.pallas_call(
-        functools.partial(pack_kernel, groups, micro_local),
-        in_specs=[pl.BlockSpec(memory_space=pltpu.HBM)] * 7,
-        out_specs=vmem_specs(groups + 1),
-        out_shape=[shape((rows, 2 * local + HD), BF)] * groups
-        + [shape((slice_rows(own), HD), BF)],
+    return pl.pallas_call(
+        functools.partial(pack_tokens_kernel, groups, micro_local),
+        in_specs=[pl.BlockSpec(memory_space=pltpu.HBM)] * 4,
+        out_specs=vmem_specs(groups),
+        out_shape=[jax.ShapeDtypeStruct((rows, 2 * local + HD), BF)] * groups,
         scratch_shapes=[
             pltpu.VMEM((rows, width), BF),
             pltpu.VMEM((rows, width), BF),
             pltpu.SMEM(starts.shape, jnp.int32),
             pltpu.SMEM(counts.shape, jnp.int32),
-            pltpu.VMEM(gain.shape, BF),
-            pltpu.VMEM(second.shape[1:], BF),
-            pltpu.SemaphoreType.DMA((5 + 2 * micro_local,)),
+            pltpu.SemaphoreType.DMA((2 + 2 * micro_local,)),
         ],
         compiler_params=PACK_PARAMS,
-        name="pack",
-    )(tokens, cotangents, starts, counts, gain, first, second)
-    return results[:groups], results[groups]
+        name="pack_tokens",
+    )(tokens, cotangents, starts, counts)
 
 
 def head_gain(weights, head):
@@ -251,22 +272,30 @@
         for parts, place in ((mine, core), (theirs, 1 - core)):
             copies.append(
                 pltpu.make_async_copy(
-                    parts[distance], weights.at[layer, place], sems.at[distance, place]
+                    parts[distance], weights.at[layer, place], sems.at[layer, place]
                 )
             )
     for copy in copies:
         copy.start()
-    for copy in copies:
-        copy.wait()
+
+    def arrived(layer):
+        for place in range(weights.shape[1]):
+            pltpu.make_async_copy(mine[0], weights.at[layer, place], sems.at[layer, place]).wait()
+
+    arrived(0)
     own = (weights.shape[2] - 16) // 2
     layers = [weights.at[pl.ds(layer, 1)] for layer in range(sections)]
     attend(x, mean[:, 0:1], layers[0], mask, probs, mixed)
     send_forward(x, layers[0], mixed, pay)
-    pay[2 * rows :, :] = gram(layers[0]).astype(BF)
+    arrived(1)
+    pay[2 * rows :, :] = fold_grams(layers[0], layers[1])
+    for layer in range(2, sections):
+        arrived(layer)
     side[0:rows, :] = to_rank(cot[...], layers[-1], own).astype(BF)
-    for layer in range(1, sections - 1):
-        base = rows + HD * (layer - 1)
-        side[base : base + HD, :] = gram(layers[layer]).astype(BF)
+    for layer in range(2, sections - 1, 2):
+        base, height, folded = gram_place(layer, sections - 1, rows)
+        both = fold_grams(layers[layer], layers[layer + 1]) if folded else gram(layers[layer])
+        side[base : base + height, :] = both.astype(BF)
 
 
 def place_rows(received, target, columns):
@@ -287,21 +316,49 @@
         mask[block] = allowed.astype(F32).astype(BF)
 
 
-def gram_of(pays, sides, layer, rows):
-    if layer == 0:
-        return total_of(pays, 2 * rows, 2 * rows + HD)
-    base = rows + HD * (layer - 1)
-    return total_of(sides, base, base + HD)
-
-
-def middle_kernel(count, layer, width, *refs):
-    pays, sides, refs = refs[:count], refs[count : 2 * count], refs[2 * count :]
+def fold_grams(weights, other):
+    row, lane = square_places()
+    upper, lower = gram(weights), gram(other)
+    diagonal = jnp.sum(jnp.where(row == lane, lower, 0.0), axis=0, keepdims=True)
+    folded = jnp.where(row <= lane, upper, lower)
+    return jnp.concatenate((folded, diagonal, jnp.zeros((15, HD), F32)), axis=0).astype(BF)
+
+
+def square_places():
+    return (
+        lax.broadcasted_iota(jnp.int32, (HD, HD), 0),
+        lax.broadcasted_iota(jnp.int32, (HD, HD), 1),
+    )
+
+
+def gram_place(layer, top, rows):
+    pair = layer // 2
+    folded = 2 * pair + 1 < top
+    base = 2 * rows if pair == 0 else rows + FOLDED * (pair - 1)
+    return base, FOLDED if folded else HD, folded
+
+
+def gram_of(sources, layer, top, rows):
+    base, height, folded = gram_place(layer, top, rows)
+    total = total_of(sources, base, base + height)
+    if not folded:
+        return total
+    row, lane = square_places()
+    square = total[0:HD]
+    if layer % 2 == 0:
+        return jnp.where(row <= lane, square, square.T)
+    lower = jnp.where(row > lane, square, square.T)
+    return jnp.where(row == lane, total[HD : HD + 1], lower)
+
+
+def middle_kernel(count, layer, top, width, *refs):
+    pays, sources, refs = refs[:count], refs[count : 2 * count], refs[2 * count :]
     if layer == 1:
-        sides, refs = (), sides + refs
+        sources, refs = pays, sources + refs
     x_before, mean_before, mask, weights_before, weights = refs[:5]
     x, mean, reduced, cross, probs, mixed, pay = refs[5:]
     receive_forward(
-        pays, gram_of(pays, sides, layer - 1, x.shape[0]), x_before, mean_before, weights_before,
+        pays, gram_of(sources, layer - 1, top, x.shape[0]), x_before, mean_before, weights_before,
         width, x, mean, reduced, cross,
     )
     attend(x, mean[:, 0:1], weights, mask, probs, mixed)
@@ -374,15 +431,15 @@
 def turn_kernel(count, layer, width, *refs):
     pays, sides, refs = refs[:count], refs[count : 2 * count], refs[2 * count :]
     (x_before, mean_before, mask, weights_before, weights, cot) = refs[:6]
-    (x, mean, reduced, cross, grads, carried, pay, last_part) = refs[6:14]
-    probs, mixed = refs[14:]
+    (x, mean, reduced, cross, grads, carried, pay) = refs[6:13]
+    probs, mixed = refs[13:]
     rows = x.shape[0]
     receive_forward(
-        pays, gram_of(pays, sides, layer - 1, rows), x_before, mean_before, weights_before,
+        pays, gram_of(sides, layer - 1, layer, rows), x_before, mean_before, weights_before,
         width, x, mean, reduced, cross,
     )
     attend(x, mean[:, 0:1], weights, mask, probs, mixed)
-    last_part[...] = to_rank(mixed[...], weights, 0).astype(BF)
+    pay[pay.shape[0] - rows :, :] = to_rank(mixed[...], weights, 0).astype(BF)
     dred = total_of(sides, 0, rows).astype(BF)
     layer_backward(
         cot, dred, x, mean[:, 0:1], mask, weights, weights_before, probs, mixed, None, grads,
@@ -407,8 +464,8 @@
     probs, mixed, reduced = refs[:3]
     refs = refs[3:]
     if with_last:
-        last_parts, cot, turn_grads = refs[:count], refs[count], refs[count + 1]
-        refs = refs[count + 2 :]
+        cot, turn_grads = refs[:2]
+        refs = refs[2:]
     keep, send = refs[:2]
     refs = refs[2:]
     if with_last:
@@ -441,7 +498,7 @@
         ).astype(BF)
     dred = dred_parts[0] if len(dred_parts) == 1 else jnp.concatenate(dred_parts, axis=0)
     if with_last:
-        last_reduced = total_of(last_parts, 0, rows).astype(BF)
+        last_reduced = total_of(pays, pays[0].shape[0] - rows, pays[0].shape[0]).astype(BF)
         second = dot_tn(last_reduced, cot[...]).astype(BF)
         for side in range(weights.shape[1]):
             grads[side, 0:rank, :] = turn_grads[side, 0:rank, :]
@@ -504,12 +561,12 @@
     def exchange(pay):
         return [pay] + [shifted(pay, shift) for shift in range(1, groups)]
 
-    token_parts, packed = pack(
-        tokens, cotangents, starts, counts, layer_gains, first_map, second_map, groups, micro_local
-    )
+    packed = pack_weights(layer_gains, first_map, second_map)
+    mine = [packed] + [across(packed, distance) for distance in range(1, sections)]
+    tokens, packed = lax.optimization_barrier((tokens, packed))
+    token_parts = pack_tokens(tokens, cotangents, starts, counts, groups, micro_local)
     received = [token_parts[0]]
     received += [shifted(token_parts[shift], shift) for shift in range(1, groups)]
-    mine = [packed] + [across(packed, distance) for distance in range(1, sections)]
     received, mine = lax.optimization_barrier((received, mine))
     theirs = [swapped(part) for part in mine]
 
@@ -554,6 +611,8 @@
         "arrange",
         scratch_shapes=[pltpu.VMEM((rows, HD), BF)],
     )
+    last_gram = gram_place(top - 1, top, rows)
+    side_rows = last_gram[0] + last_gram[1]
     probs, mixed, pay, side, weights = call(
         functools.partial(first_kernel, sections),
         (*mine, *theirs, x, cot, mask, mean),
@@ -561,8 +620,8 @@
         [
             probs_shape,
             wide_shape,
-            shaped((2 * rows + HD, HD)),
-            shaped((rows + HD * (top - 1), HD)),
+            shaped((2 * rows + FOLDED, HD)),
+            shaped((side_rows, HD)),
             weights_shape,
         ],
         "forward_first",
@@ -570,13 +629,13 @@
     )
     xs, means, reduceds, crosses = [x], [mean], [], [None]
     all_probs, all_mixed = [probs], [mixed]
-    pays = exchange(pay)
+    first_pays = pays = exchange(pay)
     arrived = exchange(side)
     for layer in range(1, top):
-        operands = (*pays, *(arrived if layer > 1 else ()))
+        operands = (*pays, *((), first_pays, arrived)[min(layer, 3) - 1])
         specs = vmem_specs(len(operands) + 3) + [layer_of(layer - 1), layer_of(layer)]
         x, mean, reduced, cross, probs, mixed, pay = call(
-            functools.partial(middle_kernel, groups, layer, float(width)),
+            functools.partial(middle_kernel, groups, layer, top, float(width)),
             (*operands, xs[-1], means[-1], mask, weights, weights),
             specs,
             [
@@ -599,7 +658,7 @@
         pays = exchange(pay)
 
     back_rows = rows + 16 * blocks
-    x, mean, reduced, cross, turn_grads, carried, pay, last_part = call(
+    x, mean, reduced, cross, turn_grads, carried, pay = call(
         functools.partial(turn_kernel, groups, top, float(width)),
         (*pays, *arrived, xs[-1], means[-1], mask, weights, weights, cot),
         vmem_specs(2 * groups + 3) + [layer_of(top - 1), layer_of(top)] + vmem_specs(1),
@@ -610,8 +669,7 @@
             cross_shape,
             shaped(grads_shape),
             wide_shape,
-            shaped((back_rows, HD)),
-            rank_shape,
+            shaped((back_rows + rows, HD)),
         ],
         "turn",
         scratch_shapes=[
@@ -627,9 +685,7 @@
     kept, taken = [None] * sections, [None] * sections
     for layer in range(top - 1, -1, -1):
         pays = exchange(pay)
-        if layer == top - 1:
-            last_parts = exchange(last_part)
-        with_last = layer == top - 2
+        with_last = layer == top - 1
         to_first = layer == 0
         operands = (
             *pays, carried, xs[layer + 1], means[layer + 1], crosses[layer + 1],
@@ -643,8 +699,8 @@
         specs += vmem_specs(3)
         outs = [half_shape] * 2
         if with_last:
-            operands += (*last_parts, cot, turn_grads)
-            specs += vmem_specs(groups + 2)
+            operands += (cot, turn_grads)
+            specs += vmem_specs(2)
             outs += [half_shape] * 2
         if not to_first:
             outs += [wide_shape, shaped((back_rows, HD))]

time: 118 us -> 116 us (0.983)
  starting transfers between devices: 48.3 us -> 43.7 us
  waiting for transfers between devices: 46.6 us -> 48.9 us
  Pallas kernels: 19.8 us -> 21.9 us
    ppermute x27 -> x24, starting transfers between devices: 39.6 us -> 35.1 us  [shifted(): lax.ppermute(value, 'z', [(i, (i + shift) % groups) for i in range(groups)])]
    ppermute x27 -> x24, waiting for transfers between devices: 30.9 us -> 32.9 us  [shifted(): lax.ppermute(value, 'z', [(i, (i + shift) % groups) for i in range(groups)])]
    pallas_call x1 -> x2, Pallas kernels: 2.3 us -> 3.87 us  [the longest x1 2.05 us: pack_tokens(): pl.pallas_call(functools.partial(pack_tokens_kernel, groups, micro_local)...]
  transfers between devices with their start and end apart: 41 -> 38, of which waited for: 17 -> 20; matrix products, arithmetic and copies ran while one was open for 0% -> 0% of each run, Pallas kernels for 5% -> 4%
where the time goes in v7:
time: 116 us
  waiting for transfers between devices  48.9 us (42%)
  starting transfers between devices  43.7 us (38%)
  Pallas kernels  21.9 us (19%)
    ppermute x24, starting transfers between devices, shifted(): lax.ppermute(value, 'z', [(i, (i + shift) % groups) for i in range(groups)])  35.1 us
    ppermute x24, waiting for transfers between devices, shifted(): lax.ppermute(value, 'z', [(i, (i + shift) % groups) for i in range(groups)])  32.9 us
    pallas_call x10, Pallas kernels, call(): pl.pallas_call(kernel, grid=(1,), in_specs=specs, out_specs=vmem_specs(le...  18 us
    ppermute x6, waiting for transfers between devices, across(): lax.ppermute(value, 'pipe', [(i, i ^ distance) for i in range(sections)])  14.1 us
    ppermute x6, starting transfers between devices, across(): lax.ppermute(value, 'pipe', [(i, i ^ distance) for i in range(sections)])  7.04 us
  transfers between devices with their start and end apart: 38, of which 20 were waited for; matrix products, arithmetic and copies ran while one was open for 0% of the time, Pallas kernels for 4%

profile of v7, /device:TPU:0, one launch (start us, length us, event | category | flops | bytes accessed | tf_op | source)
XLA Modules:
  0.0 116.3 jit_solution(15022743711327241174)
XLA Ops:
  0.6 1.8 %pack_weights.1.refs_4_ = bf16[1040,128]{1,0:T(8,128)(2,1)} custom-call(bf16[1,512]{1,0:T(2,128)(2,1)} %gain.1, bf16[1,512,128]{2,1,0:T(8,128)(2,1)} %first.1, bf16[1,128,512]{2,1,0:T(8,128)(2,1)} %second.1), custom_call_target="tpu_custom_call" | custom-call | tf_op jit(solution)/shard_map/pack_weights/pallas_call | solution.py:67
  2.5 2.1 %pack_tokens.1 = (bf16[32,2176]{1,0:T(8,128)(2,1)}, bf16[32,2176]{1,0:T(8,128)(2,1)}, bf16[32,2176]{1,0:T(8,128)(2,1)}, bf16[32,2176]{1,0:T(8,128)(2,1)}) custom-call(bf16[2,2,32,4096]{3,2,1,0:T(8,128)(2,1)} %refs_0_, bf16[2,2,32,4096]{3,2,1,0:T(8,128)(2,1)} %refs_1_.1, s32[2,2,4]{2,1,0:T(2,128)} %refs_2_.1, s32[2,2]{1,0:T(2,128)} %refs_3_.1), custom_call_target="tpu_custom_call" | custom-call | tf_op jit(solution)/shard_map/pack_tokens/pallas_call | solution.py:146
  4.5 3.1 %collective-permute-start = (bf16[32,2176]{1,0:T(8,128)(2,1)}, bf16[32,2176]{1,0:T(8,128)(2,1)S(1)}, u32[]{:S(2)}, u32[]{:S(2)}) collective-permute-start(bf16[32,2176]{1,0:T(8,128)(2,1)} %get-tuple-element.65), channel_id=1, source_target_pairs={{0,2},{2,4},{4,6},{6,0},{1,3},{3,5},{5,7},{7,1},{8,10},{10,12},{12... | collective-permute-start | bytes 417800 | tf_op jit(solution)/shard_map/ppermute | solution.py:553
  7.6 2.4 %collective-permute-start.5 = (bf16[1040,128]{1,0:T(8,128)(2,1)}, bf16[1040,128]{1,0:T(8,128)(2,1)S(1)}, u32[]{:S(2)}, u32[]{:S(2)}) collective-permute-start(bf16[1040,128]{1,0:T(8,128)(2,1)} %pack_weights.1.refs_4_), channel_id=1, source_target_pairs={{0,24},{8,16},{16,8},{24,0},{1,25},{9,17},{17,9},{25,1},{2,26},{10... | collective-permute-start | bytes 798728 | tf_op jit(solution)/shard_map/ppermute | solution.py:556
  11.1 2.6 %collective-permute-start.1 = (bf16[32,2176]{1,0:T(8,128)(2,1)}, bf16[32,2176]{1,0:T(8,128)(2,1)S(1)}, u32[]{:S(2)}, u32[]{:S(2)}) collective-permute-start(bf16[32,2176]{1,0:T(8,128)(2,1)} %get-tuple-element.66), channel_id=1, source_target_pairs={{0,4},{2,6},{4,0},{6,2},{1,5},{3,7},{5,1},{7,3},{8,12},{10,14},{12... | collective-permute-start | bytes 417800 | tf_op jit(solution)/shard_map/ppermute | solution.py:553
  13.7 1.6 %collective-permute-start.2 = (bf16[32,2176]{1,0:T(8,128)(2,1)}, bf16[32,2176]{1,0:T(8,128)(2,1)S(1)}, u32[]{:S(2)}, u32[]{:S(2)}) collective-permute-start(bf16[32,2176]{1,0:T(8,128)(2,1)} %get-tuple-element.67), channel_id=1, source_target_pairs={{0,6},{2,0},{4,2},{6,4},{1,7},{3,1},{5,3},{7,5},{8,14},{10,8},{12,... | collective-permute-start | bytes 417800 | tf_op jit(solution)/shard_map/ppermute | solution.py:553
  15.3 5.4 %collective-permute-done.1.refs_2_ = bf16[32,2176]{1,0:T(8,128)(2,1)S(1)} collective-permute-done((bf16[32,2176]{1,0:T(8,128)(2,1)}, bf16[32,2176]{1,0:T(8,128)(2,1)S(1)}, u32[]{:S(2)}, u32[]{:S(2)}) %collective-permute-start.1) | collective-permute-done | bytes 139296 | tf_op jit(solution)/shard_map/ppermute | solution.py:553
  20.7 1.6 %collective-permute-done.4.refs_2_ = bf16[1040,128]{1,0:T(8,128)(2,1)S(1)} collective-permute-done((bf16[1040,128]{1,0:T(8,128)(2,1)}, bf16[1040,128]{1,0:T(8,128)(2,1)S(1)}, u32[]{:S(2)}, u32[]{:S(2)}) %collective-permute-start.4) | collective-permute-done | bytes 266272 | tf_op jit(solution)/shard_map/ppermute | solution.py:556
  25.1 3.3 %forward_first.1 = (bf16[1,8,128,128]{3,2,1,0:T(8,128)(2,1)S(1)}, bf16[128,1024]{1,0:T(8,128)(2,1)S(1)}, bf16[400,128]{1,0:T(8,128)(2,1)S(1)}, bf16[256,128]{1,0:T(8,128)(2,1)S(1)}, bf16[4,2,1040,128]{3,2,1,0:T(8,128)(2,1)S(1)}) custom-call(bf16[1040,128]{1,0:T(8,128)(2,1)S(1)} %get-tuple-element.73.refs_0_, ...), custom_call_target="tpu_custom_call" | custom-call | tf_op jit(solution)/shard_map/forward_first/pallas_call | solution.py:586
  28.4 2.6 %collective-permute-start.12 = (bf16[400,128]{1,0:T(8,128)(2,1)S(1)}, bf16[400,128]{1,0:T(8,128)(2,1)S(1)}, u32[]{:S(2)}, u32[]{:S(2)}) collective-permute-start(bf16[400,128]{1,0:T(8,128)(2,1)S(1)} %get-tuple-element.81.refs_0_.refs_4_), channel_id=1, source_target_pairs={{0,6},{2,0},{4,2},{6,4},{1,7},{3,1},{5,3},{7,5},{8,14},{10,8},{12,... | collective-permute-start | bytes 307208 | tf_op jit(solution)/shard_map/ppermute | solution.py:553
  31.5 1.6 %collective-permute-start.10 = (bf16[400,128]{1,0:T(8,128)(2,1)S(1)}, bf16[400,128]{1,0:T(8,128)(2,1)S(1)}, u32[]{:S(2)}, u32[]{:S(2)}) collective-permute-start(bf16[400,128]{1,0:T(8,128)(2,1)S(1)} %get-tuple-element.81.refs_0_.refs_4_), channel_id=1, source_target_pairs={{0,2},{2,4},{4,6},{6,0},{1,3},{3,5},{5,7},{7,1},{8,10},{10,12},{12... | collective-permute-start | bytes 307208 | tf_op jit(solution)/shard_map/ppermute | solution.py:553
  34.3 6.7 %collective-permute-done.11.refs_2_.refs_6_ = bf16[400,128]{1,0:T(8,128)(2,1)S(1)} collective-permute-done((bf16[400,128]{1,0:T(8,128)(2,1)S(1)}, bf16[400,128]{1,0:T(8,128)(2,1)S(1)}, u32[]{:S(2)}, u32[]{:S(2)}) %collective-permute-start.11) | collective-permute-done | bytes 102432 | tf_op jit(solution)/shard_map/ppermute | solution.py:553
  41.0 2.4 %forward_middle.2 = (bf16[128,1024]{1,0:T(8,128)(2,1)S(1)}, f32[128,128]{1,0:T(8,128)S(1)}, bf16[128,128]{1,0:T(8,128)(2,1)S(1)}, f32[128,128]{1,0:T(8,128)S(1)}...) custom-call(bf16[400,128]{1,0:T(8,128)(2,1)S(1)} %get-tuple-element.81.refs_0_.re, ...), custom_call_target="tpu_custom_call" | custom-call | tf_op jit(solution)/shard_map/forward_middle/pallas_call | solution.py:586
  46.0 1.9 %collective-permute-start.13 = (bf16[256,128]{1,0:T(8,128)(2,1)S(1)}, bf16[256,128]{1,0:T(8,128)(2,1)S(1)}, u32[]{:S(2)}, u32[]{:S(2)}) collective-permute-start(bf16[256,128]{1,0:T(8,128)(2,1)S(1)} %get-tuple-element.83.refs_0_), channel_id=1, source_target_pairs={{0,2},{2,4},{4,6},{6,0},{1,3},{3,5},{5,7},{7,1},{8,10},{10,12},{12... | collective-permute-start | bytes 196616 | tf_op jit(solution)/shard_map/ppermute | solution.py:553
  47.9 1.9 %collective-permute-start.21 = (bf16[256,128]{1,0:T(8,128)(2,1)S(1)}, bf16[256,128]{1,0:T(8,128)(2,1)S(1)}, u32[]{:S(2)}, u32[]{:S(2)}) collective-permute-start(bf16[256,128]{1,0:T(8,128)(2,1)S(1)} %get-tuple-element.87.refs_4_), channel_id=1, source_target_pairs={{0,6},{2,0},{4,2},{6,4},{1,7},{3,1},{5,3},{7,5},{8,14},{10,8},{12,... | collective-permute-start | bytes 196616 | tf_op jit(solution)/shard_map/ppermute | solution.py:553
  50.4 2.7 %collective-permute-done.14.refs_2_ = bf16[256,128]{1,0:T(8,128)(2,1)S(1)} collective-permute-done((bf16[256,128]{1,0:T(8,128)(2,1)S(1)}, bf16[256,128]{1,0:T(8,128)(2,1)S(1)}, u32[]{:S(2)}, u32[]{:S(2)}) %collective-permute-start.14) | collective-permute-done | bytes 65568 | tf_op jit(solution)/shard_map/ppermute | solution.py:553
  53.1 2.4 %forward_middle.3 = (bf16[128,1024]{1,0:T(8,128)(2,1)S(1)}, f32[128,128]{1,0:T(8,128)S(1)}, bf16[128,128]{1,0:T(8,128)(2,1)S(1)}, f32[128,128]{1,0:T(8,128)S(1)}...) custom-call(bf16[256,128]{1,0:T(8,128)(2,1)S(1)} %get-tuple-element.83.refs_0_, ...), custom_call_target="tpu_custom_call" | custom-call | tf_op jit(solution)/shard_map/forward_middle/pallas_call | solution.py:586
  56.2 3.4 %collective-permute-start.17 = (bf16[256,128]{1,0:T(8,128)(2,1)S(1)}, bf16[256,128]{1,0:T(8,128)(2,1)S(1)}, u32[]{:S(2)}, u32[]{:S(2)}) collective-permute-start(bf16[256,128]{1,0:T(8,128)(2,1)S(1)} %get-tuple-element.86.refs_0_), channel_id=1, source_target_pairs={{0,4},{2,6},{4,0},{6,2},{1,5},{3,7},{5,1},{7,3},{8,12},{10,14},{12... | collective-permute-start | bytes 196616 | tf_op jit(solution)/shard_map/ppermute | solution.py:553
  59.5 1.9 %collective-permute-start.16 = (bf16[256,128]{1,0:T(8,128)(2,1)S(1)}, bf16[256,128]{1,0:T(8,128)(2,1)S(1)}, u32[]{:S(2)}, u32[]{:S(2)}) collective-permute-start(bf16[256,128]{1,0:T(8,128)(2,1)S(1)} %get-tuple-element.86.refs_0_), channel_id=1, source_target_pairs={{0,2},{2,4},{4,6},{6,0},{1,3},{3,5},{5,7},{7,1},{8,10},{10,12},{12... | collective-permute-start | bytes 196616 | tf_op jit(solution)/shard_map/ppermute | solution.py:553
  61.5 4.3 %collective-permute-done.17.refs_2_ = bf16[256,128]{1,0:T(8,128)(2,1)S(1)} collective-permute-done((bf16[256,128]{1,0:T(8,128)(2,1)S(1)}, bf16[256,128]{1,0:T(8,128)(2,1)S(1)}, u32[]{:S(2)}, u32[]{:S(2)}) %collective-permute-start.17) | collective-permute-done | bytes 65568 | tf_op jit(solution)/shard_map/ppermute | solution.py:553
  65.9 3.3 %turn.1 = (bf16[128,1024]{1,0:T(8,128)(2,1)S(1)}, f32[128,128]{1,0:T(8,128)S(1)}, bf16[128,128]{1,0:T(8,128)(2,1)S(1)}, f32[128,128]{1,0:T(8,128)S(1)}, bf16[2,2...) custom-call(bf16[256,128]{1,0:T(8,128)(2,1)S(1)} %get-tuple-element.86.refs_0_, ...), custom_call_target="tpu_custom_call" | custom-call | tf_op jit(solution)/shard_map/turn/pallas_call | solution.py:586
  70.6 1.9 %collective-permute-start.22 = (bf16[272,128]{1,0:T(8,128)(2,1)S(1)}, bf16[272,128]{1,0:T(8,128)(2,1)S(1)}, u32[]{:S(2)}, u32[]{:S(2)}) collective-permute-start(bf16[272,128]{1,0:T(8,128)(2,1)S(1)} %get-tuple-element.90.refs_0_), channel_id=1, source_target_pairs={{0,2},{2,4},{4,6},{6,0},{1,3},{3,5},{5,7},{7,1},{8,10},{10,12},{12... | collective-permute-start | bytes 208904 | tf_op jit(solution)/shard_map/ppermute | solution.py:553
  73.7 3.7 %collective-permute-done.23.refs_2_ = bf16[272,128]{1,0:T(8,128)(2,1)S(1)} collective-permute-done((bf16[272,128]{1,0:T(8,128)(2,1)S(1)}, bf16[272,128]{1,0:T(8,128)(2,1)S(1)}, u32[]{:S(2)}, u32[]{:S(2)}) %collective-permute-start.23) | collective-permute-done | bytes 69664 | tf_op jit(solution)/shard_map/ppermute | solution.py:553
  77.4 1.7 %backward.3 = (bf16[272,512]{1,0:T(8,128)(2,1)S(1)}, bf16[272,512]{1,0:T(8,128)(2,1)S(1)}, bf16[272,512]{1,0:T(8,128)(2,1)S(1)}, bf16[272,512]{1,0:T(8,128)(2,1)...) custom-call(bf16[272,128]{1,0:T(8,128)(2,1)S(1)} %get-tuple-element.90.refs_0_, ...), custom_call_target="tpu_custom_call" | custom-call | tf_op jit(solution)/shard_map/backward/pallas_call | solution.py:586
  79.1 1.7 %collective-permute-start.27 = (bf16[144,128]{1,0:T(8,128)(2,1)S(1)}, bf16[144,128]{1,0:T(8,128)(2,1)S(1)}, u32[]{:S(2)}, u32[]{:S(2)}) collective-permute-start(bf16[144,128]{1,0:T(8,128)(2,1)S(1)} %get-tuple-element.99.refs_0_), channel_id=1, source_target_pairs={{0,6},{2,0},{4,2},{6,4},{1,7},{3,1},{5,3},{7,5},{8,14},{10,8},{12,... | collective-permute-start | bytes 110600 | tf_op jit(solution)/shard_map/ppermute | solution.py:553
  81.0 1.9 %collective-permute-start.25 = (bf16[144,128]{1,0:T(8,128)(2,1)S(1)}, bf16[144,128]{1,0:T(8,128)(2,1)S(1)}, u32[]{:S(2)}, u32[]{:S(2)}) collective-permute-start(bf16[144,128]{1,0:T(8,128)(2,1)S(1)} %get-tuple-element.99.refs_0_), channel_id=1, source_target_pairs={{0,2},{2,4},{4,6},{6,0},{1,3},{3,5},{5,7},{7,1},{8,10},{10,12},{12... | collective-permute-start | bytes 110600 | tf_op jit(solution)/shard_map/ppermute | solution.py:553
  83.3 2.6 %collective-permute-done.26.refs_2_ = bf16[144,128]{1,0:T(8,128)(2,1)S(1)} collective-permute-done((bf16[144,128]{1,0:T(8,128)(2,1)S(1)}, bf16[144,128]{1,0:T(8,128)(2,1)S(1)}, u32[]{:S(2)}, u32[]{:S(2)}) %collective-permute-start.26) | collective-permute-done | bytes 36896 | tf_op jit(solution)/shard_map/ppermute | solution.py:553
  86.7 1.7 %backward.4 = (bf16[272,512]{1,0:T(8,128)(2,1)S(1)}, bf16[272,512]{1,0:T(8,128)(2,1)S(1)}, bf16[128,1024]{1,0:T(8,128)(2,1)S(1)}, bf16[144,128]{1,0:T(8,128)(2,1)S(1)}) custom-call(bf16[144,128]{1,0:T(8,128)(2,1)S(1)} %get-tuple-element.99.refs_0_, bf16[144,128]{1,0:T(8,128)(2,1)S(1)} %collective-permute-done.25.refs_1_, ...), custom_call_target="tpu_custom_call" | custom-call | tf_op jit(solution)/shard_map/backward/pallas_call | solution.py:586
  92.8 1.5 %collective-permute-done.29.refs_2_ = bf16[144,128]{1,0:T(8,128)(2,1)S(1)} collective-permute-done((bf16[144,128]{1,0:T(8,128)(2,1)S(1)}, bf16[144,128]{1,0:T(8,128)(2,1)S(1)}, u32[]{:S(2)}, u32[]{:S(2)}) %collective-permute-start.29) | collective-permute-done | bytes 36896 | tf_op jit(solution)/shard_map/ppermute | solution.py:553
  101.1 1.9 %collective-permute-start.37 = (bf16[272,512]{1,0:T(8,128)(2,1)S(1)}, bf16[272,512]{1,0:T(8,128)(2,1)S(1)}, u32[]{:S(2)}, u32[]{:S(2)}) collective-permute-start(bf16[272,512]{1,0:T(8,128)(2,1)S(1)} %get-tuple-element.122), channel_id=1, source_target_pairs={{0,24},{8,16},{16,8},{24,0},{1,25},{9,17},{17,9},{25,1},{2,26},{10... | collective-permute-start | bytes 835592 | tf_op jit(solution)/shard_map/ppermute | solution.py:556
  103.0 6.0 %collective-permute-done.35.refs_1_ = bf16[272,512]{1,0:T(8,128)(2,1)S(1)} collective-permute-done((bf16[272,512]{1,0:T(8,128)(2,1)S(1)}, bf16[272,512]{1,0:T(8,128)(2,1)S(1)}, u32[]{:S(2)}, u32[]{:S(2)}) %collective-permute-start.35) | collective-permute-done | bytes 278560 | tf_op jit(solution)/shard_map/ppermute | solution.py:556
  109.0 6.3 %collective-permute-done.36.refs_2_ = bf16[272,512]{1,0:T(8,128)(2,1)S(1)} collective-permute-done((bf16[272,512]{1,0:T(8,128)(2,1)S(1)}, bf16[272,512]{1,0:T(8,128)(2,1)S(1)}, u32[]{:S(2)}, u32[]{:S(2)}) %collective-permute-start.36) | collective-permute-done | bytes 278560 | tf_op jit(solution)/shard_map/ppermute | solution.py:556
  (60 shorter events, 25.3 us)
Async XLA Ops:
  4.5 9.2 %collective-permute-start = (bf16[32,2176]{1,0:T(8,128)(2,1)}, bf16[32,2176]{1,0:T(8,128)(2,1)S(1)}, u32[]{:S(2)}, u32[]{:S(2)}) collective-permute-start(bf16[32,2176]{1,0:T(8,128)(2,1)} %get-tuple-element.65), channel_id=1, source_target_pairs={{0,2},{2,4},{4,6},{6,0},{1,3},{3,5},{5,7},{7,1},{8,10},{10,12},{12... | collective-permute-start | bytes 417800 | tf_op jit(solution)/shard_map/ppermute | solution.py:553
  7.6 13.1 %collective-permute-start.5 = (bf16[1040,128]{1,0:T(8,128)(2,1)}, bf16[1040,128]{1,0:T(8,128)(2,1)S(1)}, u32[]{:S(2)}, u32[]{:S(2)}) collective-permute-start(bf16[1040,128]{1,0:T(8,128)(2,1)} %pack_weights.1.refs_4_), channel_id=1, source_target_pairs={{0,24},{8,16},{16,8},{24,0},{1,25},{9,17},{17,9},{25,1},{2,26},{10... | collective-permute-start | bytes 798728 | tf_op jit(solution)/shard_map/ppermute | solution.py:556
  10.0 12.2 %collective-permute-start.4 = (bf16[1040,128]{1,0:T(8,128)(2,1)}, bf16[1040,128]{1,0:T(8,128)(2,1)S(1)}, u32[]{:S(2)}, u32[]{:S(2)}) collective-permute-start(bf16[1040,128]{1,0:T(8,128)(2,1)} %pack_weights.1.refs_4_), channel_id=1, source_target_pairs={{0,16},{8,24},{16,0},{24,8},{1,17},{9,25},{17,1},{25,9},{2,18},{10... | collective-permute-start | bytes 798728 | tf_op jit(solution)/shard_map/ppermute | solution.py:556
  10.6 11.8 %collective-permute-start.3 = (bf16[1040,128]{1,0:T(8,128)(2,1)}, bf16[1040,128]{1,0:T(8,128)(2,1)S(1)}, u32[]{:S(2)}, u32[]{:S(2)}) collective-permute-start(bf16[1040,128]{1,0:T(8,128)(2,1)} %pack_weights.1.refs_4_), channel_id=1, source_target_pairs={{0,8},{8,0},{16,24},{24,16},{1,9},{9,1},{17,25},{25,17},{2,10},{10... | collective-permute-start | bytes 798728 | tf_op jit(solution)/shard_map/ppermute | solution.py:556
  11.1 9.6 %collective-permute-start.1 = (bf16[32,2176]{1,0:T(8,128)(2,1)}, bf16[32,2176]{1,0:T(8,128)(2,1)S(1)}, u32[]{:S(2)}, u32[]{:S(2)}) collective-permute-start(bf16[32,2176]{1,0:T(8,128)(2,1)} %get-tuple-element.66), channel_id=1, source_target_pairs={{0,4},{2,6},{4,0},{6,2},{1,5},{3,7},{5,1},{7,3},{8,12},{10,14},{12... | collective-permute-start | bytes 417800 | tf_op jit(solution)/shard_map/ppermute | solution.py:553
  13.7 7.0 %collective-permute-start.2 = (bf16[32,2176]{1,0:T(8,128)(2,1)}, bf16[32,2176]{1,0:T(8,128)(2,1)S(1)}, u32[]{:S(2)}, u32[]{:S(2)}) collective-permute-start(bf16[32,2176]{1,0:T(8,128)(2,1)} %get-tuple-element.67), channel_id=1, source_target_pairs={{0,6},{2,0},{4,2},{6,4},{1,7},{3,1},{5,3},{7,5},{8,14},{10,8},{12,... | collective-permute-start | bytes 417800 | tf_op jit(solution)/shard_map/ppermute | solution.py:553
  28.4 5.9 %collective-permute-start.12 = (bf16[400,128]{1,0:T(8,128)(2,1)S(1)}, bf16[400,128]{1,0:T(8,128)(2,1)S(1)}, u32[]{:S(2)}, u32[]{:S(2)}) collective-permute-start(bf16[400,128]{1,0:T(8,128)(2,1)S(1)} %get-tuple-element.81.refs_0_.refs_4_), channel_id=1, source_target_pairs={{0,6},{2,0},{4,2},{6,4},{1,7},{3,1},{5,3},{7,5},{8,14},{10,8},{12,... | collective-permute-start | bytes 307208 | tf_op jit(solution)/shard_map/ppermute | solution.py:553
  31.0 10.0 %collective-permute-start.11 = (bf16[400,128]{1,0:T(8,128)(2,1)S(1)}, bf16[400,128]{1,0:T(8,128)(2,1)S(1)}, u32[]{:S(2)}, u32[]{:S(2)}) collective-permute-start(bf16[400,128]{1,0:T(8,128)(2,1)S(1)} %get-tuple-element.81.refs_0_.refs_4_), channel_id=1, source_target_pairs={{0,4},{2,6},{4,0},{6,2},{1,5},{3,7},{5,1},{7,3},{8,12},{10,14},{12... | collective-permute-start | bytes 307208 | tf_op jit(solution)/shard_map/ppermute | solution.py:553
  31.5 9.5 %collective-permute-start.10 = (bf16[400,128]{1,0:T(8,128)(2,1)S(1)}, bf16[400,128]{1,0:T(8,128)(2,1)S(1)}, u32[]{:S(2)}, u32[]{:S(2)}) collective-permute-start(bf16[400,128]{1,0:T(8,128)(2,1)S(1)} %get-tuple-element.81.refs_0_.refs_4_), channel_id=1, source_target_pairs={{0,2},{2,4},{4,6},{6,0},{1,3},{3,5},{5,7},{7,1},{8,10},{10,12},{12... | collective-permute-start | bytes 307208 | tf_op jit(solution)/shard_map/ppermute | solution.py:553
  43.4 6.4 %collective-permute-start.15 = (bf16[256,128]{1,0:T(8,128)(2,1)S(1)}, bf16[256,128]{1,0:T(8,128)(2,1)S(1)}, u32[]{:S(2)}, u32[]{:S(2)}) collective-permute-start(bf16[256,128]{1,0:T(8,128)(2,1)S(1)} %get-tuple-element.83.refs_0_), channel_id=1, source_target_pairs={{0,6},{2,0},{4,2},{6,4},{1,7},{3,1},{5,3},{7,5},{8,14},{10,8},{12,... | collective-permute-start | bytes 196616 | tf_op jit(solution)/shard_map/ppermute | solution.py:553
  44.7 8.4 %collective-permute-start.14 = (bf16[256,128]{1,0:T(8,128)(2,1)S(1)}, bf16[256,128]{1,0:T(8,128)(2,1)S(1)}, u32[]{:S(2)}, u32[]{:S(2)}) collective-permute-start(bf16[256,128]{1,0:T(8,128)(2,1)S(1)} %get-tuple-element.83.refs_0_), channel_id=1, source_target_pairs={{0,4},{2,6},{4,0},{6,2},{1,5},{3,7},{5,1},{7,3},{8,12},{10,14},{12... | collective-permute-start | bytes 196616 | tf_op jit(solution)/shard_map/ppermute | solution.py:553
  46.0 7.2 %collective-permute-start.13 = (bf16[256,128]{1,0:T(8,128)(2,1)S(1)}, bf16[256,128]{1,0:T(8,128)(2,1)S(1)}, u32[]{:S(2)}, u32[]{:S(2)}) collective-permute-start(bf16[256,128]{1,0:T(8,128)(2,1)S(1)} %get-tuple-element.83.refs_0_), channel_id=1, source_target_pairs={{0,2},{2,4},{4,6},{6,0},{1,3},{3,5},{5,7},{7,1},{8,10},{10,12},{12... | collective-permute-start | bytes 196616 | tf_op jit(solution)/shard_map/ppermute | solution.py:553
  47.9 11.6 %collective-permute-start.21 = (bf16[256,128]{1,0:T(8,128)(2,1)S(1)}, bf16[256,128]{1,0:T(8,128)(2,1)S(1)}, u32[]{:S(2)}, u32[]{:S(2)}) collective-permute-start(bf16[256,128]{1,0:T(8,128)(2,1)S(1)} %get-tuple-element.87.refs_4_), channel_id=1, source_target_pairs={{0,6},{2,0},{4,2},{6,4},{1,7},{3,1},{5,3},{7,5},{8,14},{10,8},{12,... | collective-permute-start | bytes 196616 | tf_op jit(solution)/shard_map/ppermute | solution.py:553
  49.8 11.7 %collective-permute-start.20 = (bf16[256,128]{1,0:T(8,128)(2,1)S(1)}, bf16[256,128]{1,0:T(8,128)(2,1)S(1)}, u32[]{:S(2)}, u32[]{:S(2)}) collective-permute-start(bf16[256,128]{1,0:T(8,128)(2,1)S(1)} %get-tuple-element.87.refs_4_), channel_id=1, source_target_pairs={{0,4},{2,6},{4,0},{6,2},{1,5},{3,7},{5,1},{7,3},{8,12},{10,14},{12... | collective-permute-start | bytes 196616 | tf_op jit(solution)/shard_map/ppermute | solution.py:553
  49.8 11.7 %collective-permute-start.19 = (bf16[256,128]{1,0:T(8,128)(2,1)S(1)}, bf16[256,128]{1,0:T(8,128)(2,1)S(1)}, u32[]{:S(2)}, u32[]{:S(2)}) collective-permute-start(bf16[256,128]{1,0:T(8,128)(2,1)S(1)} %get-tuple-element.87.refs_4_), channel_id=1, source_target_pairs={{0,2},{2,4},{4,6},{6,0},{1,3},{3,5},{5,7},{7,1},{8,10},{10,12},{12... | collective-permute-start | bytes 196616 | tf_op jit(solution)/shard_map/ppermute | solution.py:553
  55.6 5.9 %collective-permute-start.18 = (bf16[256,128]{1,0:T(8,128)(2,1)S(1)}, bf16[256,128]{1,0:T(8,128)(2,1)S(1)}, u32[]{:S(2)}, u32[]{:S(2)}) collective-permute-start(bf16[256,128]{1,0:T(8,128)(2,1)S(1)} %get-tuple-element.86.refs_0_), channel_id=1, source_target_pairs={{0,6},{2,0},{4,2},{6,4},{1,7},{3,1},{5,3},{7,5},{8,14},{10,8},{12,... | collective-permute-start | bytes 196616 | tf_op jit(solution)/shard_map/ppermute | solution.py:553
  56.2 9.7 %collective-permute-start.17 = (bf16[256,128]{1,0:T(8,128)(2,1)S(1)}, bf16[256,128]{1,0:T(8,128)(2,1)S(1)}, u32[]{:S(2)}, u32[]{:S(2)}) collective-permute-start(bf16[256,128]{1,0:T(8,128)(2,1)S(1)} %get-tuple-element.86.refs_0_), channel_id=1, source_target_pairs={{0,4},{2,6},{4,0},{6,2},{1,5},{3,7},{5,1},{7,3},{8,12},{10,14},{12... | collective-permute-start | bytes 196616 | tf_op jit(solution)/shard_map/ppermute | solution.py:553
  59.5 6.3 %collective-permute-start.16 = (bf16[256,128]{1,0:T(8,128)(2,1)S(1)}, bf16[256,128]{1,0:T(8,128)(2,1)S(1)}, u32[]{:S(2)}, u32[]{:S(2)}) collective-permute-start(bf16[256,128]{1,0:T(8,128)(2,1)S(1)} %get-tuple-element.86.refs_0_), channel_id=1, source_target_pairs={{0,2},{2,4},{4,6},{6,0},{1,3},{3,5},{5,7},{7,1},{8,10},{10,12},{12... | collective-permute-start | bytes 196616 | tf_op jit(solution)/shard_map/ppermute | solution.py:553
  69.2 4.5 %collective-permute-start.24 = (bf16[272,128]{1,0:T(8,128)(2,1)S(1)}, bf16[272,128]{1,0:T(8,128)(2,1)S(1)}, u32[]{:S(2)}, u32[]{:S(2)}) collective-permute-start(bf16[272,128]{1,0:T(8,128)(2,1)S(1)} %get-tuple-element.90.refs_0_), channel_id=1, source_target_pairs={{0,6},{2,0},{4,2},{6,4},{1,7},{3,1},{5,3},{7,5},{8,14},{10,8},{12,... | collective-permute-start | bytes 208904 | tf_op jit(solution)/shard_map/ppermute | solution.py:553
  70.5 6.9 %collective-permute-start.23 = (bf16[272,128]{1,0:T(8,128)(2,1)S(1)}, bf16[272,128]{1,0:T(8,128)(2,1)S(1)}, u32[]{:S(2)}, u32[]{:S(2)}) collective-permute-start(bf16[272,128]{1,0:T(8,128)(2,1)S(1)} %get-tuple-element.90.refs_0_), channel_id=1, source_target_pairs={{0,4},{2,6},{4,0},{6,2},{1,5},{3,7},{5,1},{7,3},{8,12},{10,14},{12... | collective-permute-start | bytes 208904 | tf_op jit(solution)/shard_map/ppermute | solution.py:553
  70.6 6.8 %collective-permute-start.22 = (bf16[272,128]{1,0:T(8,128)(2,1)S(1)}, bf16[272,128]{1,0:T(8,128)(2,1)S(1)}, u32[]{:S(2)}, u32[]{:S(2)}) collective-permute-start(bf16[272,128]{1,0:T(8,128)(2,1)S(1)} %get-tuple-element.90.refs_0_), channel_id=1, source_target_pairs={{0,2},{2,4},{4,6},{6,0},{1,3},{3,5},{5,7},{7,1},{8,10},{10,12},{12... | collective-permute-start | bytes 208904 | tf_op jit(solution)/shard_map/ppermute | solution.py:553
  80.9 5.0 %collective-permute-start.26 = (bf16[144,128]{1,0:T(8,128)(2,1)S(1)}, bf16[144,128]{1,0:T(8,128)(2,1)S(1)}, u32[]{:S(2)}, u32[]{:S(2)}) collective-permute-start(bf16[144,128]{1,0:T(8,128)(2,1)S(1)} %get-tuple-element.99.refs_0_), channel_id=1, source_target_pairs={{0,4},{2,6},{4,0},{6,2},{1,5},{3,7},{5,1},{7,3},{8,12},{10,14},{12... | collective-permute-start | bytes 110600 | tf_op jit(solution)/shard_map/ppermute | solution.py:553
  81.0 5.8 %collective-permute-start.25 = (bf16[144,128]{1,0:T(8,128)(2,1)S(1)}, bf16[144,128]{1,0:T(8,128)(2,1)S(1)}, u32[]{:S(2)}, u32[]{:S(2)}) collective-permute-start(bf16[144,128]{1,0:T(8,128)(2,1)S(1)} %get-tuple-element.99.refs_0_), channel_id=1, source_target_pairs={{0,2},{2,4},{4,6},{6,0},{1,3},{3,5},{5,7},{7,1},{8,10},{10,12},{12... | collective-permute-start | bytes 110600 | tf_op jit(solution)/shard_map/ppermute | solution.py:553
  88.4 4.4 %collective-permute-start.30 = (bf16[144,128]{1,0:T(8,128)(2,1)S(1)}, bf16[144,128]{1,0:T(8,128)(2,1)S(1)}, u32[]{:S(2)}, u32[]{:S(2)}) collective-permute-start(bf16[144,128]{1,0:T(8,128)(2,1)S(1)} %get-tuple-element.105.refs_0_), channel_id=1, source_target_pairs={{0,6},{2,0},{4,2},{6,4},{1,7},{3,1},{5,3},{7,5},{8,14},{10,8},{12,... | collective-permute-start | bytes 110600 | tf_op jit(solution)/shard_map/ppermute | solution.py:553
  89.5 4.9 %collective-permute-start.29 = (bf16[144,128]{1,0:T(8,128)(2,1)S(1)}, bf16[144,128]{1,0:T(8,128)(2,1)S(1)}, u32[]{:S(2)}, u32[]{:S(2)}) collective-permute-start(bf16[144,128]{1,0:T(8,128)(2,1)S(1)} %get-tuple-element.105.refs_0_), channel_id=1, source_target_pairs={{0,4},{2,6},{4,0},{6,2},{1,5},{3,7},{5,1},{7,3},{8,12},{10,14},{12... | collective-permute-start | bytes 110600 | tf_op jit(solution)/shard_map/ppermute | solution.py:553
  90.1 5.8 %collective-permute-start.28 = (bf16[144,128]{1,0:T(8,128)(2,1)S(1)}, bf16[144,128]{1,0:T(8,128)(2,1)S(1)}, u32[]{:S(2)}, u32[]{:S(2)}) collective-permute-start(bf16[144,128]{1,0:T(8,128)(2,1)S(1)} %get-tuple-element.105.refs_0_), channel_id=1, source_target_pairs={{0,2},{2,4},{4,6},{6,0},{1,3},{3,5},{5,7},{7,1},{8,10},{10,12},{12... | collective-permute-start | bytes 110600 | tf_op jit(solution)/shard_map/ppermute | solution.py:553
  91.5 5.8 %collective-permute-start.33 = (bf16[272,512]{1,0:T(8,128)(2,1)S(1)}, bf16[272,512]{1,0:T(8,128)(2,1)S(1)}, u32[]{:S(2)}, u32[]{:S(2)}) collective-permute-start(bf16[272,512]{1,0:T(8,128)(2,1)S(1)} %get-tuple-element.117), channel_id=1, source_target_pairs={{0,1},{1,0},{2,3},{3,2},{4,5},{5,4},{6,7},{7,6},{8,9},{9,8},{10,11... | collective-permute-start | bytes 835592 | tf_op jit(solution)/shard_map/ppermute | solution.py:559
  91.5 5.8 %collective-permute-start.34 = (bf16[272,512]{1,0:T(8,128)(2,1)S(1)}, bf16[272,512]{1,0:T(8,128)(2,1)S(1)}, u32[]{:S(2)}, u32[]{:S(2)}) collective-permute-start(bf16[272,512]{1,0:T(8,128)(2,1)S(1)} %get-tuple-element.118), channel_id=1, source_target_pairs={{0,1},{1,0},{2,3},{3,2},{4,5},{5,4},{6,7},{7,6},{8,9},{9,8},{10,11... | collective-permute-start | bytes 835592 | tf_op jit(solution)/shard_map/ppermute | solution.py:559
  92.8 4.5 %collective-permute-start.32 = (bf16[272,512]{1,0:T(8,128)(2,1)S(1)}, bf16[272,512]{1,0:T(8,128)(2,1)S(1)}, u32[]{:S(2)}, u32[]{:S(2)}) collective-permute-start(bf16[272,512]{1,0:T(8,128)(2,1)S(1)} %get-tuple-element.116), channel_id=1, source_target_pairs={{0,1},{1,0},{2,3},{3,2},{4,5},{5,4},{6,7},{7,6},{8,9},{9,8},{10,11... | collective-permute-start | bytes 835592 | tf_op jit(solution)/shard_map/ppermute | solution.py:559
  99.4 9.6 %collective-permute-start.35 = (bf16[272,512]{1,0:T(8,128)(2,1)S(1)}, bf16[272,512]{1,0:T(8,128)(2,1)S(1)}, u32[]{:S(2)}, u32[]{:S(2)}) collective-permute-start(bf16[272,512]{1,0:T(8,128)(2,1)S(1)} %get-tuple-element.120), channel_id=1, source_target_pairs={{0,8},{8,0},{16,24},{24,16},{1,9},{9,1},{17,25},{25,17},{2,10},{10... | collective-permute-start | bytes 835592 | tf_op jit(solution)/shard_map/ppermute | solution.py:556
  101.0 14.4 %collective-permute-start.36 = (bf16[272,512]{1,0:T(8,128)(2,1)S(1)}, bf16[272,512]{1,0:T(8,128)(2,1)S(1)}, u32[]{:S(2)}, u32[]{:S(2)}) collective-permute-start(bf16[272,512]{1,0:T(8,128)(2,1)S(1)} %get-tuple-element.121), channel_id=1, source_target_pairs={{0,16},{8,24},{16,0},{24,8},{1,17},{9,25},{17,1},{25,9},{2,18},{10... | collective-permute-start | bytes 835592 | tf_op jit(solution)/shard_map/ppermute | solution.py:556
  101.1 14.3 %collective-permute-start.37 = (bf16[272,512]{1,0:T(8,128)(2,1)S(1)}, bf16[272,512]{1,0:T(8,128)(2,1)S(1)}, u32[]{:S(2)}, u32[]{:S(2)}) collective-permute-start(bf16[272,512]{1,0:T(8,128)(2,1)S(1)} %get-tuple-element.122), channel_id=1, source_target_pairs={{0,24},{8,16},{16,8},{24,0},{1,25},{9,17},{17,9},{25,1},{2,26},{10... | collective-permute-start | bytes 835592 | tf_op jit(solution)/shard_map/ppermute | solution.py:556
  (8 other events, 35.9 us)

commit v8 on v7

--- a/solution.py
+++ b/solution.py
@@ -45,52 +45,22 @@
     return 2 * own + 16
 
 
-def pack_weights_kernel(gain, first, second, weights, gain_in, second_in, sems):
+def pack_kernel(groups, micro_local, *refs):
+    tokens, cotangents, starts, counts, gain, first, second = refs[:7]
+    parts, weights = refs[7 : 7 + groups], refs[7 + groups]
+    tok, cot, starts_in, counts_in, gain_in, second_in, sems = refs[8 + groups :]
+    directions, micro_count, length, width = tokens.shape
+    local = width // groups
     own = first.shape[1]
+    section = lax.axis_index("pipe")
+    group = lax.axis_index("z")
+    picks = []
     copies = [
         pltpu.make_async_copy(second.at[0], second_in, sems.at[0]),
         pltpu.make_async_copy(gain, gain_in, sems.at[1]),
         pltpu.make_async_copy(first.at[0], weights.at[pl.ds(0, own)], sems.at[2]),
-    ]
-    for copy in copies:
-        copy.start()
-    for copy in copies:
-        copy.wait()
-    weights[own : 2 * own, :] = second_in[...].astype(F32).T.astype(BF)
-    gains = [gain_in[0:1, head * HD : (head + 1) * HD].astype(F32) for head in range(own // HD)]
-    gains.append(jnp.zeros((16 - own // HD, HD), F32))
-    weights[2 * own :, :] = jnp.concatenate(gains, axis=0).astype(BF)
-
-
-def pack_weights(gain, first, second):
-    own = first.shape[1]
-    return pl.pallas_call(
-        pack_weights_kernel,
-        in_specs=[pl.BlockSpec(memory_space=pltpu.HBM)] * 3,
-        out_specs=pl.BlockSpec(memory_space=pltpu.VMEM),
-        out_shape=jax.ShapeDtypeStruct((slice_rows(own), HD), BF),
-        scratch_shapes=[
-            pltpu.VMEM(gain.shape, BF),
-            pltpu.VMEM(second.shape[1:], BF),
-            pltpu.SemaphoreType.DMA((3,)),
-        ],
-        compiler_params=PACK_PARAMS,
-        name="pack_weights",
-    )(gain, first, second)
-
-
-def pack_tokens_kernel(groups, micro_local, *refs):
-    tokens, cotangents, starts, counts = refs[:4]
-    parts = refs[4 : 4 + groups]
-    tok, cot, starts_in, counts_in, sems = refs[4 + groups :]
-    directions, micro_count, length, width = tokens.shape
-    local = width // groups
-    section = lax.axis_index("pipe")
-    group = lax.axis_index("z")
-    picks = []
-    copies = [
-        pltpu.make_async_copy(starts, starts_in, sems.at[0]),
-        pltpu.make_async_copy(counts, counts_in, sems.at[1]),
+        pltpu.make_async_copy(starts, starts_in, sems.at[3]),
+        pltpu.make_async_copy(counts, counts_in, sems.at[4]),
     ]
     for micro in range(micro_local):
         wanted = section * micro_local + micro
@@ -100,18 +70,22 @@
         rows = pl.ds(micro * length, length)
         copies.append(
             pltpu.make_async_copy(
-                tokens.at[direction, place], tok.at[rows], sems.at[2 + 2 * micro]
+                tokens.at[direction, place], tok.at[rows], sems.at[5 + 2 * micro]
             )
         )
         copies.append(
             pltpu.make_async_copy(
-                cotangents.at[direction, place], cot.at[rows], sems.at[3 + 2 * micro]
+                cotangents.at[direction, place], cot.at[rows], sems.at[6 + 2 * micro]
             )
         )
     for copy in copies:
         copy.start()
     for copy in copies:
         copy.wait()
+    weights[own : 2 * own, :] = second_in[...].astype(F32).T.astype(BF)
+    gains = [gain_in[0:1, head * HD : (head + 1) * HD].astype(F32) for head in range(own // HD)]
+    gains.append(jnp.zeros((16 - own // HD, HD), F32))
+    weights[2 * own :, :] = jnp.concatenate(gains, axis=0).astype(BF)
     for micro, (keep, direction, place) in enumerate(picks):
         rows = slice(micro * length, (micro + 1) * length)
         widened = tok[rows, :].astype(F32)
@@ -130,7 +104,7 @@
             jnp.where(lane == 1, mean_high.astype(F32), mean_low.astype(F32)),
         ).astype(BF)
         for shift in range(groups):
-            start = pl.multiple_of(((group + shift) % groups) * local, local)
+            start = pl.multiple_of((group ^ shift) * local, local)
             parts[shift][rows, 0:local] = tok[rows, pl.ds(start, local)]
             cotangent = cot[rows, pl.ds(start, local)]
             parts[shift][rows, local : 2 * local] = jnp.where(
@@ -139,25 +113,31 @@
             parts[shift][rows, 2 * local :] = tail
 
 
-def pack_tokens(tokens, cotangents, starts, counts, groups, micro_local):
+def pack(tokens, cotangents, starts, counts, gain, first, second, groups, micro_local):
     length, width = tokens.shape[2:]
+    own = first.shape[1]
     local = width // groups
     rows = micro_local * length
-    return pl.pallas_call(
-        functools.partial(pack_tokens_kernel, groups, micro_local),
-        in_specs=[pl.BlockSpec(memory_space=pltpu.HBM)] * 4,
-        out_specs=vmem_specs(groups),
-        out_shape=[jax.ShapeDtypeStruct((rows, 2 * local + HD), BF)] * groups,
+    shape = jax.ShapeDtypeStruct
+    results = pl.pallas_call(
+        functools.partial(pack_kernel, groups, micro_local),
+        in_specs=[pl.BlockSpec(memory_space=pltpu.HBM)] * 7,
+        out_specs=vmem_specs(groups + 1),
+        out_shape=[shape((rows, 2 * local + HD), BF)] * groups
+        + [shape((slice_rows(own), HD), BF)],
         scratch_shapes=[
             pltpu.VMEM((rows, width), BF),
             pltpu.VMEM((rows, width), BF),
             pltpu.SMEM(starts.shape, jnp.int32),
             pltpu.SMEM(counts.shape, jnp.int32),
-            pltpu.SemaphoreType.DMA((2 + 2 * micro_local,)),
+            pltpu.VMEM(gain.shape, BF),
+            pltpu.VMEM(second.shape[1:], BF),
+            pltpu.SemaphoreType.DMA((5 + 2 * micro_local,)),
         ],
         compiler_params=PACK_PARAMS,
-        name="pack_tokens",
-    )(tokens, cotangents, starts, counts)
+        name="pack",
+    )(tokens, cotangents, starts, counts, gain, first, second)
+    return results[:groups], results[groups]
 
 
 def head_gain(weights, head):
@@ -299,10 +279,9 @@
 
 
 def place_rows(received, target, columns):
-    groups = len(received)
     rows = received[0].shape[0]
     for shift, part in enumerate(received):
-        source = (lax.axis_index("z") + groups - shift) % groups
+        source = lax.axis_index("z") ^ shift
         target[pl.ds(pl.multiple_of(source * rows, rows), rows), :] = part[:, columns]
 
 
@@ -550,7 +529,7 @@
     top = sections - 1
 
     def shifted(value, shift):
-        return lax.ppermute(value, "z", [(i, (i + shift) % groups) for i in range(groups)])
+        return lax.ppermute(value, "z", [(i, i ^ shift) for i in range(groups)])
 
     def across(value, distance):
         return lax.ppermute(value, "pipe", [(i, i ^ distance) for i in range(sections)])
@@ -561,10 +540,10 @@
     def exchange(pay):
         return [pay] + [shifted(pay, shift) for shift in range(1, groups)]
 
-    packed = pack_weights(layer_gains, first_map, second_map)
+    token_parts, packed = pack(
+        tokens, cotangents, starts, counts, layer_gains, first_map, second_map, groups, micro_local
+    )
     mine = [packed] + [across(packed, distance) for distance in range(1, sections)]
-    tokens, packed = lax.optimization_barrier((tokens, packed))
-    token_parts = pack_tokens(tokens, cotangents, starts, counts, groups, micro_local)
     received = [token_parts[0]]
     received += [shifted(token_parts[shift], shift) for shift in range(1, groups)]
     received, mine = lax.optimization_barrier((received, mine))

time: 116 us -> 115 us (level)
  waiting for transfers between devices: 48.9 us -> 44.4 us
  starting transfers between devices: 43.7 us -> 47.4 us
  Pallas kernels: 21.9 us -> 20.3 us
    ppermute x24, starting transfers between devices: 35.1 us -> 38.7 us  [shifted(): return lax.ppermute(value, 'z', [(i, i ^ shift) for i in range(groups)])]
    ppermute x6, waiting for transfers between devices: 14.1 us -> 12 us  [across(): lax.ppermute(value, 'pipe', [(i, i ^ distance) for i in range(sections)])]
    ppermute x24, waiting for transfers between devices: 32.9 us -> 30.8 us  [shifted(): return lax.ppermute(value, 'z', [(i, i ^ shift) for i in range(groups)])]
    pallas_call x2 -> x1, Pallas kernels: 3.87 us -> 2.29 us  [pack(): pl.pallas_call(functools.partial(pack_kernel, groups, micro_local), in_sp...]
  transfers between devices with their start and end apart: 38 -> 38, of which waited for: 20 -> 16; matrix products, arithmetic and copies ran while one was open for 0% -> 0% of each run, Pallas kernels for 4% -> 4%
where the time goes in v8:
time: 115 us
  starting transfers between devices  47.4 us (41%)
  waiting for transfers between devices  44.4 us (39%)
  Pallas kernels  20.3 us (18%)
  local copies, waits for them, and re-layouts  1.86 us (2%)
    ppermute x24, starting transfers between devices, shifted(): return lax.ppermute(value, 'z', [(i, i ^ shift) for i in range(groups)])  38.7 us
    ppermute x24, waiting for transfers between devices, shifted(): return lax.ppermute(value, 'z', [(i, i ^ shift) for i in range(groups)])  30.8 us
    pallas_call x10, Pallas kernels, call(): pl.pallas_call(kernel, grid=(1,), in_specs=specs, out_specs=vmem_specs(le...  18 us
    ppermute x6, waiting for transfers between devices, across(): lax.ppermute(value, 'pipe', [(i, i ^ distance) for i in range(sections)])  12 us
    ppermute x6, starting transfers between devices, across(): lax.ppermute(value, 'pipe', [(i, i ^ distance) for i in range(sections)])  7.04 us
  transfers between devices with their start and end apart: 38, of which 16 were waited for; matrix products, arithmetic and copies ran while one was open for 0% of the time, Pallas kernels for 4%

profile of v8, /device:TPU:0, one launch (start us, length us, event | category | flops | bytes accessed | tf_op | source)
XLA Modules:
  0.0 114.8 jit_solution(16163868004355659304)
XLA Ops:
  0.6 2.3 %pack.1 = (bf16[32,2176]{1,0:T(8,128)(2,1)}, bf16[32,2176]{1,0:T(8,128)(2,1)}, bf16[32,2176]{1,0:T(8,128)(2,1)}, bf16[32,2176]{1,0:T(8,128)(2,1)}, bf16[1040,128]{1,0:T(8,128)(2,1)}) custom-call(bf16[2,2,32,4096]{3,2,1,0:T(8,128)(2,1)} %refs_0_.1, bf16[2,2,32,4096]{3,2,1,0:T(8,128)(2,1)} %refs_1_.1, s32[2,2,4]{2,1,0:T(2,128)} %refs_2_.1, s32[2,2]{1,0:T(2,128)} %refs_3_.1, ...), custom_call_target="tpu_custom_call" | custom-call | tf_op jit(solution)/shard_map/pack/pallas_call | solution.py:122
  2.9 3.1 %collective-permute-start = (bf16[32,2176]{1,0:T(8,128)(2,1)}, bf16[32,2176]{1,0:T(8,128)(2,1)S(1)}, u32[]{:S(2)}, u32[]{:S(2)}) collective-permute-start(bf16[32,2176]{1,0:T(8,128)(2,1)} %get-tuple-element.64), channel_id=1, source_target_pairs={{0,2},{2,0},{4,6},{6,4},{1,3},{3,1},{5,7},{7,5},{8,10},{10,8},{12,... | collective-permute-start | bytes 417800 | tf_op jit(solution)/shard_map/ppermute | solution.py:532
  6.0 2.4 %collective-permute-start.5 = (bf16[1040,128]{1,0:T(8,128)(2,1)}, bf16[1040,128]{1,0:T(8,128)(2,1)S(1)}, u32[]{:S(2)}, u32[]{:S(2)}) collective-permute-start(bf16[1040,128]{1,0:T(8,128)(2,1)} %get-tuple-element.72.refs_4_), channel_id=1, source_target_pairs={{0,24},{8,16},{16,8},{24,0},{1,25},{9,17},{17,9},{25,1},{2,26},{10... | collective-permute-start | bytes 798728 | tf_op jit(solution)/shard_map/ppermute | solution.py:535
  9.5 2.6 %collective-permute-start.1 = (bf16[32,2176]{1,0:T(8,128)(2,1)}, bf16[32,2176]{1,0:T(8,128)(2,1)S(1)}, u32[]{:S(2)}, u32[]{:S(2)}) collective-permute-start(bf16[32,2176]{1,0:T(8,128)(2,1)} %get-tuple-element.65), channel_id=1, source_target_pairs={{0,4},{2,6},{4,0},{6,2},{1,5},{3,7},{5,1},{7,3},{8,12},{10,14},{12... | collective-permute-start | bytes 417800 | tf_op jit(solution)/shard_map/ppermute | solution.py:532
  12.1 1.6 %collective-permute-start.2 = (bf16[32,2176]{1,0:T(8,128)(2,1)}, bf16[32,2176]{1,0:T(8,128)(2,1)S(1)}, u32[]{:S(2)}, u32[]{:S(2)}) collective-permute-start(bf16[32,2176]{1,0:T(8,128)(2,1)} %get-tuple-element.66), channel_id=1, source_target_pairs={{0,6},{2,4},{4,2},{6,0},{1,7},{3,5},{5,3},{7,1},{8,14},{10,12},{12... | collective-permute-start | bytes 417800 | tf_op jit(solution)/shard_map/ppermute | solution.py:532
  13.7 7.6 %collective-permute-done.1.refs_2_ = bf16[32,2176]{1,0:T(8,128)(2,1)S(1)} collective-permute-done((bf16[32,2176]{1,0:T(8,128)(2,1)}, bf16[32,2176]{1,0:T(8,128)(2,1)S(1)}, u32[]{:S(2)}, u32[]{:S(2)}) %collective-permute-start.1) | collective-permute-done | bytes 139296 | tf_op jit(solution)/shard_map/ppermute | solution.py:532
  24.5 3.4 %forward_first.1 = (bf16[1,8,128,128]{3,2,1,0:T(8,128)(2,1)S(1)}, bf16[128,1024]{1,0:T(8,128)(2,1)S(1)}, bf16[400,128]{1,0:T(8,128)(2,1)S(1)}, bf16[256,128]{1,0:T(8,128)(2,1)S(1)}, bf16[4,2,1040,128]{3,2,1,0:T(8,128)(2,1)S(1)}) custom-call(bf16[1040,128]{1,0:T(8,128)(2,1)S(1)} %get-tuple-element.73.refs_0_, ...), custom_call_target="tpu_custom_call" | custom-call | tf_op jit(solution)/shard_map/forward_first/pallas_call | solution.py:565
  27.9 3.3 %collective-permute-start.12 = (bf16[400,128]{1,0:T(8,128)(2,1)S(1)}, bf16[400,128]{1,0:T(8,128)(2,1)S(1)}, u32[]{:S(2)}, u32[]{:S(2)}) collective-permute-start(bf16[400,128]{1,0:T(8,128)(2,1)S(1)} %get-tuple-element.81.refs_0_.refs_4_), channel_id=1, source_target_pairs={{0,6},{2,4},{4,2},{6,0},{1,7},{3,5},{5,3},{7,1},{8,14},{10,12},{12... | collective-permute-start | bytes 307208 | tf_op jit(solution)/shard_map/ppermute | solution.py:532
  32.7 2.0 %collective-permute-done.12.refs_3_.refs_7_ = bf16[400,128]{1,0:T(8,128)(2,1)S(1)} collective-permute-done((bf16[400,128]{1,0:T(8,128)(2,1)S(1)}, bf16[400,128]{1,0:T(8,128)(2,1)S(1)}, u32[]{:S(2)}, u32[]{:S(2)}) %collective-permute-start.12) | collective-permute-done | bytes 102432 | tf_op jit(solution)/shard_map/ppermute | solution.py:532
  34.7 6.5 %collective-permute-done.11.refs_2_.refs_6_ = bf16[400,128]{1,0:T(8,128)(2,1)S(1)} collective-permute-done((bf16[400,128]{1,0:T(8,128)(2,1)S(1)}, bf16[400,128]{1,0:T(8,128)(2,1)S(1)}, u32[]{:S(2)}, u32[]{:S(2)}) %collective-permute-start.11) | collective-permute-done | bytes 102432 | tf_op jit(solution)/shard_map/ppermute | solution.py:532
  41.2 2.4 %forward_middle.2 = (bf16[128,1024]{1,0:T(8,128)(2,1)S(1)}, f32[128,128]{1,0:T(8,128)S(1)}, bf16[128,128]{1,0:T(8,128)(2,1)S(1)}, f32[128,128]{1,0:T(8,128)S(1)}...) custom-call(bf16[400,128]{1,0:T(8,128)(2,1)S(1)} %get-tuple-element.81.refs_0_.re, ...), custom_call_target="tpu_custom_call" | custom-call | tf_op jit(solution)/shard_map/forward_middle/pallas_call | solution.py:565
  43.6 3.3 %collective-permute-start.15 = (bf16[256,128]{1,0:T(8,128)(2,1)S(1)}, bf16[256,128]{1,0:T(8,128)(2,1)S(1)}, u32[]{:S(2)}, u32[]{:S(2)}) collective-permute-start(bf16[256,128]{1,0:T(8,128)(2,1)S(1)} %get-tuple-element.83.refs_0_), channel_id=1, source_target_pairs={{0,6},{2,4},{4,2},{6,0},{1,7},{3,5},{5,3},{7,1},{8,14},{10,12},{12... | collective-permute-start | bytes 196616 | tf_op jit(solution)/shard_map/ppermute | solution.py:532
  48.1 3.3 %collective-permute-start.21 = (bf16[256,128]{1,0:T(8,128)(2,1)S(1)}, bf16[256,128]{1,0:T(8,128)(2,1)S(1)}, u32[]{:S(2)}, u32[]{:S(2)}) collective-permute-start(bf16[256,128]{1,0:T(8,128)(2,1)S(1)} %get-tuple-element.87.refs_4_), channel_id=1, source_target_pairs={{0,6},{2,4},{4,2},{6,0},{1,7},{3,5},{5,3},{7,1},{8,14},{10,12},{12... | collective-permute-start | bytes 196616 | tf_op jit(solution)/shard_map/ppermute | solution.py:532
  52.5 2.7 %collective-permute-done.14.refs_2_ = bf16[256,128]{1,0:T(8,128)(2,1)S(1)} collective-permute-done((bf16[256,128]{1,0:T(8,128)(2,1)S(1)}, bf16[256,128]{1,0:T(8,128)(2,1)S(1)}, u32[]{:S(2)}, u32[]{:S(2)}) %collective-permute-start.14) | collective-permute-done | bytes 65568 | tf_op jit(solution)/shard_map/ppermute | solution.py:532
  55.2 2.4 %forward_middle.3 = (bf16[128,1024]{1,0:T(8,128)(2,1)S(1)}, f32[128,128]{1,0:T(8,128)S(1)}, bf16[128,128]{1,0:T(8,128)(2,1)S(1)}, f32[128,128]{1,0:T(8,128)S(1)}...) custom-call(bf16[256,128]{1,0:T(8,128)(2,1)S(1)} %get-tuple-element.83.refs_0_, ...), custom_call_target="tpu_custom_call" | custom-call | tf_op jit(solution)/shard_map/forward_middle/pallas_call | solution.py:565
  57.6 2.3 %collective-permute-start.18 = (bf16[256,128]{1,0:T(8,128)(2,1)S(1)}, bf16[256,128]{1,0:T(8,128)(2,1)S(1)}, u32[]{:S(2)}, u32[]{:S(2)}) collective-permute-start(bf16[256,128]{1,0:T(8,128)(2,1)S(1)} %get-tuple-element.86.refs_0_), channel_id=1, source_target_pairs={{0,6},{2,4},{4,2},{6,0},{1,7},{3,5},{5,3},{7,1},{8,14},{10,12},{12... | collective-permute-start | bytes 196616 | tf_op jit(solution)/shard_map/ppermute | solution.py:532
  59.8 2.2 %collective-permute-start.16 = (bf16[256,128]{1,0:T(8,128)(2,1)S(1)}, bf16[256,128]{1,0:T(8,128)(2,1)S(1)}, u32[]{:S(2)}, u32[]{:S(2)}) collective-permute-start(bf16[256,128]{1,0:T(8,128)(2,1)S(1)} %get-tuple-element.86.refs_0_), channel_id=1, source_target_pairs={{0,2},{2,0},{4,6},{6,4},{1,3},{3,1},{5,7},{7,5},{8,10},{10,8},{12,... | collective-permute-start | bytes 196616 | tf_op jit(solution)/shard_map/ppermute | solution.py:532
  62.0 1.7 %collective-permute-done.18.refs_3_ = bf16[256,128]{1,0:T(8,128)(2,1)S(1)} collective-permute-done((bf16[256,128]{1,0:T(8,128)(2,1)S(1)}, bf16[256,128]{1,0:T(8,128)(2,1)S(1)}, u32[]{:S(2)}, u32[]{:S(2)}) %collective-permute-start.18) | collective-permute-done | bytes 65568 | tf_op jit(solution)/shard_map/ppermute | solution.py:532
  65.1 3.3 %turn.1 = (bf16[128,1024]{1,0:T(8,128)(2,1)S(1)}, f32[128,128]{1,0:T(8,128)S(1)}, bf16[128,128]{1,0:T(8,128)(2,1)S(1)}, f32[128,128]{1,0:T(8,128)S(1)}, bf16[2,2...) custom-call(bf16[256,128]{1,0:T(8,128)(2,1)S(1)} %get-tuple-element.86.refs_0_, ...), custom_call_target="tpu_custom_call" | custom-call | tf_op jit(solution)/shard_map/turn/pallas_call | solution.py:565
  68.4 2.3 %collective-permute-start.24 = (bf16[272,128]{1,0:T(8,128)(2,1)S(1)}, bf16[272,128]{1,0:T(8,128)(2,1)S(1)}, u32[]{:S(2)}, u32[]{:S(2)}) collective-permute-start(bf16[272,128]{1,0:T(8,128)(2,1)S(1)} %get-tuple-element.90.refs_0_), channel_id=1, source_target_pairs={{0,6},{2,4},{4,2},{6,0},{1,7},{3,5},{5,3},{7,1},{8,14},{10,12},{12... | collective-permute-start | bytes 208904 | tf_op jit(solution)/shard_map/ppermute | solution.py:532
  71.1 1.7 %collective-permute-start.22 = (bf16[272,128]{1,0:T(8,128)(2,1)S(1)}, bf16[272,128]{1,0:T(8,128)(2,1)S(1)}, u32[]{:S(2)}, u32[]{:S(2)}) collective-permute-start(bf16[272,128]{1,0:T(8,128)(2,1)S(1)} %get-tuple-element.90.refs_0_), channel_id=1, source_target_pairs={{0,2},{2,0},{4,6},{6,4},{1,3},{3,1},{5,7},{7,5},{8,10},{10,8},{12,... | collective-permute-start | bytes 208904 | tf_op jit(solution)/shard_map/ppermute | solution.py:532
  72.9 1.7 %collective-permute-done.24.refs_3_ = bf16[272,128]{1,0:T(8,128)(2,1)S(1)} collective-permute-done((bf16[272,128]{1,0:T(8,128)(2,1)S(1)}, bf16[272,128]{1,0:T(8,128)(2,1)S(1)}, u32[]{:S(2)}, u32[]{:S(2)}) %collective-permute-start.24) | collective-permute-done | bytes 69664 | tf_op jit(solution)/shard_map/ppermute | solution.py:532
  74.6 2.2 %collective-permute-done.23.refs_2_ = bf16[272,128]{1,0:T(8,128)(2,1)S(1)} collective-permute-done((bf16[272,128]{1,0:T(8,128)(2,1)S(1)}, bf16[272,128]{1,0:T(8,128)(2,1)S(1)}, u32[]{:S(2)}, u32[]{:S(2)}) %collective-permute-start.23) | collective-permute-done | bytes 69664 | tf_op jit(solution)/shard_map/ppermute | solution.py:532
  76.7 1.7 %backward.3 = (bf16[272,512]{1,0:T(8,128)(2,1)S(1)}, bf16[272,512]{1,0:T(8,128)(2,1)S(1)}, bf16[272,512]{1,0:T(8,128)(2,1)S(1)}, bf16[272,512]{1,0:T(8,128)(2,1)...) custom-call(bf16[272,128]{1,0:T(8,128)(2,1)S(1)} %get-tuple-element.90.refs_0_, ...), custom_call_target="tpu_custom_call" | custom-call | tf_op jit(solution)/shard_map/backward/pallas_call | solution.py:565
  78.5 1.7 %collective-permute-start.27 = (bf16[144,128]{1,0:T(8,128)(2,1)S(1)}, bf16[144,128]{1,0:T(8,128)(2,1)S(1)}, u32[]{:S(2)}, u32[]{:S(2)}) collective-permute-start(bf16[144,128]{1,0:T(8,128)(2,1)S(1)} %get-tuple-element.99.refs_0_), channel_id=1, source_target_pairs={{0,6},{2,4},{4,2},{6,0},{1,7},{3,5},{5,3},{7,1},{8,14},{10,12},{12... | collective-permute-start | bytes 110600 | tf_op jit(solution)/shard_map/ppermute | solution.py:532
  80.4 2.5 %collective-permute-start.25 = (bf16[144,128]{1,0:T(8,128)(2,1)S(1)}, bf16[144,128]{1,0:T(8,128)(2,1)S(1)}, u32[]{:S(2)}, u32[]{:S(2)}) collective-permute-start(bf16[144,128]{1,0:T(8,128)(2,1)S(1)} %get-tuple-element.99.refs_0_), channel_id=1, source_target_pairs={{0,2},{2,0},{4,6},{6,4},{1,3},{3,1},{5,7},{7,5},{8,10},{10,8},{12,... | collective-permute-start | bytes 110600 | tf_op jit(solution)/shard_map/ppermute | solution.py:532
  85.7 1.7 %backward.4 = (bf16[272,512]{1,0:T(8,128)(2,1)S(1)}, bf16[272,512]{1,0:T(8,128)(2,1)S(1)}, bf16[128,1024]{1,0:T(8,128)(2,1)S(1)}, bf16[144,128]{1,0:T(8,128)(2,1)S(1)}) custom-call(bf16[144,128]{1,0:T(8,128)(2,1)S(1)} %get-tuple-element.99.refs_0_, bf16[144,128]{1,0:T(8,128)(2,1)S(1)} %collective-permute-done.25.refs_1_, ...), custom_call_target="tpu_custom_call" | custom-call | tf_op jit(solution)/shard_map/backward/pallas_call | solution.py:565
  87.4 2.4 %collective-permute-start.30 = (bf16[144,128]{1,0:T(8,128)(2,1)S(1)}, bf16[144,128]{1,0:T(8,128)(2,1)S(1)}, u32[]{:S(2)}, u32[]{:S(2)}) collective-permute-start(bf16[144,128]{1,0:T(8,128)(2,1)S(1)} %get-tuple-element.105.refs_0_), channel_id=1, source_target_pairs={{0,6},{2,4},{4,2},{6,0},{1,7},{3,5},{5,3},{7,1},{8,14},{10,12},{12... | collective-permute-start | bytes 110600 | tf_op jit(solution)/shard_map/ppermute | solution.py:532
  90.1 1.8 %collective-permute-start.28 = (bf16[144,128]{1,0:T(8,128)(2,1)S(1)}, bf16[144,128]{1,0:T(8,128)(2,1)S(1)}, u32[]{:S(2)}, u32[]{:S(2)}) collective-permute-start(bf16[144,128]{1,0:T(8,128)(2,1)S(1)} %get-tuple-element.105.refs_0_), channel_id=1, source_target_pairs={{0,2},{2,0},{4,6},{6,4},{1,3},{3,1},{5,7},{7,5},{8,10},{10,8},{12,... | collective-permute-start | bytes 110600 | tf_op jit(solution)/shard_map/ppermute | solution.py:532
  99.4 1.5 %collective-permute-start.36 = (bf16[272,512]{1,0:T(8,128)(2,1)S(1)}, bf16[272,512]{1,0:T(8,128)(2,1)S(1)}, u32[]{:S(2)}, u32[]{:S(2)}) collective-permute-start(bf16[272,512]{1,0:T(8,128)(2,1)S(1)} %get-tuple-element.121), channel_id=1, source_target_pairs={{0,16},{8,24},{16,0},{24,8},{1,17},{9,25},{17,1},{25,9},{2,18},{10... | collective-permute-start | bytes 835592 | tf_op jit(solution)/shard_map/ppermute | solution.py:535
  101.8 6.0 %collective-permute-done.35.refs_1_ = bf16[272,512]{1,0:T(8,128)(2,1)S(1)} collective-permute-done((bf16[272,512]{1,0:T(8,128)(2,1)S(1)}, bf16[272,512]{1,0:T(8,128)(2,1)S(1)}, u32[]{:S(2)}, u32[]{:S(2)}) %collective-permute-start.35) | collective-permute-done | bytes 278560 | tf_op jit(solution)/shard_map/ppermute | solution.py:535
  107.8 6.0 %collective-permute-done.36.refs_2_ = bf16[272,512]{1,0:T(8,128)(2,1)S(1)} collective-permute-done((bf16[272,512]{1,0:T(8,128)(2,1)S(1)}, bf16[272,512]{1,0:T(8,128)(2,1)S(1)}, u32[]{:S(2)}, u32[]{:S(2)}) %collective-permute-start.36) | collective-permute-done | bytes 278560 | tf_op jit(solution)/shard_map/ppermute | solution.py:535
  (59 shorter events, 22.5 us)
Async XLA Ops:
  2.9 9.2 %collective-permute-start = (bf16[32,2176]{1,0:T(8,128)(2,1)}, bf16[32,2176]{1,0:T(8,128)(2,1)S(1)}, u32[]{:S(2)}, u32[]{:S(2)}) collective-permute-start(bf16[32,2176]{1,0:T(8,128)(2,1)} %get-tuple-element.64), channel_id=1, source_target_pairs={{0,2},{2,0},{4,6},{6,4},{1,3},{3,1},{5,7},{7,5},{8,10},{10,8},{12,... | collective-permute-start | bytes 417800 | tf_op jit(solution)/shard_map/ppermute | solution.py:532
  6.0 15.2 %collective-permute-start.5 = (bf16[1040,128]{1,0:T(8,128)(2,1)}, bf16[1040,128]{1,0:T(8,128)(2,1)S(1)}, u32[]{:S(2)}, u32[]{:S(2)}) collective-permute-start(bf16[1040,128]{1,0:T(8,128)(2,1)} %get-tuple-element.72.refs_4_), channel_id=1, source_target_pairs={{0,24},{8,16},{16,8},{24,0},{1,25},{9,17},{17,9},{25,1},{2,26},{10... | collective-permute-start | bytes 798728 | tf_op jit(solution)/shard_map/ppermute | solution.py:535
  8.5 12.8 %collective-permute-start.4 = (bf16[1040,128]{1,0:T(8,128)(2,1)}, bf16[1040,128]{1,0:T(8,128)(2,1)S(1)}, u32[]{:S(2)}, u32[]{:S(2)}) collective-permute-start(bf16[1040,128]{1,0:T(8,128)(2,1)} %get-tuple-element.72.refs_4_), channel_id=1, source_target_pairs={{0,16},{8,24},{16,0},{24,8},{1,17},{9,25},{17,1},{25,9},{2,18},{10... | collective-permute-start | bytes 798728 | tf_op jit(solution)/shard_map/ppermute | solution.py:535
  9.0 12.3 %collective-permute-start.3 = (bf16[1040,128]{1,0:T(8,128)(2,1)}, bf16[1040,128]{1,0:T(8,128)(2,1)S(1)}, u32[]{:S(2)}, u32[]{:S(2)}) collective-permute-start(bf16[1040,128]{1,0:T(8,128)(2,1)} %get-tuple-element.72.refs_4_), channel_id=1, source_target_pairs={{0,8},{8,0},{16,24},{24,16},{1,9},{9,1},{17,25},{25,17},{2,10},{10... | collective-permute-start | bytes 798728 | tf_op jit(solution)/shard_map/ppermute | solution.py:535
  9.5 11.7 %collective-permute-start.1 = (bf16[32,2176]{1,0:T(8,128)(2,1)}, bf16[32,2176]{1,0:T(8,128)(2,1)S(1)}, u32[]{:S(2)}, u32[]{:S(2)}) collective-permute-start(bf16[32,2176]{1,0:T(8,128)(2,1)} %get-tuple-element.65), channel_id=1, source_target_pairs={{0,4},{2,6},{4,0},{6,2},{1,5},{3,7},{5,1},{7,3},{8,12},{10,14},{12... | collective-permute-start | bytes 417800 | tf_op jit(solution)/shard_map/ppermute | solution.py:532
  12.1 9.2 %collective-permute-start.2 = (bf16[32,2176]{1,0:T(8,128)(2,1)}, bf16[32,2176]{1,0:T(8,128)(2,1)S(1)}, u32[]{:S(2)}, u32[]{:S(2)}) collective-permute-start(bf16[32,2176]{1,0:T(8,128)(2,1)} %get-tuple-element.66), channel_id=1, source_target_pairs={{0,6},{2,4},{4,2},{6,0},{1,7},{3,5},{5,3},{7,1},{8,14},{10,12},{12... | collective-permute-start | bytes 417800 | tf_op jit(solution)/shard_map/ppermute | solution.py:532
  27.9 6.8 %collective-permute-start.12 = (bf16[400,128]{1,0:T(8,128)(2,1)S(1)}, bf16[400,128]{1,0:T(8,128)(2,1)S(1)}, u32[]{:S(2)}, u32[]{:S(2)}) collective-permute-start(bf16[400,128]{1,0:T(8,128)(2,1)S(1)} %get-tuple-element.81.refs_0_.refs_4_), channel_id=1, source_target_pairs={{0,6},{2,4},{4,2},{6,0},{1,7},{3,5},{5,3},{7,1},{8,14},{10,12},{12... | collective-permute-start | bytes 307208 | tf_op jit(solution)/shard_map/ppermute | solution.py:532
  31.2 10.0 %collective-permute-start.11 = (bf16[400,128]{1,0:T(8,128)(2,1)S(1)}, bf16[400,128]{1,0:T(8,128)(2,1)S(1)}, u32[]{:S(2)}, u32[]{:S(2)}) collective-permute-start(bf16[400,128]{1,0:T(8,128)(2,1)S(1)} %get-tuple-element.81.refs_0_.refs_4_), channel_id=1, source_target_pairs={{0,4},{2,6},{4,0},{6,2},{1,5},{3,7},{5,1},{7,3},{8,12},{10,14},{12... | collective-permute-start | bytes 307208 | tf_op jit(solution)/shard_map/ppermute | solution.py:532
  32.5 8.7 %collective-permute-start.10 = (bf16[400,128]{1,0:T(8,128)(2,1)S(1)}, bf16[400,128]{1,0:T(8,128)(2,1)S(1)}, u32[]{:S(2)}, u32[]{:S(2)}) collective-permute-start(bf16[400,128]{1,0:T(8,128)(2,1)S(1)} %get-tuple-element.81.refs_0_.refs_4_), channel_id=1, source_target_pairs={{0,2},{2,0},{4,6},{6,4},{1,3},{3,1},{5,7},{7,5},{8,10},{10,8},{12,... | collective-permute-start | bytes 307208 | tf_op jit(solution)/shard_map/ppermute | solution.py:532
  43.6 7.7 %collective-permute-start.15 = (bf16[256,128]{1,0:T(8,128)(2,1)S(1)}, bf16[256,128]{1,0:T(8,128)(2,1)S(1)}, u32[]{:S(2)}, u32[]{:S(2)}) collective-permute-start(bf16[256,128]{1,0:T(8,128)(2,1)S(1)} %get-tuple-element.83.refs_0_), channel_id=1, source_target_pairs={{0,6},{2,4},{4,2},{6,0},{1,7},{3,5},{5,3},{7,1},{8,14},{10,12},{12... | collective-permute-start | bytes 196616 | tf_op jit(solution)/shard_map/ppermute | solution.py:532
  47.0 8.2 %collective-permute-start.14 = (bf16[256,128]{1,0:T(8,128)(2,1)S(1)}, bf16[256,128]{1,0:T(8,128)(2,1)S(1)}, u32[]{:S(2)}, u32[]{:S(2)}) collective-permute-start(bf16[256,128]{1,0:T(8,128)(2,1)S(1)} %get-tuple-element.83.refs_0_), channel_id=1, source_target_pairs={{0,4},{2,6},{4,0},{6,2},{1,5},{3,7},{5,1},{7,3},{8,12},{10,14},{12... | collective-permute-start | bytes 196616 | tf_op jit(solution)/shard_map/ppermute | solution.py:532
  47.0 8.2 %collective-permute-start.13 = (bf16[256,128]{1,0:T(8,128)(2,1)S(1)}, bf16[256,128]{1,0:T(8,128)(2,1)S(1)}, u32[]{:S(2)}, u32[]{:S(2)}) collective-permute-start(bf16[256,128]{1,0:T(8,128)(2,1)S(1)} %get-tuple-element.83.refs_0_), channel_id=1, source_target_pairs={{0,2},{2,0},{4,6},{6,4},{1,3},{3,1},{5,7},{7,5},{8,10},{10,8},{12,... | collective-permute-start | bytes 196616 | tf_op jit(solution)/shard_map/ppermute | solution.py:532
  48.1 11.8 %collective-permute-start.21 = (bf16[256,128]{1,0:T(8,128)(2,1)S(1)}, bf16[256,128]{1,0:T(8,128)(2,1)S(1)}, u32[]{:S(2)}, u32[]{:S(2)}) collective-permute-start(bf16[256,128]{1,0:T(8,128)(2,1)S(1)} %get-tuple-element.87.refs_4_), channel_id=1, source_target_pairs={{0,6},{2,4},{4,2},{6,0},{1,7},{3,5},{5,3},{7,1},{8,14},{10,12},{12... | collective-permute-start | bytes 196616 | tf_op jit(solution)/shard_map/ppermute | solution.py:532
  51.4 10.7 %collective-permute-start.20 = (bf16[256,128]{1,0:T(8,128)(2,1)S(1)}, bf16[256,128]{1,0:T(8,128)(2,1)S(1)}, u32[]{:S(2)}, u32[]{:S(2)}) collective-permute-start(bf16[256,128]{1,0:T(8,128)(2,1)S(1)} %get-tuple-element.87.refs_4_), channel_id=1, source_target_pairs={{0,4},{2,6},{4,0},{6,2},{1,5},{3,7},{5,1},{7,3},{8,12},{10,14},{12... | collective-permute-start | bytes 196616 | tf_op jit(solution)/shard_map/ppermute | solution.py:532
  51.4 10.7 %collective-permute-start.19 = (bf16[256,128]{1,0:T(8,128)(2,1)S(1)}, bf16[256,128]{1,0:T(8,128)(2,1)S(1)}, u32[]{:S(2)}, u32[]{:S(2)}) collective-permute-start(bf16[256,128]{1,0:T(8,128)(2,1)S(1)} %get-tuple-element.87.refs_4_), channel_id=1, source_target_pairs={{0,2},{2,0},{4,6},{6,4},{1,3},{3,1},{5,7},{7,5},{8,10},{10,8},{12,... | collective-permute-start | bytes 196616 | tf_op jit(solution)/shard_map/ppermute | solution.py:532
  57.6 6.1 %collective-permute-start.18 = (bf16[256,128]{1,0:T(8,128)(2,1)S(1)}, bf16[256,128]{1,0:T(8,128)(2,1)S(1)}, u32[]{:S(2)}, u32[]{:S(2)}) collective-permute-start(bf16[256,128]{1,0:T(8,128)(2,1)S(1)} %get-tuple-element.86.refs_0_), channel_id=1, source_target_pairs={{0,6},{2,4},{4,2},{6,0},{1,7},{3,5},{5,3},{7,1},{8,14},{10,12},{12... | collective-permute-start | bytes 196616 | tf_op jit(solution)/shard_map/ppermute | solution.py:532
  59.8 5.3 %collective-permute-start.17 = (bf16[256,128]{1,0:T(8,128)(2,1)S(1)}, bf16[256,128]{1,0:T(8,128)(2,1)S(1)}, u32[]{:S(2)}, u32[]{:S(2)}) collective-permute-start(bf16[256,128]{1,0:T(8,128)(2,1)S(1)} %get-tuple-element.86.refs_0_), channel_id=1, source_target_pairs={{0,4},{2,6},{4,0},{6,2},{1,5},{3,7},{5,1},{7,3},{8,12},{10,14},{12... | collective-permute-start | bytes 196616 | tf_op jit(solution)/shard_map/ppermute | solution.py:532
  59.8 5.3 %collective-permute-start.16 = (bf16[256,128]{1,0:T(8,128)(2,1)S(1)}, bf16[256,128]{1,0:T(8,128)(2,1)S(1)}, u32[]{:S(2)}, u32[]{:S(2)}) collective-permute-start(bf16[256,128]{1,0:T(8,128)(2,1)S(1)} %get-tuple-element.86.refs_0_), channel_id=1, source_target_pairs={{0,2},{2,0},{4,6},{6,4},{1,3},{3,1},{5,7},{7,5},{8,10},{10,8},{12,... | collective-permute-start | bytes 196616 | tf_op jit(solution)/shard_map/ppermute | solution.py:532
  68.4 6.2 %collective-permute-start.24 = (bf16[272,128]{1,0:T(8,128)(2,1)S(1)}, bf16[272,128]{1,0:T(8,128)(2,1)S(1)}, u32[]{:S(2)}, u32[]{:S(2)}) collective-permute-start(bf16[272,128]{1,0:T(8,128)(2,1)S(1)} %get-tuple-element.90.refs_0_), channel_id=1, source_target_pairs={{0,6},{2,4},{4,2},{6,0},{1,7},{3,5},{5,3},{7,1},{8,14},{10,12},{12... | collective-permute-start | bytes 208904 | tf_op jit(solution)/shard_map/ppermute | solution.py:532
  70.7 6.1 %collective-permute-start.23 = (bf16[272,128]{1,0:T(8,128)(2,1)S(1)}, bf16[272,128]{1,0:T(8,128)(2,1)S(1)}, u32[]{:S(2)}, u32[]{:S(2)}) collective-permute-start(bf16[272,128]{1,0:T(8,128)(2,1)S(1)} %get-tuple-element.90.refs_0_), channel_id=1, source_target_pairs={{0,4},{2,6},{4,0},{6,2},{1,5},{3,7},{5,1},{7,3},{8,12},{10,14},{12... | collective-permute-start | bytes 208904 | tf_op jit(solution)/shard_map/ppermute | solution.py:532
  71.1 5.6 %collective-permute-start.22 = (bf16[272,128]{1,0:T(8,128)(2,1)S(1)}, bf16[272,128]{1,0:T(8,128)(2,1)S(1)}, u32[]{:S(2)}, u32[]{:S(2)}) collective-permute-start(bf16[272,128]{1,0:T(8,128)(2,1)S(1)} %get-tuple-element.90.refs_0_), channel_id=1, source_target_pairs={{0,2},{2,0},{4,6},{6,4},{1,3},{3,1},{5,7},{7,5},{8,10},{10,8},{12,... | collective-permute-start | bytes 208904 | tf_op jit(solution)/shard_map/ppermute | solution.py:532
  78.5 5.8 %collective-permute-start.27 = (bf16[144,128]{1,0:T(8,128)(2,1)S(1)}, bf16[144,128]{1,0:T(8,128)(2,1)S(1)}, u32[]{:S(2)}, u32[]{:S(2)}) collective-permute-start(bf16[144,128]{1,0:T(8,128)(2,1)S(1)} %get-tuple-element.99.refs_0_), channel_id=1, source_target_pairs={{0,6},{2,4},{4,2},{6,0},{1,7},{3,5},{5,3},{7,1},{8,14},{10,12},{12... | collective-permute-start | bytes 110600 | tf_op jit(solution)/shard_map/ppermute | solution.py:532
  80.2 5.0 %collective-permute-start.26 = (bf16[144,128]{1,0:T(8,128)(2,1)S(1)}, bf16[144,128]{1,0:T(8,128)(2,1)S(1)}, u32[]{:S(2)}, u32[]{:S(2)}) collective-permute-start(bf16[144,128]{1,0:T(8,128)(2,1)S(1)} %get-tuple-element.99.refs_0_), channel_id=1, source_target_pairs={{0,4},{2,6},{4,0},{6,2},{1,5},{3,7},{5,1},{7,3},{8,12},{10,14},{12... | collective-permute-start | bytes 110600 | tf_op jit(solution)/shard_map/ppermute | solution.py:532
  80.4 5.3 %collective-permute-start.25 = (bf16[144,128]{1,0:T(8,128)(2,1)S(1)}, bf16[144,128]{1,0:T(8,128)(2,1)S(1)}, u32[]{:S(2)}, u32[]{:S(2)}) collective-permute-start(bf16[144,128]{1,0:T(8,128)(2,1)S(1)} %get-tuple-element.99.refs_0_), channel_id=1, source_target_pairs={{0,2},{2,0},{4,6},{6,4},{1,3},{3,1},{5,7},{7,5},{8,10},{10,8},{12,... | collective-permute-start | bytes 110600 | tf_op jit(solution)/shard_map/ppermute | solution.py:532
  87.4 5.8 %collective-permute-start.30 = (bf16[144,128]{1,0:T(8,128)(2,1)S(1)}, bf16[144,128]{1,0:T(8,128)(2,1)S(1)}, u32[]{:S(2)}, u32[]{:S(2)}) collective-permute-start(bf16[144,128]{1,0:T(8,128)(2,1)S(1)} %get-tuple-element.105.refs_0_), channel_id=1, source_target_pairs={{0,6},{2,4},{4,2},{6,0},{1,7},{3,5},{5,3},{7,1},{8,14},{10,12},{12... | collective-permute-start | bytes 110600 | tf_op jit(solution)/shard_map/ppermute | solution.py:532
  89.8 4.9 %collective-permute-start.29 = (bf16[144,128]{1,0:T(8,128)(2,1)S(1)}, bf16[144,128]{1,0:T(8,128)(2,1)S(1)}, u32[]{:S(2)}, u32[]{:S(2)}) collective-permute-start(bf16[144,128]{1,0:T(8,128)(2,1)S(1)} %get-tuple-element.105.refs_0_), channel_id=1, source_target_pairs={{0,4},{2,6},{4,0},{6,2},{1,5},{3,7},{5,1},{7,3},{8,12},{10,14},{12... | collective-permute-start | bytes 110600 | tf_op jit(solution)/shard_map/ppermute | solution.py:532
  90.1 4.6 %collective-permute-start.28 = (bf16[144,128]{1,0:T(8,128)(2,1)S(1)}, bf16[144,128]{1,0:T(8,128)(2,1)S(1)}, u32[]{:S(2)}, u32[]{:S(2)}) collective-permute-start(bf16[144,128]{1,0:T(8,128)(2,1)S(1)} %get-tuple-element.105.refs_0_), channel_id=1, source_target_pairs={{0,2},{2,0},{4,6},{6,4},{1,3},{3,1},{5,7},{7,5},{8,10},{10,8},{12,... | collective-permute-start | bytes 110600 | tf_op jit(solution)/shard_map/ppermute | solution.py:532
  91.8 4.3 %collective-permute-start.33 = (bf16[272,512]{1,0:T(8,128)(2,1)S(1)}, bf16[272,512]{1,0:T(8,128)(2,1)S(1)}, u32[]{:S(2)}, u32[]{:S(2)}) collective-permute-start(bf16[272,512]{1,0:T(8,128)(2,1)S(1)} %get-tuple-element.117), channel_id=1, source_target_pairs={{0,1},{1,0},{2,3},{3,2},{4,5},{5,4},{6,7},{7,6},{8,9},{9,8},{10,11... | collective-permute-start | bytes 835592 | tf_op jit(solution)/shard_map/ppermute | solution.py:538
  91.8 4.3 %collective-permute-start.34 = (bf16[272,512]{1,0:T(8,128)(2,1)S(1)}, bf16[272,512]{1,0:T(8,128)(2,1)S(1)}, u32[]{:S(2)}, u32[]{:S(2)}) collective-permute-start(bf16[272,512]{1,0:T(8,128)(2,1)S(1)} %get-tuple-element.118), channel_id=1, source_target_pairs={{0,1},{1,0},{2,3},{3,2},{4,5},{5,4},{6,7},{7,6},{8,9},{9,8},{10,11... | collective-permute-start | bytes 835592 | tf_op jit(solution)/shard_map/ppermute | solution.py:538
  98.3 9.6 %collective-permute-start.35 = (bf16[272,512]{1,0:T(8,128)(2,1)S(1)}, bf16[272,512]{1,0:T(8,128)(2,1)S(1)}, u32[]{:S(2)}, u32[]{:S(2)}) collective-permute-start(bf16[272,512]{1,0:T(8,128)(2,1)S(1)} %get-tuple-element.120), channel_id=1, source_target_pairs={{0,8},{8,0},{16,24},{24,16},{1,9},{9,1},{17,25},{25,17},{2,10},{10... | collective-permute-start | bytes 835592 | tf_op jit(solution)/shard_map/ppermute | solution.py:535
  99.4 14.4 %collective-permute-start.36 = (bf16[272,512]{1,0:T(8,128)(2,1)S(1)}, bf16[272,512]{1,0:T(8,128)(2,1)S(1)}, u32[]{:S(2)}, u32[]{:S(2)}) collective-permute-start(bf16[272,512]{1,0:T(8,128)(2,1)S(1)} %get-tuple-element.121), channel_id=1, source_target_pairs={{0,16},{8,24},{16,0},{24,8},{1,17},{9,25},{17,1},{25,9},{2,18},{10... | collective-permute-start | bytes 835592 | tf_op jit(solution)/shard_map/ppermute | solution.py:535
  101.0 12.9 %collective-permute-start.37 = (bf16[272,512]{1,0:T(8,128)(2,1)S(1)}, bf16[272,512]{1,0:T(8,128)(2,1)S(1)}, u32[]{:S(2)}, u32[]{:S(2)}) collective-permute-start(bf16[272,512]{1,0:T(8,128)(2,1)S(1)} %get-tuple-element.122), channel_id=1, source_target_pairs={{0,24},{8,16},{16,8},{24,0},{1,25},{9,17},{17,9},{25,1},{2,26},{10... | collective-permute-start | bytes 835592 | tf_op jit(solution)/shard_map/ppermute | solution.py:535
  (8 other events, 18.0 us)

commit v9 on v8

--- a/solution.py
+++ b/solution.py
@@ -37,8 +37,8 @@
     return [pl.BlockSpec(memory_space=pltpu.VMEM)] * count
 
 
-def layer_spec(shape, layer):
-    return pl.BlockSpec((1,) + shape[1:], lambda *_: (layer, 0, 0, 0))
+def layer_of(weights, layer):
+    return weights.at[pl.ds(layer, 1)]
 
 
 def slice_rows(own):
@@ -80,12 +80,14 @@
         )
     for copy in copies:
         copy.start()
-    for copy in copies:
+    for copy in copies[:5]:
         copy.wait()
     weights[own : 2 * own, :] = second_in[...].astype(F32).T.astype(BF)
     gains = [gain_in[0:1, head * HD : (head + 1) * HD].astype(F32) for head in range(own // HD)]
     gains.append(jnp.zeros((16 - own // HD, HD), F32))
     weights[2 * own :, :] = jnp.concatenate(gains, axis=0).astype(BF)
+    for copy in copies[5:]:
+        copy.wait()
     for micro, (keep, direction, place) in enumerate(picks):
         rows = slice(micro * length, (micro + 1) * length)
         widened = tok[rows, :].astype(F32)
@@ -187,7 +189,7 @@
             normed = (x[span, part].astype(F32) * factor[span] * head_gain(weights, head)).astype(BF)
             scores = dot_nt(normed, normed) * (1.0 / HD)
             raw = jnp.where(allowed, jnp.exp(scores), 0.0)
-            prob = (raw / jnp.sum(raw, axis=1, keepdims=True)).astype(BF)
+            prob = (raw * (1.0 / jnp.sum(raw, axis=1, keepdims=True))).astype(BF)
             probs[block, head] = prob
             mixed[span, part] = dot(prob, normed).astype(BF)
 
@@ -255,8 +257,13 @@
                     parts[distance], weights.at[layer, place], sems.at[layer, place]
                 )
             )
-    for copy in copies:
-        copy.start()
+    for wanted_now in (True, False):
+        for distance in range(sections):
+
+            @pl.when((section == distance) == wanted_now)
+            def _(distance=distance):
+                copies[2 * distance].start()
+                copies[2 * distance + 1].start()
 
     def arrived(layer):
         for place in range(weights.shape[1]):
@@ -264,7 +271,7 @@
 
     arrived(0)
     own = (weights.shape[2] - 16) // 2
-    layers = [weights.at[pl.ds(layer, 1)] for layer in range(sections)]
+    layers = [layer_of(weights, layer) for layer in range(sections)]
     attend(x, mean[:, 0:1], layers[0], mask, probs, mixed)
     send_forward(x, layers[0], mixed, pay)
     arrived(1)
@@ -334,8 +341,9 @@
     pays, sources, refs = refs[:count], refs[count : 2 * count], refs[2 * count :]
     if layer == 1:
         sources, refs = pays, sources + refs
-    x_before, mean_before, mask, weights_before, weights = refs[:5]
-    x, mean, reduced, cross, probs, mixed, pay = refs[5:]
+    x_before, mean_before, mask, weights = refs[:4]
+    x, mean, reduced, cross, probs, mixed, pay = refs[4:]
+    weights_before, weights = layer_of(weights, layer - 1), layer_of(weights, layer)
     receive_forward(
         pays, gram_of(sources, layer - 1, top, x.shape[0]), x_before, mean_before, weights_before,
         width, x, mean, reduced, cross,
@@ -409,10 +417,11 @@
 
 def turn_kernel(count, layer, width, *refs):
     pays, sides, refs = refs[:count], refs[count : 2 * count], refs[2 * count :]
-    (x_before, mean_before, mask, weights_before, weights, cot) = refs[:6]
-    (x, mean, reduced, cross, grads, carried, pay) = refs[6:13]
-    probs, mixed = refs[13:]
+    x_before, mean_before, mask, weights, cot = refs[:5]
+    x, mean, reduced, cross, grads, carried, pay = refs[5:12]
+    probs, mixed = refs[12:]
     rows = x.shape[0]
+    weights_before, weights = layer_of(weights, layer - 1), layer_of(weights, layer)
     receive_forward(
         pays, gram_of(sides, layer - 1, layer, rows), x_before, mean_before, weights_before,
         width, x, mean, reduced, cross,
@@ -432,14 +441,15 @@
     send[...] = grads[1 - core]
 
 
-def back_kernel(count, with_last, to_first, width, *refs):
+def back_kernel(count, with_last, layer, width, *refs):
     pays, refs = refs[:count], refs[count:]
     carried_after, x_after, mean_after, cross_after = refs[:4]
     x, mean, mask, weights = refs[4:8]
     refs = refs[8:]
     weights_before = carried = pay = None
-    if not to_first:
-        weights_before, refs = refs[0], refs[1:]
+    if layer:
+        weights_before = layer_of(weights, layer - 1)
+    weights = layer_of(weights, layer)
     probs, mixed, reduced = refs[:3]
     refs = refs[3:]
     if with_last:
@@ -450,7 +460,7 @@
     if with_last:
         last_keep, last_send = refs[:2]
         refs = refs[2:]
-    if not to_first:
+    if layer:
         carried, pay = refs[:2]
         refs = refs[2:]
     dout, grads = refs
@@ -564,7 +574,6 @@
     def call(kernel, operands, specs, outs, name, **more):
         return pl.pallas_call(
             kernel,
-            grid=(1,),
             in_specs=specs,
             out_specs=vmem_specs(len(outs)),
             out_shape=outs,
@@ -572,9 +581,6 @@
             name=name,
             **more,
         )(*operands)
-
-    def layer_of(index):
-        return layer_spec(weights_shape.shape, index)
 
     x, cot, mask, mean, mine[0] = call(
         functools.partial(arrange_kernel, length, groups),
@@ -612,10 +618,10 @@
     arrived = exchange(side)
     for layer in range(1, top):
         operands = (*pays, *((), first_pays, arrived)[min(layer, 3) - 1])
-        specs = vmem_specs(len(operands) + 3) + [layer_of(layer - 1), layer_of(layer)]
+        specs = vmem_specs(len(operands) + 4)
         x, mean, reduced, cross, probs, mixed, pay = call(
             functools.partial(middle_kernel, groups, layer, top, float(width)),
-            (*operands, xs[-1], means[-1], mask, weights, weights),
+            (*operands, xs[-1], means[-1], mask, weights),
             specs,
             [
                 wide_shape,
@@ -639,8 +645,8 @@
     back_rows = rows + 16 * blocks
     x, mean, reduced, cross, turn_grads, carried, pay = call(
         functools.partial(turn_kernel, groups, top, float(width)),
-        (*pays, *arrived, xs[-1], means[-1], mask, weights, weights, cot),
-        vmem_specs(2 * groups + 3) + [layer_of(top - 1), layer_of(top)] + vmem_specs(1),
+        (*pays, *arrived, xs[-1], means[-1], mask, weights, cot),
+        vmem_specs(2 * groups + 5),
         [
             wide_shape,
             mean_shape,
@@ -670,23 +676,17 @@
             *pays, carried, xs[layer + 1], means[layer + 1], crosses[layer + 1],
             xs[layer], means[layer], mask, weights,
         )
-        specs = vmem_specs(len(pays) + 7) + [layer_of(layer)]
-        if not to_first:
-            operands += (weights,)
-            specs += [layer_of(layer - 1)]
         operands += (all_probs[layer], all_mixed[layer], reduceds[layer])
-        specs += vmem_specs(3)
         outs = [half_shape] * 2
         if with_last:
             operands += (cot, turn_grads)
-            specs += vmem_specs(2)
             outs += [half_shape] * 2
         if not to_first:
             outs += [wide_shape, shaped((back_rows, HD))]
         result = call(
-            functools.partial(back_kernel, groups, with_last, to_first, float(width)),
+            functools.partial(back_kernel, groups, with_last, layer, float(width)),
             operands,
-            specs,
+            vmem_specs(len(operands)),
             outs,
             "backward",
             scratch_shapes=[pltpu.VMEM(wide_shape.shape, BF), pltpu.VMEM(grads_shape, BF)],

time: 115 us -> 115 us (level)
  no operation moved by 1% of the time
where the time goes in v9:
time: 115 us
  starting transfers between devices  47.4 us (41%)
  waiting for transfers between devices  44.4 us (39%)
  Pallas kernels  20.4 us (18%)
  local copies, waits for them, and re-layouts  1.86 us (2%)
    ppermute x24, starting transfers between devices, shifted(): return lax.ppermute(value, 'z', [(i, i ^ shift) for i in range(groups)])  38.7 us
    ppermute x24, waiting for transfers between devices, shifted(): return lax.ppermute(value, 'z', [(i, i ^ shift) for i in range(groups)])  30.9 us
    pallas_call x10, Pallas kernels, call(): pl.pallas_call(kernel, in_specs=specs, out_specs=vmem_specs(len(outs)), o...  18.1 us
    ppermute x6, waiting for transfers between devices, across(): lax.ppermute(value, 'pipe', [(i, i ^ distance) for i in range(sections)])  12 us
    ppermute x6, starting transfers between devices, across(): lax.ppermute(value, 'pipe', [(i, i ^ distance) for i in range(sections)])  7.04 us
  transfers between devices with their start and end apart: 38, of which 16 were waited for; matrix products, arithmetic and copies ran while one was open for 0% of the time, Pallas kernels for 4%

profile of v9, /device:TPU:0, one launch (start us, length us, event | category | flops | bytes accessed | tf_op | source)
XLA Modules:
  0.0 114.8 jit_solution(11739422068082955563)
XLA Ops:
  0.6 2.3 %pack.1 = (bf16[32,2176]{1,0:T(8,128)(2,1)}, bf16[32,2176]{1,0:T(8,128)(2,1)}, bf16[32,2176]{1,0:T(8,128)(2,1)}, bf16[32,2176]{1,0:T(8,128)(2,1)}, bf16[1040,128]{1,0:T(8,128)(2,1)}) custom-call(bf16[2,2,32,4096]{3,2,1,0:T(8,128)(2,1)} %refs_0_.1, bf16[2,2,32,4096]{3,2,1,0:T(8,128)(2,1)} %refs_1_.1, s32[2,2,4]{2,1,0:T(2,128)} %refs_2_.1, s32[2,2]{1,0:T(2,128)} %refs_3_.1, ...), custom_call_target="tpu_custom_call" | custom-call | tf_op jit(solution)/shard_map/pack/pallas_call | solution.py:124
  2.9 3.1 %collective-permute-start = (bf16[32,2176]{1,0:T(8,128)(2,1)}, bf16[32,2176]{1,0:T(8,128)(2,1)S(1)}, u32[]{:S(2)}, u32[]{:S(2)}) collective-permute-start(bf16[32,2176]{1,0:T(8,128)(2,1)} %get-tuple-element.64), channel_id=1, source_target_pairs={{0,2},{2,0},{4,6},{6,4},{1,3},{3,1},{5,7},{7,5},{8,10},{10,8},{12,... | collective-permute-start | bytes 417800 | tf_op jit(solution)/shard_map/ppermute | solution.py:542
  6.0 2.4 %collective-permute-start.5 = (bf16[1040,128]{1,0:T(8,128)(2,1)}, bf16[1040,128]{1,0:T(8,128)(2,1)S(1)}, u32[]{:S(2)}, u32[]{:S(2)}) collective-permute-start(bf16[1040,128]{1,0:T(8,128)(2,1)} %get-tuple-element.72.refs_4_), channel_id=1, source_target_pairs={{0,24},{8,16},{16,8},{24,0},{1,25},{9,17},{17,9},{25,1},{2,26},{10... | collective-permute-start | bytes 798728 | tf_op jit(solution)/shard_map/ppermute | solution.py:545
  9.5 2.6 %collective-permute-start.1 = (bf16[32,2176]{1,0:T(8,128)(2,1)}, bf16[32,2176]{1,0:T(8,128)(2,1)S(1)}, u32[]{:S(2)}, u32[]{:S(2)}) collective-permute-start(bf16[32,2176]{1,0:T(8,128)(2,1)} %get-tuple-element.65), channel_id=1, source_target_pairs={{0,4},{2,6},{4,0},{6,2},{1,5},{3,7},{5,1},{7,3},{8,12},{10,14},{12... | collective-permute-start | bytes 417800 | tf_op jit(solution)/shard_map/ppermute | solution.py:542
  12.1 1.6 %collective-permute-start.2 = (bf16[32,2176]{1,0:T(8,128)(2,1)}, bf16[32,2176]{1,0:T(8,128)(2,1)S(1)}, u32[]{:S(2)}, u32[]{:S(2)}) collective-permute-start(bf16[32,2176]{1,0:T(8,128)(2,1)} %get-tuple-element.66), channel_id=1, source_target_pairs={{0,6},{2,4},{4,2},{6,0},{1,7},{3,5},{5,3},{7,1},{8,14},{10,12},{12... | collective-permute-start | bytes 417800 | tf_op jit(solution)/shard_map/ppermute | solution.py:542
  13.7 7.6 %collective-permute-done.1.refs_2_ = bf16[32,2176]{1,0:T(8,128)(2,1)S(1)} collective-permute-done((bf16[32,2176]{1,0:T(8,128)(2,1)}, bf16[32,2176]{1,0:T(8,128)(2,1)S(1)}, u32[]{:S(2)}, u32[]{:S(2)}) %collective-permute-start.1) | collective-permute-done | bytes 139296 | tf_op jit(solution)/shard_map/ppermute | solution.py:542
  24.5 3.4 %forward_first.1 = (bf16[1,8,128,128]{3,2,1,0:T(8,128)(2,1)S(1)}, bf16[128,1024]{1,0:T(8,128)(2,1)S(1)}, bf16[400,128]{1,0:T(8,128)(2,1)S(1)}, bf16[256,128]{1,0:T(8,128)(2,1)S(1)}, bf16[4,2,1040,128]{3,2,1,0:T(8,128)(2,1)S(1)}) custom-call(bf16[1040,128]{1,0:T(8,128)(2,1)S(1)} %get-tuple-element.73.refs_0_, ...), custom_call_target="tpu_custom_call" | custom-call | tf_op jit(solution)/shard_map/forward_first/pallas_call | solution.py:575
  27.9 3.3 %collective-permute-start.12 = (bf16[400,128]{1,0:T(8,128)(2,1)S(1)}, bf16[400,128]{1,0:T(8,128)(2,1)S(1)}, u32[]{:S(2)}, u32[]{:S(2)}) collective-permute-start(bf16[400,128]{1,0:T(8,128)(2,1)S(1)} %get-tuple-element.81.refs_0_.refs_4_), channel_id=1, source_target_pairs={{0,6},{2,4},{4,2},{6,0},{1,7},{3,5},{5,3},{7,1},{8,14},{10,12},{12... | collective-permute-start | bytes 307208 | tf_op jit(solution)/shard_map/ppermute | solution.py:542
  32.7 2.0 %collective-permute-done.12.refs_3_.refs_7_ = bf16[400,128]{1,0:T(8,128)(2,1)S(1)} collective-permute-done((bf16[400,128]{1,0:T(8,128)(2,1)S(1)}, bf16[400,128]{1,0:T(8,128)(2,1)S(1)}, u32[]{:S(2)}, u32[]{:S(2)}) %collective-permute-start.12) | collective-permute-done | bytes 102432 | tf_op jit(solution)/shard_map/ppermute | solution.py:542
  34.7 6.5 %collective-permute-done.11.refs_2_.refs_6_ = bf16[400,128]{1,0:T(8,128)(2,1)S(1)} collective-permute-done((bf16[400,128]{1,0:T(8,128)(2,1)S(1)}, bf16[400,128]{1,0:T(8,128)(2,1)S(1)}, u32[]{:S(2)}, u32[]{:S(2)}) %collective-permute-start.11) | collective-permute-done | bytes 102432 | tf_op jit(solution)/shard_map/ppermute | solution.py:542
  41.2 2.4 %forward_middle.2 = (bf16[128,1024]{1,0:T(8,128)(2,1)S(1)}, f32[128,128]{1,0:T(8,128)S(1)}, bf16[128,128]{1,0:T(8,128)(2,1)S(1)}, f32[128,128]{1,0:T(8,128)S(1)}...) custom-call(bf16[400,128]{1,0:T(8,128)(2,1)S(1)} %get-tuple-element.81.refs_0_.re, ...), custom_call_target="tpu_custom_call" | custom-call | tf_op jit(solution)/shard_map/forward_middle/pallas_call | solution.py:575
  43.6 3.3 %collective-permute-start.15 = (bf16[256,128]{1,0:T(8,128)(2,1)S(1)}, bf16[256,128]{1,0:T(8,128)(2,1)S(1)}, u32[]{:S(2)}, u32[]{:S(2)}) collective-permute-start(bf16[256,128]{1,0:T(8,128)(2,1)S(1)} %get-tuple-element.83.refs_0_), channel_id=1, source_target_pairs={{0,6},{2,4},{4,2},{6,0},{1,7},{3,5},{5,3},{7,1},{8,14},{10,12},{12... | collective-permute-start | bytes 196616 | tf_op jit(solution)/shard_map/ppermute | solution.py:542
  48.1 3.3 %collective-permute-start.21 = (bf16[256,128]{1,0:T(8,128)(2,1)S(1)}, bf16[256,128]{1,0:T(8,128)(2,1)S(1)}, u32[]{:S(2)}, u32[]{:S(2)}) collective-permute-start(bf16[256,128]{1,0:T(8,128)(2,1)S(1)} %get-tuple-element.87.refs_4_), channel_id=1, source_target_pairs={{0,6},{2,4},{4,2},{6,0},{1,7},{3,5},{5,3},{7,1},{8,14},{10,12},{12... | collective-permute-start | bytes 196616 | tf_op jit(solution)/shard_map/ppermute | solution.py:542
  52.5 2.7 %collective-permute-done.14.refs_2_ = bf16[256,128]{1,0:T(8,128)(2,1)S(1)} collective-permute-done((bf16[256,128]{1,0:T(8,128)(2,1)S(1)}, bf16[256,128]{1,0:T(8,128)(2,1)S(1)}, u32[]{:S(2)}, u32[]{:S(2)}) %collective-permute-start.14) | collective-permute-done | bytes 65568 | tf_op jit(solution)/shard_map/ppermute | solution.py:542
  55.2 2.4 %forward_middle.3 = (bf16[128,1024]{1,0:T(8,128)(2,1)S(1)}, f32[128,128]{1,0:T(8,128)S(1)}, bf16[128,128]{1,0:T(8,128)(2,1)S(1)}, f32[128,128]{1,0:T(8,128)S(1)}...) custom-call(bf16[256,128]{1,0:T(8,128)(2,1)S(1)} %get-tuple-element.83.refs_0_, ...), custom_call_target="tpu_custom_call" | custom-call | tf_op jit(solution)/shard_map/forward_middle/pallas_call | solution.py:575
  57.6 2.3 %collective-permute-start.18 = (bf16[256,128]{1,0:T(8,128)(2,1)S(1)}, bf16[256,128]{1,0:T(8,128)(2,1)S(1)}, u32[]{:S(2)}, u32[]{:S(2)}) collective-permute-start(bf16[256,128]{1,0:T(8,128)(2,1)S(1)} %get-tuple-element.86.refs_0_), channel_id=1, source_target_pairs={{0,6},{2,4},{4,2},{6,0},{1,7},{3,5},{5,3},{7,1},{8,14},{10,12},{12... | collective-permute-start | bytes 196616 | tf_op jit(solution)/shard_map/ppermute | solution.py:542
  59.9 2.2 %collective-permute-start.16 = (bf16[256,128]{1,0:T(8,128)(2,1)S(1)}, bf16[256,128]{1,0:T(8,128)(2,1)S(1)}, u32[]{:S(2)}, u32[]{:S(2)}) collective-permute-start(bf16[256,128]{1,0:T(8,128)(2,1)S(1)} %get-tuple-element.86.refs_0_), channel_id=1, source_target_pairs={{0,2},{2,0},{4,6},{6,4},{1,3},{3,1},{5,7},{7,5},{8,10},{10,8},{12,... | collective-permute-start | bytes 196616 | tf_op jit(solution)/shard_map/ppermute | solution.py:542
  62.1 1.7 %collective-permute-done.18.refs_3_ = bf16[256,128]{1,0:T(8,128)(2,1)S(1)} collective-permute-done((bf16[256,128]{1,0:T(8,128)(2,1)S(1)}, bf16[256,128]{1,0:T(8,128)(2,1)S(1)}, u32[]{:S(2)}, u32[]{:S(2)}) %collective-permute-start.18) | collective-permute-done | bytes 65568 | tf_op jit(solution)/shard_map/ppermute | solution.py:542
  65.1 3.3 %turn.1 = (bf16[128,1024]{1,0:T(8,128)(2,1)S(1)}, f32[128,128]{1,0:T(8,128)S(1)}, bf16[128,128]{1,0:T(8,128)(2,1)S(1)}, f32[128,128]{1,0:T(8,128)S(1)}, bf16[2,2...) custom-call(bf16[256,128]{1,0:T(8,128)(2,1)S(1)} %get-tuple-element.86.refs_0_, ...), custom_call_target="tpu_custom_call" | custom-call | tf_op jit(solution)/shard_map/turn/pallas_call | solution.py:575
  68.4 2.3 %collective-permute-start.24 = (bf16[272,128]{1,0:T(8,128)(2,1)S(1)}, bf16[272,128]{1,0:T(8,128)(2,1)S(1)}, u32[]{:S(2)}, u32[]{:S(2)}) collective-permute-start(bf16[272,128]{1,0:T(8,128)(2,1)S(1)} %get-tuple-element.90.refs_0_), channel_id=1, source_target_pairs={{0,6},{2,4},{4,2},{6,0},{1,7},{3,5},{5,3},{7,1},{8,14},{10,12},{12... | collective-permute-start | bytes 208904 | tf_op jit(solution)/shard_map/ppermute | solution.py:542
  71.2 1.7 %collective-permute-start.22 = (bf16[272,128]{1,0:T(8,128)(2,1)S(1)}, bf16[272,128]{1,0:T(8,128)(2,1)S(1)}, u32[]{:S(2)}, u32[]{:S(2)}) collective-permute-start(bf16[272,128]{1,0:T(8,128)(2,1)S(1)} %get-tuple-element.90.refs_0_), channel_id=1, source_target_pairs={{0,2},{2,0},{4,6},{6,4},{1,3},{3,1},{5,7},{7,5},{8,10},{10,8},{12,... | collective-permute-start | bytes 208904 | tf_op jit(solution)/shard_map/ppermute | solution.py:542
  72.9 1.7 %collective-permute-done.24.refs_3_ = bf16[272,128]{1,0:T(8,128)(2,1)S(1)} collective-permute-done((bf16[272,128]{1,0:T(8,128)(2,1)S(1)}, bf16[272,128]{1,0:T(8,128)(2,1)S(1)}, u32[]{:S(2)}, u32[]{:S(2)}) %collective-permute-start.24) | collective-permute-done | bytes 69664 | tf_op jit(solution)/shard_map/ppermute | solution.py:542
  74.6 2.2 %collective-permute-done.23.refs_2_ = bf16[272,128]{1,0:T(8,128)(2,1)S(1)} collective-permute-done((bf16[272,128]{1,0:T(8,128)(2,1)S(1)}, bf16[272,128]{1,0:T(8,128)(2,1)S(1)}, u32[]{:S(2)}, u32[]{:S(2)}) %collective-permute-start.23) | collective-permute-done | bytes 69664 | tf_op jit(solution)/shard_map/ppermute | solution.py:542
  76.8 1.7 %backward.3 = (bf16[272,512]{1,0:T(8,128)(2,1)S(1)}, bf16[272,512]{1,0:T(8,128)(2,1)S(1)}, bf16[272,512]{1,0:T(8,128)(2,1)S(1)}, bf16[272,512]{1,0:T(8,128)(2,1)...) custom-call(bf16[272,128]{1,0:T(8,128)(2,1)S(1)} %get-tuple-element.90.refs_0_, ...), custom_call_target="tpu_custom_call" | custom-call | tf_op jit(solution)/shard_map/backward/pallas_call | solution.py:575
  78.5 1.7 %collective-permute-start.27 = (bf16[144,128]{1,0:T(8,128)(2,1)S(1)}, bf16[144,128]{1,0:T(8,128)(2,1)S(1)}, u32[]{:S(2)}, u32[]{:S(2)}) collective-permute-start(bf16[144,128]{1,0:T(8,128)(2,1)S(1)} %get-tuple-element.99.refs_0_), channel_id=1, source_target_pairs={{0,6},{2,4},{4,2},{6,0},{1,7},{3,5},{5,3},{7,1},{8,14},{10,12},{12... | collective-permute-start | bytes 110600 | tf_op jit(solution)/shard_map/ppermute | solution.py:542
  80.4 2.5 %collective-permute-start.25 = (bf16[144,128]{1,0:T(8,128)(2,1)S(1)}, bf16[144,128]{1,0:T(8,128)(2,1)S(1)}, u32[]{:S(2)}, u32[]{:S(2)}) collective-permute-start(bf16[144,128]{1,0:T(8,128)(2,1)S(1)} %get-tuple-element.99.refs_0_), channel_id=1, source_target_pairs={{0,2},{2,0},{4,6},{6,4},{1,3},{3,1},{5,7},{7,5},{8,10},{10,8},{12,... | collective-permute-start | bytes 110600 | tf_op jit(solution)/shard_map/ppermute | solution.py:542
  85.7 1.7 %backward.4 = (bf16[272,512]{1,0:T(8,128)(2,1)S(1)}, bf16[272,512]{1,0:T(8,128)(2,1)S(1)}, bf16[128,1024]{1,0:T(8,128)(2,1)S(1)}, bf16[144,128]{1,0:T(8,128)(2,1)S(1)}) custom-call(bf16[144,128]{1,0:T(8,128)(2,1)S(1)} %get-tuple-element.99.refs_0_, bf16[144,128]{1,0:T(8,128)(2,1)S(1)} %collective-permute-done.25.refs_1_, ...), custom_call_target="tpu_custom_call" | custom-call | tf_op jit(solution)/shard_map/backward/pallas_call | solution.py:575
  87.4 2.4 %collective-permute-start.30 = (bf16[144,128]{1,0:T(8,128)(2,1)S(1)}, bf16[144,128]{1,0:T(8,128)(2,1)S(1)}, u32[]{:S(2)}, u32[]{:S(2)}) collective-permute-start(bf16[144,128]{1,0:T(8,128)(2,1)S(1)} %get-tuple-element.105.refs_0_), channel_id=1, source_target_pairs={{0,6},{2,4},{4,2},{6,0},{1,7},{3,5},{5,3},{7,1},{8,14},{10,12},{12... | collective-permute-start | bytes 110600 | tf_op jit(solution)/shard_map/ppermute | solution.py:542
  90.1 1.8 %collective-permute-start.28 = (bf16[144,128]{1,0:T(8,128)(2,1)S(1)}, bf16[144,128]{1,0:T(8,128)(2,1)S(1)}, u32[]{:S(2)}, u32[]{:S(2)}) collective-permute-start(bf16[144,128]{1,0:T(8,128)(2,1)S(1)} %get-tuple-element.105.refs_0_), channel_id=1, source_target_pairs={{0,2},{2,0},{4,6},{6,4},{1,3},{3,1},{5,7},{7,5},{8,10},{10,8},{12,... | collective-permute-start | bytes 110600 | tf_op jit(solution)/shard_map/ppermute | solution.py:542
  96.2 1.5 %collective-permute-done.31.refs_4_ = bf16[272,512]{1,0:T(8,128)(2,1)S(1)} collective-permute-done((bf16[272,512]{1,0:T(8,128)(2,1)S(1)}, bf16[272,512]{1,0:T(8,128)(2,1)S(1)}, u32[]{:S(2)}, u32[]{:S(2)}) %collective-permute-start.31) | collective-permute-done | bytes 278560 | tf_op jit(solution)/shard_map/ppermute | solution.py:548
  101.9 6.0 %collective-permute-done.35.refs_1_ = bf16[272,512]{1,0:T(8,128)(2,1)S(1)} collective-permute-done((bf16[272,512]{1,0:T(8,128)(2,1)S(1)}, bf16[272,512]{1,0:T(8,128)(2,1)S(1)}, u32[]{:S(2)}, u32[]{:S(2)}) %collective-permute-start.35) | collective-permute-done | bytes 278560 | tf_op jit(solution)/shard_map/ppermute | solution.py:545
  107.9 6.0 %collective-permute-done.36.refs_2_ = bf16[272,512]{1,0:T(8,128)(2,1)S(1)} collective-permute-done((bf16[272,512]{1,0:T(8,128)(2,1)S(1)}, bf16[272,512]{1,0:T(8,128)(2,1)S(1)}, u32[]{:S(2)}, u32[]{:S(2)}) %collective-permute-start.36) | collective-permute-done | bytes 278560 | tf_op jit(solution)/shard_map/ppermute | solution.py:545
  (59 shorter events, 22.5 us)
Async XLA Ops:
  2.9 9.2 %collective-permute-start = (bf16[32,2176]{1,0:T(8,128)(2,1)}, bf16[32,2176]{1,0:T(8,128)(2,1)S(1)}, u32[]{:S(2)}, u32[]{:S(2)}) collective-permute-start(bf16[32,2176]{1,0:T(8,128)(2,1)} %get-tuple-element.64), channel_id=1, source_target_pairs={{0,2},{2,0},{4,6},{6,4},{1,3},{3,1},{5,7},{7,5},{8,10},{10,8},{12,... | collective-permute-start | bytes 417800 | tf_op jit(solution)/shard_map/ppermute | solution.py:542
  6.0 15.2 %collective-permute-start.5 = (bf16[1040,128]{1,0:T(8,128)(2,1)}, bf16[1040,128]{1,0:T(8,128)(2,1)S(1)}, u32[]{:S(2)}, u32[]{:S(2)}) collective-permute-start(bf16[1040,128]{1,0:T(8,128)(2,1)} %get-tuple-element.72.refs_4_), channel_id=1, source_target_pairs={{0,24},{8,16},{16,8},{24,0},{1,25},{9,17},{17,9},{25,1},{2,26},{10... | collective-permute-start | bytes 798728 | tf_op jit(solution)/shard_map/ppermute | solution.py:545
  8.5 12.8 %collective-permute-start.4 = (bf16[1040,128]{1,0:T(8,128)(2,1)}, bf16[1040,128]{1,0:T(8,128)(2,1)S(1)}, u32[]{:S(2)}, u32[]{:S(2)}) collective-permute-start(bf16[1040,128]{1,0:T(8,128)(2,1)} %get-tuple-element.72.refs_4_), channel_id=1, source_target_pairs={{0,16},{8,24},{16,0},{24,8},{1,17},{9,25},{17,1},{25,9},{2,18},{10... | collective-permute-start | bytes 798728 | tf_op jit(solution)/shard_map/ppermute | solution.py:545
  9.0 12.3 %collective-permute-start.3 = (bf16[1040,128]{1,0:T(8,128)(2,1)}, bf16[1040,128]{1,0:T(8,128)(2,1)S(1)}, u32[]{:S(2)}, u32[]{:S(2)}) collective-permute-start(bf16[1040,128]{1,0:T(8,128)(2,1)} %get-tuple-element.72.refs_4_), channel_id=1, source_target_pairs={{0,8},{8,0},{16,24},{24,16},{1,9},{9,1},{17,25},{25,17},{2,10},{10... | collective-permute-start | bytes 798728 | tf_op jit(solution)/shard_map/ppermute | solution.py:545
  9.5 11.7 %collective-permute-start.1 = (bf16[32,2176]{1,0:T(8,128)(2,1)}, bf16[32,2176]{1,0:T(8,128)(2,1)S(1)}, u32[]{:S(2)}, u32[]{:S(2)}) collective-permute-start(bf16[32,2176]{1,0:T(8,128)(2,1)} %get-tuple-element.65), channel_id=1, source_target_pairs={{0,4},{2,6},{4,0},{6,2},{1,5},{3,7},{5,1},{7,3},{8,12},{10,14},{12... | collective-permute-start | bytes 417800 | tf_op jit(solution)/shard_map/ppermute | solution.py:542
  12.1 9.2 %collective-permute-start.2 = (bf16[32,2176]{1,0:T(8,128)(2,1)}, bf16[32,2176]{1,0:T(8,128)(2,1)S(1)}, u32[]{:S(2)}, u32[]{:S(2)}) collective-permute-start(bf16[32,2176]{1,0:T(8,128)(2,1)} %get-tuple-element.66), channel_id=1, source_target_pairs={{0,6},{2,4},{4,2},{6,0},{1,7},{3,5},{5,3},{7,1},{8,14},{10,12},{12... | collective-permute-start | bytes 417800 | tf_op jit(solution)/shard_map/ppermute | solution.py:542
  27.9 6.8 %collective-permute-start.12 = (bf16[400,128]{1,0:T(8,128)(2,1)S(1)}, bf16[400,128]{1,0:T(8,128)(2,1)S(1)}, u32[]{:S(2)}, u32[]{:S(2)}) collective-permute-start(bf16[400,128]{1,0:T(8,128)(2,1)S(1)} %get-tuple-element.81.refs_0_.refs_4_), channel_id=1, source_target_pairs={{0,6},{2,4},{4,2},{6,0},{1,7},{3,5},{5,3},{7,1},{8,14},{10,12},{12... | collective-permute-start | bytes 307208 | tf_op jit(solution)/shard_map/ppermute | solution.py:542
  31.2 10.0 %collective-permute-start.11 = (bf16[400,128]{1,0:T(8,128)(2,1)S(1)}, bf16[400,128]{1,0:T(8,128)(2,1)S(1)}, u32[]{:S(2)}, u32[]{:S(2)}) collective-permute-start(bf16[400,128]{1,0:T(8,128)(2,1)S(1)} %get-tuple-element.81.refs_0_.refs_4_), channel_id=1, source_target_pairs={{0,4},{2,6},{4,0},{6,2},{1,5},{3,7},{5,1},{7,3},{8,12},{10,14},{12... | collective-permute-start | bytes 307208 | tf_op jit(solution)/shard_map/ppermute | solution.py:542
  32.6 8.7 %collective-permute-start.10 = (bf16[400,128]{1,0:T(8,128)(2,1)S(1)}, bf16[400,128]{1,0:T(8,128)(2,1)S(1)}, u32[]{:S(2)}, u32[]{:S(2)}) collective-permute-start(bf16[400,128]{1,0:T(8,128)(2,1)S(1)} %get-tuple-element.81.refs_0_.refs_4_), channel_id=1, source_target_pairs={{0,2},{2,0},{4,6},{6,4},{1,3},{3,1},{5,7},{7,5},{8,10},{10,8},{12,... | collective-permute-start | bytes 307208 | tf_op jit(solution)/shard_map/ppermute | solution.py:542
  43.6 7.7 %collective-permute-start.15 = (bf16[256,128]{1,0:T(8,128)(2,1)S(1)}, bf16[256,128]{1,0:T(8,128)(2,1)S(1)}, u32[]{:S(2)}, u32[]{:S(2)}) collective-permute-start(bf16[256,128]{1,0:T(8,128)(2,1)S(1)} %get-tuple-element.83.refs_0_), channel_id=1, source_target_pairs={{0,6},{2,4},{4,2},{6,0},{1,7},{3,5},{5,3},{7,1},{8,14},{10,12},{12... | collective-permute-start | bytes 196616 | tf_op jit(solution)/shard_map/ppermute | solution.py:542
  47.0 8.2 %collective-permute-start.14 = (bf16[256,128]{1,0:T(8,128)(2,1)S(1)}, bf16[256,128]{1,0:T(8,128)(2,1)S(1)}, u32[]{:S(2)}, u32[]{:S(2)}) collective-permute-start(bf16[256,128]{1,0:T(8,128)(2,1)S(1)} %get-tuple-element.83.refs_0_), channel_id=1, source_target_pairs={{0,4},{2,6},{4,0},{6,2},{1,5},{3,7},{5,1},{7,3},{8,12},{10,14},{12... | collective-permute-start | bytes 196616 | tf_op jit(solution)/shard_map/ppermute | solution.py:542
  47.0 8.2 %collective-permute-start.13 = (bf16[256,128]{1,0:T(8,128)(2,1)S(1)}, bf16[256,128]{1,0:T(8,128)(2,1)S(1)}, u32[]{:S(2)}, u32[]{:S(2)}) collective-permute-start(bf16[256,128]{1,0:T(8,128)(2,1)S(1)} %get-tuple-element.83.refs_0_), channel_id=1, source_target_pairs={{0,2},{2,0},{4,6},{6,4},{1,3},{3,1},{5,7},{7,5},{8,10},{10,8},{12,... | collective-permute-start | bytes 196616 | tf_op jit(solution)/shard_map/ppermute | solution.py:542
  48.1 11.8 %collective-permute-start.21 = (bf16[256,128]{1,0:T(8,128)(2,1)S(1)}, bf16[256,128]{1,0:T(8,128)(2,1)S(1)}, u32[]{:S(2)}, u32[]{:S(2)}) collective-permute-start(bf16[256,128]{1,0:T(8,128)(2,1)S(1)} %get-tuple-element.87.refs_4_), channel_id=1, source_target_pairs={{0,6},{2,4},{4,2},{6,0},{1,7},{3,5},{5,3},{7,1},{8,14},{10,12},{12... | collective-permute-start | bytes 196616 | tf_op jit(solution)/shard_map/ppermute | solution.py:542
  51.4 10.7 %collective-permute-start.20 = (bf16[256,128]{1,0:T(8,128)(2,1)S(1)}, bf16[256,128]{1,0:T(8,128)(2,1)S(1)}, u32[]{:S(2)}, u32[]{:S(2)}) collective-permute-start(bf16[256,128]{1,0:T(8,128)(2,1)S(1)} %get-tuple-element.87.refs_4_), channel_id=1, source_target_pairs={{0,4},{2,6},{4,0},{6,2},{1,5},{3,7},{5,1},{7,3},{8,12},{10,14},{12... | collective-permute-start | bytes 196616 | tf_op jit(solution)/shard_map/ppermute | solution.py:542
  51.4 10.7 %collective-permute-start.19 = (bf16[256,128]{1,0:T(8,128)(2,1)S(1)}, bf16[256,128]{1,0:T(8,128)(2,1)S(1)}, u32[]{:S(2)}, u32[]{:S(2)}) collective-permute-start(bf16[256,128]{1,0:T(8,128)(2,1)S(1)} %get-tuple-element.87.refs_4_), channel_id=1, source_target_pairs={{0,2},{2,0},{4,6},{6,4},{1,3},{3,1},{5,7},{7,5},{8,10},{10,8},{12,... | collective-permute-start | bytes 196616 | tf_op jit(solution)/shard_map/ppermute | solution.py:542
  57.6 6.1 %collective-permute-start.18 = (bf16[256,128]{1,0:T(8,128)(2,1)S(1)}, bf16[256,128]{1,0:T(8,128)(2,1)S(1)}, u32[]{:S(2)}, u32[]{:S(2)}) collective-permute-start(bf16[256,128]{1,0:T(8,128)(2,1)S(1)} %get-tuple-element.86.refs_0_), channel_id=1, source_target_pairs={{0,6},{2,4},{4,2},{6,0},{1,7},{3,5},{5,3},{7,1},{8,14},{10,12},{12... | collective-permute-start | bytes 196616 | tf_op jit(solution)/shard_map/ppermute | solution.py:542
  59.9 5.3 %collective-permute-start.17 = (bf16[256,128]{1,0:T(8,128)(2,1)S(1)}, bf16[256,128]{1,0:T(8,128)(2,1)S(1)}, u32[]{:S(2)}, u32[]{:S(2)}) collective-permute-start(bf16[256,128]{1,0:T(8,128)(2,1)S(1)} %get-tuple-element.86.refs_0_), channel_id=1, source_target_pairs={{0,4},{2,6},{4,0},{6,2},{1,5},{3,7},{5,1},{7,3},{8,12},{10,14},{12... | collective-permute-start | bytes 196616 | tf_op jit(solution)/shard_map/ppermute | solution.py:542
  59.9 5.3 %collective-permute-start.16 = (bf16[256,128]{1,0:T(8,128)(2,1)S(1)}, bf16[256,128]{1,0:T(8,128)(2,1)S(1)}, u32[]{:S(2)}, u32[]{:S(2)}) collective-permute-start(bf16[256,128]{1,0:T(8,128)(2,1)S(1)} %get-tuple-element.86.refs_0_), channel_id=1, source_target_pairs={{0,2},{2,0},{4,6},{6,4},{1,3},{3,1},{5,7},{7,5},{8,10},{10,8},{12,... | collective-permute-start | bytes 196616 | tf_op jit(solution)/shard_map/ppermute | solution.py:542
  68.4 6.2 %collective-permute-start.24 = (bf16[272,128]{1,0:T(8,128)(2,1)S(1)}, bf16[272,128]{1,0:T(8,128)(2,1)S(1)}, u32[]{:S(2)}, u32[]{:S(2)}) collective-permute-start(bf16[272,128]{1,0:T(8,128)(2,1)S(1)} %get-tuple-element.90.refs_0_), channel_id=1, source_target_pairs={{0,6},{2,4},{4,2},{6,0},{1,7},{3,5},{5,3},{7,1},{8,14},{10,12},{12... | collective-permute-start | bytes 208904 | tf_op jit(solution)/shard_map/ppermute | solution.py:542
  70.7 6.1 %collective-permute-start.23 = (bf16[272,128]{1,0:T(8,128)(2,1)S(1)}, bf16[272,128]{1,0:T(8,128)(2,1)S(1)}, u32[]{:S(2)}, u32[]{:S(2)}) collective-permute-start(bf16[272,128]{1,0:T(8,128)(2,1)S(1)} %get-tuple-element.90.refs_0_), channel_id=1, source_target_pairs={{0,4},{2,6},{4,0},{6,2},{1,5},{3,7},{5,1},{7,3},{8,12},{10,14},{12... | collective-permute-start | bytes 208904 | tf_op jit(solution)/shard_map/ppermute | solution.py:542
  71.2 5.6 %collective-permute-start.22 = (bf16[272,128]{1,0:T(8,128)(2,1)S(1)}, bf16[272,128]{1,0:T(8,128)(2,1)S(1)}, u32[]{:S(2)}, u32[]{:S(2)}) collective-permute-start(bf16[272,128]{1,0:T(8,128)(2,1)S(1)} %get-tuple-element.90.refs_0_), channel_id=1, source_target_pairs={{0,2},{2,0},{4,6},{6,4},{1,3},{3,1},{5,7},{7,5},{8,10},{10,8},{12,... | collective-permute-start | bytes 208904 | tf_op jit(solution)/shard_map/ppermute | solution.py:542
  78.5 5.8 %collective-permute-start.27 = (bf16[144,128]{1,0:T(8,128)(2,1)S(1)}, bf16[144,128]{1,0:T(8,128)(2,1)S(1)}, u32[]{:S(2)}, u32[]{:S(2)}) collective-permute-start(bf16[144,128]{1,0:T(8,128)(2,1)S(1)} %get-tuple-element.99.refs_0_), channel_id=1, source_target_pairs={{0,6},{2,4},{4,2},{6,0},{1,7},{3,5},{5,3},{7,1},{8,14},{10,12},{12... | collective-permute-start | bytes 110600 | tf_op jit(solution)/shard_map/ppermute | solution.py:542
  80.2 5.0 %collective-permute-start.26 = (bf16[144,128]{1,0:T(8,128)(2,1)S(1)}, bf16[144,128]{1,0:T(8,128)(2,1)S(1)}, u32[]{:S(2)}, u32[]{:S(2)}) collective-permute-start(bf16[144,128]{1,0:T(8,128)(2,1)S(1)} %get-tuple-element.99.refs_0_), channel_id=1, source_target_pairs={{0,4},{2,6},{4,0},{6,2},{1,5},{3,7},{5,1},{7,3},{8,12},{10,14},{12... | collective-permute-start | bytes 110600 | tf_op jit(solution)/shard_map/ppermute | solution.py:542
  80.4 5.3 %collective-permute-start.25 = (bf16[144,128]{1,0:T(8,128)(2,1)S(1)}, bf16[144,128]{1,0:T(8,128)(2,1)S(1)}, u32[]{:S(2)}, u32[]{:S(2)}) collective-permute-start(bf16[144,128]{1,0:T(8,128)(2,1)S(1)} %get-tuple-element.99.refs_0_), channel_id=1, source_target_pairs={{0,2},{2,0},{4,6},{6,4},{1,3},{3,1},{5,7},{7,5},{8,10},{10,8},{12,... | collective-permute-start | bytes 110600 | tf_op jit(solution)/shard_map/ppermute | solution.py:542
  87.4 5.8 %collective-permute-start.30 = (bf16[144,128]{1,0:T(8,128)(2,1)S(1)}, bf16[144,128]{1,0:T(8,128)(2,1)S(1)}, u32[]{:S(2)}, u32[]{:S(2)}) collective-permute-start(bf16[144,128]{1,0:T(8,128)(2,1)S(1)} %get-tuple-element.105.refs_0_), channel_id=1, source_target_pairs={{0,6},{2,4},{4,2},{6,0},{1,7},{3,5},{5,3},{7,1},{8,14},{10,12},{12... | collective-permute-start | bytes 110600 | tf_op jit(solution)/shard_map/ppermute | solution.py:542
  89.8 4.9 %collective-permute-start.29 = (bf16[144,128]{1,0:T(8,128)(2,1)S(1)}, bf16[144,128]{1,0:T(8,128)(2,1)S(1)}, u32[]{:S(2)}, u32[]{:S(2)}) collective-permute-start(bf16[144,128]{1,0:T(8,128)(2,1)S(1)} %get-tuple-element.105.refs_0_), channel_id=1, source_target_pairs={{0,4},{2,6},{4,0},{6,2},{1,5},{3,7},{5,1},{7,3},{8,12},{10,14},{12... | collective-permute-start | bytes 110600 | tf_op jit(solution)/shard_map/ppermute | solution.py:542
  90.1 4.6 %collective-permute-start.28 = (bf16[144,128]{1,0:T(8,128)(2,1)S(1)}, bf16[144,128]{1,0:T(8,128)(2,1)S(1)}, u32[]{:S(2)}, u32[]{:S(2)}) collective-permute-start(bf16[144,128]{1,0:T(8,128)(2,1)S(1)} %get-tuple-element.105.refs_0_), channel_id=1, source_target_pairs={{0,2},{2,0},{4,6},{6,4},{1,3},{3,1},{5,7},{7,5},{8,10},{10,8},{12,... | collective-permute-start | bytes 110600 | tf_op jit(solution)/shard_map/ppermute | solution.py:542
  91.9 4.3 %collective-permute-start.33 = (bf16[272,512]{1,0:T(8,128)(2,1)S(1)}, bf16[272,512]{1,0:T(8,128)(2,1)S(1)}, u32[]{:S(2)}, u32[]{:S(2)}) collective-permute-start(bf16[272,512]{1,0:T(8,128)(2,1)S(1)} %get-tuple-element.117), channel_id=1, source_target_pairs={{0,1},{1,0},{2,3},{3,2},{4,5},{5,4},{6,7},{7,6},{8,9},{9,8},{10,11... | collective-permute-start | bytes 835592 | tf_op jit(solution)/shard_map/ppermute | solution.py:548
  91.9 4.4 %collective-permute-start.34 = (bf16[272,512]{1,0:T(8,128)(2,1)S(1)}, bf16[272,512]{1,0:T(8,128)(2,1)S(1)}, u32[]{:S(2)}, u32[]{:S(2)}) collective-permute-start(bf16[272,512]{1,0:T(8,128)(2,1)S(1)} %get-tuple-element.118), channel_id=1, source_target_pairs={{0,1},{1,0},{2,3},{3,2},{4,5},{5,4},{6,7},{7,6},{8,9},{9,8},{10,11... | collective-permute-start | bytes 835592 | tf_op jit(solution)/shard_map/ppermute | solution.py:548
  98.3 9.6 %collective-permute-start.35 = (bf16[272,512]{1,0:T(8,128)(2,1)S(1)}, bf16[272,512]{1,0:T(8,128)(2,1)S(1)}, u32[]{:S(2)}, u32[]{:S(2)}) collective-permute-start(bf16[272,512]{1,0:T(8,128)(2,1)S(1)} %get-tuple-element.120), channel_id=1, source_target_pairs={{0,8},{8,0},{16,24},{24,16},{1,9},{9,1},{17,25},{25,17},{2,10},{10... | collective-permute-start | bytes 835592 | tf_op jit(solution)/shard_map/ppermute | solution.py:545
  99.5 14.4 %collective-permute-start.36 = (bf16[272,512]{1,0:T(8,128)(2,1)S(1)}, bf16[272,512]{1,0:T(8,128)(2,1)S(1)}, u32[]{:S(2)}, u32[]{:S(2)}) collective-permute-start(bf16[272,512]{1,0:T(8,128)(2,1)S(1)} %get-tuple-element.121), channel_id=1, source_target_pairs={{0,16},{8,24},{16,0},{24,8},{1,17},{9,25},{17,1},{25,9},{2,18},{10... | collective-permute-start | bytes 835592 | tf_op jit(solution)/shard_map/ppermute | solution.py:545
  100.9 12.9 %collective-permute-start.37 = (bf16[272,512]{1,0:T(8,128)(2,1)S(1)}, bf16[272,512]{1,0:T(8,128)(2,1)S(1)}, u32[]{:S(2)}, u32[]{:S(2)}) collective-permute-start(bf16[272,512]{1,0:T(8,128)(2,1)S(1)} %get-tuple-element.122), channel_id=1, source_target_pairs={{0,24},{8,16},{16,8},{24,0},{1,25},{9,17},{17,9},{25,1},{2,26},{10... | collective-permute-start | bytes 835592 | tf_op jit(solution)/shard_map/ppermute | solution.py:545
  (8 other events, 18.0 us)

commit v10 on v9

--- a/solution.py
+++ b/solution.py
@@ -181,17 +181,21 @@
     rows, local = x.shape
     size = block_size(rows)
     factor = lax.rsqrt(mean + EPS)
+    heads = range(local // HD)
+    gains = [head_gain(weights, head) for head in heads]
     for block in range(rows // size):
         span = slice(block * size, (block + 1) * size)
         allowed = mask[block] > 0
-        for head in range(local // HD):
-            part = slice(head * HD, (head + 1) * HD)
-            normed = (x[span, part].astype(F32) * factor[span] * head_gain(weights, head)).astype(BF)
-            scores = dot_nt(normed, normed) * (1.0 / HD)
-            raw = jnp.where(allowed, jnp.exp(scores), 0.0)
-            prob = (raw * (1.0 / jnp.sum(raw, axis=1, keepdims=True))).astype(BF)
-            probs[block, head] = prob
-            mixed[span, part] = dot(prob, normed).astype(BF)
+        wide = x[span, :].astype(F32) * factor[span]
+        normed = [(wide[:, head * HD : (head + 1) * HD] * gains[head]).astype(BF) for head in heads]
+        scores = [dot_nt(value, value) for value in normed]
+        raw = [jnp.where(allowed, jnp.exp(score * (1.0 / HD)), 0.0) for score in scores]
+        shares = [1.0 / jnp.sum(value, axis=1, keepdims=True) for value in raw]
+        prob = [(value * share).astype(BF) for value, share in zip(raw, shares)]
+        result = [dot(left, right).astype(BF) for left, right in zip(prob, normed)]
+        for head in heads:
+            probs[block, head] = prob[head]
+            mixed[span, head * HD : (head + 1) * HD] = result[head]
 
 
 def send_forward(x, weights, mixed, pay):
@@ -371,32 +375,41 @@
     back_mixed = [
         from_rank(dred, weights, 0, side).astype(BF) for side in range(weights.shape[1])
     ]
-    gain_sums = [None] * (local // HD)
+    heads = range(local // HD)
+    gains = [head_gain(weights, head) for head in heads]
+    gain_sums = [None] * len(heads)
     for block in range(rows // size):
         span = slice(block * size, (block + 1) * size)
         scale = factor[span]
+        parts = [slice(head * HD, (head + 1) * HD) for head in heads]
+        wide = [x[span, part].astype(F32) for part in parts]
+        prob = [probs[block, head] for head in heads]
+        onward = [None if carried is None else dout[span, part].astype(F32) for part in parts]
+        unit = [value * scale for value in wide]
+        normed = [(value * gain).astype(BF) for value, gain in zip(unit, gains)]
+        upstream = []
+        for head in heads:
+            inner = (head % per_slice) * HD
+            upstream.append(back_mixed[head // per_slice][span, inner : inner + HD])
+        back_prob = [dot_nt(left, right) for left, right in zip(upstream, normed)]
+        through = [dot_tn(left, right) for left, right in zip(prob, upstream)]
+        both = []
+        for head in heads:
+            prob_wide = prob[head].astype(F32)
+            inner_sum = jnp.sum(back_prob[head] * prob_wide, axis=1, keepdims=True)
+            back_score = prob_wide * (back_prob[head] - inner_sum) * (1.0 / HD)
+            both.append((back_score + back_score.T).astype(BF))
+        back_normed = [
+            (through[head] + dot(both[head], normed[head])).astype(BF).astype(F32) for head in heads
+        ]
         norm_dot = jnp.zeros((size, HD), F32)
-        for head in range(local // HD):
-            part = slice(head * HD, (head + 1) * HD)
-            side, inner = head // per_slice, (head % per_slice) * HD
-            wide = x[span, part].astype(F32)
-            gain = head_gain(weights, head)
-            unit = wide * scale
-            normed = (unit * gain).astype(BF)
-            prob = probs[block, head]
-            upstream = back_mixed[side][span, inner : inner + HD]
-            back_prob = dot_nt(upstream, normed)
-            prob_wide = prob.astype(F32)
-            inner_sum = jnp.sum(back_prob * prob_wide, axis=1, keepdims=True)
-            back_score = prob_wide * (back_prob - inner_sum) * (1.0 / HD)
-            both = (back_score + back_score.T).astype(BF)
-            back_normed = (dot_tn(prob, upstream) + dot(both, normed)).astype(BF).astype(F32)
-            term = jnp.sum(back_normed * unit, axis=0, keepdims=True)
+        for head in heads:
+            term = jnp.sum(back_normed[head] * unit[head], axis=0, keepdims=True)
             gain_sums[head] = term if gain_sums[head] is None else gain_sums[head] + term
             if carried is not None:
-                scaled = back_normed * gain
-                norm_dot = norm_dot + scaled * wide
-                carried[span, part] = (dout[span, part].astype(F32) + scaled * scale).astype(BF)
+                scaled = back_normed[head] * gains[head]
+                norm_dot = norm_dot + scaled * wide[head]
+                carried[span, parts[head]] = (onward[head] + scaled * scale).astype(BF)
         if carried is not None:
             column = jnp.broadcast_to(jnp.sum(norm_dot, axis=1, keepdims=True), (size, size))
             line = column.T[0:1, :]

time: 115 us -> 110 us (0.957)
  Pallas kernels: 20.4 us -> 15.2 us
    pallas_call x10, Pallas kernels: 18.1 us -> 12.9 us  [call(): pl.pallas_call(kernel, in_specs=specs, out_specs=vmem_specs(len(outs)), o...]
  transfers between devices with their start and end apart: 38 -> 38, of which waited for: 16 -> 15; matrix products, arithmetic and copies ran while one was open for 0% -> 0% of each run, Pallas kernels for 4% -> 3%
where the time goes in v10:
time: 110 us
  starting transfers between devices  47.4 us (43%)
  waiting for transfers between devices  44.9 us (41%)
  Pallas kernels  15.2 us (14%)
  local copies, waits for them, and re-layouts  1.86 us (2%)
    ppermute x24, starting transfers between devices, shifted(): return lax.ppermute(value, 'z', [(i, i ^ shift) for i in range(groups)])  38.7 us
    ppermute x24, waiting for transfers between devices, shifted(): return lax.ppermute(value, 'z', [(i, i ^ shift) for i in range(groups)])  30.6 us
    pallas_call x10, Pallas kernels, call(): pl.pallas_call(kernel, in_specs=specs, out_specs=vmem_specs(len(outs)), o...  12.9 us
    ppermute x6, waiting for transfers between devices, across(): lax.ppermute(value, 'pipe', [(i, i ^ distance) for i in range(sections)])  12.8 us
    ppermute x6, starting transfers between devices, across(): lax.ppermute(value, 'pipe', [(i, i ^ distance) for i in range(sections)])  7.04 us
    pallas_call x1, Pallas kernels, pack(): pl.pallas_call(functools.partial(pack_kernel, groups, micro_local), in_sp...  2.28 us
  transfers between devices with their start and end apart: 38, of which 15 were waited for; matrix products, arithmetic and copies ran while one was open for 0% of the time, Pallas kernels for 3%

profile of v10, /device:TPU:0, one launch (start us, length us, event | category | flops | bytes accessed | tf_op | source)
XLA Modules:
  0.0 110.1 jit_solution(1012047022845211951)
XLA Ops:
  0.6 2.3 %pack.1 = (bf16[32,2176]{1,0:T(8,128)(2,1)}, bf16[32,2176]{1,0:T(8,128)(2,1)}, bf16[32,2176]{1,0:T(8,128)(2,1)}, bf16[32,2176]{1,0:T(8,128)(2,1)}, bf16[1040,128]{1,0:T(8,128)(2,1)}) custom-call(bf16[2,2,32,4096]{3,2,1,0:T(8,128)(2,1)} %refs_0_.1, bf16[2,2,32,4096]{3,2,1,0:T(8,128)(2,1)} %refs_1_.1, s32[2,2,4]{2,1,0:T(2,128)} %refs_2_.1, s32[2,2]{1,0:T(2,128)} %refs_3_.1, ...), custom_call_target="tpu_custom_call" | custom-call | tf_op jit(solution)/shard_map/pack/pallas_call | solution.py:124
  2.9 3.1 %collective-permute-start = (bf16[32,2176]{1,0:T(8,128)(2,1)}, bf16[32,2176]{1,0:T(8,128)(2,1)S(1)}, u32[]{:S(2)}, u32[]{:S(2)}) collective-permute-start(bf16[32,2176]{1,0:T(8,128)(2,1)} %get-tuple-element.64), channel_id=1, source_target_pairs={{0,2},{2,0},{4,6},{6,4},{1,3},{3,1},{5,7},{7,5},{8,10},{10,8},{12,... | collective-permute-start | bytes 417800 | tf_op jit(solution)/shard_map/ppermute | solution.py:555
  6.0 2.4 %collective-permute-start.5 = (bf16[1040,128]{1,0:T(8,128)(2,1)}, bf16[1040,128]{1,0:T(8,128)(2,1)S(1)}, u32[]{:S(2)}, u32[]{:S(2)}) collective-permute-start(bf16[1040,128]{1,0:T(8,128)(2,1)} %get-tuple-element.72.refs_4_), channel_id=1, source_target_pairs={{0,24},{8,16},{16,8},{24,0},{1,25},{9,17},{17,9},{25,1},{2,26},{10... | collective-permute-start | bytes 798728 | tf_op jit(solution)/shard_map/ppermute | solution.py:558
  9.5 2.6 %collective-permute-start.1 = (bf16[32,2176]{1,0:T(8,128)(2,1)}, bf16[32,2176]{1,0:T(8,128)(2,1)S(1)}, u32[]{:S(2)}, u32[]{:S(2)}) collective-permute-start(bf16[32,2176]{1,0:T(8,128)(2,1)} %get-tuple-element.65), channel_id=1, source_target_pairs={{0,4},{2,6},{4,0},{6,2},{1,5},{3,7},{5,1},{7,3},{8,12},{10,14},{12... | collective-permute-start | bytes 417800 | tf_op jit(solution)/shard_map/ppermute | solution.py:555
  12.1 1.6 %collective-permute-start.2 = (bf16[32,2176]{1,0:T(8,128)(2,1)}, bf16[32,2176]{1,0:T(8,128)(2,1)S(1)}, u32[]{:S(2)}, u32[]{:S(2)}) collective-permute-start(bf16[32,2176]{1,0:T(8,128)(2,1)} %get-tuple-element.66), channel_id=1, source_target_pairs={{0,6},{2,4},{4,2},{6,0},{1,7},{3,5},{5,3},{7,1},{8,14},{10,12},{12... | collective-permute-start | bytes 417800 | tf_op jit(solution)/shard_map/ppermute | solution.py:555
  13.7 7.6 %collective-permute-done.1.refs_2_ = bf16[32,2176]{1,0:T(8,128)(2,1)S(1)} collective-permute-done((bf16[32,2176]{1,0:T(8,128)(2,1)}, bf16[32,2176]{1,0:T(8,128)(2,1)S(1)}, u32[]{:S(2)}, u32[]{:S(2)}) %collective-permute-start.1) | collective-permute-done | bytes 139296 | tf_op jit(solution)/shard_map/ppermute | solution.py:555
  24.5 1.9 %forward_first.1 = (bf16[1,8,128,128]{3,2,1,0:T(8,128)(2,1)S(1)}, bf16[128,1024]{1,0:T(8,128)(2,1)S(1)}, bf16[400,128]{1,0:T(8,128)(2,1)S(1)}, bf16[256,128]{1,0:T(8,128)(2,1)S(1)}, bf16[4,2,1040,128]{3,2,1,0:T(8,128)(2,1)S(1)}) custom-call(bf16[1040,128]{1,0:T(8,128)(2,1)S(1)} %get-tuple-element.73.refs_0_, ...), custom_call_target="tpu_custom_call" | custom-call | tf_op jit(solution)/shard_map/forward_first/pallas_call | solution.py:588
  26.4 3.3 %collective-permute-start.12 = (bf16[400,128]{1,0:T(8,128)(2,1)S(1)}, bf16[400,128]{1,0:T(8,128)(2,1)S(1)}, u32[]{:S(2)}, u32[]{:S(2)}) collective-permute-start(bf16[400,128]{1,0:T(8,128)(2,1)S(1)} %get-tuple-element.81.refs_0_.refs_4_), channel_id=1, source_target_pairs={{0,6},{2,4},{4,2},{6,0},{1,7},{3,5},{5,3},{7,1},{8,14},{10,12},{12... | collective-permute-start | bytes 307208 | tf_op jit(solution)/shard_map/ppermute | solution.py:555
  31.2 2.0 %collective-permute-done.12.refs_3_.refs_7_ = bf16[400,128]{1,0:T(8,128)(2,1)S(1)} collective-permute-done((bf16[400,128]{1,0:T(8,128)(2,1)S(1)}, bf16[400,128]{1,0:T(8,128)(2,1)S(1)}, u32[]{:S(2)}, u32[]{:S(2)}) %collective-permute-start.12) | collective-permute-done | bytes 102432 | tf_op jit(solution)/shard_map/ppermute | solution.py:555
  33.2 6.5 %collective-permute-done.11.refs_2_.refs_6_ = bf16[400,128]{1,0:T(8,128)(2,1)S(1)} collective-permute-done((bf16[400,128]{1,0:T(8,128)(2,1)S(1)}, bf16[400,128]{1,0:T(8,128)(2,1)S(1)}, u32[]{:S(2)}, u32[]{:S(2)}) %collective-permute-start.11) | collective-permute-done | bytes 102432 | tf_op jit(solution)/shard_map/ppermute | solution.py:555
  41.0 3.3 %collective-permute-start.15 = (bf16[256,128]{1,0:T(8,128)(2,1)S(1)}, bf16[256,128]{1,0:T(8,128)(2,1)S(1)}, u32[]{:S(2)}, u32[]{:S(2)}) collective-permute-start(bf16[256,128]{1,0:T(8,128)(2,1)S(1)} %get-tuple-element.83.refs_0_), channel_id=1, source_target_pairs={{0,6},{2,4},{4,2},{6,0},{1,7},{3,5},{5,3},{7,1},{8,14},{10,12},{12... | collective-permute-start | bytes 196616 | tf_op jit(solution)/shard_map/ppermute | solution.py:555
  45.5 3.3 %collective-permute-start.21 = (bf16[256,128]{1,0:T(8,128)(2,1)S(1)}, bf16[256,128]{1,0:T(8,128)(2,1)S(1)}, u32[]{:S(2)}, u32[]{:S(2)}) collective-permute-start(bf16[256,128]{1,0:T(8,128)(2,1)S(1)} %get-tuple-element.87.refs_4_), channel_id=1, source_target_pairs={{0,6},{2,4},{4,2},{6,0},{1,7},{3,5},{5,3},{7,1},{8,14},{10,12},{12... | collective-permute-start | bytes 196616 | tf_op jit(solution)/shard_map/ppermute | solution.py:555
  49.9 2.6 %collective-permute-done.14.refs_2_ = bf16[256,128]{1,0:T(8,128)(2,1)S(1)} collective-permute-done((bf16[256,128]{1,0:T(8,128)(2,1)S(1)}, bf16[256,128]{1,0:T(8,128)(2,1)S(1)}, u32[]{:S(2)}, u32[]{:S(2)}) %collective-permute-start.14) | collective-permute-done | bytes 65568 | tf_op jit(solution)/shard_map/ppermute | solution.py:555
  55.1 3.2 %collective-permute-start.16 = (bf16[256,128]{1,0:T(8,128)(2,1)S(1)}, bf16[256,128]{1,0:T(8,128)(2,1)S(1)}, u32[]{:S(2)}, u32[]{:S(2)}) collective-permute-start(bf16[256,128]{1,0:T(8,128)(2,1)S(1)} %get-tuple-element.86.refs_0_), channel_id=1, source_target_pairs={{0,2},{2,0},{4,6},{6,4},{1,3},{3,1},{5,7},{7,5},{8,10},{10,8},{12,... | collective-permute-start | bytes 196616 | tf_op jit(solution)/shard_map/ppermute | solution.py:555
  58.3 1.7 %collective-permute-done.18.refs_3_ = bf16[256,128]{1,0:T(8,128)(2,1)S(1)} collective-permute-done((bf16[256,128]{1,0:T(8,128)(2,1)S(1)}, bf16[256,128]{1,0:T(8,128)(2,1)S(1)}, u32[]{:S(2)}, u32[]{:S(2)}) %collective-permute-start.18) | collective-permute-done | bytes 65568 | tf_op jit(solution)/shard_map/ppermute | solution.py:555
  61.4 2.2 %turn.1 = (bf16[128,1024]{1,0:T(8,128)(2,1)S(1)}, f32[128,128]{1,0:T(8,128)S(1)}, bf16[128,128]{1,0:T(8,128)(2,1)S(1)}, f32[128,128]{1,0:T(8,128)S(1)}, bf16[2,2...) custom-call(bf16[256,128]{1,0:T(8,128)(2,1)S(1)} %get-tuple-element.86.refs_0_, ...), custom_call_target="tpu_custom_call" | custom-call | tf_op jit(solution)/shard_map/turn/pallas_call | solution.py:588
  63.6 2.3 %collective-permute-start.24 = (bf16[272,128]{1,0:T(8,128)(2,1)S(1)}, bf16[272,128]{1,0:T(8,128)(2,1)S(1)}, u32[]{:S(2)}, u32[]{:S(2)}) collective-permute-start(bf16[272,128]{1,0:T(8,128)(2,1)S(1)} %get-tuple-element.90.refs_0_), channel_id=1, source_target_pairs={{0,6},{2,4},{4,2},{6,0},{1,7},{3,5},{5,3},{7,1},{8,14},{10,12},{12... | collective-permute-start | bytes 208904 | tf_op jit(solution)/shard_map/ppermute | solution.py:555
  66.3 1.7 %collective-permute-start.22 = (bf16[272,128]{1,0:T(8,128)(2,1)S(1)}, bf16[272,128]{1,0:T(8,128)(2,1)S(1)}, u32[]{:S(2)}, u32[]{:S(2)}) collective-permute-start(bf16[272,128]{1,0:T(8,128)(2,1)S(1)} %get-tuple-element.90.refs_0_), channel_id=1, source_target_pairs={{0,2},{2,0},{4,6},{6,4},{1,3},{3,1},{5,7},{7,5},{8,10},{10,8},{12,... | collective-permute-start | bytes 208904 | tf_op jit(solution)/shard_map/ppermute | solution.py:555
  68.0 1.8 %collective-permute-done.24.refs_3_ = bf16[272,128]{1,0:T(8,128)(2,1)S(1)} collective-permute-done((bf16[272,128]{1,0:T(8,128)(2,1)S(1)}, bf16[272,128]{1,0:T(8,128)(2,1)S(1)}, u32[]{:S(2)}, u32[]{:S(2)}) %collective-permute-start.24) | collective-permute-done | bytes 69664 | tf_op jit(solution)/shard_map/ppermute | solution.py:555
  69.9 1.7 %collective-permute-done.23.refs_2_ = bf16[272,128]{1,0:T(8,128)(2,1)S(1)} collective-permute-done((bf16[272,128]{1,0:T(8,128)(2,1)S(1)}, bf16[272,128]{1,0:T(8,128)(2,1)S(1)}, u32[]{:S(2)}, u32[]{:S(2)}) %collective-permute-start.23) | collective-permute-done | bytes 69664 | tf_op jit(solution)/shard_map/ppermute | solution.py:555
  71.6 1.6 %backward.3 = (bf16[272,512]{1,0:T(8,128)(2,1)S(1)}, bf16[272,512]{1,0:T(8,128)(2,1)S(1)}, bf16[272,512]{1,0:T(8,128)(2,1)S(1)}, bf16[272,512]{1,0:T(8,128)(2,1)...) custom-call(bf16[272,128]{1,0:T(8,128)(2,1)S(1)} %get-tuple-element.90.refs_0_, ...), custom_call_target="tpu_custom_call" | custom-call | tf_op jit(solution)/shard_map/backward/pallas_call | solution.py:588
  73.2 2.6 %collective-permute-start.27 = (bf16[144,128]{1,0:T(8,128)(2,1)S(1)}, bf16[144,128]{1,0:T(8,128)(2,1)S(1)}, u32[]{:S(2)}, u32[]{:S(2)}) collective-permute-start(bf16[144,128]{1,0:T(8,128)(2,1)S(1)} %get-tuple-element.99.refs_0_), channel_id=1, source_target_pairs={{0,6},{2,4},{4,2},{6,0},{1,7},{3,5},{5,3},{7,1},{8,14},{10,12},{12... | collective-permute-start | bytes 110600 | tf_op jit(solution)/shard_map/ppermute | solution.py:555
  75.8 1.9 %collective-permute-start.25 = (bf16[144,128]{1,0:T(8,128)(2,1)S(1)}, bf16[144,128]{1,0:T(8,128)(2,1)S(1)}, u32[]{:S(2)}, u32[]{:S(2)}) collective-permute-start(bf16[144,128]{1,0:T(8,128)(2,1)S(1)} %get-tuple-element.99.refs_0_), channel_id=1, source_target_pairs={{0,2},{2,0},{4,6},{6,4},{1,3},{3,1},{5,7},{7,5},{8,10},{10,8},{12,... | collective-permute-start | bytes 110600 | tf_op jit(solution)/shard_map/ppermute | solution.py:555
  77.6 1.5 %collective-permute-done.27.refs_3_ = bf16[144,128]{1,0:T(8,128)(2,1)S(1)} collective-permute-done((bf16[144,128]{1,0:T(8,128)(2,1)S(1)}, bf16[144,128]{1,0:T(8,128)(2,1)S(1)}, u32[]{:S(2)}, u32[]{:S(2)}) %collective-permute-start.27) | collective-permute-done | bytes 36896 | tf_op jit(solution)/shard_map/ppermute | solution.py:555
  79.2 1.5 %collective-permute-done.26.refs_2_ = bf16[144,128]{1,0:T(8,128)(2,1)S(1)} collective-permute-done((bf16[144,128]{1,0:T(8,128)(2,1)S(1)}, bf16[144,128]{1,0:T(8,128)(2,1)S(1)}, u32[]{:S(2)}, u32[]{:S(2)}) %collective-permute-start.26) | collective-permute-done | bytes 36896 | tf_op jit(solution)/shard_map/ppermute | solution.py:555
  80.6 1.6 %backward.4 = (bf16[272,512]{1,0:T(8,128)(2,1)S(1)}, bf16[272,512]{1,0:T(8,128)(2,1)S(1)}, bf16[128,1024]{1,0:T(8,128)(2,1)S(1)}, bf16[144,128]{1,0:T(8,128)(2,1)S(1)}) custom-call(bf16[144,128]{1,0:T(8,128)(2,1)S(1)} %get-tuple-element.99.refs_0_, bf16[144,128]{1,0:T(8,128)(2,1)S(1)} %collective-permute-done.25.refs_1_, ...), custom_call_target="tpu_custom_call" | custom-call | tf_op jit(solution)/shard_map/backward/pallas_call | solution.py:588
  82.2 1.9 %collective-permute-start.30 = (bf16[144,128]{1,0:T(8,128)(2,1)S(1)}, bf16[144,128]{1,0:T(8,128)(2,1)S(1)}, u32[]{:S(2)}, u32[]{:S(2)}) collective-permute-start(bf16[144,128]{1,0:T(8,128)(2,1)S(1)} %get-tuple-element.105.refs_0_), channel_id=1, source_target_pairs={{0,6},{2,4},{4,2},{6,0},{1,7},{3,5},{5,3},{7,1},{8,14},{10,12},{12... | collective-permute-start | bytes 110600 | tf_op jit(solution)/shard_map/ppermute | solution.py:555
  84.7 1.9 %collective-permute-start.28 = (bf16[144,128]{1,0:T(8,128)(2,1)S(1)}, bf16[144,128]{1,0:T(8,128)(2,1)S(1)}, u32[]{:S(2)}, u32[]{:S(2)}) collective-permute-start(bf16[144,128]{1,0:T(8,128)(2,1)S(1)} %get-tuple-element.105.refs_0_), channel_id=1, source_target_pairs={{0,2},{2,0},{4,6},{6,4},{1,3},{3,1},{5,7},{7,5},{8,10},{10,8},{12,... | collective-permute-start | bytes 110600 | tf_op jit(solution)/shard_map/ppermute | solution.py:555
  90.8 1.5 %collective-permute-done.31.refs_4_ = bf16[272,512]{1,0:T(8,128)(2,1)S(1)} collective-permute-done((bf16[272,512]{1,0:T(8,128)(2,1)S(1)}, bf16[272,512]{1,0:T(8,128)(2,1)S(1)}, u32[]{:S(2)}, u32[]{:S(2)}) %collective-permute-start.31) | collective-permute-done | bytes 278560 | tf_op jit(solution)/shard_map/ppermute | solution.py:561
  92.8 1.9 %collective-permute-start.35 = (bf16[272,512]{1,0:T(8,128)(2,1)S(1)}, bf16[272,512]{1,0:T(8,128)(2,1)S(1)}, u32[]{:S(2)}, u32[]{:S(2)}) collective-permute-start(bf16[272,512]{1,0:T(8,128)(2,1)S(1)} %get-tuple-element.120), channel_id=1, source_target_pairs={{0,8},{8,0},{16,24},{24,16},{1,9},{9,1},{17,25},{25,17},{2,10},{10... | collective-permute-start | bytes 835592 | tf_op jit(solution)/shard_map/ppermute | solution.py:558
  96.4 6.0 %collective-permute-done.35.refs_1_ = bf16[272,512]{1,0:T(8,128)(2,1)S(1)} collective-permute-done((bf16[272,512]{1,0:T(8,128)(2,1)S(1)}, bf16[272,512]{1,0:T(8,128)(2,1)S(1)}, u32[]{:S(2)}, u32[]{:S(2)}) %collective-permute-start.35) | collective-permute-done | bytes 278560 | tf_op jit(solution)/shard_map/ppermute | solution.py:558
  102.4 6.8 %collective-permute-done.36.refs_2_ = bf16[272,512]{1,0:T(8,128)(2,1)S(1)} collective-permute-done((bf16[272,512]{1,0:T(8,128)(2,1)S(1)}, bf16[272,512]{1,0:T(8,128)(2,1)S(1)}, u32[]{:S(2)}, u32[]{:S(2)}) %collective-permute-start.36) | collective-permute-done | bytes 278560 | tf_op jit(solution)/shard_map/ppermute | solution.py:558
  (59 shorter events, 21.4 us)
Async XLA Ops:
  2.9 9.2 %collective-permute-start = (bf16[32,2176]{1,0:T(8,128)(2,1)}, bf16[32,2176]{1,0:T(8,128)(2,1)S(1)}, u32[]{:S(2)}, u32[]{:S(2)}) collective-permute-start(bf16[32,2176]{1,0:T(8,128)(2,1)} %get-tuple-element.64), channel_id=1, source_target_pairs={{0,2},{2,0},{4,6},{6,4},{1,3},{3,1},{5,7},{7,5},{8,10},{10,8},{12,... | collective-permute-start | bytes 417800 | tf_op jit(solution)/shard_map/ppermute | solution.py:555
  6.0 15.2 %collective-permute-start.5 = (bf16[1040,128]{1,0:T(8,128)(2,1)}, bf16[1040,128]{1,0:T(8,128)(2,1)S(1)}, u32[]{:S(2)}, u32[]{:S(2)}) collective-permute-start(bf16[1040,128]{1,0:T(8,128)(2,1)} %get-tuple-element.72.refs_4_), channel_id=1, source_target_pairs={{0,24},{8,16},{16,8},{24,0},{1,25},{9,17},{17,9},{25,1},{2,26},{10... | collective-permute-start | bytes 798728 | tf_op jit(solution)/shard_map/ppermute | solution.py:558
  8.5 12.8 %collective-permute-start.4 = (bf16[1040,128]{1,0:T(8,128)(2,1)}, bf16[1040,128]{1,0:T(8,128)(2,1)S(1)}, u32[]{:S(2)}, u32[]{:S(2)}) collective-permute-start(bf16[1040,128]{1,0:T(8,128)(2,1)} %get-tuple-element.72.refs_4_), channel_id=1, source_target_pairs={{0,16},{8,24},{16,0},{24,8},{1,17},{9,25},{17,1},{25,9},{2,18},{10... | collective-permute-start | bytes 798728 | tf_op jit(solution)/shard_map/ppermute | solution.py:558
  9.0 12.3 %collective-permute-start.3 = (bf16[1040,128]{1,0:T(8,128)(2,1)}, bf16[1040,128]{1,0:T(8,128)(2,1)S(1)}, u32[]{:S(2)}, u32[]{:S(2)}) collective-permute-start(bf16[1040,128]{1,0:T(8,128)(2,1)} %get-tuple-element.72.refs_4_), channel_id=1, source_target_pairs={{0,8},{8,0},{16,24},{24,16},{1,9},{9,1},{17,25},{25,17},{2,10},{10... | collective-permute-start | bytes 798728 | tf_op jit(solution)/shard_map/ppermute | solution.py:558
  9.5 11.7 %collective-permute-start.1 = (bf16[32,2176]{1,0:T(8,128)(2,1)}, bf16[32,2176]{1,0:T(8,128)(2,1)S(1)}, u32[]{:S(2)}, u32[]{:S(2)}) collective-permute-start(bf16[32,2176]{1,0:T(8,128)(2,1)} %get-tuple-element.65), channel_id=1, source_target_pairs={{0,4},{2,6},{4,0},{6,2},{1,5},{3,7},{5,1},{7,3},{8,12},{10,14},{12... | collective-permute-start | bytes 417800 | tf_op jit(solution)/shard_map/ppermute | solution.py:555
  12.1 9.2 %collective-permute-start.2 = (bf16[32,2176]{1,0:T(8,128)(2,1)}, bf16[32,2176]{1,0:T(8,128)(2,1)S(1)}, u32[]{:S(2)}, u32[]{:S(2)}) collective-permute-start(bf16[32,2176]{1,0:T(8,128)(2,1)} %get-tuple-element.66), channel_id=1, source_target_pairs={{0,6},{2,4},{4,2},{6,0},{1,7},{3,5},{5,3},{7,1},{8,14},{10,12},{12... | collective-permute-start | bytes 417800 | tf_op jit(solution)/shard_map/ppermute | solution.py:555
  26.4 6.8 %collective-permute-start.12 = (bf16[400,128]{1,0:T(8,128)(2,1)S(1)}, bf16[400,128]{1,0:T(8,128)(2,1)S(1)}, u32[]{:S(2)}, u32[]{:S(2)}) collective-permute-start(bf16[400,128]{1,0:T(8,128)(2,1)S(1)} %get-tuple-element.81.refs_0_.refs_4_), channel_id=1, source_target_pairs={{0,6},{2,4},{4,2},{6,0},{1,7},{3,5},{5,3},{7,1},{8,14},{10,12},{12... | collective-permute-start | bytes 307208 | tf_op jit(solution)/shard_map/ppermute | solution.py:555
  29.7 10.0 %collective-permute-start.11 = (bf16[400,128]{1,0:T(8,128)(2,1)S(1)}, bf16[400,128]{1,0:T(8,128)(2,1)S(1)}, u32[]{:S(2)}, u32[]{:S(2)}) collective-permute-start(bf16[400,128]{1,0:T(8,128)(2,1)S(1)} %get-tuple-element.81.refs_0_.refs_4_), channel_id=1, source_target_pairs={{0,4},{2,6},{4,0},{6,2},{1,5},{3,7},{5,1},{7,3},{8,12},{10,14},{12... | collective-permute-start | bytes 307208 | tf_op jit(solution)/shard_map/ppermute | solution.py:555
  31.0 8.7 %collective-permute-start.10 = (bf16[400,128]{1,0:T(8,128)(2,1)S(1)}, bf16[400,128]{1,0:T(8,128)(2,1)S(1)}, u32[]{:S(2)}, u32[]{:S(2)}) collective-permute-start(bf16[400,128]{1,0:T(8,128)(2,1)S(1)} %get-tuple-element.81.refs_0_.refs_4_), channel_id=1, source_target_pairs={{0,2},{2,0},{4,6},{6,4},{1,3},{3,1},{5,7},{7,5},{8,10},{10,8},{12,... | collective-permute-start | bytes 307208 | tf_op jit(solution)/shard_map/ppermute | solution.py:555
  41.0 7.7 %collective-permute-start.15 = (bf16[256,128]{1,0:T(8,128)(2,1)S(1)}, bf16[256,128]{1,0:T(8,128)(2,1)S(1)}, u32[]{:S(2)}, u32[]{:S(2)}) collective-permute-start(bf16[256,128]{1,0:T(8,128)(2,1)S(1)} %get-tuple-element.83.refs_0_), channel_id=1, source_target_pairs={{0,6},{2,4},{4,2},{6,0},{1,7},{3,5},{5,3},{7,1},{8,14},{10,12},{12... | collective-permute-start | bytes 196616 | tf_op jit(solution)/shard_map/ppermute | solution.py:555
  44.4 8.2 %collective-permute-start.14 = (bf16[256,128]{1,0:T(8,128)(2,1)S(1)}, bf16[256,128]{1,0:T(8,128)(2,1)S(1)}, u32[]{:S(2)}, u32[]{:S(2)}) collective-permute-start(bf16[256,128]{1,0:T(8,128)(2,1)S(1)} %get-tuple-element.83.refs_0_), channel_id=1, source_target_pairs={{0,4},{2,6},{4,0},{6,2},{1,5},{3,7},{5,1},{7,3},{8,12},{10,14},{12... | collective-permute-start | bytes 196616 | tf_op jit(solution)/shard_map/ppermute | solution.py:555
  44.4 8.2 %collective-permute-start.13 = (bf16[256,128]{1,0:T(8,128)(2,1)S(1)}, bf16[256,128]{1,0:T(8,128)(2,1)S(1)}, u32[]{:S(2)}, u32[]{:S(2)}) collective-permute-start(bf16[256,128]{1,0:T(8,128)(2,1)S(1)} %get-tuple-element.83.refs_0_), channel_id=1, source_target_pairs={{0,2},{2,0},{4,6},{6,4},{1,3},{3,1},{5,7},{7,5},{8,10},{10,8},{12,... | collective-permute-start | bytes 196616 | tf_op jit(solution)/shard_map/ppermute | solution.py:555
  45.5 9.6 %collective-permute-start.21 = (bf16[256,128]{1,0:T(8,128)(2,1)S(1)}, bf16[256,128]{1,0:T(8,128)(2,1)S(1)}, u32[]{:S(2)}, u32[]{:S(2)}) collective-permute-start(bf16[256,128]{1,0:T(8,128)(2,1)S(1)} %get-tuple-element.87.refs_4_), channel_id=1, source_target_pairs={{0,6},{2,4},{4,2},{6,0},{1,7},{3,5},{5,3},{7,1},{8,14},{10,12},{12... | collective-permute-start | bytes 196616 | tf_op jit(solution)/shard_map/ppermute | solution.py:555
  48.8 9.6 %collective-permute-start.20 = (bf16[256,128]{1,0:T(8,128)(2,1)S(1)}, bf16[256,128]{1,0:T(8,128)(2,1)S(1)}, u32[]{:S(2)}, u32[]{:S(2)}) collective-permute-start(bf16[256,128]{1,0:T(8,128)(2,1)S(1)} %get-tuple-element.87.refs_4_), channel_id=1, source_target_pairs={{0,4},{2,6},{4,0},{6,2},{1,5},{3,7},{5,1},{7,3},{8,12},{10,14},{12... | collective-permute-start | bytes 196616 | tf_op jit(solution)/shard_map/ppermute | solution.py:555
  48.8 9.6 %collective-permute-start.19 = (bf16[256,128]{1,0:T(8,128)(2,1)S(1)}, bf16[256,128]{1,0:T(8,128)(2,1)S(1)}, u32[]{:S(2)}, u32[]{:S(2)}) collective-permute-start(bf16[256,128]{1,0:T(8,128)(2,1)S(1)} %get-tuple-element.87.refs_4_), channel_id=1, source_target_pairs={{0,2},{2,0},{4,6},{6,4},{1,3},{3,1},{5,7},{7,5},{8,10},{10,8},{12,... | collective-permute-start | bytes 196616 | tf_op jit(solution)/shard_map/ppermute | solution.py:555
  53.9 6.2 %collective-permute-start.18 = (bf16[256,128]{1,0:T(8,128)(2,1)S(1)}, bf16[256,128]{1,0:T(8,128)(2,1)S(1)}, u32[]{:S(2)}, u32[]{:S(2)}) collective-permute-start(bf16[256,128]{1,0:T(8,128)(2,1)S(1)} %get-tuple-element.86.refs_0_), channel_id=1, source_target_pairs={{0,6},{2,4},{4,2},{6,0},{1,7},{3,5},{5,3},{7,1},{8,14},{10,12},{12... | collective-permute-start | bytes 196616 | tf_op jit(solution)/shard_map/ppermute | solution.py:555
  55.1 6.3 %collective-permute-start.17 = (bf16[256,128]{1,0:T(8,128)(2,1)S(1)}, bf16[256,128]{1,0:T(8,128)(2,1)S(1)}, u32[]{:S(2)}, u32[]{:S(2)}) collective-permute-start(bf16[256,128]{1,0:T(8,128)(2,1)S(1)} %get-tuple-element.86.refs_0_), channel_id=1, source_target_pairs={{0,4},{2,6},{4,0},{6,2},{1,5},{3,7},{5,1},{7,3},{8,12},{10,14},{12... | collective-permute-start | bytes 196616 | tf_op jit(solution)/shard_map/ppermute | solution.py:555
  55.1 6.3 %collective-permute-start.16 = (bf16[256,128]{1,0:T(8,128)(2,1)S(1)}, bf16[256,128]{1,0:T(8,128)(2,1)S(1)}, u32[]{:S(2)}, u32[]{:S(2)}) collective-permute-start(bf16[256,128]{1,0:T(8,128)(2,1)S(1)} %get-tuple-element.86.refs_0_), channel_id=1, source_target_pairs={{0,2},{2,0},{4,6},{6,4},{1,3},{3,1},{5,7},{7,5},{8,10},{10,8},{12,... | collective-permute-start | bytes 196616 | tf_op jit(solution)/shard_map/ppermute | solution.py:555
  63.6 6.3 %collective-permute-start.24 = (bf16[272,128]{1,0:T(8,128)(2,1)S(1)}, bf16[272,128]{1,0:T(8,128)(2,1)S(1)}, u32[]{:S(2)}, u32[]{:S(2)}) collective-permute-start(bf16[272,128]{1,0:T(8,128)(2,1)S(1)} %get-tuple-element.90.refs_0_), channel_id=1, source_target_pairs={{0,6},{2,4},{4,2},{6,0},{1,7},{3,5},{5,3},{7,1},{8,14},{10,12},{12... | collective-permute-start | bytes 208904 | tf_op jit(solution)/shard_map/ppermute | solution.py:555
  65.8 5.7 %collective-permute-start.23 = (bf16[272,128]{1,0:T(8,128)(2,1)S(1)}, bf16[272,128]{1,0:T(8,128)(2,1)S(1)}, u32[]{:S(2)}, u32[]{:S(2)}) collective-permute-start(bf16[272,128]{1,0:T(8,128)(2,1)S(1)} %get-tuple-element.90.refs_0_), channel_id=1, source_target_pairs={{0,4},{2,6},{4,0},{6,2},{1,5},{3,7},{5,1},{7,3},{8,12},{10,14},{12... | collective-permute-start | bytes 208904 | tf_op jit(solution)/shard_map/ppermute | solution.py:555
  66.3 5.3 %collective-permute-start.22 = (bf16[272,128]{1,0:T(8,128)(2,1)S(1)}, bf16[272,128]{1,0:T(8,128)(2,1)S(1)}, u32[]{:S(2)}, u32[]{:S(2)}) collective-permute-start(bf16[272,128]{1,0:T(8,128)(2,1)S(1)} %get-tuple-element.90.refs_0_), channel_id=1, source_target_pairs={{0,2},{2,0},{4,6},{6,4},{1,3},{3,1},{5,7},{7,5},{8,10},{10,8},{12,... | collective-permute-start | bytes 208904 | tf_op jit(solution)/shard_map/ppermute | solution.py:555
  73.2 6.0 %collective-permute-start.27 = (bf16[144,128]{1,0:T(8,128)(2,1)S(1)}, bf16[144,128]{1,0:T(8,128)(2,1)S(1)}, u32[]{:S(2)}, u32[]{:S(2)}) collective-permute-start(bf16[144,128]{1,0:T(8,128)(2,1)S(1)} %get-tuple-element.99.refs_0_), channel_id=1, source_target_pairs={{0,6},{2,4},{4,2},{6,0},{1,7},{3,5},{5,3},{7,1},{8,14},{10,12},{12... | collective-permute-start | bytes 110600 | tf_op jit(solution)/shard_map/ppermute | solution.py:555
  75.8 4.9 %collective-permute-start.26 = (bf16[144,128]{1,0:T(8,128)(2,1)S(1)}, bf16[144,128]{1,0:T(8,128)(2,1)S(1)}, u32[]{:S(2)}, u32[]{:S(2)}) collective-permute-start(bf16[144,128]{1,0:T(8,128)(2,1)S(1)} %get-tuple-element.99.refs_0_), channel_id=1, source_target_pairs={{0,4},{2,6},{4,0},{6,2},{1,5},{3,7},{5,1},{7,3},{8,12},{10,14},{12... | collective-permute-start | bytes 110600 | tf_op jit(solution)/shard_map/ppermute | solution.py:555
  75.8 4.9 %collective-permute-start.25 = (bf16[144,128]{1,0:T(8,128)(2,1)S(1)}, bf16[144,128]{1,0:T(8,128)(2,1)S(1)}, u32[]{:S(2)}, u32[]{:S(2)}) collective-permute-start(bf16[144,128]{1,0:T(8,128)(2,1)S(1)} %get-tuple-element.99.refs_0_), channel_id=1, source_target_pairs={{0,2},{2,0},{4,6},{6,4},{1,3},{3,1},{5,7},{7,5},{8,10},{10,8},{12,... | collective-permute-start | bytes 110600 | tf_op jit(solution)/shard_map/ppermute | solution.py:555
  82.2 5.8 %collective-permute-start.30 = (bf16[144,128]{1,0:T(8,128)(2,1)S(1)}, bf16[144,128]{1,0:T(8,128)(2,1)S(1)}, u32[]{:S(2)}, u32[]{:S(2)}) collective-permute-start(bf16[144,128]{1,0:T(8,128)(2,1)S(1)} %get-tuple-element.105.refs_0_), channel_id=1, source_target_pairs={{0,6},{2,4},{4,2},{6,0},{1,7},{3,5},{5,3},{7,1},{8,14},{10,12},{12... | collective-permute-start | bytes 110600 | tf_op jit(solution)/shard_map/ppermute | solution.py:555
  84.1 5.3 %collective-permute-start.29 = (bf16[144,128]{1,0:T(8,128)(2,1)S(1)}, bf16[144,128]{1,0:T(8,128)(2,1)S(1)}, u32[]{:S(2)}, u32[]{:S(2)}) collective-permute-start(bf16[144,128]{1,0:T(8,128)(2,1)S(1)} %get-tuple-element.105.refs_0_), channel_id=1, source_target_pairs={{0,4},{2,6},{4,0},{6,2},{1,5},{3,7},{5,1},{7,3},{8,12},{10,14},{12... | collective-permute-start | bytes 110600 | tf_op jit(solution)/shard_map/ppermute | solution.py:555
  84.7 4.7 %collective-permute-start.28 = (bf16[144,128]{1,0:T(8,128)(2,1)S(1)}, bf16[144,128]{1,0:T(8,128)(2,1)S(1)}, u32[]{:S(2)}, u32[]{:S(2)}) collective-permute-start(bf16[144,128]{1,0:T(8,128)(2,1)S(1)} %get-tuple-element.105.refs_0_), channel_id=1, source_target_pairs={{0,2},{2,0},{4,6},{6,4},{1,3},{3,1},{5,7},{7,5},{8,10},{10,8},{12,... | collective-permute-start | bytes 110600 | tf_op jit(solution)/shard_map/ppermute | solution.py:555
  86.6 4.1 %collective-permute-start.33 = (bf16[272,512]{1,0:T(8,128)(2,1)S(1)}, bf16[272,512]{1,0:T(8,128)(2,1)S(1)}, u32[]{:S(2)}, u32[]{:S(2)}) collective-permute-start(bf16[272,512]{1,0:T(8,128)(2,1)S(1)} %get-tuple-element.117), channel_id=1, source_target_pairs={{0,1},{1,0},{2,3},{3,2},{4,5},{5,4},{6,7},{7,6},{8,9},{9,8},{10,11... | collective-permute-start | bytes 835592 | tf_op jit(solution)/shard_map/ppermute | solution.py:561
  86.6 4.1 %collective-permute-start.34 = (bf16[272,512]{1,0:T(8,128)(2,1)S(1)}, bf16[272,512]{1,0:T(8,128)(2,1)S(1)}, u32[]{:S(2)}, u32[]{:S(2)}) collective-permute-start(bf16[272,512]{1,0:T(8,128)(2,1)S(1)} %get-tuple-element.118), channel_id=1, source_target_pairs={{0,1},{1,0},{2,3},{3,2},{4,5},{5,4},{6,7},{7,6},{8,9},{9,8},{10,11... | collective-permute-start | bytes 835592 | tf_op jit(solution)/shard_map/ppermute | solution.py:561
  92.8 9.5 %collective-permute-start.35 = (bf16[272,512]{1,0:T(8,128)(2,1)S(1)}, bf16[272,512]{1,0:T(8,128)(2,1)S(1)}, u32[]{:S(2)}, u32[]{:S(2)}) collective-permute-start(bf16[272,512]{1,0:T(8,128)(2,1)S(1)} %get-tuple-element.120), channel_id=1, source_target_pairs={{0,8},{8,0},{16,24},{24,16},{1,9},{9,1},{17,25},{25,17},{2,10},{10... | collective-permute-start | bytes 835592 | tf_op jit(solution)/shard_map/ppermute | solution.py:558
  94.8 14.4 %collective-permute-start.36 = (bf16[272,512]{1,0:T(8,128)(2,1)S(1)}, bf16[272,512]{1,0:T(8,128)(2,1)S(1)}, u32[]{:S(2)}, u32[]{:S(2)}) collective-permute-start(bf16[272,512]{1,0:T(8,128)(2,1)S(1)} %get-tuple-element.121), channel_id=1, source_target_pairs={{0,16},{8,24},{16,0},{24,8},{1,17},{9,25},{17,1},{25,9},{2,18},{10... | collective-permute-start | bytes 835592 | tf_op jit(solution)/shard_map/ppermute | solution.py:558
  96.0 13.1 %collective-permute-start.37 = (bf16[272,512]{1,0:T(8,128)(2,1)S(1)}, bf16[272,512]{1,0:T(8,128)(2,1)S(1)}, u32[]{:S(2)}, u32[]{:S(2)}) collective-permute-start(bf16[272,512]{1,0:T(8,128)(2,1)S(1)} %get-tuple-element.122), channel_id=1, source_target_pairs={{0,24},{8,16},{16,8},{24,0},{1,25},{9,17},{17,9},{25,1},{2,26},{10... | collective-permute-start | bytes 835592 | tf_op jit(solution)/shard_map/ppermute | solution.py:558
  (8 other events, 17.8 us)

commit v11 on v10

--- a/solution.py
+++ b/solution.py
@@ -234,8 +234,9 @@
         ).astype(BF)
 
 
-def arrange_kernel(length, groups, *refs):
-    received, packed = refs[:groups], refs[groups]
+def arrange_kernel(length, order, *refs):
+    groups = len(order)
+    received, packed = [refs[order.index(place)] for place in range(groups)], refs[groups]
     x, cot, mask, mean, packed_out, tails = refs[groups + 1 :]
     rows, local = x.shape
     place_rows(received, tails, slice(2 * local, None))
@@ -249,7 +250,7 @@
 
 def first_kernel(sections, *refs):
     mine, theirs = refs[:sections], refs[sections : 2 * sections]
-    x, cot, mask, mean, probs, mixed, pay, side, weights, sems = refs[2 * sections :]
+    x, mask, mean, probs, mixed, pay, weights, sems = refs[2 * sections :]
     section, core = lax.axis_index("pipe"), lax.axis_index("core")
     rows = x.shape[0]
     copies = []
@@ -282,6 +283,13 @@
     pay[2 * rows :, :] = fold_grams(layers[0], layers[1])
     for layer in range(2, sections):
         arrived(layer)
+
+
+def side_kernel(weights, cot, side):
+    rows = cot.shape[0]
+    sections = weights.shape[0]
+    own = (weights.shape[2] - 16) // 2
+    layers = [layer_of(weights, layer) for layer in range(sections)]
     side[0:rows, :] = to_rank(cot[...], layers[-1], own).astype(BF)
     for layer in range(2, sections - 1, 2):
         base, height, folded = gram_place(layer, sections - 1, rows)
@@ -356,22 +364,12 @@
     send_forward(x, weights, mixed, pay)
 
 
-def layer_backward(
-    dout, dred, x, mean, mask, weights, weights_before, probs, mixed, reduced, grads, carried, pay
-):
+def layer_backward(dout, dred, x, mean, weights, weights_before, probs, gain_row, carried, pay):
     rows, local = x.shape
     size = block_size(rows)
     own = (weights.shape[2] - 16) // 2
     per_slice = own // HD
-    rank = dred.shape[1]
     factor = lax.rsqrt(mean + EPS)
-    first = dot_tn(dred, mixed[...]).astype(BF)
-    for side in range(weights.shape[1]):
-        grads[side, 0:rank, :] = first[:, side * own : (side + 1) * own]
-    if reduced is not None:
-        second = dot_tn(reduced, dout[...]).astype(BF)
-        for side in range(weights.shape[1]):
-            grads[side, rank : 2 * rank, :] = second[:, side * own : (side + 1) * own]
     back_mixed = [
         from_rank(dred, weights, 0, side).astype(BF) for side in range(weights.shape[1])
     ]
@@ -419,9 +417,8 @@
                 (high.astype(F32), low.astype(F32), jnp.zeros((14, size), F32)), axis=0
             ).astype(BF)
     zeros = jnp.zeros((15, HD), F32)
-    for head in range(local // HD):
-        side, inner = head // per_slice, (head % per_slice) * HD
-        grads[side, 2 * rank : 2 * rank + 16, inner : inner + HD] = jnp.concatenate(
+    for head in heads:
+        gain_row[:, head * HD : (head + 1) * HD] = jnp.concatenate(
             (gain_sums[head], zeros), axis=0
         ).astype(BF)
     if carried is not None:
@@ -431,8 +428,7 @@
 def turn_kernel(count, layer, width, *refs):
     pays, sides, refs = refs[:count], refs[count : 2 * count], refs[2 * count :]
     x_before, mean_before, mask, weights, cot = refs[:5]
-    x, mean, reduced, cross, grads, carried, pay = refs[5:12]
-    probs, mixed = refs[12:]
+    x, mean, reduced, cross, mixed, dred_out, gain_row, carried, pay, probs = refs[5:]
     rows = x.shape[0]
     weights_before, weights = layer_of(weights, layer - 1), layer_of(weights, layer)
     receive_forward(
@@ -440,78 +436,82 @@
         width, x, mean, reduced, cross,
     )
     attend(x, mean[:, 0:1], weights, mask, probs, mixed)
+    dred = total_of(sides, 0, rows).astype(BF)
+    dred_out[...] = dred
+    layer_backward(
+        cot[...], dred, x, mean[:, 0:1], weights, weights_before, probs, gain_row, carried, pay
+    )
     pay[pay.shape[0] - rows :, :] = to_rank(mixed[...], weights, 0).astype(BF)
-    dred = total_of(sides, 0, rows).astype(BF)
-    layer_backward(
-        cot, dred, x, mean[:, 0:1], mask, weights, weights_before, probs, mixed, None, grads,
-        carried, pay,
-    )
-
-
-def split_sides(grads, keep, send):
-    core = lax.axis_index("core")
-    keep[...] = grads[core]
-    send[...] = grads[1 - core]
-
-
-def back_kernel(count, with_last, layer, width, *refs):
-    pays, refs = refs[:count], refs[count:]
-    carried_after, x_after, mean_after, cross_after = refs[:4]
-    x, mean, mask, weights = refs[4:8]
-    refs = refs[8:]
-    weights_before = carried = pay = None
-    if layer:
-        weights_before = layer_of(weights, layer - 1)
-    weights = layer_of(weights, layer)
-    probs, mixed, reduced = refs[:3]
-    refs = refs[3:]
-    if with_last:
-        cot, turn_grads = refs[:2]
-        refs = refs[2:]
-    keep, send = refs[:2]
-    refs = refs[2:]
-    if with_last:
-        last_keep, last_send = refs[:2]
-        refs = refs[2:]
-    if layer:
-        carried, pay = refs[:2]
-        refs = refs[2:]
-    dout, grads = refs
-    rows, local = x.shape
+
+
+def receive_backward(pays, carried_after, x_after, mean_after, cross_after, width):
+    rows = x_after.shape[0]
     size = block_size(rows)
-    own = (weights.shape[2] - 16) // 2
-    rank = reduced.shape[1]
-    dred_parts = []
+    douts, dreds = [], []
     for block in range(rows // size):
         span = slice(block * size, (block + 1) * size)
         base = rows + 16 * block
         lines = total_of(pays, base, base + 16)
-        line = lines[0:1] + lines[1:2]
-        column = jnp.broadcast_to(line, (size, size)).T
+        column = jnp.broadcast_to(lines[0:1] + lines[1:2], (size, size)).T
         factor = lax.rsqrt(mean_after[span, 0:1] + EPS)
         pull = column[:, 0:1] * (factor * factor * factor / width)
-        dred_parts.append(
-            (
-                total_of(pays, block * size, (block + 1) * size) - cross_after[span, :] * pull
-            ).astype(BF)
+        own_total = total_of(pays, block * size, (block + 1) * size)
+        dreds.append((own_total - cross_after[span, :] * pull).astype(BF))
+        douts.append(
+            (carried_after[span, :].astype(F32) - x_after[span, :].astype(F32) * pull).astype(BF)
         )
-        dout[span, :] = (
-            carried_after[span, :].astype(F32) - x_after[span, :].astype(F32) * pull
-        ).astype(BF)
-    dred = dred_parts[0] if len(dred_parts) == 1 else jnp.concatenate(dred_parts, axis=0)
-    if with_last:
-        last_reduced = total_of(pays, pays[0].shape[0] - rows, pays[0].shape[0]).astype(BF)
-        second = dot_tn(last_reduced, cot[...]).astype(BF)
-        for side in range(weights.shape[1]):
-            grads[side, 0:rank, :] = turn_grads[side, 0:rank, :]
-            grads[side, rank : 2 * rank, :] = second[:, side * own : (side + 1) * own]
-            grads[side, 2 * rank :, :] = turn_grads[side, 2 * rank :, :]
-        split_sides(grads, last_keep, last_send)
+    if len(douts) == 1:
+        return douts[0], dreds[0]
+    return jnp.concatenate(douts, axis=0), jnp.concatenate(dreds, axis=0)
+
+
+def back_kernel(count, layer, width, *refs):
+    pays, refs = refs[:count], refs[count:]
+    carried_after, x_after, mean_after, cross_after, x, mean, weights, probs = refs[:8]
+    carried, pay, dout_out, dred_out, gain_row = refs[8:]
+    dout, dred = receive_backward(pays, carried_after, x_after, mean_after, cross_after, width)
     layer_backward(
-        dout, dred, x, mean[:, 0:1], mask, weights, weights_before, probs, mixed, reduced[...],
-        grads, carried, pay,
-    )
-    split_sides(grads, keep, send)
+        dout, dred, x, mean[:, 0:1], layer_of(weights, layer), layer_of(weights, layer - 1), probs,
+        gain_row, carried, pay,
+    )
+    dout_out[...] = dout
+    dred_out[...] = dred
+
+
+def split_grads(first, second, gain_row, wide, keep, send):
+    rank = first.shape[0]
+    own = keep.shape[1]
+    core = lax.axis_index("core")
+    wide[0:rank, :] = first.astype(BF)
+    wide[rank : 2 * rank, :] = second.astype(BF)
+    if gain_row is not None:
+        wide[2 * rank :, :] = gain_row[...]
+    keep[...] = wide[:, pl.ds(pl.multiple_of(core * own, own), own)]
+    send[...] = wide[:, pl.ds(pl.multiple_of((1 - core) * own, own), own)]
+
+
+def grads_kernel(count, *refs):
+    sources, refs = refs[:count], refs[count:]
+    dout, dred, mixed, gain_row, keep, send, wide = refs
+    rows = dout.shape[0]
+    height = sources[0].shape[0]
+    reduced = total_of(sources, height - rows, height).astype(BF)
+    first, second = dot_tn(dred[...], mixed[...]), dot_tn(reduced, dout[...])
+    split_grads(first, second, gain_row, wide, keep, send)
+
+
+def back_first_kernel(count, width, *refs):
+    pays, refs = refs[:count], refs[count:]
+    carried_after, x_after, mean_after, cross_after, x, mean, weights, probs, mixed = refs[:9]
+    reduced, keep, send, wide = refs[9:]
+    rank = reduced.shape[1]
+    dout, dred = receive_backward(pays, carried_after, x_after, mean_after, cross_after, width)
+    first, second = dot_tn(dred, mixed[...]), dot_tn(reduced[...], dout)
+    layer_backward(
+        dout, dred, x, mean[:, 0:1], layer_of(weights, 0), None, probs, wide.at[pl.ds(2 * rank, 16)],
+        None, None,
+    )
+    split_grads(first, second, None, wide, keep, send)
 
 
 def combine_kernel(sections, *refs):
@@ -567,8 +567,8 @@
         tokens, cotangents, starts, counts, layer_gains, first_map, second_map, groups, micro_local
     )
     mine = [packed] + [across(packed, distance) for distance in range(1, sections)]
-    received = [token_parts[0]]
-    received += [shifted(token_parts[shift], shift) for shift in range(1, groups)]
+    order = [0] + list(range(groups - 1, 0, -1))
+    received = [token_parts[0]] + [shifted(token_parts[place], place) for place in order[1:]]
     received, mine = lax.optimization_barrier((received, mine))
     theirs = [swapped(part) for part in mine]
 
@@ -596,7 +596,7 @@
         )(*operands)
 
     x, cot, mask, mean, mine[0] = call(
-        functools.partial(arrange_kernel, length, groups),
+        functools.partial(arrange_kernel, length, order),
         (*received, mine[0]),
         vmem_specs(groups + 1),
         [
@@ -611,23 +611,18 @@
     )
     last_gram = gram_place(top - 1, top, rows)
     side_rows = last_gram[0] + last_gram[1]
-    probs, mixed, pay, side, weights = call(
+    probs, mixed, pay, weights = call(
         functools.partial(first_kernel, sections),
-        (*mine, *theirs, x, cot, mask, mean),
-        vmem_specs(2 * sections + 4),
-        [
-            probs_shape,
-            wide_shape,
-            shaped((2 * rows + FOLDED, HD)),
-            shaped((side_rows, HD)),
-            weights_shape,
-        ],
+        (*mine, *theirs, x, mask, mean),
+        vmem_specs(2 * sections + 3),
+        [probs_shape, wide_shape, shaped((2 * rows + FOLDED, HD)), weights_shape],
         "forward_first",
         scratch_shapes=[pltpu.SemaphoreType.DMA((sections, sides))],
     )
     xs, means, reduceds, crosses = [x], [mean], [], [None]
     all_probs, all_mixed = [probs], [mixed]
     first_pays = pays = exchange(pay)
+    side = call(side_kernel, (weights, cot), vmem_specs(2), [shaped((side_rows, HD))], "side")[0]
     arrived = exchange(side)
     for layer in range(1, top):
         operands = (*pays, *((), first_pays, arrived)[min(layer, 3) - 1])
@@ -656,7 +651,9 @@
         pays = exchange(pay)
 
     back_rows = rows + 16 * blocks
-    x, mean, reduced, cross, turn_grads, carried, pay = call(
+    gain_shape = shaped((16, local))
+    wide_scratch = [pltpu.VMEM((2 * rank + 16, local), BF)]
+    x, mean, reduced, cross, mixed, dred, gain_row, carried, pay = call(
         functools.partial(turn_kernel, groups, top, float(width)),
         (*pays, *arrived, xs[-1], means[-1], mask, weights, cot),
         vmem_specs(2 * groups + 5),
@@ -665,54 +662,72 @@
             mean_shape,
             rank_shape,
             cross_shape,
-            shaped(grads_shape),
+            wide_shape,
+            rank_shape,
+            gain_shape,
             wide_shape,
             shaped((back_rows + rows, HD)),
         ],
         "turn",
-        scratch_shapes=[
-            pltpu.VMEM(probs_shape.shape, BF),
-            pltpu.VMEM(wide_shape.shape, BF),
-        ],
+        scratch_shapes=[pltpu.VMEM(probs_shape.shape, BF)],
     )
     xs.append(x)
     means.append(mean)
     reduceds.append(reduced)
     crosses.append(cross)
-
-    kept, taken = [None] * sections, [None] * sections
-    for layer in range(top - 1, -1, -1):
-        pays = exchange(pay)
-        with_last = layer == top - 1
-        to_first = layer == 0
+    all_mixed.append(mixed)
+
+    def gradients(layer, sources, dout, dred, gain_row):
+        operands = (*sources, dout, dred, all_mixed[layer], gain_row)
+        keep, send = call(
+            functools.partial(grads_kernel, len(sources)),
+            operands,
+            vmem_specs(len(operands)),
+            [half_shape] * 2,
+            "weight_grads",
+            scratch_shapes=wide_scratch,
+        )
+        return keep, send
+
+    pays = exchange(pay)
+    halves = [None] * sections
+    waiting = [(top, pays, cot, dred, gain_row)]
+    for layer in range(top - 1, 0, -1):
         operands = (
             *pays, carried, xs[layer + 1], means[layer + 1], crosses[layer + 1],
-            xs[layer], means[layer], mask, weights,
+            xs[layer], means[layer], weights, all_probs[layer],
         )
-        operands += (all_probs[layer], all_mixed[layer], reduceds[layer])
-        outs = [half_shape] * 2
-        if with_last:
-            operands += (cot, turn_grads)
-            outs += [half_shape] * 2
-        if not to_first:
-            outs += [wide_shape, shaped((back_rows, HD))]
-        result = call(
-            functools.partial(back_kernel, groups, with_last, layer, float(width)),
+        carried, pay, dout, dred, gain_row = call(
+            functools.partial(back_kernel, groups, layer, float(width)),
             operands,
             vmem_specs(len(operands)),
-            outs,
+            [wide_shape, shaped((back_rows, HD)), wide_shape, rank_shape, gain_shape],
             "backward",
-            scratch_shapes=[pltpu.VMEM(wide_shape.shape, BF), pltpu.VMEM(grads_shape, BF)],
         )
-        kept[layer], taken[layer] = result[0], swapped(result[1])
-        if with_last:
-            kept[top], taken[top] = result[2], swapped(result[3])
-        if not to_first:
-            carried, pay = result[-2:]
+        pays = exchange(pay)
+        waiting.append((layer, [reduceds[layer]], dout, dred, gain_row))
+        done = [gradients(*item) for item in waiting]
+        pays, done = lax.optimization_barrier((pays, done))
+        for item, (keep, send) in zip(waiting, done):
+            halves[item[0]] = (keep, swapped(send))
+        waiting = []
+    operands = (
+        *pays, carried, xs[1], means[1], crosses[1], xs[0], means[0], weights, all_probs[0],
+        all_mixed[0], reduceds[0],
+    )
+    keep, send = call(
+        functools.partial(back_first_kernel, groups, float(width)),
+        operands,
+        vmem_specs(len(operands)),
+        [half_shape] * 2,
+        "backward_first",
+        scratch_shapes=wide_scratch,
+    )
+    halves[0] = (keep, swapped(send))
 
     parts = call(
         functools.partial(combine_kernel, sections),
-        (*kept, *taken),
+        [pair[side] for side in range(2) for pair in halves],
         vmem_specs(2 * sections),
         [half_shape] * sections,
         "combine",

time: 110 us -> 109 us (level)
  waiting for transfers between devices: 44.9 us -> 39.1 us
  starting transfers between devices: 47.4 us -> 52 us
    ppermute x24, waiting for transfers between devices: 30.6 us -> 24.1 us  [shifted(): return lax.ppermute(value, 'z', [(i, i ^ shift) for i in range(groups)])]
    ppermute x24, starting transfers between devices: 38.7 us -> 42.8 us  [shifted(): return lax.ppermute(value, 'z', [(i, i ^ shift) for i in range(groups)])]
    pallas_call x10 -> x14, Pallas kernels: 12.9 us -> 13.2 us  [call(): pl.pallas_call(kernel, in_specs=specs, out_specs=vmem_specs(len(outs)), o...]
  transfers between devices with their start and end apart: 38 -> 38, of which waited for: 15 -> 20; matrix products, arithmetic and copies ran while one was open for 0% -> 0% of each run, Pallas kernels for 3% -> 4%
where the time goes in v11:
time: 109 us
  starting transfers between devices  52 us (48%)
  waiting for transfers between devices  39.1 us (36%)
  Pallas kernels  15.5 us (14%)
  local copies, waits for them, and re-layouts  1.86 us (2%)
    ppermute x24, starting transfers between devices, shifted(): return lax.ppermute(value, 'z', [(i, i ^ shift) for i in range(groups)])  42.8 us
    ppermute x24, waiting for transfers between devices, shifted(): return lax.ppermute(value, 'z', [(i, i ^ shift) for i in range(groups)])  24.1 us
    ppermute x6, waiting for transfers between devices, across(): lax.ppermute(value, 'pipe', [(i, i ^ distance) for i in range(sections)])  13.5 us
    pallas_call x14, Pallas kernels, call(): pl.pallas_call(kernel, in_specs=specs, out_specs=vmem_specs(len(outs)), o...  13.2 us
    ppermute x6, starting transfers between devices, across(): lax.ppermute(value, 'pipe', [(i, i ^ distance) for i in range(sections)])  7.04 us
    pallas_call x1, Pallas kernels, pack(): pl.pallas_call(functools.partial(pack_kernel, groups, micro_local), in_sp...  2.28 us
  transfers between devices with their start and end apart: 38, of which 20 were waited for; matrix products, arithmetic and copies ran while one was open for 0% of the time, Pallas kernels for 4%

profile of v11, /device:TPU:0, one launch (start us, length us, event | category | flops | bytes accessed | tf_op | source)
XLA Modules:
  0.0 109.2 jit_solution(1323488917416789138)
XLA Ops:
  0.6 2.3 %pack.1 = (bf16[32,2176]{1,0:T(8,128)(2,1)}, bf16[32,2176]{1,0:T(8,128)(2,1)}, bf16[32,2176]{1,0:T(8,128)(2,1)}, bf16[32,2176]{1,0:T(8,128)(2,1)}, bf16[1040,128]{1,0:T(8,128)(2,1)}) custom-call(bf16[2,2,32,4096]{3,2,1,0:T(8,128)(2,1)} %refs_0_.1, bf16[2,2,32,4096]{3,2,1,0:T(8,128)(2,1)} %refs_1_.1, s32[2,2,4]{2,1,0:T(2,128)} %refs_2_.1, s32[2,2]{1,0:T(2,128)} %refs_3_.1, ...), custom_call_target="tpu_custom_call" | custom-call | tf_op jit(solution)/shard_map/pack/pallas_call | solution.py:124
  2.9 5.1 %collective-permute-start = (bf16[32,2176]{1,0:T(8,128)(2,1)}, bf16[32,2176]{1,0:T(8,128)(2,1)S(1)}, u32[]{:S(2)}, u32[]{:S(2)}) collective-permute-start(bf16[32,2176]{1,0:T(8,128)(2,1)} %get-tuple-element.85), channel_id=1, source_target_pairs={{0,6},{2,4},{4,2},{6,0},{1,7},{3,5},{5,3},{7,1},{8,14},{10,12},{12... | collective-permute-start | bytes 417800 | tf_op jit(solution)/shard_map/ppermute | solution.py:555
  8.0 2.4 %collective-permute-start.5 = (bf16[1040,128]{1,0:T(8,128)(2,1)}, bf16[1040,128]{1,0:T(8,128)(2,1)S(1)}, u32[]{:S(2)}, u32[]{:S(2)}) collective-permute-start(bf16[1040,128]{1,0:T(8,128)(2,1)} %get-tuple-element.93.refs_4_), channel_id=1, source_target_pairs={{0,24},{8,16},{16,8},{24,0},{1,25},{9,17},{17,9},{25,1},{2,26},{10... | collective-permute-start | bytes 798728 | tf_op jit(solution)/shard_map/ppermute | solution.py:558
  12.0 6.5 %collective-permute-start.2 = (bf16[32,2176]{1,0:T(8,128)(2,1)}, bf16[32,2176]{1,0:T(8,128)(2,1)S(1)}, u32[]{:S(2)}, u32[]{:S(2)}) collective-permute-start(bf16[32,2176]{1,0:T(8,128)(2,1)} %get-tuple-element.87), channel_id=1, source_target_pairs={{0,2},{2,0},{4,6},{6,4},{1,3},{3,1},{5,7},{7,5},{8,10},{10,8},{12,... | collective-permute-start | bytes 417800 | tf_op jit(solution)/shard_map/ppermute | solution.py:555
  18.6 1.6 %collective-permute-done.1.refs_2_ = bf16[32,2176]{1,0:T(8,128)(2,1)S(1)} collective-permute-done((bf16[32,2176]{1,0:T(8,128)(2,1)}, bf16[32,2176]{1,0:T(8,128)(2,1)S(1)}, u32[]{:S(2)}, u32[]{:S(2)}) %collective-permute-start.1) | collective-permute-done | bytes 139296 | tf_op jit(solution)/shard_map/ppermute | solution.py:555
  20.1 1.7 %collective-permute-done.2.refs_3_ = bf16[32,2176]{1,0:T(8,128)(2,1)S(1)} collective-permute-done((bf16[32,2176]{1,0:T(8,128)(2,1)}, bf16[32,2176]{1,0:T(8,128)(2,1)S(1)}, u32[]{:S(2)}, u32[]{:S(2)}) %collective-permute-start.2) | collective-permute-done | bytes 139296 | tf_op jit(solution)/shard_map/ppermute | solution.py:555
  26.0 1.6 %forward_first.1 = (bf16[1,8,128,128]{3,2,1,0:T(8,128)(2,1)S(1)}, bf16[128,1024]{1,0:T(8,128)(2,1)S(1)}, bf16[400,128]{1,0:T(8,128)(2,1)S(1)}, bf16[4,2,1040,128]{3,2,1,0:T(8,128)(2,1)S(1)}) custom-call(bf16[1040,128]{1,0:T(8,128)(2,1)S(1)} %get-tuple-element.94.refs_0_, bf16[1040,128]{1,0:T(8,128)(2,1)S(1)} %collective-permute-done.3.refs_1_, ...), custom_call_target="tpu_custom_call" | custom-call | tf_op jit(solution)/shard_map/forward_first/pallas_call | solution.py:588
  27.6 1.6 %collective-permute-start.12 = (bf16[400,128]{1,0:T(8,128)(2,1)S(1)}, bf16[400,128]{1,0:T(8,128)(2,1)S(1)}, u32[]{:S(2)}, u32[]{:S(2)}) collective-permute-start(bf16[400,128]{1,0:T(8,128)(2,1)S(1)} %get-tuple-element.101.refs_0_.refs_4_), channel_id=1, source_target_pairs={{0,6},{2,4},{4,2},{6,0},{1,7},{3,5},{5,3},{7,1},{8,14},{10,12},{12... | collective-permute-start | bytes 307208 | tf_op jit(solution)/shard_map/ppermute | solution.py:555
  30.2 1.8 %collective-permute-start.10 = (bf16[400,128]{1,0:T(8,128)(2,1)S(1)}, bf16[400,128]{1,0:T(8,128)(2,1)S(1)}, u32[]{:S(2)}, u32[]{:S(2)}) collective-permute-start(bf16[400,128]{1,0:T(8,128)(2,1)S(1)} %get-tuple-element.101.refs_0_.refs_4_), channel_id=1, source_target_pairs={{0,2},{2,0},{4,6},{6,4},{1,3},{3,1},{5,7},{7,5},{8,10},{10,8},{12,... | collective-permute-start | bytes 307208 | tf_op jit(solution)/shard_map/ppermute | solution.py:555
  32.0 3.3 %collective-permute-done.12.refs_3_.refs_7_ = bf16[400,128]{1,0:T(8,128)(2,1)S(1)} collective-permute-done((bf16[400,128]{1,0:T(8,128)(2,1)S(1)}, bf16[400,128]{1,0:T(8,128)(2,1)S(1)}, u32[]{:S(2)}, u32[]{:S(2)}) %collective-permute-start.12) | collective-permute-done | bytes 102432 | tf_op jit(solution)/shard_map/ppermute | solution.py:555
  35.3 4.3 %collective-permute-done.11.refs_2_.refs_6_ = bf16[400,128]{1,0:T(8,128)(2,1)S(1)} collective-permute-done((bf16[400,128]{1,0:T(8,128)(2,1)S(1)}, bf16[400,128]{1,0:T(8,128)(2,1)S(1)}, u32[]{:S(2)}, u32[]{:S(2)}) %collective-permute-start.11) | collective-permute-done | bytes 102432 | tf_op jit(solution)/shard_map/ppermute | solution.py:555
  41.0 2.5 %collective-permute-start.15 = (bf16[256,128]{1,0:T(8,128)(2,1)S(1)}, bf16[256,128]{1,0:T(8,128)(2,1)S(1)}, u32[]{:S(2)}, u32[]{:S(2)}) collective-permute-start(bf16[256,128]{1,0:T(8,128)(2,1)S(1)} %get-tuple-element.103.refs_0_), channel_id=1, source_target_pairs={{0,6},{2,4},{4,2},{6,0},{1,7},{3,5},{5,3},{7,1},{8,14},{10,12},{12... | collective-permute-start | bytes 196616 | tf_op jit(solution)/shard_map/ppermute | solution.py:555
  43.4 2.0 %collective-permute-start.13 = (bf16[256,128]{1,0:T(8,128)(2,1)S(1)}, bf16[256,128]{1,0:T(8,128)(2,1)S(1)}, u32[]{:S(2)}, u32[]{:S(2)}) collective-permute-start(bf16[256,128]{1,0:T(8,128)(2,1)S(1)} %get-tuple-element.103.refs_0_), channel_id=1, source_target_pairs={{0,2},{2,0},{4,6},{6,4},{1,3},{3,1},{5,7},{7,5},{8,10},{10,8},{12,... | collective-permute-start | bytes 196616 | tf_op jit(solution)/shard_map/ppermute | solution.py:555
  45.7 2.5 %collective-permute-start.21 = (bf16[256,128]{1,0:T(8,128)(2,1)S(1)}, bf16[256,128]{1,0:T(8,128)(2,1)S(1)}, u32[]{:S(2)}, u32[]{:S(2)}) collective-permute-start(bf16[256,128]{1,0:T(8,128)(2,1)S(1)} %side.1.refs_4_), channel_id=1, source_target_pairs={{0,6},{2,4},{4,2},{6,0},{1,7},{3,5},{5,3},{7,1},{8,14},{10,12},{12... | collective-permute-start | bytes 196616 | tf_op jit(solution)/shard_map/ppermute | solution.py:555
  48.2 2.0 %collective-permute-start.19 = (bf16[256,128]{1,0:T(8,128)(2,1)S(1)}, bf16[256,128]{1,0:T(8,128)(2,1)S(1)}, u32[]{:S(2)}, u32[]{:S(2)}) collective-permute-start(bf16[256,128]{1,0:T(8,128)(2,1)S(1)} %side.1.refs_4_), channel_id=1, source_target_pairs={{0,2},{2,0},{4,6},{6,4},{1,3},{3,1},{5,7},{7,5},{8,10},{10,8},{12,... | collective-permute-start | bytes 196616 | tf_op jit(solution)/shard_map/ppermute | solution.py:555
  52.2 2.6 %collective-permute-start.18 = (bf16[256,128]{1,0:T(8,128)(2,1)S(1)}, bf16[256,128]{1,0:T(8,128)(2,1)S(1)}, u32[]{:S(2)}, u32[]{:S(2)}) collective-permute-start(bf16[256,128]{1,0:T(8,128)(2,1)S(1)} %get-tuple-element.106.refs_0_), channel_id=1, source_target_pairs={{0,6},{2,4},{4,2},{6,0},{1,7},{3,5},{5,3},{7,1},{8,14},{10,12},{12... | collective-permute-start | bytes 196616 | tf_op jit(solution)/shard_map/ppermute | solution.py:555
  54.8 1.9 %collective-permute-start.16 = (bf16[256,128]{1,0:T(8,128)(2,1)S(1)}, bf16[256,128]{1,0:T(8,128)(2,1)S(1)}, u32[]{:S(2)}, u32[]{:S(2)}) collective-permute-start(bf16[256,128]{1,0:T(8,128)(2,1)S(1)} %get-tuple-element.106.refs_0_), channel_id=1, source_target_pairs={{0,2},{2,0},{4,6},{6,4},{1,3},{3,1},{5,7},{7,5},{8,10},{10,8},{12,... | collective-permute-start | bytes 196616 | tf_op jit(solution)/shard_map/ppermute | solution.py:555
  56.6 2.1 %collective-permute-done.18.refs_3_ = bf16[256,128]{1,0:T(8,128)(2,1)S(1)} collective-permute-done((bf16[256,128]{1,0:T(8,128)(2,1)S(1)}, bf16[256,128]{1,0:T(8,128)(2,1)S(1)}, u32[]{:S(2)}, u32[]{:S(2)}) %collective-permute-start.18) | collective-permute-done | bytes 65568 | tf_op jit(solution)/shard_map/ppermute | solution.py:555
  58.8 1.6 %collective-permute-done.17.refs_2_ = bf16[256,128]{1,0:T(8,128)(2,1)S(1)} collective-permute-done((bf16[256,128]{1,0:T(8,128)(2,1)S(1)}, bf16[256,128]{1,0:T(8,128)(2,1)S(1)}, u32[]{:S(2)}, u32[]{:S(2)}) %collective-permute-start.17) | collective-permute-done | bytes 65568 | tf_op jit(solution)/shard_map/ppermute | solution.py:555
  60.4 2.1 %turn.1 = (bf16[128,1024]{1,0:T(8,128)(2,1)S(1)}, f32[128,128]{1,0:T(8,128)S(1)}, bf16[128,128]{1,0:T(8,128)(2,1)S(1)}, f32[128,128]{1,0:T(8,128)S(1)}, bf16[128...) custom-call(bf16[256,128]{1,0:T(8,128)(2,1)S(1)} %get-tuple-element., ...), custom_call_target="tpu_custom_call" | custom-call | tf_op jit(solution)/shard_map/turn/pallas_call | solution.py:588
  62.4 2.4 %collective-permute-start.24 = (bf16[272,128]{1,0:T(8,128)(2,1)S(1)}, bf16[272,128]{1,0:T(8,128)(2,1)S(1)}, u32[]{:S(2)}, u32[]{:S(2)}) collective-permute-start(bf16[272,128]{1,0:T(8,128)(2,1)S(1)} %get-tuple-element.110.refs_0_), channel_id=1, source_target_pairs={{0,6},{2,4},{4,2},{6,0},{1,7},{3,5},{5,3},{7,1},{8,14},{10,12},{12... | collective-permute-start | bytes 208904 | tf_op jit(solution)/shard_map/ppermute | solution.py:555
  64.9 2.0 %collective-permute-start.22 = (bf16[272,128]{1,0:T(8,128)(2,1)S(1)}, bf16[272,128]{1,0:T(8,128)(2,1)S(1)}, u32[]{:S(2)}, u32[]{:S(2)}) collective-permute-start(bf16[272,128]{1,0:T(8,128)(2,1)S(1)} %get-tuple-element.110.refs_0_), channel_id=1, source_target_pairs={{0,2},{2,0},{4,6},{6,4},{1,3},{3,1},{5,7},{7,5},{8,10},{10,8},{12,... | collective-permute-start | bytes 208904 | tf_op jit(solution)/shard_map/ppermute | solution.py:555
  66.9 2.0 %collective-permute-done.24.refs_3_ = bf16[272,128]{1,0:T(8,128)(2,1)S(1)} collective-permute-done((bf16[272,128]{1,0:T(8,128)(2,1)S(1)}, bf16[272,128]{1,0:T(8,128)(2,1)S(1)}, u32[]{:S(2)}, u32[]{:S(2)}) %collective-permute-start.24) | collective-permute-done | bytes 69664 | tf_op jit(solution)/shard_map/ppermute | solution.py:555
  68.9 2.4 %collective-permute-done.23.refs_2_ = bf16[272,128]{1,0:T(8,128)(2,1)S(1)} collective-permute-done((bf16[272,128]{1,0:T(8,128)(2,1)S(1)}, bf16[272,128]{1,0:T(8,128)(2,1)S(1)}, u32[]{:S(2)}, u32[]{:S(2)}) %collective-permute-start.23) | collective-permute-done | bytes 69664 | tf_op jit(solution)/shard_map/ppermute | solution.py:555
  72.5 2.6 %collective-permute-start.27 = (bf16[144,128]{1,0:T(8,128)(2,1)S(1)}, bf16[144,128]{1,0:T(8,128)(2,1)S(1)}, u32[]{:S(2)}, u32[]{:S(2)}) collective-permute-start(bf16[144,128]{1,0:T(8,128)(2,1)S(1)} %get-tuple-element.129.refs_0_), channel_id=1, source_target_pairs={{0,6},{2,4},{4,2},{6,0},{1,7},{3,5},{5,3},{7,1},{8,14},{10,12},{12... | collective-permute-start | bytes 110600 | tf_op jit(solution)/shard_map/ppermute | solution.py:555
  75.1 1.9 %collective-permute-start.25 = (bf16[144,128]{1,0:T(8,128)(2,1)S(1)}, bf16[144,128]{1,0:T(8,128)(2,1)S(1)}, u32[]{:S(2)}, u32[]{:S(2)}) collective-permute-start(bf16[144,128]{1,0:T(8,128)(2,1)S(1)} %get-tuple-element.129.refs_0_), channel_id=1, source_target_pairs={{0,2},{2,0},{4,6},{6,4},{1,3},{3,1},{5,7},{7,5},{8,10},{10,8},{12,... | collective-permute-start | bytes 110600 | tf_op jit(solution)/shard_map/ppermute | solution.py:555
  78.3 1.6 %collective-permute-done.26.refs_2_ = bf16[144,128]{1,0:T(8,128)(2,1)S(1)} collective-permute-done((bf16[144,128]{1,0:T(8,128)(2,1)S(1)}, bf16[144,128]{1,0:T(8,128)(2,1)S(1)}, u32[]{:S(2)}, u32[]{:S(2)}) %collective-permute-start.26) | collective-permute-done | bytes 36896 | tf_op jit(solution)/shard_map/ppermute | solution.py:555
  81.2 1.8 %collective-permute-start.30 = (bf16[144,128]{1,0:T(8,128)(2,1)S(1)}, bf16[144,128]{1,0:T(8,128)(2,1)S(1)}, u32[]{:S(2)}, u32[]{:S(2)}) collective-permute-start(bf16[144,128]{1,0:T(8,128)(2,1)S(1)} %get-tuple-element.144.refs_0_), channel_id=1, source_target_pairs={{0,6},{2,4},{4,2},{6,0},{1,7},{3,5},{5,3},{7,1},{8,14},{10,12},{12... | collective-permute-start | bytes 110600 | tf_op jit(solution)/shard_map/ppermute | solution.py:555
  83.7 2.0 %collective-permute-start.28 = (bf16[144,128]{1,0:T(8,128)(2,1)S(1)}, bf16[144,128]{1,0:T(8,128)(2,1)S(1)}, u32[]{:S(2)}, u32[]{:S(2)}) collective-permute-start(bf16[144,128]{1,0:T(8,128)(2,1)S(1)} %get-tuple-element.144.refs_0_), channel_id=1, source_target_pairs={{0,2},{2,0},{4,6},{6,4},{1,3},{3,1},{5,7},{7,5},{8,10},{10,8},{12,... | collective-permute-start | bytes 110600 | tf_op jit(solution)/shard_map/ppermute | solution.py:555
  93.7 1.9 %collective-permute-start.36 = (bf16[272,512]{1,0:T(8,128)(2,1)S(1)}, bf16[272,512]{1,0:T(8,128)(2,1)S(1)}, u32[]{:S(2)}, u32[]{:S(2)}) collective-permute-start(bf16[272,512]{1,0:T(8,128)(2,1)S(1)} %get-tuple-element.163), channel_id=1, source_target_pairs={{0,16},{8,24},{16,0},{24,8},{1,17},{9,25},{17,1},{25,9},{2,18},{10... | collective-permute-start | bytes 835592 | tf_op jit(solution)/shard_map/ppermute | solution.py:558
  95.7 6.0 %collective-permute-done.35.refs_1_ = bf16[272,512]{1,0:T(8,128)(2,1)S(1)} collective-permute-done((bf16[272,512]{1,0:T(8,128)(2,1)S(1)}, bf16[272,512]{1,0:T(8,128)(2,1)S(1)}, u32[]{:S(2)}, u32[]{:S(2)}) %collective-permute-start.35) | collective-permute-done | bytes 278560 | tf_op jit(solution)/shard_map/ppermute | solution.py:558
  101.7 6.5 %collective-permute-done.36.refs_2_ = bf16[272,512]{1,0:T(8,128)(2,1)S(1)} collective-permute-done((bf16[272,512]{1,0:T(8,128)(2,1)S(1)}, bf16[272,512]{1,0:T(8,128)(2,1)S(1)}, u32[]{:S(2)}, u32[]{:S(2)}) %collective-permute-start.36) | collective-permute-done | bytes 278560 | tf_op jit(solution)/shard_map/ppermute | solution.py:558
  (63 shorter events, 24.1 us)
Async XLA Ops:
  2.9 9.1 %collective-permute-start = (bf16[32,2176]{1,0:T(8,128)(2,1)}, bf16[32,2176]{1,0:T(8,128)(2,1)S(1)}, u32[]{:S(2)}, u32[]{:S(2)}) collective-permute-start(bf16[32,2176]{1,0:T(8,128)(2,1)} %get-tuple-element.85), channel_id=1, source_target_pairs={{0,6},{2,4},{4,2},{6,0},{1,7},{3,5},{5,3},{7,1},{8,14},{10,12},{12... | collective-permute-start | bytes 417800 | tf_op jit(solution)/shard_map/ppermute | solution.py:555
  8.0 13.8 %collective-permute-start.5 = (bf16[1040,128]{1,0:T(8,128)(2,1)}, bf16[1040,128]{1,0:T(8,128)(2,1)S(1)}, u32[]{:S(2)}, u32[]{:S(2)}) collective-permute-start(bf16[1040,128]{1,0:T(8,128)(2,1)} %get-tuple-element.93.refs_4_), channel_id=1, source_target_pairs={{0,24},{8,16},{16,8},{24,0},{1,25},{9,17},{17,9},{25,1},{2,26},{10... | collective-permute-start | bytes 798728 | tf_op jit(solution)/shard_map/ppermute | solution.py:558
  10.5 12.2 %collective-permute-start.4 = (bf16[1040,128]{1,0:T(8,128)(2,1)}, bf16[1040,128]{1,0:T(8,128)(2,1)S(1)}, u32[]{:S(2)}, u32[]{:S(2)}) collective-permute-start(bf16[1040,128]{1,0:T(8,128)(2,1)} %get-tuple-element.93.refs_4_), channel_id=1, source_target_pairs={{0,16},{8,24},{16,0},{24,8},{1,17},{9,25},{17,1},{25,9},{2,18},{10... | collective-permute-start | bytes 798728 | tf_op jit(solution)/shard_map/ppermute | solution.py:558
  11.0 11.8 %collective-permute-start.3 = (bf16[1040,128]{1,0:T(8,128)(2,1)}, bf16[1040,128]{1,0:T(8,128)(2,1)S(1)}, u32[]{:S(2)}, u32[]{:S(2)}) collective-permute-start(bf16[1040,128]{1,0:T(8,128)(2,1)} %get-tuple-element.93.refs_4_), channel_id=1, source_target_pairs={{0,8},{8,0},{16,24},{24,16},{1,9},{9,1},{17,25},{25,17},{2,10},{10... | collective-permute-start | bytes 798728 | tf_op jit(solution)/shard_map/ppermute | solution.py:558
  11.5 8.6 %collective-permute-start.1 = (bf16[32,2176]{1,0:T(8,128)(2,1)}, bf16[32,2176]{1,0:T(8,128)(2,1)S(1)}, u32[]{:S(2)}, u32[]{:S(2)}) collective-permute-start(bf16[32,2176]{1,0:T(8,128)(2,1)} %get-tuple-element.86), channel_id=1, source_target_pairs={{0,4},{2,6},{4,0},{6,2},{1,5},{3,7},{5,1},{7,3},{8,12},{10,14},{12... | collective-permute-start | bytes 417800 | tf_op jit(solution)/shard_map/ppermute | solution.py:555
  12.0 9.8 %collective-permute-start.2 = (bf16[32,2176]{1,0:T(8,128)(2,1)}, bf16[32,2176]{1,0:T(8,128)(2,1)S(1)}, u32[]{:S(2)}, u32[]{:S(2)}) collective-permute-start(bf16[32,2176]{1,0:T(8,128)(2,1)} %get-tuple-element.87), channel_id=1, source_target_pairs={{0,2},{2,0},{4,6},{6,4},{1,3},{3,1},{5,7},{7,5},{8,10},{10,8},{12,... | collective-permute-start | bytes 417800 | tf_op jit(solution)/shard_map/ppermute | solution.py:555
  27.6 7.7 %collective-permute-start.12 = (bf16[400,128]{1,0:T(8,128)(2,1)S(1)}, bf16[400,128]{1,0:T(8,128)(2,1)S(1)}, u32[]{:S(2)}, u32[]{:S(2)}) collective-permute-start(bf16[400,128]{1,0:T(8,128)(2,1)S(1)} %get-tuple-element.101.refs_0_.refs_4_), channel_id=1, source_target_pairs={{0,6},{2,4},{4,2},{6,0},{1,7},{3,5},{5,3},{7,1},{8,14},{10,12},{12... | collective-permute-start | bytes 307208 | tf_op jit(solution)/shard_map/ppermute | solution.py:555
  29.1 10.5 %collective-permute-start.11 = (bf16[400,128]{1,0:T(8,128)(2,1)S(1)}, bf16[400,128]{1,0:T(8,128)(2,1)S(1)}, u32[]{:S(2)}, u32[]{:S(2)}) collective-permute-start(bf16[400,128]{1,0:T(8,128)(2,1)S(1)} %get-tuple-element.101.refs_0_.refs_4_), channel_id=1, source_target_pairs={{0,4},{2,6},{4,0},{6,2},{1,5},{3,7},{5,1},{7,3},{8,12},{10,14},{12... | collective-permute-start | bytes 307208 | tf_op jit(solution)/shard_map/ppermute | solution.py:555
  30.2 9.4 %collective-permute-start.10 = (bf16[400,128]{1,0:T(8,128)(2,1)S(1)}, bf16[400,128]{1,0:T(8,128)(2,1)S(1)}, u32[]{:S(2)}, u32[]{:S(2)}) collective-permute-start(bf16[400,128]{1,0:T(8,128)(2,1)S(1)} %get-tuple-element.101.refs_0_.refs_4_), channel_id=1, source_target_pairs={{0,2},{2,0},{4,6},{6,4},{1,3},{3,1},{5,7},{7,5},{8,10},{10,8},{12,... | collective-permute-start | bytes 307208 | tf_op jit(solution)/shard_map/ppermute | solution.py:555
  41.0 7.2 %collective-permute-start.15 = (bf16[256,128]{1,0:T(8,128)(2,1)S(1)}, bf16[256,128]{1,0:T(8,128)(2,1)S(1)}, u32[]{:S(2)}, u32[]{:S(2)}) collective-permute-start(bf16[256,128]{1,0:T(8,128)(2,1)S(1)} %get-tuple-element.103.refs_0_), channel_id=1, source_target_pairs={{0,6},{2,4},{4,2},{6,0},{1,7},{3,5},{5,3},{7,1},{8,14},{10,12},{12... | collective-permute-start | bytes 196616 | tf_op jit(solution)/shard_map/ppermute | solution.py:555
  43.4 7.4 %collective-permute-start.14 = (bf16[256,128]{1,0:T(8,128)(2,1)S(1)}, bf16[256,128]{1,0:T(8,128)(2,1)S(1)}, u32[]{:S(2)}, u32[]{:S(2)}) collective-permute-start(bf16[256,128]{1,0:T(8,128)(2,1)S(1)} %get-tuple-element.103.refs_0_), channel_id=1, source_target_pairs={{0,4},{2,6},{4,0},{6,2},{1,5},{3,7},{5,1},{7,3},{8,12},{10,14},{12... | collective-permute-start | bytes 196616 | tf_op jit(solution)/shard_map/ppermute | solution.py:555
  43.4 7.4 %collective-permute-start.13 = (bf16[256,128]{1,0:T(8,128)(2,1)S(1)}, bf16[256,128]{1,0:T(8,128)(2,1)S(1)}, u32[]{:S(2)}, u32[]{:S(2)}) collective-permute-start(bf16[256,128]{1,0:T(8,128)(2,1)S(1)} %get-tuple-element.103.refs_0_), channel_id=1, source_target_pairs={{0,2},{2,0},{4,6},{6,4},{1,3},{3,1},{5,7},{7,5},{8,10},{10,8},{12,... | collective-permute-start | bytes 196616 | tf_op jit(solution)/shard_map/ppermute | solution.py:555
  45.7 9.1 %collective-permute-start.21 = (bf16[256,128]{1,0:T(8,128)(2,1)S(1)}, bf16[256,128]{1,0:T(8,128)(2,1)S(1)}, u32[]{:S(2)}, u32[]{:S(2)}) collective-permute-start(bf16[256,128]{1,0:T(8,128)(2,1)S(1)} %side.1.refs_4_), channel_id=1, source_target_pairs={{0,6},{2,4},{4,2},{6,0},{1,7},{3,5},{5,3},{7,1},{8,14},{10,12},{12... | collective-permute-start | bytes 196616 | tf_op jit(solution)/shard_map/ppermute | solution.py:555
  48.2 8.4 %collective-permute-start.20 = (bf16[256,128]{1,0:T(8,128)(2,1)S(1)}, bf16[256,128]{1,0:T(8,128)(2,1)S(1)}, u32[]{:S(2)}, u32[]{:S(2)}) collective-permute-start(bf16[256,128]{1,0:T(8,128)(2,1)S(1)} %side.1.refs_4_), channel_id=1, source_target_pairs={{0,4},{2,6},{4,0},{6,2},{1,5},{3,7},{5,1},{7,3},{8,12},{10,14},{12... | collective-permute-start | bytes 196616 | tf_op jit(solution)/shard_map/ppermute | solution.py:555
  48.2 8.4 %collective-permute-start.19 = (bf16[256,128]{1,0:T(8,128)(2,1)S(1)}, bf16[256,128]{1,0:T(8,128)(2,1)S(1)}, u32[]{:S(2)}, u32[]{:S(2)}) collective-permute-start(bf16[256,128]{1,0:T(8,128)(2,1)S(1)} %side.1.refs_4_), channel_id=1, source_target_pairs={{0,2},{2,0},{4,6},{6,4},{1,3},{3,1},{5,7},{7,5},{8,10},{10,8},{12,... | collective-permute-start | bytes 196616 | tf_op jit(solution)/shard_map/ppermute | solution.py:555
  52.2 6.6 %collective-permute-start.18 = (bf16[256,128]{1,0:T(8,128)(2,1)S(1)}, bf16[256,128]{1,0:T(8,128)(2,1)S(1)}, u32[]{:S(2)}, u32[]{:S(2)}) collective-permute-start(bf16[256,128]{1,0:T(8,128)(2,1)S(1)} %get-tuple-element.106.refs_0_), channel_id=1, source_target_pairs={{0,6},{2,4},{4,2},{6,0},{1,7},{3,5},{5,3},{7,1},{8,14},{10,12},{12... | collective-permute-start | bytes 196616 | tf_op jit(solution)/shard_map/ppermute | solution.py:555
  54.7 5.6 %collective-permute-start.17 = (bf16[256,128]{1,0:T(8,128)(2,1)S(1)}, bf16[256,128]{1,0:T(8,128)(2,1)S(1)}, u32[]{:S(2)}, u32[]{:S(2)}) collective-permute-start(bf16[256,128]{1,0:T(8,128)(2,1)S(1)} %get-tuple-element.106.refs_0_), channel_id=1, source_target_pairs={{0,4},{2,6},{4,0},{6,2},{1,5},{3,7},{5,1},{7,3},{8,12},{10,14},{12... | collective-permute-start | bytes 196616 | tf_op jit(solution)/shard_map/ppermute | solution.py:555
  54.8 5.6 %collective-permute-start.16 = (bf16[256,128]{1,0:T(8,128)(2,1)S(1)}, bf16[256,128]{1,0:T(8,128)(2,1)S(1)}, u32[]{:S(2)}, u32[]{:S(2)}) collective-permute-start(bf16[256,128]{1,0:T(8,128)(2,1)S(1)} %get-tuple-element.106.refs_0_), channel_id=1, source_target_pairs={{0,2},{2,0},{4,6},{6,4},{1,3},{3,1},{5,7},{7,5},{8,10},{10,8},{12,... | collective-permute-start | bytes 196616 | tf_op jit(solution)/shard_map/ppermute | solution.py:555
  62.4 6.4 %collective-permute-start.24 = (bf16[272,128]{1,0:T(8,128)(2,1)S(1)}, bf16[272,128]{1,0:T(8,128)(2,1)S(1)}, u32[]{:S(2)}, u32[]{:S(2)}) collective-permute-start(bf16[272,128]{1,0:T(8,128)(2,1)S(1)} %get-tuple-element.110.refs_0_), channel_id=1, source_target_pairs={{0,6},{2,4},{4,2},{6,0},{1,7},{3,5},{5,3},{7,1},{8,14},{10,12},{12... | collective-permute-start | bytes 208904 | tf_op jit(solution)/shard_map/ppermute | solution.py:555
  64.9 6.4 %collective-permute-start.23 = (bf16[272,128]{1,0:T(8,128)(2,1)S(1)}, bf16[272,128]{1,0:T(8,128)(2,1)S(1)}, u32[]{:S(2)}, u32[]{:S(2)}) collective-permute-start(bf16[272,128]{1,0:T(8,128)(2,1)S(1)} %get-tuple-element.110.refs_0_), channel_id=1, source_target_pairs={{0,4},{2,6},{4,0},{6,2},{1,5},{3,7},{5,1},{7,3},{8,12},{10,14},{12... | collective-permute-start | bytes 208904 | tf_op jit(solution)/shard_map/ppermute | solution.py:555
  64.9 6.4 %collective-permute-start.22 = (bf16[272,128]{1,0:T(8,128)(2,1)S(1)}, bf16[272,128]{1,0:T(8,128)(2,1)S(1)}, u32[]{:S(2)}, u32[]{:S(2)}) collective-permute-start(bf16[272,128]{1,0:T(8,128)(2,1)S(1)} %get-tuple-element.110.refs_0_), channel_id=1, source_target_pairs={{0,2},{2,0},{4,6},{6,4},{1,3},{3,1},{5,7},{7,5},{8,10},{10,8},{12,... | collective-permute-start | bytes 208904 | tf_op jit(solution)/shard_map/ppermute | solution.py:555
  72.5 5.8 %collective-permute-start.27 = (bf16[144,128]{1,0:T(8,128)(2,1)S(1)}, bf16[144,128]{1,0:T(8,128)(2,1)S(1)}, u32[]{:S(2)}, u32[]{:S(2)}) collective-permute-start(bf16[144,128]{1,0:T(8,128)(2,1)S(1)} %get-tuple-element.129.refs_0_), channel_id=1, source_target_pairs={{0,6},{2,4},{4,2},{6,0},{1,7},{3,5},{5,3},{7,1},{8,14},{10,12},{12... | collective-permute-start | bytes 110600 | tf_op jit(solution)/shard_map/ppermute | solution.py:555
  75.1 4.9 %collective-permute-start.26 = (bf16[144,128]{1,0:T(8,128)(2,1)S(1)}, bf16[144,128]{1,0:T(8,128)(2,1)S(1)}, u32[]{:S(2)}, u32[]{:S(2)}) collective-permute-start(bf16[144,128]{1,0:T(8,128)(2,1)S(1)} %get-tuple-element.129.refs_0_), channel_id=1, source_target_pairs={{0,4},{2,6},{4,0},{6,2},{1,5},{3,7},{5,1},{7,3},{8,12},{10,14},{12... | collective-permute-start | bytes 110600 | tf_op jit(solution)/shard_map/ppermute | solution.py:555
  75.1 4.9 %collective-permute-start.25 = (bf16[144,128]{1,0:T(8,128)(2,1)S(1)}, bf16[144,128]{1,0:T(8,128)(2,1)S(1)}, u32[]{:S(2)}, u32[]{:S(2)}) collective-permute-start(bf16[144,128]{1,0:T(8,128)(2,1)S(1)} %get-tuple-element.129.refs_0_), channel_id=1, source_target_pairs={{0,2},{2,0},{4,6},{6,4},{1,3},{3,1},{5,7},{7,5},{8,10},{10,8},{12,... | collective-permute-start | bytes 110600 | tf_op jit(solution)/shard_map/ppermute | solution.py:555
  81.2 6.2 %collective-permute-start.30 = (bf16[144,128]{1,0:T(8,128)(2,1)S(1)}, bf16[144,128]{1,0:T(8,128)(2,1)S(1)}, u32[]{:S(2)}, u32[]{:S(2)}) collective-permute-start(bf16[144,128]{1,0:T(8,128)(2,1)S(1)} %get-tuple-element.144.refs_0_), channel_id=1, source_target_pairs={{0,6},{2,4},{4,2},{6,0},{1,7},{3,5},{5,3},{7,1},{8,14},{10,12},{12... | collective-permute-start | bytes 110600 | tf_op jit(solution)/shard_map/ppermute | solution.py:555
  83.0 5.3 %collective-permute-start.29 = (bf16[144,128]{1,0:T(8,128)(2,1)S(1)}, bf16[144,128]{1,0:T(8,128)(2,1)S(1)}, u32[]{:S(2)}, u32[]{:S(2)}) collective-permute-start(bf16[144,128]{1,0:T(8,128)(2,1)S(1)} %get-tuple-element.144.refs_0_), channel_id=1, source_target_pairs={{0,4},{2,6},{4,0},{6,2},{1,5},{3,7},{5,1},{7,3},{8,12},{10,14},{12... | collective-permute-start | bytes 110600 | tf_op jit(solution)/shard_map/ppermute | solution.py:555
  83.7 4.6 %collective-permute-start.28 = (bf16[144,128]{1,0:T(8,128)(2,1)S(1)}, bf16[144,128]{1,0:T(8,128)(2,1)S(1)}, u32[]{:S(2)}, u32[]{:S(2)}) collective-permute-start(bf16[144,128]{1,0:T(8,128)(2,1)S(1)} %get-tuple-element.144.refs_0_), channel_id=1, source_target_pairs={{0,2},{2,0},{4,6},{6,4},{1,3},{3,1},{5,7},{7,5},{8,10},{10,8},{12,... | collective-permute-start | bytes 110600 | tf_op jit(solution)/shard_map/ppermute | solution.py:555
  85.7 4.5 %collective-permute-start.33 = (bf16[272,512]{1,0:T(8,128)(2,1)S(1)}, bf16[272,512]{1,0:T(8,128)(2,1)S(1)}, u32[]{:S(2)}, u32[]{:S(2)}) collective-permute-start(bf16[272,512]{1,0:T(8,128)(2,1)S(1)} %get-tuple-element.159), channel_id=1, source_target_pairs={{0,1},{1,0},{2,3},{3,2},{4,5},{5,4},{6,7},{7,6},{8,9},{9,8},{10,11... | collective-permute-start | bytes 835592 | tf_op jit(solution)/shard_map/ppermute | solution.py:561
  85.7 4.5 %collective-permute-start.34 = (bf16[272,512]{1,0:T(8,128)(2,1)S(1)}, bf16[272,512]{1,0:T(8,128)(2,1)S(1)}, u32[]{:S(2)}, u32[]{:S(2)}) collective-permute-start(bf16[272,512]{1,0:T(8,128)(2,1)S(1)} %get-tuple-element.160), channel_id=1, source_target_pairs={{0,1},{1,0},{2,3},{3,2},{4,5},{5,4},{6,7},{7,6},{8,9},{9,8},{10,11... | collective-permute-start | bytes 835592 | tf_op jit(solution)/shard_map/ppermute | solution.py:561
  92.2 9.6 %collective-permute-start.35 = (bf16[272,512]{1,0:T(8,128)(2,1)S(1)}, bf16[272,512]{1,0:T(8,128)(2,1)S(1)}, u32[]{:S(2)}, u32[]{:S(2)}) collective-permute-start(bf16[272,512]{1,0:T(8,128)(2,1)S(1)} %get-tuple-element.162), channel_id=1, source_target_pairs={{0,8},{8,0},{16,24},{24,16},{1,9},{9,1},{17,25},{25,17},{2,10},{10... | collective-permute-start | bytes 835592 | tf_op jit(solution)/shard_map/ppermute | solution.py:558
  93.7 14.5 %collective-permute-start.36 = (bf16[272,512]{1,0:T(8,128)(2,1)S(1)}, bf16[272,512]{1,0:T(8,128)(2,1)S(1)}, u32[]{:S(2)}, u32[]{:S(2)}) collective-permute-start(bf16[272,512]{1,0:T(8,128)(2,1)S(1)} %get-tuple-element.163), channel_id=1, source_target_pairs={{0,16},{8,24},{16,0},{24,8},{1,17},{9,25},{17,1},{25,9},{2,18},{10... | collective-permute-start | bytes 835592 | tf_op jit(solution)/shard_map/ppermute | solution.py:558
  95.6 12.6 %collective-permute-start.37 = (bf16[272,512]{1,0:T(8,128)(2,1)S(1)}, bf16[272,512]{1,0:T(8,128)(2,1)S(1)}, u32[]{:S(2)}, u32[]{:S(2)}) collective-permute-start(bf16[272,512]{1,0:T(8,128)(2,1)S(1)} %get-tuple-element.164), channel_id=1, source_target_pairs={{0,24},{8,16},{16,8},{24,0},{1,25},{9,17},{17,9},{25,1},{2,26},{10... | collective-permute-start | bytes 835592 | tf_op jit(solution)/shard_map/ppermute | solution.py:558
  (8 other events, 17.0 us)

commit v12 on v11

--- a/solution.py
+++ b/solution.py
@@ -234,10 +234,15 @@
         ).astype(BF)
 
 
+def own_kernel(part, packed, part_out, packed_out):
+    part_out[...] = part[...]
+    packed_out[...] = packed[...]
+
+
 def arrange_kernel(length, order, *refs):
     groups = len(order)
-    received, packed = [refs[order.index(place)] for place in range(groups)], refs[groups]
-    x, cot, mask, mean, packed_out, tails = refs[groups + 1 :]
+    received = [refs[order.index(place)] for place in range(groups)]
+    x, cot, mask, mean, tails = refs[groups:]
     rows, local = x.shape
     place_rows(received, tails, slice(2 * local, None))
     place_rows(received, x, slice(0, local))
@@ -245,7 +250,6 @@
     tail = tails[...].astype(F32)
     mean[...] = jnp.broadcast_to(tail[:, 1:2] + tail[:, 2:3], mean.shape)
     build_mask(tail[:, 0:1], mask, block_size(rows), length)
-    packed_out[...] = packed[...]
 
 
 def first_kernel(sections, *refs):
@@ -560,8 +564,10 @@
     def swapped(value):
         return lax.ppermute(value, "core", [(i, 1 - i) for i in range(sides)])
 
+    exchange_order = sorted(range(1, groups), key=lambda place: (place != 3, place))
+
     def exchange(pay):
-        return [pay] + [shifted(pay, shift) for shift in range(1, groups)]
+        return [pay] + [shifted(pay, place) for place in exchange_order]
 
     token_parts, packed = pack(
         tokens, cotangents, starts, counts, layer_gains, first_map, second_map, groups, micro_local
@@ -569,20 +575,8 @@
     mine = [packed] + [across(packed, distance) for distance in range(1, sections)]
     order = [0] + list(range(groups - 1, 0, -1))
     received = [token_parts[0]] + [shifted(token_parts[place], place) for place in order[1:]]
-    received, mine = lax.optimization_barrier((received, mine))
-    theirs = [swapped(part) for part in mine]
-
     def shaped(shape, kind=BF):
         return jax.ShapeDtypeStruct(shape, kind)
-
-    wide_shape = shaped((rows, local))
-    mean_shape = shaped((rows, HD), F32)
-    rank_shape = shaped((rows, rank))
-    cross_shape = shaped((rows, rank), F32)
-    probs_shape = shaped((blocks, heads, size, size))
-    grads_shape = (sides, 2 * rank + 16, own)
-    half_shape = shaped(grads_shape[1:])
-    weights_shape = shaped((sections, sides, slice_rows(own), HD))
 
     def call(kernel, operands, specs, outs, name, **more):
         return pl.pallas_call(
@@ -595,17 +589,30 @@
             **more,
         )(*operands)
 
-    x, cot, mask, mean, mine[0] = call(
+    received[0], mine[0] = call(
+        own_kernel,
+        (received[0], packed),
+        vmem_specs(2),
+        [shaped(received[0].shape), shaped(packed.shape)],
+        "own_parts",
+    )
+    received, mine = lax.optimization_barrier((received, mine))
+    theirs = [swapped(part) for part in mine]
+
+    wide_shape = shaped((rows, local))
+    mean_shape = shaped((rows, HD), F32)
+    rank_shape = shaped((rows, rank))
+    cross_shape = shaped((rows, rank), F32)
+    probs_shape = shaped((blocks, heads, size, size))
+    grads_shape = (sides, 2 * rank + 16, own)
+    half_shape = shaped(grads_shape[1:])
+    weights_shape = shaped((sections, sides, slice_rows(own), HD))
+
+    x, cot, mask, mean = call(
         functools.partial(arrange_kernel, length, order),
-        (*received, mine[0]),
-        vmem_specs(groups + 1),
-        [
-            wide_shape,
-            wide_shape,
-            shaped((blocks, size, size)),
-            mean_shape,
-            shaped(packed.shape),
-        ],
+        received,
+        vmem_specs(groups),
+        [wide_shape, wide_shape, shaped((blocks, size, size)), mean_shape],
         "arrange",
         scratch_shapes=[pltpu.VMEM((rows, HD), BF)],
     )

time: 109 us -> 111 us (1.018)
  waiting for transfers between devices: 39.1 us -> 40.5 us
    ppermute x8, waiting for transfers between devices: 1.46 us -> 2.86 us  [swapped(): return lax.ppermute(value, 'core', [(i, 1 - i) for i in range(sides)])]
    pallas_call x14 -> x15, Pallas kernels: 13.2 us -> 13.2 us  [call(): pl.pallas_call(kernel, in_specs=specs, out_specs=vmem_specs(len(outs)), o...]
  transfers between devices with their start and end apart: 38 -> 38, of which waited for: 20 -> 23; matrix products, arithmetic and copies ran while one was open for 0% -> 0% of each run, Pallas kernels for 4% -> 4%
where the time goes in v12:
time: 111 us
  starting transfers between devices  52.1 us (47%)
  waiting for transfers between devices  40.5 us (36%)
  Pallas kernels  15.5 us (14%)
  local copies, waits for them, and re-layouts  1.86 us (2%)
    ppermute x24, starting transfers between devices, shifted(): return lax.ppermute(value, 'z', [(i, i ^ shift) for i in range(groups)])  43 us
    ppermute x24, waiting for transfers between devices, shifted(): return lax.ppermute(value, 'z', [(i, i ^ shift) for i in range(groups)])  24.3 us
    ppermute x6, waiting for transfers between devices, across(): lax.ppermute(value, 'pipe', [(i, i ^ distance) for i in range(sections)])  13.3 us
    pallas_call x15, Pallas kernels, call(): pl.pallas_call(kernel, in_specs=specs, out_specs=vmem_specs(len(outs)), o...  13.2 us
    ppermute x6, starting transfers between devices, across(): lax.ppermute(value, 'pipe', [(i, i ^ distance) for i in range(sections)])  7.04 us
    ppermute x8, waiting for transfers between devices, swapped(): return lax.ppermute(value, 'core', [(i, 1 - i) for i in range(sides)])  2.86 us
    pallas_call x1, Pallas kernels, pack(): pl.pallas_call(functools.partial(pack_kernel, groups, micro_local), in_sp...  2.28 us
  transfers between devices with their start and end apart: 38, of which 23 were waited for; matrix products, arithmetic and copies ran while one was open for 0% of the time, Pallas kernels for 4%

profile of v12, /device:TPU:0, one launch (start us, length us, event | category | flops | bytes accessed | tf_op | source)
XLA Modules:
  0.0 110.8 jit_solution(9890720078411325929)
XLA Ops:
  0.6 2.3 %pack.1 = (bf16[32,2176]{1,0:T(8,128)(2,1)}, bf16[32,2176]{1,0:T(8,128)(2,1)}, bf16[32,2176]{1,0:T(8,128)(2,1)}, bf16[32,2176]{1,0:T(8,128)(2,1)}, bf16[1040,128]{1,0:T(8,128)(2,1)}) custom-call(bf16[2,2,32,4096]{3,2,1,0:T(8,128)(2,1)} %refs_0_.1, bf16[2,2,32,4096]{3,2,1,0:T(8,128)(2,1)} %refs_1_.1, s32[2,2,4]{2,1,0:T(2,128)} %refs_2_.1, s32[2,2]{1,0:T(2,128)} %refs_3_.1, ...), custom_call_target="tpu_custom_call" | custom-call | tf_op jit(solution)/shard_map/pack/pallas_call | solution.py:124
  2.9 5.1 %collective-permute-start = (bf16[32,2176]{1,0:T(8,128)(2,1)}, bf16[32,2176]{1,0:T(8,128)(2,1)S(1)}, u32[]{:S(2)}, u32[]{:S(2)}) collective-permute-start(bf16[32,2176]{1,0:T(8,128)(2,1)} %get-tuple-element.88), channel_id=1, source_target_pairs={{0,6},{2,4},{4,2},{6,0},{1,7},{3,5},{5,3},{7,1},{8,14},{10,12},{12... | collective-permute-start | bytes 417800 | tf_op jit(solution)/shard_map/ppermute | solution.py:559
  8.0 2.4 %collective-permute-start.5 = (bf16[1040,128]{1,0:T(8,128)(2,1)}, bf16[1040,128]{1,0:T(8,128)(2,1)S(1)}, u32[]{:S(2)}, u32[]{:S(2)}) collective-permute-start(bf16[1040,128]{1,0:T(8,128)(2,1)} %get-tuple-element.86.packed), channel_id=1, source_target_pairs={{0,24},{8,16},{16,8},{24,0},{1,25},{9,17},{17,9},{25,1},{2,26},{10... | collective-permute-start | bytes 798728 | tf_op jit(solution)/shard_map/ppermute | solution.py:562
  12.0 6.5 %collective-permute-start.2 = (bf16[32,2176]{1,0:T(8,128)(2,1)}, bf16[32,2176]{1,0:T(8,128)(2,1)S(1)}, u32[]{:S(2)}, u32[]{:S(2)}) collective-permute-start(bf16[32,2176]{1,0:T(8,128)(2,1)} %get-tuple-element.90), channel_id=1, source_target_pairs={{0,2},{2,0},{4,6},{6,4},{1,3},{3,1},{5,7},{7,5},{8,10},{10,8},{12,... | collective-permute-start | bytes 417800 | tf_op jit(solution)/shard_map/ppermute | solution.py:559
  20.5 1.3 %collective-permute-done.2.refs_3_ = bf16[32,2176]{1,0:T(8,128)(2,1)S(1)} collective-permute-done((bf16[32,2176]{1,0:T(8,128)(2,1)}, bf16[32,2176]{1,0:T(8,128)(2,1)S(1)}, u32[]{:S(2)}, u32[]{:S(2)}) %collective-permute-start.2) | collective-permute-done | bytes 139296 | tf_op jit(solution)/shard_map/ppermute | solution.py:559
  25.5 1.6 %forward_first.1 = (bf16[1,8,128,128]{3,2,1,0:T(8,128)(2,1)S(1)}, bf16[128,1024]{1,0:T(8,128)(2,1)S(1)}, bf16[400,128]{1,0:T(8,128)(2,1)S(1)}, bf16[4,2,1040,128]{3,2,1,0:T(8,128)(2,1)S(1)}) custom-call(bf16[1040,128]{1,0:T(8,128)(2,1)S(1)} %get-tuple-element.92.refs_0_, bf16[1040,128]{1,0:T(8,128)(2,1)S(1)} %collective-permute-done.3.refs_1_, ...), custom_call_target="tpu_custom_call" | custom-call | tf_op jit(solution)/shard_map/forward_first/pallas_call | solution.py:582
  27.0 2.1 %collective-permute-start.12 = (bf16[400,128]{1,0:T(8,128)(2,1)S(1)}, bf16[400,128]{1,0:T(8,128)(2,1)S(1)}, u32[]{:S(2)}, u32[]{:S(2)}) collective-permute-start(bf16[400,128]{1,0:T(8,128)(2,1)S(1)} %get-tuple-element.103.refs_0_.refs_4_), channel_id=1, source_target_pairs={{0,4},{2,6},{4,0},{6,2},{1,5},{3,7},{5,1},{7,3},{8,12},{10,14},{12... | collective-permute-start | bytes 307208 | tf_op jit(solution)/shard_map/ppermute | solution.py:559
  29.2 2.3 %collective-permute-start.10 = (bf16[400,128]{1,0:T(8,128)(2,1)S(1)}, bf16[400,128]{1,0:T(8,128)(2,1)S(1)}, u32[]{:S(2)}, u32[]{:S(2)}) collective-permute-start(bf16[400,128]{1,0:T(8,128)(2,1)S(1)} %get-tuple-element.103.refs_0_.refs_4_), channel_id=1, source_target_pairs={{0,6},{2,4},{4,2},{6,0},{1,7},{3,5},{5,3},{7,1},{8,14},{10,12},{12... | collective-permute-start | bytes 307208 | tf_op jit(solution)/shard_map/ppermute | solution.py:559
  31.5 5.1 %collective-permute-done.12.refs_3_.refs_7_ = bf16[400,128]{1,0:T(8,128)(2,1)S(1)} collective-permute-done((bf16[400,128]{1,0:T(8,128)(2,1)S(1)}, bf16[400,128]{1,0:T(8,128)(2,1)S(1)}, u32[]{:S(2)}, u32[]{:S(2)}) %collective-permute-start.12) | collective-permute-done | bytes 102432 | tf_op jit(solution)/shard_map/ppermute | solution.py:559
  36.6 1.5 %collective-permute-done.10.refs_1_.refs_5_ = bf16[400,128]{1,0:T(8,128)(2,1)S(1)} collective-permute-done((bf16[400,128]{1,0:T(8,128)(2,1)S(1)}, bf16[400,128]{1,0:T(8,128)(2,1)S(1)}, u32[]{:S(2)}, u32[]{:S(2)}) %collective-permute-start.10) | collective-permute-done | bytes 102432 | tf_op jit(solution)/shard_map/ppermute | solution.py:559
  39.4 2.2 %collective-permute-start.15 = (bf16[256,128]{1,0:T(8,128)(2,1)S(1)}, bf16[256,128]{1,0:T(8,128)(2,1)S(1)}, u32[]{:S(2)}, u32[]{:S(2)}) collective-permute-start(bf16[256,128]{1,0:T(8,128)(2,1)S(1)} %get-tuple-element.105.refs_0_), channel_id=1, source_target_pairs={{0,4},{2,6},{4,0},{6,2},{1,5},{3,7},{5,1},{7,3},{8,12},{10,14},{12... | collective-permute-start | bytes 196616 | tf_op jit(solution)/shard_map/ppermute | solution.py:559
  42.4 1.4 %collective-permute-start.13 = (bf16[256,128]{1,0:T(8,128)(2,1)S(1)}, bf16[256,128]{1,0:T(8,128)(2,1)S(1)}, u32[]{:S(2)}, u32[]{:S(2)}) collective-permute-start(bf16[256,128]{1,0:T(8,128)(2,1)S(1)} %get-tuple-element.105.refs_0_), channel_id=1, source_target_pairs={{0,6},{2,4},{4,2},{6,0},{1,7},{3,5},{5,3},{7,1},{8,14},{10,12},{12... | collective-permute-start | bytes 196616 | tf_op jit(solution)/shard_map/ppermute | solution.py:559
  45.4 1.8 %collective-permute-start.20 = (bf16[256,128]{1,0:T(8,128)(2,1)S(1)}, bf16[256,128]{1,0:T(8,128)(2,1)S(1)}, u32[]{:S(2)}, u32[]{:S(2)}) collective-permute-start(bf16[256,128]{1,0:T(8,128)(2,1)S(1)} %side.1.refs_4_), channel_id=1, source_target_pairs={{0,2},{2,0},{4,6},{6,4},{1,3},{3,1},{5,7},{7,5},{8,10},{10,8},{12,... | collective-permute-start | bytes 196616 | tf_op jit(solution)/shard_map/ppermute | solution.py:559
  49.5 1.3 %forward_middle.3 = (bf16[128,1024]{1,0:T(8,128)(2,1)S(1)}, f32[128,128]{1,0:T(8,128)S(1)}, bf16[128,128]{1,0:T(8,128)(2,1)S(1)}, f32[128,128]{1,0:T(8,128)S(1)}...) custom-call(bf16[256,128]{1,0:T(8,128)(2,1)S(1)} %get-tuple-element.105.refs_0_, ...), custom_call_target="tpu_custom_call" | custom-call | tf_op jit(solution)/shard_map/forward_middle/pallas_call | solution.py:582
  50.8 2.8 %collective-permute-start.18 = (bf16[256,128]{1,0:T(8,128)(2,1)S(1)}, bf16[256,128]{1,0:T(8,128)(2,1)S(1)}, u32[]{:S(2)}, u32[]{:S(2)}) collective-permute-start(bf16[256,128]{1,0:T(8,128)(2,1)S(1)} %get-tuple-element.108.refs_0_), channel_id=1, source_target_pairs={{0,4},{2,6},{4,0},{6,2},{1,5},{3,7},{5,1},{7,3},{8,12},{10,14},{12... | collective-permute-start | bytes 196616 | tf_op jit(solution)/shard_map/ppermute | solution.py:559
  53.6 2.2 %collective-permute-start.16 = (bf16[256,128]{1,0:T(8,128)(2,1)S(1)}, bf16[256,128]{1,0:T(8,128)(2,1)S(1)}, u32[]{:S(2)}, u32[]{:S(2)}) collective-permute-start(bf16[256,128]{1,0:T(8,128)(2,1)S(1)} %get-tuple-element.108.refs_0_), channel_id=1, source_target_pairs={{0,6},{2,4},{4,2},{6,0},{1,7},{3,5},{5,3},{7,1},{8,14},{10,12},{12... | collective-permute-start | bytes 196616 | tf_op jit(solution)/shard_map/ppermute | solution.py:559
  55.8 2.7 %collective-permute-done.18.refs_3_ = bf16[256,128]{1,0:T(8,128)(2,1)S(1)} collective-permute-done((bf16[256,128]{1,0:T(8,128)(2,1)S(1)}, bf16[256,128]{1,0:T(8,128)(2,1)S(1)}, u32[]{:S(2)}, u32[]{:S(2)}) %collective-permute-start.18) | collective-permute-done | bytes 65568 | tf_op jit(solution)/shard_map/ppermute | solution.py:559
  59.8 2.1 %turn.1 = (bf16[128,1024]{1,0:T(8,128)(2,1)S(1)}, f32[128,128]{1,0:T(8,128)S(1)}, bf16[128,128]{1,0:T(8,128)(2,1)S(1)}, f32[128,128]{1,0:T(8,128)S(1)}, bf16[128...) custom-call(bf16[256,128]{1,0:T(8,128)(2,1)S(1)} %get-tuple-element., ...), custom_call_target="tpu_custom_call" | custom-call | tf_op jit(solution)/shard_map/turn/pallas_call | solution.py:582
  61.8 1.6 %collective-permute-start.24 = (bf16[272,128]{1,0:T(8,128)(2,1)S(1)}, bf16[272,128]{1,0:T(8,128)(2,1)S(1)}, u32[]{:S(2)}, u32[]{:S(2)}) collective-permute-start(bf16[272,128]{1,0:T(8,128)(2,1)S(1)} %get-tuple-element.112.refs_0_), channel_id=1, source_target_pairs={{0,4},{2,6},{4,0},{6,2},{1,5},{3,7},{5,1},{7,3},{8,12},{10,14},{12... | collective-permute-start | bytes 208904 | tf_op jit(solution)/shard_map/ppermute | solution.py:559
  64.7 1.6 %collective-permute-start.22 = (bf16[272,128]{1,0:T(8,128)(2,1)S(1)}, bf16[272,128]{1,0:T(8,128)(2,1)S(1)}, u32[]{:S(2)}, u32[]{:S(2)}) collective-permute-start(bf16[272,128]{1,0:T(8,128)(2,1)S(1)} %get-tuple-element.112.refs_0_), channel_id=1, source_target_pairs={{0,6},{2,4},{4,2},{6,0},{1,7},{3,5},{5,3},{7,1},{8,14},{10,12},{12... | collective-permute-start | bytes 208904 | tf_op jit(solution)/shard_map/ppermute | solution.py:559
  66.3 1.8 %collective-permute-done.24.refs_3_ = bf16[272,128]{1,0:T(8,128)(2,1)S(1)} collective-permute-done((bf16[272,128]{1,0:T(8,128)(2,1)S(1)}, bf16[272,128]{1,0:T(8,128)(2,1)S(1)}, u32[]{:S(2)}, u32[]{:S(2)}) %collective-permute-start.24) | collective-permute-done | bytes 69664 | tf_op jit(solution)/shard_map/ppermute | solution.py:559
  68.4 2.3 %collective-permute-done.22.refs_1_ = bf16[272,128]{1,0:T(8,128)(2,1)S(1)} collective-permute-done((bf16[272,128]{1,0:T(8,128)(2,1)S(1)}, bf16[272,128]{1,0:T(8,128)(2,1)S(1)}, u32[]{:S(2)}, u32[]{:S(2)}) %collective-permute-start.22) | collective-permute-done | bytes 69664 | tf_op jit(solution)/shard_map/ppermute | solution.py:559
  72.1 2.2 %collective-permute-start.26 = (bf16[144,128]{1,0:T(8,128)(2,1)S(1)}, bf16[144,128]{1,0:T(8,128)(2,1)S(1)}, u32[]{:S(2)}, u32[]{:S(2)}) collective-permute-start(bf16[144,128]{1,0:T(8,128)(2,1)S(1)} %get-tuple-element.131.refs_0_), channel_id=1, source_target_pairs={{0,2},{2,0},{4,6},{6,4},{1,3},{3,1},{5,7},{7,5},{8,10},{10,8},{12,... | collective-permute-start | bytes 110600 | tf_op jit(solution)/shard_map/ppermute | solution.py:559
  74.3 2.2 %collective-permute-start.25 = (bf16[144,128]{1,0:T(8,128)(2,1)S(1)}, bf16[144,128]{1,0:T(8,128)(2,1)S(1)}, u32[]{:S(2)}, u32[]{:S(2)}) collective-permute-start(bf16[144,128]{1,0:T(8,128)(2,1)S(1)} %get-tuple-element.131.refs_0_), channel_id=1, source_target_pairs={{0,6},{2,4},{4,2},{6,0},{1,7},{3,5},{5,3},{7,1},{8,14},{10,12},{12... | collective-permute-start | bytes 110600 | tf_op jit(solution)/shard_map/ppermute | solution.py:559
  77.2 2.8 %collective-permute-done.25.refs_1_ = bf16[144,128]{1,0:T(8,128)(2,1)S(1)} collective-permute-done((bf16[144,128]{1,0:T(8,128)(2,1)S(1)}, bf16[144,128]{1,0:T(8,128)(2,1)S(1)}, u32[]{:S(2)}, u32[]{:S(2)}) %collective-permute-start.25) | collective-permute-done | bytes 36896 | tf_op jit(solution)/shard_map/ppermute | solution.py:559
  81.4 2.9 %collective-permute-start.29 = (bf16[144,128]{1,0:T(8,128)(2,1)S(1)}, bf16[144,128]{1,0:T(8,128)(2,1)S(1)}, u32[]{:S(2)}, u32[]{:S(2)}) collective-permute-start(bf16[144,128]{1,0:T(8,128)(2,1)S(1)} %get-tuple-element.146.refs_0_), channel_id=1, source_target_pairs={{0,2},{2,0},{4,6},{6,4},{1,3},{3,1},{5,7},{7,5},{8,10},{10,8},{12,... | collective-permute-start | bytes 110600 | tf_op jit(solution)/shard_map/ppermute | solution.py:559
  84.3 1.5 %collective-permute-start.28 = (bf16[144,128]{1,0:T(8,128)(2,1)S(1)}, bf16[144,128]{1,0:T(8,128)(2,1)S(1)}, u32[]{:S(2)}, u32[]{:S(2)}) collective-permute-start(bf16[144,128]{1,0:T(8,128)(2,1)S(1)} %get-tuple-element.146.refs_0_), channel_id=1, source_target_pairs={{0,6},{2,4},{4,2},{6,0},{1,7},{3,5},{5,3},{7,1},{8,14},{10,12},{12... | collective-permute-start | bytes 110600 | tf_op jit(solution)/shard_map/ppermute | solution.py:559
  86.7 3.4 %collective-permute-done.28.refs_1_ = bf16[144,128]{1,0:T(8,128)(2,1)S(1)} collective-permute-done((bf16[144,128]{1,0:T(8,128)(2,1)S(1)}, bf16[144,128]{1,0:T(8,128)(2,1)S(1)}, u32[]{:S(2)}, u32[]{:S(2)}) %collective-permute-start.28) | collective-permute-done | bytes 36896 | tf_op jit(solution)/shard_map/ppermute | solution.py:559
  93.9 1.5 %collective-permute-start.35 = (bf16[272,512]{1,0:T(8,128)(2,1)S(1)}, bf16[272,512]{1,0:T(8,128)(2,1)S(1)}, u32[]{:S(2)}, u32[]{:S(2)}) collective-permute-start(bf16[272,512]{1,0:T(8,128)(2,1)S(1)} %get-tuple-element.164), channel_id=1, source_target_pairs={{0,8},{8,0},{16,24},{24,16},{1,9},{9,1},{17,25},{25,17},{2,10},{10... | collective-permute-start | bytes 835592 | tf_op jit(solution)/shard_map/ppermute | solution.py:562
  95.4 1.4 %collective-permute-start.36 = (bf16[272,512]{1,0:T(8,128)(2,1)S(1)}, bf16[272,512]{1,0:T(8,128)(2,1)S(1)}, u32[]{:S(2)}, u32[]{:S(2)}) collective-permute-start(bf16[272,512]{1,0:T(8,128)(2,1)S(1)} %get-tuple-element.165), channel_id=1, source_target_pairs={{0,16},{8,24},{16,0},{24,8},{1,17},{9,25},{17,1},{25,9},{2,18},{10... | collective-permute-start | bytes 835592 | tf_op jit(solution)/shard_map/ppermute | solution.py:562
  97.5 6.0 %collective-permute-done.35.refs_1_ = bf16[272,512]{1,0:T(8,128)(2,1)S(1)} collective-permute-done((bf16[272,512]{1,0:T(8,128)(2,1)S(1)}, bf16[272,512]{1,0:T(8,128)(2,1)S(1)}, u32[]{:S(2)}, u32[]{:S(2)}) %collective-permute-start.35) | collective-permute-done | bytes 278560 | tf_op jit(solution)/shard_map/ppermute | solution.py:562
  103.5 6.3 %collective-permute-done.36.refs_2_ = bf16[272,512]{1,0:T(8,128)(2,1)S(1)} collective-permute-done((bf16[272,512]{1,0:T(8,128)(2,1)S(1)}, bf16[272,512]{1,0:T(8,128)(2,1)S(1)}, u32[]{:S(2)}, u32[]{:S(2)}) %collective-permute-start.36) | collective-permute-done | bytes 278560 | tf_op jit(solution)/shard_map/ppermute | solution.py:562
  (64 shorter events, 25.6 us)
Async XLA Ops:
  2.9 9.1 %collective-permute-start = (bf16[32,2176]{1,0:T(8,128)(2,1)}, bf16[32,2176]{1,0:T(8,128)(2,1)S(1)}, u32[]{:S(2)}, u32[]{:S(2)}) collective-permute-start(bf16[32,2176]{1,0:T(8,128)(2,1)} %get-tuple-element.88), channel_id=1, source_target_pairs={{0,6},{2,4},{4,2},{6,0},{1,7},{3,5},{5,3},{7,1},{8,14},{10,12},{12... | collective-permute-start | bytes 417800 | tf_op jit(solution)/shard_map/ppermute | solution.py:559
  8.0 13.8 %collective-permute-start.5 = (bf16[1040,128]{1,0:T(8,128)(2,1)}, bf16[1040,128]{1,0:T(8,128)(2,1)S(1)}, u32[]{:S(2)}, u32[]{:S(2)}) collective-permute-start(bf16[1040,128]{1,0:T(8,128)(2,1)} %get-tuple-element.86.packed), channel_id=1, source_target_pairs={{0,24},{8,16},{16,8},{24,0},{1,25},{9,17},{17,9},{25,1},{2,26},{10... | collective-permute-start | bytes 798728 | tf_op jit(solution)/shard_map/ppermute | solution.py:562
  10.5 12.2 %collective-permute-start.4 = (bf16[1040,128]{1,0:T(8,128)(2,1)}, bf16[1040,128]{1,0:T(8,128)(2,1)S(1)}, u32[]{:S(2)}, u32[]{:S(2)}) collective-permute-start(bf16[1040,128]{1,0:T(8,128)(2,1)} %get-tuple-element.86.packed), channel_id=1, source_target_pairs={{0,16},{8,24},{16,0},{24,8},{1,17},{9,25},{17,1},{25,9},{2,18},{10... | collective-permute-start | bytes 798728 | tf_op jit(solution)/shard_map/ppermute | solution.py:562
  11.0 11.8 %collective-permute-start.3 = (bf16[1040,128]{1,0:T(8,128)(2,1)}, bf16[1040,128]{1,0:T(8,128)(2,1)S(1)}, u32[]{:S(2)}, u32[]{:S(2)}) collective-permute-start(bf16[1040,128]{1,0:T(8,128)(2,1)} %get-tuple-element.86.packed), channel_id=1, source_target_pairs={{0,8},{8,0},{16,24},{24,16},{1,9},{9,1},{17,25},{25,17},{2,10},{10... | collective-permute-start | bytes 798728 | tf_op jit(solution)/shard_map/ppermute | solution.py:562
  11.5 8.9 %collective-permute-start.1 = (bf16[32,2176]{1,0:T(8,128)(2,1)}, bf16[32,2176]{1,0:T(8,128)(2,1)S(1)}, u32[]{:S(2)}, u32[]{:S(2)}) collective-permute-start(bf16[32,2176]{1,0:T(8,128)(2,1)} %get-tuple-element.89), channel_id=1, source_target_pairs={{0,4},{2,6},{4,0},{6,2},{1,5},{3,7},{5,1},{7,3},{8,12},{10,14},{12... | collective-permute-start | bytes 417800 | tf_op jit(solution)/shard_map/ppermute | solution.py:559
  12.0 9.8 %collective-permute-start.2 = (bf16[32,2176]{1,0:T(8,128)(2,1)}, bf16[32,2176]{1,0:T(8,128)(2,1)S(1)}, u32[]{:S(2)}, u32[]{:S(2)}) collective-permute-start(bf16[32,2176]{1,0:T(8,128)(2,1)} %get-tuple-element.90), channel_id=1, source_target_pairs={{0,2},{2,0},{4,6},{6,4},{1,3},{3,1},{5,7},{7,5},{8,10},{10,8},{12,... | collective-permute-start | bytes 417800 | tf_op jit(solution)/shard_map/ppermute | solution.py:559
  27.0 9.5 %collective-permute-start.12 = (bf16[400,128]{1,0:T(8,128)(2,1)S(1)}, bf16[400,128]{1,0:T(8,128)(2,1)S(1)}, u32[]{:S(2)}, u32[]{:S(2)}) collective-permute-start(bf16[400,128]{1,0:T(8,128)(2,1)S(1)} %get-tuple-element.103.refs_0_.refs_4_), channel_id=1, source_target_pairs={{0,4},{2,6},{4,0},{6,2},{1,5},{3,7},{5,1},{7,3},{8,12},{10,14},{12... | collective-permute-start | bytes 307208 | tf_op jit(solution)/shard_map/ppermute | solution.py:559
  29.2 7.4 %collective-permute-start.11 = (bf16[400,128]{1,0:T(8,128)(2,1)S(1)}, bf16[400,128]{1,0:T(8,128)(2,1)S(1)}, u32[]{:S(2)}, u32[]{:S(2)}) collective-permute-start(bf16[400,128]{1,0:T(8,128)(2,1)S(1)} %get-tuple-element.103.refs_0_.refs_4_), channel_id=1, source_target_pairs={{0,2},{2,0},{4,6},{6,4},{1,3},{3,1},{5,7},{7,5},{8,10},{10,8},{12,... | collective-permute-start | bytes 307208 | tf_op jit(solution)/shard_map/ppermute | solution.py:559
  29.2 8.8 %collective-permute-start.10 = (bf16[400,128]{1,0:T(8,128)(2,1)S(1)}, bf16[400,128]{1,0:T(8,128)(2,1)S(1)}, u32[]{:S(2)}, u32[]{:S(2)}) collective-permute-start(bf16[400,128]{1,0:T(8,128)(2,1)S(1)} %get-tuple-element.103.refs_0_.refs_4_), channel_id=1, source_target_pairs={{0,6},{2,4},{4,2},{6,0},{1,7},{3,5},{5,3},{7,1},{8,14},{10,12},{12... | collective-permute-start | bytes 307208 | tf_op jit(solution)/shard_map/ppermute | solution.py:559
  39.4 8.2 %collective-permute-start.15 = (bf16[256,128]{1,0:T(8,128)(2,1)S(1)}, bf16[256,128]{1,0:T(8,128)(2,1)S(1)}, u32[]{:S(2)}, u32[]{:S(2)}) collective-permute-start(bf16[256,128]{1,0:T(8,128)(2,1)S(1)} %get-tuple-element.105.refs_0_), channel_id=1, source_target_pairs={{0,4},{2,6},{4,0},{6,2},{1,5},{3,7},{5,1},{7,3},{8,12},{10,14},{12... | collective-permute-start | bytes 196616 | tf_op jit(solution)/shard_map/ppermute | solution.py:559
  41.5 7.1 %collective-permute-start.14 = (bf16[256,128]{1,0:T(8,128)(2,1)S(1)}, bf16[256,128]{1,0:T(8,128)(2,1)S(1)}, u32[]{:S(2)}, u32[]{:S(2)}) collective-permute-start(bf16[256,128]{1,0:T(8,128)(2,1)S(1)} %get-tuple-element.105.refs_0_), channel_id=1, source_target_pairs={{0,2},{2,0},{4,6},{6,4},{1,3},{3,1},{5,7},{7,5},{8,10},{10,8},{12,... | collective-permute-start | bytes 196616 | tf_op jit(solution)/shard_map/ppermute | solution.py:559
  42.4 7.1 %collective-permute-start.13 = (bf16[256,128]{1,0:T(8,128)(2,1)S(1)}, bf16[256,128]{1,0:T(8,128)(2,1)S(1)}, u32[]{:S(2)}, u32[]{:S(2)}) collective-permute-start(bf16[256,128]{1,0:T(8,128)(2,1)S(1)} %get-tuple-element.105.refs_0_), channel_id=1, source_target_pairs={{0,6},{2,4},{4,2},{6,0},{1,7},{3,5},{5,3},{7,1},{8,14},{10,12},{12... | collective-permute-start | bytes 196616 | tf_op jit(solution)/shard_map/ppermute | solution.py:559
  44.1 9.5 %collective-permute-start.21 = (bf16[256,128]{1,0:T(8,128)(2,1)S(1)}, bf16[256,128]{1,0:T(8,128)(2,1)S(1)}, u32[]{:S(2)}, u32[]{:S(2)}) collective-permute-start(bf16[256,128]{1,0:T(8,128)(2,1)S(1)} %side.1.refs_4_), channel_id=1, source_target_pairs={{0,4},{2,6},{4,0},{6,2},{1,5},{3,7},{5,1},{7,3},{8,12},{10,14},{12... | collective-permute-start | bytes 196616 | tf_op jit(solution)/shard_map/ppermute | solution.py:559
  45.4 10.5 %collective-permute-start.20 = (bf16[256,128]{1,0:T(8,128)(2,1)S(1)}, bf16[256,128]{1,0:T(8,128)(2,1)S(1)}, u32[]{:S(2)}, u32[]{:S(2)}) collective-permute-start(bf16[256,128]{1,0:T(8,128)(2,1)S(1)} %side.1.refs_4_), channel_id=1, source_target_pairs={{0,2},{2,0},{4,6},{6,4},{1,3},{3,1},{5,7},{7,5},{8,10},{10,8},{12,... | collective-permute-start | bytes 196616 | tf_op jit(solution)/shard_map/ppermute | solution.py:559
  47.6 8.3 %collective-permute-start.19 = (bf16[256,128]{1,0:T(8,128)(2,1)S(1)}, bf16[256,128]{1,0:T(8,128)(2,1)S(1)}, u32[]{:S(2)}, u32[]{:S(2)}) collective-permute-start(bf16[256,128]{1,0:T(8,128)(2,1)S(1)} %side.1.refs_4_), channel_id=1, source_target_pairs={{0,6},{2,4},{4,2},{6,0},{1,7},{3,5},{5,3},{7,1},{8,14},{10,12},{12... | collective-permute-start | bytes 196616 | tf_op jit(solution)/shard_map/ppermute | solution.py:559
  50.8 7.7 %collective-permute-start.18 = (bf16[256,128]{1,0:T(8,128)(2,1)S(1)}, bf16[256,128]{1,0:T(8,128)(2,1)S(1)}, u32[]{:S(2)}, u32[]{:S(2)}) collective-permute-start(bf16[256,128]{1,0:T(8,128)(2,1)S(1)} %get-tuple-element.108.refs_0_), channel_id=1, source_target_pairs={{0,4},{2,6},{4,0},{6,2},{1,5},{3,7},{5,1},{7,3},{8,12},{10,14},{12... | collective-permute-start | bytes 196616 | tf_op jit(solution)/shard_map/ppermute | solution.py:559
  53.6 4.9 %collective-permute-start.17 = (bf16[256,128]{1,0:T(8,128)(2,1)S(1)}, bf16[256,128]{1,0:T(8,128)(2,1)S(1)}, u32[]{:S(2)}, u32[]{:S(2)}) collective-permute-start(bf16[256,128]{1,0:T(8,128)(2,1)S(1)} %get-tuple-element.108.refs_0_), channel_id=1, source_target_pairs={{0,2},{2,0},{4,6},{6,4},{1,3},{3,1},{5,7},{7,5},{8,10},{10,8},{12,... | collective-permute-start | bytes 196616 | tf_op jit(solution)/shard_map/ppermute | solution.py:559
  53.6 6.2 %collective-permute-start.16 = (bf16[256,128]{1,0:T(8,128)(2,1)S(1)}, bf16[256,128]{1,0:T(8,128)(2,1)S(1)}, u32[]{:S(2)}, u32[]{:S(2)}) collective-permute-start(bf16[256,128]{1,0:T(8,128)(2,1)S(1)} %get-tuple-element.108.refs_0_), channel_id=1, source_target_pairs={{0,6},{2,4},{4,2},{6,0},{1,7},{3,5},{5,3},{7,1},{8,14},{10,12},{12... | collective-permute-start | bytes 196616 | tf_op jit(solution)/shard_map/ppermute | solution.py:559
  61.8 6.3 %collective-permute-start.24 = (bf16[272,128]{1,0:T(8,128)(2,1)S(1)}, bf16[272,128]{1,0:T(8,128)(2,1)S(1)}, u32[]{:S(2)}, u32[]{:S(2)}) collective-permute-start(bf16[272,128]{1,0:T(8,128)(2,1)S(1)} %get-tuple-element.112.refs_0_), channel_id=1, source_target_pairs={{0,4},{2,6},{4,0},{6,2},{1,5},{3,7},{5,1},{7,3},{8,12},{10,14},{12... | collective-permute-start | bytes 208904 | tf_op jit(solution)/shard_map/ppermute | solution.py:559
  63.5 5.0 %collective-permute-start.23 = (bf16[272,128]{1,0:T(8,128)(2,1)S(1)}, bf16[272,128]{1,0:T(8,128)(2,1)S(1)}, u32[]{:S(2)}, u32[]{:S(2)}) collective-permute-start(bf16[272,128]{1,0:T(8,128)(2,1)S(1)} %get-tuple-element.112.refs_0_), channel_id=1, source_target_pairs={{0,2},{2,0},{4,6},{6,4},{1,3},{3,1},{5,7},{7,5},{8,10},{10,8},{12,... | collective-permute-start | bytes 208904 | tf_op jit(solution)/shard_map/ppermute | solution.py:559
  64.7 6.1 %collective-permute-start.22 = (bf16[272,128]{1,0:T(8,128)(2,1)S(1)}, bf16[272,128]{1,0:T(8,128)(2,1)S(1)}, u32[]{:S(2)}, u32[]{:S(2)}) collective-permute-start(bf16[272,128]{1,0:T(8,128)(2,1)S(1)} %get-tuple-element.112.refs_0_), channel_id=1, source_target_pairs={{0,6},{2,4},{4,2},{6,0},{1,7},{3,5},{5,3},{7,1},{8,14},{10,12},{12... | collective-permute-start | bytes 208904 | tf_op jit(solution)/shard_map/ppermute | solution.py:559
  72.0 5.2 %collective-permute-start.27 = (bf16[144,128]{1,0:T(8,128)(2,1)S(1)}, bf16[144,128]{1,0:T(8,128)(2,1)S(1)}, u32[]{:S(2)}, u32[]{:S(2)}) collective-permute-start(bf16[144,128]{1,0:T(8,128)(2,1)S(1)} %get-tuple-element.131.refs_0_), channel_id=1, source_target_pairs={{0,4},{2,6},{4,0},{6,2},{1,5},{3,7},{5,1},{7,3},{8,12},{10,14},{12... | collective-permute-start | bytes 110600 | tf_op jit(solution)/shard_map/ppermute | solution.py:559
  72.1 5.1 %collective-permute-start.26 = (bf16[144,128]{1,0:T(8,128)(2,1)S(1)}, bf16[144,128]{1,0:T(8,128)(2,1)S(1)}, u32[]{:S(2)}, u32[]{:S(2)}) collective-permute-start(bf16[144,128]{1,0:T(8,128)(2,1)S(1)} %get-tuple-element.131.refs_0_), channel_id=1, source_target_pairs={{0,2},{2,0},{4,6},{6,4},{1,3},{3,1},{5,7},{7,5},{8,10},{10,8},{12,... | collective-permute-start | bytes 110600 | tf_op jit(solution)/shard_map/ppermute | solution.py:559
  74.3 5.8 %collective-permute-start.25 = (bf16[144,128]{1,0:T(8,128)(2,1)S(1)}, bf16[144,128]{1,0:T(8,128)(2,1)S(1)}, u32[]{:S(2)}, u32[]{:S(2)}) collective-permute-start(bf16[144,128]{1,0:T(8,128)(2,1)S(1)} %get-tuple-element.131.refs_0_), channel_id=1, source_target_pairs={{0,6},{2,4},{4,2},{6,0},{1,7},{3,5},{5,3},{7,1},{8,14},{10,12},{12... | collective-permute-start | bytes 110600 | tf_op jit(solution)/shard_map/ppermute | solution.py:559
  81.4 5.3 %collective-permute-start.30 = (bf16[144,128]{1,0:T(8,128)(2,1)S(1)}, bf16[144,128]{1,0:T(8,128)(2,1)S(1)}, u32[]{:S(2)}, u32[]{:S(2)}) collective-permute-start(bf16[144,128]{1,0:T(8,128)(2,1)S(1)} %get-tuple-element.146.refs_0_), channel_id=1, source_target_pairs={{0,4},{2,6},{4,0},{6,2},{1,5},{3,7},{5,1},{7,3},{8,12},{10,14},{12... | collective-permute-start | bytes 110600 | tf_op jit(solution)/shard_map/ppermute | solution.py:559
  81.4 5.3 %collective-permute-start.29 = (bf16[144,128]{1,0:T(8,128)(2,1)S(1)}, bf16[144,128]{1,0:T(8,128)(2,1)S(1)}, u32[]{:S(2)}, u32[]{:S(2)}) collective-permute-start(bf16[144,128]{1,0:T(8,128)(2,1)S(1)} %get-tuple-element.146.refs_0_), channel_id=1, source_target_pairs={{0,2},{2,0},{4,6},{6,4},{1,3},{3,1},{5,7},{7,5},{8,10},{10,8},{12,... | collective-permute-start | bytes 110600 | tf_op jit(solution)/shard_map/ppermute | solution.py:559
  84.3 5.8 %collective-permute-start.28 = (bf16[144,128]{1,0:T(8,128)(2,1)S(1)}, bf16[144,128]{1,0:T(8,128)(2,1)S(1)}, u32[]{:S(2)}, u32[]{:S(2)}) collective-permute-start(bf16[144,128]{1,0:T(8,128)(2,1)S(1)} %get-tuple-element.146.refs_0_), channel_id=1, source_target_pairs={{0,6},{2,4},{4,2},{6,0},{1,7},{3,5},{5,3},{7,1},{8,14},{10,12},{12... | collective-permute-start | bytes 110600 | tf_op jit(solution)/shard_map/ppermute | solution.py:559
  85.8 6.1 %collective-permute-start.33 = (bf16[272,512]{1,0:T(8,128)(2,1)S(1)}, bf16[272,512]{1,0:T(8,128)(2,1)S(1)}, u32[]{:S(2)}, u32[]{:S(2)}) collective-permute-start(bf16[272,512]{1,0:T(8,128)(2,1)S(1)} %get-tuple-element.161), channel_id=1, source_target_pairs={{0,1},{1,0},{2,3},{3,2},{4,5},{5,4},{6,7},{7,6},{8,9},{9,8},{10,11... | collective-permute-start | bytes 835592 | tf_op jit(solution)/shard_map/ppermute | solution.py:565
  85.8 6.1 %collective-permute-start.34 = (bf16[272,512]{1,0:T(8,128)(2,1)S(1)}, bf16[272,512]{1,0:T(8,128)(2,1)S(1)}, u32[]{:S(2)}, u32[]{:S(2)}) collective-permute-start(bf16[272,512]{1,0:T(8,128)(2,1)S(1)} %get-tuple-element.162), channel_id=1, source_target_pairs={{0,1},{1,0},{2,3},{3,2},{4,5},{5,4},{6,7},{7,6},{8,9},{9,8},{10,11... | collective-permute-start | bytes 835592 | tf_op jit(solution)/shard_map/ppermute | solution.py:565
  93.9 9.6 %collective-permute-start.35 = (bf16[272,512]{1,0:T(8,128)(2,1)S(1)}, bf16[272,512]{1,0:T(8,128)(2,1)S(1)}, u32[]{:S(2)}, u32[]{:S(2)}) collective-permute-start(bf16[272,512]{1,0:T(8,128)(2,1)S(1)} %get-tuple-element.164), channel_id=1, source_target_pairs={{0,8},{8,0},{16,24},{24,16},{1,9},{9,1},{17,25},{25,17},{2,10},{10... | collective-permute-start | bytes 835592 | tf_op jit(solution)/shard_map/ppermute | solution.py:562
  95.4 14.4 %collective-permute-start.36 = (bf16[272,512]{1,0:T(8,128)(2,1)S(1)}, bf16[272,512]{1,0:T(8,128)(2,1)S(1)}, u32[]{:S(2)}, u32[]{:S(2)}) collective-permute-start(bf16[272,512]{1,0:T(8,128)(2,1)S(1)} %get-tuple-element.165), channel_id=1, source_target_pairs={{0,16},{8,24},{16,0},{24,8},{1,17},{9,25},{17,1},{25,9},{2,18},{10... | collective-permute-start | bytes 835592 | tf_op jit(solution)/shard_map/ppermute | solution.py:562
  96.9 13.0 %collective-permute-start.37 = (bf16[272,512]{1,0:T(8,128)(2,1)S(1)}, bf16[272,512]{1,0:T(8,128)(2,1)S(1)}, u32[]{:S(2)}, u32[]{:S(2)}) collective-permute-start(bf16[272,512]{1,0:T(8,128)(2,1)S(1)} %get-tuple-element.166), channel_id=1, source_target_pairs={{0,24},{8,16},{16,8},{24,0},{1,25},{9,17},{17,9},{25,1},{2,26},{10... | collective-permute-start | bytes 835592 | tf_op jit(solution)/shard_map/ppermute | solution.py:562
  (8 other events, 12.8 us)

commit v13 on v12

--- a/solution.py
+++ b/solution.py
@@ -234,9 +234,10 @@
         ).astype(BF)
 
 
-def own_kernel(part, packed, part_out, packed_out):
+def own_kernel(part, packed, early, part_out, packed_out, early_out):
     part_out[...] = part[...]
     packed_out[...] = packed[...]
+    early_out[...] = early[...]
 
 
 def arrange_kernel(length, order, *refs):
@@ -482,11 +483,13 @@
     dred_out[...] = dred
 
 
-def split_grads(first, second, gain_row, wide, keep, send):
-    rank = first.shape[0]
+def split_grads(dred, mixed, second, gain_row, wide, keep, send):
+    rank = second.shape[0]
     own = keep.shape[1]
     core = lax.axis_index("core")
-    wide[0:rank, :] = first.astype(BF)
+    for head in range(mixed.shape[1] // HD):
+        part = slice(head * HD, (head + 1) * HD)
+        wide[0:HD, head * rank : (head + 1) * rank] = dot_tn(mixed[:, part], dred).astype(BF)
     wide[rank : 2 * rank, :] = second.astype(BF)
     if gain_row is not None:
         wide[2 * rank :, :] = gain_row[...]
@@ -500,8 +503,8 @@
     rows = dout.shape[0]
     height = sources[0].shape[0]
     reduced = total_of(sources, height - rows, height).astype(BF)
-    first, second = dot_tn(dred[...], mixed[...]), dot_tn(reduced, dout[...])
-    split_grads(first, second, gain_row, wide, keep, send)
+    second = dot_tn(reduced, dout[...])
+    split_grads(dred[...], mixed, second, gain_row, wide, keep, send)
 
 
 def back_first_kernel(count, width, *refs):
@@ -510,12 +513,12 @@
     reduced, keep, send, wide = refs[9:]
     rank = reduced.shape[1]
     dout, dred = receive_backward(pays, carried_after, x_after, mean_after, cross_after, width)
-    first, second = dot_tn(dred, mixed[...]), dot_tn(reduced[...], dout)
+    second = dot_tn(reduced[...], dout)
     layer_backward(
         dout, dred, x, mean[:, 0:1], layer_of(weights, 0), None, probs, wide.at[pl.ds(2 * rank, 16)],
         None, None,
     )
-    split_grads(first, second, None, wide, keep, send)
+    split_grads(dred, mixed, second, None, wide, keep, send)
 
 
 def combine_kernel(sections, *refs):
@@ -535,7 +538,8 @@
     total = parts[0][...].astype(F32)
     for part in parts[1:]:
         total = total + part[...].astype(F32)
-    first[0] = total[0:rank].T
+    for block in range(first.shape[1] // HD):
+        first[0, block * HD : (block + 1) * HD, :] = total[0:HD, block * rank : (block + 1) * rank]
     second[0] = total[rank : 2 * rank]
     gain[...] = total[2 * rank : 2 * rank + 1]
 
@@ -564,10 +568,8 @@
     def swapped(value):
         return lax.ppermute(value, "core", [(i, 1 - i) for i in range(sides)])
 
-    exchange_order = sorted(range(1, groups), key=lambda place: (place != 3, place))
-
     def exchange(pay):
-        return [pay] + [shifted(pay, place) for place in exchange_order]
+        return [pay] + [shifted(pay, place) for place in range(1, groups)]
 
     token_parts, packed = pack(
         tokens, cotangents, starts, counts, layer_gains, first_map, second_map, groups, micro_local
@@ -589,11 +591,11 @@
             **more,
         )(*operands)
 
-    received[0], mine[0] = call(
+    received[0], mine[0], mine[1] = call(
         own_kernel,
-        (received[0], packed),
-        vmem_specs(2),
-        [shaped(received[0].shape), shaped(packed.shape)],
+        (received[0], packed, mine[1]),
+        vmem_specs(3),
+        [shaped(received[0].shape), shaped(packed.shape), shaped(packed.shape)],
         "own_parts",
     )
     received, mine = lax.optimization_barrier((received, mine))

time: 111 us -> 109 us (0.982)
  starting transfers between devices: 52.1 us -> 47.6 us
  waiting for transfers between devices: 40.5 us -> 42.6 us
    ppermute x24, starting transfers between devices: 43 us -> 37.4 us  [shifted(): return lax.ppermute(value, 'z', [(i, i ^ shift) for i in range(groups)])]
    ppermute x24, waiting for transfers between devices: 24.3 us -> 25.5 us  [shifted(): return lax.ppermute(value, 'z', [(i, i ^ shift) for i in range(groups)])]
  transfers between devices with their start and end apart: 38 -> 38, of which waited for: 23 -> 21; matrix products, arithmetic and copies ran while one was open for 0% -> 0% of each run, Pallas kernels for 4% -> 4%
where the time goes in v13:
time: 109 us; the launch traced here: 108 us
  starting transfers between devices  47.6 us (44%)
  waiting for transfers between devices  42.6 us (39%)
  Pallas kernels  15.5 us (14%)
  local copies, waits for them, and re-layouts  1.86 us (2%)
    ppermute x24, starting transfers between devices, shifted(): return lax.ppermute(value, 'z', [(i, i ^ shift) for i in range(groups)])  37.4 us
    ppermute x24, waiting for transfers between devices, shifted(): return lax.ppermute(value, 'z', [(i, i ^ shift) for i in range(groups)])  25.5 us
    ppermute x6, waiting for transfers between devices, across(): lax.ppermute(value, 'pipe', [(i, i ^ distance) for i in range(sections)])  14.2 us
    pallas_call x15, Pallas kernels, call(): pl.pallas_call(kernel, in_specs=specs, out_specs=vmem_specs(len(outs)), o...  13.2 us
    ppermute x6, starting transfers between devices, across(): lax.ppermute(value, 'pipe', [(i, i ^ distance) for i in range(sections)])  8.1 us
    ppermute x8, waiting for transfers between devices, swapped(): return lax.ppermute(value, 'core', [(i, 1 - i) for i in range(sides)])  2.86 us
    pallas_call x1, Pallas kernels, pack(): pl.pallas_call(functools.partial(pack_kernel, groups, micro_local), in_sp...  2.28 us
  transfers between devices with their start and end apart: 38, of which 21 were waited for; matrix products, arithmetic and copies ran while one was open for 0% of the time, Pallas kernels for 4%

profile of v13, /device:TPU:0, one launch (start us, length us, event | category | flops | bytes accessed | tf_op | source)
XLA Modules:
  0.0 108.4 jit_solution(423294876198432455)
XLA Ops:
  0.6 2.3 %pack.1 = (bf16[32,2176]{1,0:T(8,128)(2,1)}, bf16[32,2176]{1,0:T(8,128)(2,1)}, bf16[32,2176]{1,0:T(8,128)(2,1)}, bf16[32,2176]{1,0:T(8,128)(2,1)}, bf16[1040,128]{1,0:T(8,128)(2,1)}) custom-call(bf16[2,2,32,4096]{3,2,1,0:T(8,128)(2,1)} %refs_0_.1, bf16[2,2,32,4096]{3,2,1,0:T(8,128)(2,1)} %refs_1_.1, s32[2,2,4]{2,1,0:T(2,128)} %refs_2_.1, s32[2,2]{1,0:T(2,128)} %refs_3_.1, ...), custom_call_target="tpu_custom_call" | custom-call | tf_op jit(solution)/shard_map/pack/pallas_call | solution.py:124
  2.9 3.0 %collective-permute-start = (bf16[1040,128]{1,0:T(8,128)(2,1)}, bf16[1040,128]{1,0:T(8,128)(2,1)S(1)}, u32[]{:S(2)}, u32[]{:S(2)}) collective-permute-start(bf16[1040,128]{1,0:T(8,128)(2,1)} %get-tuple-element.87.packed), channel_id=1, source_target_pairs={{0,8},{8,0},{16,24},{24,16},{1,9},{9,1},{17,25},{25,17},{2,10},{10... | collective-permute-start | bytes 798728 | tf_op jit(solution)/shard_map/ppermute | solution.py:566
  7.5 4.1 %collective-permute-start.1 = (bf16[32,2176]{1,0:T(8,128)(2,1)}, bf16[32,2176]{1,0:T(8,128)(2,1)S(1)}, u32[]{:S(2)}, u32[]{:S(2)}) collective-permute-start(bf16[32,2176]{1,0:T(8,128)(2,1)} %get-tuple-element.89), channel_id=1, source_target_pairs={{0,6},{2,4},{4,2},{6,0},{1,7},{3,5},{5,3},{7,1},{8,14},{10,12},{12... | collective-permute-start | bytes 417800 | tf_op jit(solution)/shard_map/ppermute | solution.py:563
  11.5 1.8 %collective-permute-done.early = bf16[1040,128]{1,0:T(8,128)(2,1)S(1)} collective-permute-done((bf16[1040,128]{1,0:T(8,128)(2,1)}, bf16[1040,128]{1,0:T(8,128)(2,1)S(1)}, u32[]{:S(2)}, u32[]{:S(2)}) %collective-permute-start) | collective-permute-done | bytes 266272 | tf_op jit(solution)/shard_map/ppermute | solution.py:566
  13.4 2.1 %collective-permute-start.3 = (bf16[32,2176]{1,0:T(8,128)(2,1)}, bf16[32,2176]{1,0:T(8,128)(2,1)S(1)}, u32[]{:S(2)}, u32[]{:S(2)}) collective-permute-start(bf16[32,2176]{1,0:T(8,128)(2,1)} %get-tuple-element.91), channel_id=1, source_target_pairs={{0,2},{2,0},{4,6},{6,4},{1,3},{3,1},{5,7},{7,5},{8,10},{10,8},{12,... | collective-permute-start | bytes 417800 | tf_op jit(solution)/shard_map/ppermute | solution.py:563
  17.4 5.3 %collective-permute-done.2.refs_2_ = bf16[32,2176]{1,0:T(8,128)(2,1)S(1)} collective-permute-done((bf16[32,2176]{1,0:T(8,128)(2,1)}, bf16[32,2176]{1,0:T(8,128)(2,1)S(1)}, u32[]{:S(2)}, u32[]{:S(2)}) %collective-permute-start.2) | collective-permute-done | bytes 139296 | tf_op jit(solution)/shard_map/ppermute | solution.py:563
  25.4 1.6 %forward_first.1 = (bf16[1,8,128,128]{3,2,1,0:T(8,128)(2,1)S(1)}, bf16[128,1024]{1,0:T(8,128)(2,1)S(1)}, bf16[400,128]{1,0:T(8,128)(2,1)S(1)}, bf16[4,2,1040,128]{3,2,1,0:T(8,128)(2,1)S(1)}) custom-call(bf16[1040,128]{1,0:T(8,128)(2,1)S(1)} %get-tuple-element.94.refs_0_, bf16[1040,128]{1,0:T(8,128)(2,1)S(1)} %get-tuple-element.95.refs_1_, ...), custom_call_target="tpu_custom_call" | custom-call | tf_op jit(solution)/shard_map/forward_first/pallas_call | solution.py:584
  27.0 2.5 %collective-permute-start.12 = (bf16[400,128]{1,0:T(8,128)(2,1)S(1)}, bf16[400,128]{1,0:T(8,128)(2,1)S(1)}, u32[]{:S(2)}, u32[]{:S(2)}) collective-permute-start(bf16[400,128]{1,0:T(8,128)(2,1)S(1)} %get-tuple-element.105.refs_0_.refs_4_), channel_id=1, source_target_pairs={{0,6},{2,4},{4,2},{6,0},{1,7},{3,5},{5,3},{7,1},{8,14},{10,12},{12... | collective-permute-start | bytes 307208 | tf_op jit(solution)/shard_map/ppermute | solution.py:563
  29.5 1.9 %collective-permute-start.10 = (bf16[400,128]{1,0:T(8,128)(2,1)S(1)}, bf16[400,128]{1,0:T(8,128)(2,1)S(1)}, u32[]{:S(2)}, u32[]{:S(2)}) collective-permute-start(bf16[400,128]{1,0:T(8,128)(2,1)S(1)} %get-tuple-element.105.refs_0_.refs_4_), channel_id=1, source_target_pairs={{0,2},{2,0},{4,6},{6,4},{1,3},{3,1},{5,7},{7,5},{8,10},{10,8},{12,... | collective-permute-start | bytes 307208 | tf_op jit(solution)/shard_map/ppermute | solution.py:563
  31.4 3.2 %collective-permute-done.12.refs_3_.refs_7_ = bf16[400,128]{1,0:T(8,128)(2,1)S(1)} collective-permute-done((bf16[400,128]{1,0:T(8,128)(2,1)S(1)}, bf16[400,128]{1,0:T(8,128)(2,1)S(1)}, u32[]{:S(2)}, u32[]{:S(2)}) %collective-permute-start.12) | collective-permute-done | bytes 102432 | tf_op jit(solution)/shard_map/ppermute | solution.py:563
  34.7 3.5 %collective-permute-done.11.refs_2_.refs_6_ = bf16[400,128]{1,0:T(8,128)(2,1)S(1)} collective-permute-done((bf16[400,128]{1,0:T(8,128)(2,1)S(1)}, bf16[400,128]{1,0:T(8,128)(2,1)S(1)}, u32[]{:S(2)}, u32[]{:S(2)}) %collective-permute-start.11) | collective-permute-done | bytes 102432 | tf_op jit(solution)/shard_map/ppermute | solution.py:563
  39.5 2.5 %collective-permute-start.15 = (bf16[256,128]{1,0:T(8,128)(2,1)S(1)}, bf16[256,128]{1,0:T(8,128)(2,1)S(1)}, u32[]{:S(2)}, u32[]{:S(2)}) collective-permute-start(bf16[256,128]{1,0:T(8,128)(2,1)S(1)} %get-tuple-element.107.refs_0_), channel_id=1, source_target_pairs={{0,6},{2,4},{4,2},{6,0},{1,7},{3,5},{5,3},{7,1},{8,14},{10,12},{12... | collective-permute-start | bytes 196616 | tf_op jit(solution)/shard_map/ppermute | solution.py:563
  42.0 1.9 %collective-permute-start.13 = (bf16[256,128]{1,0:T(8,128)(2,1)S(1)}, bf16[256,128]{1,0:T(8,128)(2,1)S(1)}, u32[]{:S(2)}, u32[]{:S(2)}) collective-permute-start(bf16[256,128]{1,0:T(8,128)(2,1)S(1)} %get-tuple-element.107.refs_0_), channel_id=1, source_target_pairs={{0,2},{2,0},{4,6},{6,4},{1,3},{3,1},{5,7},{7,5},{8,10},{10,8},{12,... | collective-permute-start | bytes 196616 | tf_op jit(solution)/shard_map/ppermute | solution.py:563
  44.3 2.5 %collective-permute-start.21 = (bf16[256,128]{1,0:T(8,128)(2,1)S(1)}, bf16[256,128]{1,0:T(8,128)(2,1)S(1)}, u32[]{:S(2)}, u32[]{:S(2)}) collective-permute-start(bf16[256,128]{1,0:T(8,128)(2,1)S(1)} %side.1.refs_4_), channel_id=1, source_target_pairs={{0,6},{2,4},{4,2},{6,0},{1,7},{3,5},{5,3},{7,1},{8,14},{10,12},{12... | collective-permute-start | bytes 196616 | tf_op jit(solution)/shard_map/ppermute | solution.py:563
  46.8 1.9 %collective-permute-start.19 = (bf16[256,128]{1,0:T(8,128)(2,1)S(1)}, bf16[256,128]{1,0:T(8,128)(2,1)S(1)}, u32[]{:S(2)}, u32[]{:S(2)}) collective-permute-start(bf16[256,128]{1,0:T(8,128)(2,1)S(1)} %side.1.refs_4_), channel_id=1, source_target_pairs={{0,2},{2,0},{4,6},{6,4},{1,3},{3,1},{5,7},{7,5},{8,10},{10,8},{12,... | collective-permute-start | bytes 196616 | tf_op jit(solution)/shard_map/ppermute | solution.py:563
  50.1 3.5 %collective-permute-start.18 = (bf16[256,128]{1,0:T(8,128)(2,1)S(1)}, bf16[256,128]{1,0:T(8,128)(2,1)S(1)}, u32[]{:S(2)}, u32[]{:S(2)}) collective-permute-start(bf16[256,128]{1,0:T(8,128)(2,1)S(1)} %get-tuple-element.110.refs_0_), channel_id=1, source_target_pairs={{0,6},{2,4},{4,2},{6,0},{1,7},{3,5},{5,3},{7,1},{8,14},{10,12},{12... | collective-permute-start | bytes 196616 | tf_op jit(solution)/shard_map/ppermute | solution.py:563
  54.6 2.0 %collective-permute-done.18.refs_3_ = bf16[256,128]{1,0:T(8,128)(2,1)S(1)} collective-permute-done((bf16[256,128]{1,0:T(8,128)(2,1)S(1)}, bf16[256,128]{1,0:T(8,128)(2,1)S(1)}, u32[]{:S(2)}, u32[]{:S(2)}) %collective-permute-start.18) | collective-permute-done | bytes 65568 | tf_op jit(solution)/shard_map/ppermute | solution.py:563
  56.6 2.9 %collective-permute-done.17.refs_2_ = bf16[256,128]{1,0:T(8,128)(2,1)S(1)} collective-permute-done((bf16[256,128]{1,0:T(8,128)(2,1)S(1)}, bf16[256,128]{1,0:T(8,128)(2,1)S(1)}, u32[]{:S(2)}, u32[]{:S(2)}) %collective-permute-start.17) | collective-permute-done | bytes 65568 | tf_op jit(solution)/shard_map/ppermute | solution.py:563
  59.4 2.1 %turn.1 = (bf16[128,1024]{1,0:T(8,128)(2,1)S(1)}, f32[128,128]{1,0:T(8,128)S(1)}, bf16[128,128]{1,0:T(8,128)(2,1)S(1)}, f32[128,128]{1,0:T(8,128)S(1)}, bf16[128...) custom-call(bf16[256,128]{1,0:T(8,128)(2,1)S(1)} %get-tuple-element., ...), custom_call_target="tpu_custom_call" | custom-call | tf_op jit(solution)/shard_map/turn/pallas_call | solution.py:584
  61.5 2.5 %collective-permute-start.24 = (bf16[272,128]{1,0:T(8,128)(2,1)S(1)}, bf16[272,128]{1,0:T(8,128)(2,1)S(1)}, u32[]{:S(2)}, u32[]{:S(2)}) collective-permute-start(bf16[272,128]{1,0:T(8,128)(2,1)S(1)} %get-tuple-element.114.refs_0_), channel_id=1, source_target_pairs={{0,6},{2,4},{4,2},{6,0},{1,7},{3,5},{5,3},{7,1},{8,14},{10,12},{12... | collective-permute-start | bytes 208904 | tf_op jit(solution)/shard_map/ppermute | solution.py:563
  64.0 1.9 %collective-permute-start.22 = (bf16[272,128]{1,0:T(8,128)(2,1)S(1)}, bf16[272,128]{1,0:T(8,128)(2,1)S(1)}, u32[]{:S(2)}, u32[]{:S(2)}) collective-permute-start(bf16[272,128]{1,0:T(8,128)(2,1)S(1)} %get-tuple-element.114.refs_0_), channel_id=1, source_target_pairs={{0,2},{2,0},{4,6},{6,4},{1,3},{3,1},{5,7},{7,5},{8,10},{10,8},{12,... | collective-permute-start | bytes 208904 | tf_op jit(solution)/shard_map/ppermute | solution.py:563
  66.0 2.4 %collective-permute-done.24.refs_3_ = bf16[272,128]{1,0:T(8,128)(2,1)S(1)} collective-permute-done((bf16[272,128]{1,0:T(8,128)(2,1)S(1)}, bf16[272,128]{1,0:T(8,128)(2,1)S(1)}, u32[]{:S(2)}, u32[]{:S(2)}) %collective-permute-start.24) | collective-permute-done | bytes 69664 | tf_op jit(solution)/shard_map/ppermute | solution.py:563
  68.3 2.1 %collective-permute-done.23.refs_2_ = bf16[272,128]{1,0:T(8,128)(2,1)S(1)} collective-permute-done((bf16[272,128]{1,0:T(8,128)(2,1)S(1)}, bf16[272,128]{1,0:T(8,128)(2,1)S(1)}, u32[]{:S(2)}, u32[]{:S(2)}) %collective-permute-start.23) | collective-permute-done | bytes 69664 | tf_op jit(solution)/shard_map/ppermute | solution.py:563
  71.7 2.5 %collective-permute-start.27 = (bf16[144,128]{1,0:T(8,128)(2,1)S(1)}, bf16[144,128]{1,0:T(8,128)(2,1)S(1)}, u32[]{:S(2)}, u32[]{:S(2)}) collective-permute-start(bf16[144,128]{1,0:T(8,128)(2,1)S(1)} %get-tuple-element.133.refs_0_), channel_id=1, source_target_pairs={{0,6},{2,4},{4,2},{6,0},{1,7},{3,5},{5,3},{7,1},{8,14},{10,12},{12... | collective-permute-start | bytes 110600 | tf_op jit(solution)/shard_map/ppermute | solution.py:563
  74.3 1.9 %collective-permute-start.25 = (bf16[144,128]{1,0:T(8,128)(2,1)S(1)}, bf16[144,128]{1,0:T(8,128)(2,1)S(1)}, u32[]{:S(2)}, u32[]{:S(2)}) collective-permute-start(bf16[144,128]{1,0:T(8,128)(2,1)S(1)} %get-tuple-element.133.refs_0_), channel_id=1, source_target_pairs={{0,2},{2,0},{4,6},{6,4},{1,3},{3,1},{5,7},{7,5},{8,10},{10,8},{12,... | collective-permute-start | bytes 110600 | tf_op jit(solution)/shard_map/ppermute | solution.py:563
  77.6 1.6 %collective-permute-done.26.refs_2_ = bf16[144,128]{1,0:T(8,128)(2,1)S(1)} collective-permute-done((bf16[144,128]{1,0:T(8,128)(2,1)S(1)}, bf16[144,128]{1,0:T(8,128)(2,1)S(1)}, u32[]{:S(2)}, u32[]{:S(2)}) %collective-permute-start.26) | collective-permute-done | bytes 36896 | tf_op jit(solution)/shard_map/ppermute | solution.py:563
  80.4 2.0 %collective-permute-start.30 = (bf16[144,128]{1,0:T(8,128)(2,1)S(1)}, bf16[144,128]{1,0:T(8,128)(2,1)S(1)}, u32[]{:S(2)}, u32[]{:S(2)}) collective-permute-start(bf16[144,128]{1,0:T(8,128)(2,1)S(1)} %get-tuple-element.148.refs_0_), channel_id=1, source_target_pairs={{0,6},{2,4},{4,2},{6,0},{1,7},{3,5},{5,3},{7,1},{8,14},{10,12},{12... | collective-permute-start | bytes 110600 | tf_op jit(solution)/shard_map/ppermute | solution.py:563
  82.9 1.9 %collective-permute-start.28 = (bf16[144,128]{1,0:T(8,128)(2,1)S(1)}, bf16[144,128]{1,0:T(8,128)(2,1)S(1)}, u32[]{:S(2)}, u32[]{:S(2)}) collective-permute-start(bf16[144,128]{1,0:T(8,128)(2,1)S(1)} %get-tuple-element.148.refs_0_), channel_id=1, source_target_pairs={{0,2},{2,0},{4,6},{6,4},{1,3},{3,1},{5,7},{7,5},{8,10},{10,8},{12,... | collective-permute-start | bytes 110600 | tf_op jit(solution)/shard_map/ppermute | solution.py:563
  91.6 1.5 %collective-permute-start.35 = (bf16[272,512]{1,0:T(8,128)(2,1)S(1)}, bf16[272,512]{1,0:T(8,128)(2,1)S(1)}, u32[]{:S(2)}, u32[]{:S(2)}) collective-permute-start(bf16[272,512]{1,0:T(8,128)(2,1)S(1)} %get-tuple-element.166), channel_id=1, source_target_pairs={{0,8},{8,0},{16,24},{24,16},{1,9},{9,1},{17,25},{25,17},{2,10},{10... | collective-permute-start | bytes 835592 | tf_op jit(solution)/shard_map/ppermute | solution.py:566
  93.1 1.5 %collective-permute-start.36 = (bf16[272,512]{1,0:T(8,128)(2,1)S(1)}, bf16[272,512]{1,0:T(8,128)(2,1)S(1)}, u32[]{:S(2)}, u32[]{:S(2)}) collective-permute-start(bf16[272,512]{1,0:T(8,128)(2,1)S(1)} %get-tuple-element.167), channel_id=1, source_target_pairs={{0,16},{8,24},{16,0},{24,8},{1,17},{9,25},{17,1},{25,9},{2,18},{10... | collective-permute-start | bytes 835592 | tf_op jit(solution)/shard_map/ppermute | solution.py:566
  95.1 6.0 %collective-permute-done.35.refs_1_ = bf16[272,512]{1,0:T(8,128)(2,1)S(1)} collective-permute-done((bf16[272,512]{1,0:T(8,128)(2,1)S(1)}, bf16[272,512]{1,0:T(8,128)(2,1)S(1)}, u32[]{:S(2)}, u32[]{:S(2)}) %collective-permute-start.35) | collective-permute-done | bytes 278560 | tf_op jit(solution)/shard_map/ppermute | solution.py:566
  101.1 6.4 %collective-permute-done.36.refs_2_ = bf16[272,512]{1,0:T(8,128)(2,1)S(1)} collective-permute-done((bf16[272,512]{1,0:T(8,128)(2,1)S(1)}, bf16[272,512]{1,0:T(8,128)(2,1)S(1)}, u32[]{:S(2)}, u32[]{:S(2)}) %collective-permute-start.36) | collective-permute-done | bytes 278560 | tf_op jit(solution)/shard_map/ppermute | solution.py:566
  (64 shorter events, 22.7 us)
Async XLA Ops:
  2.9 10.4 %collective-permute-start = (bf16[1040,128]{1,0:T(8,128)(2,1)}, bf16[1040,128]{1,0:T(8,128)(2,1)S(1)}, u32[]{:S(2)}, u32[]{:S(2)}) collective-permute-start(bf16[1040,128]{1,0:T(8,128)(2,1)} %get-tuple-element.87.packed), channel_id=1, source_target_pairs={{0,8},{8,0},{16,24},{24,16},{1,9},{9,1},{17,25},{25,17},{2,10},{10... | collective-permute-start | bytes 798728 | tf_op jit(solution)/shard_map/ppermute | solution.py:566
  5.9 16.8 %collective-permute-start.5 = (bf16[1040,128]{1,0:T(8,128)(2,1)}, bf16[1040,128]{1,0:T(8,128)(2,1)S(1)}, u32[]{:S(2)}, u32[]{:S(2)}) collective-permute-start(bf16[1040,128]{1,0:T(8,128)(2,1)} %get-tuple-element.87.packed), channel_id=1, source_target_pairs={{0,24},{8,16},{16,8},{24,0},{1,25},{9,17},{17,9},{25,1},{2,26},{10... | collective-permute-start | bytes 798728 | tf_op jit(solution)/shard_map/ppermute | solution.py:566
  7.4 15.3 %collective-permute-start.4 = (bf16[1040,128]{1,0:T(8,128)(2,1)}, bf16[1040,128]{1,0:T(8,128)(2,1)S(1)}, u32[]{:S(2)}, u32[]{:S(2)}) collective-permute-start(bf16[1040,128]{1,0:T(8,128)(2,1)} %get-tuple-element.87.packed), channel_id=1, source_target_pairs={{0,16},{8,24},{16,0},{24,8},{1,17},{9,25},{17,1},{25,9},{2,18},{10... | collective-permute-start | bytes 798728 | tf_op jit(solution)/shard_map/ppermute | solution.py:566
  7.5 9.9 %collective-permute-start.1 = (bf16[32,2176]{1,0:T(8,128)(2,1)}, bf16[32,2176]{1,0:T(8,128)(2,1)S(1)}, u32[]{:S(2)}, u32[]{:S(2)}) collective-permute-start(bf16[32,2176]{1,0:T(8,128)(2,1)} %get-tuple-element.89), channel_id=1, source_target_pairs={{0,6},{2,4},{4,2},{6,0},{1,7},{3,5},{5,3},{7,1},{8,14},{10,12},{12... | collective-permute-start | bytes 417800 | tf_op jit(solution)/shard_map/ppermute | solution.py:563
  11.5 11.1 %collective-permute-start.2 = (bf16[32,2176]{1,0:T(8,128)(2,1)}, bf16[32,2176]{1,0:T(8,128)(2,1)S(1)}, u32[]{:S(2)}, u32[]{:S(2)}) collective-permute-start(bf16[32,2176]{1,0:T(8,128)(2,1)} %get-tuple-element.90), channel_id=1, source_target_pairs={{0,4},{2,6},{4,0},{6,2},{1,5},{3,7},{5,1},{7,3},{8,12},{10,14},{12... | collective-permute-start | bytes 417800 | tf_op jit(solution)/shard_map/ppermute | solution.py:563
  13.4 9.3 %collective-permute-start.3 = (bf16[32,2176]{1,0:T(8,128)(2,1)}, bf16[32,2176]{1,0:T(8,128)(2,1)S(1)}, u32[]{:S(2)}, u32[]{:S(2)}) collective-permute-start(bf16[32,2176]{1,0:T(8,128)(2,1)} %get-tuple-element.91), channel_id=1, source_target_pairs={{0,2},{2,0},{4,6},{6,4},{1,3},{3,1},{5,7},{7,5},{8,10},{10,8},{12,... | collective-permute-start | bytes 417800 | tf_op jit(solution)/shard_map/ppermute | solution.py:563
  27.0 7.7 %collective-permute-start.12 = (bf16[400,128]{1,0:T(8,128)(2,1)S(1)}, bf16[400,128]{1,0:T(8,128)(2,1)S(1)}, u32[]{:S(2)}, u32[]{:S(2)}) collective-permute-start(bf16[400,128]{1,0:T(8,128)(2,1)S(1)} %get-tuple-element.105.refs_0_.refs_4_), channel_id=1, source_target_pairs={{0,6},{2,4},{4,2},{6,0},{1,7},{3,5},{5,3},{7,1},{8,14},{10,12},{12... | collective-permute-start | bytes 307208 | tf_op jit(solution)/shard_map/ppermute | solution.py:563
  29.5 8.6 %collective-permute-start.11 = (bf16[400,128]{1,0:T(8,128)(2,1)S(1)}, bf16[400,128]{1,0:T(8,128)(2,1)S(1)}, u32[]{:S(2)}, u32[]{:S(2)}) collective-permute-start(bf16[400,128]{1,0:T(8,128)(2,1)S(1)} %get-tuple-element.105.refs_0_.refs_4_), channel_id=1, source_target_pairs={{0,4},{2,6},{4,0},{6,2},{1,5},{3,7},{5,1},{7,3},{8,12},{10,14},{12... | collective-permute-start | bytes 307208 | tf_op jit(solution)/shard_map/ppermute | solution.py:563
  29.5 8.6 %collective-permute-start.10 = (bf16[400,128]{1,0:T(8,128)(2,1)S(1)}, bf16[400,128]{1,0:T(8,128)(2,1)S(1)}, u32[]{:S(2)}, u32[]{:S(2)}) collective-permute-start(bf16[400,128]{1,0:T(8,128)(2,1)S(1)} %get-tuple-element.105.refs_0_.refs_4_), channel_id=1, source_target_pairs={{0,2},{2,0},{4,6},{6,4},{1,3},{3,1},{5,7},{7,5},{8,10},{10,8},{12,... | collective-permute-start | bytes 307208 | tf_op jit(solution)/shard_map/ppermute | solution.py:563
  39.5 7.3 %collective-permute-start.15 = (bf16[256,128]{1,0:T(8,128)(2,1)S(1)}, bf16[256,128]{1,0:T(8,128)(2,1)S(1)}, u32[]{:S(2)}, u32[]{:S(2)}) collective-permute-start(bf16[256,128]{1,0:T(8,128)(2,1)S(1)} %get-tuple-element.107.refs_0_), channel_id=1, source_target_pairs={{0,6},{2,4},{4,2},{6,0},{1,7},{3,5},{5,3},{7,1},{8,14},{10,12},{12... | collective-permute-start | bytes 196616 | tf_op jit(solution)/shard_map/ppermute | solution.py:563
  42.0 6.7 %collective-permute-start.14 = (bf16[256,128]{1,0:T(8,128)(2,1)S(1)}, bf16[256,128]{1,0:T(8,128)(2,1)S(1)}, u32[]{:S(2)}, u32[]{:S(2)}) collective-permute-start(bf16[256,128]{1,0:T(8,128)(2,1)S(1)} %get-tuple-element.107.refs_0_), channel_id=1, source_target_pairs={{0,4},{2,6},{4,0},{6,2},{1,5},{3,7},{5,1},{7,3},{8,12},{10,14},{12... | collective-permute-start | bytes 196616 | tf_op jit(solution)/shard_map/ppermute | solution.py:563
  42.0 6.7 %collective-permute-start.13 = (bf16[256,128]{1,0:T(8,128)(2,1)S(1)}, bf16[256,128]{1,0:T(8,128)(2,1)S(1)}, u32[]{:S(2)}, u32[]{:S(2)}) collective-permute-start(bf16[256,128]{1,0:T(8,128)(2,1)S(1)} %get-tuple-element.107.refs_0_), channel_id=1, source_target_pairs={{0,2},{2,0},{4,6},{6,4},{1,3},{3,1},{5,7},{7,5},{8,10},{10,8},{12,... | collective-permute-start | bytes 196616 | tf_op jit(solution)/shard_map/ppermute | solution.py:563
  44.3 9.3 %collective-permute-start.21 = (bf16[256,128]{1,0:T(8,128)(2,1)S(1)}, bf16[256,128]{1,0:T(8,128)(2,1)S(1)}, u32[]{:S(2)}, u32[]{:S(2)}) collective-permute-start(bf16[256,128]{1,0:T(8,128)(2,1)S(1)} %side.1.refs_4_), channel_id=1, source_target_pairs={{0,6},{2,4},{4,2},{6,0},{1,7},{3,5},{5,3},{7,1},{8,14},{10,12},{12... | collective-permute-start | bytes 196616 | tf_op jit(solution)/shard_map/ppermute | solution.py:563
  46.8 7.8 %collective-permute-start.20 = (bf16[256,128]{1,0:T(8,128)(2,1)S(1)}, bf16[256,128]{1,0:T(8,128)(2,1)S(1)}, u32[]{:S(2)}, u32[]{:S(2)}) collective-permute-start(bf16[256,128]{1,0:T(8,128)(2,1)S(1)} %side.1.refs_4_), channel_id=1, source_target_pairs={{0,4},{2,6},{4,0},{6,2},{1,5},{3,7},{5,1},{7,3},{8,12},{10,14},{12... | collective-permute-start | bytes 196616 | tf_op jit(solution)/shard_map/ppermute | solution.py:563
  46.8 7.8 %collective-permute-start.19 = (bf16[256,128]{1,0:T(8,128)(2,1)S(1)}, bf16[256,128]{1,0:T(8,128)(2,1)S(1)}, u32[]{:S(2)}, u32[]{:S(2)}) collective-permute-start(bf16[256,128]{1,0:T(8,128)(2,1)S(1)} %side.1.refs_4_), channel_id=1, source_target_pairs={{0,2},{2,0},{4,6},{6,4},{1,3},{3,1},{5,7},{7,5},{8,10},{10,8},{12,... | collective-permute-start | bytes 196616 | tf_op jit(solution)/shard_map/ppermute | solution.py:563
  50.1 6.4 %collective-permute-start.18 = (bf16[256,128]{1,0:T(8,128)(2,1)S(1)}, bf16[256,128]{1,0:T(8,128)(2,1)S(1)}, u32[]{:S(2)}, u32[]{:S(2)}) collective-permute-start(bf16[256,128]{1,0:T(8,128)(2,1)S(1)} %get-tuple-element.110.refs_0_), channel_id=1, source_target_pairs={{0,6},{2,4},{4,2},{6,0},{1,7},{3,5},{5,3},{7,1},{8,14},{10,12},{12... | collective-permute-start | bytes 196616 | tf_op jit(solution)/shard_map/ppermute | solution.py:563
  53.6 5.9 %collective-permute-start.17 = (bf16[256,128]{1,0:T(8,128)(2,1)S(1)}, bf16[256,128]{1,0:T(8,128)(2,1)S(1)}, u32[]{:S(2)}, u32[]{:S(2)}) collective-permute-start(bf16[256,128]{1,0:T(8,128)(2,1)S(1)} %get-tuple-element.110.refs_0_), channel_id=1, source_target_pairs={{0,4},{2,6},{4,0},{6,2},{1,5},{3,7},{5,1},{7,3},{8,12},{10,14},{12... | collective-permute-start | bytes 196616 | tf_op jit(solution)/shard_map/ppermute | solution.py:563
  53.6 5.9 %collective-permute-start.16 = (bf16[256,128]{1,0:T(8,128)(2,1)S(1)}, bf16[256,128]{1,0:T(8,128)(2,1)S(1)}, u32[]{:S(2)}, u32[]{:S(2)}) collective-permute-start(bf16[256,128]{1,0:T(8,128)(2,1)S(1)} %get-tuple-element.110.refs_0_), channel_id=1, source_target_pairs={{0,2},{2,0},{4,6},{6,4},{1,3},{3,1},{5,7},{7,5},{8,10},{10,8},{12,... | collective-permute-start | bytes 196616 | tf_op jit(solution)/shard_map/ppermute | solution.py:563
  61.5 6.8 %collective-permute-start.24 = (bf16[272,128]{1,0:T(8,128)(2,1)S(1)}, bf16[272,128]{1,0:T(8,128)(2,1)S(1)}, u32[]{:S(2)}, u32[]{:S(2)}) collective-permute-start(bf16[272,128]{1,0:T(8,128)(2,1)S(1)} %get-tuple-element.114.refs_0_), channel_id=1, source_target_pairs={{0,6},{2,4},{4,2},{6,0},{1,7},{3,5},{5,3},{7,1},{8,14},{10,12},{12... | collective-permute-start | bytes 208904 | tf_op jit(solution)/shard_map/ppermute | solution.py:563
  64.0 6.4 %collective-permute-start.23 = (bf16[272,128]{1,0:T(8,128)(2,1)S(1)}, bf16[272,128]{1,0:T(8,128)(2,1)S(1)}, u32[]{:S(2)}, u32[]{:S(2)}) collective-permute-start(bf16[272,128]{1,0:T(8,128)(2,1)S(1)} %get-tuple-element.114.refs_0_), channel_id=1, source_target_pairs={{0,4},{2,6},{4,0},{6,2},{1,5},{3,7},{5,1},{7,3},{8,12},{10,14},{12... | collective-permute-start | bytes 208904 | tf_op jit(solution)/shard_map/ppermute | solution.py:563
  64.0 6.4 %collective-permute-start.22 = (bf16[272,128]{1,0:T(8,128)(2,1)S(1)}, bf16[272,128]{1,0:T(8,128)(2,1)S(1)}, u32[]{:S(2)}, u32[]{:S(2)}) collective-permute-start(bf16[272,128]{1,0:T(8,128)(2,1)S(1)} %get-tuple-element.114.refs_0_), channel_id=1, source_target_pairs={{0,2},{2,0},{4,6},{6,4},{1,3},{3,1},{5,7},{7,5},{8,10},{10,8},{12,... | collective-permute-start | bytes 208904 | tf_op jit(solution)/shard_map/ppermute | solution.py:563
  71.7 5.8 %collective-permute-start.27 = (bf16[144,128]{1,0:T(8,128)(2,1)S(1)}, bf16[144,128]{1,0:T(8,128)(2,1)S(1)}, u32[]{:S(2)}, u32[]{:S(2)}) collective-permute-start(bf16[144,128]{1,0:T(8,128)(2,1)S(1)} %get-tuple-element.133.refs_0_), channel_id=1, source_target_pairs={{0,6},{2,4},{4,2},{6,0},{1,7},{3,5},{5,3},{7,1},{8,14},{10,12},{12... | collective-permute-start | bytes 110600 | tf_op jit(solution)/shard_map/ppermute | solution.py:563
  74.3 4.9 %collective-permute-start.26 = (bf16[144,128]{1,0:T(8,128)(2,1)S(1)}, bf16[144,128]{1,0:T(8,128)(2,1)S(1)}, u32[]{:S(2)}, u32[]{:S(2)}) collective-permute-start(bf16[144,128]{1,0:T(8,128)(2,1)S(1)} %get-tuple-element.133.refs_0_), channel_id=1, source_target_pairs={{0,4},{2,6},{4,0},{6,2},{1,5},{3,7},{5,1},{7,3},{8,12},{10,14},{12... | collective-permute-start | bytes 110600 | tf_op jit(solution)/shard_map/ppermute | solution.py:563
  74.3 4.9 %collective-permute-start.25 = (bf16[144,128]{1,0:T(8,128)(2,1)S(1)}, bf16[144,128]{1,0:T(8,128)(2,1)S(1)}, u32[]{:S(2)}, u32[]{:S(2)}) collective-permute-start(bf16[144,128]{1,0:T(8,128)(2,1)S(1)} %get-tuple-element.133.refs_0_), channel_id=1, source_target_pairs={{0,2},{2,0},{4,6},{6,4},{1,3},{3,1},{5,7},{7,5},{8,10},{10,8},{12,... | collective-permute-start | bytes 110600 | tf_op jit(solution)/shard_map/ppermute | solution.py:563
  80.4 5.9 %collective-permute-start.30 = (bf16[144,128]{1,0:T(8,128)(2,1)S(1)}, bf16[144,128]{1,0:T(8,128)(2,1)S(1)}, u32[]{:S(2)}, u32[]{:S(2)}) collective-permute-start(bf16[144,128]{1,0:T(8,128)(2,1)S(1)} %get-tuple-element.148.refs_0_), channel_id=1, source_target_pairs={{0,6},{2,4},{4,2},{6,0},{1,7},{3,5},{5,3},{7,1},{8,14},{10,12},{12... | collective-permute-start | bytes 110600 | tf_op jit(solution)/shard_map/ppermute | solution.py:563
  82.4 5.3 %collective-permute-start.29 = (bf16[144,128]{1,0:T(8,128)(2,1)S(1)}, bf16[144,128]{1,0:T(8,128)(2,1)S(1)}, u32[]{:S(2)}, u32[]{:S(2)}) collective-permute-start(bf16[144,128]{1,0:T(8,128)(2,1)S(1)} %get-tuple-element.148.refs_0_), channel_id=1, source_target_pairs={{0,4},{2,6},{4,0},{6,2},{1,5},{3,7},{5,1},{7,3},{8,12},{10,14},{12... | collective-permute-start | bytes 110600 | tf_op jit(solution)/shard_map/ppermute | solution.py:563
  82.9 4.7 %collective-permute-start.28 = (bf16[144,128]{1,0:T(8,128)(2,1)S(1)}, bf16[144,128]{1,0:T(8,128)(2,1)S(1)}, u32[]{:S(2)}, u32[]{:S(2)}) collective-permute-start(bf16[144,128]{1,0:T(8,128)(2,1)S(1)} %get-tuple-element.148.refs_0_), channel_id=1, source_target_pairs={{0,2},{2,0},{4,6},{6,4},{1,3},{3,1},{5,7},{7,5},{8,10},{10,8},{12,... | collective-permute-start | bytes 110600 | tf_op jit(solution)/shard_map/ppermute | solution.py:563
  84.8 4.7 %collective-permute-start.33 = (bf16[272,512]{1,0:T(8,128)(2,1)S(1)}, bf16[272,512]{1,0:T(8,128)(2,1)S(1)}, u32[]{:S(2)}, u32[]{:S(2)}) collective-permute-start(bf16[272,512]{1,0:T(8,128)(2,1)S(1)} %get-tuple-element.163), channel_id=1, source_target_pairs={{0,1},{1,0},{2,3},{3,2},{4,5},{5,4},{6,7},{7,6},{8,9},{9,8},{10,11... | collective-permute-start | bytes 835592 | tf_op jit(solution)/shard_map/ppermute | solution.py:569
  84.8 4.7 %collective-permute-start.34 = (bf16[272,512]{1,0:T(8,128)(2,1)S(1)}, bf16[272,512]{1,0:T(8,128)(2,1)S(1)}, u32[]{:S(2)}, u32[]{:S(2)}) collective-permute-start(bf16[272,512]{1,0:T(8,128)(2,1)S(1)} %get-tuple-element.164), channel_id=1, source_target_pairs={{0,1},{1,0},{2,3},{3,2},{4,5},{5,4},{6,7},{7,6},{8,9},{9,8},{10,11... | collective-permute-start | bytes 835592 | tf_op jit(solution)/shard_map/ppermute | solution.py:569
  91.6 9.6 %collective-permute-start.35 = (bf16[272,512]{1,0:T(8,128)(2,1)S(1)}, bf16[272,512]{1,0:T(8,128)(2,1)S(1)}, u32[]{:S(2)}, u32[]{:S(2)}) collective-permute-start(bf16[272,512]{1,0:T(8,128)(2,1)S(1)} %get-tuple-element.166), channel_id=1, source_target_pairs={{0,8},{8,0},{16,24},{24,16},{1,9},{9,1},{17,25},{25,17},{2,10},{10... | collective-permute-start | bytes 835592 | tf_op jit(solution)/shard_map/ppermute | solution.py:566
  93.1 14.4 %collective-permute-start.36 = (bf16[272,512]{1,0:T(8,128)(2,1)S(1)}, bf16[272,512]{1,0:T(8,128)(2,1)S(1)}, u32[]{:S(2)}, u32[]{:S(2)}) collective-permute-start(bf16[272,512]{1,0:T(8,128)(2,1)S(1)} %get-tuple-element.167), channel_id=1, source_target_pairs={{0,16},{8,24},{16,0},{24,8},{1,17},{9,25},{17,1},{25,9},{2,18},{10... | collective-permute-start | bytes 835592 | tf_op jit(solution)/shard_map/ppermute | solution.py:566
  94.6 12.9 %collective-permute-start.37 = (bf16[272,512]{1,0:T(8,128)(2,1)S(1)}, bf16[272,512]{1,0:T(8,128)(2,1)S(1)}, u32[]{:S(2)}, u32[]{:S(2)}) collective-permute-start(bf16[272,512]{1,0:T(8,128)(2,1)S(1)} %get-tuple-element.168), channel_id=1, source_target_pairs={{0,24},{8,16},{16,8},{24,0},{1,25},{9,17},{17,9},{25,1},{2,26},{10... | collective-permute-start | bytes 835592 | tf_op jit(solution)/shard_map/ppermute | solution.py:566
  (8 other events, 12.8 us)

commit v14 on v13

--- a/solution.py
+++ b/solution.py
@@ -483,42 +483,59 @@
     dred_out[...] = dred
 
 
-def split_grads(dred, mixed, second, gain_row, wide, keep, send):
-    rank = second.shape[0]
+def split_grads(dred, mixed, reduced, dout, wide, keep, send):
+    rank = reduced.shape[1]
     own = keep.shape[1]
     core = lax.axis_index("core")
+    second = dot_tn(reduced, dout)
     for head in range(mixed.shape[1] // HD):
         part = slice(head * HD, (head + 1) * HD)
         wide[0:HD, head * rank : (head + 1) * rank] = dot_tn(mixed[:, part], dred).astype(BF)
-    wide[rank : 2 * rank, :] = second.astype(BF)
-    if gain_row is not None:
-        wide[2 * rank :, :] = gain_row[...]
+    wide[rank:, :] = second.astype(BF)
     keep[...] = wide[:, pl.ds(pl.multiple_of(core * own, own), own)]
     send[...] = wide[:, pl.ds(pl.multiple_of((1 - core) * own, own), own)]
 
 
 def grads_kernel(count, *refs):
     sources, refs = refs[:count], refs[count:]
-    dout, dred, mixed, gain_row, keep, send, wide = refs
+    dout, dred, mixed, keep, send, wide = refs
     rows = dout.shape[0]
     height = sources[0].shape[0]
     reduced = total_of(sources, height - rows, height).astype(BF)
-    second = dot_tn(reduced, dout[...])
-    split_grads(dred[...], mixed, second, gain_row, wide, keep, send)
-
-
-def back_first_kernel(count, width, *refs):
+    split_grads(dred[...], mixed, reduced, dout[...], wide, keep, send)
+
+
+def grads_first_kernel(count, width, *refs):
     pays, refs = refs[:count], refs[count:]
-    carried_after, x_after, mean_after, cross_after, x, mean, weights, probs, mixed = refs[:9]
-    reduced, keep, send, wide = refs[9:]
-    rank = reduced.shape[1]
+    carried_after, x_after, mean_after, cross_after, mixed, reduced = refs[:6]
+    keep, send, dout_out, dred_out, wide = refs[6:]
     dout, dred = receive_backward(pays, carried_after, x_after, mean_after, cross_after, width)
-    second = dot_tn(reduced[...], dout)
+    split_grads(dred, mixed, reduced[...], dout, wide, keep, send)
+    dout_out[...] = dout
+    dred_out[...] = dred
+
+
+def back_first_kernel(dout, dred, x, mean, weights, probs, gain_row):
     layer_backward(
-        dout, dred, x, mean[:, 0:1], layer_of(weights, 0), None, probs, wide.at[pl.ds(2 * rank, 16)],
-        None, None,
-    )
-    split_grads(dred, mixed, second, None, wide, keep, send)
+        dout[...], dred[...], x, mean[:, 0:1], layer_of(weights, 0), None, probs, gain_row, None, None
+    )
+
+
+def split_gains_kernel(sections, *refs):
+    rows, keep, send = refs[:sections], refs[sections], refs[sections + 1]
+    own = keep.shape[1]
+    core = lax.axis_index("core")
+    for layer, row in enumerate(rows):
+        span = slice(layer * 16, (layer + 1) * 16)
+        keep[span, :] = row[:, pl.ds(pl.multiple_of(core * own, own), own)]
+        send[span, :] = row[:, pl.ds(pl.multiple_of((1 - core) * own, own), own)]
+
+
+def combine_gains_kernel(keep, swapped, *outs):
+    section = lax.axis_index("pipe")
+    for distance, out in enumerate(outs):
+        span = pl.ds(pl.multiple_of((section ^ distance) * 16, 16), 16)
+        out[...] = (keep[span, :].astype(F32) + swapped[span, :].astype(F32)).astype(BF)
 
 
 def combine_kernel(sections, *refs):
@@ -532,8 +549,8 @@
 
 
 def finish_kernel(sections, *refs):
-    parts = refs[:sections]
-    gain, first, second = refs[sections:]
+    parts, gain_parts = refs[:sections], refs[sections : 2 * sections]
+    gain, first, second = refs[2 * sections :]
     rank = second.shape[1]
     total = parts[0][...].astype(F32)
     for part in parts[1:]:
@@ -541,7 +558,7 @@
     for block in range(first.shape[1] // HD):
         first[0, block * HD : (block + 1) * HD, :] = total[0:HD, block * rank : (block + 1) * rank]
     second[0] = total[rank : 2 * rank]
-    gain[...] = total[2 * rank : 2 * rank + 1]
+    gain[...] = total_of(gain_parts, 0, 16)[0:1]
 
 
 def per_device(tokens, cotangents, starts, counts, layer_gains, first_map, second_map):
@@ -606,8 +623,8 @@
     rank_shape = shaped((rows, rank))
     cross_shape = shaped((rows, rank), F32)
     probs_shape = shaped((blocks, heads, size, size))
-    grads_shape = (sides, 2 * rank + 16, own)
-    half_shape = shaped(grads_shape[1:])
+    half_shape = shaped((2 * rank, own))
+    gain_half = shaped((sections * 16, own))
     weights_shape = shaped((sections, sides, slice_rows(own), HD))
 
     x, cot, mask, mean = call(
@@ -661,7 +678,7 @@
 
     back_rows = rows + 16 * blocks
     gain_shape = shaped((16, local))
-    wide_scratch = [pltpu.VMEM((2 * rank + 16, local), BF)]
+    wide_scratch = [pltpu.VMEM((2 * rank, local), BF)]
     x, mean, reduced, cross, mixed, dred, gain_row, carried, pay = call(
         functools.partial(turn_kernel, groups, top, float(width)),
         (*pays, *arrived, xs[-1], means[-1], mask, weights, cot),
@@ -686,8 +703,8 @@
     crosses.append(cross)
     all_mixed.append(mixed)
 
-    def gradients(layer, sources, dout, dred, gain_row):
-        operands = (*sources, dout, dred, all_mixed[layer], gain_row)
+    def gradients(layer, sources, dout, dred):
+        operands = (*sources, dout, dred, all_mixed[layer])
         keep, send = call(
             functools.partial(grads_kernel, len(sources)),
             operands,
@@ -700,7 +717,8 @@
 
     pays = exchange(pay)
     halves = [None] * sections
-    waiting = [(top, pays, cot, dred, gain_row)]
+    waiting = [(top, pays, cot, dred)]
+    gain_rows = [gain_row]
     for layer in range(top - 1, 0, -1):
         operands = (
             *pays, carried, xs[layer + 1], means[layer + 1], crosses[layer + 1],
@@ -714,25 +732,44 @@
             "backward",
         )
         pays = exchange(pay)
-        waiting.append((layer, [reduceds[layer]], dout, dred, gain_row))
+        waiting.append((layer, [reduceds[layer]], dout, dred))
+        gain_rows.insert(0, gain_row)
         done = [gradients(*item) for item in waiting]
         pays, done = lax.optimization_barrier((pays, done))
         for item, (keep, send) in zip(waiting, done):
             halves[item[0]] = (keep, swapped(send))
         waiting = []
-    operands = (
-        *pays, carried, xs[1], means[1], crosses[1], xs[0], means[0], weights, all_probs[0],
-        all_mixed[0], reduceds[0],
-    )
-    keep, send = call(
-        functools.partial(back_first_kernel, groups, float(width)),
+    operands = (*pays, carried, xs[1], means[1], crosses[1], all_mixed[0], reduceds[0])
+    keep, send, dout, dred = call(
+        functools.partial(grads_first_kernel, groups, float(width)),
         operands,
         vmem_specs(len(operands)),
-        [half_shape] * 2,
+        [half_shape, half_shape, wide_shape, rank_shape],
+        "weight_grads_first",
+        scratch_shapes=wide_scratch,
+    )
+    halves[0] = (keep, swapped(send))
+    gain_row = call(
+        back_first_kernel,
+        (dout, dred, xs[0], means[0], weights, all_probs[0]),
+        vmem_specs(6),
+        [gain_shape],
         "backward_first",
-        scratch_shapes=wide_scratch,
-    )
-    halves[0] = (keep, swapped(send))
+    )[0]
+    gain_keep, gain_send = call(
+        functools.partial(split_gains_kernel, sections),
+        (gain_row, *gain_rows),
+        vmem_specs(sections),
+        [gain_half] * 2,
+        "split_gains",
+    )
+    gain_parts = call(
+        combine_gains_kernel,
+        (gain_keep, swapped(gain_send)),
+        vmem_specs(2),
+        [shaped((16, own))] * sections,
+        "combine_gains",
+    )
 
     parts = call(
         functools.partial(combine_kernel, sections),
@@ -740,13 +777,15 @@
         vmem_specs(2 * sections),
         [half_shape] * sections,
         "combine",
-        scratch_shapes=[pltpu.VMEM((sections,) + grads_shape[1:], BF)],
+        scratch_shapes=[pltpu.VMEM((sections,) + half_shape.shape, BF)],
     )
     arrived = [parts[0]] + [across(parts[distance], distance) for distance in range(1, sections)]
+    arrived += [gain_parts[0]]
+    arrived += [across(gain_parts[distance], distance) for distance in range(1, sections)]
     gain_grad, first_grad, second_grad = call(
         functools.partial(finish_kernel, sections),
         arrived,
-        vmem_specs(sections),
+        vmem_specs(2 * sections),
         [
             shaped((1, own), F32),
             shaped((1, own, rank), F32),

time: 109 us -> 111 us (1.018)
  starting transfers between devices: 47.6 us -> 53.2 us
  waiting for transfers between devices: 42.6 us -> 39.1 us
    ppermute x6 -> x9, starting transfers between devices: 8.1 us -> 13.6 us  [across(): lax.ppermute(value, 'pipe', [(i, i ^ distance) for i in range(sections)])]
    ppermute x6 -> x9, waiting for transfers between devices: 14.2 us -> 9.55 us  [across(): lax.ppermute(value, 'pipe', [(i, i ^ distance) for i in range(sections)])]
    ppermute x8 -> x9, waiting for transfers between devices: 2.86 us -> 4.05 us  [swapped(): return lax.ppermute(value, 'core', [(i, 1 - i) for i in range(sides)])]
    pallas_call x15 -> x18, Pallas kernels: 13.2 us -> 13.4 us  [call(): pl.pallas_call(kernel, in_specs=specs, out_specs=vmem_specs(len(outs)), o...]
    ppermute x8 -> x9, starting transfers between devices: 2.16 us -> 2.23 us  [swapped(): return lax.ppermute(value, 'core', [(i, 1 - i) for i in range(sides)])]
  transfers between devices with their start and end apart: 38 -> 42, of which waited for: 21 -> 22; matrix products, arithmetic and copies ran while one was open for 0% -> 0% of each run, Pallas kernels for 4% -> 4%
where the time goes in v14:
time: 111 us
  starting transfers between devices  53.2 us (48%)
  waiting for transfers between devices  39.1 us (35%)
  Pallas kernels  15.7 us (14%)
  local copies, waits for them, and re-layouts  1.86 us (2%)
    ppermute x24, starting transfers between devices, shifted(): return lax.ppermute(value, 'z', [(i, i ^ shift) for i in range(groups)])  37.4 us
    ppermute x24, waiting for transfers between devices, shifted(): return lax.ppermute(value, 'z', [(i, i ^ shift) for i in range(groups)])  25.5 us
    ppermute x9, starting transfers between devices, across(): lax.ppermute(value, 'pipe', [(i, i ^ distance) for i in range(sections)])  13.6 us
    pallas_call x18, Pallas kernels, call(): pl.pallas_call(kernel, in_specs=specs, out_specs=vmem_specs(len(outs)), o...  13.4 us
    ppermute x9, waiting for transfers between devices, across(): lax.ppermute(value, 'pipe', [(i, i ^ distance) for i in range(sections)])  9.55 us
    ppermute x9, waiting for transfers between devices, swapped(): return lax.ppermute(value, 'core', [(i, 1 - i) for i in range(sides)])  4.05 us
    pallas_call x1, Pallas kernels, pack(): pl.pallas_call(functools.partial(pack_kernel, groups, micro_local), in_sp...  2.28 us
    ppermute x9, starting transfers between devices, swapped(): return lax.ppermute(value, 'core', [(i, 1 - i) for i in range(sides)])  2.23 us
  transfers between devices with their start and end apart: 42, of which 22 were waited for; matrix products, arithmetic and copies ran while one was open for 0% of the time, Pallas kernels for 4%

profile of v14, /device:TPU:0, one launch (start us, length us, event | category | flops | bytes accessed | tf_op | source)
XLA Modules:
  0.0 110.7 jit_solution(11531354779661787462)
XLA Ops:
  0.6 2.3 %pack.1 = (bf16[32,2176]{1,0:T(8,128)(2,1)}, bf16[32,2176]{1,0:T(8,128)(2,1)}, bf16[32,2176]{1,0:T(8,128)(2,1)}, bf16[32,2176]{1,0:T(8,128)(2,1)}, bf16[1040,128]{1,0:T(8,128)(2,1)}) custom-call(bf16[2,2,32,4096]{3,2,1,0:T(8,128)(2,1)} %refs_0_.1, bf16[2,2,32,4096]{3,2,1,0:T(8,128)(2,1)} %refs_1_.1, s32[2,2,4]{2,1,0:T(2,128)} %refs_2_.1, s32[2,2]{1,0:T(2,128)} %refs_3_.1, ...), custom_call_target="tpu_custom_call" | custom-call | tf_op jit(solution)/shard_map/pack/pallas_call | solution.py:124
  2.9 3.0 %collective-permute-start = (bf16[1040,128]{1,0:T(8,128)(2,1)}, bf16[1040,128]{1,0:T(8,128)(2,1)S(1)}, u32[]{:S(2)}, u32[]{:S(2)}) collective-permute-start(bf16[1040,128]{1,0:T(8,128)(2,1)} %get-tuple-element.95.packed), channel_id=1, source_target_pairs={{0,8},{8,0},{16,24},{24,16},{1,9},{9,1},{17,25},{25,17},{2,10},{10... | collective-permute-start | bytes 798728 | tf_op jit(solution)/shard_map/ppermute | solution.py:583
  7.5 4.1 %collective-permute-start.1 = (bf16[32,2176]{1,0:T(8,128)(2,1)}, bf16[32,2176]{1,0:T(8,128)(2,1)S(1)}, u32[]{:S(2)}, u32[]{:S(2)}) collective-permute-start(bf16[32,2176]{1,0:T(8,128)(2,1)} %get-tuple-element.97), channel_id=1, source_target_pairs={{0,6},{2,4},{4,2},{6,0},{1,7},{3,5},{5,3},{7,1},{8,14},{10,12},{12... | collective-permute-start | bytes 417800 | tf_op jit(solution)/shard_map/ppermute | solution.py:580
  11.5 1.8 %collective-permute-done.early = bf16[1040,128]{1,0:T(8,128)(2,1)S(1)} collective-permute-done((bf16[1040,128]{1,0:T(8,128)(2,1)}, bf16[1040,128]{1,0:T(8,128)(2,1)S(1)}, u32[]{:S(2)}, u32[]{:S(2)}) %collective-permute-start) | collective-permute-done | bytes 266272 | tf_op jit(solution)/shard_map/ppermute | solution.py:583
  13.4 2.1 %collective-permute-start.3 = (bf16[32,2176]{1,0:T(8,128)(2,1)}, bf16[32,2176]{1,0:T(8,128)(2,1)S(1)}, u32[]{:S(2)}, u32[]{:S(2)}) collective-permute-start(bf16[32,2176]{1,0:T(8,128)(2,1)} %get-tuple-element.99), channel_id=1, source_target_pairs={{0,2},{2,0},{4,6},{6,4},{1,3},{3,1},{5,7},{7,5},{8,10},{10,8},{12,... | collective-permute-start | bytes 417800 | tf_op jit(solution)/shard_map/ppermute | solution.py:580
  17.4 5.3 %collective-permute-done.2.refs_2_ = bf16[32,2176]{1,0:T(8,128)(2,1)S(1)} collective-permute-done((bf16[32,2176]{1,0:T(8,128)(2,1)}, bf16[32,2176]{1,0:T(8,128)(2,1)S(1)}, u32[]{:S(2)}, u32[]{:S(2)}) %collective-permute-start.2) | collective-permute-done | bytes 139296 | tf_op jit(solution)/shard_map/ppermute | solution.py:580
  27.0 2.5 %collective-permute-start.12 = (bf16[400,128]{1,0:T(8,128)(2,1)S(1)}, bf16[400,128]{1,0:T(8,128)(2,1)S(1)}, u32[]{:S(2)}, u32[]{:S(2)}) collective-permute-start(bf16[400,128]{1,0:T(8,128)(2,1)S(1)} %get-tuple-element.113.refs_0_.refs_4_), channel_id=1, source_target_pairs={{0,6},{2,4},{4,2},{6,0},{1,7},{3,5},{5,3},{7,1},{8,14},{10,12},{12... | collective-permute-start | bytes 307208 | tf_op jit(solution)/shard_map/ppermute | solution.py:580
  29.5 1.9 %collective-permute-start.10 = (bf16[400,128]{1,0:T(8,128)(2,1)S(1)}, bf16[400,128]{1,0:T(8,128)(2,1)S(1)}, u32[]{:S(2)}, u32[]{:S(2)}) collective-permute-start(bf16[400,128]{1,0:T(8,128)(2,1)S(1)} %get-tuple-element.113.refs_0_.refs_4_), channel_id=1, source_target_pairs={{0,2},{2,0},{4,6},{6,4},{1,3},{3,1},{5,7},{7,5},{8,10},{10,8},{12,... | collective-permute-start | bytes 307208 | tf_op jit(solution)/shard_map/ppermute | solution.py:580
  31.5 3.2 %collective-permute-done.12.refs_3_.refs_7_ = bf16[400,128]{1,0:T(8,128)(2,1)S(1)} collective-permute-done((bf16[400,128]{1,0:T(8,128)(2,1)S(1)}, bf16[400,128]{1,0:T(8,128)(2,1)S(1)}, u32[]{:S(2)}, u32[]{:S(2)}) %collective-permute-start.12) | collective-permute-done | bytes 102432 | tf_op jit(solution)/shard_map/ppermute | solution.py:580
  34.7 3.5 %collective-permute-done.11.refs_2_.refs_6_ = bf16[400,128]{1,0:T(8,128)(2,1)S(1)} collective-permute-done((bf16[400,128]{1,0:T(8,128)(2,1)S(1)}, bf16[400,128]{1,0:T(8,128)(2,1)S(1)}, u32[]{:S(2)}, u32[]{:S(2)}) %collective-permute-start.11) | collective-permute-done | bytes 102432 | tf_op jit(solution)/shard_map/ppermute | solution.py:580
  39.5 2.5 %collective-permute-start.15 = (bf16[256,128]{1,0:T(8,128)(2,1)S(1)}, bf16[256,128]{1,0:T(8,128)(2,1)S(1)}, u32[]{:S(2)}, u32[]{:S(2)}) collective-permute-start(bf16[256,128]{1,0:T(8,128)(2,1)S(1)} %get-tuple-element.115.refs_0_), channel_id=1, source_target_pairs={{0,6},{2,4},{4,2},{6,0},{1,7},{3,5},{5,3},{7,1},{8,14},{10,12},{12... | collective-permute-start | bytes 196616 | tf_op jit(solution)/shard_map/ppermute | solution.py:580
  42.0 1.9 %collective-permute-start.13 = (bf16[256,128]{1,0:T(8,128)(2,1)S(1)}, bf16[256,128]{1,0:T(8,128)(2,1)S(1)}, u32[]{:S(2)}, u32[]{:S(2)}) collective-permute-start(bf16[256,128]{1,0:T(8,128)(2,1)S(1)} %get-tuple-element.115.refs_0_), channel_id=1, source_target_pairs={{0,2},{2,0},{4,6},{6,4},{1,3},{3,1},{5,7},{7,5},{8,10},{10,8},{12,... | collective-permute-start | bytes 196616 | tf_op jit(solution)/shard_map/ppermute | solution.py:580
  44.3 2.5 %collective-permute-start.21 = (bf16[256,128]{1,0:T(8,128)(2,1)S(1)}, bf16[256,128]{1,0:T(8,128)(2,1)S(1)}, u32[]{:S(2)}, u32[]{:S(2)}) collective-permute-start(bf16[256,128]{1,0:T(8,128)(2,1)S(1)} %side.1.refs_4_), channel_id=1, source_target_pairs={{0,6},{2,4},{4,2},{6,0},{1,7},{3,5},{5,3},{7,1},{8,14},{10,12},{12... | collective-permute-start | bytes 196616 | tf_op jit(solution)/shard_map/ppermute | solution.py:580
  46.8 1.9 %collective-permute-start.19 = (bf16[256,128]{1,0:T(8,128)(2,1)S(1)}, bf16[256,128]{1,0:T(8,128)(2,1)S(1)}, u32[]{:S(2)}, u32[]{:S(2)}) collective-permute-start(bf16[256,128]{1,0:T(8,128)(2,1)S(1)} %side.1.refs_4_), channel_id=1, source_target_pairs={{0,2},{2,0},{4,6},{6,4},{1,3},{3,1},{5,7},{7,5},{8,10},{10,8},{12,... | collective-permute-start | bytes 196616 | tf_op jit(solution)/shard_map/ppermute | solution.py:580
  50.1 3.5 %collective-permute-start.18 = (bf16[256,128]{1,0:T(8,128)(2,1)S(1)}, bf16[256,128]{1,0:T(8,128)(2,1)S(1)}, u32[]{:S(2)}, u32[]{:S(2)}) collective-permute-start(bf16[256,128]{1,0:T(8,128)(2,1)S(1)} %get-tuple-element.118.refs_0_), channel_id=1, source_target_pairs={{0,6},{2,4},{4,2},{6,0},{1,7},{3,5},{5,3},{7,1},{8,14},{10,12},{12... | collective-permute-start | bytes 196616 | tf_op jit(solution)/shard_map/ppermute | solution.py:580
  54.6 2.0 %collective-permute-done.18.refs_3_ = bf16[256,128]{1,0:T(8,128)(2,1)S(1)} collective-permute-done((bf16[256,128]{1,0:T(8,128)(2,1)S(1)}, bf16[256,128]{1,0:T(8,128)(2,1)S(1)}, u32[]{:S(2)}, u32[]{:S(2)}) %collective-permute-start.18) | collective-permute-done | bytes 65568 | tf_op jit(solution)/shard_map/ppermute | solution.py:580
  56.5 2.9 %collective-permute-done.17.refs_2_ = bf16[256,128]{1,0:T(8,128)(2,1)S(1)} collective-permute-done((bf16[256,128]{1,0:T(8,128)(2,1)S(1)}, bf16[256,128]{1,0:T(8,128)(2,1)S(1)}, u32[]{:S(2)}, u32[]{:S(2)}) %collective-permute-start.17) | collective-permute-done | bytes 65568 | tf_op jit(solution)/shard_map/ppermute | solution.py:580
  59.4 2.1 %turn.1 = (bf16[128,1024]{1,0:T(8,128)(2,1)S(1)}, f32[128,128]{1,0:T(8,128)S(1)}, bf16[128,128]{1,0:T(8,128)(2,1)S(1)}, f32[128,128]{1,0:T(8,128)S(1)}, bf16[128...) custom-call(bf16[256,128]{1,0:T(8,128)(2,1)S(1)} %get-tuple-element., ...), custom_call_target="tpu_custom_call" | custom-call | tf_op jit(solution)/shard_map/turn/pallas_call | solution.py:601
  61.5 2.5 %collective-permute-start.24 = (bf16[272,128]{1,0:T(8,128)(2,1)S(1)}, bf16[272,128]{1,0:T(8,128)(2,1)S(1)}, u32[]{:S(2)}, u32[]{:S(2)}) collective-permute-start(bf16[272,128]{1,0:T(8,128)(2,1)S(1)} %get-tuple-element.122.refs_0_), channel_id=1, source_target_pairs={{0,6},{2,4},{4,2},{6,0},{1,7},{3,5},{5,3},{7,1},{8,14},{10,12},{12... | collective-permute-start | bytes 208904 | tf_op jit(solution)/shard_map/ppermute | solution.py:580
  64.1 1.9 %collective-permute-start.22 = (bf16[272,128]{1,0:T(8,128)(2,1)S(1)}, bf16[272,128]{1,0:T(8,128)(2,1)S(1)}, u32[]{:S(2)}, u32[]{:S(2)}) collective-permute-start(bf16[272,128]{1,0:T(8,128)(2,1)S(1)} %get-tuple-element.122.refs_0_), channel_id=1, source_target_pairs={{0,2},{2,0},{4,6},{6,4},{1,3},{3,1},{5,7},{7,5},{8,10},{10,8},{12,... | collective-permute-start | bytes 208904 | tf_op jit(solution)/shard_map/ppermute | solution.py:580
  66.0 2.4 %collective-permute-done.24.refs_3_ = bf16[272,128]{1,0:T(8,128)(2,1)S(1)} collective-permute-done((bf16[272,128]{1,0:T(8,128)(2,1)S(1)}, bf16[272,128]{1,0:T(8,128)(2,1)S(1)}, u32[]{:S(2)}, u32[]{:S(2)}) %collective-permute-start.24) | collective-permute-done | bytes 69664 | tf_op jit(solution)/shard_map/ppermute | solution.py:580
  68.4 2.1 %collective-permute-done.23.refs_2_ = bf16[272,128]{1,0:T(8,128)(2,1)S(1)} collective-permute-done((bf16[272,128]{1,0:T(8,128)(2,1)S(1)}, bf16[272,128]{1,0:T(8,128)(2,1)S(1)}, u32[]{:S(2)}, u32[]{:S(2)}) %collective-permute-start.23) | collective-permute-done | bytes 69664 | tf_op jit(solution)/shard_map/ppermute | solution.py:580
  71.8 2.5 %collective-permute-start.27 = (bf16[144,128]{1,0:T(8,128)(2,1)S(1)}, bf16[144,128]{1,0:T(8,128)(2,1)S(1)}, u32[]{:S(2)}, u32[]{:S(2)}) collective-permute-start(bf16[144,128]{1,0:T(8,128)(2,1)S(1)} %get-tuple-element.139.refs_0_), channel_id=1, source_target_pairs={{0,6},{2,4},{4,2},{6,0},{1,7},{3,5},{5,3},{7,1},{8,14},{10,12},{12... | collective-permute-start | bytes 110600 | tf_op jit(solution)/shard_map/ppermute | solution.py:580
  74.3 1.9 %collective-permute-start.25 = (bf16[144,128]{1,0:T(8,128)(2,1)S(1)}, bf16[144,128]{1,0:T(8,128)(2,1)S(1)}, u32[]{:S(2)}, u32[]{:S(2)}) collective-permute-start(bf16[144,128]{1,0:T(8,128)(2,1)S(1)} %get-tuple-element.139.refs_0_), channel_id=1, source_target_pairs={{0,2},{2,0},{4,6},{6,4},{1,3},{3,1},{5,7},{7,5},{8,10},{10,8},{12,... | collective-permute-start | bytes 110600 | tf_op jit(solution)/shard_map/ppermute | solution.py:580
  77.6 1.6 %collective-permute-done.26.refs_2_ = bf16[144,128]{1,0:T(8,128)(2,1)S(1)} collective-permute-done((bf16[144,128]{1,0:T(8,128)(2,1)S(1)}, bf16[144,128]{1,0:T(8,128)(2,1)S(1)}, u32[]{:S(2)}, u32[]{:S(2)}) %collective-permute-start.26) | collective-permute-done | bytes 36896 | tf_op jit(solution)/shard_map/ppermute | solution.py:580
  80.4 2.0 %collective-permute-start.30 = (bf16[144,128]{1,0:T(8,128)(2,1)S(1)}, bf16[144,128]{1,0:T(8,128)(2,1)S(1)}, u32[]{:S(2)}, u32[]{:S(2)}) collective-permute-start(bf16[144,128]{1,0:T(8,128)(2,1)S(1)} %get-tuple-element.153.refs_0_), channel_id=1, source_target_pairs={{0,6},{2,4},{4,2},{6,0},{1,7},{3,5},{5,3},{7,1},{8,14},{10,12},{12... | collective-permute-start | bytes 110600 | tf_op jit(solution)/shard_map/ppermute | solution.py:580
  83.0 1.9 %collective-permute-start.28 = (bf16[144,128]{1,0:T(8,128)(2,1)S(1)}, bf16[144,128]{1,0:T(8,128)(2,1)S(1)}, u32[]{:S(2)}, u32[]{:S(2)}) collective-permute-start(bf16[144,128]{1,0:T(8,128)(2,1)S(1)} %get-tuple-element.153.refs_0_), channel_id=1, source_target_pairs={{0,2},{2,0},{4,6},{6,4},{1,3},{3,1},{5,7},{7,5},{8,10},{10,8},{12,... | collective-permute-start | bytes 110600 | tf_op jit(solution)/shard_map/ppermute | solution.py:580
  90.8 1.6 %collective-permute-start.35 = (bf16[256,512]{1,0:T(8,128)(2,1)S(1)}, bf16[256,512]{1,0:T(8,128)(2,1)S(1)}, u32[]{:S(2)}, u32[]{:S(2)}) collective-permute-start(bf16[256,512]{1,0:T(8,128)(2,1)S(1)} %get-tuple-element.170), channel_id=1, source_target_pairs={{0,8},{8,0},{16,24},{24,16},{1,9},{9,1},{17,25},{25,17},{2,10},{10... | collective-permute-start | bytes 786440 | tf_op jit(solution)/shard_map/ppermute | solution.py:583
  96.6 1.6 %collective-permute-start.39 = (bf16[16,512]{1,0:T(8,128)(2,1)S(1)}, bf16[16,512]{1,0:T(8,128)(2,1)S(1)}, u32[]{:S(2)}, u32[]{:S(2)}) collective-permute-start(bf16[16,512]{1,0:T(8,128)(2,1)S(1)} %get-tuple-element.182), channel_id=1, source_target_pairs={{0,8},{8,0},{16,24},{24,16},{1,9},{9,1},{17,25},{25,17},{2,10},{10... | collective-permute-start | bytes 49160 | tf_op jit(solution)/shard_map/ppermute | solution.py:583
  99.7 5.5 %collective-permute-done.39.refs_5_ = bf16[16,512]{1,0:T(8,128)(2,1)S(1)} collective-permute-done((bf16[16,512]{1,0:T(8,128)(2,1)S(1)}, bf16[16,512]{1,0:T(8,128)(2,1)S(1)}, u32[]{:S(2)}, u32[]{:S(2)}) %collective-permute-start.39) | collective-permute-done | bytes 16416 | tf_op jit(solution)/shard_map/ppermute | solution.py:583
  105.2 2.4 %collective-permute-start.41 = (bf16[16,512]{1,0:T(8,128)(2,1)S(1)}, bf16[16,512]{1,0:T(8,128)(2,1)S(1)}, u32[]{:S(2)}, u32[]{:S(2)}) collective-permute-start(bf16[16,512]{1,0:T(8,128)(2,1)S(1)} %get-tuple-element.184), channel_id=1, source_target_pairs={{0,24},{8,16},{16,8},{24,0},{1,25},{9,17},{17,9},{25,1},{2,26},{10... | collective-permute-start | bytes 49160 | tf_op jit(solution)/shard_map/ppermute | solution.py:583
  107.6 2.2 %collective-permute-done.41.refs_7_ = bf16[16,512]{1,0:T(8,128)(2,1)S(1)} collective-permute-done((bf16[16,512]{1,0:T(8,128)(2,1)S(1)}, bf16[16,512]{1,0:T(8,128)(2,1)S(1)}, u32[]{:S(2)}, u32[]{:S(2)}) %collective-permute-start.41) | collective-permute-done | bytes 16416 | tf_op jit(solution)/shard_map/ppermute | solution.py:583
  (75 shorter events, 28.7 us)
Async XLA Ops:
  2.9 10.4 %collective-permute-start = (bf16[1040,128]{1,0:T(8,128)(2,1)}, bf16[1040,128]{1,0:T(8,128)(2,1)S(1)}, u32[]{:S(2)}, u32[]{:S(2)}) collective-permute-start(bf16[1040,128]{1,0:T(8,128)(2,1)} %get-tuple-element.95.packed), channel_id=1, source_target_pairs={{0,8},{8,0},{16,24},{24,16},{1,9},{9,1},{17,25},{25,17},{2,10},{10... | collective-permute-start | bytes 798728 | tf_op jit(solution)/shard_map/ppermute | solution.py:583
  5.9 16.8 %collective-permute-start.5 = (bf16[1040,128]{1,0:T(8,128)(2,1)}, bf16[1040,128]{1,0:T(8,128)(2,1)S(1)}, u32[]{:S(2)}, u32[]{:S(2)}) collective-permute-start(bf16[1040,128]{1,0:T(8,128)(2,1)} %get-tuple-element.95.packed), channel_id=1, source_target_pairs={{0,24},{8,16},{16,8},{24,0},{1,25},{9,17},{17,9},{25,1},{2,26},{10... | collective-permute-start | bytes 798728 | tf_op jit(solution)/shard_map/ppermute | solution.py:583
  7.4 15.3 %collective-permute-start.4 = (bf16[1040,128]{1,0:T(8,128)(2,1)}, bf16[1040,128]{1,0:T(8,128)(2,1)S(1)}, u32[]{:S(2)}, u32[]{:S(2)}) collective-permute-start(bf16[1040,128]{1,0:T(8,128)(2,1)} %get-tuple-element.95.packed), channel_id=1, source_target_pairs={{0,16},{8,24},{16,0},{24,8},{1,17},{9,25},{17,1},{25,9},{2,18},{10... | collective-permute-start | bytes 798728 | tf_op jit(solution)/shard_map/ppermute | solution.py:583
  7.5 9.9 %collective-permute-start.1 = (bf16[32,2176]{1,0:T(8,128)(2,1)}, bf16[32,2176]{1,0:T(8,128)(2,1)S(1)}, u32[]{:S(2)}, u32[]{:S(2)}) collective-permute-start(bf16[32,2176]{1,0:T(8,128)(2,1)} %get-tuple-element.97), channel_id=1, source_target_pairs={{0,6},{2,4},{4,2},{6,0},{1,7},{3,5},{5,3},{7,1},{8,14},{10,12},{12... | collective-permute-start | bytes 417800 | tf_op jit(solution)/shard_map/ppermute | solution.py:580
  11.5 11.1 %collective-permute-start.2 = (bf16[32,2176]{1,0:T(8,128)(2,1)}, bf16[32,2176]{1,0:T(8,128)(2,1)S(1)}, u32[]{:S(2)}, u32[]{:S(2)}) collective-permute-start(bf16[32,2176]{1,0:T(8,128)(2,1)} %get-tuple-element.98), channel_id=1, source_target_pairs={{0,4},{2,6},{4,0},{6,2},{1,5},{3,7},{5,1},{7,3},{8,12},{10,14},{12... | collective-permute-start | bytes 417800 | tf_op jit(solution)/shard_map/ppermute | solution.py:580
  13.4 9.3 %collective-permute-start.3 = (bf16[32,2176]{1,0:T(8,128)(2,1)}, bf16[32,2176]{1,0:T(8,128)(2,1)S(1)}, u32[]{:S(2)}, u32[]{:S(2)}) collective-permute-start(bf16[32,2176]{1,0:T(8,128)(2,1)} %get-tuple-element.99), channel_id=1, source_target_pairs={{0,2},{2,0},{4,6},{6,4},{1,3},{3,1},{5,7},{7,5},{8,10},{10,8},{12,... | collective-permute-start | bytes 417800 | tf_op jit(solution)/shard_map/ppermute | solution.py:580
  27.0 7.7 %collective-permute-start.12 = (bf16[400,128]{1,0:T(8,128)(2,1)S(1)}, bf16[400,128]{1,0:T(8,128)(2,1)S(1)}, u32[]{:S(2)}, u32[]{:S(2)}) collective-permute-start(bf16[400,128]{1,0:T(8,128)(2,1)S(1)} %get-tuple-element.113.refs_0_.refs_4_), channel_id=1, source_target_pairs={{0,6},{2,4},{4,2},{6,0},{1,7},{3,5},{5,3},{7,1},{8,14},{10,12},{12... | collective-permute-start | bytes 307208 | tf_op jit(solution)/shard_map/ppermute | solution.py:580
  29.5 8.6 %collective-permute-start.11 = (bf16[400,128]{1,0:T(8,128)(2,1)S(1)}, bf16[400,128]{1,0:T(8,128)(2,1)S(1)}, u32[]{:S(2)}, u32[]{:S(2)}) collective-permute-start(bf16[400,128]{1,0:T(8,128)(2,1)S(1)} %get-tuple-element.113.refs_0_.refs_4_), channel_id=1, source_target_pairs={{0,4},{2,6},{4,0},{6,2},{1,5},{3,7},{5,1},{7,3},{8,12},{10,14},{12... | collective-permute-start | bytes 307208 | tf_op jit(solution)/shard_map/ppermute | solution.py:580
  29.5 8.6 %collective-permute-start.10 = (bf16[400,128]{1,0:T(8,128)(2,1)S(1)}, bf16[400,128]{1,0:T(8,128)(2,1)S(1)}, u32[]{:S(2)}, u32[]{:S(2)}) collective-permute-start(bf16[400,128]{1,0:T(8,128)(2,1)S(1)} %get-tuple-element.113.refs_0_.refs_4_), channel_id=1, source_target_pairs={{0,2},{2,0},{4,6},{6,4},{1,3},{3,1},{5,7},{7,5},{8,10},{10,8},{12,... | collective-permute-start | bytes 307208 | tf_op jit(solution)/shard_map/ppermute | solution.py:580
  39.5 7.3 %collective-permute-start.15 = (bf16[256,128]{1,0:T(8,128)(2,1)S(1)}, bf16[256,128]{1,0:T(8,128)(2,1)S(1)}, u32[]{:S(2)}, u32[]{:S(2)}) collective-permute-start(bf16[256,128]{1,0:T(8,128)(2,1)S(1)} %get-tuple-element.115.refs_0_), channel_id=1, source_target_pairs={{0,6},{2,4},{4,2},{6,0},{1,7},{3,5},{5,3},{7,1},{8,14},{10,12},{12... | collective-permute-start | bytes 196616 | tf_op jit(solution)/shard_map/ppermute | solution.py:580
  42.0 6.7 %collective-permute-start.14 = (bf16[256,128]{1,0:T(8,128)(2,1)S(1)}, bf16[256,128]{1,0:T(8,128)(2,1)S(1)}, u32[]{:S(2)}, u32[]{:S(2)}) collective-permute-start(bf16[256,128]{1,0:T(8,128)(2,1)S(1)} %get-tuple-element.115.refs_0_), channel_id=1, source_target_pairs={{0,4},{2,6},{4,0},{6,2},{1,5},{3,7},{5,1},{7,3},{8,12},{10,14},{12... | collective-permute-start | bytes 196616 | tf_op jit(solution)/shard_map/ppermute | solution.py:580
  42.0 6.7 %collective-permute-start.13 = (bf16[256,128]{1,0:T(8,128)(2,1)S(1)}, bf16[256,128]{1,0:T(8,128)(2,1)S(1)}, u32[]{:S(2)}, u32[]{:S(2)}) collective-permute-start(bf16[256,128]{1,0:T(8,128)(2,1)S(1)} %get-tuple-element.115.refs_0_), channel_id=1, source_target_pairs={{0,2},{2,0},{4,6},{6,4},{1,3},{3,1},{5,7},{7,5},{8,10},{10,8},{12,... | collective-permute-start | bytes 196616 | tf_op jit(solution)/shard_map/ppermute | solution.py:580
  44.3 9.3 %collective-permute-start.21 = (bf16[256,128]{1,0:T(8,128)(2,1)S(1)}, bf16[256,128]{1,0:T(8,128)(2,1)S(1)}, u32[]{:S(2)}, u32[]{:S(2)}) collective-permute-start(bf16[256,128]{1,0:T(8,128)(2,1)S(1)} %side.1.refs_4_), channel_id=1, source_target_pairs={{0,6},{2,4},{4,2},{6,0},{1,7},{3,5},{5,3},{7,1},{8,14},{10,12},{12... | collective-permute-start | bytes 196616 | tf_op jit(solution)/shard_map/ppermute | solution.py:580
  46.8 7.8 %collective-permute-start.20 = (bf16[256,128]{1,0:T(8,128)(2,1)S(1)}, bf16[256,128]{1,0:T(8,128)(2,1)S(1)}, u32[]{:S(2)}, u32[]{:S(2)}) collective-permute-start(bf16[256,128]{1,0:T(8,128)(2,1)S(1)} %side.1.refs_4_), channel_id=1, source_target_pairs={{0,4},{2,6},{4,0},{6,2},{1,5},{3,7},{5,1},{7,3},{8,12},{10,14},{12... | collective-permute-start | bytes 196616 | tf_op jit(solution)/shard_map/ppermute | solution.py:580
  46.8 7.8 %collective-permute-start.19 = (bf16[256,128]{1,0:T(8,128)(2,1)S(1)}, bf16[256,128]{1,0:T(8,128)(2,1)S(1)}, u32[]{:S(2)}, u32[]{:S(2)}) collective-permute-start(bf16[256,128]{1,0:T(8,128)(2,1)S(1)} %side.1.refs_4_), channel_id=1, source_target_pairs={{0,2},{2,0},{4,6},{6,4},{1,3},{3,1},{5,7},{7,5},{8,10},{10,8},{12,... | collective-permute-start | bytes 196616 | tf_op jit(solution)/shard_map/ppermute | solution.py:580
  50.1 6.4 %collective-permute-start.18 = (bf16[256,128]{1,0:T(8,128)(2,1)S(1)}, bf16[256,128]{1,0:T(8,128)(2,1)S(1)}, u32[]{:S(2)}, u32[]{:S(2)}) collective-permute-start(bf16[256,128]{1,0:T(8,128)(2,1)S(1)} %get-tuple-element.118.refs_0_), channel_id=1, source_target_pairs={{0,6},{2,4},{4,2},{6,0},{1,7},{3,5},{5,3},{7,1},{8,14},{10,12},{12... | collective-permute-start | bytes 196616 | tf_op jit(solution)/shard_map/ppermute | solution.py:580
  53.6 5.9 %collective-permute-start.17 = (bf16[256,128]{1,0:T(8,128)(2,1)S(1)}, bf16[256,128]{1,0:T(8,128)(2,1)S(1)}, u32[]{:S(2)}, u32[]{:S(2)}) collective-permute-start(bf16[256,128]{1,0:T(8,128)(2,1)S(1)} %get-tuple-element.118.refs_0_), channel_id=1, source_target_pairs={{0,4},{2,6},{4,0},{6,2},{1,5},{3,7},{5,1},{7,3},{8,12},{10,14},{12... | collective-permute-start | bytes 196616 | tf_op jit(solution)/shard_map/ppermute | solution.py:580
  53.6 5.9 %collective-permute-start.16 = (bf16[256,128]{1,0:T(8,128)(2,1)S(1)}, bf16[256,128]{1,0:T(8,128)(2,1)S(1)}, u32[]{:S(2)}, u32[]{:S(2)}) collective-permute-start(bf16[256,128]{1,0:T(8,128)(2,1)S(1)} %get-tuple-element.118.refs_0_), channel_id=1, source_target_pairs={{0,2},{2,0},{4,6},{6,4},{1,3},{3,1},{5,7},{7,5},{8,10},{10,8},{12,... | collective-permute-start | bytes 196616 | tf_op jit(solution)/shard_map/ppermute | solution.py:580
  61.5 6.8 %collective-permute-start.24 = (bf16[272,128]{1,0:T(8,128)(2,1)S(1)}, bf16[272,128]{1,0:T(8,128)(2,1)S(1)}, u32[]{:S(2)}, u32[]{:S(2)}) collective-permute-start(bf16[272,128]{1,0:T(8,128)(2,1)S(1)} %get-tuple-element.122.refs_0_), channel_id=1, source_target_pairs={{0,6},{2,4},{4,2},{6,0},{1,7},{3,5},{5,3},{7,1},{8,14},{10,12},{12... | collective-permute-start | bytes 208904 | tf_op jit(solution)/shard_map/ppermute | solution.py:580
  64.1 6.4 %collective-permute-start.23 = (bf16[272,128]{1,0:T(8,128)(2,1)S(1)}, bf16[272,128]{1,0:T(8,128)(2,1)S(1)}, u32[]{:S(2)}, u32[]{:S(2)}) collective-permute-start(bf16[272,128]{1,0:T(8,128)(2,1)S(1)} %get-tuple-element.122.refs_0_), channel_id=1, source_target_pairs={{0,4},{2,6},{4,0},{6,2},{1,5},{3,7},{5,1},{7,3},{8,12},{10,14},{12... | collective-permute-start | bytes 208904 | tf_op jit(solution)/shard_map/ppermute | solution.py:580
  64.1 6.4 %collective-permute-start.22 = (bf16[272,128]{1,0:T(8,128)(2,1)S(1)}, bf16[272,128]{1,0:T(8,128)(2,1)S(1)}, u32[]{:S(2)}, u32[]{:S(2)}) collective-permute-start(bf16[272,128]{1,0:T(8,128)(2,1)S(1)} %get-tuple-element.122.refs_0_), channel_id=1, source_target_pairs={{0,2},{2,0},{4,6},{6,4},{1,3},{3,1},{5,7},{7,5},{8,10},{10,8},{12,... | collective-permute-start | bytes 208904 | tf_op jit(solution)/shard_map/ppermute | solution.py:580
  71.8 5.8 %collective-permute-start.27 = (bf16[144,128]{1,0:T(8,128)(2,1)S(1)}, bf16[144,128]{1,0:T(8,128)(2,1)S(1)}, u32[]{:S(2)}, u32[]{:S(2)}) collective-permute-start(bf16[144,128]{1,0:T(8,128)(2,1)S(1)} %get-tuple-element.139.refs_0_), channel_id=1, source_target_pairs={{0,6},{2,4},{4,2},{6,0},{1,7},{3,5},{5,3},{7,1},{8,14},{10,12},{12... | collective-permute-start | bytes 110600 | tf_op jit(solution)/shard_map/ppermute | solution.py:580
  74.3 4.9 %collective-permute-start.26 = (bf16[144,128]{1,0:T(8,128)(2,1)S(1)}, bf16[144,128]{1,0:T(8,128)(2,1)S(1)}, u32[]{:S(2)}, u32[]{:S(2)}) collective-permute-start(bf16[144,128]{1,0:T(8,128)(2,1)S(1)} %get-tuple-element.139.refs_0_), channel_id=1, source_target_pairs={{0,4},{2,6},{4,0},{6,2},{1,5},{3,7},{5,1},{7,3},{8,12},{10,14},{12... | collective-permute-start | bytes 110600 | tf_op jit(solution)/shard_map/ppermute | solution.py:580
  74.3 4.9 %collective-permute-start.25 = (bf16[144,128]{1,0:T(8,128)(2,1)S(1)}, bf16[144,128]{1,0:T(8,128)(2,1)S(1)}, u32[]{:S(2)}, u32[]{:S(2)}) collective-permute-start(bf16[144,128]{1,0:T(8,128)(2,1)S(1)} %get-tuple-element.139.refs_0_), channel_id=1, source_target_pairs={{0,2},{2,0},{4,6},{6,4},{1,3},{3,1},{5,7},{7,5},{8,10},{10,8},{12,... | collective-permute-start | bytes 110600 | tf_op jit(solution)/shard_map/ppermute | solution.py:580
  80.4 5.9 %collective-permute-start.30 = (bf16[144,128]{1,0:T(8,128)(2,1)S(1)}, bf16[144,128]{1,0:T(8,128)(2,1)S(1)}, u32[]{:S(2)}, u32[]{:S(2)}) collective-permute-start(bf16[144,128]{1,0:T(8,128)(2,1)S(1)} %get-tuple-element.153.refs_0_), channel_id=1, source_target_pairs={{0,6},{2,4},{4,2},{6,0},{1,7},{3,5},{5,3},{7,1},{8,14},{10,12},{12... | collective-permute-start | bytes 110600 | tf_op jit(solution)/shard_map/ppermute | solution.py:580
  82.5 5.3 %collective-permute-start.29 = (bf16[144,128]{1,0:T(8,128)(2,1)S(1)}, bf16[144,128]{1,0:T(8,128)(2,1)S(1)}, u32[]{:S(2)}, u32[]{:S(2)}) collective-permute-start(bf16[144,128]{1,0:T(8,128)(2,1)S(1)} %get-tuple-element.153.refs_0_), channel_id=1, source_target_pairs={{0,4},{2,6},{4,0},{6,2},{1,5},{3,7},{5,1},{7,3},{8,12},{10,14},{12... | collective-permute-start | bytes 110600 | tf_op jit(solution)/shard_map/ppermute | solution.py:580
  83.0 4.7 %collective-permute-start.28 = (bf16[144,128]{1,0:T(8,128)(2,1)S(1)}, bf16[144,128]{1,0:T(8,128)(2,1)S(1)}, u32[]{:S(2)}, u32[]{:S(2)}) collective-permute-start(bf16[144,128]{1,0:T(8,128)(2,1)S(1)} %get-tuple-element.153.refs_0_), channel_id=1, source_target_pairs={{0,2},{2,0},{4,6},{6,4},{1,3},{3,1},{5,7},{7,5},{8,10},{10,8},{12,... | collective-permute-start | bytes 110600 | tf_op jit(solution)/shard_map/ppermute | solution.py:580
  90.8 19.1 %collective-permute-start.35 = (bf16[256,512]{1,0:T(8,128)(2,1)S(1)}, bf16[256,512]{1,0:T(8,128)(2,1)S(1)}, u32[]{:S(2)}, u32[]{:S(2)}) collective-permute-start(bf16[256,512]{1,0:T(8,128)(2,1)S(1)} %get-tuple-element.170), channel_id=1, source_target_pairs={{0,8},{8,0},{16,24},{24,16},{1,9},{9,1},{17,25},{25,17},{2,10},{10... | collective-permute-start | bytes 786440 | tf_op jit(solution)/shard_map/ppermute | solution.py:583
  92.3 17.5 %collective-permute-start.36 = (bf16[256,512]{1,0:T(8,128)(2,1)S(1)}, bf16[256,512]{1,0:T(8,128)(2,1)S(1)}, u32[]{:S(2)}, u32[]{:S(2)}) collective-permute-start(bf16[256,512]{1,0:T(8,128)(2,1)S(1)} %get-tuple-element.171), channel_id=1, source_target_pairs={{0,16},{8,24},{16,0},{24,8},{1,17},{9,25},{17,1},{25,9},{2,18},{10... | collective-permute-start | bytes 786440 | tf_op jit(solution)/shard_map/ppermute | solution.py:583
  93.8 16.0 %collective-permute-start.37 = (bf16[256,512]{1,0:T(8,128)(2,1)S(1)}, bf16[256,512]{1,0:T(8,128)(2,1)S(1)}, u32[]{:S(2)}, u32[]{:S(2)}) collective-permute-start(bf16[256,512]{1,0:T(8,128)(2,1)S(1)} %get-tuple-element.172), channel_id=1, source_target_pairs={{0,24},{8,16},{16,8},{24,0},{1,25},{9,17},{17,9},{25,1},{2,26},{10... | collective-permute-start | bytes 786440 | tf_op jit(solution)/shard_map/ppermute | solution.py:583
  96.6 8.6 %collective-permute-start.39 = (bf16[16,512]{1,0:T(8,128)(2,1)S(1)}, bf16[16,512]{1,0:T(8,128)(2,1)S(1)}, u32[]{:S(2)}, u32[]{:S(2)}) collective-permute-start(bf16[16,512]{1,0:T(8,128)(2,1)S(1)} %get-tuple-element.182), channel_id=1, source_target_pairs={{0,8},{8,0},{16,24},{24,16},{1,9},{9,1},{17,25},{25,17},{2,10},{10... | collective-permute-start | bytes 49160 | tf_op jit(solution)/shard_map/ppermute | solution.py:583
  98.2 9.5 %collective-permute-start.40 = (bf16[16,512]{1,0:T(8,128)(2,1)S(1)}, bf16[16,512]{1,0:T(8,128)(2,1)S(1)}, u32[]{:S(2)}, u32[]{:S(2)}) collective-permute-start(bf16[16,512]{1,0:T(8,128)(2,1)S(1)} %get-tuple-element.183), channel_id=1, source_target_pairs={{0,16},{8,24},{16,0},{24,8},{1,17},{9,25},{17,1},{25,9},{2,18},{10... | collective-permute-start | bytes 49160 | tf_op jit(solution)/shard_map/ppermute | solution.py:583
  (12 other events, 26.7 us)

commit v15 on v13

--- a/solution.py
+++ b/solution.py
@@ -523,12 +523,15 @@
 
 def combine_kernel(sections, *refs):
     kept, swapped = refs[:sections], refs[sections : 2 * sections]
-    outs, sums = refs[2 * sections : 3 * sections], refs[3 * sections]
+    outs = refs[2 * sections :]
     section = lax.axis_index("pipe")
-    for layer in range(sections):
-        sums[layer] = (kept[layer][...].astype(F32) + swapped[layer][...].astype(F32)).astype(BF)
     for distance in range(sections):
-        outs[distance][...] = sums[section ^ distance]
+        for layer in range(sections):
+
+            @pl.when(section == layer ^ distance)
+            def _(distance=distance, layer=layer):
+                total = kept[layer][...].astype(F32) + swapped[layer][...].astype(F32)
+                outs[distance][...] = total.astype(BF)
 
 
 def finish_kernel(sections, *refs):
@@ -716,7 +719,8 @@
         pays = exchange(pay)
         waiting.append((layer, [reduceds[layer]], dout, dred, gain_row))
         done = [gradients(*item) for item in waiting]
-        pays, done = lax.optimization_barrier((pays, done))
+        if layer > 1:
+            pays, done = lax.optimization_barrier((pays, done))
         for item, (keep, send) in zip(waiting, done):
             halves[item[0]] = (keep, swapped(send))
         waiting = []
@@ -740,7 +744,6 @@
         vmem_specs(2 * sections),
         [half_shape] * sections,
         "combine",
-        scratch_shapes=[pltpu.VMEM((sections,) + grads_shape[1:], BF)],
     )
     arrived = [parts[0]] + [across(parts[distance], distance) for distance in range(1, sections)]
     gain_grad, first_grad, second_grad = call(

time: 109 us -> 108 us (level)
  transfers between devices with their start and end apart: 38 -> 38, of which waited for: 21 -> 20; matrix products, arithmetic and copies ran while one was open for 0% -> 0% of each run, Pallas kernels for 4% -> 4%
where the time goes in v15:
time: 108 us
  starting transfers between devices  47.2 us (44%)
  waiting for transfers between devices  42.6 us (39%)
  Pallas kernels  15.2 us (14%)
  local copies, waits for them, and re-layouts  1.86 us (2%)
    ppermute x24, starting transfers between devices, shifted(): return lax.ppermute(value, 'z', [(i, i ^ shift) for i in range(groups)])  37.4 us
    ppermute x24, waiting for transfers between devices, shifted(): return lax.ppermute(value, 'z', [(i, i ^ shift) for i in range(groups)])  25.5 us
    ppermute x6, waiting for transfers between devices, across(): lax.ppermute(value, 'pipe', [(i, i ^ distance) for i in range(sections)])  14.2 us
    pallas_call x15, Pallas kernels, call(): pl.pallas_call(kernel, in_specs=specs, out_specs=vmem_specs(len(outs)), o...  12.9 us
    ppermute x6, starting transfers between devices, across(): lax.ppermute(value, 'pipe', [(i, i ^ distance) for i in range(sections)])  8.1 us
    ppermute x8, waiting for transfers between devices, swapped(): return lax.ppermute(value, 'core', [(i, 1 - i) for i in range(sides)])  2.93 us
    pallas_call x1, Pallas kernels, pack(): pl.pallas_call(functools.partial(pack_kernel, groups, micro_local), in_sp...  2.28 us
  transfers between devices with their start and end apart: 38, of which 20 were waited for; matrix products, arithmetic and copies ran while one was open for 0% of the time, Pallas kernels for 4%

profile of v15, /device:TPU:0, one launch (start us, length us, event | category | flops | bytes accessed | tf_op | source)
XLA Modules:
  0.0 107.7 jit_solution(1950195976661528462)
XLA Ops:
  0.6 2.3 %pack.1 = (bf16[32,2176]{1,0:T(8,128)(2,1)}, bf16[32,2176]{1,0:T(8,128)(2,1)}, bf16[32,2176]{1,0:T(8,128)(2,1)}, bf16[32,2176]{1,0:T(8,128)(2,1)}, bf16[1040,128]{1,0:T(8,128)(2,1)}) custom-call(bf16[2,2,32,4096]{3,2,1,0:T(8,128)(2,1)} %refs_0_.1, bf16[2,2,32,4096]{3,2,1,0:T(8,128)(2,1)} %refs_1_.1, s32[2,2,4]{2,1,0:T(2,128)} %refs_2_.1, s32[2,2]{1,0:T(2,128)} %refs_3_.1, ...), custom_call_target="tpu_custom_call" | custom-call | tf_op jit(solution)/shard_map/pack/pallas_call | solution.py:124
  2.9 3.0 %collective-permute-start = (bf16[1040,128]{1,0:T(8,128)(2,1)}, bf16[1040,128]{1,0:T(8,128)(2,1)S(1)}, u32[]{:S(2)}, u32[]{:S(2)}) collective-permute-start(bf16[1040,128]{1,0:T(8,128)(2,1)} %get-tuple-element.81.packed), channel_id=1, source_target_pairs={{0,8},{8,0},{16,24},{24,16},{1,9},{9,1},{17,25},{25,17},{2,10},{10... | collective-permute-start | bytes 798728 | tf_op jit(solution)/shard_map/ppermute | solution.py:569
  7.5 4.1 %collective-permute-start.1 = (bf16[32,2176]{1,0:T(8,128)(2,1)}, bf16[32,2176]{1,0:T(8,128)(2,1)S(1)}, u32[]{:S(2)}, u32[]{:S(2)}) collective-permute-start(bf16[32,2176]{1,0:T(8,128)(2,1)} %get-tuple-element.83), channel_id=1, source_target_pairs={{0,6},{2,4},{4,2},{6,0},{1,7},{3,5},{5,3},{7,1},{8,14},{10,12},{12... | collective-permute-start | bytes 417800 | tf_op jit(solution)/shard_map/ppermute | solution.py:566
  11.5 1.8 %collective-permute-done.early = bf16[1040,128]{1,0:T(8,128)(2,1)S(1)} collective-permute-done((bf16[1040,128]{1,0:T(8,128)(2,1)}, bf16[1040,128]{1,0:T(8,128)(2,1)S(1)}, u32[]{:S(2)}, u32[]{:S(2)}) %collective-permute-start) | collective-permute-done | bytes 266272 | tf_op jit(solution)/shard_map/ppermute | solution.py:569
  13.4 2.1 %collective-permute-start.3 = (bf16[32,2176]{1,0:T(8,128)(2,1)}, bf16[32,2176]{1,0:T(8,128)(2,1)S(1)}, u32[]{:S(2)}, u32[]{:S(2)}) collective-permute-start(bf16[32,2176]{1,0:T(8,128)(2,1)} %get-tuple-element.85), channel_id=1, source_target_pairs={{0,2},{2,0},{4,6},{6,4},{1,3},{3,1},{5,7},{7,5},{8,10},{10,8},{12,... | collective-permute-start | bytes 417800 | tf_op jit(solution)/shard_map/ppermute | solution.py:566
  17.4 5.3 %collective-permute-done.2.refs_2_ = bf16[32,2176]{1,0:T(8,128)(2,1)S(1)} collective-permute-done((bf16[32,2176]{1,0:T(8,128)(2,1)}, bf16[32,2176]{1,0:T(8,128)(2,1)S(1)}, u32[]{:S(2)}, u32[]{:S(2)}) %collective-permute-start.2) | collective-permute-done | bytes 139296 | tf_op jit(solution)/shard_map/ppermute | solution.py:566
  25.4 1.6 %forward_first.1 = (bf16[1,8,128,128]{3,2,1,0:T(8,128)(2,1)S(1)}, bf16[128,1024]{1,0:T(8,128)(2,1)S(1)}, bf16[400,128]{1,0:T(8,128)(2,1)S(1)}, bf16[4,2,1040,128]{3,2,1,0:T(8,128)(2,1)S(1)}) custom-call(bf16[1040,128]{1,0:T(8,128)(2,1)S(1)} %get-tuple-element.88.refs_0_, bf16[1040,128]{1,0:T(8,128)(2,1)S(1)} %get-tuple-element.89.refs_1_, ...), custom_call_target="tpu_custom_call" | custom-call | tf_op jit(solution)/shard_map/forward_first/pallas_call | solution.py:587
  27.0 2.5 %collective-permute-start.12 = (bf16[400,128]{1,0:T(8,128)(2,1)S(1)}, bf16[400,128]{1,0:T(8,128)(2,1)S(1)}, u32[]{:S(2)}, u32[]{:S(2)}) collective-permute-start(bf16[400,128]{1,0:T(8,128)(2,1)S(1)} %get-tuple-element.99.refs_0_.refs_4_), channel_id=1, source_target_pairs={{0,6},{2,4},{4,2},{6,0},{1,7},{3,5},{5,3},{7,1},{8,14},{10,12},{12... | collective-permute-start | bytes 307208 | tf_op jit(solution)/shard_map/ppermute | solution.py:566
  29.5 1.9 %collective-permute-start.10 = (bf16[400,128]{1,0:T(8,128)(2,1)S(1)}, bf16[400,128]{1,0:T(8,128)(2,1)S(1)}, u32[]{:S(2)}, u32[]{:S(2)}) collective-permute-start(bf16[400,128]{1,0:T(8,128)(2,1)S(1)} %get-tuple-element.99.refs_0_.refs_4_), channel_id=1, source_target_pairs={{0,2},{2,0},{4,6},{6,4},{1,3},{3,1},{5,7},{7,5},{8,10},{10,8},{12,... | collective-permute-start | bytes 307208 | tf_op jit(solution)/shard_map/ppermute | solution.py:566
  31.4 3.2 %collective-permute-done.12.refs_3_.refs_7_ = bf16[400,128]{1,0:T(8,128)(2,1)S(1)} collective-permute-done((bf16[400,128]{1,0:T(8,128)(2,1)S(1)}, bf16[400,128]{1,0:T(8,128)(2,1)S(1)}, u32[]{:S(2)}, u32[]{:S(2)}) %collective-permute-start.12) | collective-permute-done | bytes 102432 | tf_op jit(solution)/shard_map/ppermute | solution.py:566
  34.7 3.5 %collective-permute-done.11.refs_2_.refs_6_ = bf16[400,128]{1,0:T(8,128)(2,1)S(1)} collective-permute-done((bf16[400,128]{1,0:T(8,128)(2,1)S(1)}, bf16[400,128]{1,0:T(8,128)(2,1)S(1)}, u32[]{:S(2)}, u32[]{:S(2)}) %collective-permute-start.11) | collective-permute-done | bytes 102432 | tf_op jit(solution)/shard_map/ppermute | solution.py:566
  39.5 2.5 %collective-permute-start.15 = (bf16[256,128]{1,0:T(8,128)(2,1)S(1)}, bf16[256,128]{1,0:T(8,128)(2,1)S(1)}, u32[]{:S(2)}, u32[]{:S(2)}) collective-permute-start(bf16[256,128]{1,0:T(8,128)(2,1)S(1)} %get-tuple-element.101.refs_0_), channel_id=1, source_target_pairs={{0,6},{2,4},{4,2},{6,0},{1,7},{3,5},{5,3},{7,1},{8,14},{10,12},{12... | collective-permute-start | bytes 196616 | tf_op jit(solution)/shard_map/ppermute | solution.py:566
  42.0 1.9 %collective-permute-start.13 = (bf16[256,128]{1,0:T(8,128)(2,1)S(1)}, bf16[256,128]{1,0:T(8,128)(2,1)S(1)}, u32[]{:S(2)}, u32[]{:S(2)}) collective-permute-start(bf16[256,128]{1,0:T(8,128)(2,1)S(1)} %get-tuple-element.101.refs_0_), channel_id=1, source_target_pairs={{0,2},{2,0},{4,6},{6,4},{1,3},{3,1},{5,7},{7,5},{8,10},{10,8},{12,... | collective-permute-start | bytes 196616 | tf_op jit(solution)/shard_map/ppermute | solution.py:566
  44.3 2.5 %collective-permute-start.21 = (bf16[256,128]{1,0:T(8,128)(2,1)S(1)}, bf16[256,128]{1,0:T(8,128)(2,1)S(1)}, u32[]{:S(2)}, u32[]{:S(2)}) collective-permute-start(bf16[256,128]{1,0:T(8,128)(2,1)S(1)} %side.1.refs_4_), channel_id=1, source_target_pairs={{0,6},{2,4},{4,2},{6,0},{1,7},{3,5},{5,3},{7,1},{8,14},{10,12},{12... | collective-permute-start | bytes 196616 | tf_op jit(solution)/shard_map/ppermute | solution.py:566
  46.8 1.9 %collective-permute-start.19 = (bf16[256,128]{1,0:T(8,128)(2,1)S(1)}, bf16[256,128]{1,0:T(8,128)(2,1)S(1)}, u32[]{:S(2)}, u32[]{:S(2)}) collective-permute-start(bf16[256,128]{1,0:T(8,128)(2,1)S(1)} %side.1.refs_4_), channel_id=1, source_target_pairs={{0,2},{2,0},{4,6},{6,4},{1,3},{3,1},{5,7},{7,5},{8,10},{10,8},{12,... | collective-permute-start | bytes 196616 | tf_op jit(solution)/shard_map/ppermute | solution.py:566
  50.1 3.5 %collective-permute-start.18 = (bf16[256,128]{1,0:T(8,128)(2,1)S(1)}, bf16[256,128]{1,0:T(8,128)(2,1)S(1)}, u32[]{:S(2)}, u32[]{:S(2)}) collective-permute-start(bf16[256,128]{1,0:T(8,128)(2,1)S(1)} %get-tuple-element.104.refs_0_), channel_id=1, source_target_pairs={{0,6},{2,4},{4,2},{6,0},{1,7},{3,5},{5,3},{7,1},{8,14},{10,12},{12... | collective-permute-start | bytes 196616 | tf_op jit(solution)/shard_map/ppermute | solution.py:566
  54.6 2.0 %collective-permute-done.18.refs_3_ = bf16[256,128]{1,0:T(8,128)(2,1)S(1)} collective-permute-done((bf16[256,128]{1,0:T(8,128)(2,1)S(1)}, bf16[256,128]{1,0:T(8,128)(2,1)S(1)}, u32[]{:S(2)}, u32[]{:S(2)}) %collective-permute-start.18) | collective-permute-done | bytes 65568 | tf_op jit(solution)/shard_map/ppermute | solution.py:566
  56.6 2.9 %collective-permute-done.17.refs_2_ = bf16[256,128]{1,0:T(8,128)(2,1)S(1)} collective-permute-done((bf16[256,128]{1,0:T(8,128)(2,1)S(1)}, bf16[256,128]{1,0:T(8,128)(2,1)S(1)}, u32[]{:S(2)}, u32[]{:S(2)}) %collective-permute-start.17) | collective-permute-done | bytes 65568 | tf_op jit(solution)/shard_map/ppermute | solution.py:566
  59.4 2.1 %turn.1 = (bf16[128,1024]{1,0:T(8,128)(2,1)S(1)}, f32[128,128]{1,0:T(8,128)S(1)}, bf16[128,128]{1,0:T(8,128)(2,1)S(1)}, f32[128,128]{1,0:T(8,128)S(1)}, bf16[128...) custom-call(bf16[256,128]{1,0:T(8,128)(2,1)S(1)} %get-tuple-element., ...), custom_call_target="tpu_custom_call" | custom-call | tf_op jit(solution)/shard_map/turn/pallas_call | solution.py:587
  61.5 2.5 %collective-permute-start.24 = (bf16[272,128]{1,0:T(8,128)(2,1)S(1)}, bf16[272,128]{1,0:T(8,128)(2,1)S(1)}, u32[]{:S(2)}, u32[]{:S(2)}) collective-permute-start(bf16[272,128]{1,0:T(8,128)(2,1)S(1)} %get-tuple-element.108.refs_0_), channel_id=1, source_target_pairs={{0,6},{2,4},{4,2},{6,0},{1,7},{3,5},{5,3},{7,1},{8,14},{10,12},{12... | collective-permute-start | bytes 208904 | tf_op jit(solution)/shard_map/ppermute | solution.py:566
  64.0 1.9 %collective-permute-start.22 = (bf16[272,128]{1,0:T(8,128)(2,1)S(1)}, bf16[272,128]{1,0:T(8,128)(2,1)S(1)}, u32[]{:S(2)}, u32[]{:S(2)}) collective-permute-start(bf16[272,128]{1,0:T(8,128)(2,1)S(1)} %get-tuple-element.108.refs_0_), channel_id=1, source_target_pairs={{0,2},{2,0},{4,6},{6,4},{1,3},{3,1},{5,7},{7,5},{8,10},{10,8},{12,... | collective-permute-start | bytes 208904 | tf_op jit(solution)/shard_map/ppermute | solution.py:566
  66.0 2.4 %collective-permute-done.24.refs_3_ = bf16[272,128]{1,0:T(8,128)(2,1)S(1)} collective-permute-done((bf16[272,128]{1,0:T(8,128)(2,1)S(1)}, bf16[272,128]{1,0:T(8,128)(2,1)S(1)}, u32[]{:S(2)}, u32[]{:S(2)}) %collective-permute-start.24) | collective-permute-done | bytes 69664 | tf_op jit(solution)/shard_map/ppermute | solution.py:566
  68.3 2.1 %collective-permute-done.23.refs_2_ = bf16[272,128]{1,0:T(8,128)(2,1)S(1)} collective-permute-done((bf16[272,128]{1,0:T(8,128)(2,1)S(1)}, bf16[272,128]{1,0:T(8,128)(2,1)S(1)}, u32[]{:S(2)}, u32[]{:S(2)}) %collective-permute-start.23) | collective-permute-done | bytes 69664 | tf_op jit(solution)/shard_map/ppermute | solution.py:566
  71.7 2.5 %collective-permute-start.27 = (bf16[144,128]{1,0:T(8,128)(2,1)S(1)}, bf16[144,128]{1,0:T(8,128)(2,1)S(1)}, u32[]{:S(2)}, u32[]{:S(2)}) collective-permute-start(bf16[144,128]{1,0:T(8,128)(2,1)S(1)} %get-tuple-element.127.refs_0_), channel_id=1, source_target_pairs={{0,6},{2,4},{4,2},{6,0},{1,7},{3,5},{5,3},{7,1},{8,14},{10,12},{12... | collective-permute-start | bytes 110600 | tf_op jit(solution)/shard_map/ppermute | solution.py:566
  74.3 1.9 %collective-permute-start.25 = (bf16[144,128]{1,0:T(8,128)(2,1)S(1)}, bf16[144,128]{1,0:T(8,128)(2,1)S(1)}, u32[]{:S(2)}, u32[]{:S(2)}) collective-permute-start(bf16[144,128]{1,0:T(8,128)(2,1)S(1)} %get-tuple-element.127.refs_0_), channel_id=1, source_target_pairs={{0,2},{2,0},{4,6},{6,4},{1,3},{3,1},{5,7},{7,5},{8,10},{10,8},{12,... | collective-permute-start | bytes 110600 | tf_op jit(solution)/shard_map/ppermute | solution.py:566
  77.6 1.6 %collective-permute-done.26.refs_2_ = bf16[144,128]{1,0:T(8,128)(2,1)S(1)} collective-permute-done((bf16[144,128]{1,0:T(8,128)(2,1)S(1)}, bf16[144,128]{1,0:T(8,128)(2,1)S(1)}, u32[]{:S(2)}, u32[]{:S(2)}) %collective-permute-start.26) | collective-permute-done | bytes 36896 | tf_op jit(solution)/shard_map/ppermute | solution.py:566
  80.4 2.0 %collective-permute-start.30 = (bf16[144,128]{1,0:T(8,128)(2,1)S(1)}, bf16[144,128]{1,0:T(8,128)(2,1)S(1)}, u32[]{:S(2)}, u32[]{:S(2)}) collective-permute-start(bf16[144,128]{1,0:T(8,128)(2,1)S(1)} %get-tuple-element.134.refs_0_), channel_id=1, source_target_pairs={{0,6},{2,4},{4,2},{6,0},{1,7},{3,5},{5,3},{7,1},{8,14},{10,12},{12... | collective-permute-start | bytes 110600 | tf_op jit(solution)/shard_map/ppermute | solution.py:566
  82.9 1.9 %collective-permute-start.28 = (bf16[144,128]{1,0:T(8,128)(2,1)S(1)}, bf16[144,128]{1,0:T(8,128)(2,1)S(1)}, u32[]{:S(2)}, u32[]{:S(2)}) collective-permute-start(bf16[144,128]{1,0:T(8,128)(2,1)S(1)} %get-tuple-element.134.refs_0_), channel_id=1, source_target_pairs={{0,2},{2,0},{4,6},{6,4},{1,3},{3,1},{5,7},{7,5},{8,10},{10,8},{12,... | collective-permute-start | bytes 110600 | tf_op jit(solution)/shard_map/ppermute | solution.py:566
  89.1 1.5 %collective-permute-done.31.refs_4_ = bf16[272,512]{1,0:T(8,128)(2,1)S(1)} collective-permute-done((bf16[272,512]{1,0:T(8,128)(2,1)S(1)}, bf16[272,512]{1,0:T(8,128)(2,1)S(1)}, u32[]{:S(2)}, u32[]{:S(2)}) %collective-permute-start.31) | collective-permute-done | bytes 278560 | tf_op jit(solution)/shard_map/ppermute | solution.py:572
  90.9 1.5 %collective-permute-start.35 = (bf16[272,512]{1,0:T(8,128)(2,1)S(1)}, bf16[272,512]{1,0:T(8,128)(2,1)S(1)}, u32[]{:S(2)}, u32[]{:S(2)}) collective-permute-start(bf16[272,512]{1,0:T(8,128)(2,1)S(1)} %get-tuple-element.154), channel_id=1, source_target_pairs={{0,8},{8,0},{16,24},{24,16},{1,9},{9,1},{17,25},{25,17},{2,10},{10... | collective-permute-start | bytes 835592 | tf_op jit(solution)/shard_map/ppermute | solution.py:569
  94.5 6.0 %collective-permute-done.35.refs_1_ = bf16[272,512]{1,0:T(8,128)(2,1)S(1)} collective-permute-done((bf16[272,512]{1,0:T(8,128)(2,1)S(1)}, bf16[272,512]{1,0:T(8,128)(2,1)S(1)}, u32[]{:S(2)}, u32[]{:S(2)}) %collective-permute-start.35) | collective-permute-done | bytes 278560 | tf_op jit(solution)/shard_map/ppermute | solution.py:569
  100.5 6.4 %collective-permute-done.36.refs_2_ = bf16[272,512]{1,0:T(8,128)(2,1)S(1)} collective-permute-done((bf16[272,512]{1,0:T(8,128)(2,1)S(1)}, bf16[272,512]{1,0:T(8,128)(2,1)S(1)}, u32[]{:S(2)}, u32[]{:S(2)}) %collective-permute-start.36) | collective-permute-done | bytes 278560 | tf_op jit(solution)/shard_map/ppermute | solution.py:569
  (64 shorter events, 22.0 us)
Async XLA Ops:
  2.9 10.4 %collective-permute-start = (bf16[1040,128]{1,0:T(8,128)(2,1)}, bf16[1040,128]{1,0:T(8,128)(2,1)S(1)}, u32[]{:S(2)}, u32[]{:S(2)}) collective-permute-start(bf16[1040,128]{1,0:T(8,128)(2,1)} %get-tuple-element.81.packed), channel_id=1, source_target_pairs={{0,8},{8,0},{16,24},{24,16},{1,9},{9,1},{17,25},{25,17},{2,10},{10... | collective-permute-start | bytes 798728 | tf_op jit(solution)/shard_map/ppermute | solution.py:569
  5.9 16.8 %collective-permute-start.5 = (bf16[1040,128]{1,0:T(8,128)(2,1)}, bf16[1040,128]{1,0:T(8,128)(2,1)S(1)}, u32[]{:S(2)}, u32[]{:S(2)}) collective-permute-start(bf16[1040,128]{1,0:T(8,128)(2,1)} %get-tuple-element.81.packed), channel_id=1, source_target_pairs={{0,24},{8,16},{16,8},{24,0},{1,25},{9,17},{17,9},{25,1},{2,26},{10... | collective-permute-start | bytes 798728 | tf_op jit(solution)/shard_map/ppermute | solution.py:569
  7.4 15.3 %collective-permute-start.4 = (bf16[1040,128]{1,0:T(8,128)(2,1)}, bf16[1040,128]{1,0:T(8,128)(2,1)S(1)}, u32[]{:S(2)}, u32[]{:S(2)}) collective-permute-start(bf16[1040,128]{1,0:T(8,128)(2,1)} %get-tuple-element.81.packed), channel_id=1, source_target_pairs={{0,16},{8,24},{16,0},{24,8},{1,17},{9,25},{17,1},{25,9},{2,18},{10... | collective-permute-start | bytes 798728 | tf_op jit(solution)/shard_map/ppermute | solution.py:569
  7.5 9.9 %collective-permute-start.1 = (bf16[32,2176]{1,0:T(8,128)(2,1)}, bf16[32,2176]{1,0:T(8,128)(2,1)S(1)}, u32[]{:S(2)}, u32[]{:S(2)}) collective-permute-start(bf16[32,2176]{1,0:T(8,128)(2,1)} %get-tuple-element.83), channel_id=1, source_target_pairs={{0,6},{2,4},{4,2},{6,0},{1,7},{3,5},{5,3},{7,1},{8,14},{10,12},{12... | collective-permute-start | bytes 417800 | tf_op jit(solution)/shard_map/ppermute | solution.py:566
  11.5 11.1 %collective-permute-start.2 = (bf16[32,2176]{1,0:T(8,128)(2,1)}, bf16[32,2176]{1,0:T(8,128)(2,1)S(1)}, u32[]{:S(2)}, u32[]{:S(2)}) collective-permute-start(bf16[32,2176]{1,0:T(8,128)(2,1)} %get-tuple-element.84), channel_id=1, source_target_pairs={{0,4},{2,6},{4,0},{6,2},{1,5},{3,7},{5,1},{7,3},{8,12},{10,14},{12... | collective-permute-start | bytes 417800 | tf_op jit(solution)/shard_map/ppermute | solution.py:566
  13.4 9.3 %collective-permute-start.3 = (bf16[32,2176]{1,0:T(8,128)(2,1)}, bf16[32,2176]{1,0:T(8,128)(2,1)S(1)}, u32[]{:S(2)}, u32[]{:S(2)}) collective-permute-start(bf16[32,2176]{1,0:T(8,128)(2,1)} %get-tuple-element.85), channel_id=1, source_target_pairs={{0,2},{2,0},{4,6},{6,4},{1,3},{3,1},{5,7},{7,5},{8,10},{10,8},{12,... | collective-permute-start | bytes 417800 | tf_op jit(solution)/shard_map/ppermute | solution.py:566
  27.0 7.7 %collective-permute-start.12 = (bf16[400,128]{1,0:T(8,128)(2,1)S(1)}, bf16[400,128]{1,0:T(8,128)(2,1)S(1)}, u32[]{:S(2)}, u32[]{:S(2)}) collective-permute-start(bf16[400,128]{1,0:T(8,128)(2,1)S(1)} %get-tuple-element.99.refs_0_.refs_4_), channel_id=1, source_target_pairs={{0,6},{2,4},{4,2},{6,0},{1,7},{3,5},{5,3},{7,1},{8,14},{10,12},{12... | collective-permute-start | bytes 307208 | tf_op jit(solution)/shard_map/ppermute | solution.py:566
  29.5 8.6 %collective-permute-start.11 = (bf16[400,128]{1,0:T(8,128)(2,1)S(1)}, bf16[400,128]{1,0:T(8,128)(2,1)S(1)}, u32[]{:S(2)}, u32[]{:S(2)}) collective-permute-start(bf16[400,128]{1,0:T(8,128)(2,1)S(1)} %get-tuple-element.99.refs_0_.refs_4_), channel_id=1, source_target_pairs={{0,4},{2,6},{4,0},{6,2},{1,5},{3,7},{5,1},{7,3},{8,12},{10,14},{12... | collective-permute-start | bytes 307208 | tf_op jit(solution)/shard_map/ppermute | solution.py:566
  29.5 8.6 %collective-permute-start.10 = (bf16[400,128]{1,0:T(8,128)(2,1)S(1)}, bf16[400,128]{1,0:T(8,128)(2,1)S(1)}, u32[]{:S(2)}, u32[]{:S(2)}) collective-permute-start(bf16[400,128]{1,0:T(8,128)(2,1)S(1)} %get-tuple-element.99.refs_0_.refs_4_), channel_id=1, source_target_pairs={{0,2},{2,0},{4,6},{6,4},{1,3},{3,1},{5,7},{7,5},{8,10},{10,8},{12,... | collective-permute-start | bytes 307208 | tf_op jit(solution)/shard_map/ppermute | solution.py:566
  39.5 7.3 %collective-permute-start.15 = (bf16[256,128]{1,0:T(8,128)(2,1)S(1)}, bf16[256,128]{1,0:T(8,128)(2,1)S(1)}, u32[]{:S(2)}, u32[]{:S(2)}) collective-permute-start(bf16[256,128]{1,0:T(8,128)(2,1)S(1)} %get-tuple-element.101.refs_0_), channel_id=1, source_target_pairs={{0,6},{2,4},{4,2},{6,0},{1,7},{3,5},{5,3},{7,1},{8,14},{10,12},{12... | collective-permute-start | bytes 196616 | tf_op jit(solution)/shard_map/ppermute | solution.py:566
  42.0 6.7 %collective-permute-start.14 = (bf16[256,128]{1,0:T(8,128)(2,1)S(1)}, bf16[256,128]{1,0:T(8,128)(2,1)S(1)}, u32[]{:S(2)}, u32[]{:S(2)}) collective-permute-start(bf16[256,128]{1,0:T(8,128)(2,1)S(1)} %get-tuple-element.101.refs_0_), channel_id=1, source_target_pairs={{0,4},{2,6},{4,0},{6,2},{1,5},{3,7},{5,1},{7,3},{8,12},{10,14},{12... | collective-permute-start | bytes 196616 | tf_op jit(solution)/shard_map/ppermute | solution.py:566
  42.0 6.7 %collective-permute-start.13 = (bf16[256,128]{1,0:T(8,128)(2,1)S(1)}, bf16[256,128]{1,0:T(8,128)(2,1)S(1)}, u32[]{:S(2)}, u32[]{:S(2)}) collective-permute-start(bf16[256,128]{1,0:T(8,128)(2,1)S(1)} %get-tuple-element.101.refs_0_), channel_id=1, source_target_pairs={{0,2},{2,0},{4,6},{6,4},{1,3},{3,1},{5,7},{7,5},{8,10},{10,8},{12,... | collective-permute-start | bytes 196616 | tf_op jit(solution)/shard_map/ppermute | solution.py:566
  44.3 9.3 %collective-permute-start.21 = (bf16[256,128]{1,0:T(8,128)(2,1)S(1)}, bf16[256,128]{1,0:T(8,128)(2,1)S(1)}, u32[]{:S(2)}, u32[]{:S(2)}) collective-permute-start(bf16[256,128]{1,0:T(8,128)(2,1)S(1)} %side.1.refs_4_), channel_id=1, source_target_pairs={{0,6},{2,4},{4,2},{6,0},{1,7},{3,5},{5,3},{7,1},{8,14},{10,12},{12... | collective-permute-start | bytes 196616 | tf_op jit(solution)/shard_map/ppermute | solution.py:566
  46.8 7.8 %collective-permute-start.20 = (bf16[256,128]{1,0:T(8,128)(2,1)S(1)}, bf16[256,128]{1,0:T(8,128)(2,1)S(1)}, u32[]{:S(2)}, u32[]{:S(2)}) collective-permute-start(bf16[256,128]{1,0:T(8,128)(2,1)S(1)} %side.1.refs_4_), channel_id=1, source_target_pairs={{0,4},{2,6},{4,0},{6,2},{1,5},{3,7},{5,1},{7,3},{8,12},{10,14},{12... | collective-permute-start | bytes 196616 | tf_op jit(solution)/shard_map/ppermute | solution.py:566
  46.8 7.8 %collective-permute-start.19 = (bf16[256,128]{1,0:T(8,128)(2,1)S(1)}, bf16[256,128]{1,0:T(8,128)(2,1)S(1)}, u32[]{:S(2)}, u32[]{:S(2)}) collective-permute-start(bf16[256,128]{1,0:T(8,128)(2,1)S(1)} %side.1.refs_4_), channel_id=1, source_target_pairs={{0,2},{2,0},{4,6},{6,4},{1,3},{3,1},{5,7},{7,5},{8,10},{10,8},{12,... | collective-permute-start | bytes 196616 | tf_op jit(solution)/shard_map/ppermute | solution.py:566
  50.1 6.4 %collective-permute-start.18 = (bf16[256,128]{1,0:T(8,128)(2,1)S(1)}, bf16[256,128]{1,0:T(8,128)(2,1)S(1)}, u32[]{:S(2)}, u32[]{:S(2)}) collective-permute-start(bf16[256,128]{1,0:T(8,128)(2,1)S(1)} %get-tuple-element.104.refs_0_), channel_id=1, source_target_pairs={{0,6},{2,4},{4,2},{6,0},{1,7},{3,5},{5,3},{7,1},{8,14},{10,12},{12... | collective-permute-start | bytes 196616 | tf_op jit(solution)/shard_map/ppermute | solution.py:566
  53.6 5.9 %collective-permute-start.17 = (bf16[256,128]{1,0:T(8,128)(2,1)S(1)}, bf16[256,128]{1,0:T(8,128)(2,1)S(1)}, u32[]{:S(2)}, u32[]{:S(2)}) collective-permute-start(bf16[256,128]{1,0:T(8,128)(2,1)S(1)} %get-tuple-element.104.refs_0_), channel_id=1, source_target_pairs={{0,4},{2,6},{4,0},{6,2},{1,5},{3,7},{5,1},{7,3},{8,12},{10,14},{12... | collective-permute-start | bytes 196616 | tf_op jit(solution)/shard_map/ppermute | solution.py:566
  53.6 5.9 %collective-permute-start.16 = (bf16[256,128]{1,0:T(8,128)(2,1)S(1)}, bf16[256,128]{1,0:T(8,128)(2,1)S(1)}, u32[]{:S(2)}, u32[]{:S(2)}) collective-permute-start(bf16[256,128]{1,0:T(8,128)(2,1)S(1)} %get-tuple-element.104.refs_0_), channel_id=1, source_target_pairs={{0,2},{2,0},{4,6},{6,4},{1,3},{3,1},{5,7},{7,5},{8,10},{10,8},{12,... | collective-permute-start | bytes 196616 | tf_op jit(solution)/shard_map/ppermute | solution.py:566
  61.5 6.8 %collective-permute-start.24 = (bf16[272,128]{1,0:T(8,128)(2,1)S(1)}, bf16[272,128]{1,0:T(8,128)(2,1)S(1)}, u32[]{:S(2)}, u32[]{:S(2)}) collective-permute-start(bf16[272,128]{1,0:T(8,128)(2,1)S(1)} %get-tuple-element.108.refs_0_), channel_id=1, source_target_pairs={{0,6},{2,4},{4,2},{6,0},{1,7},{3,5},{5,3},{7,1},{8,14},{10,12},{12... | collective-permute-start | bytes 208904 | tf_op jit(solution)/shard_map/ppermute | solution.py:566
  64.0 6.4 %collective-permute-start.23 = (bf16[272,128]{1,0:T(8,128)(2,1)S(1)}, bf16[272,128]{1,0:T(8,128)(2,1)S(1)}, u32[]{:S(2)}, u32[]{:S(2)}) collective-permute-start(bf16[272,128]{1,0:T(8,128)(2,1)S(1)} %get-tuple-element.108.refs_0_), channel_id=1, source_target_pairs={{0,4},{2,6},{4,0},{6,2},{1,5},{3,7},{5,1},{7,3},{8,12},{10,14},{12... | collective-permute-start | bytes 208904 | tf_op jit(solution)/shard_map/ppermute | solution.py:566
  64.0 6.4 %collective-permute-start.22 = (bf16[272,128]{1,0:T(8,128)(2,1)S(1)}, bf16[272,128]{1,0:T(8,128)(2,1)S(1)}, u32[]{:S(2)}, u32[]{:S(2)}) collective-permute-start(bf16[272,128]{1,0:T(8,128)(2,1)S(1)} %get-tuple-element.108.refs_0_), channel_id=1, source_target_pairs={{0,2},{2,0},{4,6},{6,4},{1,3},{3,1},{5,7},{7,5},{8,10},{10,8},{12,... | collective-permute-start | bytes 208904 | tf_op jit(solution)/shard_map/ppermute | solution.py:566
  71.7 5.8 %collective-permute-start.27 = (bf16[144,128]{1,0:T(8,128)(2,1)S(1)}, bf16[144,128]{1,0:T(8,128)(2,1)S(1)}, u32[]{:S(2)}, u32[]{:S(2)}) collective-permute-start(bf16[144,128]{1,0:T(8,128)(2,1)S(1)} %get-tuple-element.127.refs_0_), channel_id=1, source_target_pairs={{0,6},{2,4},{4,2},{6,0},{1,7},{3,5},{5,3},{7,1},{8,14},{10,12},{12... | collective-permute-start | bytes 110600 | tf_op jit(solution)/shard_map/ppermute | solution.py:566
  74.3 4.9 %collective-permute-start.26 = (bf16[144,128]{1,0:T(8,128)(2,1)S(1)}, bf16[144,128]{1,0:T(8,128)(2,1)S(1)}, u32[]{:S(2)}, u32[]{:S(2)}) collective-permute-start(bf16[144,128]{1,0:T(8,128)(2,1)S(1)} %get-tuple-element.127.refs_0_), channel_id=1, source_target_pairs={{0,4},{2,6},{4,0},{6,2},{1,5},{3,7},{5,1},{7,3},{8,12},{10,14},{12... | collective-permute-start | bytes 110600 | tf_op jit(solution)/shard_map/ppermute | solution.py:566
  74.3 4.9 %collective-permute-start.25 = (bf16[144,128]{1,0:T(8,128)(2,1)S(1)}, bf16[144,128]{1,0:T(8,128)(2,1)S(1)}, u32[]{:S(2)}, u32[]{:S(2)}) collective-permute-start(bf16[144,128]{1,0:T(8,128)(2,1)S(1)} %get-tuple-element.127.refs_0_), channel_id=1, source_target_pairs={{0,2},{2,0},{4,6},{6,4},{1,3},{3,1},{5,7},{7,5},{8,10},{10,8},{12,... | collective-permute-start | bytes 110600 | tf_op jit(solution)/shard_map/ppermute | solution.py:566
  80.4 5.9 %collective-permute-start.30 = (bf16[144,128]{1,0:T(8,128)(2,1)S(1)}, bf16[144,128]{1,0:T(8,128)(2,1)S(1)}, u32[]{:S(2)}, u32[]{:S(2)}) collective-permute-start(bf16[144,128]{1,0:T(8,128)(2,1)S(1)} %get-tuple-element.134.refs_0_), channel_id=1, source_target_pairs={{0,6},{2,4},{4,2},{6,0},{1,7},{3,5},{5,3},{7,1},{8,14},{10,12},{12... | collective-permute-start | bytes 110600 | tf_op jit(solution)/shard_map/ppermute | solution.py:566
  82.4 5.3 %collective-permute-start.29 = (bf16[144,128]{1,0:T(8,128)(2,1)S(1)}, bf16[144,128]{1,0:T(8,128)(2,1)S(1)}, u32[]{:S(2)}, u32[]{:S(2)}) collective-permute-start(bf16[144,128]{1,0:T(8,128)(2,1)S(1)} %get-tuple-element.134.refs_0_), channel_id=1, source_target_pairs={{0,4},{2,6},{4,0},{6,2},{1,5},{3,7},{5,1},{7,3},{8,12},{10,14},{12... | collective-permute-start | bytes 110600 | tf_op jit(solution)/shard_map/ppermute | solution.py:566
  82.9 4.7 %collective-permute-start.28 = (bf16[144,128]{1,0:T(8,128)(2,1)S(1)}, bf16[144,128]{1,0:T(8,128)(2,1)S(1)}, u32[]{:S(2)}, u32[]{:S(2)}) collective-permute-start(bf16[144,128]{1,0:T(8,128)(2,1)S(1)} %get-tuple-element.134.refs_0_), channel_id=1, source_target_pairs={{0,2},{2,0},{4,6},{6,4},{1,3},{3,1},{5,7},{7,5},{8,10},{10,8},{12,... | collective-permute-start | bytes 110600 | tf_op jit(solution)/shard_map/ppermute | solution.py:566
  85.2 3.8 %collective-permute-start.32 = (bf16[272,512]{1,0:T(8,128)(2,1)S(1)}, bf16[272,512]{1,0:T(8,128)(2,1)S(1)}, u32[]{:S(2)}, u32[]{:S(2)}) collective-permute-start(bf16[272,512]{1,0:T(8,128)(2,1)S(1)} %get-tuple-element.150), channel_id=1, source_target_pairs={{0,1},{1,0},{2,3},{3,2},{4,5},{5,4},{6,7},{7,6},{8,9},{9,8},{10,11... | collective-permute-start | bytes 835592 | tf_op jit(solution)/shard_map/ppermute | solution.py:572
  85.3 3.8 %collective-permute-start.33 = (bf16[272,512]{1,0:T(8,128)(2,1)S(1)}, bf16[272,512]{1,0:T(8,128)(2,1)S(1)}, u32[]{:S(2)}, u32[]{:S(2)}) collective-permute-start(bf16[272,512]{1,0:T(8,128)(2,1)S(1)} %get-tuple-element.151), channel_id=1, source_target_pairs={{0,1},{1,0},{2,3},{3,2},{4,5},{5,4},{6,7},{7,6},{8,9},{9,8},{10,11... | collective-permute-start | bytes 835592 | tf_op jit(solution)/shard_map/ppermute | solution.py:572
  90.9 9.6 %collective-permute-start.35 = (bf16[272,512]{1,0:T(8,128)(2,1)S(1)}, bf16[272,512]{1,0:T(8,128)(2,1)S(1)}, u32[]{:S(2)}, u32[]{:S(2)}) collective-permute-start(bf16[272,512]{1,0:T(8,128)(2,1)S(1)} %get-tuple-element.154), channel_id=1, source_target_pairs={{0,8},{8,0},{16,24},{24,16},{1,9},{9,1},{17,25},{25,17},{2,10},{10... | collective-permute-start | bytes 835592 | tf_op jit(solution)/shard_map/ppermute | solution.py:569
  92.4 14.4 %collective-permute-start.36 = (bf16[272,512]{1,0:T(8,128)(2,1)S(1)}, bf16[272,512]{1,0:T(8,128)(2,1)S(1)}, u32[]{:S(2)}, u32[]{:S(2)}) collective-permute-start(bf16[272,512]{1,0:T(8,128)(2,1)S(1)} %get-tuple-element.155), channel_id=1, source_target_pairs={{0,16},{8,24},{16,0},{24,8},{1,17},{9,25},{17,1},{25,9},{2,18},{10... | collective-permute-start | bytes 835592 | tf_op jit(solution)/shard_map/ppermute | solution.py:569
  93.9 12.9 %collective-permute-start.37 = (bf16[272,512]{1,0:T(8,128)(2,1)S(1)}, bf16[272,512]{1,0:T(8,128)(2,1)S(1)}, u32[]{:S(2)}, u32[]{:S(2)}) collective-permute-start(bf16[272,512]{1,0:T(8,128)(2,1)S(1)} %get-tuple-element.156), channel_id=1, source_target_pairs={{0,24},{8,16},{16,8},{24,0},{1,25},{9,17},{17,9},{25,1},{2,26},{10... | collective-permute-start | bytes 835592 | tf_op jit(solution)/shard_map/ppermute | solution.py:569
  (8 other events, 13.7 us)

commit v16 on v15

--- a/solution.py
+++ b/solution.py
@@ -534,6 +534,54 @@
                 outs[distance][...] = total.astype(BF)
 
 
+def combine_halves_kernel(*refs):
+    kept, swapped = refs[:4], refs[4:8]
+    mine, by_x, by_y, later_x, later_y = refs[8:]
+    rows = mine.shape[0]
+    half = mine.shape[1] // 2
+    section = lax.axis_index("pipe")
+    for distance in range(4):
+        for layer in range(4):
+
+            @pl.when(section == layer ^ distance)
+            def _(distance=distance, layer=layer):
+                total = kept[layer][...].astype(F32) + swapped[layer][...].astype(F32)
+                total = total.astype(BF)
+                left, right = total[:, :half], total[:, half:]
+                if distance == 0:
+                    mine[...] = total
+                elif distance == 1:
+                    by_x[0:rows, :] = right
+                    later_x[...] = left
+                elif distance == 2:
+                    by_y[0:rows, :] = left
+                    later_y[...] = right
+                else:
+                    by_x[rows:, :] = right
+                    by_y[rows:, :] = left
+
+
+def relay_kernel(later_x, later_y, from_x, from_y, to_x, to_y):
+    rows = later_x.shape[0]
+    to_x[...] = (later_x[...].astype(F32) + from_y[rows:, :].astype(F32)).astype(BF)
+    to_y[...] = (later_y[...].astype(F32) + from_x[rows:, :].astype(F32)).astype(BF)
+
+
+def finish_halves_kernel(mine, from_x, from_y, last_x, last_y, gain, first, second):
+    rank = second.shape[1]
+    rows = mine.shape[0]
+    half = mine.shape[1] // 2
+    for side, (direct, relayed) in enumerate(((from_y, last_x), (from_x, last_y))):
+        span = slice(side * half, (side + 1) * half)
+        total = mine[:, span].astype(F32) + direct[0:rows, :].astype(F32)
+        total = total + relayed[...].astype(F32)
+        for block in range(half // rank):
+            base = side * half + block * HD
+            first[0, base : base + HD, :] = total[0:HD, block * rank : (block + 1) * rank]
+        second[0, :, span] = total[rank : 2 * rank]
+        gain[:, span] = total[2 * rank : 2 * rank + 1]
+
+
 def finish_kernel(sections, *refs):
     parts = refs[:sections]
     gain, first, second = refs[sections:]
@@ -738,9 +786,43 @@
     )
     halves[0] = (keep, swapped(send))
 
+    gradients_of = [
+        shaped((1, own), F32),
+        shaped((1, own, rank), F32),
+        shaped((1, rank, own), F32),
+    ]
+    pieces = [pair[side] for side in range(2) for pair in halves]
+    if sections == 4 and own % (2 * HD) == 0:
+        height = half_shape.shape[0]
+        double = shaped((2 * height, own // 2))
+        single = shaped((height, own // 2))
+        whole, by_x, by_y, later_x, later_y = call(
+            combine_halves_kernel,
+            pieces,
+            vmem_specs(8),
+            [half_shape, double, double, single, single],
+            "combine",
+        )
+        from_x, from_y = across(by_x, 1), across(by_y, 2)
+        to_x, to_y = call(
+            relay_kernel,
+            (later_x, later_y, from_x, from_y),
+            vmem_specs(4),
+            [single, single],
+            "relay",
+        )
+        return tuple(
+            call(
+                finish_halves_kernel,
+                (whole, from_x, from_y, across(to_x, 1), across(to_y, 2)),
+                vmem_specs(5),
+                gradients_of,
+                "finish",
+            )
+        )
     parts = call(
         functools.partial(combine_kernel, sections),
-        [pair[side] for side in range(2) for pair in halves],
+        pieces,
         vmem_specs(2 * sections),
         [half_shape] * sections,
         "combine",
@@ -750,11 +832,7 @@
         functools.partial(finish_kernel, sections),
         arrived,
         vmem_specs(sections),
-        [
-            shaped((1, own), F32),
-            shaped((1, own, rank), F32),
-            shaped((1, rank, own), F32),
-        ],
+        gradients_of,
         "finish",
     )
     return (gain_grad, first_grad, second_grad)

time: 108 us -> 108 us (level)
  waiting for transfers between devices: 42.6 us -> 40.7 us
  starting transfers between devices: 47.2 us -> 48.8 us
    ppermute x6 -> x7, waiting for transfers between devices: 14.2 us -> 12.3 us  [across(): lax.ppermute(value, 'pipe', [(i, i ^ distance) for i in range(sections)])]
    ppermute x6 -> x7, starting transfers between devices: 8.1 us -> 9.7 us  [across(): lax.ppermute(value, 'pipe', [(i, i ^ distance) for i in range(sections)])]
    pallas_call x15 -> x16, Pallas kernels: 12.9 us -> 13 us  [call(): pl.pallas_call(kernel, in_specs=specs, out_specs=vmem_specs(len(outs)), o...]
  transfers between devices with their start and end apart: 38 -> 39, of which waited for: 20 -> 22; matrix products, arithmetic and copies ran while one was open for 0% -> 0% of each run, Pallas kernels for 4% -> 4%
where the time goes in v16:
time: 108 us; the launch traced here: 107 us
  starting transfers between devices  48.8 us (45%)
  waiting for transfers between devices  40.7 us (38%)
  Pallas kernels  15.3 us (14%)
  local copies, waits for them, and re-layouts  1.86 us (2%)
    ppermute x24, starting transfers between devices, shifted(): return lax.ppermute(value, 'z', [(i, i ^ shift) for i in range(groups)])  37.4 us
    ppermute x24, waiting for transfers between devices, shifted(): return lax.ppermute(value, 'z', [(i, i ^ shift) for i in range(groups)])  25.5 us
    pallas_call x16, Pallas kernels, call(): pl.pallas_call(kernel, in_specs=specs, out_specs=vmem_specs(len(outs)), o...  13 us
    ppermute x7, waiting for transfers between devices, across(): lax.ppermute(value, 'pipe', [(i, i ^ distance) for i in range(sections)])  12.3 us
    ppermute x7, starting transfers between devices, across(): lax.ppermute(value, 'pipe', [(i, i ^ distance) for i in range(sections)])  9.7 us
    ppermute x8, waiting for transfers between devices, swapped(): return lax.ppermute(value, 'core', [(i, 1 - i) for i in range(sides)])  2.93 us
    pallas_call x1, Pallas kernels, pack(): pl.pallas_call(functools.partial(pack_kernel, groups, micro_local), in_sp...  2.28 us
  transfers between devices with their start and end apart: 39, of which 22 were waited for; matrix products, arithmetic and copies ran while one was open for 0% of the time, Pallas kernels for 4%

profile of v16, /device:TPU:0, one launch (start us, length us, event | category | flops | bytes accessed | tf_op | source)
XLA Modules:
  0.0 107.4 jit_solution(11579747032098975566)
XLA Ops:
  0.6 2.3 %pack.1 = (bf16[32,2176]{1,0:T(8,128)(2,1)}, bf16[32,2176]{1,0:T(8,128)(2,1)}, bf16[32,2176]{1,0:T(8,128)(2,1)}, bf16[32,2176]{1,0:T(8,128)(2,1)}, bf16[1040,128]{1,0:T(8,128)(2,1)}) custom-call(bf16[2,2,32,4096]{3,2,1,0:T(8,128)(2,1)} %refs_0_.1, bf16[2,2,32,4096]{3,2,1,0:T(8,128)(2,1)} %refs_1_.1, s32[2,2,4]{2,1,0:T(2,128)} %refs_2_.1, s32[2,2]{1,0:T(2,128)} %refs_3_.1, ...), custom_call_target="tpu_custom_call" | custom-call | tf_op jit(solution)/shard_map/pack/pallas_call | solution.py:124
  2.9 3.0 %collective-permute-start = (bf16[1040,128]{1,0:T(8,128)(2,1)}, bf16[1040,128]{1,0:T(8,128)(2,1)S(1)}, u32[]{:S(2)}, u32[]{:S(2)}) collective-permute-start(bf16[1040,128]{1,0:T(8,128)(2,1)} %get-tuple-element.84.packed), channel_id=1, source_target_pairs={{0,8},{8,0},{16,24},{24,16},{1,9},{9,1},{17,25},{25,17},{2,10},{10... | collective-permute-start | bytes 798728 | tf_op jit(solution)/shard_map/ppermute | solution.py:617
  7.5 4.1 %collective-permute-start.1 = (bf16[32,2176]{1,0:T(8,128)(2,1)}, bf16[32,2176]{1,0:T(8,128)(2,1)S(1)}, u32[]{:S(2)}, u32[]{:S(2)}) collective-permute-start(bf16[32,2176]{1,0:T(8,128)(2,1)} %get-tuple-element.86), channel_id=1, source_target_pairs={{0,6},{2,4},{4,2},{6,0},{1,7},{3,5},{5,3},{7,1},{8,14},{10,12},{12... | collective-permute-start | bytes 417800 | tf_op jit(solution)/shard_map/ppermute | solution.py:614
  11.5 1.8 %collective-permute-done.early = bf16[1040,128]{1,0:T(8,128)(2,1)S(1)} collective-permute-done((bf16[1040,128]{1,0:T(8,128)(2,1)}, bf16[1040,128]{1,0:T(8,128)(2,1)S(1)}, u32[]{:S(2)}, u32[]{:S(2)}) %collective-permute-start) | collective-permute-done | bytes 266272 | tf_op jit(solution)/shard_map/ppermute | solution.py:617
  13.4 2.1 %collective-permute-start.3 = (bf16[32,2176]{1,0:T(8,128)(2,1)}, bf16[32,2176]{1,0:T(8,128)(2,1)S(1)}, u32[]{:S(2)}, u32[]{:S(2)}) collective-permute-start(bf16[32,2176]{1,0:T(8,128)(2,1)} %get-tuple-element.88), channel_id=1, source_target_pairs={{0,2},{2,0},{4,6},{6,4},{1,3},{3,1},{5,7},{7,5},{8,10},{10,8},{12,... | collective-permute-start | bytes 417800 | tf_op jit(solution)/shard_map/ppermute | solution.py:614
  17.4 5.3 %collective-permute-done.2.refs_2_ = bf16[32,2176]{1,0:T(8,128)(2,1)S(1)} collective-permute-done((bf16[32,2176]{1,0:T(8,128)(2,1)}, bf16[32,2176]{1,0:T(8,128)(2,1)S(1)}, u32[]{:S(2)}, u32[]{:S(2)}) %collective-permute-start.2) | collective-permute-done | bytes 139296 | tf_op jit(solution)/shard_map/ppermute | solution.py:614
  25.4 1.6 %forward_first.1 = (bf16[1,8,128,128]{3,2,1,0:T(8,128)(2,1)S(1)}, bf16[128,1024]{1,0:T(8,128)(2,1)S(1)}, bf16[400,128]{1,0:T(8,128)(2,1)S(1)}, bf16[4,2,1040,128]{3,2,1,0:T(8,128)(2,1)S(1)}) custom-call(bf16[1040,128]{1,0:T(8,128)(2,1)S(1)} %get-tuple-element.91.refs_0_, bf16[1040,128]{1,0:T(8,128)(2,1)S(1)} %get-tuple-element.92.refs_1_, ...), custom_call_target="tpu_custom_call" | custom-call | tf_op jit(solution)/shard_map/forward_first/pallas_call | solution.py:635
  27.0 2.5 %collective-permute-start.12 = (bf16[400,128]{1,0:T(8,128)(2,1)S(1)}, bf16[400,128]{1,0:T(8,128)(2,1)S(1)}, u32[]{:S(2)}, u32[]{:S(2)}) collective-permute-start(bf16[400,128]{1,0:T(8,128)(2,1)S(1)} %get-tuple-element.102.refs_0_.refs_4_), channel_id=1, source_target_pairs={{0,6},{2,4},{4,2},{6,0},{1,7},{3,5},{5,3},{7,1},{8,14},{10,12},{12... | collective-permute-start | bytes 307208 | tf_op jit(solution)/shard_map/ppermute | solution.py:614
  29.5 1.9 %collective-permute-start.10 = (bf16[400,128]{1,0:T(8,128)(2,1)S(1)}, bf16[400,128]{1,0:T(8,128)(2,1)S(1)}, u32[]{:S(2)}, u32[]{:S(2)}) collective-permute-start(bf16[400,128]{1,0:T(8,128)(2,1)S(1)} %get-tuple-element.102.refs_0_.refs_4_), channel_id=1, source_target_pairs={{0,2},{2,0},{4,6},{6,4},{1,3},{3,1},{5,7},{7,5},{8,10},{10,8},{12,... | collective-permute-start | bytes 307208 | tf_op jit(solution)/shard_map/ppermute | solution.py:614
  31.4 3.2 %collective-permute-done.12.refs_3_.refs_7_ = bf16[400,128]{1,0:T(8,128)(2,1)S(1)} collective-permute-done((bf16[400,128]{1,0:T(8,128)(2,1)S(1)}, bf16[400,128]{1,0:T(8,128)(2,1)S(1)}, u32[]{:S(2)}, u32[]{:S(2)}) %collective-permute-start.12) | collective-permute-done | bytes 102432 | tf_op jit(solution)/shard_map/ppermute | solution.py:614
  34.7 3.5 %collective-permute-done.11.refs_2_.refs_6_ = bf16[400,128]{1,0:T(8,128)(2,1)S(1)} collective-permute-done((bf16[400,128]{1,0:T(8,128)(2,1)S(1)}, bf16[400,128]{1,0:T(8,128)(2,1)S(1)}, u32[]{:S(2)}, u32[]{:S(2)}) %collective-permute-start.11) | collective-permute-done | bytes 102432 | tf_op jit(solution)/shard_map/ppermute | solution.py:614
  39.5 2.5 %collective-permute-start.15 = (bf16[256,128]{1,0:T(8,128)(2,1)S(1)}, bf16[256,128]{1,0:T(8,128)(2,1)S(1)}, u32[]{:S(2)}, u32[]{:S(2)}) collective-permute-start(bf16[256,128]{1,0:T(8,128)(2,1)S(1)} %get-tuple-element.104.refs_0_), channel_id=1, source_target_pairs={{0,6},{2,4},{4,2},{6,0},{1,7},{3,5},{5,3},{7,1},{8,14},{10,12},{12... | collective-permute-start | bytes 196616 | tf_op jit(solution)/shard_map/ppermute | solution.py:614
  42.0 1.9 %collective-permute-start.13 = (bf16[256,128]{1,0:T(8,128)(2,1)S(1)}, bf16[256,128]{1,0:T(8,128)(2,1)S(1)}, u32[]{:S(2)}, u32[]{:S(2)}) collective-permute-start(bf16[256,128]{1,0:T(8,128)(2,1)S(1)} %get-tuple-element.104.refs_0_), channel_id=1, source_target_pairs={{0,2},{2,0},{4,6},{6,4},{1,3},{3,1},{5,7},{7,5},{8,10},{10,8},{12,... | collective-permute-start | bytes 196616 | tf_op jit(solution)/shard_map/ppermute | solution.py:614
  44.3 2.5 %collective-permute-start.21 = (bf16[256,128]{1,0:T(8,128)(2,1)S(1)}, bf16[256,128]{1,0:T(8,128)(2,1)S(1)}, u32[]{:S(2)}, u32[]{:S(2)}) collective-permute-start(bf16[256,128]{1,0:T(8,128)(2,1)S(1)} %side.1.refs_4_), channel_id=1, source_target_pairs={{0,6},{2,4},{4,2},{6,0},{1,7},{3,5},{5,3},{7,1},{8,14},{10,12},{12... | collective-permute-start | bytes 196616 | tf_op jit(solution)/shard_map/ppermute | solution.py:614
  46.8 1.9 %collective-permute-start.19 = (bf16[256,128]{1,0:T(8,128)(2,1)S(1)}, bf16[256,128]{1,0:T(8,128)(2,1)S(1)}, u32[]{:S(2)}, u32[]{:S(2)}) collective-permute-start(bf16[256,128]{1,0:T(8,128)(2,1)S(1)} %side.1.refs_4_), channel_id=1, source_target_pairs={{0,2},{2,0},{4,6},{6,4},{1,3},{3,1},{5,7},{7,5},{8,10},{10,8},{12,... | collective-permute-start | bytes 196616 | tf_op jit(solution)/shard_map/ppermute | solution.py:614
  50.1 3.5 %collective-permute-start.18 = (bf16[256,128]{1,0:T(8,128)(2,1)S(1)}, bf16[256,128]{1,0:T(8,128)(2,1)S(1)}, u32[]{:S(2)}, u32[]{:S(2)}) collective-permute-start(bf16[256,128]{1,0:T(8,128)(2,1)S(1)} %get-tuple-element.107.refs_0_), channel_id=1, source_target_pairs={{0,6},{2,4},{4,2},{6,0},{1,7},{3,5},{5,3},{7,1},{8,14},{10,12},{12... | collective-permute-start | bytes 196616 | tf_op jit(solution)/shard_map/ppermute | solution.py:614
  54.6 2.0 %collective-permute-done.18.refs_3_ = bf16[256,128]{1,0:T(8,128)(2,1)S(1)} collective-permute-done((bf16[256,128]{1,0:T(8,128)(2,1)S(1)}, bf16[256,128]{1,0:T(8,128)(2,1)S(1)}, u32[]{:S(2)}, u32[]{:S(2)}) %collective-permute-start.18) | collective-permute-done | bytes 65568 | tf_op jit(solution)/shard_map/ppermute | solution.py:614
  56.6 2.9 %collective-permute-done.17.refs_2_ = bf16[256,128]{1,0:T(8,128)(2,1)S(1)} collective-permute-done((bf16[256,128]{1,0:T(8,128)(2,1)S(1)}, bf16[256,128]{1,0:T(8,128)(2,1)S(1)}, u32[]{:S(2)}, u32[]{:S(2)}) %collective-permute-start.17) | collective-permute-done | bytes 65568 | tf_op jit(solution)/shard_map/ppermute | solution.py:614
  59.4 2.1 %turn.1 = (bf16[128,1024]{1,0:T(8,128)(2,1)S(1)}, f32[128,128]{1,0:T(8,128)S(1)}, bf16[128,128]{1,0:T(8,128)(2,1)S(1)}, f32[128,128]{1,0:T(8,128)S(1)}, bf16[128...) custom-call(bf16[256,128]{1,0:T(8,128)(2,1)S(1)} %get-tuple-element., ...), custom_call_target="tpu_custom_call" | custom-call | tf_op jit(solution)/shard_map/turn/pallas_call | solution.py:635
  61.5 2.5 %collective-permute-start.24 = (bf16[272,128]{1,0:T(8,128)(2,1)S(1)}, bf16[272,128]{1,0:T(8,128)(2,1)S(1)}, u32[]{:S(2)}, u32[]{:S(2)}) collective-permute-start(bf16[272,128]{1,0:T(8,128)(2,1)S(1)} %get-tuple-element.111.refs_0_), channel_id=1, source_target_pairs={{0,6},{2,4},{4,2},{6,0},{1,7},{3,5},{5,3},{7,1},{8,14},{10,12},{12... | collective-permute-start | bytes 208904 | tf_op jit(solution)/shard_map/ppermute | solution.py:614
  64.0 1.9 %collective-permute-start.22 = (bf16[272,128]{1,0:T(8,128)(2,1)S(1)}, bf16[272,128]{1,0:T(8,128)(2,1)S(1)}, u32[]{:S(2)}, u32[]{:S(2)}) collective-permute-start(bf16[272,128]{1,0:T(8,128)(2,1)S(1)} %get-tuple-element.111.refs_0_), channel_id=1, source_target_pairs={{0,2},{2,0},{4,6},{6,4},{1,3},{3,1},{5,7},{7,5},{8,10},{10,8},{12,... | collective-permute-start | bytes 208904 | tf_op jit(solution)/shard_map/ppermute | solution.py:614
  66.0 2.4 %collective-permute-done.24.refs_3_ = bf16[272,128]{1,0:T(8,128)(2,1)S(1)} collective-permute-done((bf16[272,128]{1,0:T(8,128)(2,1)S(1)}, bf16[272,128]{1,0:T(8,128)(2,1)S(1)}, u32[]{:S(2)}, u32[]{:S(2)}) %collective-permute-start.24) | collective-permute-done | bytes 69664 | tf_op jit(solution)/shard_map/ppermute | solution.py:614
  68.3 2.1 %collective-permute-done.23.refs_2_ = bf16[272,128]{1,0:T(8,128)(2,1)S(1)} collective-permute-done((bf16[272,128]{1,0:T(8,128)(2,1)S(1)}, bf16[272,128]{1,0:T(8,128)(2,1)S(1)}, u32[]{:S(2)}, u32[]{:S(2)}) %collective-permute-start.23) | collective-permute-done | bytes 69664 | tf_op jit(solution)/shard_map/ppermute | solution.py:614
  71.7 2.5 %collective-permute-start.27 = (bf16[144,128]{1,0:T(8,128)(2,1)S(1)}, bf16[144,128]{1,0:T(8,128)(2,1)S(1)}, u32[]{:S(2)}, u32[]{:S(2)}) collective-permute-start(bf16[144,128]{1,0:T(8,128)(2,1)S(1)} %get-tuple-element.130.refs_0_), channel_id=1, source_target_pairs={{0,6},{2,4},{4,2},{6,0},{1,7},{3,5},{5,3},{7,1},{8,14},{10,12},{12... | collective-permute-start | bytes 110600 | tf_op jit(solution)/shard_map/ppermute | solution.py:614
  74.2 1.9 %collective-permute-start.25 = (bf16[144,128]{1,0:T(8,128)(2,1)S(1)}, bf16[144,128]{1,0:T(8,128)(2,1)S(1)}, u32[]{:S(2)}, u32[]{:S(2)}) collective-permute-start(bf16[144,128]{1,0:T(8,128)(2,1)S(1)} %get-tuple-element.130.refs_0_), channel_id=1, source_target_pairs={{0,2},{2,0},{4,6},{6,4},{1,3},{3,1},{5,7},{7,5},{8,10},{10,8},{12,... | collective-permute-start | bytes 110600 | tf_op jit(solution)/shard_map/ppermute | solution.py:614
  77.6 1.5 %collective-permute-done.26.refs_2_ = bf16[144,128]{1,0:T(8,128)(2,1)S(1)} collective-permute-done((bf16[144,128]{1,0:T(8,128)(2,1)S(1)}, bf16[144,128]{1,0:T(8,128)(2,1)S(1)}, u32[]{:S(2)}, u32[]{:S(2)}) %collective-permute-start.26) | collective-permute-done | bytes 36896 | tf_op jit(solution)/shard_map/ppermute | solution.py:614
  80.4 2.0 %collective-permute-start.30 = (bf16[144,128]{1,0:T(8,128)(2,1)S(1)}, bf16[144,128]{1,0:T(8,128)(2,1)S(1)}, u32[]{:S(2)}, u32[]{:S(2)}) collective-permute-start(bf16[144,128]{1,0:T(8,128)(2,1)S(1)} %get-tuple-element.137.refs_0_), channel_id=1, source_target_pairs={{0,6},{2,4},{4,2},{6,0},{1,7},{3,5},{5,3},{7,1},{8,14},{10,12},{12... | collective-permute-start | bytes 110600 | tf_op jit(solution)/shard_map/ppermute | solution.py:614
  82.9 1.9 %collective-permute-start.28 = (bf16[144,128]{1,0:T(8,128)(2,1)S(1)}, bf16[144,128]{1,0:T(8,128)(2,1)S(1)}, u32[]{:S(2)}, u32[]{:S(2)}) collective-permute-start(bf16[144,128]{1,0:T(8,128)(2,1)S(1)} %get-tuple-element.137.refs_0_), channel_id=1, source_target_pairs={{0,2},{2,0},{4,6},{6,4},{1,3},{3,1},{5,7},{7,5},{8,10},{10,8},{12,... | collective-permute-start | bytes 110600 | tf_op jit(solution)/shard_map/ppermute | solution.py:614
  89.1 1.5 %collective-permute-done.31.refs_4_ = bf16[272,512]{1,0:T(8,128)(2,1)S(1)} collective-permute-done((bf16[272,512]{1,0:T(8,128)(2,1)S(1)}, bf16[272,512]{1,0:T(8,128)(2,1)S(1)}, u32[]{:S(2)}, u32[]{:S(2)}) %collective-permute-start.31) | collective-permute-done | bytes 278560 | tf_op jit(solution)/shard_map/ppermute | solution.py:620
  90.9 1.6 %collective-permute-start.35 = (bf16[544,256]{1,0:T(8,128)(2,1)S(1)}, bf16[544,256]{1,0:T(8,128)(2,1)S(1)}, u32[]{:S(2)}, u32[]{:S(2)}) collective-permute-start(bf16[544,256]{1,0:T(8,128)(2,1)S(1)} %get-tuple-element.157), channel_id=1, source_target_pairs={{0,8},{8,0},{16,24},{24,16},{1,9},{9,1},{17,25},{25,17},{2,10},{10... | collective-permute-start | bytes 835592 | tf_op jit(solution)/shard_map/ppermute | solution.py:617
  93.9 5.7 %collective-permute-done.35.from_x = bf16[544,256]{1,0:T(8,128)(2,1)S(1)} collective-permute-done((bf16[544,256]{1,0:T(8,128)(2,1)S(1)}, bf16[544,256]{1,0:T(8,128)(2,1)S(1)}, u32[]{:S(2)}, u32[]{:S(2)}) %collective-permute-start.35) | collective-permute-done | bytes 278560 | tf_op jit(solution)/shard_map/ppermute | solution.py:617
  103.0 3.0 %collective-permute-done.37.last_x = bf16[272,256]{1,0:T(8,128)(2,1)S(1)} collective-permute-done((bf16[272,256]{1,0:T(8,128)(2,1)S(1)}, bf16[272,256]{1,0:T(8,128)(2,1)S(1)}, u32[]{:S(2)}, u32[]{:S(2)}) %collective-permute-start.37) | collective-permute-done | bytes 139296 | tf_op jit(solution)/shard_map/ppermute | solution.py:617
  (67 shorter events, 25.4 us)
Async XLA Ops:
  2.9 10.4 %collective-permute-start = (bf16[1040,128]{1,0:T(8,128)(2,1)}, bf16[1040,128]{1,0:T(8,128)(2,1)S(1)}, u32[]{:S(2)}, u32[]{:S(2)}) collective-permute-start(bf16[1040,128]{1,0:T(8,128)(2,1)} %get-tuple-element.84.packed), channel_id=1, source_target_pairs={{0,8},{8,0},{16,24},{24,16},{1,9},{9,1},{17,25},{25,17},{2,10},{10... | collective-permute-start | bytes 798728 | tf_op jit(solution)/shard_map/ppermute | solution.py:617
  5.9 16.8 %collective-permute-start.5 = (bf16[1040,128]{1,0:T(8,128)(2,1)}, bf16[1040,128]{1,0:T(8,128)(2,1)S(1)}, u32[]{:S(2)}, u32[]{:S(2)}) collective-permute-start(bf16[1040,128]{1,0:T(8,128)(2,1)} %get-tuple-element.84.packed), channel_id=1, source_target_pairs={{0,24},{8,16},{16,8},{24,0},{1,25},{9,17},{17,9},{25,1},{2,26},{10... | collective-permute-start | bytes 798728 | tf_op jit(solution)/shard_map/ppermute | solution.py:617
  7.4 15.3 %collective-permute-start.4 = (bf16[1040,128]{1,0:T(8,128)(2,1)}, bf16[1040,128]{1,0:T(8,128)(2,1)S(1)}, u32[]{:S(2)}, u32[]{:S(2)}) collective-permute-start(bf16[1040,128]{1,0:T(8,128)(2,1)} %get-tuple-element.84.packed), channel_id=1, source_target_pairs={{0,16},{8,24},{16,0},{24,8},{1,17},{9,25},{17,1},{25,9},{2,18},{10... | collective-permute-start | bytes 798728 | tf_op jit(solution)/shard_map/ppermute | solution.py:617
  7.5 9.9 %collective-permute-start.1 = (bf16[32,2176]{1,0:T(8,128)(2,1)}, bf16[32,2176]{1,0:T(8,128)(2,1)S(1)}, u32[]{:S(2)}, u32[]{:S(2)}) collective-permute-start(bf16[32,2176]{1,0:T(8,128)(2,1)} %get-tuple-element.86), channel_id=1, source_target_pairs={{0,6},{2,4},{4,2},{6,0},{1,7},{3,5},{5,3},{7,1},{8,14},{10,12},{12... | collective-permute-start | bytes 417800 | tf_op jit(solution)/shard_map/ppermute | solution.py:614
  11.5 11.1 %collective-permute-start.2 = (bf16[32,2176]{1,0:T(8,128)(2,1)}, bf16[32,2176]{1,0:T(8,128)(2,1)S(1)}, u32[]{:S(2)}, u32[]{:S(2)}) collective-permute-start(bf16[32,2176]{1,0:T(8,128)(2,1)} %get-tuple-element.87), channel_id=1, source_target_pairs={{0,4},{2,6},{4,0},{6,2},{1,5},{3,7},{5,1},{7,3},{8,12},{10,14},{12... | collective-permute-start | bytes 417800 | tf_op jit(solution)/shard_map/ppermute | solution.py:614
  13.4 9.3 %collective-permute-start.3 = (bf16[32,2176]{1,0:T(8,128)(2,1)}, bf16[32,2176]{1,0:T(8,128)(2,1)S(1)}, u32[]{:S(2)}, u32[]{:S(2)}) collective-permute-start(bf16[32,2176]{1,0:T(8,128)(2,1)} %get-tuple-element.88), channel_id=1, source_target_pairs={{0,2},{2,0},{4,6},{6,4},{1,3},{3,1},{5,7},{7,5},{8,10},{10,8},{12,... | collective-permute-start | bytes 417800 | tf_op jit(solution)/shard_map/ppermute | solution.py:614
  27.0 7.7 %collective-permute-start.12 = (bf16[400,128]{1,0:T(8,128)(2,1)S(1)}, bf16[400,128]{1,0:T(8,128)(2,1)S(1)}, u32[]{:S(2)}, u32[]{:S(2)}) collective-permute-start(bf16[400,128]{1,0:T(8,128)(2,1)S(1)} %get-tuple-element.102.refs_0_.refs_4_), channel_id=1, source_target_pairs={{0,6},{2,4},{4,2},{6,0},{1,7},{3,5},{5,3},{7,1},{8,14},{10,12},{12... | collective-permute-start | bytes 307208 | tf_op jit(solution)/shard_map/ppermute | solution.py:614
  29.5 8.6 %collective-permute-start.11 = (bf16[400,128]{1,0:T(8,128)(2,1)S(1)}, bf16[400,128]{1,0:T(8,128)(2,1)S(1)}, u32[]{:S(2)}, u32[]{:S(2)}) collective-permute-start(bf16[400,128]{1,0:T(8,128)(2,1)S(1)} %get-tuple-element.102.refs_0_.refs_4_), channel_id=1, source_target_pairs={{0,4},{2,6},{4,0},{6,2},{1,5},{3,7},{5,1},{7,3},{8,12},{10,14},{12... | collective-permute-start | bytes 307208 | tf_op jit(solution)/shard_map/ppermute | solution.py:614
  29.5 8.6 %collective-permute-start.10 = (bf16[400,128]{1,0:T(8,128)(2,1)S(1)}, bf16[400,128]{1,0:T(8,128)(2,1)S(1)}, u32[]{:S(2)}, u32[]{:S(2)}) collective-permute-start(bf16[400,128]{1,0:T(8,128)(2,1)S(1)} %get-tuple-element.102.refs_0_.refs_4_), channel_id=1, source_target_pairs={{0,2},{2,0},{4,6},{6,4},{1,3},{3,1},{5,7},{7,5},{8,10},{10,8},{12,... | collective-permute-start | bytes 307208 | tf_op jit(solution)/shard_map/ppermute | solution.py:614
  39.5 7.3 %collective-permute-start.15 = (bf16[256,128]{1,0:T(8,128)(2,1)S(1)}, bf16[256,128]{1,0:T(8,128)(2,1)S(1)}, u32[]{:S(2)}, u32[]{:S(2)}) collective-permute-start(bf16[256,128]{1,0:T(8,128)(2,1)S(1)} %get-tuple-element.104.refs_0_), channel_id=1, source_target_pairs={{0,6},{2,4},{4,2},{6,0},{1,7},{3,5},{5,3},{7,1},{8,14},{10,12},{12... | collective-permute-start | bytes 196616 | tf_op jit(solution)/shard_map/ppermute | solution.py:614
  42.0 6.7 %collective-permute-start.14 = (bf16[256,128]{1,0:T(8,128)(2,1)S(1)}, bf16[256,128]{1,0:T(8,128)(2,1)S(1)}, u32[]{:S(2)}, u32[]{:S(2)}) collective-permute-start(bf16[256,128]{1,0:T(8,128)(2,1)S(1)} %get-tuple-element.104.refs_0_), channel_id=1, source_target_pairs={{0,4},{2,6},{4,0},{6,2},{1,5},{3,7},{5,1},{7,3},{8,12},{10,14},{12... | collective-permute-start | bytes 196616 | tf_op jit(solution)/shard_map/ppermute | solution.py:614
  42.0 6.7 %collective-permute-start.13 = (bf16[256,128]{1,0:T(8,128)(2,1)S(1)}, bf16[256,128]{1,0:T(8,128)(2,1)S(1)}, u32[]{:S(2)}, u32[]{:S(2)}) collective-permute-start(bf16[256,128]{1,0:T(8,128)(2,1)S(1)} %get-tuple-element.104.refs_0_), channel_id=1, source_target_pairs={{0,2},{2,0},{4,6},{6,4},{1,3},{3,1},{5,7},{7,5},{8,10},{10,8},{12,... | collective-permute-start | bytes 196616 | tf_op jit(solution)/shard_map/ppermute | solution.py:614
  44.3 9.3 %collective-permute-start.21 = (bf16[256,128]{1,0:T(8,128)(2,1)S(1)}, bf16[256,128]{1,0:T(8,128)(2,1)S(1)}, u32[]{:S(2)}, u32[]{:S(2)}) collective-permute-start(bf16[256,128]{1,0:T(8,128)(2,1)S(1)} %side.1.refs_4_), channel_id=1, source_target_pairs={{0,6},{2,4},{4,2},{6,0},{1,7},{3,5},{5,3},{7,1},{8,14},{10,12},{12... | collective-permute-start | bytes 196616 | tf_op jit(solution)/shard_map/ppermute | solution.py:614
  46.8 7.8 %collective-permute-start.20 = (bf16[256,128]{1,0:T(8,128)(2,1)S(1)}, bf16[256,128]{1,0:T(8,128)(2,1)S(1)}, u32[]{:S(2)}, u32[]{:S(2)}) collective-permute-start(bf16[256,128]{1,0:T(8,128)(2,1)S(1)} %side.1.refs_4_), channel_id=1, source_target_pairs={{0,4},{2,6},{4,0},{6,2},{1,5},{3,7},{5,1},{7,3},{8,12},{10,14},{12... | collective-permute-start | bytes 196616 | tf_op jit(solution)/shard_map/ppermute | solution.py:614
  46.8 7.8 %collective-permute-start.19 = (bf16[256,128]{1,0:T(8,128)(2,1)S(1)}, bf16[256,128]{1,0:T(8,128)(2,1)S(1)}, u32[]{:S(2)}, u32[]{:S(2)}) collective-permute-start(bf16[256,128]{1,0:T(8,128)(2,1)S(1)} %side.1.refs_4_), channel_id=1, source_target_pairs={{0,2},{2,0},{4,6},{6,4},{1,3},{3,1},{5,7},{7,5},{8,10},{10,8},{12,... | collective-permute-start | bytes 196616 | tf_op jit(solution)/shard_map/ppermute | solution.py:614
  50.1 6.4 %collective-permute-start.18 = (bf16[256,128]{1,0:T(8,128)(2,1)S(1)}, bf16[256,128]{1,0:T(8,128)(2,1)S(1)}, u32[]{:S(2)}, u32[]{:S(2)}) collective-permute-start(bf16[256,128]{1,0:T(8,128)(2,1)S(1)} %get-tuple-element.107.refs_0_), channel_id=1, source_target_pairs={{0,6},{2,4},{4,2},{6,0},{1,7},{3,5},{5,3},{7,1},{8,14},{10,12},{12... | collective-permute-start | bytes 196616 | tf_op jit(solution)/shard_map/ppermute | solution.py:614
  53.6 5.9 %collective-permute-start.17 = (bf16[256,128]{1,0:T(8,128)(2,1)S(1)}, bf16[256,128]{1,0:T(8,128)(2,1)S(1)}, u32[]{:S(2)}, u32[]{:S(2)}) collective-permute-start(bf16[256,128]{1,0:T(8,128)(2,1)S(1)} %get-tuple-element.107.refs_0_), channel_id=1, source_target_pairs={{0,4},{2,6},{4,0},{6,2},{1,5},{3,7},{5,1},{7,3},{8,12},{10,14},{12... | collective-permute-start | bytes 196616 | tf_op jit(solution)/shard_map/ppermute | solution.py:614
  53.6 5.9 %collective-permute-start.16 = (bf16[256,128]{1,0:T(8,128)(2,1)S(1)}, bf16[256,128]{1,0:T(8,128)(2,1)S(1)}, u32[]{:S(2)}, u32[]{:S(2)}) collective-permute-start(bf16[256,128]{1,0:T(8,128)(2,1)S(1)} %get-tuple-element.107.refs_0_), channel_id=1, source_target_pairs={{0,2},{2,0},{4,6},{6,4},{1,3},{3,1},{5,7},{7,5},{8,10},{10,8},{12,... | collective-permute-start | bytes 196616 | tf_op jit(solution)/shard_map/ppermute | solution.py:614
  61.5 6.8 %collective-permute-start.24 = (bf16[272,128]{1,0:T(8,128)(2,1)S(1)}, bf16[272,128]{1,0:T(8,128)(2,1)S(1)}, u32[]{:S(2)}, u32[]{:S(2)}) collective-permute-start(bf16[272,128]{1,0:T(8,128)(2,1)S(1)} %get-tuple-element.111.refs_0_), channel_id=1, source_target_pairs={{0,6},{2,4},{4,2},{6,0},{1,7},{3,5},{5,3},{7,1},{8,14},{10,12},{12... | collective-permute-start | bytes 208904 | tf_op jit(solution)/shard_map/ppermute | solution.py:614
  64.0 6.4 %collective-permute-start.23 = (bf16[272,128]{1,0:T(8,128)(2,1)S(1)}, bf16[272,128]{1,0:T(8,128)(2,1)S(1)}, u32[]{:S(2)}, u32[]{:S(2)}) collective-permute-start(bf16[272,128]{1,0:T(8,128)(2,1)S(1)} %get-tuple-element.111.refs_0_), channel_id=1, source_target_pairs={{0,4},{2,6},{4,0},{6,2},{1,5},{3,7},{5,1},{7,3},{8,12},{10,14},{12... | collective-permute-start | bytes 208904 | tf_op jit(solution)/shard_map/ppermute | solution.py:614
  64.0 6.4 %collective-permute-start.22 = (bf16[272,128]{1,0:T(8,128)(2,1)S(1)}, bf16[272,128]{1,0:T(8,128)(2,1)S(1)}, u32[]{:S(2)}, u32[]{:S(2)}) collective-permute-start(bf16[272,128]{1,0:T(8,128)(2,1)S(1)} %get-tuple-element.111.refs_0_), channel_id=1, source_target_pairs={{0,2},{2,0},{4,6},{6,4},{1,3},{3,1},{5,7},{7,5},{8,10},{10,8},{12,... | collective-permute-start | bytes 208904 | tf_op jit(solution)/shard_map/ppermute | solution.py:614
  71.7 5.8 %collective-permute-start.27 = (bf16[144,128]{1,0:T(8,128)(2,1)S(1)}, bf16[144,128]{1,0:T(8,128)(2,1)S(1)}, u32[]{:S(2)}, u32[]{:S(2)}) collective-permute-start(bf16[144,128]{1,0:T(8,128)(2,1)S(1)} %get-tuple-element.130.refs_0_), channel_id=1, source_target_pairs={{0,6},{2,4},{4,2},{6,0},{1,7},{3,5},{5,3},{7,1},{8,14},{10,12},{12... | collective-permute-start | bytes 110600 | tf_op jit(solution)/shard_map/ppermute | solution.py:614
  74.2 4.9 %collective-permute-start.26 = (bf16[144,128]{1,0:T(8,128)(2,1)S(1)}, bf16[144,128]{1,0:T(8,128)(2,1)S(1)}, u32[]{:S(2)}, u32[]{:S(2)}) collective-permute-start(bf16[144,128]{1,0:T(8,128)(2,1)S(1)} %get-tuple-element.130.refs_0_), channel_id=1, source_target_pairs={{0,4},{2,6},{4,0},{6,2},{1,5},{3,7},{5,1},{7,3},{8,12},{10,14},{12... | collective-permute-start | bytes 110600 | tf_op jit(solution)/shard_map/ppermute | solution.py:614
  74.2 4.9 %collective-permute-start.25 = (bf16[144,128]{1,0:T(8,128)(2,1)S(1)}, bf16[144,128]{1,0:T(8,128)(2,1)S(1)}, u32[]{:S(2)}, u32[]{:S(2)}) collective-permute-start(bf16[144,128]{1,0:T(8,128)(2,1)S(1)} %get-tuple-element.130.refs_0_), channel_id=1, source_target_pairs={{0,2},{2,0},{4,6},{6,4},{1,3},{3,1},{5,7},{7,5},{8,10},{10,8},{12,... | collective-permute-start | bytes 110600 | tf_op jit(solution)/shard_map/ppermute | solution.py:614
  80.4 5.9 %collective-permute-start.30 = (bf16[144,128]{1,0:T(8,128)(2,1)S(1)}, bf16[144,128]{1,0:T(8,128)(2,1)S(1)}, u32[]{:S(2)}, u32[]{:S(2)}) collective-permute-start(bf16[144,128]{1,0:T(8,128)(2,1)S(1)} %get-tuple-element.137.refs_0_), channel_id=1, source_target_pairs={{0,6},{2,4},{4,2},{6,0},{1,7},{3,5},{5,3},{7,1},{8,14},{10,12},{12... | collective-permute-start | bytes 110600 | tf_op jit(solution)/shard_map/ppermute | solution.py:614
  82.4 5.3 %collective-permute-start.29 = (bf16[144,128]{1,0:T(8,128)(2,1)S(1)}, bf16[144,128]{1,0:T(8,128)(2,1)S(1)}, u32[]{:S(2)}, u32[]{:S(2)}) collective-permute-start(bf16[144,128]{1,0:T(8,128)(2,1)S(1)} %get-tuple-element.137.refs_0_), channel_id=1, source_target_pairs={{0,4},{2,6},{4,0},{6,2},{1,5},{3,7},{5,1},{7,3},{8,12},{10,14},{12... | collective-permute-start | bytes 110600 | tf_op jit(solution)/shard_map/ppermute | solution.py:614
  82.9 4.7 %collective-permute-start.28 = (bf16[144,128]{1,0:T(8,128)(2,1)S(1)}, bf16[144,128]{1,0:T(8,128)(2,1)S(1)}, u32[]{:S(2)}, u32[]{:S(2)}) collective-permute-start(bf16[144,128]{1,0:T(8,128)(2,1)S(1)} %get-tuple-element.137.refs_0_), channel_id=1, source_target_pairs={{0,2},{2,0},{4,6},{6,4},{1,3},{3,1},{5,7},{7,5},{8,10},{10,8},{12,... | collective-permute-start | bytes 110600 | tf_op jit(solution)/shard_map/ppermute | solution.py:614
  85.2 3.8 %collective-permute-start.32 = (bf16[272,512]{1,0:T(8,128)(2,1)S(1)}, bf16[272,512]{1,0:T(8,128)(2,1)S(1)}, u32[]{:S(2)}, u32[]{:S(2)}) collective-permute-start(bf16[272,512]{1,0:T(8,128)(2,1)S(1)} %get-tuple-element.153), channel_id=1, source_target_pairs={{0,1},{1,0},{2,3},{3,2},{4,5},{5,4},{6,7},{7,6},{8,9},{9,8},{10,11... | collective-permute-start | bytes 835592 | tf_op jit(solution)/shard_map/ppermute | solution.py:620
  90.9 8.8 %collective-permute-start.35 = (bf16[544,256]{1,0:T(8,128)(2,1)S(1)}, bf16[544,256]{1,0:T(8,128)(2,1)S(1)}, u32[]{:S(2)}, u32[]{:S(2)}) collective-permute-start(bf16[544,256]{1,0:T(8,128)(2,1)S(1)} %get-tuple-element.157), channel_id=1, source_target_pairs={{0,8},{8,0},{16,24},{24,16},{1,9},{9,1},{17,25},{25,17},{2,10},{10... | collective-permute-start | bytes 835592 | tf_op jit(solution)/shard_map/ppermute | solution.py:617
  92.4 8.4 %collective-permute-start.36 = (bf16[544,256]{1,0:T(8,128)(2,1)S(1)}, bf16[544,256]{1,0:T(8,128)(2,1)S(1)}, u32[]{:S(2)}, u32[]{:S(2)}) collective-permute-start(bf16[544,256]{1,0:T(8,128)(2,1)S(1)} %get-tuple-element.158), channel_id=1, source_target_pairs={{0,16},{8,24},{16,0},{24,8},{1,17},{9,25},{17,1},{25,9},{2,18},{10... | collective-permute-start | bytes 835592 | tf_op jit(solution)/shard_map/ppermute | solution.py:617
  100.9 5.1 %collective-permute-start.37 = (bf16[272,256]{1,0:T(8,128)(2,1)S(1)}, bf16[272,256]{1,0:T(8,128)(2,1)S(1)}, u32[]{:S(2)}, u32[]{:S(2)}) collective-permute-start(bf16[272,256]{1,0:T(8,128)(2,1)S(1)} %get-tuple-element.161), channel_id=1, source_target_pairs={{0,8},{8,0},{16,24},{24,16},{1,9},{9,1},{17,25},{25,17},{2,10},{10... | collective-permute-start | bytes 417800 | tf_op jit(solution)/shard_map/ppermute | solution.py:617
  101.5 5.1 %collective-permute-start.38 = (bf16[272,256]{1,0:T(8,128)(2,1)S(1)}, bf16[272,256]{1,0:T(8,128)(2,1)S(1)}, u32[]{:S(2)}, u32[]{:S(2)}) collective-permute-start(bf16[272,256]{1,0:T(8,128)(2,1)S(1)} %get-tuple-element.162), channel_id=1, source_target_pairs={{0,16},{8,24},{16,0},{24,8},{1,17},{9,25},{17,1},{25,9},{2,18},{10... | collective-permute-start | bytes 417800 | tf_op jit(solution)/shard_map/ppermute | solution.py:617
  (9 other events, 17.4 us)

commit v17 on v16

--- a/solution.py
+++ b/solution.py
@@ -620,7 +620,10 @@
         return lax.ppermute(value, "core", [(i, 1 - i) for i in range(sides)])
 
     def exchange(pay):
-        return [pay] + [shifted(pay, place) for place in range(1, groups)]
+        return [pay] + [
+            shifted(pay, place)
+            for place in sorted(range(1, groups), key=lambda place: (place > 2, -place))
+        ]
 
     token_parts, packed = pack(
         tokens, cotangents, starts, counts, layer_gains, first_map, second_map, groups, micro_local

time: 108 us -> 106 us (0.981)
  transfers between devices with their start and end apart: 39 -> 39, of which waited for: 22 -> 26; matrix products, arithmetic and copies ran while one was open for 0% -> 0% of each run, Pallas kernels for 4% -> 4%
where the time goes in v17:
time: 106 us
  starting transfers between devices  48.5 us (46%)
  waiting for transfers between devices  39.8 us (38%)
  Pallas kernels  15.3 us (14%)
  local copies, waits for them, and re-layouts  1.86 us (2%)
    ppermute x24, starting transfers between devices, shifted(): return lax.ppermute(value, 'z', [(i, i ^ shift) for i in range(groups)])  37.1 us
    ppermute x24, waiting for transfers between devices, shifted(): return lax.ppermute(value, 'z', [(i, i ^ shift) for i in range(groups)])  24.6 us
    pallas_call x16, Pallas kernels, call(): pl.pallas_call(kernel, in_specs=specs, out_specs=vmem_specs(len(outs)), o...  13 us
    ppermute x7, waiting for transfers between devices, across(): lax.ppermute(value, 'pipe', [(i, i ^ distance) for i in range(sections)])  12.3 us
    ppermute x7, starting transfers between devices, across(): lax.ppermute(value, 'pipe', [(i, i ^ distance) for i in range(sections)])  9.72 us
    ppermute x8, waiting for transfers between devices, swapped(): return lax.ppermute(value, 'core', [(i, 1 - i) for i in range(sides)])  2.93 us
    pallas_call x1, Pallas kernels, pack(): pl.pallas_call(functools.partial(pack_kernel, groups, micro_local), in_sp...  2.28 us
  transfers between devices with their start and end apart: 39, of which 26 were waited for; matrix products, arithmetic and copies ran while one was open for 0% of the time, Pallas kernels for 4%

profile of v17, /device:TPU:0, one launch (start us, length us, event | category | flops | bytes accessed | tf_op | source)
XLA Modules:
  0.0 106.3 jit_solution(14138426325310429300)
XLA Ops:
  0.6 2.3 %pack.1 = (bf16[32,2176]{1,0:T(8,128)(2,1)}, bf16[32,2176]{1,0:T(8,128)(2,1)}, bf16[32,2176]{1,0:T(8,128)(2,1)}, bf16[32,2176]{1,0:T(8,128)(2,1)}, bf16[1040,128]{1,0:T(8,128)(2,1)}) custom-call(bf16[2,2,32,4096]{3,2,1,0:T(8,128)(2,1)} %refs_0_.1, bf16[2,2,32,4096]{3,2,1,0:T(8,128)(2,1)} %refs_1_.1, s32[2,2,4]{2,1,0:T(2,128)} %refs_2_.1, s32[2,2]{1,0:T(2,128)} %refs_3_.1, ...), custom_call_target="tpu_custom_call" | custom-call | tf_op jit(solution)/shard_map/pack/pallas_call | solution.py:124
  2.9 3.0 %collective-permute-start = (bf16[1040,128]{1,0:T(8,128)(2,1)}, bf16[1040,128]{1,0:T(8,128)(2,1)S(1)}, u32[]{:S(2)}, u32[]{:S(2)}) collective-permute-start(bf16[1040,128]{1,0:T(8,128)(2,1)} %get-tuple-element.84.packed), channel_id=1, source_target_pairs={{0,8},{8,0},{16,24},{24,16},{1,9},{9,1},{17,25},{25,17},{2,10},{10... | collective-permute-start | bytes 798728 | tf_op jit(solution)/shard_map/ppermute | solution.py:617
  5.9 1.5 %collective-permute-start.5 = (bf16[1040,128]{1,0:T(8,128)(2,1)}, bf16[1040,128]{1,0:T(8,128)(2,1)S(1)}, u32[]{:S(2)}, u32[]{:S(2)}) collective-permute-start(bf16[1040,128]{1,0:T(8,128)(2,1)} %get-tuple-element.84.packed), channel_id=1, source_target_pairs={{0,24},{8,16},{16,8},{24,0},{1,25},{9,17},{17,9},{25,1},{2,26},{10... | collective-permute-start | bytes 798728 | tf_op jit(solution)/shard_map/ppermute | solution.py:617
  7.5 4.1 %collective-permute-start.1 = (bf16[32,2176]{1,0:T(8,128)(2,1)}, bf16[32,2176]{1,0:T(8,128)(2,1)S(1)}, u32[]{:S(2)}, u32[]{:S(2)}) collective-permute-start(bf16[32,2176]{1,0:T(8,128)(2,1)} %get-tuple-element.86), channel_id=1, source_target_pairs={{0,6},{2,4},{4,2},{6,0},{1,7},{3,5},{5,3},{7,1},{8,14},{10,12},{12... | collective-permute-start | bytes 417800 | tf_op jit(solution)/shard_map/ppermute | solution.py:614
  11.5 1.8 %collective-permute-done.early = bf16[1040,128]{1,0:T(8,128)(2,1)S(1)} collective-permute-done((bf16[1040,128]{1,0:T(8,128)(2,1)}, bf16[1040,128]{1,0:T(8,128)(2,1)S(1)}, u32[]{:S(2)}, u32[]{:S(2)}) %collective-permute-start) | collective-permute-done | bytes 266272 | tf_op jit(solution)/shard_map/ppermute | solution.py:617
  13.4 2.1 %collective-permute-start.3 = (bf16[32,2176]{1,0:T(8,128)(2,1)}, bf16[32,2176]{1,0:T(8,128)(2,1)S(1)}, u32[]{:S(2)}, u32[]{:S(2)}) collective-permute-start(bf16[32,2176]{1,0:T(8,128)(2,1)} %get-tuple-element.88), channel_id=1, source_target_pairs={{0,2},{2,0},{4,6},{6,4},{1,3},{3,1},{5,7},{7,5},{8,10},{10,8},{12,... | collective-permute-start | bytes 417800 | tf_op jit(solution)/shard_map/ppermute | solution.py:614
  17.4 5.3 %collective-permute-done.2.refs_2_ = bf16[32,2176]{1,0:T(8,128)(2,1)S(1)} collective-permute-done((bf16[32,2176]{1,0:T(8,128)(2,1)}, bf16[32,2176]{1,0:T(8,128)(2,1)S(1)}, u32[]{:S(2)}, u32[]{:S(2)}) %collective-permute-start.2) | collective-permute-done | bytes 139296 | tf_op jit(solution)/shard_map/ppermute | solution.py:614
  25.4 1.6 %forward_first.1 = (bf16[1,8,128,128]{3,2,1,0:T(8,128)(2,1)S(1)}, bf16[128,1024]{1,0:T(8,128)(2,1)S(1)}, bf16[400,128]{1,0:T(8,128)(2,1)S(1)}, bf16[4,2,1040,128]{3,2,1,0:T(8,128)(2,1)S(1)}) custom-call(bf16[1040,128]{1,0:T(8,128)(2,1)S(1)} %get-tuple-element.91.refs_0_, bf16[1040,128]{1,0:T(8,128)(2,1)S(1)} %get-tuple-element.92.refs_1_, ...), custom_call_target="tpu_custom_call" | custom-call | tf_op jit(solution)/shard_map/forward_first/pallas_call | solution.py:638
  27.0 2.5 %collective-permute-start.12 = (bf16[400,128]{1,0:T(8,128)(2,1)S(1)}, bf16[400,128]{1,0:T(8,128)(2,1)S(1)}, u32[]{:S(2)}, u32[]{:S(2)}) collective-permute-start(bf16[400,128]{1,0:T(8,128)(2,1)S(1)} %get-tuple-element.102.refs_0_.refs_4_), channel_id=1, source_target_pairs={{0,6},{2,4},{4,2},{6,0},{1,7},{3,5},{5,3},{7,1},{8,14},{10,12},{12... | collective-permute-start | bytes 307208 | tf_op jit(solution)/shard_map/ppermute | solution.py:614
  29.5 1.9 %collective-permute-start.10 = (bf16[400,128]{1,0:T(8,128)(2,1)S(1)}, bf16[400,128]{1,0:T(8,128)(2,1)S(1)}, u32[]{:S(2)}, u32[]{:S(2)}) collective-permute-start(bf16[400,128]{1,0:T(8,128)(2,1)S(1)} %get-tuple-element.102.refs_0_.refs_4_), channel_id=1, source_target_pairs={{0,4},{2,6},{4,0},{6,2},{1,5},{3,7},{5,1},{7,3},{8,12},{10,14},{12... | collective-permute-start | bytes 307208 | tf_op jit(solution)/shard_map/ppermute | solution.py:614
  31.4 3.2 %collective-permute-done.12.refs_3_.refs_7_ = bf16[400,128]{1,0:T(8,128)(2,1)S(1)} collective-permute-done((bf16[400,128]{1,0:T(8,128)(2,1)S(1)}, bf16[400,128]{1,0:T(8,128)(2,1)S(1)}, u32[]{:S(2)}, u32[]{:S(2)}) %collective-permute-start.12) | collective-permute-done | bytes 102432 | tf_op jit(solution)/shard_map/ppermute | solution.py:614
  34.6 3.5 %collective-permute-done.11.refs_2_.refs_6_ = bf16[400,128]{1,0:T(8,128)(2,1)S(1)} collective-permute-done((bf16[400,128]{1,0:T(8,128)(2,1)S(1)}, bf16[400,128]{1,0:T(8,128)(2,1)S(1)}, u32[]{:S(2)}, u32[]{:S(2)}) %collective-permute-start.11) | collective-permute-done | bytes 102432 | tf_op jit(solution)/shard_map/ppermute | solution.py:614
  39.5 1.8 %collective-permute-start.15 = (bf16[256,128]{1,0:T(8,128)(2,1)S(1)}, bf16[256,128]{1,0:T(8,128)(2,1)S(1)}, u32[]{:S(2)}, u32[]{:S(2)}) collective-permute-start(bf16[256,128]{1,0:T(8,128)(2,1)S(1)} %get-tuple-element.104.refs_0_), channel_id=1, source_target_pairs={{0,6},{2,4},{4,2},{6,0},{1,7},{3,5},{5,3},{7,1},{8,14},{10,12},{12... | collective-permute-start | bytes 196616 | tf_op jit(solution)/shard_map/ppermute | solution.py:614
  41.8 2.2 %collective-permute-start.13 = (bf16[256,128]{1,0:T(8,128)(2,1)S(1)}, bf16[256,128]{1,0:T(8,128)(2,1)S(1)}, u32[]{:S(2)}, u32[]{:S(2)}) collective-permute-start(bf16[256,128]{1,0:T(8,128)(2,1)S(1)} %get-tuple-element.104.refs_0_), channel_id=1, source_target_pairs={{0,4},{2,6},{4,0},{6,2},{1,5},{3,7},{5,1},{7,3},{8,12},{10,14},{12... | collective-permute-start | bytes 196616 | tf_op jit(solution)/shard_map/ppermute | solution.py:614
  44.3 1.8 %collective-permute-start.21 = (bf16[256,128]{1,0:T(8,128)(2,1)S(1)}, bf16[256,128]{1,0:T(8,128)(2,1)S(1)}, u32[]{:S(2)}, u32[]{:S(2)}) collective-permute-start(bf16[256,128]{1,0:T(8,128)(2,1)S(1)} %side.1.refs_4_), channel_id=1, source_target_pairs={{0,6},{2,4},{4,2},{6,0},{1,7},{3,5},{5,3},{7,1},{8,14},{10,12},{12... | collective-permute-start | bytes 196616 | tf_op jit(solution)/shard_map/ppermute | solution.py:614
  46.4 2.3 %collective-permute-start.19 = (bf16[256,128]{1,0:T(8,128)(2,1)S(1)}, bf16[256,128]{1,0:T(8,128)(2,1)S(1)}, u32[]{:S(2)}, u32[]{:S(2)}) collective-permute-start(bf16[256,128]{1,0:T(8,128)(2,1)S(1)} %side.1.refs_4_), channel_id=1, source_target_pairs={{0,4},{2,6},{4,0},{6,2},{1,5},{3,7},{5,1},{7,3},{8,12},{10,14},{12... | collective-permute-start | bytes 196616 | tf_op jit(solution)/shard_map/ppermute | solution.py:614
  51.0 1.7 %collective-permute-start.18 = (bf16[256,128]{1,0:T(8,128)(2,1)S(1)}, bf16[256,128]{1,0:T(8,128)(2,1)S(1)}, u32[]{:S(2)}, u32[]{:S(2)}) collective-permute-start(bf16[256,128]{1,0:T(8,128)(2,1)S(1)} %get-tuple-element.107.refs_0_), channel_id=1, source_target_pairs={{0,6},{2,4},{4,2},{6,0},{1,7},{3,5},{5,3},{7,1},{8,14},{10,12},{12... | collective-permute-start | bytes 196616 | tf_op jit(solution)/shard_map/ppermute | solution.py:614
  52.8 2.7 %collective-permute-start.16 = (bf16[256,128]{1,0:T(8,128)(2,1)S(1)}, bf16[256,128]{1,0:T(8,128)(2,1)S(1)}, u32[]{:S(2)}, u32[]{:S(2)}) collective-permute-start(bf16[256,128]{1,0:T(8,128)(2,1)S(1)} %get-tuple-element.107.refs_0_), channel_id=1, source_target_pairs={{0,4},{2,6},{4,0},{6,2},{1,5},{3,7},{5,1},{7,3},{8,12},{10,14},{12... | collective-permute-start | bytes 196616 | tf_op jit(solution)/shard_map/ppermute | solution.py:614
  57.3 1.6 %collective-permute-done.17.refs_2_ = bf16[256,128]{1,0:T(8,128)(2,1)S(1)} collective-permute-done((bf16[256,128]{1,0:T(8,128)(2,1)S(1)}, bf16[256,128]{1,0:T(8,128)(2,1)S(1)}, u32[]{:S(2)}, u32[]{:S(2)}) %collective-permute-start.17) | collective-permute-done | bytes 65568 | tf_op jit(solution)/shard_map/ppermute | solution.py:614
  58.9 2.1 %turn.1 = (bf16[128,1024]{1,0:T(8,128)(2,1)S(1)}, f32[128,128]{1,0:T(8,128)S(1)}, bf16[128,128]{1,0:T(8,128)(2,1)S(1)}, f32[128,128]{1,0:T(8,128)S(1)}, bf16[128...) custom-call(bf16[256,128]{1,0:T(8,128)(2,1)S(1)} %get-tuple-element., ...), custom_call_target="tpu_custom_call" | custom-call | tf_op jit(solution)/shard_map/turn/pallas_call | solution.py:638
  60.9 2.1 %collective-permute-start.24 = (bf16[272,128]{1,0:T(8,128)(2,1)S(1)}, bf16[272,128]{1,0:T(8,128)(2,1)S(1)}, u32[]{:S(2)}, u32[]{:S(2)}) collective-permute-start(bf16[272,128]{1,0:T(8,128)(2,1)S(1)} %get-tuple-element.111.refs_0_), channel_id=1, source_target_pairs={{0,6},{2,4},{4,2},{6,0},{1,7},{3,5},{5,3},{7,1},{8,14},{10,12},{12... | collective-permute-start | bytes 208904 | tf_op jit(solution)/shard_map/ppermute | solution.py:614
  63.4 2.0 %collective-permute-start.22 = (bf16[272,128]{1,0:T(8,128)(2,1)S(1)}, bf16[272,128]{1,0:T(8,128)(2,1)S(1)}, u32[]{:S(2)}, u32[]{:S(2)}) collective-permute-start(bf16[272,128]{1,0:T(8,128)(2,1)S(1)} %get-tuple-element.111.refs_0_), channel_id=1, source_target_pairs={{0,4},{2,6},{4,0},{6,2},{1,5},{3,7},{5,1},{7,3},{8,12},{10,14},{12... | collective-permute-start | bytes 208904 | tf_op jit(solution)/shard_map/ppermute | solution.py:614
  65.4 2.2 %collective-permute-done.24.refs_3_ = bf16[272,128]{1,0:T(8,128)(2,1)S(1)} collective-permute-done((bf16[272,128]{1,0:T(8,128)(2,1)S(1)}, bf16[272,128]{1,0:T(8,128)(2,1)S(1)}, u32[]{:S(2)}, u32[]{:S(2)}) %collective-permute-start.24) | collective-permute-done | bytes 69664 | tf_op jit(solution)/shard_map/ppermute | solution.py:614
  70.1 3.2 %collective-permute-start.27 = (bf16[144,128]{1,0:T(8,128)(2,1)S(1)}, bf16[144,128]{1,0:T(8,128)(2,1)S(1)}, u32[]{:S(2)}, u32[]{:S(2)}) collective-permute-start(bf16[144,128]{1,0:T(8,128)(2,1)S(1)} %get-tuple-element.130.refs_0_), channel_id=1, source_target_pairs={{0,6},{2,4},{4,2},{6,0},{1,7},{3,5},{5,3},{7,1},{8,14},{10,12},{12... | collective-permute-start | bytes 110600 | tf_op jit(solution)/shard_map/ppermute | solution.py:614
  79.5 1.5 %collective-permute-start.30 = (bf16[144,128]{1,0:T(8,128)(2,1)S(1)}, bf16[144,128]{1,0:T(8,128)(2,1)S(1)}, u32[]{:S(2)}, u32[]{:S(2)}) collective-permute-start(bf16[144,128]{1,0:T(8,128)(2,1)S(1)} %get-tuple-element.137.refs_0_), channel_id=1, source_target_pairs={{0,6},{2,4},{4,2},{6,0},{1,7},{3,5},{5,3},{7,1},{8,14},{10,12},{12... | collective-permute-start | bytes 110600 | tf_op jit(solution)/shard_map/ppermute | solution.py:614
  81.6 2.3 %collective-permute-start.28 = (bf16[144,128]{1,0:T(8,128)(2,1)S(1)}, bf16[144,128]{1,0:T(8,128)(2,1)S(1)}, u32[]{:S(2)}, u32[]{:S(2)}) collective-permute-start(bf16[144,128]{1,0:T(8,128)(2,1)S(1)} %get-tuple-element.137.refs_0_), channel_id=1, source_target_pairs={{0,4},{2,6},{4,0},{6,2},{1,5},{3,7},{5,1},{7,3},{8,12},{10,14},{12... | collective-permute-start | bytes 110600 | tf_op jit(solution)/shard_map/ppermute | solution.py:614
  87.9 1.5 %collective-permute-done.31.refs_4_ = bf16[272,512]{1,0:T(8,128)(2,1)S(1)} collective-permute-done((bf16[272,512]{1,0:T(8,128)(2,1)S(1)}, bf16[272,512]{1,0:T(8,128)(2,1)S(1)}, u32[]{:S(2)}, u32[]{:S(2)}) %collective-permute-start.31) | collective-permute-done | bytes 278560 | tf_op jit(solution)/shard_map/ppermute | solution.py:620
  89.7 1.5 %collective-permute-start.35 = (bf16[544,256]{1,0:T(8,128)(2,1)S(1)}, bf16[544,256]{1,0:T(8,128)(2,1)S(1)}, u32[]{:S(2)}, u32[]{:S(2)}) collective-permute-start(bf16[544,256]{1,0:T(8,128)(2,1)S(1)} %get-tuple-element.157), channel_id=1, source_target_pairs={{0,8},{8,0},{16,24},{24,16},{1,9},{9,1},{17,25},{25,17},{2,10},{10... | collective-permute-start | bytes 835592 | tf_op jit(solution)/shard_map/ppermute | solution.py:617
  91.3 1.5 %collective-permute-start.36 = (bf16[544,256]{1,0:T(8,128)(2,1)S(1)}, bf16[544,256]{1,0:T(8,128)(2,1)S(1)}, u32[]{:S(2)}, u32[]{:S(2)}) collective-permute-start(bf16[544,256]{1,0:T(8,128)(2,1)S(1)} %get-tuple-element.158), channel_id=1, source_target_pairs={{0,16},{8,24},{16,0},{24,8},{1,17},{9,25},{17,1},{25,9},{2,18},{10... | collective-permute-start | bytes 835592 | tf_op jit(solution)/shard_map/ppermute | solution.py:617
  92.8 5.7 %collective-permute-done.35.from_x = bf16[544,256]{1,0:T(8,128)(2,1)S(1)} collective-permute-done((bf16[544,256]{1,0:T(8,128)(2,1)S(1)}, bf16[544,256]{1,0:T(8,128)(2,1)S(1)}, u32[]{:S(2)}, u32[]{:S(2)}) %collective-permute-start.35) | collective-permute-done | bytes 278560 | tf_op jit(solution)/shard_map/ppermute | solution.py:617
  100.4 1.5 %collective-permute-start.38 = (bf16[272,256]{1,0:T(8,128)(2,1)S(1)}, bf16[272,256]{1,0:T(8,128)(2,1)S(1)}, u32[]{:S(2)}, u32[]{:S(2)}) collective-permute-start(bf16[272,256]{1,0:T(8,128)(2,1)S(1)} %get-tuple-element.162), channel_id=1, source_target_pairs={{0,16},{8,24},{16,0},{24,8},{1,17},{9,25},{17,1},{25,9},{2,18},{10... | collective-permute-start | bytes 417800 | tf_op jit(solution)/shard_map/ppermute | solution.py:617
  101.9 3.0 %collective-permute-done.37.last_x = bf16[272,256]{1,0:T(8,128)(2,1)S(1)} collective-permute-done((bf16[272,256]{1,0:T(8,128)(2,1)S(1)}, bf16[272,256]{1,0:T(8,128)(2,1)S(1)}, u32[]{:S(2)}, u32[]{:S(2)}) %collective-permute-start.37) | collective-permute-done | bytes 139296 | tf_op jit(solution)/shard_map/ppermute | solution.py:617
  (67 shorter events, 28.2 us)
Async XLA Ops:
  2.9 10.4 %collective-permute-start = (bf16[1040,128]{1,0:T(8,128)(2,1)}, bf16[1040,128]{1,0:T(8,128)(2,1)S(1)}, u32[]{:S(2)}, u32[]{:S(2)}) collective-permute-start(bf16[1040,128]{1,0:T(8,128)(2,1)} %get-tuple-element.84.packed), channel_id=1, source_target_pairs={{0,8},{8,0},{16,24},{24,16},{1,9},{9,1},{17,25},{25,17},{2,10},{10... | collective-permute-start | bytes 798728 | tf_op jit(solution)/shard_map/ppermute | solution.py:617
  5.9 16.8 %collective-permute-start.5 = (bf16[1040,128]{1,0:T(8,128)(2,1)}, bf16[1040,128]{1,0:T(8,128)(2,1)S(1)}, u32[]{:S(2)}, u32[]{:S(2)}) collective-permute-start(bf16[1040,128]{1,0:T(8,128)(2,1)} %get-tuple-element.84.packed), channel_id=1, source_target_pairs={{0,24},{8,16},{16,8},{24,0},{1,25},{9,17},{17,9},{25,1},{2,26},{10... | collective-permute-start | bytes 798728 | tf_op jit(solution)/shard_map/ppermute | solution.py:617
  7.4 15.3 %collective-permute-start.4 = (bf16[1040,128]{1,0:T(8,128)(2,1)}, bf16[1040,128]{1,0:T(8,128)(2,1)S(1)}, u32[]{:S(2)}, u32[]{:S(2)}) collective-permute-start(bf16[1040,128]{1,0:T(8,128)(2,1)} %get-tuple-element.84.packed), channel_id=1, source_target_pairs={{0,16},{8,24},{16,0},{24,8},{1,17},{9,25},{17,1},{25,9},{2,18},{10... | collective-permute-start | bytes 798728 | tf_op jit(solution)/shard_map/ppermute | solution.py:617
  7.5 9.9 %collective-permute-start.1 = (bf16[32,2176]{1,0:T(8,128)(2,1)}, bf16[32,2176]{1,0:T(8,128)(2,1)S(1)}, u32[]{:S(2)}, u32[]{:S(2)}) collective-permute-start(bf16[32,2176]{1,0:T(8,128)(2,1)} %get-tuple-element.86), channel_id=1, source_target_pairs={{0,6},{2,4},{4,2},{6,0},{1,7},{3,5},{5,3},{7,1},{8,14},{10,12},{12... | collective-permute-start | bytes 417800 | tf_op jit(solution)/shard_map/ppermute | solution.py:614
  11.5 11.1 %collective-permute-start.2 = (bf16[32,2176]{1,0:T(8,128)(2,1)}, bf16[32,2176]{1,0:T(8,128)(2,1)S(1)}, u32[]{:S(2)}, u32[]{:S(2)}) collective-permute-start(bf16[32,2176]{1,0:T(8,128)(2,1)} %get-tuple-element.87), channel_id=1, source_target_pairs={{0,4},{2,6},{4,0},{6,2},{1,5},{3,7},{5,1},{7,3},{8,12},{10,14},{12... | collective-permute-start | bytes 417800 | tf_op jit(solution)/shard_map/ppermute | solution.py:614
  13.4 9.3 %collective-permute-start.3 = (bf16[32,2176]{1,0:T(8,128)(2,1)}, bf16[32,2176]{1,0:T(8,128)(2,1)S(1)}, u32[]{:S(2)}, u32[]{:S(2)}) collective-permute-start(bf16[32,2176]{1,0:T(8,128)(2,1)} %get-tuple-element.88), channel_id=1, source_target_pairs={{0,2},{2,0},{4,6},{6,4},{1,3},{3,1},{5,7},{7,5},{8,10},{10,8},{12,... | collective-permute-start | bytes 417800 | tf_op jit(solution)/shard_map/ppermute | solution.py:614
  27.0 7.7 %collective-permute-start.12 = (bf16[400,128]{1,0:T(8,128)(2,1)S(1)}, bf16[400,128]{1,0:T(8,128)(2,1)S(1)}, u32[]{:S(2)}, u32[]{:S(2)}) collective-permute-start(bf16[400,128]{1,0:T(8,128)(2,1)S(1)} %get-tuple-element.102.refs_0_.refs_4_), channel_id=1, source_target_pairs={{0,6},{2,4},{4,2},{6,0},{1,7},{3,5},{5,3},{7,1},{8,14},{10,12},{12... | collective-permute-start | bytes 307208 | tf_op jit(solution)/shard_map/ppermute | solution.py:614
  29.5 8.6 %collective-permute-start.11 = (bf16[400,128]{1,0:T(8,128)(2,1)S(1)}, bf16[400,128]{1,0:T(8,128)(2,1)S(1)}, u32[]{:S(2)}, u32[]{:S(2)}) collective-permute-start(bf16[400,128]{1,0:T(8,128)(2,1)S(1)} %get-tuple-element.102.refs_0_.refs_4_), channel_id=1, source_target_pairs={{0,2},{2,0},{4,6},{6,4},{1,3},{3,1},{5,7},{7,5},{8,10},{10,8},{12,... | collective-permute-start | bytes 307208 | tf_op jit(solution)/shard_map/ppermute | solution.py:614
  29.5 8.6 %collective-permute-start.10 = (bf16[400,128]{1,0:T(8,128)(2,1)S(1)}, bf16[400,128]{1,0:T(8,128)(2,1)S(1)}, u32[]{:S(2)}, u32[]{:S(2)}) collective-permute-start(bf16[400,128]{1,0:T(8,128)(2,1)S(1)} %get-tuple-element.102.refs_0_.refs_4_), channel_id=1, source_target_pairs={{0,4},{2,6},{4,0},{6,2},{1,5},{3,7},{5,1},{7,3},{8,12},{10,14},{12... | collective-permute-start | bytes 307208 | tf_op jit(solution)/shard_map/ppermute | solution.py:614
  39.5 6.9 %collective-permute-start.15 = (bf16[256,128]{1,0:T(8,128)(2,1)S(1)}, bf16[256,128]{1,0:T(8,128)(2,1)S(1)}, u32[]{:S(2)}, u32[]{:S(2)}) collective-permute-start(bf16[256,128]{1,0:T(8,128)(2,1)S(1)} %get-tuple-element.104.refs_0_), channel_id=1, source_target_pairs={{0,6},{2,4},{4,2},{6,0},{1,7},{3,5},{5,3},{7,1},{8,14},{10,12},{12... | collective-permute-start | bytes 196616 | tf_op jit(solution)/shard_map/ppermute | solution.py:614
  41.3 7.4 %collective-permute-start.14 = (bf16[256,128]{1,0:T(8,128)(2,1)S(1)}, bf16[256,128]{1,0:T(8,128)(2,1)S(1)}, u32[]{:S(2)}, u32[]{:S(2)}) collective-permute-start(bf16[256,128]{1,0:T(8,128)(2,1)S(1)} %get-tuple-element.104.refs_0_), channel_id=1, source_target_pairs={{0,2},{2,0},{4,6},{6,4},{1,3},{3,1},{5,7},{7,5},{8,10},{10,8},{12,... | collective-permute-start | bytes 196616 | tf_op jit(solution)/shard_map/ppermute | solution.py:614
  41.8 8.0 %collective-permute-start.13 = (bf16[256,128]{1,0:T(8,128)(2,1)S(1)}, bf16[256,128]{1,0:T(8,128)(2,1)S(1)}, u32[]{:S(2)}, u32[]{:S(2)}) collective-permute-start(bf16[256,128]{1,0:T(8,128)(2,1)S(1)} %get-tuple-element.104.refs_0_), channel_id=1, source_target_pairs={{0,4},{2,6},{4,0},{6,2},{1,5},{3,7},{5,1},{7,3},{8,12},{10,14},{12... | collective-permute-start | bytes 196616 | tf_op jit(solution)/shard_map/ppermute | solution.py:614
  44.3 8.5 %collective-permute-start.21 = (bf16[256,128]{1,0:T(8,128)(2,1)S(1)}, bf16[256,128]{1,0:T(8,128)(2,1)S(1)}, u32[]{:S(2)}, u32[]{:S(2)}) collective-permute-start(bf16[256,128]{1,0:T(8,128)(2,1)S(1)} %side.1.refs_4_), channel_id=1, source_target_pairs={{0,6},{2,4},{4,2},{6,0},{1,7},{3,5},{5,3},{7,1},{8,14},{10,12},{12... | collective-permute-start | bytes 196616 | tf_op jit(solution)/shard_map/ppermute | solution.py:614
  46.1 9.4 %collective-permute-start.20 = (bf16[256,128]{1,0:T(8,128)(2,1)S(1)}, bf16[256,128]{1,0:T(8,128)(2,1)S(1)}, u32[]{:S(2)}, u32[]{:S(2)}) collective-permute-start(bf16[256,128]{1,0:T(8,128)(2,1)S(1)} %side.1.refs_4_), channel_id=1, source_target_pairs={{0,2},{2,0},{4,6},{6,4},{1,3},{3,1},{5,7},{7,5},{8,10},{10,8},{12,... | collective-permute-start | bytes 196616 | tf_op jit(solution)/shard_map/ppermute | solution.py:614
  46.4 9.6 %collective-permute-start.19 = (bf16[256,128]{1,0:T(8,128)(2,1)S(1)}, bf16[256,128]{1,0:T(8,128)(2,1)S(1)}, u32[]{:S(2)}, u32[]{:S(2)}) collective-permute-start(bf16[256,128]{1,0:T(8,128)(2,1)S(1)} %side.1.refs_4_), channel_id=1, source_target_pairs={{0,4},{2,6},{4,0},{6,2},{1,5},{3,7},{5,1},{7,3},{8,12},{10,14},{12... | collective-permute-start | bytes 196616 | tf_op jit(solution)/shard_map/ppermute | solution.py:614
  51.0 6.3 %collective-permute-start.18 = (bf16[256,128]{1,0:T(8,128)(2,1)S(1)}, bf16[256,128]{1,0:T(8,128)(2,1)S(1)}, u32[]{:S(2)}, u32[]{:S(2)}) collective-permute-start(bf16[256,128]{1,0:T(8,128)(2,1)S(1)} %get-tuple-element.107.refs_0_), channel_id=1, source_target_pairs={{0,6},{2,4},{4,2},{6,0},{1,7},{3,5},{5,3},{7,1},{8,14},{10,12},{12... | collective-permute-start | bytes 196616 | tf_op jit(solution)/shard_map/ppermute | solution.py:614
  52.8 6.1 %collective-permute-start.17 = (bf16[256,128]{1,0:T(8,128)(2,1)S(1)}, bf16[256,128]{1,0:T(8,128)(2,1)S(1)}, u32[]{:S(2)}, u32[]{:S(2)}) collective-permute-start(bf16[256,128]{1,0:T(8,128)(2,1)S(1)} %get-tuple-element.107.refs_0_), channel_id=1, source_target_pairs={{0,2},{2,0},{4,6},{6,4},{1,3},{3,1},{5,7},{7,5},{8,10},{10,8},{12,... | collective-permute-start | bytes 196616 | tf_op jit(solution)/shard_map/ppermute | solution.py:614
  52.8 6.1 %collective-permute-start.16 = (bf16[256,128]{1,0:T(8,128)(2,1)S(1)}, bf16[256,128]{1,0:T(8,128)(2,1)S(1)}, u32[]{:S(2)}, u32[]{:S(2)}) collective-permute-start(bf16[256,128]{1,0:T(8,128)(2,1)S(1)} %get-tuple-element.107.refs_0_), channel_id=1, source_target_pairs={{0,4},{2,6},{4,0},{6,2},{1,5},{3,7},{5,1},{7,3},{8,12},{10,14},{12... | collective-permute-start | bytes 196616 | tf_op jit(solution)/shard_map/ppermute | solution.py:614
  60.9 6.7 %collective-permute-start.24 = (bf16[272,128]{1,0:T(8,128)(2,1)S(1)}, bf16[272,128]{1,0:T(8,128)(2,1)S(1)}, u32[]{:S(2)}, u32[]{:S(2)}) collective-permute-start(bf16[272,128]{1,0:T(8,128)(2,1)S(1)} %get-tuple-element.111.refs_0_), channel_id=1, source_target_pairs={{0,6},{2,4},{4,2},{6,0},{1,7},{3,5},{5,3},{7,1},{8,14},{10,12},{12... | collective-permute-start | bytes 208904 | tf_op jit(solution)/shard_map/ppermute | solution.py:614
  63.1 5.2 %collective-permute-start.23 = (bf16[272,128]{1,0:T(8,128)(2,1)S(1)}, bf16[272,128]{1,0:T(8,128)(2,1)S(1)}, u32[]{:S(2)}, u32[]{:S(2)}) collective-permute-start(bf16[272,128]{1,0:T(8,128)(2,1)S(1)} %get-tuple-element.111.refs_0_), channel_id=1, source_target_pairs={{0,2},{2,0},{4,6},{6,4},{1,3},{3,1},{5,7},{7,5},{8,10},{10,8},{12,... | collective-permute-start | bytes 208904 | tf_op jit(solution)/shard_map/ppermute | solution.py:614
  63.4 5.5 %collective-permute-start.22 = (bf16[272,128]{1,0:T(8,128)(2,1)S(1)}, bf16[272,128]{1,0:T(8,128)(2,1)S(1)}, u32[]{:S(2)}, u32[]{:S(2)}) collective-permute-start(bf16[272,128]{1,0:T(8,128)(2,1)S(1)} %get-tuple-element.111.refs_0_), channel_id=1, source_target_pairs={{0,4},{2,6},{4,0},{6,2},{1,5},{3,7},{5,1},{7,3},{8,12},{10,14},{12... | collective-permute-start | bytes 208904 | tf_op jit(solution)/shard_map/ppermute | solution.py:614
  70.1 5.8 %collective-permute-start.27 = (bf16[144,128]{1,0:T(8,128)(2,1)S(1)}, bf16[144,128]{1,0:T(8,128)(2,1)S(1)}, u32[]{:S(2)}, u32[]{:S(2)}) collective-permute-start(bf16[144,128]{1,0:T(8,128)(2,1)S(1)} %get-tuple-element.130.refs_0_), channel_id=1, source_target_pairs={{0,6},{2,4},{4,2},{6,0},{1,7},{3,5},{5,3},{7,1},{8,14},{10,12},{12... | collective-permute-start | bytes 110600 | tf_op jit(solution)/shard_map/ppermute | solution.py:614
  73.3 4.0 %collective-permute-start.26 = (bf16[144,128]{1,0:T(8,128)(2,1)S(1)}, bf16[144,128]{1,0:T(8,128)(2,1)S(1)}, u32[]{:S(2)}, u32[]{:S(2)}) collective-permute-start(bf16[144,128]{1,0:T(8,128)(2,1)S(1)} %get-tuple-element.130.refs_0_), channel_id=1, source_target_pairs={{0,2},{2,0},{4,6},{6,4},{1,3},{3,1},{5,7},{7,5},{8,10},{10,8},{12,... | collective-permute-start | bytes 110600 | tf_op jit(solution)/shard_map/ppermute | solution.py:614
  73.3 4.9 %collective-permute-start.25 = (bf16[144,128]{1,0:T(8,128)(2,1)S(1)}, bf16[144,128]{1,0:T(8,128)(2,1)S(1)}, u32[]{:S(2)}, u32[]{:S(2)}) collective-permute-start(bf16[144,128]{1,0:T(8,128)(2,1)S(1)} %get-tuple-element.130.refs_0_), channel_id=1, source_target_pairs={{0,4},{2,6},{4,0},{6,2},{1,5},{3,7},{5,1},{7,3},{8,12},{10,14},{12... | collective-permute-start | bytes 110600 | tf_op jit(solution)/shard_map/ppermute | solution.py:614
  79.5 5.9 %collective-permute-start.30 = (bf16[144,128]{1,0:T(8,128)(2,1)S(1)}, bf16[144,128]{1,0:T(8,128)(2,1)S(1)}, u32[]{:S(2)}, u32[]{:S(2)}) collective-permute-start(bf16[144,128]{1,0:T(8,128)(2,1)S(1)} %get-tuple-element.137.refs_0_), channel_id=1, source_target_pairs={{0,6},{2,4},{4,2},{6,0},{1,7},{3,5},{5,3},{7,1},{8,14},{10,12},{12... | collective-permute-start | bytes 110600 | tf_op jit(solution)/shard_map/ppermute | solution.py:614
  81.0 4.4 %collective-permute-start.29 = (bf16[144,128]{1,0:T(8,128)(2,1)S(1)}, bf16[144,128]{1,0:T(8,128)(2,1)S(1)}, u32[]{:S(2)}, u32[]{:S(2)}) collective-permute-start(bf16[144,128]{1,0:T(8,128)(2,1)S(1)} %get-tuple-element.137.refs_0_), channel_id=1, source_target_pairs={{0,2},{2,0},{4,6},{6,4},{1,3},{3,1},{5,7},{7,5},{8,10},{10,8},{12,... | collective-permute-start | bytes 110600 | tf_op jit(solution)/shard_map/ppermute | solution.py:614
  81.6 4.9 %collective-permute-start.28 = (bf16[144,128]{1,0:T(8,128)(2,1)S(1)}, bf16[144,128]{1,0:T(8,128)(2,1)S(1)}, u32[]{:S(2)}, u32[]{:S(2)}) collective-permute-start(bf16[144,128]{1,0:T(8,128)(2,1)S(1)} %get-tuple-element.137.refs_0_), channel_id=1, source_target_pairs={{0,4},{2,6},{4,0},{6,2},{1,5},{3,7},{5,1},{7,3},{8,12},{10,14},{12... | collective-permute-start | bytes 110600 | tf_op jit(solution)/shard_map/ppermute | solution.py:614
  84.3 3.6 %collective-permute-start.32 = (bf16[272,512]{1,0:T(8,128)(2,1)S(1)}, bf16[272,512]{1,0:T(8,128)(2,1)S(1)}, u32[]{:S(2)}, u32[]{:S(2)}) collective-permute-start(bf16[272,512]{1,0:T(8,128)(2,1)S(1)} %get-tuple-element.153), channel_id=1, source_target_pairs={{0,1},{1,0},{2,3},{3,2},{4,5},{5,4},{6,7},{7,6},{8,9},{9,8},{10,11... | collective-permute-start | bytes 835592 | tf_op jit(solution)/shard_map/ppermute | solution.py:620
  89.7 8.8 %collective-permute-start.35 = (bf16[544,256]{1,0:T(8,128)(2,1)S(1)}, bf16[544,256]{1,0:T(8,128)(2,1)S(1)}, u32[]{:S(2)}, u32[]{:S(2)}) collective-permute-start(bf16[544,256]{1,0:T(8,128)(2,1)S(1)} %get-tuple-element.157), channel_id=1, source_target_pairs={{0,8},{8,0},{16,24},{24,16},{1,9},{9,1},{17,25},{25,17},{2,10},{10... | collective-permute-start | bytes 835592 | tf_op jit(solution)/shard_map/ppermute | solution.py:617
  91.3 8.4 %collective-permute-start.36 = (bf16[544,256]{1,0:T(8,128)(2,1)S(1)}, bf16[544,256]{1,0:T(8,128)(2,1)S(1)}, u32[]{:S(2)}, u32[]{:S(2)}) collective-permute-start(bf16[544,256]{1,0:T(8,128)(2,1)S(1)} %get-tuple-element.158), channel_id=1, source_target_pairs={{0,16},{8,24},{16,0},{24,8},{1,17},{9,25},{17,1},{25,9},{2,18},{10... | collective-permute-start | bytes 835592 | tf_op jit(solution)/shard_map/ppermute | solution.py:617
  99.8 5.1 %collective-permute-start.37 = (bf16[272,256]{1,0:T(8,128)(2,1)S(1)}, bf16[272,256]{1,0:T(8,128)(2,1)S(1)}, u32[]{:S(2)}, u32[]{:S(2)}) collective-permute-start(bf16[272,256]{1,0:T(8,128)(2,1)S(1)} %get-tuple-element.161), channel_id=1, source_target_pairs={{0,8},{8,0},{16,24},{24,16},{1,9},{9,1},{17,25},{25,17},{2,10},{10... | collective-permute-start | bytes 417800 | tf_op jit(solution)/shard_map/ppermute | solution.py:617
  100.4 5.1 %collective-permute-start.38 = (bf16[272,256]{1,0:T(8,128)(2,1)S(1)}, bf16[272,256]{1,0:T(8,128)(2,1)S(1)}, u32[]{:S(2)}, u32[]{:S(2)}) collective-permute-start(bf16[272,256]{1,0:T(8,128)(2,1)S(1)} %get-tuple-element.162), channel_id=1, source_target_pairs={{0,16},{8,24},{16,0},{24,8},{1,17},{9,25},{17,1},{25,9},{2,18},{10... | collective-permute-start | bytes 417800 | tf_op jit(solution)/shard_map/ppermute | solution.py:617
  (9 other events, 16.9 us)
